TPU v7x, 32 devices: a whole 2x2x4 slice. The times are simulated.
32 devices in a mesh: seq: 16 (over z, y, x), head: 2 (over core).
Axes of the slice: x: 2, y: 2, z: 4, core: 2. Of those that a mesh axis runs over, the one named last changes fastest.
Arguments:
- text_rows: bfloat16 [2048, 4096], P('seq', 'head'), may hold values from -6 to 6
- picture_rows: bfloat16 [512, 4096], P('seq', 'head'), may hold values from -6 to 6
- picture_slots: int32 [512], P('seq'), may hold values from 0 to 2047, as said below
- norm_gain: float32 [4096], replicated, may hold values from 0.1 to 1.9
- w_query: bfloat16 [4096, 4096], P('seq', 'head'), may hold values from -1 to 1
- w_key: bfloat16 [4096, 1024], P('seq', 'head'), may hold values from -1 to 1
- w_value: bfloat16 [4096, 1024], P('seq', 'head'), may hold values from -0.09375 to 0.09375
- w_out: bfloat16 [4096, 4096], P('head', 'seq'), may hold values from -0.5 to 0.5
- cache_keys: bfloat16 [1024, 1024], P('seq', 'head'), may hold values from -500 to 500
- cache_values: bfloat16 [1024, 1024], P('seq', 'head'), may hold values from -6 to 6
- recompute_rows: bfloat16 [128, 4096], P('seq', 'head'), may hold values from -6 to 6
- recompute_slots: int32 [128], P('seq'), may hold values from 0 to 1023, as said below
Outputs:
- mixed: bfloat16 [2048, 4096], P('seq', 'head')
Inputs may be any that keep to these rules, and one draw needn't show every extreme that they name: `picture_slots`: distinct stream positions, in runs of 256 consecutive positions, one run a tile; the first tile's run starts at position 1024 and the last tile's run ends at the stream's last position. `recompute_slots`: each aligned block b of 8 entries names distinct rows of cache rows b * 64 to (b + 1) * 64 - 1.
All inputs are finite; a program needn't handle non-finite values.
Results may differ from a plain program's by a relative error of at most 0.02.
Values may be sent and summed in bfloat16 or wider, within the bound.
No kernel may reach another device: no remote copies, remote signals or barrier semaphores. Data moves between devices by JAX's collectives and lax.ppermute only.
A program may use at most 128 MiB of HBM per device.

v0:
```python
import jax
import jax.numpy as jnp
from jax import lax
from jax.sharding import PartitionSpec as P

D = 4096
HD = 128


EPSILON = 1e-05
ROPE_BASE = 1000000.0
NEG_FILL = -1e30


def rotate(values, positions):
    half = values.shape[-1] // 2
    freqs = ROPE_BASE ** (-jnp.arange(half, dtype=jnp.float32) / half)
    angles = positions[:, None] * freqs[None, :]
    cosine = jnp.cos(angles)[:, None, :]
    sine = jnp.sin(angles)[:, None, :]
    first = values[..., :half]
    second = values[..., half:]
    return jnp.concatenate(
        [first * cosine - second * sine, second * cosine + first * sine], axis=-1
    )


def scaled(rows_wide, squares, gain):
    return (rows_wide * lax.rsqrt(squares / D + EPSILON)[:, None] * gain[None, :]).astype(
        jnp.bfloat16
    )


def attend(carry, key_piece, value_piece, queries, allowed):
    best, total, accum = carry
    count = key_piece.shape[0]
    kv_local = queries.shape[0]
    keys_split = key_piece.reshape(count, kv_local, HD)
    values_split = value_piece.reshape(count, kv_local, HD)
    scores = jnp.einsum(
        "kgtd,nkd->kgtn", queries, keys_split, preferred_element_type=jnp.float32
    ) * HD ** (-0.5)
    scores = jnp.where(allowed, scores, NEG_FILL)
    fresh = jnp.maximum(best, jnp.max(scores, axis=-1))
    factor = jnp.exp(best - fresh)
    weights = jnp.where(allowed, jnp.exp(scores - fresh[..., None]), 0.0)
    total = total * factor + jnp.sum(weights, axis=-1)
    accum = accum * factor[..., None] + jnp.einsum(
        "kgtn,nkd->kgtd",
        weights.astype(jnp.bfloat16),
        values_split,
        preferred_element_type=jnp.float32,
    )
    return (fresh, total, accum)


def on_device(
    text_rows,
    picture_rows,
    picture_slots,
    norm_gain,
    w_query,
    w_key,
    w_value,
    w_out,
    cache_keys,
    cache_values,
    recompute_rows,
    recompute_slots,
):
    tok_rows = text_rows.shape[0]
    rec_count = recompute_rows.shape[0]
    cache_rows = cache_keys.shape[0]
    seq_index = lax.axis_index("seq")
    local_pos = seq_index * tok_rows + jnp.arange(tok_rows, dtype=jnp.int32)
    rows_piece = lax.all_gather(picture_rows, "seq", axis=0, tiled=True)
    slots_piece = lax.all_gather(picture_slots, "seq", axis=0, tiled=True)
    select = (slots_piece[None, :] == local_pos[:, None]).astype(jnp.bfloat16)
    placed = jnp.dot(select, rows_piece, preferred_element_type=jnp.float32)
    hits = jnp.sum(select.astype(jnp.float32), axis=1)
    added, hits = (placed, hits)
    stream = jnp.where(hits[:, None] > 0.5, added, text_rows.astype(jnp.float32)).astype(
        jnp.bfloat16
    )
    slice_width = stream.shape[1]
    gain_slice = lax.dynamic_slice_in_dim(
        norm_gain, lax.axis_index("head") * slice_width, slice_width, 0
    )
    stream_wide = stream.astype(jnp.float32)
    rec_wide = recompute_rows.astype(jnp.float32)
    stream_sq, rec_sq = lax.psum(
        (jnp.sum(stream_wide * stream_wide, axis=1), jnp.sum(rec_wide * rec_wide, axis=1)), "head"
    )
    normed, rec_normed = (
        lax.all_gather(scaled(stream_wide, stream_sq, gain_slice), "head", axis=1, tiled=True),
        lax.all_gather(scaled(rec_wide, rec_sq, gain_slice), "head", axis=1, tiled=True),
    )
    stacked = jnp.concatenate([normed, rec_normed], axis=0)
    query_cols = w_query.shape[1]
    key_cols = w_key.shape[1]
    pieces = (
        lax.all_gather(w_query, "seq", axis=0, tiled=True),
        lax.all_gather(w_key, "seq", axis=0, tiled=True),
        lax.all_gather(w_value, "seq", axis=0, tiled=True),
    )
    query_all = jnp.dot(stacked, pieces[0], preferred_element_type=jnp.float32)
    key_all = jnp.dot(stacked, pieces[1], preferred_element_type=jnp.float32)
    value_all = jnp.dot(stacked, pieces[2], preferred_element_type=jnp.float32)
    cache_total = cache_rows * lax.axis_size("seq")
    stream_pos = (cache_total + local_pos).astype(jnp.float32)
    rec_pos = recompute_slots.astype(jnp.float32)
    heads_local = query_cols // HD
    kv_local = key_cols // HD
    group = heads_local // kv_local
    rot_query = rotate(query_all[:tok_rows].reshape(tok_rows, heads_local, HD), stream_pos).astype(
        jnp.bfloat16
    )
    rot_key = (
        rotate(key_all[:tok_rows].reshape(tok_rows, kv_local, HD), stream_pos)
        .astype(jnp.bfloat16)
        .reshape(tok_rows, key_cols)
    )
    values_new = value_all[:tok_rows].astype(jnp.bfloat16)
    rot_rec_key = (
        rotate(key_all[tok_rows:].reshape(rec_count, kv_local, HD), rec_pos)
        .astype(jnp.bfloat16)
        .reshape(rec_count, key_cols)
    )
    rec_values = value_all[tok_rows:].astype(jnp.bfloat16)
    local_slots = recompute_slots - seq_index * cache_rows
    select = local_slots[:, None] == jnp.arange(cache_rows, dtype=jnp.int32)[None, :]
    replaced = jnp.any(select, axis=0)[:, None]
    select_cols = select.astype(jnp.bfloat16).T
    new_keys = jnp.dot(select_cols, rot_rec_key, preferred_element_type=jnp.float32).astype(
        jnp.bfloat16
    )
    new_values = jnp.dot(select_cols, rec_values, preferred_element_type=jnp.float32).astype(
        jnp.bfloat16
    )
    cache_k = jnp.where(replaced, new_keys, cache_keys)
    cache_v = jnp.where(replaced, new_values, cache_values)
    queries = jnp.transpose(rot_query.reshape(tok_rows, kv_local, group, HD), (1, 2, 0, 3))
    carry_start = (
        jnp.full((kv_local, group, tok_rows), NEG_FILL, jnp.float32),
        jnp.zeros((kv_local, group, tok_rows), jnp.float32),
        jnp.zeros((kv_local, group, tok_rows, HD), jnp.float32),
    )
    pieces = (
        lax.all_gather(cache_k, "seq", axis=0, tiled=True),
        lax.all_gather(cache_v, "seq", axis=0, tiled=True),
    )
    allowed = jnp.ones((tok_rows, pieces[0].shape[0]), jnp.bool_)
    carry_mid = attend(carry_start, pieces[0], pieces[1], queries, allowed)
    pieces = (
        lax.all_gather(rot_key, "seq", axis=0, tiled=True),
        lax.all_gather(values_new, "seq", axis=0, tiled=True),
    )
    key_pos = jnp.arange(pieces[0].shape[0], dtype=jnp.int32)
    allowed = key_pos[None, :] <= local_pos[:, None]
    best, total, accum = attend(carry_mid, pieces[0], pieces[1], queries, allowed)
    attended = (
        jnp.transpose(accum / total[..., None], (2, 0, 1, 3))
        .reshape(tok_rows, query_cols)
        .astype(jnp.bfloat16)
    )
    partial_out = jnp.dot(
        attended,
        lax.all_gather(w_out, "seq", axis=1, tiled=True),
        preferred_element_type=jnp.float32,
    )
    return lax.psum_scatter(
        partial_out.astype(jnp.bfloat16), "head", scatter_dimension=1, tiled=True
    )


def solution(mesh):
    return jax.shard_map(
        on_device,
        mesh=mesh,
        in_specs=(
            P("seq", "head"),
            P("seq", "head"),
            P("seq"),
            P(),
            P("seq", "head"),
            P("seq", "head"),
            P("seq", "head"),
            P("head", "seq"),
            P("seq", "head"),
            P("seq", "head"),
            P("seq", "head"),
            P("seq"),
        ),
        out_specs=P("seq", "head"),
        check_vma=False,
    )
```

profile of v0, /device:TPU:8, one launch (start us, length us, event | category | flops | bytes accessed | tf_op | source)
XLA Modules:
  0.0 934.7 jit_solution(1580203487817966158)
XLA Ops:
  6.5 0.7 all-gather.11.cloned.1.call-update
  7.3 1.2 dynamic-slice
  9.2 0.7 dynamic_slice.3
  9.9 0.8 dynamic-update-slice
  10.8 13.6 %all-reduce = s32[512]{0:T(512)S(1)} all-reduce(s32[512]{0:T(512)S(1)} %dynamic-update-slice), channel_id=1, replica_groups=mesh['seq'=16,'head'=2] {'seq'}, use_global_device_ids=true, to_apply=%add | all-reduce | flops 512 | bytes 4096
  24.4 0.9 fusion.40
  25.3 0.2 convert_reduce_fusion
  25.4 46.7 %all-gather.11.cloned.1.call-done = bf16[512,2048]{1,0:T(8,128)(2,1)} async-done(((bf16[32,2048]{1,0:T(8,128)(2,1)}), bf16[512,2048]{1,0:T(8,128)(2,1)}) %all-gather.11.cloned.1.call-update) | async-done | bytes 2097168 | tf_op jit(solution)/shard_map/all_gather | solution.py:76
  72.1 2.3 multiply_reduce_fusion.1
  74.4 2.5 all-reduce.1
  76.9 1.0 multiply_convert_fusion
  77.9 0.0 all-gather.21.cloned.1.call-start
  77.9 0.7 all-gather.21.cloned.1.call-update
  78.7 0.5 all-gather.17.cloned.1.call-update
  79.2 0.7 fusion.62
  80.0 0.1 fusion.50
  80.1 0.8 fusion.42
  80.9 1.8 all_gather.39
  82.8 3.2 all-gather.13.cloned.1.call-done
  85.9 1.3 constant_dynamic-update-slice_fusion.1
  87.2 78.5 %all-gather.21.cloned.1.call-done = bf16[4096,512]{1,0:T(8,128)(2,1)} async-done(((bf16[256,512]{1,0:T(8,128)(2,1)}), bf16[4096,512]{1,0:T(8,128)(2,1)}) %all-gather.21.cloned.1.call-update) | async-done | bytes 4194320 | tf_op jit(solution)/shard_map/all_gather | solution.py:104
  165.7 3.0 convolution_convert_fusion.1
  168.7 0.9 fusion.30
  169.6 0.0 all-gather.19.cloned.1.call-start
  169.7 0.1 multiply_cosine_fusion.1
  169.8 73.3 %all-gather.17.cloned.1.call-done = bf16[4096,512]{1,0:T(8,128)(2,1)} async-done(((bf16[256,512]{1,0:T(8,128)(2,1)}), bf16[4096,512]{1,0:T(8,128)(2,1)}) %all-gather.17.cloned.1.call-update) | async-done | bytes 4194320 | tf_op jit(solution)/shard_map/all_gather | solution.py:103
  243.1 3.0 fusion.63
  246.0 0.1 subtract_convert_fusion.2
  246.1 0.9 fusion.29
  247.0 0.0 all-gather.27.cloned.1.call-start
  247.1 0.7 slice.57
  247.8 0.0 all-gather.15.cloned.1.call-start
  247.9 0.7 all-gather.15.cloned.1.call-update
  248.6 0.3 multiply_cosine_fusion
  249.0 0.1 reshape.184
  249.1 0.3 subtract_convert_fusion.1
  249.3 0.2 pad_maximum_fusion
  249.5 0.8 copy.29
  250.3 0.0 all-gather.29.cloned.1.call-start
  250.4 0.5 all-gather.29.cloned.1.call-update
  250.9 0.2 reduce-scatter.2.cloned.1.call-start
  251.2 0.2 iota_compare_fusion
  251.4 47.3 %all-gather.23.cloned.1.call-done = bf16[1024,512]{1,0:T(8,128)(2,1)} async-done(((bf16[64,512]{1,0:T(8,128)(2,1)}), bf16[1024,512]{1,0:T(8,128)(2,1)}) %all-gather.23.cloned.1.call-update) | async-done | bytes 1048592 | tf_op jit(solution)/shard_map/all_gather | solution.py:150
  298.7 2.3 copy.38
  300.9 54.5 %all-gather.19.cloned.1.call-done = bf16[1024,512]{1,0:T(8,128)(2,1)} async-done(((bf16[64,512]{1,0:T(8,128)(2,1)}), bf16[1024,512]{1,0:T(8,128)(2,1)}) %all-gather.19.cloned.1.call-update) | async-done | bytes 1048592 | tf_op jit(solution)/shard_map/all_gather | solution.py:149
  355.4 2.2 reshape.182
  357.6 61.1 %all-gather.27.cloned.1.call-done = bf16[2048,512]{1,0:T(8,128)(2,1)} async-done(((bf16[128,512]{1,0:T(8,128)(2,1)}), bf16[2048,512]{1,0:T(8,128)(2,1)}) %all-gather.27.cloned.1.call-update) | async-done | bytes 2097168 | tf_op jit(solution)/shard_map/all_gather | solution.py:156
  418.7 4.0 copy.41
  422.6 187.2 %all-gather.15.cloned.1.call-done = bf16[4096,2048]{1,0:T(8,128)(2,1)} async-done(((bf16[256,2048]{1,0:T(8,128)(2,1)}), bf16[4096,2048]{1,0:T(8,128)(2,1)}) %all-gather.15.cloned.1.call-update) | async-done | bytes 16777232 | tf_op jit(solution)/shard_map/all_gather | solution.py:102
  609.8 8.2 convolution_bitcast_fusion
  618.0 0.2 copy.42
  618.2 0.5 subtract_convert_fusion
  618.8 0.1 copy.26
  618.9 0.1 copy.25
  619.1 4.6 multiply_reduce_fusion
  623.6 50.4 %all-gather.25.cloned.1.call-done = bf16[2048,512]{0,1:T(8,128)(2,1)} async-done(((bf16[128,512]{0,1:T(8,128)(2,1)}), bf16[2048,512]{0,1:T(8,128)(2,1)}) %all-gather.25.cloned.1.call-update) | async-done | bytes 2097168 | tf_op jit(solution)/shard_map/all_gather | solution.py:155
  674.0 5.1 fusion
  679.2 1.8 fusion.6
  680.9 5.0 fusion.1
  685.9 2.8 fusion.26
  688.8 5.9 divide_convert_fusion
  694.7 214.2 %all-gather.29.cloned.1.call-done = bf16[2048,4096]{1,0:T(8,128)(2,1)} async-done(((bf16[2048,256]{1,0:T(8,128)(2,1)}), bf16[2048,4096]{1,0:T(8,128)(2,1)}) %all-gather.29.cloned.1.call-update) | async-done | bytes 16777232 | tf_op jit(solution)/shard_map/all_gather | solution.py:168
  908.9 9.1 convolution_convert_fusion
  918.1 10.1 %reduce-scatter.2.cloned.1.call-done = bf16[128,2048]{1,0:T(8,128)(2,1)} async-done(((bf16[128,4096]{1,0:T(8,128)(2,1)}), bf16[128,2048]{1,0:T(8,128)(2,1)}) %reduce-scatter.2.cloned.1.call-update) | async-done | bytes 524304 | tf_op jit(solution)/shard_map/reduce_scatter | solution.py:171
  (33 shorter events, 0.4 us)
Async XLA Ops:
  6.5 162.2 %copy-start.4 = (bf16[64,512]{1,0:T(8,128)(2,1)S(1)}, bf16[64,512]{1,0:T(8,128)(2,1)}, u32[]{:S(2)}) copy-start(bf16[64,512]{1,0:T(8,128)(2,1)} %param.21) | copy-start | bytes 196612
  6.5 65.6 %all-gather.11.cloned.1.call-start = ((), (), s32[]{:S(2)}) async-start(), calls=%async_computation.1 | async-start | bytes 2228224 | tf_op jit(solution)/shard_map/all_gather | solution.py:76
  7.3 78.7 %all-gather.13.cloned.1.call-start = ((), (), s32[]{:S(2)}) async-start(), calls=%async_computation.2 | async-start | bytes 1572864 | tf_op jit(solution)/shard_map/all_gather | solution.py:95
  74.4 171.7 %copy-start.3 = (bf16[64,512]{1,0:T(8,128)(2,1)S(1)}, bf16[64,512]{1,0:T(8,128)(2,1)}, u32[]{:S(2)}) copy-start(bf16[64,512]{1,0:T(8,128)(2,1)} %param.20) | copy-start | bytes 196612
  77.9 87.9 %all-gather.21.cloned.1.call-start = ((), (), s32[]{:S(2)}) async-start(), calls=%async_computation.6 | async-start | bytes 4456448 | tf_op jit(solution)/shard_map/all_gather | solution.py:104
  78.6 164.5 %all-gather.17.cloned.1.call-start = ((), (), s32[]{:S(2)}) async-start(), calls=%async_computation.4 | async-start | bytes 4456448 | tf_op jit(solution)/shard_map/all_gather | solution.py:103
  79.2 219.5 %all-gather.23.cloned.1.call-start = ((), (), s32[]{:S(2)}) async-start(), calls=%async_computation.7 | async-start | bytes 1114112 | tf_op jit(solution)/shard_map/all_gather | solution.py:150
  169.6 185.7 %all-gather.19.cloned.1.call-start = ((), (), s32[]{:S(2)}) async-start(), calls=%async_computation.5 | async-start | bytes 1114112 | tf_op jit(solution)/shard_map/all_gather | solution.py:149
  247.0 171.6 %all-gather.27.cloned.1.call-start = ((), (), s32[]{:S(2)}) async-start(), calls=%async_computation.9 | async-start | bytes 2228224 | tf_op jit(solution)/shard_map/all_gather | solution.py:156
  247.8 362.0 %all-gather.15.cloned.1.call-start = ((), (), s32[]{:S(2)}) async-start(), calls=%async_computation.3 | async-start | bytes 17825792 | tf_op jit(solution)/shard_map/all_gather | solution.py:102
  248.6 425.5 %all-gather.25.cloned.1.call-start = ((), (), s32[]{:S(2)}) async-start(), calls=%async_computation.8 | async-start | bytes 2228224 | tf_op jit(solution)/shard_map/all_gather | solution.py:155
  250.3 658.6 %all-gather.29.cloned.1.call-start = ((), (), s32[]{:S(2)}) async-start(), calls=%async_computation.10 | async-start | bytes 17825792 | tf_op jit(solution)/shard_map/all_gather | solution.py:168
  250.9 677.3 %reduce-scatter.2.cloned.1.call-start = ((), (), s32[]{:S(2)}) async-start(), calls=%async_computation.11 | async-start | bytes 1572864 | tf_op jit(solution)/shard_map/reduce_scatter | solution.py:171
  609.8 9.2 copy-start.2
  674.0 5.1 copy-start
  680.9 5.0 copy-start.1
Sparse Core Ops, SparseCore 0:
  10.1 61.9 all-gather.10
  78.0 7.8 all-gather.12
  88.7 76.9 all-gather.20
  168.4 74.6 all-gather.16
  245.7 52.9 all-gather.22
  301.3 54.0 all-gather.18
  358.1 60.4 all-gather.26
  421.4 188.3 all-gather.14
  612.6 61.4 all-gather.24
  676.6 232.2 all-gather.28
  918.2 9.9 reduce-scatter.1
where the time goes:
time: 937 us; the launch traced here: 935 us
  waiting for transfers between devices  830 us (89%)
  matrix products  45.7 us (5%)
  blocking collectives  17.9 us (2%)
  local copies, waits for them, and re-layouts  14.5 us (2%)
  between operations  14.1 us (2%)
  other arithmetic  12.2 us (1%)
    all_gather x1, waiting for transfers between devices, on_device(): lax.all_gather(w_out, 'seq', axis=1, tiled=True)  214 us
    all_gather x1, waiting for transfers between devices, on_device(): lax.all_gather(w_query, 'seq', axis=0, tiled=True)  187 us
    all_gather x1, waiting for transfers between devices, on_device(): lax.all_gather(w_value, 'seq', axis=0, tiled=True)  78.5 us
    all_gather x1, waiting for transfers between devices, on_device(): lax.all_gather(w_key, 'seq', axis=0, tiled=True)  73.3 us
    all_gather x1, waiting for transfers between devices, on_device(): lax.all_gather(values_new, 'seq', axis=0, tiled=True)  61.1 us
    all_gather x1, waiting for transfers between devices, on_device(): lax.all_gather(cache_k, 'seq', axis=0, tiled=True)  54.5 us
    all_gather x1, waiting for transfers between devices, on_device(): lax.all_gather(rot_key, 'seq', axis=0, tiled=True)  50.4 us
    all_gather x1, waiting for transfers between devices, on_device(): lax.all_gather(cache_v, 'seq', axis=0, tiled=True)  47.3 us
  transfers between devices with their start and end apart: 11, of which 11 were waited for; matrix products, arithmetic and copies ran while one was open for 6% of the time, Pallas kernels for 0%

commit v1 on v0

--- a/solution.py
+++ b/solution.py
@@ -1,6 +1,8 @@
 import jax
 import jax.numpy as jnp
 from jax import lax
+from jax.experimental import pallas as pl
+from jax.experimental.pallas import tpu as pltpu
 from jax.sharding import PartitionSpec as P
 
 D = 4096
@@ -173,24 +175,355 @@
     )
 
 
+LEVELS = 4
+PLANE = 4
+REC_PAD = 16
+TILE_RUN = 256
+
+
+def permuted(value, move):
+    perm = []
+    for level in range(LEVELS):
+        for place in range(PLANE):
+            for core in range(2):
+                target = move(level, place, core)
+                if target is not None:
+                    to_level, to_place, to_core = target
+                    perm.append(
+                        (
+                            (level * PLANE + place) * 2 + core,
+                            (to_level * PLANE + to_place) * 2 + to_core,
+                        )
+                    )
+    return lax.ppermute(value, ("seq", "head"), perm)
+
+
+def up(value, steps):
+    return permuted(value, lambda z, p, c: ((z + steps) % LEVELS, p, c))
+
+
+def other_core(value):
+    return permuted(value, lambda z, p, c: (z, p, 1 - c))
+
+
+def in_plane(piece):
+    near = permuted(piece, lambda z, p, c: (z, p ^ (1 + c), c))
+    far = permuted(piece, lambda z, p, c: (z, p ^ (2 - c), c))
+    both = permuted(near, lambda z, p, c: (z, p ^ (2 - c), c))
+    return [piece, near, far, both]
+
+
+def place_of(which, place, core):
+    if which == 0:
+        return place
+    if which == 3:
+        return place ^ 3
+    return place ^ (1 + core) if which == 1 else place ^ (2 - core)
+
+
+def project_kernel(where_ref, *refs):
+    acts = refs[:8]
+    weights = refs[8:24]
+    caches = refs[24:28]
+    cos_ref, sin_ref, query_ref, kv_ref, x_ref = refs[28:]
+    level, place, core = where_ref[0], where_ref[1], where_ref[2]
+    rows = acts[0].shape[0]
+    depth = weights[0].shape[0]
+    width = acts[0].shape[1]
+    tok = rows - REC_PAD
+    mine = pl.multiple_of(core * width, width)
+    others = pl.multiple_of((1 - core) * width, width)
+    for k in range(LEVELS):
+        x_ref[k * rows : (k + 1) * rows, pl.ds(mine, width)] = acts[2 * k][...]
+        x_ref[k * rows : (k + 1) * rows, pl.ds(others, width)] = acts[2 * k + 1][...]
+    total = None
+    for d in range(LEVELS):
+        from_level = lax.rem(level + LEVELS - d, LEVELS)
+        for j in range(PLANE):
+            block = from_level * PLANE + place_of(j, place, core)
+            start = pl.multiple_of(block * depth, depth)
+            part = jnp.dot(
+                x_ref[:, pl.ds(start, depth)],
+                weights[d * PLANE + j][...],
+                preferred_element_type=jnp.float32,
+            )
+            total = part if total is None else total + part
+    for k in range(LEVELS):
+        at = lax.rem(level + LEVELS - k, LEVELS)
+        block = total[k * rows : (k + 1) * rows]
+        cosine = cos_ref[at]
+        sine = sin_ref[at]
+
+        def turned(values, cosine, sine):
+            return values * cosine + pltpu.roll(values, HD // 2, 1) * sine
+
+        for h in range(4):
+            head = turned(block[:tok, h * HD : (h + 1) * HD], cosine[:tok], sine[:tok])
+            query_ref[at, h] = head.astype(jnp.bfloat16)
+        keys = turned(block[:, 4 * HD : 5 * HD], cosine, sine)
+        values = block[:, 5 * HD : 6 * HD]
+        both = jnp.concatenate([keys, values], axis=1)
+        kv_ref[LEVELS * 64 // 128 + at] = both[:tok].astype(jnp.bfloat16)
+        cached = caches[k][0:64, :].astype(jnp.float32)
+        slots = caches[k][64:80, :].astype(jnp.int32)
+        row = lax.broadcasted_iota(jnp.int32, cached.shape, 0)
+        for r in range(8):
+            cached = jnp.where(row == slots[r : r + 1], both[tok + r : tok + r + 1], cached)
+        half = lax.rem(at, 2)
+        kv_ref[at // 2, pl.ds(pl.multiple_of(half * 64, 64), 64)] = cached.astype(jnp.bfloat16)
+
+
+def attend_kernel(where_ref, query_ref, kv0, kv1, kv2, kv3, out_ref):
+    place, core = where_ref[1], where_ref[2]
+    pieces = (kv0, kv1, kv2, kv3)
+    tok = query_ref.shape[2]
+    old = LEVELS // 2
+    row = lax.broadcasted_iota(jnp.int32, (tok, tok), 0)
+    col = lax.broadcasted_iota(jnp.int32, (tok, tok), 1)
+    scale = HD ** (-0.5) * 1.4426950408889634
+    for i in range(LEVELS):
+        count = (old + i + 1) * tok
+        queries = query_ref[i].reshape(4 * tok, HD)
+        scores = []
+        best = None
+        for j in range(PLANE):
+            theirs = place_of(j, place, core)
+            keys = pieces[j][0 : old + i + 1, :, 0:HD].reshape(count, HD)
+            raw = lax.dot_general(
+                queries, keys, (((1,), (1,)), ((), ())), preferred_element_type=jnp.float32
+            )
+            if j == 0:
+                allowed = col <= row
+            else:
+                allowed = jnp.broadcast_to(theirs, (tok, tok)) < place
+            allowed = jnp.concatenate([allowed] * 4, axis=0)
+            last = jnp.where(allowed, raw[:, count - tok :], NEG_FILL)
+            raw = jnp.concatenate([raw[:, : count - tok], last], axis=1)
+            top = jnp.max(raw, axis=1, keepdims=True)
+            best = top if best is None else jnp.maximum(best, top)
+            scores.append(raw)
+        total, accum = 0.0, 0.0
+        for j in range(PLANE):
+            weights = jnp.exp2((scores[j] - best) * scale)
+            total = total + jnp.sum(weights, axis=1, keepdims=True)
+            values = pieces[j][0 : old + i + 1, :, HD : 2 * HD].reshape(count, HD)
+            accum = accum + jnp.dot(
+                weights.astype(jnp.bfloat16), values, preferred_element_type=jnp.float32
+            )
+        result = (accum / total).astype(jnp.bfloat16)
+        for h in range(4):
+            out_ref[i * tok : (i + 1) * tok, h * HD : (h + 1) * HD] = result[
+                h * tok : (h + 1) * tok
+            ]
+
+
+def output_kernel(where_ref, attended_ref, *refs):
+    weights = refs[:16]
+    mine_ref, other_ref = refs[16:]
+    level, place, core = where_ref[0], where_ref[1], where_ref[2]
+    width = weights[0].shape[1]
+    half = LEVELS * PLANE // 2
+    for d in range(LEVELS):
+        from_level = lax.rem(level + LEVELS - d, LEVELS)
+        for j in range(PLANE):
+            block = from_level * PLANE + place_of(j, place, core)
+            start = pl.multiple_of(lax.rem(block, half) * width, width)
+            part = jnp.dot(
+                attended_ref[...], weights[d * PLANE + j][...], preferred_element_type=jnp.float32
+            )
+
+            @pl.when(block // half == core)
+            def _():
+                mine_ref[:, pl.ds(start, width)] = part
+
+            @pl.when(block // half != core)
+            def _():
+                other_ref[:, pl.ds(start, width)] = part.astype(jnp.bfloat16)
+
+
+SMEM = pl.BlockSpec(memory_space=pltpu.SMEM)
+VMEM = pl.BlockSpec(memory_space=pltpu.VMEM)
+PARAMS = pltpu.CompilerParams(vmem_limit_bytes=48 * 1024 * 1024)
+
+
+def by_levels(
+    text_rows,
+    picture_rows,
+    picture_slots,
+    norm_gain,
+    w_query,
+    w_key,
+    w_value,
+    w_out,
+    cache_keys,
+    cache_values,
+    recompute_rows,
+    recompute_slots,
+):
+    seq_index = lax.axis_index("seq")
+    core = lax.axis_index("head")
+    level, place = seq_index // PLANE, seq_index % PLANE
+    where = jnp.stack([level, place, core]).astype(jnp.int32)
+    tok, width = text_rows.shape
+    rec = recompute_rows.shape[0]
+    cache_rows = cache_keys.shape[0]
+    depth = w_query.shape[0]
+
+    def group_of(level_at):
+        q = lax.dynamic_slice_in_dim(w_query, level_at * 4 * HD, 4 * HD, 1)
+        k = lax.dynamic_slice_in_dim(w_key, level_at * HD, HD, 1)
+        v = lax.dynamic_slice_in_dim(w_value, level_at * HD, HD, 1)
+        return jnp.concatenate([q, k, v], axis=1)
+
+    local_slots = (recompute_slots - seq_index * cache_rows).astype(jnp.bfloat16)
+    slot_rows = jnp.broadcast_to(
+        jnp.pad(local_slots, (0, REC_PAD - rec))[:, None], (REC_PAD, 2 * HD)
+    )
+
+    def cache_of(level_at):
+        k = lax.dynamic_slice_in_dim(cache_keys, level_at * HD, HD, 1)
+        v = lax.dynamic_slice_in_dim(cache_values, level_at * HD, HD, 1)
+        return jnp.concatenate([jnp.concatenate([k, v], axis=1), slot_rows], axis=0)
+
+    def out_of(level_at):
+        return lax.dynamic_slice_in_dim(w_out, level_at * 4 * HD, 4 * HD, 0)
+
+    weights, caches = [], []
+    for d in range(LEVELS):
+        to_level = (level + d) % LEVELS
+        piece, cached = group_of(to_level), cache_of(to_level)
+        if d:
+            piece, cached = up(piece, d), up(cached, d)
+        caches.append(cached)
+        weights += in_plane(piece)
+
+    stream_len = tok * LEVELS * PLANE
+    tile_owners = TILE_RUN // tok
+    first = stream_len // 2 // tok
+    last = (stream_len - TILE_RUN) // tok
+    owners = [first + i for i in range(tile_owners)] + [last + i for i in range(tile_owners)]
+    senders = tok // picture_rows.shape[0]
+    received = []
+    for k in range(senders):
+        perm = [
+            ((i * senders + k) * 2 + c, owner * 2 + c)
+            for i, owner in enumerate(owners)
+            for c in range(2)
+        ]
+        received.append(lax.ppermute(picture_rows, ("seq", "head"), perm))
+    placed = jnp.concatenate(received, axis=0)
+    is_owner = jnp.any(seq_index == jnp.array(owners, jnp.int32))
+    stream = jnp.where(is_owner, placed, text_rows)
+
+    rows = jnp.concatenate(
+        [stream, recompute_rows, jnp.zeros((REC_PAD - rec, width), stream.dtype)], axis=0
+    )
+    wide = rows.astype(jnp.float32)
+    squares = jnp.sum(wide * wide, axis=1)
+    squares = squares + other_core(squares)
+    gain = lax.dynamic_slice_in_dim(norm_gain, core * width, width, 0)
+    normed = scaled(wide, squares, gain)
+
+    acts, held = [], normed
+    for k in range(LEVELS):
+        if k:
+            held = up(held, 1)
+        acts += [held, other_core(held)]
+
+    half = HD // 2
+    freqs = ROPE_BASE ** (-jnp.arange(half, dtype=jnp.float32) / half)
+    level_start = (jnp.arange(LEVELS, dtype=jnp.int32) * PLANE + place)[:, None]
+    stream_pos = (
+        cache_rows * LEVELS * PLANE + level_start * tok + jnp.arange(tok, dtype=jnp.int32)[None]
+    ).astype(jnp.float32)
+    order = (level - jnp.arange(LEVELS, dtype=jnp.int32)) % LEVELS
+    slots = jnp.stack([c[cache_rows:, 0] for c in caches])[order].astype(jnp.float32)
+    rec_pos = slots + (level_start * cache_rows).astype(jnp.float32)
+    positions = jnp.concatenate([stream_pos, rec_pos], axis=1)
+    angles = positions[..., None] * freqs
+    cosine, sine = jnp.cos(angles), jnp.sin(angles)
+    cosine = jnp.concatenate([cosine, cosine], axis=-1)
+    sine = jnp.concatenate([-sine, sine], axis=-1)
+
+    blocks = LEVELS * cache_rows // tok + LEVELS
+    query, kv = pl.pallas_call(
+        project_kernel,
+        out_shape=(
+            jax.ShapeDtypeStruct((LEVELS, 4, tok, HD), jnp.bfloat16),
+            jax.ShapeDtypeStruct((blocks, tok, 2 * HD), jnp.bfloat16),
+        ),
+        in_specs=[SMEM] + [VMEM] * 30,
+        out_specs=(VMEM, VMEM),
+        scratch_shapes=[pltpu.VMEM((LEVELS * (tok + REC_PAD), 2 * width), jnp.bfloat16)],
+        compiler_params=PARAMS,
+        name="project",
+    )(where, *acts, *weights, *caches, cosine, sine)
+
+    attended = pl.pallas_call(
+        attend_kernel,
+        out_shape=jax.ShapeDtypeStruct((LEVELS * tok, 4 * HD), jnp.bfloat16),
+        in_specs=[SMEM] + [VMEM] * 5,
+        out_specs=VMEM,
+        compiler_params=PARAMS,
+        name="attend",
+    )(where, query, *in_plane(kv))
+
+    out_weights = []
+    for d in range(LEVELS):
+        piece = out_of((level + d) % LEVELS)
+        if d:
+            piece = up(piece, d)
+        out_weights += in_plane(piece)
+    mine, other = pl.pallas_call(
+        output_kernel,
+        out_shape=(
+            jax.ShapeDtypeStruct((LEVELS * tok, width), jnp.float32),
+            jax.ShapeDtypeStruct((LEVELS * tok, width), jnp.bfloat16),
+        ),
+        in_specs=[SMEM] + [VMEM] * 17,
+        out_specs=(VMEM, VMEM),
+        compiler_params=PARAMS,
+        name="output",
+    )(where, attended, *out_weights)
+    summed = (mine + other_core(other).astype(jnp.float32)).reshape(LEVELS, tok, width)
+    result = lax.dynamic_index_in_dim(summed, level, 0, keepdims=False)
+    for d in range(1, LEVELS):
+        block = lax.dynamic_index_in_dim(summed, (level + d) % LEVELS, 0, keepdims=False)
+        result = result + up(block.astype(jnp.bfloat16), d).astype(jnp.float32)
+    return result.astype(jnp.bfloat16)
+
+
 def solution(mesh):
-    return jax.shard_map(
-        on_device,
-        mesh=mesh,
-        in_specs=(
-            P("seq", "head"),
-            P("seq", "head"),
-            P("seq"),
-            P(),
-            P("seq", "head"),
-            P("seq", "head"),
-            P("seq", "head"),
-            P("head", "seq"),
-            P("seq", "head"),
-            P("seq", "head"),
-            P("seq", "head"),
-            P("seq"),
-        ),
-        out_specs=P("seq", "head"),
-        check_vma=False,
-    )
+    def run(*args):
+        kv_local = args[5].shape[1] // HD // mesh.shape["head"]
+        levels_fit = (
+            mesh.shape["seq"] == LEVELS * PLANE
+            and mesh.shape["head"] == 2
+            and kv_local == LEVELS
+            and args[1].shape[0] == 2 * TILE_RUN
+            and args[0].shape[0] == 2048
+            and args[8].shape[0] == 1024
+            and args[10].shape[0] == 128
+        )
+        return jax.shard_map(
+            by_levels if levels_fit else on_device,
+            mesh=mesh,
+            in_specs=(
+                P("seq", "head"),
+                P("seq", "head"),
+                P("seq"),
+                P(),
+                P("seq", "head"),
+                P("seq", "head"),
+                P("seq", "head"),
+                P("head", "seq"),
+                P("seq", "head"),
+                P("seq", "head"),
+                P("seq", "head"),
+                P("seq"),
+            ),
+            out_specs=P("seq", "head"),
+            check_vma=False,
+        )(*args)
+
+    return run

time: 937 us -> 263 us (0.28)
  waiting for transfers between devices: 830 us -> 145 us
  starting transfers between devices: 0.58 us -> 58 us
  matrix products: 45.7 us -> 0 us
  Pallas kernels: 0 us -> 27.3 us
  blocking collectives: 17.9 us -> 0 us
  between operations: 14.1 us -> 0.47 us
    all_gather x10 -> x0, waiting for transfers between devices: 816 us -> none  [the longest x1 214 us: on_device(): lax.all_gather(w_out, 'seq', axis=1, tiled=True)]
    ppermute x0 -> x52, waiting for transfers between devices: none -> 145 us  [the longest x48 145 us: permuted(): return lax.ppermute(value, ('seq', 'head'), perm)]
    ppermute x0 -> x52, starting transfers between devices: none -> 58 us  [the longest x48 47.8 us: permuted(): return lax.ppermute(value, ('seq', 'head'), perm)]
    dot_general x11 -> x0, matrix products: 45.7 us -> none  [the longest x2 9.65 us: attend(): jnp.einsum('kgtd,nkd->kgtn', queries, keys_split, preferred_element_type=...]
    pallas_call x0 -> x3, Pallas kernels: none -> 27.3 us  [the longest x1 10.4 us: by_levels(): pl.pallas_call(output_kernel, out_shape=(jax.ShapeDtypeStruct((LEVELS * t...]
    unnamed x1 -> x0, blocking collectives: 13.6 us -> none
    reduce_scatter x1 -> x0, waiting for transfers between devices: 10.1 us -> none  [on_device(): lax.psum_scatter(partial_out.astype(jnp.bfloat16), 'head', scatter_dimens...]
  transfers between devices with their start and end apart: 11 -> 52, of which waited for: 11 -> 22; matrix products, arithmetic and copies ran while one was open for 6% -> 6% of each run, Pallas kernels for 0% -> 7%
where the time goes in v1:
time: 263 us; the launch traced here: 258 us
  waiting for transfers between devices  145 us (55%)
  starting transfers between devices  58 us (22%)
  Pallas kernels  27.3 us (10%)
  other arithmetic  15.4 us (6%)
  local copies, waits for them, and re-layouts  11.2 us (4%)
    ppermute x48, waiting for transfers between devices, permuted(): return lax.ppermute(value, ('seq', 'head'), perm)  145 us
    ppermute x48, starting transfers between devices, permuted(): return lax.ppermute(value, ('seq', 'head'), perm)  47.8 us
    pallas_call x1, Pallas kernels, by_levels(): pl.pallas_call(output_kernel, out_shape=(jax.ShapeDtypeStruct((LEVELS * t...  10.4 us
    ppermute x4, starting transfers between devices, by_levels(): received.append(lax.ppermute(picture_rows, ('seq', 'head'), perm))  10.2 us
    pallas_call x1, Pallas kernels, by_levels(): pl.pallas_call(attend_kernel, out_shape=jax.ShapeDtypeStruct((LEVELS * to...  8.5 us
    pallas_call x1, Pallas kernels, by_levels(): pl.pallas_call(project_kernel, out_shape=(jax.ShapeDtypeStruct((LEVELS, 4...  8.37 us
  transfers between devices with their start and end apart: 52, of which 22 were waited for; matrix products, arithmetic and copies ran while one was open for 6% of the time, Pallas kernels for 7%

profile of v1, /device:TPU:8, one launch (start us, length us, event | category | flops | bytes accessed | tf_op | source)
XLA Modules:
  0.0 257.5 jit_solution(9306997817121646451)
XLA Ops:
  0.7 8.2 %collective-permute-start = (bf16[32,2048]{1,0:T(8,128)(2,1)}, bf16[32,2048]{1,0:T(8,128)(2,1)S(1)}, u32[]{:S(2)}, u32[]{:S(2)}) collective-permute-start(bf16[32,2048]{1,0:T(8,128)(2,1)} %param.14), channel_id=1, source_target_pairs={{0,16},{1,17},{8,18},{9,19},{16,28},{17,29},{24,30},{25,31}} | collective-permute-start | bytes 393224 | tf_op jit(solution)/shard_map/ppermute | solution.py:413
  11.6 0.8 constant_dynamic-slice_fusion.4
  12.5 0.7 maximum_maximum_fusion.4
  13.2 1.3 constant_dynamic-slice_fusion.14
  15.4 0.7 constant_dynamic-slice_fusion.12
  16.1 2.0 collective-permute-start.27
  18.2 0.7 maximum_select_fusion
  19.3 1.3 collective-permute-start.19
  21.4 2.0 fusion.2.refs_0_
  23.4 1.5 collective-permute-start.6
  24.9 0.8 pad_maximum_fusion.1
  26.4 0.9 constant_dynamic-slice_fusion
  27.3 0.8 pad_maximum_fusion.3
  28.2 2.2 collective-permute-start.28
  30.4 30.5 %collective-permute-done.28.refs_26_ = bf16[80,256]{1,0:T(8,128)(2,1)} collective-permute-done((bf16[80,256]{1,0:T(8,128)(2,1)S(1)}, bf16[80,256]{1,0:T(8,128)(2,1)}, u32[]{:S(2)}, u32[]{:S(2)}) %collective-permute-start.28) | collective-permute-done | bytes 40992 | tf_op jit(solution)/shard_map/ppermute | solution.py:198
  60.9 2.4 collective-permute-start.13
  63.6 1.7 collective-permute-start.8
  65.3 2.1 collective-permute-start.23
  68.0 4.6 %collective-permute-done.13.refs_10_ = bf16[256,768]{1,0:T(8,128)(2,1)S(1)} collective-permute-done((bf16[256,768]{1,0:T(8,128)(2,1)S(1)}, bf16[256,768]{1,0:T(8,128)(2,1)S(1)}, u32[]{:S(2)}, u32[]{:S(2)}) %collective-permute-start.13) | collective-permute-done | bytes 393248 | tf_op jit(solution)/shard_map/ppermute | solution.py:198
  72.6 1.7 collective-permute-start.21
  75.1 14.0 %collective-permute-done.23.refs_20_ = bf16[256,768]{1,0:T(8,128)(2,1)} collective-permute-done((bf16[256,768]{1,0:T(8,128)(2,1)}, bf16[256,768]{1,0:T(8,128)(2,1)}, u32[]{:S(2)}, u32[]{:S(2)}) %collective-permute-start.23) | collective-permute-done | bytes 393248 | tf_op jit(solution)/shard_map/ppermute | solution.py:198
  89.5 1.7 collective-permute-start.16
  91.3 1.7 collective-permute-start.10
  93.2 1.8 collective-permute-start.14
  95.3 0.8 slice_reduce_fusion.1
  96.1 5.0 %collective-permute-done.17.refs_14_ = bf16[256,768]{1,0:T(8,128)(2,1)S(1)} collective-permute-done((bf16[256,768]{1,0:T(8,128)(2,1)S(1)}, bf16[256,768]{1,0:T(8,128)(2,1)S(1)}, u32[]{:S(2)}, u32[]{:S(2)}) %collective-permute-start.17) | collective-permute-done | bytes 393248 | tf_op jit(solution)/shard_map/ppermute | solution.py:198
  101.6 0.7 copy-done.1
  102.3 1.7 collective-permute-start.22
  105.3 3.8 %collective-permute-done.14.refs_11_ = bf16[256,768]{1,0:T(8,128)(2,1)} collective-permute-done((bf16[256,768]{1,0:T(8,128)(2,1)S(1)}, bf16[256,768]{1,0:T(8,128)(2,1)}, u32[]{:S(2)}, u32[]{:S(2)}) %collective-permute-start.14) | collective-permute-done | bytes 393248 | tf_op jit(solution)/shard_map/ppermute | solution.py:198
  109.1 4.2 %collective-permute-done.25.refs_22_ = bf16[256,768]{1,0:T(8,128)(2,1)} collective-permute-done((bf16[256,768]{1,0:T(8,128)(2,1)}, bf16[256,768]{1,0:T(8,128)(2,1)}, u32[]{:S(2)}, u32[]{:S(2)}) %collective-permute-start.25) | collective-permute-done | bytes 393248 | tf_op jit(solution)/shard_map/ppermute | solution.py:198
  114.3 3.2 %collective-permute-done.22.refs_19_ = bf16[256,768]{1,0:T(8,128)(2,1)} collective-permute-done((bf16[256,768]{1,0:T(8,128)(2,1)S(1)}, bf16[256,768]{1,0:T(8,128)(2,1)}, u32[]{:S(2)}, u32[]{:S(2)}) %collective-permute-start.22) | collective-permute-done | bytes 393248 | tf_op jit(solution)/shard_map/ppermute | solution.py:198
  117.9 1.1 fusion.9
  119.3 2.6 %collective-permute-done.18.refs_15_ = bf16[256,768]{1,0:T(8,128)(2,1)S(1)} collective-permute-done((bf16[256,768]{1,0:T(8,128)(2,1)}, bf16[256,768]{1,0:T(8,128)(2,1)S(1)}, u32[]{:S(2)}, u32[]{:S(2)}) %collective-permute-start.18) | collective-permute-done | bytes 393248 | tf_op jit(solution)/shard_map/ppermute | solution.py:198
  122.1 4.0 %collective-permute-done.26.refs_23_ = bf16[256,768]{1,0:T(8,128)(2,1)S(1)} collective-permute-done((bf16[256,768]{1,0:T(8,128)(2,1)}, bf16[256,768]{1,0:T(8,128)(2,1)S(1)}, u32[]{:S(2)}, u32[]{:S(2)}) %collective-permute-start.26) | collective-permute-done | bytes 393248 | tf_op jit(solution)/shard_map/ppermute | solution.py:198
  126.1 1.0 collective-permute-start.36
  127.2 1.6 collective-permute-start.40
  128.8 0.8 copy-done.6
  129.8 8.4 %project.1 = (bf16[4,4,128,128]{3,2,1,0:T(8,128)(2,1)}, bf16[6,128,256]{2,1,0:T(8,128)(2,1)S(1)}) custom-call(s32[3]{0:T(128)S(1)} %pad_add_fusion.where_ref, bf16[144,2048]{1,0:T(8,128)(2,1)} %fusion.2.refs_0_, bf16[144,2048]{1,0:T(8,128)(2,1)} %collective-permute-done.5.refs_1_, bf16[144,2048]{1,0:T(8,128)(2,1)} %collective-permute-done.6.refs_2_, ...), custom_call_target="tpu_custom_call" | custom-call | tf_op jit(solution)/shard_map/project/pallas_call | solution.py:449
  138.2 2.0 collective-permute-start.30
  140.8 1.5 collective-permute-start.46
  142.3 3.7 %collective-permute-done.40.refs_8_ = bf16[512,256]{1,0:T(8,128)(2,1)S(1)} collective-permute-done((bf16[512,256]{1,0:T(8,128)(2,1)S(1)}, bf16[512,256]{1,0:T(8,128)(2,1)S(1)}, u32[]{:S(2)}, u32[]{:S(2)}) %collective-permute-start.40) | collective-permute-done | bytes 262176 | tf_op jit(solution)/shard_map/ppermute | solution.py:198
  146.0 1.1 collective-permute-start.45
  147.1 2.3 collective-permute-done.34.refs_2_
  150.2 1.2 collective-permute-start.32
  151.5 4.4 %collective-permute-done.33.refs_1_ = bf16[512,256]{1,0:T(8,128)(2,1)S(1)} collective-permute-done((bf16[512,256]{1,0:T(8,128)(2,1)S(1)}, bf16[512,256]{1,0:T(8,128)(2,1)S(1)}, u32[]{:S(2)}, u32[]{:S(2)}) %collective-permute-start.33) | collective-permute-done | bytes 262176 | tf_op jit(solution)/shard_map/ppermute | solution.py:198
  156.4 1.8 collective-permute-start.37
  158.2 3.3 %collective-permute-done.45.refs_13_ = bf16[512,256]{1,0:T(8,128)(2,1)S(1)} collective-permute-done((bf16[512,256]{1,0:T(8,128)(2,1)S(1)}, bf16[512,256]{1,0:T(8,128)(2,1)S(1)}, u32[]{:S(2)}, u32[]{:S(2)}) %collective-permute-start.45) | collective-permute-done | bytes 262176 | tf_op jit(solution)/shard_map/ppermute | solution.py:198
  161.5 2.0 collective-permute-start.41
  163.5 8.6 %collective-permute-done.38.refs_6_ = bf16[512,256]{1,0:T(8,128)(2,1)S(1)} collective-permute-done((bf16[512,256]{1,0:T(8,128)(2,1)S(1)}, bf16[512,256]{1,0:T(8,128)(2,1)S(1)}, u32[]{:S(2)}, u32[]{:S(2)}) %collective-permute-start.38) | collective-permute-done | bytes 262176 | tf_op jit(solution)/shard_map/ppermute | solution.py:198
  172.8 1.3 collective-permute-start.35
  174.9 1.3 collective-permute-start.39
  176.9 1.0 copy-done
  177.9 8.5 %attend.1.attended_ref = bf16[512,512]{1,0:T(8,128)(2,1)S(1)} custom-call(s32[3]{0:T(128)S(1)} %pad_add_fusion.where_ref, bf16[4,4,128,128]{3,2,1,0:T(8,128)(2,1)S(1)} %copy-done, bf16[6,128,256]{2,1,0:T(8,128)(2,1)S(1)} %get-tuple-element.10.kv0, bf16[6,128,256]{2,1,0:T(8,128)(2,1)S(1)} %collective-permute-done.30.kv1, ...), custom_call_target="tpu_custom_call" | custom-call | tf_op jit(solution)/shard_map/attend/pallas_call | solution.py:462
  186.9 2.8 %collective-permute-done.43.refs_11_ = bf16[512,256]{1,0:T(8,128)(2,1)S(1)} collective-permute-done((bf16[512,256]{1,0:T(8,128)(2,1)S(1)}, bf16[512,256]{1,0:T(8,128)(2,1)S(1)}, u32[]{:S(2)}, u32[]{:S(2)}) %collective-permute-start.43) | collective-permute-done | bytes 262176 | tf_op jit(solution)/shard_map/ppermute | solution.py:198
  189.7 10.4 %output.1 = (f32[512,2048]{1,0:T(8,128)}, bf16[512,2048]{1,0:T(8,128)(2,1)}) custom-call(s32[3]{0:T(128)S(1)} %pad_add_fusion.where_ref, bf16[512,512]{1,0:T(8,128)(2,1)S(1)} %attend.1.attended_ref, bf16[512,256]{1,0:T(8,128)(2,1)S(1)} %get-tuple-element.18.refs_0_, bf16[512,256]{1,0:T(8,128)(2,1)S(1)} %collective-permute-done.33.refs_1_, ...), custom_call_target="tpu_custom_call" | custom-call | tf_op jit(solution)/shard_map/output/pallas_call | solution.py:477
  200.1 4.4 %collective-permute-done.48 = bf16[512,2048]{1,0:T(8,128)(2,1)S(1)} collective-permute-done((bf16[512,2048]{1,0:T(8,128)(2,1)}, bf16[512,2048]{1,0:T(8,128)(2,1)S(1)}, u32[]{:S(2)}, u32[]{:S(2)}) %collective-permute-start.48) | collective-permute-done | bytes 2097184 | tf_op jit(solution)/shard_map/ppermute | solution.py:198
  204.5 2.8 %convert_add_fusion = f32[512,2048]{1,0:T(8,128)S(1)} fusion(f32[512,2048]{1,0:T(8,128)} %get-tuple-element.11, bf16[512,2048]{1,0:T(8,128)(2,1)S(1)} %collective-permute-done.48), kind=kLoop, calls=%fused_computation.1 | loop fusion | flops 2097152 | bytes 10485760 | tf_op jit(solution)/shard_map/add | solution.py:488
  207.3 2.0 copy-done.3
  210.0 1.5 collective-permute-start.51
  211.5 1.5 collective-permute-start.50
  213.0 11.3 %collective-permute-done.49 = bf16[128,2048]{1,0:T(8,128)(2,1)S(1)} collective-permute-done((bf16[128,2048]{1,0:T(8,128)(2,1)S(1)}, bf16[128,2048]{1,0:T(8,128)(2,1)S(1)}, u32[]{:S(2)}, u32[]{:S(2)}) %collective-permute-start.49) | collective-permute-done | bytes 524320 | tf_op jit(solution)/shard_map/ppermute | solution.py:198
  224.3 12.2 %collective-permute-done.51 = bf16[128,2048]{1,0:T(8,128)(2,1)S(1)} collective-permute-done((bf16[128,2048]{1,0:T(8,128)(2,1)S(1)}, bf16[128,2048]{1,0:T(8,128)(2,1)S(1)}, u32[]{:S(2)}, u32[]{:S(2)}) %collective-permute-start.51) | collective-permute-done | bytes 524320 | tf_op jit(solution)/shard_map/ppermute | solution.py:198
  236.5 18.7 %collective-permute-done.50 = bf16[128,2048]{1,0:T(8,128)(2,1)S(1)} collective-permute-done((bf16[128,2048]{1,0:T(8,128)(2,1)S(1)}, bf16[128,2048]{1,0:T(8,128)(2,1)S(1)}, u32[]{:S(2)}, u32[]{:S(2)}) %collective-permute-start.50) | collective-permute-done | bytes 524320 | tf_op jit(solution)/shard_map/ppermute | solution.py:198
  255.2 2.3 fusion.5
  (126 shorter events, 18.0 us)
Async XLA Ops:
  0.0 16.1 %collective-permute-start.1 = (bf16[32,2048]{1,0:T(8,128)(2,1)}, bf16[32,2048]{1,0:T(8,128)(2,1)S(1)}, u32[]{:S(2)}, u32[]{:S(2)}) collective-permute-start(bf16[32,2048]{1,0:T(8,128)(2,1)} %param.14), channel_id=1, source_target_pairs={{2,16},{3,17},{10,18},{11,19},{18,28},{19,29},{26,30},{27,31}} | collective-permute-start | bytes 393224 | tf_op jit(solution)/shard_map/ppermute | solution.py:413
  0.7 17.5 %collective-permute-start = (bf16[32,2048]{1,0:T(8,128)(2,1)}, bf16[32,2048]{1,0:T(8,128)(2,1)S(1)}, u32[]{:S(2)}, u32[]{:S(2)}) collective-permute-start(bf16[32,2048]{1,0:T(8,128)(2,1)} %param.14), channel_id=1, source_target_pairs={{0,16},{1,17},{8,18},{9,19},{16,28},{17,29},{24,30},{25,31}} | collective-permute-start | bytes 393224 | tf_op jit(solution)/shard_map/ppermute | solution.py:413
  8.8 9.3 %collective-permute-start.3 = (bf16[32,2048]{1,0:T(8,128)(2,1)}, bf16[32,2048]{1,0:T(8,128)(2,1)S(1)}, u32[]{:S(2)}, u32[]{:S(2)}) collective-permute-start(bf16[32,2048]{1,0:T(8,128)(2,1)} %param.14), channel_id=1, source_target_pairs={{6,16},{7,17},{14,18},{15,19},{22,28},{23,29},{30,30},{31,31}} | collective-permute-start | bytes 393224 | tf_op jit(solution)/shard_map/ppermute | solution.py:413
  9.5 8.6 %collective-permute-start.2 = (bf16[32,2048]{1,0:T(8,128)(2,1)}, bf16[32,2048]{1,0:T(8,128)(2,1)S(1)}, u32[]{:S(2)}, u32[]{:S(2)}) collective-permute-start(bf16[32,2048]{1,0:T(8,128)(2,1)} %param.14), channel_id=1, source_target_pairs={{4,16},{5,17},{12,18},{13,19},{20,28},{21,29},{28,30},{29,31}} | collective-permute-start | bytes 393224 | tf_op jit(solution)/shard_map/ppermute | solution.py:413
  12.5 2.9 %copy-start.15 = (bf16[256,512]{1,0:T(8,128)(2,1)S(1)}, bf16[256,512]{1,0:T(8,128)(2,1)}, u32[]{:S(2)}) copy-start(bf16[256,512]{1,0:T(8,128)(2,1)} %param.18) | copy-start | bytes 786436
  13.2 14.9 %collective-permute-start.29 = (bf16[80,256]{1,0:T(8,128)(2,1)}, bf16[80,256]{1,0:T(8,128)(2,1)S(1)}, u32[]{:S(2)}, u32[]{:S(2)}) collective-permute-start(bf16[80,256]{1,0:T(8,128)(2,1)} %get-tuple-element.45), channel_id=1, source_target_pairs={{0,24},{1,25},{2,26},{3,27},{4,28},{5,29},{6,30},{7,31},{8,0},{9,1... | collective-permute-start | bytes 122888 | tf_op jit(solution)/shard_map/ppermute | solution.py:198
  13.2 4.9 %copy-start.8 = (bf16[128,2048]{1,0:T(8,128)(2,1)S(1)}, bf16[128,2048]{1,0:T(8,128)(2,1)}, u32[]{:S(2)}) copy-start(bf16[128,2048]{1,0:T(8,128)(2,1)} %param.13) | copy-start | bytes 1572868
  15.4 3.6 %copy-start.17 = (bf16[8,2048]{1,0:T(8,128)(2,1)S(1)}, bf16[8,2048]{1,0:T(8,128)(2,1)}, u32[]{:S(2)}) copy-start(bf16[8,2048]{1,0:T(8,128)(2,1)} %param.22) | copy-start | bytes 98308
  16.1 4.5 %copy-start.19 = (f32[4096]{0:T(1024)S(1)}, f32[4096]{0:T(1024)}, u32[]{:S(2)}) copy-start(f32[4096]{0:T(1024)} %param.15) | copy-start | bytes 49156
  16.1 14.3 %collective-permute-start.27 = (bf16[80,256]{1,0:T(8,128)(2,1)}, bf16[80,256]{1,0:T(8,128)(2,1)S(1)}, u32[]{:S(2)}, u32[]{:S(2)}) collective-permute-start(bf16[80,256]{1,0:T(8,128)(2,1)} %get-tuple-element.46), channel_id=1, source_target_pairs={{0,8},{1,9},{2,10},{3,11},{4,12},{5,13},{6,14},{7,15},{8,16},{9,17... | collective-permute-start | bytes 122888 | tf_op jit(solution)/shard_map/ppermute | solution.py:198
  19.2 1.4 collective-permute-start.4
  19.3 7.1 %copy-start.4 = (bf16[2048,256]{1,0:T(8,128)(2,1)S(1)}, bf16[2048,256]{1,0:T(8,128)(2,1)}, u32[]{:S(2)}) copy-start(bf16[2048,256]{1,0:T(8,128)(2,1)} %param.19) | copy-start | bytes 3145732
  19.3 44.0 %collective-permute-start.19 = (bf16[256,768]{1,0:T(8,128)(2,1)S(1)}, bf16[256,768]{1,0:T(8,128)(2,1)S(1)}, u32[]{:S(2)}, u32[]{:S(2)}) collective-permute-start(bf16[256,768]{1,0:T(8,128)(2,1)S(1)} %pad_maximum_fusion.2), channel_id=1, source_target_pairs={{0,16},{1,17},{2,18},{3,19},{4,20},{5,21},{6,22},{7,23},{8,24},{9,... | collective-permute-start | bytes 1179656 | tf_op jit(solution)/shard_map/ppermute | solution.py:198
  20.6 4.3 %copy-start.13 = (bf16[256,128]{1,0:T(8,128)(2,1)S(1)}, bf16[256,128]{1,0:T(8,128)(2,1)}, u32[]{:S(2)}) copy-start(bf16[256,128]{1,0:T(8,128)(2,1)} %get-tuple-element.29) | copy-start | bytes 196612
  20.6 4.3 %copy-start.14 = (bf16[256,128]{1,0:T(8,128)(2,1)S(1)}, bf16[256,128]{1,0:T(8,128)(2,1)}, u32[]{:S(2)}) copy-start(bf16[256,128]{1,0:T(8,128)(2,1)} %get-tuple-element.57) | copy-start | bytes 196612
  23.4 40.2 %collective-permute-start.6 = (bf16[144,2048]{1,0:T(8,128)(2,1)}, bf16[144,2048]{1,0:T(8,128)(2,1)}, u32[]{:S(2)}, u32[]{:S(2)}) collective-permute-start(bf16[144,2048]{1,0:T(8,128)(2,1)} %fusion.2.refs_0_), channel_id=1, source_target_pairs={{0,8},{1,9},{2,10},{3,11},{4,12},{5,13},{6,14},{7,15},{8,16},{9,17... | collective-permute-start | bytes 1769480 | tf_op jit(solution)/shard_map/ppermute | solution.py:198
  25.7 39.6 %collective-permute-start.15 = (bf16[256,768]{1,0:T(8,128)(2,1)}, bf16[256,768]{1,0:T(8,128)(2,1)S(1)}, u32[]{:S(2)}, u32[]{:S(2)}) collective-permute-start(bf16[256,768]{1,0:T(8,128)(2,1)} %pad_maximum_fusion.1), channel_id=1, source_target_pairs={{0,8},{1,9},{2,10},{3,11},{4,12},{5,13},{6,14},{7,15},{8,16},{9,17... | collective-permute-start | bytes 1179656 | tf_op jit(solution)/shard_map/ppermute | solution.py:198
  27.3 76.7 %copy-start.20 = (bf16[1,16]{1,0:T(2,128)(2,1)S(1)}, bf16[1,16]{1,0:T(2,128)(2,1)}, u32[]{:S(2)}) copy-start(bf16[1,16]{1,0:T(2,128)(2,1)} %get-tuple-element.43) | copy-start | bytes 100
  28.2 32.8 %collective-permute-start.28 = (bf16[80,256]{1,0:T(8,128)(2,1)S(1)}, bf16[80,256]{1,0:T(8,128)(2,1)}, u32[]{:S(2)}, u32[]{:S(2)}) collective-permute-start(bf16[80,256]{1,0:T(8,128)(2,1)S(1)} %copy-done.18), channel_id=1, source_target_pairs={{0,16},{1,17},{2,18},{3,19},{4,20},{5,21},{6,22},{7,23},{8,24},{9,... | collective-permute-start | bytes 122888 | tf_op jit(solution)/shard_map/ppermute | solution.py:198
  30.4 59.1 %collective-permute-start.5 = (bf16[144,2048]{1,0:T(8,128)(2,1)}, bf16[144,2048]{1,0:T(8,128)(2,1)}, u32[]{:S(2)}, u32[]{:S(2)}) collective-permute-start(bf16[144,2048]{1,0:T(8,128)(2,1)} %fusion.2.refs_0_), channel_id=1, source_target_pairs={{0,1},{1,0},{2,3},{3,2},{4,5},{5,4},{6,7},{7,6},{8,9},{9,8},{10,11... | collective-permute-start | bytes 1769480 | tf_op jit(solution)/shard_map/ppermute | solution.py:198
  60.9 11.7 %collective-permute-start.13 = (bf16[256,768]{1,0:T(8,128)(2,1)S(1)}, bf16[256,768]{1,0:T(8,128)(2,1)S(1)}, u32[]{:S(2)}, u32[]{:S(2)}) collective-permute-start(bf16[256,768]{1,0:T(8,128)(2,1)S(1)} %pad_maximum_fusion.refs_8_), channel_id=1, source_target_pairs={{0,4},{1,3},{2,6},{3,1},{4,0},{5,7},{6,2},{7,5},{8,12},{9,11},{10,... | collective-permute-start | bytes 1179656 | tf_op jit(solution)/shard_map/ppermute | solution.py:198
  63.4 11.0 %collective-permute-start.12 = (bf16[256,768]{1,0:T(8,128)(2,1)S(1)}, bf16[256,768]{1,0:T(8,128)(2,1)S(1)}, u32[]{:S(2)}, u32[]{:S(2)}) collective-permute-start(bf16[256,768]{1,0:T(8,128)(2,1)S(1)} %pad_maximum_fusion.refs_8_), channel_id=1, source_target_pairs={{0,2},{1,5},{2,0},{3,7},{4,6},{5,1},{6,4},{7,3},{8,10},{9,13},{10,... | collective-permute-start | bytes 1179656 | tf_op jit(solution)/shard_map/ppermute | solution.py:198
  63.6 27.7 %collective-permute-start.8 = (bf16[144,2048]{1,0:T(8,128)(2,1)}, bf16[144,2048]{1,0:T(8,128)(2,1)}, u32[]{:S(2)}, u32[]{:S(2)}) collective-permute-start(bf16[144,2048]{1,0:T(8,128)(2,1)} %collective-permute-done.6.refs_2_), channel_id=1, source_target_pairs={{0,8},{1,9},{2,10},{3,11},{4,12},{5,13},{6,14},{7,15},{8,16},{9,17... | collective-permute-start | bytes 1769480 | tf_op jit(solution)/shard_map/ppermute | solution.py:198
  65.3 23.8 %collective-permute-start.23 = (bf16[256,768]{1,0:T(8,128)(2,1)}, bf16[256,768]{1,0:T(8,128)(2,1)}, u32[]{:S(2)}, u32[]{:S(2)}) collective-permute-start(bf16[256,768]{1,0:T(8,128)(2,1)} %pad_maximum_fusion.3), channel_id=1, source_target_pairs={{0,24},{1,25},{2,26},{3,27},{4,28},{5,29},{6,30},{7,31},{8,0},{9,1... | collective-permute-start | bytes 1179656 | tf_op jit(solution)/shard_map/ppermute | solution.py:198
  72.6 20.6 %collective-permute-start.21 = (bf16[256,768]{1,0:T(8,128)(2,1)S(1)}, bf16[256,768]{1,0:T(8,128)(2,1)S(1)}, u32[]{:S(2)}, u32[]{:S(2)}) collective-permute-start(bf16[256,768]{1,0:T(8,128)(2,1)S(1)} %collective-permute-done.19.refs_16_), channel_id=1, source_target_pairs={{0,4},{1,3},{2,6},{3,1},{4,0},{5,7},{6,2},{7,5},{8,12},{9,11},{10,... | collective-permute-start | bytes 1179656 | tf_op jit(solution)/shard_map/ppermute | solution.py:198
  74.4 20.6 %collective-permute-start.20 = (bf16[256,768]{1,0:T(8,128)(2,1)S(1)}, bf16[256,768]{1,0:T(8,128)(2,1)S(1)}, u32[]{:S(2)}, u32[]{:S(2)}) collective-permute-start(bf16[256,768]{1,0:T(8,128)(2,1)S(1)} %collective-permute-done.19.refs_16_), channel_id=1, source_target_pairs={{0,2},{1,5},{2,0},{3,7},{4,6},{5,1},{6,4},{7,3},{8,10},{9,13},{10,... | collective-permute-start | bytes 1179656 | tf_op jit(solution)/shard_map/ppermute | solution.py:198
  89.2 11.9 %collective-permute-start.17 = (bf16[256,768]{1,0:T(8,128)(2,1)S(1)}, bf16[256,768]{1,0:T(8,128)(2,1)S(1)}, u32[]{:S(2)}, u32[]{:S(2)}) collective-permute-start(bf16[256,768]{1,0:T(8,128)(2,1)S(1)} %collective-permute-done.15.refs_12_), channel_id=1, source_target_pairs={{0,4},{1,3},{2,6},{3,1},{4,0},{5,7},{6,2},{7,5},{8,12},{9,11},{10,... | collective-permute-start | bytes 1179656 | tf_op jit(solution)/shard_map/ppermute | solution.py:198
  89.5 12.1 %collective-permute-start.16 = (bf16[256,768]{1,0:T(8,128)(2,1)S(1)}, bf16[256,768]{1,0:T(8,128)(2,1)S(1)}, u32[]{:S(2)}, u32[]{:S(2)}) collective-permute-start(bf16[256,768]{1,0:T(8,128)(2,1)S(1)} %collective-permute-done.15.refs_12_), channel_id=1, source_target_pairs={{0,2},{1,5},{2,0},{3,7},{4,6},{5,1},{6,4},{7,3},{8,10},{9,13},{10,... | collective-permute-start | bytes 1179656 | tf_op jit(solution)/shard_map/ppermute | solution.py:198
  91.3 22.0 %collective-permute-start.10 = (bf16[144,2048]{1,0:T(8,128)(2,1)}, bf16[144,2048]{1,0:T(8,128)(2,1)}, u32[]{:S(2)}, u32[]{:S(2)}) collective-permute-start(bf16[144,2048]{1,0:T(8,128)(2,1)} %collective-permute-done.8.refs_4_), channel_id=1, source_target_pairs={{0,8},{1,9},{2,10},{3,11},{4,12},{5,13},{6,14},{7,15},{8,16},{9,17... | collective-permute-start | bytes 1769480 | tf_op jit(solution)/shard_map/ppermute | solution.py:198
  93.2 15.8 %collective-permute-start.14 = (bf16[256,768]{1,0:T(8,128)(2,1)S(1)}, bf16[256,768]{1,0:T(8,128)(2,1)}, u32[]{:S(2)}, u32[]{:S(2)}) collective-permute-start(bf16[256,768]{1,0:T(8,128)(2,1)S(1)} %collective-permute-done.12.refs_9_), channel_id=1, source_target_pairs={{0,4},{1,3},{2,6},{3,1},{4,0},{5,7},{6,2},{7,5},{8,12},{9,11},{10,... | collective-permute-start | bytes 1179656 | tf_op jit(solution)/shard_map/ppermute | solution.py:198
  95.0 18.3 %collective-permute-start.25 = (bf16[256,768]{1,0:T(8,128)(2,1)}, bf16[256,768]{1,0:T(8,128)(2,1)}, u32[]{:S(2)}, u32[]{:S(2)}) collective-permute-start(bf16[256,768]{1,0:T(8,128)(2,1)} %collective-permute-done.23.refs_20_), channel_id=1, source_target_pairs={{0,4},{1,3},{2,6},{3,1},{4,0},{5,7},{6,2},{7,5},{8,12},{9,11},{10,... | collective-permute-start | bytes 1179656 | tf_op jit(solution)/shard_map/ppermute | solution.py:198
  101.1 12.7 %collective-permute-start.24 = (bf16[256,768]{1,0:T(8,128)(2,1)}, bf16[256,768]{1,0:T(8,128)(2,1)}, u32[]{:S(2)}, u32[]{:S(2)}) collective-permute-start(bf16[256,768]{1,0:T(8,128)(2,1)} %collective-permute-done.23.refs_20_), channel_id=1, source_target_pairs={{0,2},{1,5},{2,0},{3,7},{4,6},{5,1},{6,4},{7,3},{8,10},{9,13},{10,... | collective-permute-start | bytes 1179656 | tf_op jit(solution)/shard_map/ppermute | solution.py:198
  102.3 15.2 %collective-permute-start.22 = (bf16[256,768]{1,0:T(8,128)(2,1)S(1)}, bf16[256,768]{1,0:T(8,128)(2,1)}, u32[]{:S(2)}, u32[]{:S(2)}) collective-permute-start(bf16[256,768]{1,0:T(8,128)(2,1)S(1)} %collective-permute-done.20.refs_17_), channel_id=1, source_target_pairs={{0,4},{1,3},{2,6},{3,1},{4,0},{5,7},{6,2},{7,5},{8,12},{9,11},{10,... | collective-permute-start | bytes 1179656 | tf_op jit(solution)/shard_map/ppermute | solution.py:198
  109.1 18.1 %collective-permute-start.7 = (bf16[144,2048]{1,0:T(8,128)(2,1)}, bf16[144,2048]{1,0:T(8,128)(2,1)S(1)}, u32[]{:S(2)}, u32[]{:S(2)}) collective-permute-start(bf16[144,2048]{1,0:T(8,128)(2,1)} %collective-permute-done.6.refs_2_), channel_id=1, source_target_pairs={{0,1},{1,0},{2,3},{3,2},{4,5},{5,4},{6,7},{7,6},{8,9},{9,8},{10,11... | collective-permute-start | bytes 1769480 | tf_op jit(solution)/shard_map/ppermute | solution.py:198
  113.3 15.5 %collective-permute-start.9 = (bf16[144,2048]{1,0:T(8,128)(2,1)}, bf16[144,2048]{1,0:T(8,128)(2,1)S(1)}, u32[]{:S(2)}, u32[]{:S(2)}) collective-permute-start(bf16[144,2048]{1,0:T(8,128)(2,1)} %collective-permute-done.8.refs_4_), channel_id=1, source_target_pairs={{0,1},{1,0},{2,3},{3,2},{4,5},{5,4},{6,7},{7,6},{8,9},{9,8},{10,11... | collective-permute-start | bytes 1769480 | tf_op jit(solution)/shard_map/ppermute | solution.py:198
  113.3 15.5 %collective-permute-start.11 = (bf16[144,2048]{1,0:T(8,128)(2,1)}, bf16[144,2048]{1,0:T(8,128)(2,1)S(1)}, u32[]{:S(2)}, u32[]{:S(2)}) collective-permute-start(bf16[144,2048]{1,0:T(8,128)(2,1)} %collective-permute-done.10.refs_6_), channel_id=1, source_target_pairs={{0,1},{1,0},{2,3},{3,2},{4,5},{5,4},{6,7},{7,6},{8,9},{9,8},{10,11... | collective-permute-start | bytes 1769480 | tf_op jit(solution)/shard_map/ppermute | solution.py:198
  113.8 8.1 %copy-start.12 = (bf16[512,256]{1,0:T(8,128)(2,1)S(1)}, bf16[512,256]{1,0:T(8,128)(2,1)}, u32[]{:S(2)}) copy-start(bf16[512,256]{1,0:T(8,128)(2,1)} %get-tuple-element.16) | copy-start | bytes 786436
  113.8 12.3 %copy-start.11 = (bf16[512,256]{1,0:T(8,128)(2,1)S(1)}, bf16[512,256]{1,0:T(8,128)(2,1)}, u32[]{:S(2)}) copy-start(bf16[512,256]{1,0:T(8,128)(2,1)} %get-tuple-element.17) | copy-start | bytes 786436
  113.8 13.4 %copy-start.10 = (bf16[512,256]{1,0:T(8,128)(2,1)S(1)}, bf16[512,256]{1,0:T(8,128)(2,1)}, u32[]{:S(2)}) copy-start(bf16[512,256]{1,0:T(8,128)(2,1)} %get-tuple-element.19) | copy-start | bytes 786436
  113.8 16.0 %copy-start.2 = (bf16[256,768]{1,0:T(8,128)(2,1)S(1)}, bf16[256,768]{1,0:T(8,128)(2,1)}, u32[]{:S(2)}) copy-start(bf16[256,768]{1,0:T(8,128)(2,1)} %copy-done.1) | copy-start | bytes 1179652
  113.8 8.1 %collective-permute-start.18 = (bf16[256,768]{1,0:T(8,128)(2,1)}, bf16[256,768]{1,0:T(8,128)(2,1)S(1)}, u32[]{:S(2)}, u32[]{:S(2)}) collective-permute-start(bf16[256,768]{1,0:T(8,128)(2,1)} %copy-done.1), channel_id=1, source_target_pairs={{0,4},{1,3},{2,6},{3,1},{4,0},{5,7},{6,2},{7,5},{8,12},{9,11},{10,... | collective-permute-start | bytes 1179656 | tf_op jit(solution)/shard_map/ppermute | solution.py:198
  117.5 8.6 %collective-permute-start.26 = (bf16[256,768]{1,0:T(8,128)(2,1)}, bf16[256,768]{1,0:T(8,128)(2,1)S(1)}, u32[]{:S(2)}, u32[]{:S(2)}) collective-permute-start(bf16[256,768]{1,0:T(8,128)(2,1)} %collective-permute-done.24.refs_21_), channel_id=1, source_target_pairs={{0,4},{1,3},{2,6},{3,1},{4,0},{5,7},{6,2},{7,5},{8,12},{9,11},{10,... | collective-permute-start | bytes 1179656 | tf_op jit(solution)/shard_map/ppermute | solution.py:198
  121.9 18.6 %collective-permute-start.44 = (bf16[512,256]{1,0:T(8,128)(2,1)S(1)}, bf16[512,256]{1,0:T(8,128)(2,1)S(1)}, u32[]{:S(2)}, u32[]{:S(2)}) collective-permute-start(bf16[512,256]{1,0:T(8,128)(2,1)S(1)} %copy-done.12), channel_id=1, source_target_pairs={{0,24},{1,25},{2,26},{3,27},{4,28},{5,29},{6,30},{7,31},{8,0},{9,1... | collective-permute-start | bytes 786440 | tf_op jit(solution)/shard_map/ppermute | solution.py:198
  126.1 14.7 %collective-permute-start.36 = (bf16[512,256]{1,0:T(8,128)(2,1)S(1)}, bf16[512,256]{1,0:T(8,128)(2,1)S(1)}, u32[]{:S(2)}, u32[]{:S(2)}) collective-permute-start(bf16[512,256]{1,0:T(8,128)(2,1)S(1)} %copy-done.11), channel_id=1, source_target_pairs={{0,8},{1,9},{2,10},{3,11},{4,12},{5,13},{6,14},{7,15},{8,16},{9,17... | collective-permute-start | bytes 786440 | tf_op jit(solution)/shard_map/ppermute | solution.py:198
  127.2 18.8 %collective-permute-start.40 = (bf16[512,256]{1,0:T(8,128)(2,1)S(1)}, bf16[512,256]{1,0:T(8,128)(2,1)S(1)}, u32[]{:S(2)}, u32[]{:S(2)}) collective-permute-start(bf16[512,256]{1,0:T(8,128)(2,1)S(1)} %copy-done.10), channel_id=1, source_target_pairs={{0,16},{1,17},{2,18},{3,19},{4,20},{5,21},{6,22},{7,23},{8,24},{9,... | collective-permute-start | bytes 786440 | tf_op jit(solution)/shard_map/ppermute | solution.py:198
  138.2 12.1 %collective-permute-start.30 = (bf16[6,128,256]{2,1,0:T(8,128)(2,1)S(1)}, bf16[6,128,256]{2,1,0:T(8,128)(2,1)S(1)}, u32[]{:S(2)}, u32[]{:S(2)}) collective-permute-start(bf16[6,128,256]{2,1,0:T(8,128)(2,1)S(1)} %get-tuple-element.10.kv0), channel_id=1, source_target_pairs={{0,2},{1,5},{2,0},{3,7},{4,6},{5,1},{6,4},{7,3},{8,10},{9,13},{10,... | collective-permute-start | bytes 1179656 | tf_op jit(solution)/shard_map/ppermute | solution.py:198
  140.2 9.2 %collective-permute-start.34 = (bf16[512,256]{1,0:T(8,128)(2,1)S(1)}, bf16[512,256]{1,0:T(8,128)(2,1)S(1)}, u32[]{:S(2)}, u32[]{:S(2)}) collective-permute-start(bf16[512,256]{1,0:T(8,128)(2,1)S(1)} %get-tuple-element.18.refs_0_), channel_id=1, source_target_pairs={{0,4},{1,3},{2,6},{3,1},{4,0},{5,7},{6,2},{7,5},{8,12},{9,11},{10,... | collective-permute-start | bytes 786440 | tf_op jit(solution)/shard_map/ppermute | solution.py:198
  140.5 15.3 %collective-permute-start.33 = (bf16[512,256]{1,0:T(8,128)(2,1)S(1)}, bf16[512,256]{1,0:T(8,128)(2,1)S(1)}, u32[]{:S(2)}, u32[]{:S(2)}) collective-permute-start(bf16[512,256]{1,0:T(8,128)(2,1)S(1)} %get-tuple-element.18.refs_0_), channel_id=1, source_target_pairs={{0,2},{1,5},{2,0},{3,7},{4,6},{5,1},{6,4},{7,3},{8,10},{9,13},{10,... | collective-permute-start | bytes 786440 | tf_op jit(solution)/shard_map/ppermute | solution.py:198
  140.8 15.5 %collective-permute-start.46 = (bf16[512,256]{1,0:T(8,128)(2,1)S(1)}, bf16[512,256]{1,0:T(8,128)(2,1)S(1)}, u32[]{:S(2)}, u32[]{:S(2)}) collective-permute-start(bf16[512,256]{1,0:T(8,128)(2,1)S(1)} %collective-permute-done.44.refs_12_), channel_id=1, source_target_pairs={{0,4},{1,3},{2,6},{3,1},{4,0},{5,7},{6,2},{7,5},{8,12},{9,11},{10,... | collective-permute-start | bytes 786440 | tf_op jit(solution)/shard_map/ppermute | solution.py:198
  146.0 15.5 %collective-permute-start.45 = (bf16[512,256]{1,0:T(8,128)(2,1)S(1)}, bf16[512,256]{1,0:T(8,128)(2,1)S(1)}, u32[]{:S(2)}, u32[]{:S(2)}) collective-permute-start(bf16[512,256]{1,0:T(8,128)(2,1)S(1)} %collective-permute-done.44.refs_12_), channel_id=1, source_target_pairs={{0,2},{1,5},{2,0},{3,7},{4,6},{5,1},{6,4},{7,3},{8,10},{9,13},{10,... | collective-permute-start | bytes 786440 | tf_op jit(solution)/shard_map/ppermute | solution.py:198
  149.4 25.4 %collective-permute-start.31 = (bf16[6,128,256]{2,1,0:T(8,128)(2,1)S(1)}, bf16[6,128,256]{2,1,0:T(8,128)(2,1)S(1)}, u32[]{:S(2)}, u32[]{:S(2)}) collective-permute-start(bf16[6,128,256]{2,1,0:T(8,128)(2,1)S(1)} %get-tuple-element.10.kv0), channel_id=1, source_target_pairs={{0,4},{1,3},{2,6},{3,1},{4,0},{5,7},{6,2},{7,5},{8,12},{9,11},{10,... | collective-permute-start | bytes 1179656 | tf_op jit(solution)/shard_map/ppermute | solution.py:198
  150.2 25.9 %collective-permute-start.32 = (bf16[6,128,256]{2,1,0:T(8,128)(2,1)S(1)}, bf16[6,128,256]{2,1,0:T(8,128)(2,1)S(1)}, u32[]{:S(2)}, u32[]{:S(2)}) collective-permute-start(bf16[6,128,256]{2,1,0:T(8,128)(2,1)S(1)} %collective-permute-done.30.kv1), channel_id=1, source_target_pairs={{0,4},{1,3},{2,6},{3,1},{4,0},{5,7},{6,2},{7,5},{8,12},{9,11},{10,... | collective-permute-start | bytes 1179656 | tf_op jit(solution)/shard_map/ppermute | solution.py:198
  155.8 16.3 %collective-permute-start.38 = (bf16[512,256]{1,0:T(8,128)(2,1)S(1)}, bf16[512,256]{1,0:T(8,128)(2,1)S(1)}, u32[]{:S(2)}, u32[]{:S(2)}) collective-permute-start(bf16[512,256]{1,0:T(8,128)(2,1)S(1)} %collective-permute-done.36.refs_4_), channel_id=1, source_target_pairs={{0,4},{1,3},{2,6},{3,1},{4,0},{5,7},{6,2},{7,5},{8,12},{9,11},{10,... | collective-permute-start | bytes 786440 | tf_op jit(solution)/shard_map/ppermute | solution.py:198
  156.4 16.5 %collective-permute-start.37 = (bf16[512,256]{1,0:T(8,128)(2,1)S(1)}, bf16[512,256]{1,0:T(8,128)(2,1)S(1)}, u32[]{:S(2)}, u32[]{:S(2)}) collective-permute-start(bf16[512,256]{1,0:T(8,128)(2,1)S(1)} %collective-permute-done.36.refs_4_), channel_id=1, source_target_pairs={{0,2},{1,5},{2,0},{3,7},{4,6},{5,1},{6,4},{7,3},{8,10},{9,13},{10,... | collective-permute-start | bytes 786440 | tf_op jit(solution)/shard_map/ppermute | solution.py:198
  161.5 12.7 %collective-permute-start.41 = (bf16[512,256]{1,0:T(8,128)(2,1)S(1)}, bf16[512,256]{1,0:T(8,128)(2,1)S(1)}, u32[]{:S(2)}, u32[]{:S(2)}) collective-permute-start(bf16[512,256]{1,0:T(8,128)(2,1)S(1)} %collective-permute-done.40.refs_8_), channel_id=1, source_target_pairs={{0,2},{1,5},{2,0},{3,7},{4,6},{5,1},{6,4},{7,3},{8,10},{9,13},{10,... | collective-permute-start | bytes 786440 | tf_op jit(solution)/shard_map/ppermute | solution.py:198
  172.1 14.4 %collective-permute-start.42 = (bf16[512,256]{1,0:T(8,128)(2,1)S(1)}, bf16[512,256]{1,0:T(8,128)(2,1)S(1)}, u32[]{:S(2)}, u32[]{:S(2)}) collective-permute-start(bf16[512,256]{1,0:T(8,128)(2,1)S(1)} %collective-permute-done.40.refs_8_), channel_id=1, source_target_pairs={{0,4},{1,3},{2,6},{3,1},{4,0},{5,7},{6,2},{7,5},{8,12},{9,11},{10,... | collective-permute-start | bytes 786440 | tf_op jit(solution)/shard_map/ppermute | solution.py:198
  172.8 13.6 %collective-permute-start.35 = (bf16[512,256]{1,0:T(8,128)(2,1)S(1)}, bf16[512,256]{1,0:T(8,128)(2,1)S(1)}, u32[]{:S(2)}, u32[]{:S(2)}) collective-permute-start(bf16[512,256]{1,0:T(8,128)(2,1)S(1)} %collective-permute-done.33.refs_1_), channel_id=1, source_target_pairs={{0,4},{1,3},{2,6},{3,1},{4,0},{5,7},{6,2},{7,5},{8,12},{9,11},{10,... | collective-permute-start | bytes 786440 | tf_op jit(solution)/shard_map/ppermute | solution.py:198
  174.1 12.3 %collective-permute-start.47 = (bf16[512,256]{1,0:T(8,128)(2,1)S(1)}, bf16[512,256]{1,0:T(8,128)(2,1)S(1)}, u32[]{:S(2)}, u32[]{:S(2)}) collective-permute-start(bf16[512,256]{1,0:T(8,128)(2,1)S(1)} %collective-permute-done.45.refs_13_), channel_id=1, source_target_pairs={{0,4},{1,3},{2,6},{3,1},{4,0},{5,7},{6,2},{7,5},{8,12},{9,11},{10,... | collective-permute-start | bytes 786440 | tf_op jit(solution)/shard_map/ppermute | solution.py:198
  174.9 12.0 %collective-permute-start.39 = (bf16[512,256]{1,0:T(8,128)(2,1)S(1)}, bf16[512,256]{1,0:T(8,128)(2,1)S(1)}, u32[]{:S(2)}, u32[]{:S(2)}) collective-permute-start(bf16[512,256]{1,0:T(8,128)(2,1)S(1)} %collective-permute-done.37.refs_5_), channel_id=1, source_target_pairs={{0,4},{1,3},{2,6},{3,1},{4,0},{5,7},{6,2},{7,5},{8,12},{9,11},{10,... | collective-permute-start | bytes 786440 | tf_op jit(solution)/shard_map/ppermute | solution.py:198
  176.2 13.5 %collective-permute-start.43 = (bf16[512,256]{1,0:T(8,128)(2,1)S(1)}, bf16[512,256]{1,0:T(8,128)(2,1)S(1)}, u32[]{:S(2)}, u32[]{:S(2)}) collective-permute-start(bf16[512,256]{1,0:T(8,128)(2,1)S(1)} %collective-permute-done.41.refs_9_), channel_id=1, source_target_pairs={{0,4},{1,3},{2,6},{3,1},{4,0},{5,7},{6,2},{7,5},{8,12},{9,11},{10,... | collective-permute-start | bytes 786440 | tf_op jit(solution)/shard_map/ppermute | solution.py:198
  200.1 4.4 %collective-permute-start.48 = (bf16[512,2048]{1,0:T(8,128)(2,1)}, bf16[512,2048]{1,0:T(8,128)(2,1)S(1)}, u32[]{:S(2)}, u32[]{:S(2)}) collective-permute-start(bf16[512,2048]{1,0:T(8,128)(2,1)} %get-tuple-element.12), channel_id=1, source_target_pairs={{0,1},{1,0},{2,3},{3,2},{4,5},{5,4},{6,7},{7,6},{8,9},{9,8},{10,11... | collective-permute-start | bytes 6291464 | tf_op jit(solution)/shard_map/ppermute | solution.py:198
  209.5 14.8 %collective-permute-start.49 = (bf16[128,2048]{1,0:T(8,128)(2,1)S(1)}, bf16[128,2048]{1,0:T(8,128)(2,1)S(1)}, u32[]{:S(2)}, u32[]{:S(2)}) collective-permute-start(bf16[128,2048]{1,0:T(8,128)(2,1)S(1)} %get-tuple-element.13), channel_id=1, source_target_pairs={{0,8},{1,9},{2,10},{3,11},{4,12},{5,13},{6,14},{7,15},{8,16},{9,17... | collective-permute-start | bytes 1572872 | tf_op jit(solution)/shard_map/ppermute | solution.py:198
  210.0 26.5 %collective-permute-start.51 = (bf16[128,2048]{1,0:T(8,128)(2,1)S(1)}, bf16[128,2048]{1,0:T(8,128)(2,1)S(1)}, u32[]{:S(2)}, u32[]{:S(2)}) collective-permute-start(bf16[128,2048]{1,0:T(8,128)(2,1)S(1)} %get-tuple-element.14), channel_id=1, source_target_pairs={{0,24},{1,25},{2,26},{3,27},{4,28},{5,29},{6,30},{7,31},{8,0},{9,1... | collective-permute-start | bytes 1572872 | tf_op jit(solution)/shard_map/ppermute | solution.py:198
  211.5 43.7 %collective-permute-start.50 = (bf16[128,2048]{1,0:T(8,128)(2,1)S(1)}, bf16[128,2048]{1,0:T(8,128)(2,1)S(1)}, u32[]{:S(2)}, u32[]{:S(2)}) collective-permute-start(bf16[128,2048]{1,0:T(8,128)(2,1)S(1)} %get-tuple-element.15), channel_id=1, source_target_pairs={{0,16},{1,17},{2,18},{3,19},{4,20},{5,21},{6,22},{7,23},{8,24},{9,... | collective-permute-start | bytes 1572872 | tf_op jit(solution)/shard_map/ppermute | solution.py:198
  (10 other events, 15.8 us)

commit v2 on v1

--- a/solution.py
+++ b/solution.py
@@ -177,8 +177,10 @@
 
 LEVELS = 4
 PLANE = 4
+TILE_RUN = 256
+CACHED = 64
+REC = 8
 REC_PAD = 16
-TILE_RUN = 256
 
 
 def permuted(value, move):
@@ -206,11 +208,18 @@
     return permuted(value, lambda z, p, c: (z, p, 1 - c))
 
 
-def in_plane(piece):
-    near = permuted(piece, lambda z, p, c: (z, p ^ (1 + c), c))
-    far = permuted(piece, lambda z, p, c: (z, p ^ (2 - c), c))
-    both = permuted(near, lambda z, p, c: (z, p ^ (2 - c), c))
-    return [piece, near, far, both]
+def to_near(value):
+    return permuted(value, lambda z, p, c: (z, p ^ (1 + c), c))
+
+
+def to_far(value):
+    return permuted(value, lambda z, p, c: (z, p ^ (2 - c), c))
+
+
+def in_plane(pieces):
+    near = to_near(pieces)
+    pair = to_far(jnp.concatenate([pieces, near], axis=0))
+    return pieces, near, pair
 
 
 def place_of(which, place, core):
@@ -221,16 +230,39 @@
     return place ^ (1 + core) if which == 1 else place ^ (2 - core)
 
 
+def level_before(level, steps):
+    return lax.rem(level + LEVELS - steps, LEVELS)
+
+
+def piece_at(groups, which, steps):
+    for levels, refs in groups:
+        if steps in levels:
+            at = levels.index(steps)
+            if which < 2:
+                return refs[which].at[at]
+            return refs[2].at[(which - 2) * len(levels) + at]
+    return None
+
+
+GROUPS = ((0,), (1,), (2, 3))
+
+
+def grouped(refs):
+    return [(levels, refs[3 * i : 3 * i + 3]) for i, levels in enumerate(GROUPS)]
+
+
+def turned(values, cosine, sine):
+    return values * cosine + pltpu.roll(values, HD // 2, 1) * sine
+
+
 def project_kernel(where_ref, *refs):
     acts = refs[:8]
-    weights = refs[8:24]
-    caches = refs[24:28]
-    cos_ref, sin_ref, query_ref, kv_ref, x_ref = refs[28:]
+    groups = grouped(refs[8:17])
+    cos_ref, sin_ref, query_ref, kv_ref, x_ref = refs[17:]
     level, place, core = where_ref[0], where_ref[1], where_ref[2]
-    rows = acts[0].shape[0]
-    depth = weights[0].shape[0]
-    width = acts[0].shape[1]
+    rows, width = acts[0].shape
     tok = rows - REC_PAD
+    depth = 2 * width // (LEVELS * PLANE)
     mine = pl.multiple_of(core * width, width)
     others = pl.multiple_of((1 - core) * width, width)
     for k in range(LEVELS):
@@ -238,77 +270,97 @@
         x_ref[k * rows : (k + 1) * rows, pl.ds(others, width)] = acts[2 * k + 1][...]
     total = None
     for d in range(LEVELS):
-        from_level = lax.rem(level + LEVELS - d, LEVELS)
         for j in range(PLANE):
-            block = from_level * PLANE + place_of(j, place, core)
+            block = level_before(level, d) * PLANE + place_of(j, place, core)
             start = pl.multiple_of(block * depth, depth)
             part = jnp.dot(
                 x_ref[:, pl.ds(start, depth)],
-                weights[d * PLANE + j][...],
+                piece_at(groups, j, d)[0:depth, :],
                 preferred_element_type=jnp.float32,
             )
             total = part if total is None else total + part
+    lane = lax.broadcasted_iota(jnp.int32, (REC, CACHED), 1)
     for k in range(LEVELS):
-        at = lax.rem(level + LEVELS - k, LEVELS)
+        at = level_before(level, k)
         block = total[k * rows : (k + 1) * rows]
-        cosine = cos_ref[at]
-        sine = sin_ref[at]
-
-        def turned(values, cosine, sine):
-            return values * cosine + pltpu.roll(values, HD // 2, 1) * sine
-
+        cosine, sine = cos_ref[at], sin_ref[at]
         for h in range(4):
             head = turned(block[:tok, h * HD : (h + 1) * HD], cosine[:tok], sine[:tok])
             query_ref[at, h] = head.astype(jnp.bfloat16)
-        keys = turned(block[:, 4 * HD : 5 * HD], cosine, sine)
-        values = block[:, 5 * HD : 6 * HD]
-        both = jnp.concatenate([keys, values], axis=1)
-        kv_ref[LEVELS * 64 // 128 + at] = both[:tok].astype(jnp.bfloat16)
-        cached = caches[k][0:64, :].astype(jnp.float32)
-        slots = caches[k][64:80, :].astype(jnp.int32)
-        row = lax.broadcasted_iota(jnp.int32, cached.shape, 0)
-        for r in range(8):
-            cached = jnp.where(row == slots[r : r + 1], both[tok + r : tok + r + 1], cached)
-        half = lax.rem(at, 2)
-        kv_ref[at // 2, pl.ds(pl.multiple_of(half * 64, 64), 64)] = cached.astype(jnp.bfloat16)
-
-
-def attend_kernel(where_ref, query_ref, kv0, kv1, kv2, kv3, out_ref):
-    place, core = where_ref[1], where_ref[2]
-    pieces = (kv0, kv1, kv2, kv3)
+        keys = turned(block[:tok, 4 * HD : 5 * HD], cosine[:tok], sine[:tok])
+        kv_ref[at, 0:tok, 0:HD] = keys.astype(jnp.bfloat16)
+        kv_ref[at, 0:tok, HD : 2 * HD] = block[:tok, 5 * HD : 6 * HD].astype(jnp.bfloat16)
+        slots = piece_at(groups, 0, k)[depth : depth + REC_PAD, 4 * HD : 4 * HD + CACHED]
+        chosen = (slots[0:REC].astype(jnp.int32) == lane).astype(jnp.float32)
+        rec_cos, rec_sin = (
+            jnp.dot(
+                chosen,
+                table[tok : tok + CACHED],
+                preferred_element_type=jnp.float32,
+                precision=lax.Precision.HIGHEST,
+            )
+            for table in (cosine, sine)
+        )
+        rec_keys = turned(block[tok : tok + REC, 4 * HD : 5 * HD], rec_cos, rec_sin)
+        both = jnp.concatenate([rec_keys, block[tok : tok + REC, 5 * HD : 6 * HD]], axis=1)
+        both = jnp.concatenate([both, jnp.zeros_like(both)], axis=0)
+        kv_ref[at, tok : tok + REC_PAD, :] = both.astype(jnp.bfloat16)
+
+
+def attend_kernel(where_ref, query_ref, *refs):
+    kv_mine, kv_near, kv_pair = refs[:3]
+    groups = grouped(refs[3:12])
+    out_ref, cache_ref = refs[12:]
+    level, place, core = where_ref[0], where_ref[1], where_ref[2]
+    kvs = (kv_mine.at[0], kv_near.at[0], kv_pair.at[0], kv_pair.at[1])
     tok = query_ref.shape[2]
-    old = LEVELS // 2
+    line = lax.broadcasted_iota(jnp.int32, (CACHED, 2 * HD), 0)
+    for j in range(PLANE):
+        for d in range(LEVELS):
+            at = level_before(level, d)
+            piece = piece_at(groups, j, d)
+            slots = piece[0:REC_PAD, 4 * HD : 6 * HD].astype(jnp.int32)
+            cached = jnp.concatenate(
+                [piece[:, 0 : 2 * HD], piece[:, 2 * HD : 4 * HD]], axis=0
+            ).astype(jnp.float32)
+            fresh = kvs[j][at, tok : tok + REC_PAD, :].astype(jnp.float32)
+            for r in range(REC):
+                cached = jnp.where(line == slots[r : r + 1], fresh[r : r + 1], cached)
+            cache_ref[j, d * CACHED : (d + 1) * CACHED, :] = cached.astype(jnp.bfloat16)
     row = lax.broadcasted_iota(jnp.int32, (tok, tok), 0)
     col = lax.broadcasted_iota(jnp.int32, (tok, tok), 1)
     scale = HD ** (-0.5) * 1.4426950408889634
+
+    def scores_of(queries, keys):
+        return lax.dot_general(
+            queries, keys, (((1,), (1,)), ((), ())), preferred_element_type=jnp.float32
+        )
+
     for i in range(LEVELS):
-        count = (old + i + 1) * tok
         queries = query_ref[i].reshape(4 * tok, HD)
-        scores = []
-        best = None
+        scores, values = [], []
         for j in range(PLANE):
-            theirs = place_of(j, place, core)
-            keys = pieces[j][0 : old + i + 1, :, 0:HD].reshape(count, HD)
-            raw = lax.dot_general(
-                queries, keys, (((1,), (1,)), ((), ())), preferred_element_type=jnp.float32
-            )
+            scores.append(scores_of(queries, cache_ref[j, :, 0:HD]))
+            values.append(cache_ref[j, :, HD : 2 * HD])
+            if i:
+                scores.append(scores_of(queries, kvs[j][0:i, 0:tok, 0:HD].reshape(i * tok, HD)))
+                values.append(kvs[j][0:i, 0:tok, HD : 2 * HD].reshape(i * tok, HD))
+            raw = scores_of(queries, kvs[j][i, 0:tok, 0:HD])
             if j == 0:
                 allowed = col <= row
             else:
-                allowed = jnp.broadcast_to(theirs, (tok, tok)) < place
-            allowed = jnp.concatenate([allowed] * 4, axis=0)
-            last = jnp.where(allowed, raw[:, count - tok :], NEG_FILL)
-            raw = jnp.concatenate([raw[:, : count - tok], last], axis=1)
-            top = jnp.max(raw, axis=1, keepdims=True)
-            best = top if best is None else jnp.maximum(best, top)
-            scores.append(raw)
+                allowed = jnp.broadcast_to(place_of(j, place, core), (tok, tok)) < place
+            scores.append(jnp.where(jnp.concatenate([allowed] * 4, axis=0), raw, NEG_FILL))
+            values.append(kvs[j][i, 0:tok, HD : 2 * HD])
+        best = jnp.max(scores[0], axis=1, keepdims=True)
+        for raw in scores[1:]:
+            best = jnp.maximum(best, jnp.max(raw, axis=1, keepdims=True))
         total, accum = 0.0, 0.0
-        for j in range(PLANE):
-            weights = jnp.exp2((scores[j] - best) * scale)
+        for raw, value in zip(scores, values):
+            weights = jnp.exp2((raw - best) * scale)
             total = total + jnp.sum(weights, axis=1, keepdims=True)
-            values = pieces[j][0 : old + i + 1, :, HD : 2 * HD].reshape(count, HD)
             accum = accum + jnp.dot(
-                weights.astype(jnp.bfloat16), values, preferred_element_type=jnp.float32
+                weights.astype(jnp.bfloat16), value, preferred_element_type=jnp.float32
             )
         result = (accum / total).astype(jnp.bfloat16)
         for h in range(4):
@@ -317,28 +369,29 @@
             ]
 
 
-def output_kernel(where_ref, attended_ref, *refs):
-    weights = refs[:16]
-    mine_ref, other_ref = refs[16:]
+def output_kernel(where_ref, *refs):
+    heads = refs[:LEVELS]
+    w_mine, w_near, w_pair, mine_ref, other_ref = refs[LEVELS:]
+    weights = (w_mine.at[0], w_near.at[0], w_pair.at[0], w_pair.at[1])
     level, place, core = where_ref[0], where_ref[1], where_ref[2]
-    width = weights[0].shape[1]
-    half = LEVELS * PLANE // 2
-    for d in range(LEVELS):
-        from_level = lax.rem(level + LEVELS - d, LEVELS)
-        for j in range(PLANE):
-            block = from_level * PLANE + place_of(j, place, core)
-            start = pl.multiple_of(lax.rem(block, half) * width, width)
+    depth = heads[0].shape[1]
+    width = w_mine.shape[2]
+    part_rows = mine_ref.shape[1]
+    for j in range(PLANE):
+        total = None
+        for k in range(LEVELS):
+            start = pl.multiple_of(level_before(level, k) * depth, depth)
             part = jnp.dot(
-                attended_ref[...], weights[d * PLANE + j][...], preferred_element_type=jnp.float32
+                heads[k][...],
+                weights[j][pl.ds(start, depth), :],
+                preferred_element_type=jnp.float32,
             )
-
-            @pl.when(block // half == core)
-            def _():
-                mine_ref[:, pl.ds(start, width)] = part
-
-            @pl.when(block // half != core)
-            def _():
-                other_ref[:, pl.ds(start, width)] = part.astype(jnp.bfloat16)
+            total = part if total is None else total + part
+        to = pl.multiple_of(place_of(j, place, core) * width, width)
+        split = total.reshape(LEVELS, 2, part_rows, width)
+        first, second = split[:, 0], split[:, 1]
+        mine_ref[:, :, pl.ds(to, width)] = jnp.where(core == 0, first, second)
+        other_ref[:, :, pl.ds(to, width)] = jnp.where(core == 0, second, first).astype(jnp.bfloat16)
 
 
 SMEM = pl.BlockSpec(memory_space=pltpu.SMEM)
@@ -365,37 +418,7 @@
     level, place = seq_index // PLANE, seq_index % PLANE
     where = jnp.stack([level, place, core]).astype(jnp.int32)
     tok, width = text_rows.shape
-    rec = recompute_rows.shape[0]
-    cache_rows = cache_keys.shape[0]
     depth = w_query.shape[0]
-
-    def group_of(level_at):
-        q = lax.dynamic_slice_in_dim(w_query, level_at * 4 * HD, 4 * HD, 1)
-        k = lax.dynamic_slice_in_dim(w_key, level_at * HD, HD, 1)
-        v = lax.dynamic_slice_in_dim(w_value, level_at * HD, HD, 1)
-        return jnp.concatenate([q, k, v], axis=1)
-
-    local_slots = (recompute_slots - seq_index * cache_rows).astype(jnp.bfloat16)
-    slot_rows = jnp.broadcast_to(
-        jnp.pad(local_slots, (0, REC_PAD - rec))[:, None], (REC_PAD, 2 * HD)
-    )
-
-    def cache_of(level_at):
-        k = lax.dynamic_slice_in_dim(cache_keys, level_at * HD, HD, 1)
-        v = lax.dynamic_slice_in_dim(cache_values, level_at * HD, HD, 1)
-        return jnp.concatenate([jnp.concatenate([k, v], axis=1), slot_rows], axis=0)
-
-    def out_of(level_at):
-        return lax.dynamic_slice_in_dim(w_out, level_at * 4 * HD, 4 * HD, 0)
-
-    weights, caches = [], []
-    for d in range(LEVELS):
-        to_level = (level + d) % LEVELS
-        piece, cached = group_of(to_level), cache_of(to_level)
-        if d:
-            piece, cached = up(piece, d), up(cached, d)
-        caches.append(cached)
-        weights += in_plane(piece)
 
     stream_len = tok * LEVELS * PLANE
     tile_owners = TILE_RUN // tok
@@ -415,16 +438,38 @@
     is_owner = jnp.any(seq_index == jnp.array(owners, jnp.int32))
     stream = jnp.where(is_owner, placed, text_rows)
 
+    slots = (recompute_slots - seq_index * CACHED).astype(jnp.bfloat16)
+    slot_rows = jnp.broadcast_to(
+        jnp.pad(slots, (0, CACHED // 2 - REC))[:, None], (CACHED // 2, 2 * HD)
+    )
+
+    def piece_for(to_level):
+        q = lax.dynamic_slice_in_dim(w_query, to_level * 4 * HD, 4 * HD, 1)
+        k, v, old_k, old_v = (
+            lax.dynamic_slice_in_dim(a, to_level * HD, HD, 1)
+            for a in (w_key, w_value, cache_keys, cache_values)
+        )
+        old = jnp.concatenate([old_k, old_v], axis=1)
+        half = CACHED // 2
+        old = jnp.concatenate([old[:half], old[half:], slot_rows], axis=1)
+        return jnp.concatenate([jnp.concatenate([q, k, v], axis=1), old], axis=0)[None]
+
+    pieces = [piece_for((level + d) % LEVELS) for d in range(LEVELS)]
+    moved = [up(piece, d) if d else piece for d, piece in enumerate(pieces)]
+    gathered = []
+    for levels in GROUPS:
+        group = [moved[d] for d in levels]
+        gathered += in_plane(group[0] if len(group) == 1 else jnp.concatenate(group, axis=0))
+
     rows = jnp.concatenate(
-        [stream, recompute_rows, jnp.zeros((REC_PAD - rec, width), stream.dtype)], axis=0
+        [stream, recompute_rows, jnp.zeros((REC_PAD - REC, width), stream.dtype)], axis=0
     )
     wide = rows.astype(jnp.float32)
     squares = jnp.sum(wide * wide, axis=1)
     squares = squares + other_core(squares)
     gain = lax.dynamic_slice_in_dim(norm_gain, core * width, width, 0)
-    normed = scaled(wide, squares, gain)
-
-    acts, held = [], normed
+    held = scaled(wide, squares, gain)
+    acts = []
     for k in range(LEVELS):
         if k:
             held = up(held, 1)
@@ -432,65 +477,85 @@
 
     half = HD // 2
     freqs = ROPE_BASE ** (-jnp.arange(half, dtype=jnp.float32) / half)
-    level_start = (jnp.arange(LEVELS, dtype=jnp.int32) * PLANE + place)[:, None]
+    blocks = (jnp.arange(LEVELS, dtype=jnp.int32) * PLANE + place)[:, None]
     stream_pos = (
-        cache_rows * LEVELS * PLANE + level_start * tok + jnp.arange(tok, dtype=jnp.int32)[None]
+        CACHED * LEVELS * PLANE + blocks * tok + jnp.arange(tok, dtype=jnp.int32)[None]
     ).astype(jnp.float32)
-    order = (level - jnp.arange(LEVELS, dtype=jnp.int32)) % LEVELS
-    slots = jnp.stack([c[cache_rows:, 0] for c in caches])[order].astype(jnp.float32)
-    rec_pos = slots + (level_start * cache_rows).astype(jnp.float32)
-    positions = jnp.concatenate([stream_pos, rec_pos], axis=1)
-    angles = positions[..., None] * freqs
+    cache_pos = (blocks * CACHED + jnp.arange(CACHED, dtype=jnp.int32)[None]).astype(jnp.float32)
+    angles = jnp.concatenate([stream_pos, cache_pos], axis=1)[..., None] * freqs
     cosine, sine = jnp.cos(angles), jnp.sin(angles)
     cosine = jnp.concatenate([cosine, cosine], axis=-1)
     sine = jnp.concatenate([-sine, sine], axis=-1)
 
-    blocks = LEVELS * cache_rows // tok + LEVELS
     query, kv = pl.pallas_call(
         project_kernel,
         out_shape=(
             jax.ShapeDtypeStruct((LEVELS, 4, tok, HD), jnp.bfloat16),
-            jax.ShapeDtypeStruct((blocks, tok, 2 * HD), jnp.bfloat16),
+            jax.ShapeDtypeStruct((LEVELS, tok + REC_PAD, 2 * HD), jnp.bfloat16),
         ),
-        in_specs=[SMEM] + [VMEM] * 30,
+        in_specs=[SMEM] + [VMEM] * 19,
         out_specs=(VMEM, VMEM),
         scratch_shapes=[pltpu.VMEM((LEVELS * (tok + REC_PAD), 2 * width), jnp.bfloat16)],
         compiler_params=PARAMS,
         name="project",
-    )(where, *acts, *weights, *caches, cosine, sine)
+    )(where, *acts, *gathered, cosine, sine)
+
+    kv_mine, kv_near, kv_pair = in_plane(kv[None])
+    old_rows = [
+        pl.BlockSpec(
+            (a.shape[0], CACHED // 2, a.shape[2]), lambda i: (0, depth // (CACHED // 2), 0)
+        )
+        for a in gathered
+    ]
+
+    def whole(shape):
+        return pl.BlockSpec(shape, lambda i: (0,) * len(shape))
 
     attended = pl.pallas_call(
         attend_kernel,
+        grid=(1,),
         out_shape=jax.ShapeDtypeStruct((LEVELS * tok, 4 * HD), jnp.bfloat16),
-        in_specs=[SMEM] + [VMEM] * 5,
-        out_specs=VMEM,
+        in_specs=[SMEM]
+        + [whole(a.shape) for a in (query, kv_mine, kv_near, kv_pair)]
+        + old_rows,
+        out_specs=whole((LEVELS * tok, 4 * HD)),
+        scratch_shapes=[pltpu.VMEM((PLANE, LEVELS * CACHED, 2 * HD), jnp.bfloat16)],
         compiler_params=PARAMS,
         name="attend",
-    )(where, query, *in_plane(kv))
-
-    out_weights = []
-    for d in range(LEVELS):
-        piece = out_of((level + d) % LEVELS)
-        if d:
-            piece = up(piece, d)
-        out_weights += in_plane(piece)
+    )(where, query, kv_mine, kv_near, kv_pair, *gathered)
+
+    w_out, kv_pair = lax.optimization_barrier((w_out, kv_pair))
+    out_weights = in_plane(w_out[None])
+    heads = [attended]
+    for k in range(1, LEVELS):
+        heads.append(up(heads[-1], 1))
+    part = tok // 2
+    wide_cols = PLANE * w_out.shape[1]
     mine, other = pl.pallas_call(
         output_kernel,
         out_shape=(
-            jax.ShapeDtypeStruct((LEVELS * tok, width), jnp.float32),
-            jax.ShapeDtypeStruct((LEVELS * tok, width), jnp.bfloat16),
+            jax.ShapeDtypeStruct((LEVELS, part, wide_cols), jnp.float32),
+            jax.ShapeDtypeStruct((LEVELS, part, wide_cols), jnp.bfloat16),
         ),
-        in_specs=[SMEM] + [VMEM] * 17,
+        in_specs=[SMEM] + [VMEM] * (LEVELS + 3),
         out_specs=(VMEM, VMEM),
         compiler_params=PARAMS,
         name="output",
-    )(where, attended, *out_weights)
-    summed = (mine + other_core(other).astype(jnp.float32)).reshape(LEVELS, tok, width)
-    result = lax.dynamic_index_in_dim(summed, level, 0, keepdims=False)
-    for d in range(1, LEVELS):
+    )(where, *heads, *out_weights)
+    summed = (mine + other_core(other).astype(jnp.float32)).astype(jnp.bfloat16)
+    columns = []
+    for d in range(LEVELS):
         block = lax.dynamic_index_in_dim(summed, (level + d) % LEVELS, 0, keepdims=False)
-        result = result + up(block.astype(jnp.bfloat16), d).astype(jnp.float32)
-    return result.astype(jnp.bfloat16)
+        columns.append(up(block, d) if d else block)
+    by_level = jnp.stack(columns)[(level - jnp.arange(LEVELS, dtype=jnp.int32)) % LEVELS]
+    halves = by_level.reshape(2, LEVELS // 2, part, wide_cols)
+    keep = lax.dynamic_index_in_dim(halves, core, 0, keepdims=False)
+    give = lax.dynamic_index_in_dim(halves, 1 - core, 0, keepdims=False)
+    got = other_core(give)
+    top = jnp.where(core == 0, keep, got)
+    low = jnp.where(core == 0, got, keep)
+    both = jnp.stack([top, low])
+    return jnp.transpose(both, (0, 2, 1, 3)).reshape(tok, width)
 
 
 def solution(mesh):
@@ -502,8 +567,8 @@
             and kv_local == LEVELS
             and args[1].shape[0] == 2 * TILE_RUN
             and args[0].shape[0] == 2048
-            and args[8].shape[0] == 1024
-            and args[10].shape[0] == 128
+            and args[8].shape[0] == LEVELS * PLANE * CACHED
+            and args[10].shape[0] == LEVELS * PLANE * REC
         )
         return jax.shard_map(
             by_levels if levels_fit else on_device,

time: 263 us -> 238 us (0.905)
  starting transfers between devices: 58 us -> 42.3 us
  waiting for transfers between devices: 145 us -> 154 us
  other arithmetic: 15.4 us -> 9 us
  Pallas kernels: 27.3 us -> 21.6 us
  local copies, waits for them, and re-layouts: 11.2 us -> 7.07 us
    ppermute x48 -> x29, starting transfers between devices: 47.8 us -> 27.8 us  [permuted(): return lax.ppermute(value, ('seq', 'head'), perm)]
    ppermute x4, waiting for transfers between devices: 0.01 us -> 16.9 us  [by_levels(): received.append(lax.ppermute(picture_rows, ('seq', 'head'), perm))]
    ppermute x48 -> x29, waiting for transfers between devices: 145 us -> 137 us  [permuted(): return lax.ppermute(value, ('seq', 'head'), perm)]
    pallas_call x2, Pallas kernels: 18.9 us -> 13.8 us  [the longest x1 9.82 us: by_levels(): pl.pallas_call(attend_kernel, grid=(1,), out_shape=jax.ShapeDtypeStruct((...]
    ppermute x4, starting transfers between devices: 10.2 us -> 14.6 us  [by_levels(): received.append(lax.ppermute(picture_rows, ('seq', 'head'), perm))]
    add x2 -> x1, other arithmetic: 3.5 us -> 0.01 us  [by_levels(): CACHED * LEVELS * PLANE + blocks * tok]
    convert_element_type x4, other arithmetic: 3.6 us -> 0.94 us  [the longest x1 0.66 us: by_levels(): slots = (recompute_slots - seq_index * CACHED).astype(jnp.bfloat16)]
  transfers between devices with their start and end apart: 52 -> 33, of which waited for: 22 -> 21; matrix products, arithmetic and copies ran while one was open for 6% -> 5% of each run, Pallas kernels for 7% -> 4%
where the time goes in v2:
time: 238 us; the launch traced here: 235 us
  waiting for transfers between devices  154 us (65%)
  starting transfers between devices  42.3 us (18%)
  Pallas kernels  21.6 us (9%)
  other arithmetic  9 us (4%)
  local copies, waits for them, and re-layouts  7.07 us (3%)
    ppermute x29, waiting for transfers between devices, permuted(): return lax.ppermute(value, ('seq', 'head'), perm)  137 us
    ppermute x29, starting transfers between devices, permuted(): return lax.ppermute(value, ('seq', 'head'), perm)  27.8 us
    ppermute x4, waiting for transfers between devices, by_levels(): received.append(lax.ppermute(picture_rows, ('seq', 'head'), perm))  16.9 us
    ppermute x4, starting transfers between devices, by_levels(): received.append(lax.ppermute(picture_rows, ('seq', 'head'), perm))  14.6 us
    pallas_call x1, Pallas kernels, by_levels(): pl.pallas_call(attend_kernel, grid=(1,), out_shape=jax.ShapeDtypeStruct((...  9.82 us
    pallas_call x1, Pallas kernels, by_levels(): pl.pallas_call(project_kernel, out_shape=(jax.ShapeDtypeStruct((LEVELS, 4...  7.75 us
  transfers between devices with their start and end apart: 33, of which 21 were waited for; matrix products, arithmetic and copies ran while one was open for 5% of the time, Pallas kernels for 4%

profile of v2, /device:TPU:8, one launch (start us, length us, event | category | flops | bytes accessed | tf_op | source)
XLA Modules:
  0.0 234.5 jit_solution(16278883245048489553)
XLA Ops:
  0.0 0.8 collective-permute-start.3
  0.8 1.3 collective-permute-start.2
  2.1 1.3 collective-permute-start.1
  3.4 11.1 %collective-permute-start = (bf16[32,2048]{1,0:T(8,128)(2,1)}, bf16[32,2048]{1,0:T(8,128)(2,1)}, u32[]{:S(2)}, u32[]{:S(2)}) collective-permute-start(bf16[32,2048]{1,0:T(8,128)(2,1)} %param.14), channel_id=1, source_target_pairs={{0,16},{1,17},{8,18},{9,19},{16,28},{17,29},{24,30},{25,31}} | collective-permute-start | bytes 393224 | tf_op jit(solution)/shard_map/ppermute | solution.py:436
  14.6 0.7 subtract_convert_fusion
  15.2 0.8 constant_dynamic-slice_fusion.1
  16.1 1.1 constant_dynamic-slice_fusion.3
  17.3 0.1 constant_dynamic-slice_fusion.5
  17.7 0.8 fusion.36
  18.6 0.7 compare_reduce_fusion
  19.3 16.9 %collective-permute-done = bf16[32,2048]{1,0:T(8,128)(2,1)} collective-permute-done((bf16[32,2048]{1,0:T(8,128)(2,1)}, bf16[32,2048]{1,0:T(8,128)(2,1)}, u32[]{:S(2)}, u32[]{:S(2)}) %collective-permute-start) | collective-permute-done | bytes 131104 | tf_op jit(solution)/shard_map/ppermute | solution.py:436
  36.2 1.8 maximum_select_fusion
  38.0 0.3 fusion
  38.4 1.1 collective-permute-done.4
  39.5 5.5 %collective-permute-done.17 = bf16[1,288,768]{2,1,0:T(8,128)(2,1)S(1)} collective-permute-done((bf16[1,288,768]{2,1,0:T(8,128)(2,1)S(1)}, bf16[1,288,768]{2,1,0:T(8,128)(2,1)S(1)}, u32[]{:S(2)}, u32[]{:S(2)}) %collective-permute-start.17) | collective-permute-done | bytes 442400 | tf_op jit(solution)/shard_map/ppermute | solution.py:200
  45.2 0.4 fusion.2.refs_0_
  45.7 3.9 %collective-permute-start.14 = (bf16[1,288,768]{2,1,0:T(8,128)(2,1)}, bf16[1,288,768]{2,1,0:T(8,128)(2,1)S(1)}, u32[]{:S(2)}, u32[]{:S(2)}) collective-permute-start(bf16[1,288,768]{2,1,0:T(8,128)(2,1)} %get-tuple-element.42), channel_id=1, source_target_pairs={{0,8},{1,9},{2,10},{3,11},{4,12},{5,13},{6,14},{7,15},{8,16},{9,17... | collective-permute-start | bytes 1327112 | tf_op jit(solution)/shard_map/ppermute | solution.py:200
  49.6 2.0 collective-permute-start.12
  51.6 10.3 %collective-permute-done.6.refs_2_ = bf16[144,2048]{1,0:T(8,128)(2,1)S(1)} collective-permute-done((bf16[144,2048]{1,0:T(8,128)(2,1)S(1)}, bf16[144,2048]{1,0:T(8,128)(2,1)S(1)}, u32[]{:S(2)}, u32[]{:S(2)}) %collective-permute-start.6) | collective-permute-done | bytes 589856 | tf_op jit(solution)/shard_map/ppermute | solution.py:200
  61.9 1.5 collective-permute-start.8
  63.4 1.5 pad_maximum_fusion.1
  64.9 6.5 %collective-permute-done.14.refs_11_.refs_6_ = bf16[1,288,768]{2,1,0:T(8,128)(2,1)S(1)} collective-permute-done((bf16[1,288,768]{2,1,0:T(8,128)(2,1)}, bf16[1,288,768]{2,1,0:T(8,128)(2,1)S(1)}, u32[]{:S(2)}, u32[]{:S(2)}) %collective-permute-start.14) | collective-permute-done | bytes 442400 | tf_op jit(solution)/shard_map/ppermute | solution.py:200
  71.4 2.0 collective-permute-start.15
  73.5 9.2 %collective-permute-done.8.refs_4_ = bf16[144,2048]{1,0:T(8,128)(2,1)} collective-permute-done((bf16[144,2048]{1,0:T(8,128)(2,1)S(1)}, bf16[144,2048]{1,0:T(8,128)(2,1)}, u32[]{:S(2)}, u32[]{:S(2)}) %collective-permute-start.8) | collective-permute-done | bytes 589856 | tf_op jit(solution)/shard_map/ppermute | solution.py:200
  82.7 1.4 collective-permute-start.10
  84.1 0.4 collective-permute-done.15.refs_12_.refs_7_
  84.6 2.1 collective-permute-start.16
  86.9 11.6 %collective-permute-done.10.refs_6_ = bf16[144,2048]{1,0:T(8,128)(2,1)S(1)} collective-permute-done((bf16[144,2048]{1,0:T(8,128)(2,1)}, bf16[144,2048]{1,0:T(8,128)(2,1)S(1)}, u32[]{:S(2)}, u32[]{:S(2)}) %collective-permute-start.10) | collective-permute-done | bytes 589856 | tf_op jit(solution)/shard_map/ppermute | solution.py:200
  98.6 1.4 fusion.39
  100.0 0.2 pad_maximum_fusion.10.refs_17_
  100.2 0.2 pad_maximum_fusion.11.refs_18_
  100.4 1.5 collective-permute-done.13.refs_10_.refs_5_
  101.8 9.5 %collective-permute-done.16.refs_13_.refs_8_ = bf16[2,288,768]{2,1,0:T(8,128)(2,1)S(1)} collective-permute-done((bf16[2,288,768]{2,1,0:T(8,128)(2,1)S(1)}, bf16[2,288,768]{2,1,0:T(8,128)(2,1)S(1)}, u32[]{:S(2)}, u32[]{:S(2)}) %collective-permute-start.16) | collective-permute-done | bytes 884768 | tf_op jit(solution)/shard_map/ppermute | solution.py:200
  111.4 0.9 copy-done.3
  112.2 0.2 copy-done.10
  112.4 0.2 copy-done.11
  112.6 7.7 %project.1 = (bf16[4,4,128,128]{3,2,1,0:T(8,128)(2,1)S(1)}, bf16[4,144,256]{2,1,0:T(8,128)(2,1)S(1)}) custom-call(s32[3]{0:T(128)S(1)} %pad_add_fusion.where_ref, bf16[144,2048]{1,0:T(8,128)(2,1)S(1)} %fusion.2.refs_0_, bf16[144,2048]{1,0:T(8,128)(2,1)S(1)} %collective-permute-done.5.refs_1_, bf16[144,2048]{1,0:T(8,128)(2,1)S(1)} %collective-permute-done.6.refs_2_, ...), custom_call_target="tpu_custom_call" | custom-call | tf_op jit(solution)/shard_map/project/pallas_call | solution.py:490
  120.4 2.1 collective-permute-start.21
  122.5 6.9 %collective-permute-done.21.refs_1_ = bf16[1,4,144,256]{3,2,1,0:T(8,128)(2,1)S(1)} collective-permute-done((bf16[1,4,144,256]{3,2,1,0:T(8,128)(2,1)S(1)}, bf16[1,4,144,256]{3,2,1,0:T(8,128)(2,1)S(1)}, u32[]{:S(2)}, u32[]{:S(2)}) %collective-permute-start.21) | collective-permute-done | bytes 294944 | tf_op jit(solution)/shard_map/ppermute | solution.py:200
  129.5 13.0 %collective-permute-done.22.refs_2_ = bf16[2,4,144,256]{3,2,1,0:T(8,128)(2,1)S(1)} collective-permute-done((bf16[2,4,144,256]{3,2,1,0:T(8,128)(2,1)S(1)}, bf16[2,4,144,256]{3,2,1,0:T(8,128)(2,1)S(1)}, u32[]{:S(2)}, u32[]{:S(2)}) %collective-permute-start.22) | collective-permute-done | bytes 589856 | tf_op jit(solution)/shard_map/ppermute | solution.py:200
  142.5 3.2 %collective-permute-start.26 = (bf16[1,2048,256]{2,1,0:T(8,128)(2,1)S(1)}, bf16[1,2048,256]{2,1,0:T(8,128)(2,1)S(1)}, u32[]{:S(2)}, u32[]{:S(2)}) collective-permute-start(bf16[1,2048,256]{2,1,0:T(8,128)(2,1)S(1)} %bitcast.43), channel_id=1, source_target_pairs={{0,2},{1,5},{2,0},{3,7},{4,6},{5,1},{6,4},{7,3},{8,10},{9,13},{10,... | collective-permute-start | bytes 3145736 | tf_op jit(solution)/shard_map/ppermute | solution.py:200
  145.7 16.9 %collective-permute-done.26.refs_5_ = bf16[1,2048,256]{2,1,0:T(8,128)(2,1)S(1)} collective-permute-done((bf16[1,2048,256]{2,1,0:T(8,128)(2,1)S(1)}, bf16[1,2048,256]{2,1,0:T(8,128)(2,1)S(1)}, u32[]{:S(2)}, u32[]{:S(2)}) %collective-permute-start.26) | collective-permute-done | bytes 1048608 | tf_op jit(solution)/shard_map/ppermute | solution.py:200
  162.6 0.2 pad_maximum_fusion
  162.8 9.8 %attend.1.refs_0_ = bf16[512,512]{1,0:T(8,128)(2,1)S(1)} custom-call(s32[3]{0:T(128)S(1)} %pad_add_fusion.where_ref, bf16[4,4,128,128]{3,2,1,0:T(8,128)(2,1)S(1)} %get-tuple-element.10.query_ref, bf16[1,4,144,256]{3,2,1,0:T(8,128)(2,1)S(1)} %bitcast.48, bf16[1,4,144,256]{3,2,1,0:T(8,128)(2,1)S(1)} %collective-permute-done.21.refs_1_, ...), custom_call_target="tpu_custom_call" | custom-call | tf_op jit(solution)/shard_map/attend/pallas_call | solution.py:514
  172.7 0.2 collective-permute-start.23
  172.9 12.3 %collective-permute-done.23.refs_1_ = bf16[512,512]{1,0:T(8,128)(2,1)S(1)} collective-permute-done((bf16[512,512]{1,0:T(8,128)(2,1)S(1)}, bf16[512,512]{1,0:T(8,128)(2,1)S(1)}, u32[]{:S(2)}, u32[]{:S(2)}) %collective-permute-start.23) | collective-permute-done | bytes 524320 | tf_op jit(solution)/shard_map/ppermute | solution.py:200
  185.2 1.7 collective-permute-start.24
  186.9 11.5 %collective-permute-done.24.refs_2_ = bf16[512,512]{1,0:T(8,128)(2,1)S(1)} collective-permute-done((bf16[512,512]{1,0:T(8,128)(2,1)S(1)}, bf16[512,512]{1,0:T(8,128)(2,1)S(1)}, u32[]{:S(2)}, u32[]{:S(2)}) %collective-permute-start.24) | collective-permute-done | bytes 524320 | tf_op jit(solution)/shard_map/ppermute | solution.py:200
  198.3 1.6 collective-permute-start.25
  200.0 8.1 %collective-permute-done.25.refs_3_ = bf16[512,512]{1,0:T(8,128)(2,1)S(1)} collective-permute-done((bf16[512,512]{1,0:T(8,128)(2,1)S(1)}, bf16[512,512]{1,0:T(8,128)(2,1)S(1)}, u32[]{:S(2)}, u32[]{:S(2)}) %collective-permute-start.25) | collective-permute-done | bytes 524320 | tf_op jit(solution)/shard_map/ppermute | solution.py:200
  208.0 1.3 copy-done.7
  209.4 4.0 %output.1 = (f32[4,64,1024]{2,1,0:T(8,128)S(1)}, bf16[4,64,1024]{2,1,0:T(8,128)(2,1)S(1)}) custom-call(s32[3]{0:T(128)S(1)} %pad_add_fusion.where_ref, bf16[512,512]{1,0:T(8,128)(2,1)S(1)} %attend.1.refs_0_, bf16[512,512]{1,0:T(8,128)(2,1)S(1)} %collective-permute-done.23.refs_1_, bf16[512,512]{1,0:T(8,128)(2,1)S(1)} %collective-permute-done.24.refs_2_, ...), custom_call_target="tpu_custom_call" | custom-call | tf_op jit(solution)/shard_map/output/pallas_call | solution.py:534
  213.5 1.9 collective-permute-done.28
  215.4 0.1 add_convert_fusion
  215.6 3.9 %collective-permute-start.31 = (bf16[64,1024]{1,0:T(8,128)(2,1)S(1)}, bf16[64,1024]{1,0:T(8,128)(2,1)S(1)}, u32[]{:S(2)}, u32[]{:S(2)}) collective-permute-start(bf16[64,1024]{1,0:T(8,128)(2,1)S(1)} %get-tuple-element.22), channel_id=1, source_target_pairs={{0,24},{1,25},{2,26},{3,27},{4,28},{5,29},{6,30},{7,31},{8,0},{9,1... | collective-permute-start | bytes 393224 | tf_op jit(solution)/shard_map/ppermute | solution.py:200
  219.4 1.5 collective-permute-start.29
  221.0 2.6 %collective-permute-done.31 = bf16[64,1024]{1,0:T(8,128)(2,1)S(1)} collective-permute-done((bf16[64,1024]{1,0:T(8,128)(2,1)S(1)}, bf16[64,1024]{1,0:T(8,128)(2,1)S(1)}, u32[]{:S(2)}, u32[]{:S(2)}) %collective-permute-start.31) | collective-permute-done | bytes 131104 | tf_op jit(solution)/shard_map/ppermute | solution.py:200
  223.7 4.3 %collective-permute-done.30 = bf16[64,1024]{1,0:T(8,128)(2,1)S(1)} collective-permute-done((bf16[64,1024]{1,0:T(8,128)(2,1)S(1)}, bf16[64,1024]{1,0:T(8,128)(2,1)S(1)}, u32[]{:S(2)}, u32[]{:S(2)}) %collective-permute-start.30) | collective-permute-done | bytes 131104 | tf_op jit(solution)/shard_map/ppermute | solution.py:200
  227.9 2.7 %collective-permute-done.29 = bf16[64,1024]{1,0:T(8,128)(2,1)S(1)} collective-permute-done((bf16[64,1024]{1,0:T(8,128)(2,1)S(1)}, bf16[64,1024]{1,0:T(8,128)(2,1)S(1)}, u32[]{:S(2)}, u32[]{:S(2)}) %collective-permute-start.29) | collective-permute-done | bytes 131104 | tf_op jit(solution)/shard_map/ppermute | solution.py:200
  230.7 0.6 gather_fusion
  231.3 0.1 collective-permute-start.32
  231.4 1.5 collective-permute-done.32
  233.0 0.5 copy.13
  233.6 0.9 copy.14
  (83 shorter events, 1.7 us)
Async XLA Ops:
  0.0 17.3 %copy-start.8 = (bf16[256,2048]{1,0:T(8,128)(2,1)S(1)}, bf16[256,2048]{1,0:T(8,128)(2,1)}, u32[]{:S(2)}) copy-start(bf16[256,2048]{1,0:T(8,128)(2,1)} %param.16) | copy-start | bytes 3145732
  0.0 19.3 %collective-permute-start.3 = (bf16[32,2048]{1,0:T(8,128)(2,1)}, bf16[32,2048]{1,0:T(8,128)(2,1)S(1)}, u32[]{:S(2)}, u32[]{:S(2)}) collective-permute-start(bf16[32,2048]{1,0:T(8,128)(2,1)} %param.14), channel_id=1, source_target_pairs={{6,16},{7,17},{14,18},{15,19},{22,28},{23,29},{30,30},{31,31}} | collective-permute-start | bytes 393224 | tf_op jit(solution)/shard_map/ppermute | solution.py:436
  0.8 18.5 %collective-permute-start.2 = (bf16[32,2048]{1,0:T(8,128)(2,1)}, bf16[32,2048]{1,0:T(8,128)(2,1)}, u32[]{:S(2)}, u32[]{:S(2)}) collective-permute-start(bf16[32,2048]{1,0:T(8,128)(2,1)} %param.14), channel_id=1, source_target_pairs={{4,16},{5,17},{12,18},{13,19},{20,28},{21,29},{28,30},{29,31}} | collective-permute-start | bytes 393224 | tf_op jit(solution)/shard_map/ppermute | solution.py:436
  2.1 17.2 %collective-permute-start.1 = (bf16[32,2048]{1,0:T(8,128)(2,1)}, bf16[32,2048]{1,0:T(8,128)(2,1)}, u32[]{:S(2)}, u32[]{:S(2)}) collective-permute-start(bf16[32,2048]{1,0:T(8,128)(2,1)} %param.14), channel_id=1, source_target_pairs={{2,16},{3,17},{10,18},{11,19},{18,28},{19,29},{26,30},{27,31}} | collective-permute-start | bytes 393224 | tf_op jit(solution)/shard_map/ppermute | solution.py:436
  3.4 32.8 %collective-permute-start = (bf16[32,2048]{1,0:T(8,128)(2,1)}, bf16[32,2048]{1,0:T(8,128)(2,1)}, u32[]{:S(2)}, u32[]{:S(2)}) collective-permute-start(bf16[32,2048]{1,0:T(8,128)(2,1)} %param.14), channel_id=1, source_target_pairs={{0,16},{1,17},{8,18},{9,19},{16,28},{17,29},{24,30},{25,31}} | collective-permute-start | bytes 393224 | tf_op jit(solution)/shard_map/ppermute | solution.py:436
  17.6 1.1 copy-start.14
  17.6 18.6 %copy-start.12 = (bf16[128,2048]{1,0:T(8,128)(2,1)S(1)}, bf16[128,2048]{1,0:T(8,128)(2,1)}, u32[]{:S(2)}) copy-start(bf16[128,2048]{1,0:T(8,128)(2,1)} %param.13) | copy-start | bytes 1572868
  17.6 27.5 %collective-permute-start.17 = (bf16[1,288,768]{2,1,0:T(8,128)(2,1)S(1)}, bf16[1,288,768]{2,1,0:T(8,128)(2,1)S(1)}, u32[]{:S(2)}, u32[]{:S(2)}) collective-permute-start(bf16[1,288,768]{2,1,0:T(8,128)(2,1)S(1)} %get-tuple-element.43), channel_id=1, source_target_pairs={{0,16},{1,17},{2,18},{3,19},{4,20},{5,21},{6,22},{7,23},{8,24},{9,... | collective-permute-start | bytes 1327112 | tf_op jit(solution)/shard_map/ppermute | solution.py:200
  18.5 19.5 %copy-start.13 = (bf16[8,2048]{1,0:T(8,128)(2,1)S(1)}, bf16[8,2048]{1,0:T(8,128)(2,1)}, u32[]{:S(2)}) copy-start(bf16[8,2048]{1,0:T(8,128)(2,1)} %param.22) | copy-start | bytes 98308
  19.3 25.8 %collective-permute-start.18 = (bf16[1,288,768]{2,1,0:T(8,128)(2,1)S(1)}, bf16[1,288,768]{2,1,0:T(8,128)(2,1)S(1)}, u32[]{:S(2)}, u32[]{:S(2)}) collective-permute-start(bf16[1,288,768]{2,1,0:T(8,128)(2,1)S(1)} %get-tuple-element.41), channel_id=1, source_target_pairs={{0,24},{1,25},{2,26},{3,27},{4,28},{5,29},{6,30},{7,31},{8,0},{9,1... | collective-permute-start | bytes 1327112 | tf_op jit(solution)/shard_map/ppermute | solution.py:200
  38.3 1.2 collective-permute-start.4
  38.4 6.8 %dynamic-slice-start = ((f32[4096]{0:T(1024)}, s32[]{:T(128)}), f32[2048]{0:T(1024)S(1)}, s32[]{:S(2)}) async-start(f32[4096]{0:T(1024)} %param.15, s32[]{:T(128)} %select_n.142), calls=%async_computation | async-start | bytes 16896 | tf_op jit(solution)/shard_map/dynamic_slice | solution.py:470
  45.1 16.8 %copy-start.6 = (bf16[2,288,768]{2,1,0:T(8,128)(2,1)}, bf16[2,288,768]{2,1,0:T(8,128)(2,1)S(1)}, u32[]{:S(2)}) copy-start(bf16[2,288,768]{2,1,0:T(8,128)(2,1)S(1)} %constant_dynamic-update-slice_fusion.refs_14_.refs_9_) | copy-start | bytes 2654212
  45.1 18.3 %collective-permute-start.19 = (bf16[2,288,768]{2,1,0:T(8,128)(2,1)S(1)}, bf16[2,288,768]{2,1,0:T(8,128)(2,1)S(1)}, u32[]{:S(2)}, u32[]{:S(2)}) collective-permute-start(bf16[2,288,768]{2,1,0:T(8,128)(2,1)S(1)} %constant_dynamic-update-slice_fusion.refs_14_.refs_9_), channel_id=1, source_target_pairs={{0,2},{1,5},{2,0},{3,7},{4,6},{5,1},{6,4},{7,3},{8,10},{9,13},{10,... | collective-permute-start | bytes 2654216 | tf_op jit(solution)/shard_map/ppermute | solution.py:200
  45.6 16.3 %collective-permute-start.6 = (bf16[144,2048]{1,0:T(8,128)(2,1)S(1)}, bf16[144,2048]{1,0:T(8,128)(2,1)S(1)}, u32[]{:S(2)}, u32[]{:S(2)}) collective-permute-start(bf16[144,2048]{1,0:T(8,128)(2,1)S(1)} %fusion.2.refs_0_), channel_id=1, source_target_pairs={{0,8},{1,9},{2,10},{3,11},{4,12},{5,13},{6,14},{7,15},{8,16},{9,17... | collective-permute-start | bytes 1769480 | tf_op jit(solution)/shard_map/ppermute | solution.py:200
  45.7 25.7 %collective-permute-start.14 = (bf16[1,288,768]{2,1,0:T(8,128)(2,1)}, bf16[1,288,768]{2,1,0:T(8,128)(2,1)S(1)}, u32[]{:S(2)}, u32[]{:S(2)}) collective-permute-start(bf16[1,288,768]{2,1,0:T(8,128)(2,1)} %get-tuple-element.42), channel_id=1, source_target_pairs={{0,8},{1,9},{2,10},{3,11},{4,12},{5,13},{6,14},{7,15},{8,16},{9,17... | collective-permute-start | bytes 1327112 | tf_op jit(solution)/shard_map/ppermute | solution.py:200
  49.6 23.9 %collective-permute-start.12 = (bf16[1,288,768]{2,1,0:T(8,128)(2,1)S(1)}, bf16[1,288,768]{2,1,0:T(8,128)(2,1)S(1)}, u32[]{:S(2)}, u32[]{:S(2)}) collective-permute-start(bf16[1,288,768]{2,1,0:T(8,128)(2,1)S(1)} %get-tuple-element.44.refs_8_.refs_3_), channel_id=1, source_target_pairs={{0,2},{1,5},{2,0},{3,7},{4,6},{5,1},{6,4},{7,3},{8,10},{9,13},{10,... | collective-permute-start | bytes 1327112 | tf_op jit(solution)/shard_map/ppermute | solution.py:200
  61.9 20.8 %collective-permute-start.8 = (bf16[144,2048]{1,0:T(8,128)(2,1)S(1)}, bf16[144,2048]{1,0:T(8,128)(2,1)}, u32[]{:S(2)}, u32[]{:S(2)}) collective-permute-start(bf16[144,2048]{1,0:T(8,128)(2,1)S(1)} %collective-permute-done.6.refs_2_), channel_id=1, source_target_pairs={{0,8},{1,9},{2,10},{3,11},{4,12},{5,13},{6,14},{7,15},{8,16},{9,17... | collective-permute-start | bytes 1769480 | tf_op jit(solution)/shard_map/ppermute | solution.py:200
  63.4 1.5 copy-start.5
  64.9 46.5 %collective-permute-start.20 = (bf16[4,288,768]{2,1,0:T(8,128)(2,1)}, bf16[4,288,768]{2,1,0:T(8,128)(2,1)}, u32[]{:S(2)}, u32[]{:S(2)}) collective-permute-start(bf16[4,288,768]{2,1,0:T(8,128)(2,1)} %pad_maximum_fusion.1), channel_id=1, source_target_pairs={{0,4},{1,3},{2,6},{3,1},{4,0},{5,7},{6,2},{7,5},{8,12},{9,11},{10,... | collective-permute-start | bytes 5308424 | tf_op jit(solution)/shard_map/ppermute | solution.py:200
  64.9 19.7 %collective-permute-start.5 = (bf16[144,2048]{1,0:T(8,128)(2,1)S(1)}, bf16[144,2048]{1,0:T(8,128)(2,1)S(1)}, u32[]{:S(2)}, u32[]{:S(2)}) collective-permute-start(bf16[144,2048]{1,0:T(8,128)(2,1)S(1)} %fusion.2.refs_0_), channel_id=1, source_target_pairs={{0,1},{1,0},{2,3},{3,2},{4,5},{5,4},{6,7},{7,6},{8,9},{9,8},{10,11... | collective-permute-start | bytes 1769480 | tf_op jit(solution)/shard_map/ppermute | solution.py:200
  71.4 13.1 %collective-permute-start.15 = (bf16[1,288,768]{2,1,0:T(8,128)(2,1)S(1)}, bf16[1,288,768]{2,1,0:T(8,128)(2,1)S(1)}, u32[]{:S(2)}, u32[]{:S(2)}) collective-permute-start(bf16[1,288,768]{2,1,0:T(8,128)(2,1)S(1)} %collective-permute-done.14.refs_11_.refs_6_), channel_id=1, source_target_pairs={{0,2},{1,5},{2,0},{3,7},{4,6},{5,1},{6,4},{7,3},{8,10},{9,13},{10,... | collective-permute-start | bytes 1327112 | tf_op jit(solution)/shard_map/ppermute | solution.py:200
  73.5 13.3 %collective-permute-start.7 = (bf16[144,2048]{1,0:T(8,128)(2,1)S(1)}, bf16[144,2048]{1,0:T(8,128)(2,1)S(1)}, u32[]{:S(2)}, u32[]{:S(2)}) collective-permute-start(bf16[144,2048]{1,0:T(8,128)(2,1)S(1)} %collective-permute-done.6.refs_2_), channel_id=1, source_target_pairs={{0,1},{1,0},{2,3},{3,2},{4,5},{5,4},{6,7},{7,6},{8,9},{9,8},{10,11... | collective-permute-start | bytes 1769480 | tf_op jit(solution)/shard_map/ppermute | solution.py:200
  82.7 15.8 %collective-permute-start.10 = (bf16[144,2048]{1,0:T(8,128)(2,1)}, bf16[144,2048]{1,0:T(8,128)(2,1)S(1)}, u32[]{:S(2)}, u32[]{:S(2)}) collective-permute-start(bf16[144,2048]{1,0:T(8,128)(2,1)} %collective-permute-done.8.refs_4_), channel_id=1, source_target_pairs={{0,8},{1,9},{2,10},{3,11},{4,12},{5,13},{6,14},{7,15},{8,16},{9,17... | collective-permute-start | bytes 1769480 | tf_op jit(solution)/shard_map/ppermute | solution.py:200
  84.5 17.3 %collective-permute-start.13 = (bf16[2,288,768]{2,1,0:T(8,128)(2,1)S(1)}, bf16[2,288,768]{2,1,0:T(8,128)(2,1)S(1)}, u32[]{:S(2)}, u32[]{:S(2)}) collective-permute-start(bf16[2,288,768]{2,1,0:T(8,128)(2,1)S(1)} %pad_maximum_fusion.6), channel_id=1, source_target_pairs={{0,4},{1,3},{2,6},{3,1},{4,0},{5,7},{6,2},{7,5},{8,12},{9,11},{10,... | collective-permute-start | bytes 2654216 | tf_op jit(solution)/shard_map/ppermute | solution.py:200
  84.6 26.7 %collective-permute-start.16 = (bf16[2,288,768]{2,1,0:T(8,128)(2,1)S(1)}, bf16[2,288,768]{2,1,0:T(8,128)(2,1)S(1)}, u32[]{:S(2)}, u32[]{:S(2)}) collective-permute-start(bf16[2,288,768]{2,1,0:T(8,128)(2,1)S(1)} %pad_maximum_fusion.7), channel_id=1, source_target_pairs={{0,4},{1,3},{2,6},{3,1},{4,0},{5,7},{6,2},{7,5},{8,12},{9,11},{10,... | collective-permute-start | bytes 2654216 | tf_op jit(solution)/shard_map/ppermute | solution.py:200
  86.8 24.5 %collective-permute-start.9 = (bf16[144,2048]{1,0:T(8,128)(2,1)}, bf16[144,2048]{1,0:T(8,128)(2,1)S(1)}, u32[]{:S(2)}, u32[]{:S(2)}) collective-permute-start(bf16[144,2048]{1,0:T(8,128)(2,1)} %collective-permute-done.8.refs_4_), channel_id=1, source_target_pairs={{0,1},{1,0},{2,3},{3,2},{4,5},{5,4},{6,7},{7,6},{8,9},{9,8},{10,11... | collective-permute-start | bytes 1769480 | tf_op jit(solution)/shard_map/ppermute | solution.py:200
  98.5 1.9 copy-start.9
  98.5 12.9 %collective-permute-start.11 = (bf16[144,2048]{1,0:T(8,128)(2,1)S(1)}, bf16[144,2048]{1,0:T(8,128)(2,1)S(1)}, u32[]{:S(2)}, u32[]{:S(2)}) collective-permute-start(bf16[144,2048]{1,0:T(8,128)(2,1)S(1)} %collective-permute-done.10.refs_6_), channel_id=1, source_target_pairs={{0,1},{1,0},{2,3},{3,2},{4,5},{5,4},{6,7},{7,6},{8,9},{9,8},{10,11... | collective-permute-start | bytes 1769480 | tf_op jit(solution)/shard_map/ppermute | solution.py:200
  101.8 9.5 %copy-start.1 = (bf16[2,288,768]{2,1,0:T(8,128)(2,1)}, bf16[2,288,768]{2,1,0:T(8,128)(2,1)S(1)}, u32[]{:S(2)}) copy-start(bf16[2,288,768]{2,1,0:T(8,128)(2,1)S(1)} %collective-permute-done.13.refs_10_.refs_5_) | copy-start | bytes 2654212
  111.3 0.9 copy-start.3
  111.3 1.1 copy-start.10
  111.3 1.3 copy-start.11
  120.4 22.1 %copy-start = (bf16[2048,256]{1,0:T(8,128)(2,1)S(1)}, bf16[2048,256]{1,0:T(8,128)(2,1)}, u32[]{:S(2)}) copy-start(bf16[2048,256]{1,0:T(8,128)(2,1)} %param.19) | copy-start | bytes 3145732
  120.4 9.0 %collective-permute-start.21 = (bf16[1,4,144,256]{3,2,1,0:T(8,128)(2,1)S(1)}, bf16[1,4,144,256]{3,2,1,0:T(8,128)(2,1)S(1)}, u32[]{:S(2)}, u32[]{:S(2)}) collective-permute-start(bf16[1,4,144,256]{3,2,1,0:T(8,128)(2,1)S(1)} %bitcast.46), channel_id=1, source_target_pairs={{0,2},{1,5},{2,0},{3,7},{4,6},{5,1},{6,4},{7,3},{8,10},{9,13},{10,... | collective-permute-start | bytes 884744 | tf_op jit(solution)/shard_map/ppermute | solution.py:200
  129.4 13.0 %collective-permute-start.22 = (bf16[2,4,144,256]{3,2,1,0:T(8,128)(2,1)S(1)}, bf16[2,4,144,256]{3,2,1,0:T(8,128)(2,1)S(1)}, u32[]{:S(2)}, u32[]{:S(2)}) collective-permute-start(bf16[2,4,144,256]{3,2,1,0:T(8,128)(2,1)S(1)} %pad_maximum_fusion.8), channel_id=1, source_target_pairs={{0,4},{1,3},{2,6},{3,1},{4,0},{5,7},{6,2},{7,5},{8,12},{9,11},{10,... | collective-permute-start | bytes 1769480 | tf_op jit(solution)/shard_map/ppermute | solution.py:200
  142.4 20.4 %copy-start.2 = (bf16[2,288,768]{2,1,0:T(8,128)(2,1)S(1)}, bf16[2,288,768]{2,1,0:T(8,128)(2,1)}, u32[]{:S(2)}) copy-start(bf16[2,288,768]{2,1,0:T(8,128)(2,1)} %copy-done.1) | copy-start | bytes 2654212
  142.4 20.4 %copy-start.4 = (bf16[2,288,768]{2,1,0:T(8,128)(2,1)S(1)}, bf16[2,288,768]{2,1,0:T(8,128)(2,1)}, u32[]{:S(2)}) copy-start(bf16[2,288,768]{2,1,0:T(8,128)(2,1)} %copy-done.3) | copy-start | bytes 2654212
  142.5 20.1 %collective-permute-start.26 = (bf16[1,2048,256]{2,1,0:T(8,128)(2,1)S(1)}, bf16[1,2048,256]{2,1,0:T(8,128)(2,1)S(1)}, u32[]{:S(2)}, u32[]{:S(2)}) collective-permute-start(bf16[1,2048,256]{2,1,0:T(8,128)(2,1)S(1)} %bitcast.43), channel_id=1, source_target_pairs={{0,2},{1,5},{2,0},{3,7},{4,6},{5,1},{6,4},{7,3},{8,10},{9,13},{10,... | collective-permute-start | bytes 3145736 | tf_op jit(solution)/shard_map/ppermute | solution.py:200
  162.8 45.3 %collective-permute-start.27 = (bf16[2,2048,256]{2,1,0:T(8,128)(2,1)S(1)}, bf16[2,2048,256]{2,1,0:T(8,128)(2,1)S(1)}, u32[]{:S(2)}, u32[]{:S(2)}) collective-permute-start(bf16[2,2048,256]{2,1,0:T(8,128)(2,1)S(1)} %pad_maximum_fusion), channel_id=1, source_target_pairs={{0,4},{1,3},{2,6},{3,1},{4,0},{5,7},{6,2},{7,5},{8,12},{9,11},{10,... | collective-permute-start | bytes 6291464 | tf_op jit(solution)/shard_map/ppermute | solution.py:200
  172.7 12.5 %collective-permute-start.23 = (bf16[512,512]{1,0:T(8,128)(2,1)S(1)}, bf16[512,512]{1,0:T(8,128)(2,1)S(1)}, u32[]{:S(2)}, u32[]{:S(2)}) collective-permute-start(bf16[512,512]{1,0:T(8,128)(2,1)S(1)} %attend.1.refs_0_), channel_id=1, source_target_pairs={{0,8},{1,9},{2,10},{3,11},{4,12},{5,13},{6,14},{7,15},{8,16},{9,17... | collective-permute-start | bytes 1572872 | tf_op jit(solution)/shard_map/ppermute | solution.py:200
  185.2 13.1 %collective-permute-start.24 = (bf16[512,512]{1,0:T(8,128)(2,1)S(1)}, bf16[512,512]{1,0:T(8,128)(2,1)S(1)}, u32[]{:S(2)}, u32[]{:S(2)}) collective-permute-start(bf16[512,512]{1,0:T(8,128)(2,1)S(1)} %collective-permute-done.23.refs_1_), channel_id=1, source_target_pairs={{0,8},{1,9},{2,10},{3,11},{4,12},{5,13},{6,14},{7,15},{8,16},{9,17... | collective-permute-start | bytes 1572872 | tf_op jit(solution)/shard_map/ppermute | solution.py:200
  198.3 9.7 %collective-permute-start.25 = (bf16[512,512]{1,0:T(8,128)(2,1)S(1)}, bf16[512,512]{1,0:T(8,128)(2,1)S(1)}, u32[]{:S(2)}, u32[]{:S(2)}) collective-permute-start(bf16[512,512]{1,0:T(8,128)(2,1)S(1)} %collective-permute-done.24.refs_2_), channel_id=1, source_target_pairs={{0,8},{1,9},{2,10},{3,11},{4,12},{5,13},{6,14},{7,15},{8,16},{9,17... | collective-permute-start | bytes 1572872 | tf_op jit(solution)/shard_map/ppermute | solution.py:200
  208.0 1.3 copy-start.7
  213.4 2.0 collective-permute-start.28
  215.6 8.1 %collective-permute-start.31 = (bf16[64,1024]{1,0:T(8,128)(2,1)S(1)}, bf16[64,1024]{1,0:T(8,128)(2,1)S(1)}, u32[]{:S(2)}, u32[]{:S(2)}) collective-permute-start(bf16[64,1024]{1,0:T(8,128)(2,1)S(1)} %get-tuple-element.22), channel_id=1, source_target_pairs={{0,24},{1,25},{2,26},{3,27},{4,28},{5,29},{6,30},{7,31},{8,0},{9,1... | collective-permute-start | bytes 393224 | tf_op jit(solution)/shard_map/ppermute | solution.py:200
  219.4 8.5 %collective-permute-start.30 = (bf16[64,1024]{1,0:T(8,128)(2,1)S(1)}, bf16[64,1024]{1,0:T(8,128)(2,1)S(1)}, u32[]{:S(2)}, u32[]{:S(2)}) collective-permute-start(bf16[64,1024]{1,0:T(8,128)(2,1)S(1)} %get-tuple-element.23), channel_id=1, source_target_pairs={{0,16},{1,17},{2,18},{3,19},{4,20},{5,21},{6,22},{7,23},{8,24},{9,... | collective-permute-start | bytes 393224 | tf_op jit(solution)/shard_map/ppermute | solution.py:200
  219.4 11.2 %collective-permute-start.29 = (bf16[64,1024]{1,0:T(8,128)(2,1)S(1)}, bf16[64,1024]{1,0:T(8,128)(2,1)S(1)}, u32[]{:S(2)}, u32[]{:S(2)}) collective-permute-start(bf16[64,1024]{1,0:T(8,128)(2,1)S(1)} %get-tuple-element.24), channel_id=1, source_target_pairs={{0,8},{1,9},{2,10},{3,11},{4,12},{5,13},{6,14},{7,15},{8,16},{9,17... | collective-permute-start | bytes 393224 | tf_op jit(solution)/shard_map/ppermute | solution.py:200
  231.3 1.6 collective-permute-start.32

commit v3 on v2

--- a/solution.py
+++ b/solution.py
@@ -1,3 +1,5 @@
+import functools
+
 import jax
 import jax.numpy as jnp
 from jax import lax
@@ -204,6 +206,14 @@
     return permuted(value, lambda z, p, c: ((z + steps) % LEVELS, p, c))
 
 
+def climb(value, hop):
+    return permuted(value, lambda z, p, c: (z + 1, p, c) if hop - 1 <= z < LEVELS - 1 else None)
+
+
+def descend(value, hop):
+    return permuted(value, lambda z, p, c: (z - 1, p, c) if 0 < z <= LEVELS - hop else None)
+
+
 def other_core(value):
     return permuted(value, lambda z, p, c: (z, p, 1 - c))
 
@@ -234,40 +244,41 @@
     return lax.rem(level + LEVELS - steps, LEVELS)
 
 
-def piece_at(groups, which, steps):
-    for levels, refs in groups:
-        if steps in levels:
-            at = levels.index(steps)
-            if which < 2:
-                return refs[which].at[at]
-            return refs[2].at[(which - 2) * len(levels) + at]
-    return None
-
-
-GROUPS = ((0,), (1,), (2, 3))
-
-
-def grouped(refs):
-    return [(levels, refs[3 * i : 3 * i + 3]) for i, levels in enumerate(GROUPS)]
+GATHERED = 10
+PIECES = {
+    0: ((0, 0), (1, 0), (2, 0), (2, 1)),
+    1: ((3, 0), (4, 0), (5, 0), (5, 1)),
+    2: ((7, 0), (8, 0), (9, 0), (9, 1)),
+    3: ((3, 1), (4, 1), (6, 0), (6, 1)),
+}
+
+
+def piece_at(refs, which, steps):
+    array, index = PIECES[steps][which]
+    return refs[array].at[index]
 
 
 def turned(values, cosine, sine):
     return values * cosine + pltpu.roll(values, HD // 2, 1) * sine
 
 
-def project_kernel(where_ref, *refs):
-    acts = refs[:8]
-    groups = grouped(refs[8:17])
-    cos_ref, sin_ref, query_ref, kv_ref, x_ref = refs[17:]
+def norm_kernel(where_ref, mine_ref, other_ref, gain_ref, *out_refs):
+    out_ref = out_refs[-1]
+    core = where_ref[2]
+    width = mine_ref.shape[1]
+    mine = mine_ref[...].astype(jnp.float32)
+    other = other_ref[...].astype(jnp.float32)
+    squares = jnp.sum(mine * mine + other * other, axis=1, keepdims=True)
+    factor = lax.rsqrt(squares / D + EPSILON)
+    for values, at in ((mine, core), (other, 1 - core)):
+        to = pl.multiple_of(at * width, width)
+        out_ref[:, pl.ds(to, width)] = (values * factor * gain_ref[:, pl.ds(to, width)]).astype(
+            jnp.bfloat16
+        )
+
+
+def products(where_ref, x_ref, groups, depth):
     level, place, core = where_ref[0], where_ref[1], where_ref[2]
-    rows, width = acts[0].shape
-    tok = rows - REC_PAD
-    depth = 2 * width // (LEVELS * PLANE)
-    mine = pl.multiple_of(core * width, width)
-    others = pl.multiple_of((1 - core) * width, width)
-    for k in range(LEVELS):
-        x_ref[k * rows : (k + 1) * rows, pl.ds(mine, width)] = acts[2 * k][...]
-        x_ref[k * rows : (k + 1) * rows, pl.ds(others, width)] = acts[2 * k + 1][...]
     total = None
     for d in range(LEVELS):
         for j in range(PLANE):
@@ -279,18 +290,36 @@
                 preferred_element_type=jnp.float32,
             )
             total = part if total is None else total + part
+    return total
+
+
+def keys_kernel(where_ref, x_ref, *refs):
+    groups = refs[:GATHERED]
+    slot_refs = refs[GATHERED : GATHERED + 3]
+    cos_ref, sin_ref, kv_ref = refs[GATHERED + 3 :]
+    depth = refs[0].shape[1] - CACHED // 2
+    total = products(where_ref, x_ref, groups, depth)
+    rows = total.shape[0] // LEVELS
+    tok = rows - REC_PAD
     lane = lax.broadcasted_iota(jnp.int32, (REC, CACHED), 1)
     for k in range(LEVELS):
-        at = level_before(level, k)
+        at = where_ref[3 + k]
         block = total[k * rows : (k + 1) * rows]
         cosine, sine = cos_ref[at], sin_ref[at]
-        for h in range(4):
-            head = turned(block[:tok, h * HD : (h + 1) * HD], cosine[:tok], sine[:tok])
-            query_ref[at, h] = head.astype(jnp.bfloat16)
-        keys = turned(block[:tok, 4 * HD : 5 * HD], cosine[:tok], sine[:tok])
-        kv_ref[at, 0:tok, 0:HD] = keys.astype(jnp.bfloat16)
-        kv_ref[at, 0:tok, HD : 2 * HD] = block[:tok, 5 * HD : 6 * HD].astype(jnp.bfloat16)
-        slots = piece_at(groups, 0, k)[depth : depth + REC_PAD, 4 * HD : 4 * HD + CACHED]
+        kv_ref[0, at, 0:tok, 0:HD] = turned(block[:tok, 0:HD], cosine[:tok], sine[:tok]).astype(
+            jnp.bfloat16
+        )
+        kv_ref[0, at, 0:tok, HD : 2 * HD] = block[:tok, HD : 2 * HD].astype(jnp.bfloat16)
+        before = level_before(where_ref[0], at)
+        slots = jnp.where(
+            before == 0,
+            slot_refs[0][0, 0:REC_PAD, 0:CACHED].astype(jnp.float32),
+            jnp.where(
+                before == 2,
+                slot_refs[2][0, 0:REC_PAD, 0:CACHED].astype(jnp.float32),
+                slot_refs[1][before // 2, 0:REC_PAD, 0:CACHED].astype(jnp.float32),
+            ),
+        )
         chosen = (slots[0:REC].astype(jnp.int32) == lane).astype(jnp.float32)
         rec_cos, rec_sin = (
             jnp.dot(
@@ -301,18 +330,32 @@
             )
             for table in (cosine, sine)
         )
-        rec_keys = turned(block[tok : tok + REC, 4 * HD : 5 * HD], rec_cos, rec_sin)
-        both = jnp.concatenate([rec_keys, block[tok : tok + REC, 5 * HD : 6 * HD]], axis=1)
+        rec_keys = turned(block[tok : tok + REC, 0:HD], rec_cos, rec_sin)
+        both = jnp.concatenate([rec_keys, block[tok : tok + REC, HD : 2 * HD]], axis=1)
         both = jnp.concatenate([both, jnp.zeros_like(both)], axis=0)
-        kv_ref[at, tok : tok + REC_PAD, :] = both.astype(jnp.bfloat16)
+        kv_ref[0, at, tok : tok + REC_PAD, :] = both.astype(jnp.bfloat16)
+
+
+def queries_kernel(where_ref, x_ref, *refs):
+    groups = refs[:GATHERED]
+    cos_ref, sin_ref, query_ref = refs[GATHERED:]
+    depth = refs[0].shape[1] - CACHED // 2
+    total = products(where_ref, x_ref, groups, depth)
+    rows = total.shape[0] // LEVELS
+    tok = rows - REC_PAD
+    for k in range(LEVELS):
+        at = where_ref[3 + k]
+        cosine, sine = cos_ref[at][:tok], sin_ref[at][:tok]
+        for h in range(4):
+            head = total[k * rows : k * rows + tok, h * HD : (h + 1) * HD]
+            query_ref[at, h] = turned(head, cosine, sine).astype(jnp.bfloat16)
 
 
 def attend_kernel(where_ref, query_ref, *refs):
-    kv_mine, kv_near, kv_pair = refs[:3]
-    groups = grouped(refs[3:12])
-    out_ref, cache_ref = refs[12:]
+    kvs = [ref.at[0] for ref in refs[:4]]
+    groups = refs[4 : 4 + GATHERED]
+    out_ref, cache_ref = refs[4 + GATHERED :]
     level, place, core = where_ref[0], where_ref[1], where_ref[2]
-    kvs = (kv_mine.at[0], kv_near.at[0], kv_pair.at[0], kv_pair.at[1])
     tok = query_ref.shape[2]
     line = lax.broadcasted_iota(jnp.int32, (CACHED, 2 * HD), 0)
     for j in range(PLANE):
@@ -416,7 +459,15 @@
     seq_index = lax.axis_index("seq")
     core = lax.axis_index("head")
     level, place = seq_index // PLANE, seq_index % PLANE
-    where = jnp.stack([level, place, core]).astype(jnp.int32)
+    blocks_at = jnp.stack(
+        [
+            level,
+            jnp.where(level == 0, 1, level - 1),
+            jnp.where(level < 2, 2, jnp.where(level == 2, 3, 1)),
+            jnp.where(level < 2, 3, 0),
+        ]
+    )
+    where = jnp.concatenate([jnp.stack([level, place, core]), blocks_at]).astype(jnp.int32)
     tok, width = text_rows.shape
     depth = w_query.shape[0]
 
@@ -425,16 +476,15 @@
     first = stream_len // 2 // tok
     last = (stream_len - TILE_RUN) // tok
     owners = [first + i for i in range(tile_owners)] + [last + i for i in range(tile_owners)]
-    senders = tok // picture_rows.shape[0]
-    received = []
-    for k in range(senders):
-        perm = [
-            ((i * senders + k) * 2 + c, owner * 2 + c)
-            for i, owner in enumerate(owners)
-            for c in range(2)
-        ]
-        received.append(lax.ppermute(picture_rows, ("seq", "head"), perm))
-    placed = jnp.concatenate(received, axis=0)
+    next_pictures = permuted(picture_rows, lambda z, p, c: (z, p ^ 1, c))
+    pair = jnp.concatenate([picture_rows, next_pictures], axis=0)
+
+    def to_owner(z, p, c, place):
+        return (owners[z] // PLANE, owners[z] % PLANE, c) if p == place else None
+
+    placed = jnp.concatenate(
+        [permuted(pair, functools.partial(to_owner, place=place)) for place in (0, 2)], axis=0
+    )
     is_owner = jnp.any(seq_index == jnp.array(owners, jnp.int32))
     stream = jnp.where(is_owner, placed, text_rows)
 
@@ -454,26 +504,55 @@
         old = jnp.concatenate([old[:half], old[half:], slot_rows], axis=1)
         return jnp.concatenate([jnp.concatenate([q, k, v], axis=1), old], axis=0)[None]
 
+    def whole(shape):
+        return pl.BlockSpec(shape, lambda i: (0,) * len(shape))
+
+    block_rows = tok + REC_PAD
+
+    def normalise(normed, k, block, other):
+        return pl.pallas_call(
+            norm_kernel,
+            grid=(1,),
+            out_shape=jax.ShapeDtypeStruct((LEVELS * block_rows, 2 * width), jnp.bfloat16),
+            in_specs=[SMEM, *(whole((block_rows, width)),) * 2, whole((1, 2 * width))]
+            + [pl.BlockSpec(memory_space=pl.ANY)] * (k > 0),
+            out_specs=pl.BlockSpec((block_rows, 2 * width), lambda i: (k, 0)),
+            input_output_aliases={4: 0} if k else {},
+            compiler_params=PARAMS,
+            name="norm",
+        )(where, block, other, norm_gain[None], *([normed] if k else []))
+
     pieces = [piece_for((level + d) % LEVELS) for d in range(LEVELS)]
-    moved = [up(piece, d) if d else piece for d, piece in enumerate(pieces)]
-    gathered = []
-    for levels in GROUPS:
-        group = [moved[d] for d in levels]
-        gathered += in_plane(group[0] if len(group) == 1 else jnp.concatenate(group, axis=0))
-
     rows = jnp.concatenate(
         [stream, recompute_rows, jnp.zeros((REC_PAD - REC, width), stream.dtype)], axis=0
     )
-    wide = rows.astype(jnp.float32)
-    squares = jnp.sum(wide * wide, axis=1)
-    squares = squares + other_core(squares)
-    gain = lax.dynamic_slice_in_dim(norm_gain, core * width, width, 0)
-    held = scaled(wide, squares, gain)
-    acts = []
-    for k in range(LEVELS):
-        if k:
-            held = up(held, 1)
-        acts += [held, other_core(held)]
+    near0 = to_near(pieces[0])
+    z1, z2, z3 = (up(pieces[d], d) for d in (1, 2, 3))
+    rows, near0, z1, z3 = lax.optimization_barrier((rows, near0, z1, z3))
+    far0 = to_far(jnp.concatenate([pieces[0], near0], axis=0))
+    z13 = jnp.concatenate([z1, z3], axis=0)
+    near13 = to_near(z13)
+    u1, d1 = climb(rows, 1), descend(rows, 1)
+    u1, d1, near13, far0, z2 = lax.optimization_barrier((u1, d1, near13, far0, z2))
+    far1 = to_far(jnp.concatenate([z1, near13[0:1]], axis=0))
+    near2 = to_near(z2)
+    u2, d2 = climb(u1, 2), descend(d1, 2)
+    normed = normalise(None, 0, rows, other_core(rows))
+    block1 = jnp.where(level == 0, d1, u1)
+    other1 = other_core(block1)
+    u2, d2, normed, other1, far1, near2 = lax.optimization_barrier(
+        (u2, d2, normed, other1, far1, near2)
+    )
+    far3 = to_far(jnp.concatenate([z3, near13[1:2]], axis=0))
+    far2 = to_far(jnp.concatenate([z2, near2], axis=0))
+    u3, d3 = climb(u2, 3), descend(d2, 3)
+    normed = normalise(normed, 1, block1, other1)
+    block2 = jnp.where(level == 0, d2, jnp.where(level == 3, u2, d1))
+    normed = normalise(normed, 2, block2, other_core(block2))
+    u3, d3, normed, far3 = lax.optimization_barrier((u3, d3, normed, far3))
+    gathered = [pieces[0], near0, far0, z13, near13, far1, far3, z2, near2, far2]
+    block3 = jnp.where(level == 0, d3, jnp.where(level == 3, u3, jnp.where(level == 1, d2, u2)))
+    normed = normalise(normed, 3, block3, other_core(block3))
 
     half = HD // 2
     freqs = ROPE_BASE ** (-jnp.arange(half, dtype=jnp.float32) / half)
@@ -487,50 +566,65 @@
     cosine = jnp.concatenate([cosine, cosine], axis=-1)
     sine = jnp.concatenate([-sine, sine], axis=-1)
 
-    query, kv = pl.pallas_call(
-        project_kernel,
-        out_shape=(
-            jax.ShapeDtypeStruct((LEVELS, 4, tok, HD), jnp.bfloat16),
-            jax.ShapeDtypeStruct((LEVELS, tok + REC_PAD, 2 * HD), jnp.bfloat16),
-        ),
-        in_specs=[SMEM] + [VMEM] * 19,
-        out_specs=(VMEM, VMEM),
-        scratch_shapes=[pltpu.VMEM((LEVELS * (tok + REC_PAD), 2 * width), jnp.bfloat16)],
+    def lanes(a, width, at):
+        return pl.BlockSpec((*a.shape[:2], width), lambda i: (0, 0, at))
+
+    def old_rows(a, width, at):
+        return pl.BlockSpec(
+            (a.shape[0], CACHED // 2, width), lambda i: (0, depth // (CACHED // 2), at)
+        )
+
+    tables = [whole(cosine.shape)] * 2
+    kv = pl.pallas_call(
+        keys_kernel,
+        grid=(1,),
+        out_shape=jax.ShapeDtypeStruct((1, LEVELS, block_rows, 2 * HD), jnp.bfloat16),
+        in_specs=[SMEM, whole(normed.shape)]
+        + [lanes(a, 2 * HD, 2) for a in gathered]
+        + [old_rows(gathered[i], 2 * HD, 2) for i in (0, 3, 7)]
+        + tables,
+        out_specs=whole((1, LEVELS, block_rows, 2 * HD)),
         compiler_params=PARAMS,
-        name="project",
-    )(where, *acts, *gathered, cosine, sine)
-
-    kv_mine, kv_near, kv_pair = in_plane(kv[None])
-    old_rows = [
-        pl.BlockSpec(
-            (a.shape[0], CACHED // 2, a.shape[2]), lambda i: (0, depth // (CACHED // 2), 0)
-        )
-        for a in gathered
-    ]
-
-    def whole(shape):
-        return pl.BlockSpec(shape, lambda i: (0,) * len(shape))
-
+        name="keys",
+    )(where, normed, *gathered, gathered[0], gathered[3], gathered[7], cosine, sine)
+    kv_near, kv_far = to_near(kv), to_far(kv)
+    kv_both = to_far(kv_near)
+    query = pl.pallas_call(
+        queries_kernel,
+        grid=(1,),
+        out_shape=jax.ShapeDtypeStruct((LEVELS, 4, tok, HD), jnp.bfloat16),
+        in_specs=[SMEM, whole(normed.shape)] + [lanes(a, 4 * HD, 0) for a in gathered] + tables,
+        out_specs=whole((LEVELS, 4, tok, HD)),
+        compiler_params=PARAMS,
+        name="queries",
+    )(where, normed, *gathered, cosine, sine)
+
+    w_out, kv_both, kv_far, query = lax.optimization_barrier(
+        (w_out[None], kv_both, kv_far, query)
+    )
+    w_near = to_near(w_out)
+    kvs = (kv, kv_near, kv_far, kv_both)
     attended = pl.pallas_call(
         attend_kernel,
         grid=(1,),
         out_shape=jax.ShapeDtypeStruct((LEVELS * tok, 4 * HD), jnp.bfloat16),
-        in_specs=[SMEM]
-        + [whole(a.shape) for a in (query, kv_mine, kv_near, kv_pair)]
-        + old_rows,
+        in_specs=[SMEM, whole(query.shape)]
+        + [whole(kv.shape)] * 4
+        + [old_rows(a, 6 * HD, 0) for a in gathered],
         out_specs=whole((LEVELS * tok, 4 * HD)),
         scratch_shapes=[pltpu.VMEM((PLANE, LEVELS * CACHED, 2 * HD), jnp.bfloat16)],
         compiler_params=PARAMS,
         name="attend",
-    )(where, query, kv_mine, kv_near, kv_pair, *gathered)
-
-    w_out, kv_pair = lax.optimization_barrier((w_out, kv_pair))
-    out_weights = in_plane(w_out[None])
+    )(where, query, *kvs, *gathered)
+
     heads = [attended]
     for k in range(1, LEVELS):
         heads.append(up(heads[-1], 1))
+        if k == 1:
+            w_near, heads[1] = lax.optimization_barrier((w_near, heads[1]))
+    out_weights = [w_out, w_near, to_far(jnp.concatenate([w_out, w_near], axis=0))]
     part = tok // 2
-    wide_cols = PLANE * w_out.shape[1]
+    wide_cols = PLANE * w_out.shape[2]
     mine, other = pl.pallas_call(
         output_kernel,
         out_shape=(
@@ -543,19 +637,19 @@
         name="output",
     )(where, *heads, *out_weights)
     summed = (mine + other_core(other).astype(jnp.float32)).astype(jnp.bfloat16)
-    columns = []
-    for d in range(LEVELS):
-        block = lax.dynamic_index_in_dim(summed, (level + d) % LEVELS, 0, keepdims=False)
-        columns.append(up(block, d) if d else block)
-    by_level = jnp.stack(columns)[(level - jnp.arange(LEVELS, dtype=jnp.int32)) % LEVELS]
-    halves = by_level.reshape(2, LEVELS // 2, part, wide_cols)
-    keep = lax.dynamic_index_in_dim(halves, core, 0, keepdims=False)
-    give = lax.dynamic_index_in_dim(halves, 1 - core, 0, keepdims=False)
-    got = other_core(give)
-    top = jnp.where(core == 0, keep, got)
-    low = jnp.where(core == 0, got, keep)
-    both = jnp.stack([top, low])
-    return jnp.transpose(both, (0, 2, 1, 3)).reshape(tok, width)
+    source = (level % 2) * 2 + core
+    received = []
+    for e in range(LEVELS):
+        block = lax.dynamic_index_in_dim(summed, (source + e) % LEVELS, 0, keepdims=False)
+        received.append(
+            permuted(
+                block,
+                lambda z, p, c, e=e: (((z % 2) * 2 + c + e) % LEVELS, p, z // 2),
+            )
+        )
+    by_source = jnp.stack(received)[(level - jnp.arange(LEVELS, dtype=jnp.int32)) % LEVELS]
+    by_source = by_source.reshape(2, 2, part, wide_cols)
+    return jnp.transpose(by_source, (1, 2, 0, 3)).reshape(tok, width)
 
 
 def solution(mesh):

time: 238 us -> 233 us (0.979)
  the two profiles are of different devices: /device:TPU:8 before, /device:TPU:5 now
where the time goes in v3:
time: 233 us; the launch traced here: 232 us
  waiting for transfers between devices  113 us (48%)
  starting transfers between devices  60.2 us (26%)
  Pallas kernels  30.2 us (13%)
  other arithmetic  15.3 us (7%)
  local copies, waits for them, and re-layouts  13.1 us (6%)
    ppermute x36, waiting for transfers between devices, permuted(): return lax.ppermute(value, ('seq', 'head'), perm)  113 us
    ppermute x36, starting transfers between devices, permuted(): return lax.ppermute(value, ('seq', 'head'), perm)  60.2 us
    pallas_call x1, Pallas kernels, by_levels(): pl.pallas_call(attend_kernel, grid=(1,), out_shape=jax.ShapeDtypeStruct((...  9.84 us
    unnamed x45, local copies, waits for them, and re-layouts  8.04 us
    pallas_call x4, Pallas kernels, normalise(): pl.pallas_call(norm_kernel, grid=(1,), out_shape=jax.ShapeDtypeStruct((LE...  5.98 us
    pallas_call x1, Pallas kernels, by_levels(): pl.pallas_call(queries_kernel, grid=(1,), out_shape=jax.ShapeDtypeStruct(...  5.98 us
  transfers between devices with their start and end apart: 36, of which 16 were waited for; matrix products, arithmetic and copies ran while one was open for 6% of the time, Pallas kernels for 9%

profile of v3, /device:TPU:5, one launch (start us, length us, event | category | flops | bytes accessed | tf_op | source)
XLA Modules:
  0.0 232.4 jit_solution(8152098952112903277)
XLA Ops:
  0.0 0.9 constant_dynamic-slice_fusion
  1.0 1.1 constant_dynamic-slice_fusion.2
  3.0 0.9 fusion.33
  3.9 1.3 collective-permute-start.4
  5.2 1.2 collective-permute-start
  6.4 2.6 %collective-permute-done = bf16[32,2048]{1,0:T(8,128)(2,1)S(1)} collective-permute-done((bf16[32,2048]{1,0:T(8,128)(2,1)S(1)}, bf16[32,2048]{1,0:T(8,128)(2,1)S(1)}, u32[]{:S(2)}, u32[]{:S(2)}) %collective-permute-start) | collective-permute-done | bytes 131104 | tf_op jit(solution)/shard_map/ppermute | solution.py:202
  9.7 6.8 %collective-permute-start.2 = (bf16[64,2048]{1,0:T(8,128)(2,1)S(1)}, bf16[64,2048]{1,0:T(8,128)(2,1)S(1)}, u32[]{:S(2)}, u32[]{:S(2)}) collective-permute-start(bf16[64,2048]{1,0:T(8,128)(2,1)S(1)} %constant_dynamic-update-slice_fusion), channel_id=1, source_target_pairs={{4,16},{5,17},{12,18},{13,19},{20,28},{21,29},{28,30},{29,31}} | collective-permute-start | bytes 786440 | tf_op jit(solution)/shard_map/ppermute | solution.py:202
  17.5 2.7 %collective-permute-done.2 = bf16[64,2048]{1,0:T(8,128)(2,1)S(1)} collective-permute-done((bf16[64,2048]{1,0:T(8,128)(2,1)S(1)}, bf16[64,2048]{1,0:T(8,128)(2,1)S(1)}, u32[]{:S(2)}, u32[]{:S(2)}) %collective-permute-start.2) | collective-permute-done | bytes 262176 | tf_op jit(solution)/shard_map/ppermute | solution.py:202
  20.2 0.8 maximum_select_fusion
  20.9 1.0 maximum_maximum_fusion.mine_ref
  21.9 2.2 collective-permute-done.3.refs_1_.refs_5_
  24.1 5.5 %collective-permute-done.5 = bf16[1,288,768]{2,1,0:T(8,128)(2,1)S(1)} collective-permute-done((bf16[1,288,768]{2,1,0:T(8,128)(2,1)S(1)}, bf16[1,288,768]{2,1,0:T(8,128)(2,1)S(1)}, u32[]{:S(2)}, u32[]{:S(2)}) %collective-permute-start.5) | collective-permute-done | bytes 442400 | tf_op jit(solution)/shard_map/ppermute | solution.py:202
  29.6 1.1 pad_maximum_fusion.5
  30.9 11.2 %collective-permute-start.6 = (bf16[144,2048]{1,0:T(8,128)(2,1)}, bf16[144,2048]{1,0:T(8,128)(2,1)}, u32[]{:S(2)}, u32[]{:S(2)}) collective-permute-start(bf16[144,2048]{1,0:T(8,128)(2,1)} %maximum_maximum_fusion.mine_ref), channel_id=1, source_target_pairs={{0,8},{1,9},{2,10},{3,11},{4,12},{5,13},{6,14},{7,15},{8,16},{9,17... | collective-permute-start | bytes 1769480 | tf_op jit(solution)/shard_map/ppermute | solution.py:202
  42.1 1.3 collective-permute-start.7
  43.4 4.8 %collective-permute-start.10 = (bf16[1,288,768]{2,1,0:T(8,128)(2,1)}, bf16[1,288,768]{2,1,0:T(8,128)(2,1)S(1)}, u32[]{:S(2)}, u32[]{:S(2)}) collective-permute-start(bf16[1,288,768]{2,1,0:T(8,128)(2,1)} %get-tuple-element.85), channel_id=1, source_target_pairs={{0,16},{1,17},{2,18},{3,19},{4,20},{5,21},{6,22},{7,23},{8,24},{9,... | collective-permute-start | bytes 1327112 | tf_op jit(solution)/shard_map/ppermute | solution.py:202
  48.2 29.3 %collective-permute-done.10.refs_7_.refs_12_.refs_11_ = bf16[1,288,768]{2,1,0:T(8,128)(2,1)S(1)} collective-permute-done((bf16[1,288,768]{2,1,0:T(8,128)(2,1)}, bf16[1,288,768]{2,1,0:T(8,128)(2,1)S(1)}, u32[]{:S(2)}, u32[]{:S(2)}) %collective-permute-start.10) | collective-permute-done | bytes 442400 | tf_op jit(solution)/shard_map/ppermute | solution.py:202
  77.5 4.1 %collective-permute-start.13 = (bf16[144,2048]{1,0:T(8,128)(2,1)}, bf16[144,2048]{1,0:T(8,128)(2,1)S(1)}, u32[]{:S(2)}, u32[]{:S(2)}) collective-permute-start(bf16[144,2048]{1,0:T(8,128)(2,1)} %maximum_maximum_fusion.mine_ref), channel_id=1, source_target_pairs={{0,1},{1,0},{2,3},{3,2},{4,5},{5,4},{6,7},{7,6},{8,9},{9,8},{10,11... | collective-permute-start | bytes 1769480 | tf_op jit(solution)/shard_map/ppermute | solution.py:202
  81.6 0.9 fusion.42
  82.5 2.0 pad_maximum_fusion.6
  84.5 2.0 broadcast_select_fusion.mine_ref
  86.8 1.5 collective-permute-start.11
  88.3 1.3 collective-permute-start.12
  89.6 0.8 copy-done.5
  90.5 1.4 collective-permute-start.16
  92.5 1.1 copy-done.6
  94.2 1.8 norm.4.out_refs_0_
  96.1 6.2 %collective-permute-done.16.refs_8_.refs_12_ = bf16[1,288,768]{2,1,0:T(8,128)(2,1)} collective-permute-done((bf16[1,288,768]{2,1,0:T(8,128)(2,1)S(1)}, bf16[1,288,768]{2,1,0:T(8,128)(2,1)}, u32[]{:S(2)}, u32[]{:S(2)}) %collective-permute-start.16) | collective-permute-done | bytes 442400 | tf_op jit(solution)/shard_map/ppermute | solution.py:202
  102.3 3.0 %collective-permute-done.12 = bf16[144,2048]{1,0:T(8,128)(2,1)} collective-permute-done((bf16[144,2048]{1,0:T(8,128)(2,1)}, bf16[144,2048]{1,0:T(8,128)(2,1)}, u32[]{:S(2)}, u32[]{:S(2)}) %collective-permute-start.12) | collective-permute-done | bytes 589856 | tf_op jit(solution)/shard_map/ppermute | solution.py:202
  105.9 1.5 collective-permute-start.18
  107.4 1.3 select_select_fusion.1.mine_ref
  108.8 1.1 collective-permute-start.19
  110.0 1.1 pad_maximum_fusion.8
  111.1 1.2 collective-permute-start.22
  112.3 1.9 norm.5.out_refs_0_
  114.2 1.2 norm.6.out_refs_0_
  115.4 6.5 %collective-permute-done.18 = bf16[144,2048]{1,0:T(8,128)(2,1)S(1)} collective-permute-done((bf16[144,2048]{1,0:T(8,128)(2,1)}, bf16[144,2048]{1,0:T(8,128)(2,1)S(1)}, u32[]{:S(2)}, u32[]{:S(2)}) %collective-permute-start.18) | collective-permute-done | bytes 589856 | tf_op jit(solution)/shard_map/ppermute | solution.py:202
  121.9 1.3 select_select_fusion.mine_ref
  123.1 2.0 collective-permute-start.21
  125.1 1.5 fusion.34
  127.0 1.2 norm.7.x_ref
  128.2 2.2 copy-done
  130.3 1.0 copy-done.10
  131.3 4.4 %keys.1.refs_0_ = bf16[1,4,144,256]{3,2,1,0:T(8,128)(2,1)S(1)} custom-call(s32[7]{0:T(128)S(1)} %copy-done.8, bf16[576,4096]{1,0:T(8,128)(2,1)} %copy-done, bf16[1,288,768]{2,1,0:T(8,128)(2,1)S(1)} %get-tuple-element.88.refs_0_.refs_10_.refs_4_, bf16[1,288,768]{2,1,0:T(8,128)(2,1)S(1)} %copy-done.3, ...), custom_call_target="tpu_custom_call" | custom-call | tf_op jit(solution)/shard_map/keys/pallas_call | solution.py:578
  135.7 1.7 collective-permute-start.23
  137.4 6.2 %collective-permute-done.23.refs_1_ = bf16[1,4,144,256]{3,2,1,0:T(8,128)(2,1)S(1)} collective-permute-done((bf16[1,4,144,256]{3,2,1,0:T(8,128)(2,1)S(1)}, bf16[1,4,144,256]{3,2,1,0:T(8,128)(2,1)S(1)}, u32[]{:S(2)}, u32[]{:S(2)}) %collective-permute-start.23) | collective-permute-done | bytes 294944 | tf_op jit(solution)/shard_map/ppermute | solution.py:202
  143.9 6.0 %queries.1.query_ref = bf16[4,4,128,128]{3,2,1,0:T(8,128)(2,1)S(1)} custom-call(s32[7]{0:T(128)S(1)} %copy-done.8, bf16[576,4096]{1,0:T(8,128)(2,1)} %copy-done, bf16[1,288,768]{2,1,0:T(8,128)(2,1)S(1)} %get-tuple-element.88.refs_0_.refs_10_.refs_4_, bf16[1,288,768]{2,1,0:T(8,128)(2,1)S(1)} %copy-done.3, ...), custom_call_target="tpu_custom_call" | custom-call | tf_op jit(solution)/shard_map/queries/pallas_call | solution.py:592
  150.0 1.9 collective-permute-start.26
  151.9 9.8 %attend.1.refs_0_ = bf16[512,512]{1,0:T(8,128)(2,1)S(1)} custom-call(s32[7]{0:T(128)S(1)} %copy-done.8, bf16[4,4,128,128]{3,2,1,0:T(8,128)(2,1)S(1)} %queries.1.query_ref, bf16[1,4,144,256]{3,2,1,0:T(8,128)(2,1)S(1)} %keys.1.refs_0_, bf16[1,4,144,256]{3,2,1,0:T(8,128)(2,1)S(1)} %collective-permute-done.23.refs_1_, ...), custom_call_target="tpu_custom_call" | custom-call | tf_op jit(solution)/shard_map/attend/pallas_call | solution.py:607
  161.8 13.5 %collective-permute-done.27.refs_1_ = bf16[512,512]{1,0:T(8,128)(2,1)S(1)} collective-permute-done((bf16[512,512]{1,0:T(8,128)(2,1)S(1)}, bf16[512,512]{1,0:T(8,128)(2,1)S(1)}, u32[]{:S(2)}, u32[]{:S(2)}) %collective-permute-start.27) | collective-permute-done | bytes 524320 | tf_op jit(solution)/shard_map/ppermute | solution.py:202
  175.6 1.5 collective-permute-start.30
  177.1 13.8 %collective-permute-done.28.refs_2_ = bf16[512,512]{1,0:T(8,128)(2,1)S(1)} collective-permute-done((bf16[512,512]{1,0:T(8,128)(2,1)S(1)}, bf16[512,512]{1,0:T(8,128)(2,1)S(1)}, u32[]{:S(2)}, u32[]{:S(2)}) %collective-permute-start.28) | collective-permute-done | bytes 524320 | tf_op jit(solution)/shard_map/ppermute | solution.py:202
  190.9 12.9 %collective-permute-done.29.refs_3_ = bf16[512,512]{1,0:T(8,128)(2,1)S(1)} collective-permute-done((bf16[512,512]{1,0:T(8,128)(2,1)S(1)}, bf16[512,512]{1,0:T(8,128)(2,1)S(1)}, u32[]{:S(2)}, u32[]{:S(2)}) %collective-permute-start.29) | collective-permute-done | bytes 524320 | tf_op jit(solution)/shard_map/ppermute | solution.py:202
  203.7 1.3 copy-done.11
  205.1 4.0 %output.1 = (f32[4,64,1024]{2,1,0:T(8,128)S(1)}, bf16[4,64,1024]{2,1,0:T(8,128)(2,1)S(1)}) custom-call(s32[7]{0:T(128)S(1)} %copy-done.8, bf16[512,512]{1,0:T(8,128)(2,1)S(1)} %attend.1.refs_0_, bf16[512,512]{1,0:T(8,128)(2,1)S(1)} %collective-permute-done.27.refs_1_, bf16[512,512]{1,0:T(8,128)(2,1)S(1)} %collective-permute-done.28.refs_2_, ...), custom_call_target="tpu_custom_call" | custom-call | tf_op jit(solution)/shard_map/output/pallas_call | solution.py:628
  209.1 3.3 %collective-permute-start.31 = (bf16[4,64,1024]{2,1,0:T(8,128)(2,1)S(1)}, bf16[4,64,1024]{2,1,0:T(8,128)(2,1)S(1)}, u32[]{:S(2)}, u32[]{:S(2)}) collective-permute-start(bf16[4,64,1024]{2,1,0:T(8,128)(2,1)S(1)} %get-tuple-element.58), channel_id=1, source_target_pairs={{0,1},{1,0},{2,3},{3,2},{4,5},{5,4},{6,7},{7,6},{8,9},{9,8},{10,11... | collective-permute-start | bytes 1572872 | tf_op jit(solution)/shard_map/ppermute | solution.py:202
  212.4 1.5 collective-permute-done.31
  214.2 1.9 collective-permute-start.32
  216.1 4.5 %collective-permute-start.33 = (bf16[64,1024]{1,0:T(8,128)(2,1)S(1)}, bf16[64,1024]{1,0:T(8,128)(2,1)S(1)}, u32[]{:S(2)}, u32[]{:S(2)}) collective-permute-start(bf16[64,1024]{1,0:T(8,128)(2,1)S(1)} %get-tuple-element.68), channel_id=1, source_target_pairs={{0,8},{1,16},{2,10},{3,18},{4,12},{5,20},{6,14},{7,22},{8,24},{9,0... | collective-permute-start | bytes 393224 | tf_op jit(solution)/shard_map/ppermute | solution.py:202
  220.7 2.3 collective-permute-start.35
  223.1 0.7 collective-permute-done.33
  223.8 4.4 %collective-permute-done.34 = bf16[64,1024]{1,0:T(8,128)(2,1)S(1)} collective-permute-done((bf16[64,1024]{1,0:T(8,128)(2,1)S(1)}, bf16[64,1024]{1,0:T(8,128)(2,1)S(1)}, u32[]{:S(2)}, u32[]{:S(2)}) %collective-permute-start.34) | collective-permute-done | bytes 131104 | tf_op jit(solution)/shard_map/ppermute | solution.py:202
  228.2 2.1 collective-permute-done.35
  231.5 0.9 copy.17
  (105 shorter events, 7.7 us)
Async XLA Ops:
  0.0 2.8 %copy-start.16 = (bf16[256,2048]{1,0:T(8,128)(2,1)S(1)}, bf16[256,2048]{1,0:T(8,128)(2,1)}, u32[]{:S(2)}) copy-start(bf16[256,2048]{1,0:T(8,128)(2,1)} %param.16) | copy-start | bytes 3145732
  2.1 3.1 %copy-start.18 = (bf16[32,2048]{1,0:T(8,128)(2,1)S(1)}, bf16[32,2048]{1,0:T(8,128)(2,1)}, u32[]{:S(2)}) copy-start(bf16[32,2048]{1,0:T(8,128)(2,1)} %param.14) | copy-start | bytes 393220
  3.0 13.8 %copy-start.20 = (s32[4]{0:T(128)S(1)}, s32[4]{0:T(128)}, u32[]{:S(2)}) copy-start(s32[4]{0:T(128)} %constant.126.clone) | copy-start | bytes 52
  3.0 17.1 %copy-start.17 = (bf16[128,2048]{1,0:T(8,128)(2,1)S(1)}, bf16[128,2048]{1,0:T(8,128)(2,1)}, u32[]{:S(2)}) copy-start(bf16[128,2048]{1,0:T(8,128)(2,1)} %param.13) | copy-start | bytes 1572868
  3.9 17.0 %copy-start.19 = (bf16[8,2048]{1,0:T(8,128)(2,1)S(1)}, bf16[8,2048]{1,0:T(8,128)(2,1)}, u32[]{:S(2)}) copy-start(bf16[8,2048]{1,0:T(8,128)(2,1)} %param.22) | copy-start | bytes 98308
  3.9 18.0 %collective-permute-start.4 = (bf16[1,288,768]{2,1,0:T(8,128)(2,1)S(1)}, bf16[1,288,768]{2,1,0:T(8,128)(2,1)S(1)}, u32[]{:S(2)}, u32[]{:S(2)}) collective-permute-start(bf16[1,288,768]{2,1,0:T(8,128)(2,1)S(1)} %get-tuple-element.86), channel_id=1, source_target_pairs={{0,8},{1,9},{2,10},{3,11},{4,12},{5,13},{6,14},{7,15},{8,16},{9,17... | collective-permute-start | bytes 1327112 | tf_op jit(solution)/shard_map/ppermute | solution.py:202
  5.2 3.8 %collective-permute-start = (bf16[32,2048]{1,0:T(8,128)(2,1)S(1)}, bf16[32,2048]{1,0:T(8,128)(2,1)S(1)}, u32[]{:S(2)}, u32[]{:S(2)}) collective-permute-start(bf16[32,2048]{1,0:T(8,128)(2,1)S(1)} %copy-done.18), channel_id=1, source_target_pairs={{0,2},{1,3},{2,0},{3,1},{4,6},{5,7},{6,4},{7,5},{8,10},{9,11},{10,... | collective-permute-start | bytes 393224 | tf_op jit(solution)/shard_map/ppermute | solution.py:202
  9.0 8.4 %collective-permute-start.1 = (bf16[64,2048]{1,0:T(8,128)(2,1)S(1)}, bf16[64,2048]{1,0:T(8,128)(2,1)S(1)}, u32[]{:S(2)}, u32[]{:S(2)}) collective-permute-start(bf16[64,2048]{1,0:T(8,128)(2,1)S(1)} %constant_dynamic-update-slice_fusion), channel_id=1, source_target_pairs={{0,16},{1,17},{8,18},{9,19},{16,28},{17,29},{24,30},{25,31}} | collective-permute-start | bytes 786440 | tf_op jit(solution)/shard_map/ppermute | solution.py:202
  9.7 10.4 %collective-permute-start.2 = (bf16[64,2048]{1,0:T(8,128)(2,1)S(1)}, bf16[64,2048]{1,0:T(8,128)(2,1)S(1)}, u32[]{:S(2)}, u32[]{:S(2)}) collective-permute-start(bf16[64,2048]{1,0:T(8,128)(2,1)S(1)} %constant_dynamic-update-slice_fusion), channel_id=1, source_target_pairs={{4,16},{5,17},{12,18},{13,19},{20,28},{21,29},{28,30},{29,31}} | collective-permute-start | bytes 786440 | tf_op jit(solution)/shard_map/ppermute | solution.py:202
  16.6 7.5 %collective-permute-start.3 = (bf16[1,288,768]{2,1,0:T(8,128)(2,1)S(1)}, bf16[1,288,768]{2,1,0:T(8,128)(2,1)S(1)}, u32[]{:S(2)}, u32[]{:S(2)}) collective-permute-start(bf16[1,288,768]{2,1,0:T(8,128)(2,1)S(1)} %get-tuple-element.88.refs_0_.refs_10_.refs_4_), channel_id=1, source_target_pairs={{0,2},{1,5},{2,0},{3,7},{4,6},{5,1},{6,4},{7,3},{8,10},{9,13},{10,... | collective-permute-start | bytes 1327112 | tf_op jit(solution)/shard_map/ppermute | solution.py:202
  16.7 13.0 %collective-permute-start.5 = (bf16[1,288,768]{2,1,0:T(8,128)(2,1)S(1)}, bf16[1,288,768]{2,1,0:T(8,128)(2,1)S(1)}, u32[]{:S(2)}, u32[]{:S(2)}) collective-permute-start(bf16[1,288,768]{2,1,0:T(8,128)(2,1)S(1)} %get-tuple-element.87), channel_id=1, source_target_pairs={{0,24},{1,25},{2,26},{3,27},{4,28},{5,29},{6,30},{7,31},{8,0},{9,1... | collective-permute-start | bytes 1327112 | tf_op jit(solution)/shard_map/ppermute | solution.py:202
  21.9 21.5 %copy-start.15 = (bf16[1,288,768]{2,1,0:T(8,128)(2,1)}, bf16[1,288,768]{2,1,0:T(8,128)(2,1)S(1)}, u32[]{:S(2)}) copy-start(bf16[1,288,768]{2,1,0:T(8,128)(2,1)S(1)} %collective-permute-done.4) | copy-start | bytes 1327108
  24.1 19.3 %copy-start.2 = (bf16[1,288,768]{2,1,0:T(8,128)(2,1)}, bf16[1,288,768]{2,1,0:T(8,128)(2,1)S(1)}, u32[]{:S(2)}) copy-start(bf16[1,288,768]{2,1,0:T(8,128)(2,1)S(1)} %collective-permute-done.3.refs_1_.refs_5_) | copy-start | bytes 1327108
  29.6 1.2 copy-start.13
  30.8 50.8 %collective-permute-start.9 = (bf16[2,288,768]{2,1,0:T(8,128)(2,1)}, bf16[2,288,768]{2,1,0:T(8,128)(2,1)S(1)}, u32[]{:S(2)}, u32[]{:S(2)}) collective-permute-start(bf16[2,288,768]{2,1,0:T(8,128)(2,1)} %pad_maximum_fusion.5), channel_id=1, source_target_pairs={{0,4},{1,3},{2,6},{3,1},{4,0},{5,7},{6,2},{7,5},{8,12},{9,11},{10,... | collective-permute-start | bytes 2654216 | tf_op jit(solution)/shard_map/ppermute | solution.py:202
  30.8 50.7 %collective-permute-start.8 = (bf16[2,288,768]{2,1,0:T(8,128)(2,1)S(1)}, bf16[2,288,768]{2,1,0:T(8,128)(2,1)S(1)}, u32[]{:S(2)}, u32[]{:S(2)}) collective-permute-start(bf16[2,288,768]{2,1,0:T(8,128)(2,1)S(1)} %constant_dynamic-update-slice_fusion.2.refs_3_.refs_11_.refs_7_), channel_id=1, source_target_pairs={{0,2},{1,5},{2,0},{3,7},{4,6},{5,1},{6,4},{7,3},{8,10},{9,13},{10,... | collective-permute-start | bytes 2654216 | tf_op jit(solution)/shard_map/ppermute | solution.py:202
  30.9 50.6 %collective-permute-start.6 = (bf16[144,2048]{1,0:T(8,128)(2,1)}, bf16[144,2048]{1,0:T(8,128)(2,1)}, u32[]{:S(2)}, u32[]{:S(2)}) collective-permute-start(bf16[144,2048]{1,0:T(8,128)(2,1)} %maximum_maximum_fusion.mine_ref), channel_id=1, source_target_pairs={{0,8},{1,9},{2,10},{3,11},{4,12},{5,13},{6,14},{7,15},{8,16},{9,17... | collective-permute-start | bytes 1769480 | tf_op jit(solution)/shard_map/ppermute | solution.py:202
  42.1 39.4 %collective-permute-start.7 = (bf16[144,2048]{1,0:T(8,128)(2,1)}, bf16[144,2048]{1,0:T(8,128)(2,1)}, u32[]{:S(2)}, u32[]{:S(2)}) collective-permute-start(bf16[144,2048]{1,0:T(8,128)(2,1)} %maximum_maximum_fusion.mine_ref), channel_id=1, source_target_pairs={{8,0},{9,1},{10,2},{11,3},{12,4},{13,5},{14,6},{15,7},{16,8},{17,9... | collective-permute-start | bytes 1769480 | tf_op jit(solution)/shard_map/ppermute | solution.py:202
  43.4 34.0 %collective-permute-start.10 = (bf16[1,288,768]{2,1,0:T(8,128)(2,1)}, bf16[1,288,768]{2,1,0:T(8,128)(2,1)S(1)}, u32[]{:S(2)}, u32[]{:S(2)}) collective-permute-start(bf16[1,288,768]{2,1,0:T(8,128)(2,1)} %get-tuple-element.85), channel_id=1, source_target_pairs={{0,16},{1,17},{2,18},{3,19},{4,20},{5,21},{6,22},{7,23},{8,24},{9,... | collective-permute-start | bytes 1327112 | tf_op jit(solution)/shard_map/ppermute | solution.py:202
  77.5 12.1 %collective-permute-start.13 = (bf16[144,2048]{1,0:T(8,128)(2,1)}, bf16[144,2048]{1,0:T(8,128)(2,1)S(1)}, u32[]{:S(2)}, u32[]{:S(2)}) collective-permute-start(bf16[144,2048]{1,0:T(8,128)(2,1)} %maximum_maximum_fusion.mine_ref), channel_id=1, source_target_pairs={{0,1},{1,0},{2,3},{3,2},{4,5},{5,4},{6,7},{7,6},{8,9},{9,8},{10,11... | collective-permute-start | bytes 1769480 | tf_op jit(solution)/shard_map/ppermute | solution.py:202
  81.6 62.4 %copy-start.1 = (bf16[2,288,768]{2,1,0:T(8,128)(2,1)}, bf16[2,288,768]{2,1,0:T(8,128)(2,1)S(1)}, u32[]{:S(2)}) copy-start(bf16[2,288,768]{2,1,0:T(8,128)(2,1)S(1)} %collective-permute-done.8.refs_4_.refs_8_) | copy-start | bytes 2654212
  82.5 10.0 %copy-start.7 = (f32[4096]{0:T(1024)S(1)}, f32[4096]{0:T(1024)}, u32[]{:S(2)}) copy-start(f32[4096]{0:T(1024)} %param.15) | copy-start | bytes 49156
  84.5 20.7 %collective-permute-start.15 = (bf16[2,288,768]{2,1,0:T(8,128)(2,1)}, bf16[2,288,768]{2,1,0:T(8,128)(2,1)}, u32[]{:S(2)}, u32[]{:S(2)}) collective-permute-start(bf16[2,288,768]{2,1,0:T(8,128)(2,1)} %pad_maximum_fusion.6), channel_id=1, source_target_pairs={{0,4},{1,3},{2,6},{3,1},{4,0},{5,7},{6,2},{7,5},{8,12},{9,11},{10,... | collective-permute-start | bytes 2654216 | tf_op jit(solution)/shard_map/ppermute | solution.py:202
  86.5 15.8 %collective-permute-start.14 = (bf16[144,2048]{1,0:T(8,128)(2,1)}, bf16[144,2048]{1,0:T(8,128)(2,1)}, u32[]{:S(2)}, u32[]{:S(2)}) collective-permute-start(bf16[144,2048]{1,0:T(8,128)(2,1)} %broadcast_select_fusion.mine_ref), channel_id=1, source_target_pairs={{0,1},{1,0},{2,3},{3,2},{4,5},{5,4},{6,7},{7,6},{8,9},{9,8},{10,11... | collective-permute-start | bytes 1769480 | tf_op jit(solution)/shard_map/ppermute | solution.py:202
  86.8 15.4 %collective-permute-start.11 = (bf16[144,2048]{1,0:T(8,128)(2,1)}, bf16[144,2048]{1,0:T(8,128)(2,1)}, u32[]{:S(2)}, u32[]{:S(2)}) collective-permute-start(bf16[144,2048]{1,0:T(8,128)(2,1)} %collective-permute-done.6), channel_id=1, source_target_pairs={{8,16},{9,17},{10,18},{11,19},{12,20},{13,21},{14,22},{15,23},{16,... | collective-permute-start | bytes 1769480 | tf_op jit(solution)/shard_map/ppermute | solution.py:202
  88.3 16.9 %collective-permute-start.12 = (bf16[144,2048]{1,0:T(8,128)(2,1)}, bf16[144,2048]{1,0:T(8,128)(2,1)}, u32[]{:S(2)}, u32[]{:S(2)}) collective-permute-start(bf16[144,2048]{1,0:T(8,128)(2,1)} %collective-permute-done.7), channel_id=1, source_target_pairs={{8,0},{9,1},{10,2},{11,3},{12,4},{13,5},{14,6},{15,7},{16,8},{17,9... | collective-permute-start | bytes 1769480 | tf_op jit(solution)/shard_map/ppermute | solution.py:202
  89.6 0.9 copy-start.5
  90.5 11.8 %collective-permute-start.16 = (bf16[1,288,768]{2,1,0:T(8,128)(2,1)S(1)}, bf16[1,288,768]{2,1,0:T(8,128)(2,1)}, u32[]{:S(2)}, u32[]{:S(2)}) collective-permute-start(bf16[1,288,768]{2,1,0:T(8,128)(2,1)S(1)} %collective-permute-done.10.refs_7_.refs_12_.refs_11_), channel_id=1, source_target_pairs={{0,2},{1,5},{2,0},{3,7},{4,6},{5,1},{6,4},{7,3},{8,10},{9,13},{10,... | collective-permute-start | bytes 1327112 | tf_op jit(solution)/shard_map/ppermute | solution.py:202
  92.5 1.1 copy-start.6
  93.6 0.6 copy-start.8
  94.2 1.8 copy-start.12
  94.2 1.8 copy-start.14
  102.3 13.1 %collective-permute-start.20 = (bf16[2,288,768]{2,1,0:T(8,128)(2,1)S(1)}, bf16[2,288,768]{2,1,0:T(8,128)(2,1)S(1)}, u32[]{:S(2)}, u32[]{:S(2)}) collective-permute-start(bf16[2,288,768]{2,1,0:T(8,128)(2,1)S(1)} %pad_maximum_fusion.7), channel_id=1, source_target_pairs={{0,4},{1,3},{2,6},{3,1},{4,0},{5,7},{6,2},{7,5},{8,12},{9,11},{10,... | collective-permute-start | bytes 2654216 | tf_op jit(solution)/shard_map/ppermute | solution.py:202
  105.2 10.1 %collective-permute-start.17 = (bf16[144,2048]{1,0:T(8,128)(2,1)}, bf16[144,2048]{1,0:T(8,128)(2,1)S(1)}, u32[]{:S(2)}, u32[]{:S(2)}) collective-permute-start(bf16[144,2048]{1,0:T(8,128)(2,1)} %collective-permute-done.11), channel_id=1, source_target_pairs={{16,24},{17,25},{18,26},{19,27},{20,28},{21,29},{22,30},{23,31}} | collective-permute-start | bytes 1769480 | tf_op jit(solution)/shard_map/ppermute | solution.py:202
  105.9 15.9 %collective-permute-start.18 = (bf16[144,2048]{1,0:T(8,128)(2,1)}, bf16[144,2048]{1,0:T(8,128)(2,1)S(1)}, u32[]{:S(2)}, u32[]{:S(2)}) collective-permute-start(bf16[144,2048]{1,0:T(8,128)(2,1)} %collective-permute-done.12), channel_id=1, source_target_pairs={{8,0},{9,1},{10,2},{11,3},{12,4},{13,5},{14,6},{15,7}} | collective-permute-start | bytes 1769480 | tf_op jit(solution)/shard_map/ppermute | solution.py:202
  108.8 5.4 %collective-permute-start.19 = (bf16[144,2048]{1,0:T(8,128)(2,1)S(1)}, bf16[144,2048]{1,0:T(8,128)(2,1)S(1)}, u32[]{:S(2)}, u32[]{:S(2)}) collective-permute-start(bf16[144,2048]{1,0:T(8,128)(2,1)S(1)} %select_select_fusion.1.mine_ref), channel_id=1, source_target_pairs={{0,1},{1,0},{2,3},{3,2},{4,5},{5,4},{6,7},{7,6},{8,9},{9,8},{10,11... | collective-permute-start | bytes 1769480 | tf_op jit(solution)/shard_map/ppermute | solution.py:202
  111.1 19.2 %collective-permute-start.22 = (bf16[2,288,768]{2,1,0:T(8,128)(2,1)S(1)}, bf16[2,288,768]{2,1,0:T(8,128)(2,1)S(1)}, u32[]{:S(2)}, u32[]{:S(2)}) collective-permute-start(bf16[2,288,768]{2,1,0:T(8,128)(2,1)S(1)} %pad_maximum_fusion.8), channel_id=1, source_target_pairs={{0,4},{1,3},{2,6},{3,1},{4,0},{5,7},{6,2},{7,5},{8,12},{9,11},{10,... | collective-permute-start | bytes 2654216 | tf_op jit(solution)/shard_map/ppermute | solution.py:202
  115.4 11.4 %copy-start.9 = (bf16[2,288,768]{2,1,0:T(8,128)(2,1)}, bf16[2,288,768]{2,1,0:T(8,128)(2,1)S(1)}, u32[]{:S(2)}) copy-start(bf16[2,288,768]{2,1,0:T(8,128)(2,1)S(1)} %collective-permute-done.20.refs_6_.refs_10_) | copy-start | bytes 2654212
  123.1 3.8 %collective-permute-start.21 = (bf16[144,2048]{1,0:T(8,128)(2,1)S(1)}, bf16[144,2048]{1,0:T(8,128)(2,1)S(1)}, u32[]{:S(2)}, u32[]{:S(2)}) collective-permute-start(bf16[144,2048]{1,0:T(8,128)(2,1)S(1)} %select_select_fusion.mine_ref), channel_id=1, source_target_pairs={{0,1},{1,0},{2,3},{3,2},{4,5},{5,4},{6,7},{7,6},{8,9},{9,8},{10,11... | collective-permute-start | bytes 1769480 | tf_op jit(solution)/shard_map/ppermute | solution.py:202
  127.0 4.4 %copy-start.3 = (bf16[1,288,768]{2,1,0:T(8,128)(2,1)S(1)}, bf16[1,288,768]{2,1,0:T(8,128)(2,1)}, u32[]{:S(2)}) copy-start(bf16[1,288,768]{2,1,0:T(8,128)(2,1)} %copy-done.2) | copy-start | bytes 1327108
  128.1 2.2 copy-start
  130.3 1.0 copy-start.10
  135.7 14.3 %copy-start.4 = (bf16[2048,256]{1,0:T(8,128)(2,1)S(1)}, bf16[2048,256]{1,0:T(8,128)(2,1)}, u32[]{:S(2)}) copy-start(bf16[2048,256]{1,0:T(8,128)(2,1)} %param.19) | copy-start | bytes 3145732
  135.7 7.9 %collective-permute-start.23 = (bf16[1,4,144,256]{3,2,1,0:T(8,128)(2,1)S(1)}, bf16[1,4,144,256]{3,2,1,0:T(8,128)(2,1)S(1)}, u32[]{:S(2)}, u32[]{:S(2)}) collective-permute-start(bf16[1,4,144,256]{3,2,1,0:T(8,128)(2,1)S(1)} %keys.1.refs_0_), channel_id=1, source_target_pairs={{0,2},{1,5},{2,0},{3,7},{4,6},{5,1},{6,4},{7,3},{8,10},{9,13},{10,... | collective-permute-start | bytes 884744 | tf_op jit(solution)/shard_map/ppermute | solution.py:202
  137.4 12.5 %collective-permute-start.25 = (bf16[1,4,144,256]{3,2,1,0:T(8,128)(2,1)S(1)}, bf16[1,4,144,256]{3,2,1,0:T(8,128)(2,1)S(1)}, u32[]{:S(2)}, u32[]{:S(2)}) collective-permute-start(bf16[1,4,144,256]{3,2,1,0:T(8,128)(2,1)S(1)} %keys.1.refs_0_), channel_id=1, source_target_pairs={{0,4},{1,3},{2,6},{3,1},{4,0},{5,7},{6,2},{7,5},{8,12},{9,11},{10,... | collective-permute-start | bytes 884744 | tf_op jit(solution)/shard_map/ppermute | solution.py:202
  143.6 6.3 %collective-permute-start.24 = (bf16[1,4,144,256]{3,2,1,0:T(8,128)(2,1)S(1)}, bf16[1,4,144,256]{3,2,1,0:T(8,128)(2,1)S(1)}, u32[]{:S(2)}, u32[]{:S(2)}) collective-permute-start(bf16[1,4,144,256]{3,2,1,0:T(8,128)(2,1)S(1)} %collective-permute-done.23.refs_1_), channel_id=1, source_target_pairs={{0,4},{1,3},{2,6},{3,1},{4,0},{5,7},{6,2},{7,5},{8,12},{9,11},{10,... | collective-permute-start | bytes 884744 | tf_op jit(solution)/shard_map/ppermute | solution.py:202
  150.0 25.4 %collective-permute-start.26 = (bf16[1,2048,256]{2,1,0:T(8,128)(2,1)S(1)}, bf16[1,2048,256]{2,1,0:T(8,128)(2,1)S(1)}, u32[]{:S(2)}, u32[]{:S(2)}) collective-permute-start(bf16[1,2048,256]{2,1,0:T(8,128)(2,1)S(1)} %bitcast.36), channel_id=1, source_target_pairs={{0,2},{1,5},{2,0},{3,7},{4,6},{5,1},{6,4},{7,3},{8,10},{9,13},{10,... | collective-permute-start | bytes 3145736 | tf_op jit(solution)/shard_map/ppermute | solution.py:202
  161.7 13.6 %collective-permute-start.27 = (bf16[512,512]{1,0:T(8,128)(2,1)S(1)}, bf16[512,512]{1,0:T(8,128)(2,1)S(1)}, u32[]{:S(2)}, u32[]{:S(2)}) collective-permute-start(bf16[512,512]{1,0:T(8,128)(2,1)S(1)} %attend.1.refs_0_), channel_id=1, source_target_pairs={{0,8},{1,9},{2,10},{3,11},{4,12},{5,13},{6,14},{7,15},{8,16},{9,17... | collective-permute-start | bytes 1572872 | tf_op jit(solution)/shard_map/ppermute | solution.py:202
  175.6 28.2 %collective-permute-start.30 = (bf16[2,2048,256]{2,1,0:T(8,128)(2,1)S(1)}, bf16[2,2048,256]{2,1,0:T(8,128)(2,1)S(1)}, u32[]{:S(2)}, u32[]{:S(2)}) collective-permute-start(bf16[2,2048,256]{2,1,0:T(8,128)(2,1)S(1)} %pad_maximum_fusion), channel_id=1, source_target_pairs={{0,4},{1,3},{2,6},{3,1},{4,0},{5,7},{6,2},{7,5},{8,12},{9,11},{10,... | collective-permute-start | bytes 6291464 | tf_op jit(solution)/shard_map/ppermute | solution.py:202
  177.1 13.8 %collective-permute-start.28 = (bf16[512,512]{1,0:T(8,128)(2,1)S(1)}, bf16[512,512]{1,0:T(8,128)(2,1)S(1)}, u32[]{:S(2)}, u32[]{:S(2)}) collective-permute-start(bf16[512,512]{1,0:T(8,128)(2,1)S(1)} %collective-permute-done.27.refs_1_), channel_id=1, source_target_pairs={{0,8},{1,9},{2,10},{3,11},{4,12},{5,13},{6,14},{7,15},{8,16},{9,17... | collective-permute-start | bytes 1572872 | tf_op jit(solution)/shard_map/ppermute | solution.py:202
  190.9 12.9 %collective-permute-start.29 = (bf16[512,512]{1,0:T(8,128)(2,1)S(1)}, bf16[512,512]{1,0:T(8,128)(2,1)S(1)}, u32[]{:S(2)}, u32[]{:S(2)}) collective-permute-start(bf16[512,512]{1,0:T(8,128)(2,1)S(1)} %collective-permute-done.28.refs_2_), channel_id=1, source_target_pairs={{0,8},{1,9},{2,10},{3,11},{4,12},{5,13},{6,14},{7,15},{8,16},{9,17... | collective-permute-start | bytes 1572872 | tf_op jit(solution)/shard_map/ppermute | solution.py:202
  203.7 1.3 copy-start.11
  209.1 4.9 %collective-permute-start.31 = (bf16[4,64,1024]{2,1,0:T(8,128)(2,1)S(1)}, bf16[4,64,1024]{2,1,0:T(8,128)(2,1)S(1)}, u32[]{:S(2)}, u32[]{:S(2)}) collective-permute-start(bf16[4,64,1024]{2,1,0:T(8,128)(2,1)S(1)} %get-tuple-element.58), channel_id=1, source_target_pairs={{0,1},{1,0},{2,3},{3,2},{4,5},{5,4},{6,7},{7,6},{8,9},{9,8},{10,11... | collective-permute-start | bytes 1572872 | tf_op jit(solution)/shard_map/ppermute | solution.py:202
  214.2 8.9 %collective-permute-start.32 = (bf16[64,1024]{1,0:T(8,128)(2,1)S(1)}, bf16[64,1024]{1,0:T(8,128)(2,1)S(1)}, u32[]{:S(2)}, u32[]{:S(2)}) collective-permute-start(bf16[64,1024]{1,0:T(8,128)(2,1)S(1)} %get-tuple-element.65), channel_id=1, source_target_pairs={{0,0},{1,8},{2,2},{3,10},{4,4},{5,12},{6,6},{7,14},{8,16},{9,24},{... | collective-permute-start | bytes 393224 | tf_op jit(solution)/shard_map/ppermute | solution.py:202
  216.1 7.7 %collective-permute-start.33 = (bf16[64,1024]{1,0:T(8,128)(2,1)S(1)}, bf16[64,1024]{1,0:T(8,128)(2,1)S(1)}, u32[]{:S(2)}, u32[]{:S(2)}) collective-permute-start(bf16[64,1024]{1,0:T(8,128)(2,1)S(1)} %get-tuple-element.68), channel_id=1, source_target_pairs={{0,8},{1,16},{2,10},{3,18},{4,12},{5,20},{6,14},{7,22},{8,24},{9,0... | collective-permute-start | bytes 393224 | tf_op jit(solution)/shard_map/ppermute | solution.py:202
  220.6 7.5 %collective-permute-start.34 = (bf16[64,1024]{1,0:T(8,128)(2,1)S(1)}, bf16[64,1024]{1,0:T(8,128)(2,1)S(1)}, u32[]{:S(2)}, u32[]{:S(2)}) collective-permute-start(bf16[64,1024]{1,0:T(8,128)(2,1)S(1)} %get-tuple-element.67), channel_id=1, source_target_pairs={{0,16},{1,24},{2,18},{3,26},{4,20},{5,28},{6,22},{7,30},{8,0},{9,8... | collective-permute-start | bytes 393224 | tf_op jit(solution)/shard_map/ppermute | solution.py:202
  220.7 9.6 %collective-permute-start.35 = (bf16[64,1024]{1,0:T(8,128)(2,1)S(1)}, bf16[64,1024]{1,0:T(8,128)(2,1)S(1)}, u32[]{:S(2)}, u32[]{:S(2)}) collective-permute-start(bf16[64,1024]{1,0:T(8,128)(2,1)S(1)} %get-tuple-element.66), channel_id=1, source_target_pairs={{0,24},{1,0},{2,26},{3,2},{4,28},{5,4},{6,30},{7,6},{8,8},{9,16},{... | collective-permute-start | bytes 393224 | tf_op jit(solution)/shard_map/ppermute | solution.py:202

commit v4 on v1

--- a/solution.py
+++ b/solution.py
@@ -177,8 +177,10 @@
 
 LEVELS = 4
 PLANE = 4
+TILE_RUN = 256
+CACHED = 64
+REC = 8
 REC_PAD = 16
-TILE_RUN = 256
 
 
 def permuted(value, move):
@@ -198,6 +200,10 @@
     return lax.ppermute(value, ("seq", "head"), perm)
 
 
+def across(value, bit):
+    return permuted(value, lambda z, p, c: (z ^ bit, p, c))
+
+
 def up(value, steps):
     return permuted(value, lambda z, p, c: ((z + steps) % LEVELS, p, c))
 
@@ -206,11 +212,12 @@
     return permuted(value, lambda z, p, c: (z, p, 1 - c))
 
 
-def in_plane(piece):
-    near = permuted(piece, lambda z, p, c: (z, p ^ (1 + c), c))
-    far = permuted(piece, lambda z, p, c: (z, p ^ (2 - c), c))
-    both = permuted(near, lambda z, p, c: (z, p ^ (2 - c), c))
-    return [piece, near, far, both]
+def to_near(value):
+    return permuted(value, lambda z, p, c: (z, p ^ (1 + c), c))
+
+
+def to_far(value):
+    return permuted(value, lambda z, p, c: (z, p ^ (2 - c), c))
 
 
 def place_of(which, place, core):
@@ -221,63 +228,109 @@
     return place ^ (1 + core) if which == 1 else place ^ (2 - core)
 
 
-def project_kernel(where_ref, *refs):
-    acts = refs[:8]
-    weights = refs[8:24]
-    caches = refs[24:28]
-    cos_ref, sin_ref, query_ref, kv_ref, x_ref = refs[28:]
+def turned(values, cosine, sine):
+    return values * cosine + pltpu.roll(values, HD // 2, 1) * sine
+
+
+def products(where_ref, x_refs, pieces):
     level, place, core = where_ref[0], where_ref[1], where_ref[2]
-    rows = acts[0].shape[0]
-    depth = weights[0].shape[0]
-    width = acts[0].shape[1]
-    tok = rows - REC_PAD
-    mine = pl.multiple_of(core * width, width)
-    others = pl.multiple_of((1 - core) * width, width)
-    for k in range(LEVELS):
-        x_ref[k * rows : (k + 1) * rows, pl.ds(mine, width)] = acts[2 * k][...]
-        x_ref[k * rows : (k + 1) * rows, pl.ds(others, width)] = acts[2 * k + 1][...]
-    total = None
-    for d in range(LEVELS):
-        from_level = lax.rem(level + LEVELS - d, LEVELS)
+    totals = [None] * len(x_refs)
+    for i in range(2):
         for j in range(PLANE):
-            block = from_level * PLANE + place_of(j, place, core)
+            depth = pieces[i][j].shape[0]
+            block = lax.rem(level + i, 2) * PLANE + place_of(j, place, core)
             start = pl.multiple_of(block * depth, depth)
-            part = jnp.dot(
-                x_ref[:, pl.ds(start, depth)],
-                weights[d * PLANE + j][...],
-                preferred_element_type=jnp.float32,
-            )
-            total = part if total is None else total + part
-    for k in range(LEVELS):
-        at = lax.rem(level + LEVELS - k, LEVELS)
-        block = total[k * rows : (k + 1) * rows]
-        cosine = cos_ref[at]
-        sine = sin_ref[at]
-
-        def turned(values, cosine, sine):
-            return values * cosine + pltpu.roll(values, HD // 2, 1) * sine
-
+            weights = pieces[i][j][...]
+            for r, x_ref in enumerate(x_refs):
+                part = jnp.dot(
+                    x_ref[:, pl.ds(start, depth)], weights, preferred_element_type=jnp.float32
+                )
+                totals[r] = part if totals[r] is None else totals[r] + part
+    return totals
+
+
+def keys_part_kernel(where_ref, x0, x1, own, near, far, old0, old1, keep_ref, send_ref):
+    pieces = [[own.at[i], near.at[i], far.at[i], far.at[2 + i]] for i in range(2)]
+    rows = x0.shape[0]
+    width = 2 * HD
+    for r, total in enumerate(products(where_ref, (x0, x1), pieces)):
+        keep_ref[r * rows : (r + 1) * rows] = total[:, :width]
+        send_ref[r * rows : (r + 1) * rows] = total[:, width:].astype(jnp.bfloat16)
+    at = 2 * rows
+    for old in (old0, old1):
+        send_ref[at : at + CACHED + REC_PAD] = old[:, width:]
+        at += CACHED + REC_PAD
+
+
+def keys_join_kernel(where_ref, keep_ref, got_ref, old0, old1, cos_ref, sin_ref, kv_ref, sum_ref):
+    level = where_ref[0]
+    rows = sum_ref.shape[0]
+    block = rows // LEVELS
+    tok = block - REC_PAD
+    width = 2 * HD
+    sum_ref[...] = keep_ref[...] + got_ref[0:rows].astype(jnp.float32)
+    first = where_ref[3]
+    span = CACHED + REC_PAD
+    for n in range(LEVELS):
+        at = jnp.bitwise_xor(level, n)
+        start = pl.multiple_of(lax.rem(first + n, LEVELS) * block, 16)
+        cosine, sine = cos_ref[at], sin_ref[at]
+        fresh = sum_ref[pl.ds(start, tok), :]
+        kv_ref[2 + at, :, 0:HD] = turned(fresh[:, :HD], cosine[:tok], sine[:tok]).astype(
+            jnp.bfloat16
+        )
+        kv_ref[2 + at, :, HD:width] = fresh[:, HD:].astype(jnp.bfloat16)
+        if n < 2:
+            old = (old0, old1)[n][:, 0:width].astype(jnp.float32)
+        else:
+            old = got_ref[rows + (n - 2) * span : rows + (n - 1) * span].astype(jnp.float32)
+        slots = old[CACHED : CACHED + REC].astype(jnp.int32)
+        rec = sum_ref[pl.ds(pl.multiple_of(start + tok, 16), REC_PAD), :]
+        line = lax.broadcasted_iota(jnp.int32, (CACHED, width), 0)
+        found = jnp.zeros((CACHED, width), jnp.float32)
+        hit = jnp.zeros((CACHED, width), jnp.int32)
+        for r in range(REC):
+            same = line == slots[r : r + 1]
+            found = jnp.where(same, rec[r : r + 1], found)
+            hit = jnp.where(same, 1, hit)
+        keys = turned(found[:, :HD], cosine[tok : tok + CACHED], sine[tok : tok + CACHED])
+        found = jnp.concatenate([keys, found[:, HD:]], axis=1)
+        line_at = pl.multiple_of(lax.rem(at, 2) * CACHED, CACHED)
+        kv_ref[at // 2, pl.ds(line_at, CACHED), :] = jnp.where(
+            hit == 1, found, old[:CACHED]
+        ).astype(jnp.bfloat16)
+
+
+def queries_part_kernel(where_ref, x0, x1, *refs):
+    pieces = []
+    for own, near, far in (refs[0:3], refs[3:6]):
+        pieces.append([own.at[0], near.at[0], far.at[0], far.at[1]])
+    keep_ref, send_ref = refs[6:]
+    block = x0.shape[0] // 2
+    tok = block - REC_PAD
+    width = 4 * HD
+    for r, total in enumerate(products(where_ref, (x0, x1), pieces)):
+        for k in range(2):
+            fresh = total[k * block : k * block + tok]
+            keep_ref[2 * r + k] = fresh[:, :width]
+            send_ref[2 * r + k] = fresh[:, width:].astype(jnp.bfloat16)
+
+
+def attend_kernel(
+    where_ref, keep_ref, got_ref, cos_ref, sin_ref, kv0, kv1, kv2, kv3, out_ref, query_ref
+):
+    level, place, core = where_ref[0], where_ref[1], where_ref[2]
+    pieces = (kv0, kv1, kv2, kv3)
+    tok = keep_ref.shape[1]
+    old = LEVELS // 2
+    for n in range(LEVELS):
+        at = jnp.bitwise_xor(level, n)
+        block = lax.rem(where_ref[3] + n, LEVELS)
+        total = keep_ref[block] + got_ref[block].astype(jnp.float32)
+        cosine, sine = cos_ref[at][:tok], sin_ref[at][:tok]
         for h in range(4):
-            head = turned(block[:tok, h * HD : (h + 1) * HD], cosine[:tok], sine[:tok])
+            head = turned(total[:, h * HD : (h + 1) * HD], cosine, sine)
             query_ref[at, h] = head.astype(jnp.bfloat16)
-        keys = turned(block[:, 4 * HD : 5 * HD], cosine, sine)
-        values = block[:, 5 * HD : 6 * HD]
-        both = jnp.concatenate([keys, values], axis=1)
-        kv_ref[LEVELS * 64 // 128 + at] = both[:tok].astype(jnp.bfloat16)
-        cached = caches[k][0:64, :].astype(jnp.float32)
-        slots = caches[k][64:80, :].astype(jnp.int32)
-        row = lax.broadcasted_iota(jnp.int32, cached.shape, 0)
-        for r in range(8):
-            cached = jnp.where(row == slots[r : r + 1], both[tok + r : tok + r + 1], cached)
-        half = lax.rem(at, 2)
-        kv_ref[at // 2, pl.ds(pl.multiple_of(half * 64, 64), 64)] = cached.astype(jnp.bfloat16)
-
-
-def attend_kernel(where_ref, query_ref, kv0, kv1, kv2, kv3, out_ref):
-    place, core = where_ref[1], where_ref[2]
-    pieces = (kv0, kv1, kv2, kv3)
-    tok = query_ref.shape[2]
-    old = LEVELS // 2
     row = lax.broadcasted_iota(jnp.int32, (tok, tok), 0)
     col = lax.broadcasted_iota(jnp.int32, (tok, tok), 1)
     scale = HD ** (-0.5) * 1.4426950408889634
@@ -287,7 +340,6 @@
         scores = []
         best = None
         for j in range(PLANE):
-            theirs = place_of(j, place, core)
             keys = pieces[j][0 : old + i + 1, :, 0:HD].reshape(count, HD)
             raw = lax.dot_general(
                 queries, keys, (((1,), (1,)), ((), ())), preferred_element_type=jnp.float32
@@ -295,7 +347,7 @@
             if j == 0:
                 allowed = col <= row
             else:
-                allowed = jnp.broadcast_to(theirs, (tok, tok)) < place
+                allowed = jnp.broadcast_to(place_of(j, place, core), (tok, tok)) < place
             allowed = jnp.concatenate([allowed] * 4, axis=0)
             last = jnp.where(allowed, raw[:, count - tok :], NEG_FILL)
             raw = jnp.concatenate([raw[:, : count - tok], last], axis=1)
@@ -317,33 +369,41 @@
             ]
 
 
-def output_kernel(where_ref, attended_ref, *refs):
-    weights = refs[:16]
-    mine_ref, other_ref = refs[16:]
+def output_kernel(where_ref, own_ref, next_ref, w_own, w_near, w_far, mine_ref, other_ref):
     level, place, core = where_ref[0], where_ref[1], where_ref[2]
-    width = weights[0].shape[1]
-    half = LEVELS * PLANE // 2
-    for d in range(LEVELS):
-        from_level = lax.rem(level + LEVELS - d, LEVELS)
+    depth = own_ref.shape[1]
+    width = w_own.shape[2]
+    start = pl.multiple_of(lax.rem(level, 2) * depth, depth)
+    start_next = pl.multiple_of(lax.rem(level + 1, 2) * depth, depth)
+    for i in range(2):
         for j in range(PLANE):
-            block = from_level * PLANE + place_of(j, place, core)
-            start = pl.multiple_of(lax.rem(block, half) * width, width)
+            weights = (w_own.at[i], w_near.at[i], w_far.at[i], w_far.at[2 + i])[j]
             part = jnp.dot(
-                attended_ref[...], weights[d * PLANE + j][...], preferred_element_type=jnp.float32
+                own_ref[...], weights[pl.ds(start, depth), :], preferred_element_type=jnp.float32
+            ) + jnp.dot(
+                next_ref[...],
+                weights[pl.ds(start_next, depth), :],
+                preferred_element_type=jnp.float32,
             )
-
-            @pl.when(block // half == core)
+            to = pl.multiple_of(place_of(j, place, core) * width, width)
+            mine = (core == level // 2) if i == 0 else (core != level // 2)
+
+            @pl.when(mine)
             def _():
-                mine_ref[:, pl.ds(start, width)] = part
-
-            @pl.when(block // half != core)
+                mine_ref[:, pl.ds(to, width)] = part
+
+            @pl.when(jnp.logical_not(mine))
             def _():
-                other_ref[:, pl.ds(start, width)] = part.astype(jnp.bfloat16)
+                other_ref[:, pl.ds(to, width)] = part.astype(jnp.bfloat16)
 
 
 SMEM = pl.BlockSpec(memory_space=pltpu.SMEM)
 VMEM = pl.BlockSpec(memory_space=pltpu.VMEM)
 PARAMS = pltpu.CompilerParams(vmem_limit_bytes=48 * 1024 * 1024)
+
+
+def shaped(shape, dtype=jnp.bfloat16):
+    return jax.ShapeDtypeStruct(shape, dtype)
 
 
 def by_levels(
@@ -363,134 +423,179 @@
     seq_index = lax.axis_index("seq")
     core = lax.axis_index("head")
     level, place = seq_index // PLANE, seq_index % PLANE
-    where = jnp.stack([level, place, core]).astype(jnp.int32)
+    half_at = level // 2
+    own_first = core == half_at
+    where = jnp.stack([level, place, core, jnp.where(own_first, 0, 2)]).astype(jnp.int32)
     tok, width = text_rows.shape
-    rec = recompute_rows.shape[0]
-    cache_rows = cache_keys.shape[0]
-    depth = w_query.shape[0]
-
-    def group_of(level_at):
-        q = lax.dynamic_slice_in_dim(w_query, level_at * 4 * HD, 4 * HD, 1)
-        k = lax.dynamic_slice_in_dim(w_key, level_at * HD, HD, 1)
-        v = lax.dynamic_slice_in_dim(w_value, level_at * HD, HD, 1)
-        return jnp.concatenate([q, k, v], axis=1)
-
-    local_slots = (recompute_slots - seq_index * cache_rows).astype(jnp.bfloat16)
-    slot_rows = jnp.broadcast_to(
-        jnp.pad(local_slots, (0, REC_PAD - rec))[:, None], (REC_PAD, 2 * HD)
-    )
-
-    def cache_of(level_at):
-        k = lax.dynamic_slice_in_dim(cache_keys, level_at * HD, HD, 1)
-        v = lax.dynamic_slice_in_dim(cache_values, level_at * HD, HD, 1)
-        return jnp.concatenate([jnp.concatenate([k, v], axis=1), slot_rows], axis=0)
-
-    def out_of(level_at):
-        return lax.dynamic_slice_in_dim(w_out, level_at * 4 * HD, 4 * HD, 0)
-
-    weights, caches = [], []
-    for d in range(LEVELS):
-        to_level = (level + d) % LEVELS
-        piece, cached = group_of(to_level), cache_of(to_level)
-        if d:
-            piece, cached = up(piece, d), up(cached, d)
-        caches.append(cached)
-        weights += in_plane(piece)
+    block_rows = tok + REC_PAD
 
     stream_len = tok * LEVELS * PLANE
     tile_owners = TILE_RUN // tok
     first = stream_len // 2 // tok
     last = (stream_len - TILE_RUN) // tok
     owners = [first + i for i in range(tile_owners)] + [last + i for i in range(tile_owners)]
-    senders = tok // picture_rows.shape[0]
     received = []
-    for k in range(senders):
-        perm = [
-            ((i * senders + k) * 2 + c, owner * 2 + c)
-            for i, owner in enumerate(owners)
-            for c in range(2)
-        ]
-        received.append(lax.ppermute(picture_rows, ("seq", "head"), perm))
+    for k in range(PLANE):
+
+        def to_owner(z, p, c, k=k):
+            return (owners[z] // PLANE, owners[z] % PLANE, c) if p == k else None
+
+        received.append(permuted(picture_rows, to_owner))
     placed = jnp.concatenate(received, axis=0)
     is_owner = jnp.any(seq_index == jnp.array(owners, jnp.int32))
     stream = jnp.where(is_owner, placed, text_rows)
 
+    slots = (recompute_slots - seq_index * CACHED).astype(jnp.bfloat16)
+    slot_rows = jnp.broadcast_to(jnp.pad(slots, (0, REC_PAD - REC))[:, None], (REC_PAD, 4 * HD))
+
+    def columns(array, size, at):
+        return lax.dynamic_slice_in_dim(array, at * size, size, 1)
+
+    def key_piece(to_level):
+        def pair(k, v):
+            return [columns(a, HD, at) for at in (to_level, to_level ^ 2) for a in (k, v)]
+
+        weights = jnp.concatenate(pair(w_key, w_value), axis=1)
+        old = jnp.concatenate(pair(cache_keys, cache_values), axis=1)
+        return jnp.concatenate([weights, old, slot_rows], axis=0)
+
+    def query_piece(to_level):
+        return jnp.concatenate(
+            [columns(w_query, 4 * HD, at) for at in (to_level, to_level ^ 2)], axis=1
+        )[None]
+
+    depth = w_query.shape[0]
+    key_own = key_piece(level)
+    key_next = across(key_piece(level ^ 1), 1)
+    query_own = query_piece(level)
+    query_next = across(query_piece(level ^ 1), 1)
+    query_near = to_near(query_own)
+
     rows = jnp.concatenate(
-        [stream, recompute_rows, jnp.zeros((REC_PAD - rec, width), stream.dtype)], axis=0
+        [stream, recompute_rows, jnp.zeros((REC_PAD - REC, width), stream.dtype)], axis=0
     )
     wide = rows.astype(jnp.float32)
-    squares = jnp.sum(wide * wide, axis=1)
-    squares = squares + other_core(squares)
-    gain = lax.dynamic_slice_in_dim(norm_gain, core * width, width, 0)
-    normed = scaled(wide, squares, gain)
-
-    acts, held = [], normed
-    for k in range(LEVELS):
-        if k:
-            held = up(held, 1)
-        acts += [held, other_core(held)]
+    squares = lax.psum(jnp.sum(wide * wide, axis=1), "head")
+    normed = scaled(wide, squares, lax.dynamic_slice_in_dim(norm_gain, core * width, width, 0))
+
+    normed, key_next, query_near = lax.optimization_barrier((normed, key_next, query_near))
+    query_far = to_far(jnp.concatenate([query_own, query_near], axis=0))
+    keys = jnp.stack([key_own[:depth], key_next[:depth]])
+    old_own, old_next = key_own[depth:], key_next[depth:]
+    crossed = permuted(normed, lambda z, p, c: (z ^ 2, p, 1 - c) if c == 1 - z // 2 else None)
+    crossed, query_far, query_next = lax.optimization_barrier((crossed, query_far, query_next))
+    keys_near = to_near(keys)
+    held = jnp.where(own_first, normed, crossed)
+    next_rows = across(held, 1)
+    next_rows, keys_near = lax.optimization_barrier((next_rows, keys_near))
+    keys_far = to_far(jnp.concatenate([keys, keys_near], axis=0))
+    rows_mine = jnp.concatenate([held, next_rows], axis=0)
+    rows_other = other_core(rows_mine)
+    rows_other, keys_far = lax.optimization_barrier((rows_other, keys_far))
+    next_near = to_near(query_next)
+    next_far = to_far(jnp.concatenate([query_next, next_near], axis=0))
+
+    out_rows = w_out.shape[0] // 2
+    out_own, out_give = (
+        lax.dynamic_slice_in_dim(w_out, at * out_rows, out_rows, 0) for at in (half_at, 1 - half_at)
+    )
+    out_got = across(out_give, 2)
 
     half = HD // 2
     freqs = ROPE_BASE ** (-jnp.arange(half, dtype=jnp.float32) / half)
-    level_start = (jnp.arange(LEVELS, dtype=jnp.int32) * PLANE + place)[:, None]
+    blocks = (jnp.arange(LEVELS, dtype=jnp.int32) * PLANE + place)[:, None]
     stream_pos = (
-        cache_rows * LEVELS * PLANE + level_start * tok + jnp.arange(tok, dtype=jnp.int32)[None]
+        CACHED * LEVELS * PLANE + blocks * tok + jnp.arange(tok, dtype=jnp.int32)[None]
     ).astype(jnp.float32)
-    order = (level - jnp.arange(LEVELS, dtype=jnp.int32)) % LEVELS
-    slots = jnp.stack([c[cache_rows:, 0] for c in caches])[order].astype(jnp.float32)
-    rec_pos = slots + (level_start * cache_rows).astype(jnp.float32)
-    positions = jnp.concatenate([stream_pos, rec_pos], axis=1)
-    angles = positions[..., None] * freqs
+    cache_pos = (blocks * CACHED + jnp.arange(CACHED, dtype=jnp.int32)[None]).astype(jnp.float32)
+    angles = jnp.concatenate([stream_pos, cache_pos], axis=1)[..., None] * freqs
     cosine, sine = jnp.cos(angles), jnp.sin(angles)
     cosine = jnp.concatenate([cosine, cosine], axis=-1)
     sine = jnp.concatenate([-sine, sine], axis=-1)
 
-    blocks = LEVELS * cache_rows // tok + LEVELS
-    query, kv = pl.pallas_call(
-        project_kernel,
+    all_rows = LEVELS * block_rows
+    keep, send = pl.pallas_call(
+        keys_part_kernel,
         out_shape=(
-            jax.ShapeDtypeStruct((LEVELS, 4, tok, HD), jnp.bfloat16),
-            jax.ShapeDtypeStruct((blocks, tok, 2 * HD), jnp.bfloat16),
+            shaped((all_rows, 2 * HD), jnp.float32),
+            shaped((all_rows + 2 * (CACHED + REC_PAD), 2 * HD)),
         ),
-        in_specs=[SMEM] + [VMEM] * 30,
+        in_specs=[SMEM] + [VMEM] * 7,
         out_specs=(VMEM, VMEM),
-        scratch_shapes=[pltpu.VMEM((LEVELS * (tok + REC_PAD), 2 * width), jnp.bfloat16)],
         compiler_params=PARAMS,
-        name="project",
-    )(where, *acts, *weights, *caches, cosine, sine)
-
+        name="keys_part",
+    )(where, rows_mine, rows_other, keys, keys_near, keys_far, old_own, old_next)
+    send, rows_after, out_got = lax.optimization_barrier((send, rows_mine, out_got))
+    q_keep, q_send = pl.pallas_call(
+        queries_part_kernel,
+        out_shape=(
+            shaped((LEVELS, tok, 4 * HD), jnp.float32),
+            shaped((LEVELS, tok, 4 * HD)),
+        ),
+        in_specs=[SMEM] + [VMEM] * 8,
+        out_specs=(VMEM, VMEM),
+        compiler_params=PARAMS,
+        name="queries_part",
+    )(
+        where,
+        rows_after,
+        rows_other,
+        query_own,
+        query_near,
+        query_far,
+        query_next,
+        next_near,
+        next_far,
+    )
+    got_keys, q_send = lax.optimization_barrier((across(send, 2), q_send))
+    kv = pl.pallas_call(
+        keys_join_kernel,
+        out_shape=shaped((LEVELS // 2 + LEVELS, tok, 2 * HD)),
+        in_specs=[SMEM] + [VMEM] * 6,
+        out_specs=VMEM,
+        scratch_shapes=[pltpu.VMEM((all_rows, 2 * HD), jnp.float32)],
+        compiler_params=PARAMS,
+        name="keys_join",
+    )(where, keep, got_keys, old_own, old_next, cosine, sine)
+    kv_near, kv_far = to_near(kv), to_far(kv)
+    kv_both = to_far(kv_near)
+
+    out_pair = jnp.stack([out_own, out_got])
+    out_pair, kv_near = lax.optimization_barrier((out_pair, kv_near))
+    out_near, got_queries = lax.optimization_barrier((to_near(out_pair), across(q_send, 2)))
+    out_far = to_far(jnp.concatenate([out_pair, out_near], axis=0))
     attended = pl.pallas_call(
         attend_kernel,
-        out_shape=jax.ShapeDtypeStruct((LEVELS * tok, 4 * HD), jnp.bfloat16),
-        in_specs=[SMEM] + [VMEM] * 5,
+        out_shape=shaped((LEVELS * tok, 4 * HD)),
+        in_specs=[SMEM] + [VMEM] * 8,
         out_specs=VMEM,
+        scratch_shapes=[pltpu.VMEM((LEVELS, 4, tok, HD), jnp.bfloat16)],
         compiler_params=PARAMS,
         name="attend",
-    )(where, query, *in_plane(kv))
-
-    out_weights = []
-    for d in range(LEVELS):
-        piece = out_of((level + d) % LEVELS)
-        if d:
-            piece = up(piece, d)
-        out_weights += in_plane(piece)
+    )(where, q_keep, got_queries, cosine, sine, kv, kv_near, kv_far, kv_both)
+
+    wide_cols = PLANE * w_out.shape[1]
     mine, other = pl.pallas_call(
         output_kernel,
         out_shape=(
-            jax.ShapeDtypeStruct((LEVELS * tok, width), jnp.float32),
-            jax.ShapeDtypeStruct((LEVELS * tok, width), jnp.bfloat16),
+            shaped((LEVELS * tok, wide_cols), jnp.float32),
+            shaped((LEVELS * tok, wide_cols)),
         ),
-        in_specs=[SMEM] + [VMEM] * 17,
+        in_specs=[SMEM] + [VMEM] * 5,
         out_specs=(VMEM, VMEM),
         compiler_params=PARAMS,
         name="output",
-    )(where, attended, *out_weights)
-    summed = (mine + other_core(other).astype(jnp.float32)).reshape(LEVELS, tok, width)
-    result = lax.dynamic_index_in_dim(summed, level, 0, keepdims=False)
-    for d in range(1, LEVELS):
-        block = lax.dynamic_index_in_dim(summed, (level + d) % LEVELS, 0, keepdims=False)
-        result = result + up(block.astype(jnp.bfloat16), d).astype(jnp.float32)
-    return result.astype(jnp.bfloat16)
+    )(where, attended, across(attended, 1), out_pair, out_near, out_far)
+    summed = (mine + other_core(other).astype(jnp.float32)).reshape(LEVELS, tok, wide_cols)
+
+    def block_for(steps):
+        return lax.dynamic_index_in_dim(summed, (level + steps) % LEVELS, 0, keepdims=False)
+
+    second, first, third = (up(block_for(d).astype(jnp.bfloat16), d) for d in (2, 1, 3))
+    same = (block_for(0) + second.astype(jnp.float32)).astype(jnp.bfloat16)
+    cross = (first.astype(jnp.float32) + third.astype(jnp.float32)).astype(jnp.bfloat16)
+    even = level % 2 == 0
+    return jnp.concatenate([jnp.where(even, same, cross), jnp.where(even, cross, same)], axis=1)
 
 
 def solution(mesh):
@@ -502,8 +607,8 @@
             and kv_local == LEVELS
             and args[1].shape[0] == 2 * TILE_RUN
             and args[0].shape[0] == 2048
-            and args[8].shape[0] == 1024
-            and args[10].shape[0] == 128
+            and args[8].shape[0] == LEVELS * PLANE * CACHED
+            and args[10].shape[0] == LEVELS * PLANE * REC
         )
         return jax.shard_map(
             by_levels if levels_fit else on_device,

time: 263 us -> 249 us (0.947)
  waiting for transfers between devices: 145 us -> 136 us
  starting transfers between devices: 58 us -> 50.2 us
  other arithmetic: 15.4 us -> 19.7 us
    ppermute x4 -> x0, starting transfers between devices: 10.2 us -> none  [by_levels(): received.append(lax.ppermute(picture_rows, ('seq', 'head'), perm))]
    ppermute x48 -> x28, waiting for transfers between devices: 145 us -> 136 us  [permuted(): return lax.ppermute(value, ('seq', 'head'), perm)]
    concatenate x6 -> x9, other arithmetic: 2.38 us -> 6.82 us  [the longest x1 1.36 us: by_levels(): next_far = to_far(jnp.concatenate([query_next, next_near], axis=0))]
    convert_element_type x4 -> x3, other arithmetic: 3.6 us -> 0.8 us  [the longest x1 0.66 us: by_levels(): slots = (recompute_slots - seq_index * CACHED).astype(jnp.bfloat16)]
    another operation x1 -> x2, local copies, waits for them, and re-layouts: 0.58 us -> 3.31 us  [the longest x1 2.24 us: by_levels(): out_pair = jnp.stack([out_own, out_got])]
    ppermute x48 -> x28, starting transfers between devices: 47.8 us -> 50.2 us  [permuted(): return lax.ppermute(value, ('seq', 'head'), perm)]
    pallas_call x3 -> x5, Pallas kernels: 27.3 us -> 26.3 us  [the longest x1 8.97 us: by_levels(): pl.pallas_call(attend_kernel, out_shape=shaped((LEVELS * tok, 4 * HD)), i...]
  transfers between devices with their start and end apart: 52 -> 28, of which waited for: 22 -> 17; matrix products, arithmetic and copies ran while one was open for 6% -> 8% of each run, Pallas kernels for 7% -> 7%
where the time goes in v4:
time: 249 us; the launch traced here: 245 us
  waiting for transfers between devices  136 us (55%)
  starting transfers between devices  50.2 us (20%)
  Pallas kernels  26.3 us (11%)
  other arithmetic  19.7 us (8%)
  local copies, waits for them, and re-layouts  9.98 us (4%)
    ppermute x28, waiting for transfers between devices, permuted(): return lax.ppermute(value, ('seq', 'head'), perm)  136 us
    ppermute x28, starting transfers between devices, permuted(): return lax.ppermute(value, ('seq', 'head'), perm)  50.2 us
    pallas_call x1, Pallas kernels, by_levels(): pl.pallas_call(attend_kernel, out_shape=shaped((LEVELS * tok, 4 * HD)), i...  8.97 us
    pallas_call x1, Pallas kernels, by_levels(): pl.pallas_call(output_kernel, out_shape=(shaped((LEVELS * tok, wide_cols)...  8.71 us
  transfers between devices with their start and end apart: 28, of which 17 were waited for; matrix products, arithmetic and copies ran while one was open for 8% of the time, Pallas kernels for 7%

profile of v4, /device:TPU:8, one launch (start us, length us, event | category | flops | bytes accessed | tf_op | source)
XLA Modules:
  0.0 245.5 jit_solution(10888359359578898095)
XLA Ops:
  0.0 1.4 collective-permute-start.3
  1.4 1.3 collective-permute-start.2
  2.8 1.3 collective-permute-start.1
  4.1 11.1 %collective-permute-start = (bf16[32,2048]{1,0:T(8,128)(2,1)}, bf16[32,2048]{1,0:T(8,128)(2,1)}, u32[]{:S(2)}, u32[]{:S(2)}) collective-permute-start(bf16[32,2048]{1,0:T(8,128)(2,1)} %param.14), channel_id=1, source_target_pairs={{0,16},{1,17},{8,18},{9,19},{16,28},{17,29},{24,30},{25,31}} | collective-permute-start | bytes 393224 | tf_op jit(solution)/shard_map/ppermute | solution.py:200
  15.8 1.5 constant_dynamic-slice_fusion.3
  17.3 1.1 constant_dynamic-slice_fusion.7
  18.5 0.8 pad_maximum_fusion.10
  19.9 0.7 compare_reduce_fusion
  20.9 1.9 maximum_select_fusion
  23.1 2.5 %psum.7 = f32[144]{0:T(256)S(1)} all-reduce(f32[144]{0:T(256)S(1)} %fusion), channel_id=1, replica_groups=mesh['seq'=16,'head'=2] {'head'}, use_global_device_ids=true, to_apply=%region_2.3 | all-reduce | flops 144 | bytes 1152 | tf_op jit(solution)/shard_map/psum | solution.py:478
  25.6 1.1 fusion.2
  26.7 1.9 collective-permute-done.4
  28.5 1.5 collective-permute-done.5.refs_1_
  30.0 1.2 pad_maximum_fusion.2
  31.2 1.5 collective-permute-start.6
  32.7 0.9 maximum_bitcast_fusion.1
  33.6 1.5 collective-permute-start.8
  35.1 1.1 slice_bitcast_fusion
  36.2 15.8 %collective-permute-done.8.refs_3_ = bf16[1,256,1024]{2,1,0:T(8,128)(2,1)} collective-permute-done((bf16[1,256,1024]{2,1,0:T(8,128)(2,1)}, bf16[1,256,1024]{2,1,0:T(8,128)(2,1)}, u32[]{:S(2)}, u32[]{:S(2)}) %collective-permute-start.8) | collective-permute-done | bytes 524320 | tf_op jit(solution)/shard_map/ppermute | solution.py:200
  52.0 1.0 broadcast_select_fusion
  53.0 2.5 %collective-permute-start.9 = (bf16[144,2048]{1,0:T(8,128)(2,1)}, bf16[144,2048]{1,0:T(8,128)(2,1)S(1)}, u32[]{:S(2)}, u32[]{:S(2)}) collective-permute-start(bf16[144,2048]{1,0:T(8,128)(2,1)} %broadcast_select_fusion), channel_id=1, source_target_pairs={{0,8},{1,9},{2,10},{3,11},{4,12},{5,13},{6,14},{7,15},{8,0},{9,1},... | collective-permute-start | bytes 1769480 | tf_op jit(solution)/shard_map/ppermute | solution.py:200
  55.6 1.1 collective-permute-start.10
  56.7 2.2 dynamic-slice_bitcast_fusion
  59.0 4.4 %collective-permute-start.13 = (bf16[1024,256]{1,0:T(8,128)(2,1)}, bf16[1024,256]{1,0:T(8,128)(2,1)}, u32[]{:S(2)}, u32[]{:S(2)}) collective-permute-start(bf16[1024,256]{1,0:T(8,128)(2,1)} %get-tuple-element.61), channel_id=1, source_target_pairs={{0,16},{1,17},{2,18},{3,19},{4,20},{5,21},{6,22},{7,23},{8,24},{9,... | collective-permute-start | bytes 1572872 | tf_op jit(solution)/shard_map/ppermute | solution.py:200
  63.4 1.4 collective-permute-done.10.near
  64.8 0.8 copy-done.2
  65.7 8.7 %collective-permute-done.9 = bf16[144,2048]{1,0:T(8,128)(2,1)S(1)} collective-permute-done((bf16[144,2048]{1,0:T(8,128)(2,1)}, bf16[144,2048]{1,0:T(8,128)(2,1)S(1)}, u32[]{:S(2)}, u32[]{:S(2)}) %collective-permute-start.9) | collective-permute-done | bytes 589856 | tf_op jit(solution)/shard_map/ppermute | solution.py:200
  74.3 1.2 pad_maximum_fusion.1.x0
  75.7 1.3 pad_maximum_fusion.3
  77.6 1.4 pad_maximum_fusion.4
  79.0 1.5 collective-permute-start.15
  80.7 0.9 slice.7.old1
  81.6 10.5 %collective-permute-done.12.far = bf16[4,256,512]{2,1,0:T(8,128)(2,1)} collective-permute-done((bf16[4,256,512]{2,1,0:T(8,128)(2,1)}, bf16[4,256,512]{2,1,0:T(8,128)(2,1)}, u32[]{:S(2)}, u32[]{:S(2)}) %collective-permute-start.12) | collective-permute-done | bytes 1048608 | tf_op jit(solution)/shard_map/ppermute | solution.py:200
  92.1 3.1 %keys_part.1 = (f32[576,256]{1,0:T(8,128)S(1)}, bf16[736,256]{1,0:T(8,128)(2,1)S(1)}) custom-call(s32[4]{0:T(128)S(1)} %pad_add_fusion.where_ref, bf16[288,2048]{1,0:T(8,128)(2,1)S(1)} %pad_maximum_fusion.1.x0, bf16[288,2048]{1,0:T(8,128)(2,1)S(1)} %collective-permute-done.11.x1, bf16[2,256,512]{2,1,0:T(8,128)(2,1)S(1)} %pad_maximum_fusion.6.own, ...), custom_call_target="tpu_custom_call" | custom-call | tf_op jit(solution)/shard_map/keys_part/pallas_call | solution.py:517
  95.2 2.4 collective-permute-start.16
  97.6 1.4 fusion.7
  99.4 3.8 %collective-permute-done.15.refs_5_ = bf16[2,256,1024]{2,1,0:T(8,128)(2,1)S(1)} collective-permute-done((bf16[2,256,1024]{2,1,0:T(8,128)(2,1)S(1)}, bf16[2,256,1024]{2,1,0:T(8,128)(2,1)S(1)}, u32[]{:S(2)}, u32[]{:S(2)}) %collective-permute-start.15) | collective-permute-done | bytes 1048608 | tf_op jit(solution)/shard_map/ppermute | solution.py:200
  103.2 4.5 %queries_part.1 = (f32[4,128,512]{2,1,0:T(8,128)S(1)}, bf16[4,128,512]{2,1,0:T(8,128)(2,1)S(1)}) custom-call(s32[4]{0:T(128)S(1)} %pad_add_fusion.where_ref, bf16[288,2048]{1,0:T(8,128)(2,1)} %copy-done, bf16[288,2048]{1,0:T(8,128)(2,1)} %copy-done.1, bf16[1,256,1024]{2,1,0:T(8,128)(2,1)S(1)} %maximum_bitcast_fusion.refs_0_, ...), custom_call_target="tpu_custom_call" | custom-call | tf_op jit(solution)/shard_map/queries_part/pallas_call | solution.py:529
  107.8 5.5 %collective-permute-done.16.got_ref = bf16[736,256]{1,0:T(8,128)(2,1)S(1)} collective-permute-done((bf16[736,256]{1,0:T(8,128)(2,1)S(1)}, bf16[736,256]{1,0:T(8,128)(2,1)S(1)}, u32[]{:S(2)}, u32[]{:S(2)}) %collective-permute-start.16) | collective-permute-done | bytes 376864 | tf_op jit(solution)/shard_map/ppermute | solution.py:200
  113.3 1.0 keys_join.1.kv0
  114.3 1.6 collective-permute-start.17
  115.9 1.1 pad_maximum_fusion.5.w_own
  117.1 5.1 %collective-permute-done.17.kv1 = bf16[6,128,256]{2,1,0:T(8,128)(2,1)S(1)} collective-permute-done((bf16[6,128,256]{2,1,0:T(8,128)(2,1)S(1)}, bf16[6,128,256]{2,1,0:T(8,128)(2,1)S(1)}, u32[]{:S(2)}, u32[]{:S(2)}) %collective-permute-start.17) | collective-permute-done | bytes 393248 | tf_op jit(solution)/shard_map/ppermute | solution.py:200
  122.2 1.5 collective-permute-start.18
  123.7 3.4 %collective-permute-start.19 = (bf16[4,128,512]{2,1,0:T(8,128)(2,1)S(1)}, bf16[4,128,512]{2,1,0:T(8,128)(2,1)S(1)}, u32[]{:S(2)}, u32[]{:S(2)}) collective-permute-start(bf16[4,128,512]{2,1,0:T(8,128)(2,1)S(1)} %get-tuple-element.49), channel_id=1, source_target_pairs={{0,16},{1,17},{2,18},{3,19},{4,20},{5,21},{6,22},{7,23},{8,24},{9,... | collective-permute-start | bytes 1572872 | tf_op jit(solution)/shard_map/ppermute | solution.py:200
  127.1 19.8 %collective-permute-done.19.got_ref = bf16[4,128,512]{2,1,0:T(8,128)(2,1)S(1)} collective-permute-done((bf16[4,128,512]{2,1,0:T(8,128)(2,1)S(1)}, bf16[4,128,512]{2,1,0:T(8,128)(2,1)S(1)}, u32[]{:S(2)}, u32[]{:S(2)}) %collective-permute-start.19) | collective-permute-done | bytes 524320 | tf_op jit(solution)/shard_map/ppermute | solution.py:200
  147.0 1.8 collective-permute-start.23
  149.1 1.7 collective-permute-start.21
  150.8 26.5 %collective-permute-done.20.kv2 = bf16[6,128,256]{2,1,0:T(8,128)(2,1)S(1)} collective-permute-done((bf16[6,128,256]{2,1,0:T(8,128)(2,1)S(1)}, bf16[6,128,256]{2,1,0:T(8,128)(2,1)S(1)}, u32[]{:S(2)}, u32[]{:S(2)}) %collective-permute-start.20) | collective-permute-done | bytes 393248 | tf_op jit(solution)/shard_map/ppermute | solution.py:200
  177.4 4.2 %collective-permute-done.21.kv3 = bf16[6,128,256]{2,1,0:T(8,128)(2,1)S(1)} collective-permute-done((bf16[6,128,256]{2,1,0:T(8,128)(2,1)S(1)}, bf16[6,128,256]{2,1,0:T(8,128)(2,1)S(1)}, u32[]{:S(2)}, u32[]{:S(2)}) %collective-permute-start.21) | collective-permute-done | bytes 393248 | tf_op jit(solution)/shard_map/ppermute | solution.py:200
  181.6 9.0 %attend.1.own_ref = bf16[512,512]{1,0:T(8,128)(2,1)S(1)} custom-call(s32[4]{0:T(128)S(1)} %pad_add_fusion.where_ref, f32[4,128,512]{2,1,0:T(8,128)S(1)} %get-tuple-element.42.keep_ref, bf16[4,128,512]{2,1,0:T(8,128)(2,1)S(1)} %collective-permute-done.19.got_ref, f32[4,192,128]{2,1,0:T(8,128)S(1)} %pad_maximum_fusion.8.cos_ref, ...), custom_call_target="tpu_custom_call" | custom-call | tf_op jit(solution)/shard_map/attend/pallas_call | solution.py:567
  190.5 2.3 collective-permute-start.22
  192.8 11.2 %collective-permute-done.22.next_ref = bf16[512,512]{1,0:T(8,128)(2,1)S(1)} collective-permute-done((bf16[512,512]{1,0:T(8,128)(2,1)S(1)}, bf16[512,512]{1,0:T(8,128)(2,1)S(1)}, u32[]{:S(2)}, u32[]{:S(2)}) %collective-permute-start.22) | collective-permute-done | bytes 524320 | tf_op jit(solution)/shard_map/ppermute | solution.py:200
  204.1 1.4 copy-done.13
  205.4 8.7 %output.1 = (f32[512,1024]{1,0:T(8,128)}, bf16[512,1024]{1,0:T(8,128)(2,1)S(1)}) custom-call(s32[4]{0:T(128)S(1)} %pad_add_fusion.where_ref, bf16[512,512]{1,0:T(8,128)(2,1)S(1)} %attend.1.own_ref, bf16[512,512]{1,0:T(8,128)(2,1)S(1)} %collective-permute-done.22.next_ref, bf16[2,1024,256]{2,1,0:T(8,128)(2,1)S(1)} %pad_maximum_fusion.5.w_own, ...), custom_call_target="tpu_custom_call" | custom-call | tf_op jit(solution)/shard_map/output/pallas_call | solution.py:578
  214.1 2.7 %collective-permute-done.24 = bf16[512,1024]{1,0:T(8,128)(2,1)S(1)} collective-permute-done((bf16[512,1024]{1,0:T(8,128)(2,1)S(1)}, bf16[512,1024]{1,0:T(8,128)(2,1)S(1)}, u32[]{:S(2)}, u32[]{:S(2)}) %collective-permute-start.24) | collective-permute-done | bytes 1048608 | tf_op jit(solution)/shard_map/ppermute | solution.py:200
  216.8 1.9 convert_add_fusion
  218.8 1.8 collective-permute-start.27
  220.9 4.7 %collective-permute-start.25 = (bf16[128,1024]{1,0:T(8,128)(2,1)S(1)}, bf16[128,1024]{1,0:T(8,128)(2,1)}, u32[]{:S(2)}, u32[]{:S(2)}) collective-permute-start(bf16[128,1024]{1,0:T(8,128)(2,1)S(1)} %get-tuple-element.57), channel_id=1, source_target_pairs={{0,16},{1,17},{2,18},{3,19},{4,20},{5,21},{6,22},{7,23},{8,24},{9,... | collective-permute-start | bytes 786440 | tf_op jit(solution)/shard_map/ppermute | solution.py:200
  225.6 7.1 %collective-permute-done.27 = bf16[128,1024]{1,0:T(8,128)(2,1)S(1)} collective-permute-done((bf16[128,1024]{1,0:T(8,128)(2,1)S(1)}, bf16[128,1024]{1,0:T(8,128)(2,1)S(1)}, u32[]{:S(2)}, u32[]{:S(2)}) %collective-permute-start.27) | collective-permute-done | bytes 262176 | tf_op jit(solution)/shard_map/ppermute | solution.py:200
  232.7 3.4 %collective-permute-done.26 = bf16[128,1024]{1,0:T(8,128)(2,1)S(1)} collective-permute-done((bf16[128,1024]{1,0:T(8,128)(2,1)S(1)}, bf16[128,1024]{1,0:T(8,128)(2,1)S(1)}, u32[]{:S(2)}, u32[]{:S(2)}) %collective-permute-start.26) | collective-permute-done | bytes 262176 | tf_op jit(solution)/shard_map/ppermute | solution.py:200
  236.0 7.4 %collective-permute-done.25 = bf16[128,1024]{1,0:T(8,128)(2,1)} collective-permute-done((bf16[128,1024]{1,0:T(8,128)(2,1)S(1)}, bf16[128,1024]{1,0:T(8,128)(2,1)}, u32[]{:S(2)}, u32[]{:S(2)}) %collective-permute-start.25) | collective-permute-done | bytes 262176 | tf_op jit(solution)/shard_map/ppermute | solution.py:200
  243.4 1.1 broadcast_select_fusion.2
  244.6 0.8 pad_maximum_fusion.7
  (87 shorter events, 4.4 us)
Async XLA Ops:
  0.0 19.3 %copy-start.15 = (bf16[256,2048]{1,0:T(8,128)(2,1)S(1)}, bf16[256,2048]{1,0:T(8,128)(2,1)}, u32[]{:S(2)}) copy-start(bf16[256,2048]{1,0:T(8,128)(2,1)} %param.16) | copy-start | bytes 3145732
  0.0 20.8 %collective-permute-start.3 = (bf16[32,2048]{1,0:T(8,128)(2,1)}, bf16[32,2048]{1,0:T(8,128)(2,1)}, u32[]{:S(2)}, u32[]{:S(2)}) collective-permute-start(bf16[32,2048]{1,0:T(8,128)(2,1)} %param.14), channel_id=1, source_target_pairs={{6,16},{7,17},{14,18},{15,19},{22,28},{23,29},{30,30},{31,31}} | collective-permute-start | bytes 393224 | tf_op jit(solution)/shard_map/ppermute | solution.py:200
  1.4 19.4 %collective-permute-start.2 = (bf16[32,2048]{1,0:T(8,128)(2,1)}, bf16[32,2048]{1,0:T(8,128)(2,1)}, u32[]{:S(2)}, u32[]{:S(2)}) collective-permute-start(bf16[32,2048]{1,0:T(8,128)(2,1)} %param.14), channel_id=1, source_target_pairs={{4,16},{5,17},{12,18},{13,19},{20,28},{21,29},{28,30},{29,31}} | collective-permute-start | bytes 393224 | tf_op jit(solution)/shard_map/ppermute | solution.py:200
  2.8 18.1 %collective-permute-start.1 = (bf16[32,2048]{1,0:T(8,128)(2,1)}, bf16[32,2048]{1,0:T(8,128)(2,1)}, u32[]{:S(2)}, u32[]{:S(2)}) collective-permute-start(bf16[32,2048]{1,0:T(8,128)(2,1)} %param.14), channel_id=1, source_target_pairs={{2,16},{3,17},{10,18},{11,19},{18,28},{19,29},{26,30},{27,31}} | collective-permute-start | bytes 393224 | tf_op jit(solution)/shard_map/ppermute | solution.py:200
  4.1 16.8 %collective-permute-start = (bf16[32,2048]{1,0:T(8,128)(2,1)}, bf16[32,2048]{1,0:T(8,128)(2,1)}, u32[]{:S(2)}, u32[]{:S(2)}) collective-permute-start(bf16[32,2048]{1,0:T(8,128)(2,1)} %param.14), channel_id=1, source_target_pairs={{0,16},{1,17},{8,18},{9,19},{16,28},{17,29},{24,30},{25,31}} | collective-permute-start | bytes 393224 | tf_op jit(solution)/shard_map/ppermute | solution.py:200
  19.3 0.7 copy-start.21
  19.3 9.3 %collective-permute-start.4 = (bf16[336,512]{1,0:T(8,128)(2,1)}, bf16[336,512]{1,0:T(8,128)(2,1)}, u32[]{:S(2)}, u32[]{:S(2)}) collective-permute-start(bf16[336,512]{1,0:T(8,128)(2,1)} %pad_maximum_fusion.10), channel_id=1, source_target_pairs={{0,8},{1,9},{2,10},{3,11},{4,12},{5,13},{6,14},{7,15},{8,0},{9,1},... | collective-permute-start | bytes 1032200 | tf_op jit(solution)/shard_map/ppermute | solution.py:200
  19.3 1.6 copy-start.16
  20.7 2.1 copy-start.20
  20.7 2.1 copy-start.17
  20.8 4.8 %dynamic-slice-start = ((f32[4096]{0:T(1024)}, s32[]{:T(128)}), f32[2048]{0:T(1024)S(1)}, s32[]{:S(2)}) async-start(f32[4096]{0:T(1024)} %param.15, s32[]{:T(128)} %select_n.133), calls=%async_computation | async-start | bytes 16896 | tf_op jit(solution)/shard_map/dynamic_slice | solution.py:479
  20.8 9.2 %collective-permute-start.5 = (bf16[1,256,1024]{2,1,0:T(8,128)(2,1)S(1)}, bf16[1,256,1024]{2,1,0:T(8,128)(2,1)S(1)}, u32[]{:S(2)}, u32[]{:S(2)}) collective-permute-start(bf16[1,256,1024]{2,1,0:T(8,128)(2,1)S(1)} %maximum_bitcast_fusion.refs_0_), channel_id=1, source_target_pairs={{0,2},{1,5},{2,0},{3,7},{4,6},{5,1},{6,4},{7,3},{8,10},{9,13},{10,... | collective-permute-start | bytes 1572872 | tf_op jit(solution)/shard_map/ppermute | solution.py:200
  30.0 3.5 %copy-start.5 = (bf16[1,256,1024]{2,1,0:T(8,128)(2,1)}, bf16[1,256,1024]{2,1,0:T(8,128)(2,1)S(1)}, u32[]{:S(2)}) copy-start(bf16[1,256,1024]{2,1,0:T(8,128)(2,1)S(1)} %collective-permute-done.5.refs_1_) | copy-start | bytes 1572868
  31.2 20.8 %collective-permute-start.7 = (bf16[2,256,1024]{2,1,0:T(8,128)(2,1)}, bf16[2,256,1024]{2,1,0:T(8,128)(2,1)S(1)}, u32[]{:S(2)}, u32[]{:S(2)}) collective-permute-start(bf16[2,256,1024]{2,1,0:T(8,128)(2,1)} %pad_maximum_fusion.2), channel_id=1, source_target_pairs={{0,4},{1,3},{2,6},{3,1},{4,0},{5,7},{6,2},{7,5},{8,12},{9,11},{10,... | collective-permute-start | bytes 3145736 | tf_op jit(solution)/shard_map/ppermute | solution.py:200
  31.2 20.8 %collective-permute-start.6 = (bf16[144,2048]{1,0:T(8,128)(2,1)S(1)}, bf16[144,2048]{1,0:T(8,128)(2,1)}, u32[]{:S(2)}, u32[]{:S(2)}) collective-permute-start(bf16[144,2048]{1,0:T(8,128)(2,1)S(1)} %fusion.2), channel_id=1, source_target_pairs={{1,16},{3,18},{5,20},{7,22},{9,24},{11,26},{13,28},{15,30},{16,1},... | collective-permute-start | bytes 1769480 | tf_op jit(solution)/shard_map/ppermute | solution.py:200
  33.6 18.5 %collective-permute-start.8 = (bf16[1,256,1024]{2,1,0:T(8,128)(2,1)}, bf16[1,256,1024]{2,1,0:T(8,128)(2,1)}, u32[]{:S(2)}, u32[]{:S(2)}) collective-permute-start(bf16[1,256,1024]{2,1,0:T(8,128)(2,1)} %maximum_bitcast_fusion.1), channel_id=1, source_target_pairs={{0,8},{1,9},{2,10},{3,11},{4,12},{5,13},{6,14},{7,15},{8,0},{9,1},... | collective-permute-start | bytes 1572872 | tf_op jit(solution)/shard_map/ppermute | solution.py:200
  35.1 20.5 %copy-start.9 = (bf16[1,256,512]{2,1,0:T(8,128)(2,1)}, bf16[1,256,512]{2,1,0:T(8,128)(2,1)S(1)}, u32[]{:S(2)}) copy-start(bf16[1,256,512]{2,1,0:T(8,128)(2,1)S(1)} %maximum_bitcast_fusion.2) | copy-start | bytes 786436
  36.2 19.4 %copy-start.11 = (bf16[1,256,512]{2,1,0:T(8,128)(2,1)}, bf16[1,256,512]{2,1,0:T(8,128)(2,1)S(1)}, u32[]{:S(2)}) copy-start(bf16[1,256,512]{2,1,0:T(8,128)(2,1)S(1)} %slice_bitcast_fusion) | copy-start | bytes 786436
  52.0 3.5 %copy-start.7 = (bf16[2,256,1024]{2,1,0:T(8,128)(2,1)}, bf16[2,256,1024]{2,1,0:T(8,128)(2,1)S(1)}, u32[]{:S(2)}) copy-start(bf16[2,256,1024]{2,1,0:T(8,128)(2,1)S(1)} %collective-permute-done.7.refs_2_) | copy-start | bytes 3145732
  53.0 21.3 %collective-permute-start.9 = (bf16[144,2048]{1,0:T(8,128)(2,1)}, bf16[144,2048]{1,0:T(8,128)(2,1)S(1)}, u32[]{:S(2)}, u32[]{:S(2)}) collective-permute-start(bf16[144,2048]{1,0:T(8,128)(2,1)} %broadcast_select_fusion), channel_id=1, source_target_pairs={{0,8},{1,9},{2,10},{3,11},{4,12},{5,13},{6,14},{7,15},{8,0},{9,1},... | collective-permute-start | bytes 1769480 | tf_op jit(solution)/shard_map/ppermute | solution.py:200
  55.6 9.2 %collective-permute-start.10 = (bf16[2,256,512]{2,1,0:T(8,128)(2,1)S(1)}, bf16[2,256,512]{2,1,0:T(8,128)(2,1)S(1)}, u32[]{:S(2)}, u32[]{:S(2)}) collective-permute-start(bf16[2,256,512]{2,1,0:T(8,128)(2,1)S(1)} %pad_maximum_fusion.6.own), channel_id=1, source_target_pairs={{0,2},{1,5},{2,0},{3,7},{4,6},{5,1},{6,4},{7,3},{8,10},{9,13},{10,... | collective-permute-start | bytes 1572872 | tf_op jit(solution)/shard_map/ppermute | solution.py:200
  59.0 16.7 %copy-start.10 = (bf16[1,256,512]{2,1,0:T(8,128)(2,1)S(1)}, bf16[1,256,512]{2,1,0:T(8,128)(2,1)}, u32[]{:S(2)}) copy-start(bf16[1,256,512]{2,1,0:T(8,128)(2,1)} %copy-done.9) | copy-start | bytes 786436
  59.0 16.7 %copy-start.12 = (bf16[1,256,512]{2,1,0:T(8,128)(2,1)S(1)}, bf16[1,256,512]{2,1,0:T(8,128)(2,1)}, u32[]{:S(2)}) copy-start(bf16[1,256,512]{2,1,0:T(8,128)(2,1)} %copy-done.11) | copy-start | bytes 786436
  59.0 36.2 %collective-permute-start.13 = (bf16[1024,256]{1,0:T(8,128)(2,1)}, bf16[1024,256]{1,0:T(8,128)(2,1)}, u32[]{:S(2)}, u32[]{:S(2)}) collective-permute-start(bf16[1024,256]{1,0:T(8,128)(2,1)} %get-tuple-element.61), channel_id=1, source_target_pairs={{0,16},{1,17},{2,18},{3,19},{4,20},{5,21},{6,22},{7,23},{8,24},{9,... | collective-permute-start | bytes 1572872 | tf_op jit(solution)/shard_map/ppermute | solution.py:200
  63.4 14.2 %collective-permute-start.14 = (bf16[1,256,1024]{2,1,0:T(8,128)(2,1)}, bf16[1,256,1024]{2,1,0:T(8,128)(2,1)}, u32[]{:S(2)}, u32[]{:S(2)}) collective-permute-start(bf16[1,256,1024]{2,1,0:T(8,128)(2,1)} %collective-permute-done.8.refs_3_), channel_id=1, source_target_pairs={{0,2},{1,5},{2,0},{3,7},{4,6},{5,1},{6,4},{7,3},{8,10},{9,13},{10,... | collective-permute-start | bytes 1572872 | tf_op jit(solution)/shard_map/ppermute | solution.py:200
  64.8 0.8 copy-start.2
  74.3 1.3 copy-start.3
  75.6 16.5 %copy-start = (bf16[288,2048]{1,0:T(8,128)(2,1)}, bf16[288,2048]{1,0:T(8,128)(2,1)S(1)}, u32[]{:S(2)}) copy-start(bf16[288,2048]{1,0:T(8,128)(2,1)S(1)} %pad_maximum_fusion.1.x0) | copy-start | bytes 3538948
  75.6 16.5 %collective-permute-start.11 = (bf16[288,2048]{1,0:T(8,128)(2,1)S(1)}, bf16[288,2048]{1,0:T(8,128)(2,1)S(1)}, u32[]{:S(2)}, u32[]{:S(2)}) collective-permute-start(bf16[288,2048]{1,0:T(8,128)(2,1)S(1)} %pad_maximum_fusion.1.x0), channel_id=1, source_target_pairs={{0,1},{1,0},{2,3},{3,2},{4,5},{5,4},{6,7},{7,6},{8,9},{9,8},{10,11... | collective-permute-start | bytes 3538952 | tf_op jit(solution)/shard_map/ppermute | solution.py:200
  77.0 3.7 %copy-start.18 = (bf16[64,128]{1,0:T(8,128)(2,1)S(1)}, bf16[64,128]{1,0:T(8,128)(2,1)}, u32[]{:S(2)}) copy-start(bf16[64,128]{1,0:T(8,128)(2,1)} %get-tuple-element.87) | copy-start | bytes 49156
  77.0 3.7 %copy-start.19 = (bf16[64,128]{1,0:T(8,128)(2,1)S(1)}, bf16[64,128]{1,0:T(8,128)(2,1)}, u32[]{:S(2)}) copy-start(bf16[64,128]{1,0:T(8,128)(2,1)} %get-tuple-element.90) | copy-start | bytes 49156
  77.0 15.1 %collective-permute-start.12 = (bf16[4,256,512]{2,1,0:T(8,128)(2,1)}, bf16[4,256,512]{2,1,0:T(8,128)(2,1)}, u32[]{:S(2)}, u32[]{:S(2)}) collective-permute-start(bf16[4,256,512]{2,1,0:T(8,128)(2,1)} %pad_maximum_fusion.3), channel_id=1, source_target_pairs={{0,4},{1,3},{2,6},{3,1},{4,0},{5,7},{6,2},{7,5},{8,12},{9,11},{10,... | collective-permute-start | bytes 3145736 | tf_op jit(solution)/shard_map/ppermute | solution.py:200
  77.6 14.5 %copy-start.4 = (bf16[2,256,512]{2,1,0:T(8,128)(2,1)S(1)}, bf16[2,256,512]{2,1,0:T(8,128)(2,1)}, u32[]{:S(2)}) copy-start(bf16[2,256,512]{2,1,0:T(8,128)(2,1)} %copy-done.2) | copy-start | bytes 1572868
  79.0 24.2 %collective-permute-start.15 = (bf16[2,256,1024]{2,1,0:T(8,128)(2,1)S(1)}, bf16[2,256,1024]{2,1,0:T(8,128)(2,1)S(1)}, u32[]{:S(2)}, u32[]{:S(2)}) collective-permute-start(bf16[2,256,1024]{2,1,0:T(8,128)(2,1)S(1)} %pad_maximum_fusion.4), channel_id=1, source_target_pairs={{0,4},{1,3},{2,6},{3,1},{4,0},{5,7},{6,2},{7,5},{8,12},{9,11},{10,... | collective-permute-start | bytes 3145736 | tf_op jit(solution)/shard_map/ppermute | solution.py:200
  92.1 3.1 %copy-start.1 = (bf16[288,2048]{1,0:T(8,128)(2,1)}, bf16[288,2048]{1,0:T(8,128)(2,1)S(1)}, u32[]{:S(2)}) copy-start(bf16[288,2048]{1,0:T(8,128)(2,1)S(1)} %collective-permute-done.11.x1) | copy-start | bytes 3538948
  95.2 18.1 %collective-permute-start.16 = (bf16[736,256]{1,0:T(8,128)(2,1)S(1)}, bf16[736,256]{1,0:T(8,128)(2,1)S(1)}, u32[]{:S(2)}, u32[]{:S(2)}) collective-permute-start(bf16[736,256]{1,0:T(8,128)(2,1)S(1)} %get-tuple-element.45), channel_id=1, source_target_pairs={{0,16},{1,17},{2,18},{3,19},{4,20},{5,21},{6,22},{7,23},{8,24},{9,... | collective-permute-start | bytes 1130504 | tf_op jit(solution)/shard_map/ppermute | solution.py:200
  99.0 4.2 %copy-start.6 = (bf16[1,256,1024]{2,1,0:T(8,128)(2,1)S(1)}, bf16[1,256,1024]{2,1,0:T(8,128)(2,1)}, u32[]{:S(2)}) copy-start(bf16[1,256,1024]{2,1,0:T(8,128)(2,1)} %copy-done.5) | copy-start | bytes 1572868
  99.1 4.1 %copy-start.8 = (bf16[2,256,1024]{2,1,0:T(8,128)(2,1)S(1)}, bf16[2,256,1024]{2,1,0:T(8,128)(2,1)}, u32[]{:S(2)}) copy-start(bf16[2,256,1024]{2,1,0:T(8,128)(2,1)} %copy-done.7) | copy-start | bytes 3145732
  107.8 8.2 %copy-start.14 = (bf16[1,1024,256]{2,1,0:T(8,128)(2,1)S(1)}, bf16[1,1024,256]{2,1,0:T(8,128)(2,1)}, u32[]{:S(2)}) copy-start(bf16[1,1024,256]{2,1,0:T(8,128)(2,1)} %get-tuple-element.60) | copy-start | bytes 1572868
  114.3 7.8 %collective-permute-start.17 = (bf16[6,128,256]{2,1,0:T(8,128)(2,1)S(1)}, bf16[6,128,256]{2,1,0:T(8,128)(2,1)S(1)}, u32[]{:S(2)}, u32[]{:S(2)}) collective-permute-start(bf16[6,128,256]{2,1,0:T(8,128)(2,1)S(1)} %keys_join.1.kv0), channel_id=1, source_target_pairs={{0,2},{1,5},{2,0},{3,7},{4,6},{5,1},{6,4},{7,3},{8,10},{9,13},{10,... | collective-permute-start | bytes 1179656 | tf_op jit(solution)/shard_map/ppermute | solution.py:200
  122.2 24.7 %collective-permute-start.18 = (bf16[2,1024,256]{2,1,0:T(8,128)(2,1)S(1)}, bf16[2,1024,256]{2,1,0:T(8,128)(2,1)S(1)}, u32[]{:S(2)}, u32[]{:S(2)}) collective-permute-start(bf16[2,1024,256]{2,1,0:T(8,128)(2,1)S(1)} %pad_maximum_fusion.5.w_own), channel_id=1, source_target_pairs={{0,2},{1,5},{2,0},{3,7},{4,6},{5,1},{6,4},{7,3},{8,10},{9,13},{10,... | collective-permute-start | bytes 3145736 | tf_op jit(solution)/shard_map/ppermute | solution.py:200
  123.7 23.1 %collective-permute-start.19 = (bf16[4,128,512]{2,1,0:T(8,128)(2,1)S(1)}, bf16[4,128,512]{2,1,0:T(8,128)(2,1)S(1)}, u32[]{:S(2)}, u32[]{:S(2)}) collective-permute-start(bf16[4,128,512]{2,1,0:T(8,128)(2,1)S(1)} %get-tuple-element.49), channel_id=1, source_target_pairs={{0,16},{1,17},{2,18},{3,19},{4,20},{5,21},{6,22},{7,23},{8,24},{9,... | collective-permute-start | bytes 1572872 | tf_op jit(solution)/shard_map/ppermute | solution.py:200
  147.0 57.0 %collective-permute-start.23 = (bf16[4,1024,256]{2,1,0:T(8,128)(2,1)S(1)}, bf16[4,1024,256]{2,1,0:T(8,128)(2,1)S(1)}, u32[]{:S(2)}, u32[]{:S(2)}) collective-permute-start(bf16[4,1024,256]{2,1,0:T(8,128)(2,1)S(1)} %pad_maximum_fusion), channel_id=1, source_target_pairs={{0,4},{1,3},{2,6},{3,1},{4,0},{5,7},{6,2},{7,5},{8,12},{9,11},{10,... | collective-permute-start | bytes 6291464 | tf_op jit(solution)/shard_map/ppermute | solution.py:200
  148.8 28.5 %collective-permute-start.20 = (bf16[6,128,256]{2,1,0:T(8,128)(2,1)S(1)}, bf16[6,128,256]{2,1,0:T(8,128)(2,1)S(1)}, u32[]{:S(2)}, u32[]{:S(2)}) collective-permute-start(bf16[6,128,256]{2,1,0:T(8,128)(2,1)S(1)} %keys_join.1.kv0), channel_id=1, source_target_pairs={{0,4},{1,3},{2,6},{3,1},{4,0},{5,7},{6,2},{7,5},{8,12},{9,11},{10,... | collective-permute-start | bytes 1179656 | tf_op jit(solution)/shard_map/ppermute | solution.py:200
  149.1 32.4 %collective-permute-start.21 = (bf16[6,128,256]{2,1,0:T(8,128)(2,1)S(1)}, bf16[6,128,256]{2,1,0:T(8,128)(2,1)S(1)}, u32[]{:S(2)}, u32[]{:S(2)}) collective-permute-start(bf16[6,128,256]{2,1,0:T(8,128)(2,1)S(1)} %collective-permute-done.17.kv1), channel_id=1, source_target_pairs={{0,4},{1,3},{2,6},{3,1},{4,0},{5,7},{6,2},{7,5},{8,12},{9,11},{10,... | collective-permute-start | bytes 1179656 | tf_op jit(solution)/shard_map/ppermute | solution.py:200
  190.5 13.5 %collective-permute-start.22 = (bf16[512,512]{1,0:T(8,128)(2,1)S(1)}, bf16[512,512]{1,0:T(8,128)(2,1)S(1)}, u32[]{:S(2)}, u32[]{:S(2)}) collective-permute-start(bf16[512,512]{1,0:T(8,128)(2,1)S(1)} %attend.1.own_ref), channel_id=1, source_target_pairs={{0,8},{1,9},{2,10},{3,11},{4,12},{5,13},{6,14},{7,15},{8,0},{9,1},... | collective-permute-start | bytes 1572872 | tf_op jit(solution)/shard_map/ppermute | solution.py:200
  204.1 1.4 copy-start.13
  214.1 2.7 %collective-permute-start.24 = (bf16[512,1024]{1,0:T(8,128)(2,1)S(1)}, bf16[512,1024]{1,0:T(8,128)(2,1)S(1)}, u32[]{:S(2)}, u32[]{:S(2)}) collective-permute-start(bf16[512,1024]{1,0:T(8,128)(2,1)S(1)} %get-tuple-element.54), channel_id=1, source_target_pairs={{0,1},{1,0},{2,3},{3,2},{4,5},{5,4},{6,7},{7,6},{8,9},{9,8},{10,11... | collective-permute-start | bytes 3145736 | tf_op jit(solution)/shard_map/ppermute | solution.py:200
  218.8 13.9 %collective-permute-start.27 = (bf16[128,1024]{1,0:T(8,128)(2,1)S(1)}, bf16[128,1024]{1,0:T(8,128)(2,1)S(1)}, u32[]{:S(2)}, u32[]{:S(2)}) collective-permute-start(bf16[128,1024]{1,0:T(8,128)(2,1)S(1)} %get-tuple-element.58), channel_id=1, source_target_pairs={{0,24},{1,25},{2,26},{3,27},{4,28},{5,29},{6,30},{7,31},{8,0},{9,1... | collective-permute-start | bytes 786440 | tf_op jit(solution)/shard_map/ppermute | solution.py:200
  220.6 15.4 %collective-permute-start.26 = (bf16[128,1024]{1,0:T(8,128)(2,1)S(1)}, bf16[128,1024]{1,0:T(8,128)(2,1)S(1)}, u32[]{:S(2)}, u32[]{:S(2)}) collective-permute-start(bf16[128,1024]{1,0:T(8,128)(2,1)S(1)} %get-tuple-element.59), channel_id=1, source_target_pairs={{0,8},{1,9},{2,10},{3,11},{4,12},{5,13},{6,14},{7,15},{8,16},{9,17... | collective-permute-start | bytes 786440 | tf_op jit(solution)/shard_map/ppermute | solution.py:200
  220.9 22.5 %collective-permute-start.25 = (bf16[128,1024]{1,0:T(8,128)(2,1)S(1)}, bf16[128,1024]{1,0:T(8,128)(2,1)}, u32[]{:S(2)}, u32[]{:S(2)}) collective-permute-start(bf16[128,1024]{1,0:T(8,128)(2,1)S(1)} %get-tuple-element.57), channel_id=1, source_target_pairs={{0,16},{1,17},{2,18},{3,19},{4,20},{5,21},{6,22},{7,23},{8,24},{9,... | collective-permute-start | bytes 786440 | tf_op jit(solution)/shard_map/ppermute | solution.py:200

commit v5 on v4

--- a/solution.py
+++ b/solution.py
@@ -434,16 +434,8 @@
     first = stream_len // 2 // tok
     last = (stream_len - TILE_RUN) // tok
     owners = [first + i for i in range(tile_owners)] + [last + i for i in range(tile_owners)]
-    received = []
-    for k in range(PLANE):
-
-        def to_owner(z, p, c, k=k):
-            return (owners[z] // PLANE, owners[z] % PLANE, c) if p == k else None
-
-        received.append(permuted(picture_rows, to_owner))
-    placed = jnp.concatenate(received, axis=0)
-    is_owner = jnp.any(seq_index == jnp.array(owners, jnp.int32))
-    stream = jnp.where(is_owner, placed, text_rows)
+    assert [owner % PLANE for owner in owners] == list(range(LEVELS))
+    owner_levels = jnp.array([owner // PLANE for owner in owners], jnp.int32)
 
     slots = (recompute_slots - seq_index * CACHED).astype(jnp.bfloat16)
     slot_rows = jnp.broadcast_to(jnp.pad(slots, (0, REC_PAD - REC))[:, None], (REC_PAD, 4 * HD))
@@ -472,27 +464,57 @@
     query_near = to_near(query_own)
 
     rows = jnp.concatenate(
-        [stream, recompute_rows, jnp.zeros((REC_PAD - REC, width), stream.dtype)], axis=0
-    )
-    wide = rows.astype(jnp.float32)
-    squares = lax.psum(jnp.sum(wide * wide, axis=1), "head")
-    normed = scaled(wide, squares, lax.dynamic_slice_in_dim(norm_gain, core * width, width, 0))
-
-    normed, key_next, query_near = lax.optimization_barrier((normed, key_next, query_near))
+        [text_rows, recompute_rows, jnp.zeros((REC_PAD - REC, width), text_rows.dtype)], axis=0
+    )
+    gain = lax.dynamic_slice_in_dim(norm_gain, core * width, width, 0)
+    wide, pictures = rows.astype(jnp.float32), picture_rows.astype(jnp.float32)
+    squares, picture_squares = lax.psum(
+        (jnp.sum(wide * wide, axis=1), jnp.sum(pictures * pictures, axis=1)), "head"
+    )
+    normed = scaled(wide, squares, gain)
+    pictures = scaled(pictures, picture_squares, gain)
+    shown = [
+        permuted(pictures, lambda z, p, c, k=k: (2 * c + (k ^ (p % 2)), z, p // 2)) for k in (0, 1)
+    ]
+
+    crossed = permuted(normed, lambda z, p, c: (z ^ 2, p, 1 - c) if c == 1 - z // 2 else None)
+    crossed, key_next, query_near, *shown = lax.optimization_barrier(
+        (crossed, key_next, query_near, *shown)
+    )
     query_far = to_far(jnp.concatenate([query_own, query_near], axis=0))
     keys = jnp.stack([key_own[:depth], key_next[:depth]])
     old_own, old_next = key_own[depth:], key_next[depth:]
-    crossed = permuted(normed, lambda z, p, c: (z ^ 2, p, 1 - c) if c == 1 - z // 2 else None)
-    crossed, query_far, query_next = lax.optimization_barrier((crossed, query_far, query_next))
     keys_near = to_near(keys)
     held = jnp.where(own_first, normed, crossed)
     next_rows = across(held, 1)
-    next_rows, keys_near = lax.optimization_barrier((next_rows, keys_near))
+    odd = level % 2 == 1
+    shown_mine = jnp.concatenate(
+        [jnp.where(odd, shown[1], shown[0]), jnp.where(odd, shown[0], shown[1])], axis=0
+    )
+    shown_other = other_core(shown_mine)
+    next_rows, keys_near, shown_other, query_next, query_far = lax.optimization_barrier(
+        (next_rows, keys_near, shown_other, query_next, query_far)
+    )
     keys_far = to_far(jnp.concatenate([keys, keys_near], axis=0))
-    rows_mine = jnp.concatenate([held, next_rows], axis=0)
+    next_near = to_near(query_next)
+    shown_all = jnp.concatenate(
+        [
+            jnp.where(core == 0, shown_mine, shown_other),
+            jnp.where(core == 0, shown_other, shown_mine),
+        ],
+        axis=0,
+    )
+    shown_at = owner_levels[place]
+
+    def with_pictures(block, at):
+        return [jnp.where(at == shown_at, shown_all, block[:tok]), block[tok:]]
+
+    held_at = jnp.where(own_first, level, level ^ 2)
+    rows_mine = jnp.concatenate(
+        with_pictures(held, held_at) + with_pictures(next_rows, held_at ^ 1), axis=0
+    )
     rows_other = other_core(rows_mine)
     rows_other, keys_far = lax.optimization_barrier((rows_other, keys_far))
-    next_near = to_near(query_next)
     next_far = to_far(jnp.concatenate([query_next, next_near], axis=0))
 
     out_rows = w_out.shape[0] // 2
@@ -526,6 +548,9 @@
         name="keys_part",
     )(where, rows_mine, rows_other, keys, keys_near, keys_far, old_own, old_next)
     send, rows_after, out_got = lax.optimization_barrier((send, rows_mine, out_got))
+    out_pair = jnp.stack([out_own, out_got])
+    out_pair, next_far = lax.optimization_barrier((out_pair, next_far))
+    out_near = to_near(out_pair)
     q_keep, q_send = pl.pallas_call(
         queries_part_kernel,
         out_shape=(
@@ -560,10 +585,11 @@
     kv_near, kv_far = to_near(kv), to_far(kv)
     kv_both = to_far(kv_near)
 
-    out_pair = jnp.stack([out_own, out_got])
-    out_pair, kv_near = lax.optimization_barrier((out_pair, kv_near))
-    out_near, got_queries = lax.optimization_barrier((to_near(out_pair), across(q_send, 2)))
+    kv_far, kv_both, out_near, got_queries = lax.optimization_barrier(
+        (kv_far, kv_both, out_near, across(q_send, 2))
+    )
     out_far = to_far(jnp.concatenate([out_pair, out_near], axis=0))
+
     attended = pl.pallas_call(
         attend_kernel,
         out_shape=shaped((LEVELS * tok, 4 * HD)),

time: 249 us -> 207 us (0.83)
  waiting for transfers between devices: 136 us -> 90.2 us
  local copies, waits for them, and re-layouts: 9.98 us -> 17.1 us
    ppermute x28 -> x27, waiting for transfers between devices: 136 us -> 90.2 us  [permuted(): return lax.ppermute(value, ('seq', 'head'), perm)]
    unnamed x44 -> x56, local copies, waits for them, and re-layouts: 2.8 us -> 6.18 us
    ppermute x28 -> x27, starting transfers between devices: 50.2 us -> 48 us  [permuted(): return lax.ppermute(value, ('seq', 'head'), perm)]
  transfers between devices with their start and end apart: 28 -> 27, of which waited for: 17 -> 17; matrix products, arithmetic and copies ran while one was open for 8% -> 12% of each run, Pallas kernels for 7% -> 9%
where the time goes in v5:
time: 207 us; the launch traced here: 205 us
  waiting for transfers between devices  90.2 us (44%)
  starting transfers between devices  48 us (23%)
  Pallas kernels  26.5 us (13%)
  other arithmetic  19.2 us (9%)
  local copies, waits for them, and re-layouts  17.1 us (8%)
  blocking collectives  2.47 us (1%)
    ppermute x27, waiting for transfers between devices, permuted(): return lax.ppermute(value, ('seq', 'head'), perm)  90.2 us
    ppermute x27, starting transfers between devices, permuted(): return lax.ppermute(value, ('seq', 'head'), perm)  48 us
    pallas_call x1, Pallas kernels, by_levels(): pl.pallas_call(attend_kernel, out_shape=shaped((LEVELS * tok, 4 * HD)), i...  8.96 us
    pallas_call x1, Pallas kernels, by_levels(): pl.pallas_call(output_kernel, out_shape=(shaped((LEVELS * tok, wide_cols)...  8.73 us
    unnamed x56, local copies, waits for them, and re-layouts  6.18 us
    pallas_call x1, Pallas kernels, by_levels(): pl.pallas_call(queries_part_kernel, out_shape=(shaped((LEVELS, tok, 4 * H...  4.73 us
  transfers between devices with their start and end apart: 27, of which 17 were waited for; matrix products, arithmetic and copies ran while one was open for 12% of the time, Pallas kernels for 9%

profile of v5, /device:TPU:8, one launch (start us, length us, event | category | flops | bytes accessed | tf_op | source)
XLA Modules:
  0.0 205.2 jit_solution(14489901586714326857)
XLA Ops:
  0.0 1.3 constant_dynamic-slice_fusion.6
  1.4 1.6 collective-permute-start.2
  3.0 0.8 constant_dynamic-slice_fusion.9
  3.8 1.5 constant_dynamic-slice_fusion.3
  6.4 2.5 %all-reduce.1 = (f32[144]{0:T(256)S(1)}, f32[32]{0:T(128)S(1)}) all-reduce(f32[144]{0:T(256)S(1)} %fusion, f32[32]{0:T(128)S(1)} %fusion.4), channel_id=1, replica_groups=mesh['seq'=16,'head'=2] {'head'}, use_global_device_ids=true, to_apply=%region_1.2 | all-reduce | flops 176 | bytes 1408 | tf_op jit(solution)/shard_map/psum | solution.py:471
  9.3 1.5 collective-permute-start
  10.8 0.8 fusion.6
  11.6 3.4 %collective-permute-start.3 = (bf16[32,2048]{1,0:T(8,128)(2,1)}, bf16[32,2048]{1,0:T(8,128)(2,1)}, u32[]{:S(2)}, u32[]{:S(2)}) collective-permute-start(bf16[32,2048]{1,0:T(8,128)(2,1)} %fusion.6), channel_id=1, source_target_pairs={{0,0},{1,16},{2,8},{3,24},{4,1},{5,17},{6,9},{7,25},{8,2},{9,18},{... | collective-permute-start | bytes 393224 | tf_op jit(solution)/shard_map/ppermute | solution.py:200
  15.1 0.9 maximum_bitcast_fusion.2
  16.0 0.9 maximum_bitcast_fusion.1
  16.9 4.2 %collective-permute-done.3 = bf16[32,2048]{1,0:T(8,128)(2,1)} collective-permute-done((bf16[32,2048]{1,0:T(8,128)(2,1)}, bf16[32,2048]{1,0:T(8,128)(2,1)}, u32[]{:S(2)}, u32[]{:S(2)}) %collective-permute-start.3) | collective-permute-done | bytes 131104 | tf_op jit(solution)/shard_map/ppermute | solution.py:200
  21.8 1.2 pad_maximum_fusion.2
  23.0 13.8 %collective-permute-start.9 = (bf16[2,256,1024]{2,1,0:T(8,128)(2,1)}, bf16[2,256,1024]{2,1,0:T(8,128)(2,1)S(1)}, u32[]{:S(2)}, u32[]{:S(2)}) collective-permute-start(bf16[2,256,1024]{2,1,0:T(8,128)(2,1)} %pad_maximum_fusion.2), channel_id=1, source_target_pairs={{0,4},{1,3},{2,6},{3,1},{4,0},{5,7},{6,2},{7,5},{8,12},{9,11},{10,... | collective-permute-start | bytes 3145736 | tf_op jit(solution)/shard_map/ppermute | solution.py:200
  36.8 1.0 slice_bitcast_fusion
  38.5 1.3 broadcast_select_fusion
  39.8 1.5 collective-permute-start.5
  41.3 1.0 broadcast_select_fusion.6
  44.5 2.3 %dynamic-slice_bitcast_fusion = (bf16[1,1024,256]{2,1,0:T(8,128)(2,1)}, bf16[1024,256]{1,0:T(8,128)(2,1)}) fusion(bf16[2048,256]{1,0:T(8,128)(2,1)} %param.19, s32[]{:T(128)S(6)} %select_n.192, s32[]{:T(128)S(6)} %select_n.191), kind=kLoop, calls=%fused_computation.28 | loop fusion | bytes 2097160 | tf_op jit(solution)/shard_map/stack | solution.py:551
  46.8 0.8 slice.25
  47.6 1.2 collective-permute-start.12
  48.9 4.5 %collective-permute-done.6.near = bf16[2,256,512]{2,1,0:T(8,128)(2,1)S(1)} collective-permute-done((bf16[2,256,512]{2,1,0:T(8,128)(2,1)S(1)}, bf16[2,256,512]{2,1,0:T(8,128)(2,1)S(1)}, u32[]{:S(2)}, u32[]{:S(2)}) %collective-permute-start.6) | collective-permute-done | bytes 524320 | tf_op jit(solution)/shard_map/ppermute | solution.py:200
  53.4 7.2 %collective-permute-done.5 = bf16[144,2048]{1,0:T(8,128)(2,1)} collective-permute-done((bf16[144,2048]{1,0:T(8,128)(2,1)}, bf16[144,2048]{1,0:T(8,128)(2,1)}, u32[]{:S(2)}, u32[]{:S(2)}) %collective-permute-start.5) | collective-permute-done | bytes 589856 | tf_op jit(solution)/shard_map/ppermute | solution.py:200
  60.6 6.1 %collective-permute-start.13 = (bf16[1,256,1024]{2,1,0:T(8,128)(2,1)}, bf16[1,256,1024]{2,1,0:T(8,128)(2,1)S(1)}, u32[]{:S(2)}, u32[]{:S(2)}) collective-permute-start(bf16[1,256,1024]{2,1,0:T(8,128)(2,1)} %collective-permute-done.8.refs_3_), channel_id=1, source_target_pairs={{0,2},{1,5},{2,0},{3,7},{4,6},{5,1},{6,4},{7,3},{8,10},{9,13},{10,... | collective-permute-start | bytes 1572872 | tf_op jit(solution)/shard_map/ppermute | solution.py:200
  66.6 1.0 broadcast_select_fusion.2
  67.7 1.5 slice_select_fusion
  69.2 0.8 slice.22
  70.2 0.9 copy-done.3
  71.6 1.1 pad_maximum_fusion.3
  72.7 1.5 collective-permute-done.13.refs_4_
  74.2 2.1 %pad_maximum_fusion.5 = bf16[2,256,1024]{2,1,0:T(8,128)(2,1)} fusion(bf16[1,256,1024]{2,1,0:T(8,128)(2,1)S(1)} %collective-permute-done.13.refs_4_, bf16[1,256,1024]{2,1,0:T(8,128)(2,1)} %collective-permute-done.8.refs_3_), kind=kLoop, calls=%fused_computation.11 | loop fusion | flops 524288 | bytes 2097152 | tf_op jit(solution)/shard_map/concatenate | solution.py:518
  76.4 0.8 copy-done.7
  78.0 0.9 slice.23.old1
  78.9 8.9 %collective-permute-done.11.far = bf16[4,256,512]{2,1,0:T(8,128)(2,1)} collective-permute-done((bf16[4,256,512]{2,1,0:T(8,128)(2,1)}, bf16[4,256,512]{2,1,0:T(8,128)(2,1)}, u32[]{:S(2)}, u32[]{:S(2)}) %collective-permute-start.11) | collective-permute-done | bytes 1048608 | tf_op jit(solution)/shard_map/ppermute | solution.py:200
  87.9 1.0 copy-done.4
  88.9 3.1 %keys_part.1 = (f32[576,256]{1,0:T(8,128)S(1)}, bf16[736,256]{1,0:T(8,128)(2,1)S(1)}) custom-call(s32[4]{0:T(128)S(1)} %pad_add_fusion.where_ref, bf16[288,2048]{1,0:T(8,128)(2,1)S(1)} %pad_maximum_fusion.1.x0, bf16[288,2048]{1,0:T(8,128)(2,1)S(1)} %collective-permute-done.10.x1, bf16[2,256,512]{2,1,0:T(8,128)(2,1)S(1)} %pad_maximum_fusion.6.own, ...), custom_call_target="tpu_custom_call" | custom-call | tf_op jit(solution)/shard_map/keys_part/pallas_call | solution.py:539
  92.0 1.4 collective-permute-start.15
  93.4 1.1 pad_maximum_fusion.4.w_own
  94.6 4.5 %collective-permute-done.14.refs_5_ = bf16[2,256,1024]{2,1,0:T(8,128)(2,1)} collective-permute-done((bf16[2,256,1024]{2,1,0:T(8,128)(2,1)}, bf16[2,256,1024]{2,1,0:T(8,128)(2,1)}, u32[]{:S(2)}, u32[]{:S(2)}) %collective-permute-start.14) | collective-permute-done | bytes 1048608 | tf_op jit(solution)/shard_map/ppermute | solution.py:200
  99.3 1.4 fusion.10
  101.9 4.7 %queries_part.1 = (f32[4,128,512]{2,1,0:T(8,128)S(1)}, bf16[4,128,512]{2,1,0:T(8,128)(2,1)S(1)}) custom-call(s32[4]{0:T(128)S(1)} %pad_add_fusion.where_ref, bf16[288,2048]{1,0:T(8,128)(2,1)} %copy-done, bf16[288,2048]{1,0:T(8,128)(2,1)} %copy-done.1, bf16[1,256,1024]{2,1,0:T(8,128)(2,1)S(1)} %maximum_bitcast_fusion.refs_0_, ...), custom_call_target="tpu_custom_call" | custom-call | tf_op jit(solution)/shard_map/queries_part/pallas_call | solution.py:554
  106.7 1.3 collective-permute-done.15.got_ref
  108.0 1.0 keys_join.1.kv0
  109.0 1.8 collective-permute-start.17
  110.8 3.4 %collective-permute-start.20 = (bf16[4,128,512]{2,1,0:T(8,128)(2,1)S(1)}, bf16[4,128,512]{2,1,0:T(8,128)(2,1)S(1)}, u32[]{:S(2)}, u32[]{:S(2)}) collective-permute-start(bf16[4,128,512]{2,1,0:T(8,128)(2,1)S(1)} %get-tuple-element.56), channel_id=1, source_target_pairs={{0,16},{1,17},{2,18},{3,19},{4,20},{5,21},{6,22},{7,23},{8,24},{9,... | collective-permute-start | bytes 1572872 | tf_op jit(solution)/shard_map/ppermute | solution.py:200
  114.2 1.4 collective-permute-start.16
  115.6 4.6 %collective-permute-done.17.kv1 = bf16[6,128,256]{2,1,0:T(8,128)(2,1)S(1)} collective-permute-done((bf16[6,128,256]{2,1,0:T(8,128)(2,1)S(1)}, bf16[6,128,256]{2,1,0:T(8,128)(2,1)S(1)}, u32[]{:S(2)}, u32[]{:S(2)}) %collective-permute-start.17) | collective-permute-done | bytes 393248 | tf_op jit(solution)/shard_map/ppermute | solution.py:200
  120.2 1.8 collective-permute-done.16.kv2
  122.0 13.2 %collective-permute-done.20.got_ref = bf16[4,128,512]{2,1,0:T(8,128)(2,1)S(1)} collective-permute-done((bf16[4,128,512]{2,1,0:T(8,128)(2,1)S(1)}, bf16[4,128,512]{2,1,0:T(8,128)(2,1)S(1)}, u32[]{:S(2)}, u32[]{:S(2)}) %collective-permute-start.20) | collective-permute-done | bytes 524320 | tf_op jit(solution)/shard_map/ppermute | solution.py:200
  135.4 1.4 collective-permute-start.22
  136.8 9.0 %attend.1.own_ref = bf16[512,512]{1,0:T(8,128)(2,1)S(1)} custom-call(s32[4]{0:T(128)S(1)} %pad_add_fusion.where_ref, f32[4,128,512]{2,1,0:T(8,128)S(1)} %get-tuple-element.50.keep_ref, bf16[4,128,512]{2,1,0:T(8,128)(2,1)S(1)} %collective-permute-done.20.got_ref, f32[4,192,128]{2,1,0:T(8,128)S(1)} %pad_maximum_fusion.9.cos_ref, ...), custom_call_target="tpu_custom_call" | custom-call | tf_op jit(solution)/shard_map/attend/pallas_call | solution.py:593
  145.8 2.3 %collective-permute-start.21 = (bf16[512,512]{1,0:T(8,128)(2,1)S(1)}, bf16[512,512]{1,0:T(8,128)(2,1)S(1)}, u32[]{:S(2)}, u32[]{:S(2)}) collective-permute-start(bf16[512,512]{1,0:T(8,128)(2,1)S(1)} %attend.1.own_ref), channel_id=1, source_target_pairs={{0,8},{1,9},{2,10},{3,11},{4,12},{5,13},{6,14},{7,15},{8,0},{9,1},... | collective-permute-start | bytes 1572872 | tf_op jit(solution)/shard_map/ppermute | solution.py:200
  148.1 12.5 %collective-permute-done.21.next_ref = bf16[512,512]{1,0:T(8,128)(2,1)S(1)} collective-permute-done((bf16[512,512]{1,0:T(8,128)(2,1)S(1)}, bf16[512,512]{1,0:T(8,128)(2,1)S(1)}, u32[]{:S(2)}, u32[]{:S(2)}) %collective-permute-start.21) | collective-permute-done | bytes 524320 | tf_op jit(solution)/shard_map/ppermute | solution.py:200
  160.5 0.9 collective-permute-done.22.w_far
  161.5 1.4 copy-done.16
  162.8 8.7 %output.1 = (f32[512,1024]{1,0:T(8,128)}, bf16[512,1024]{1,0:T(8,128)(2,1)S(1)}) custom-call(s32[4]{0:T(128)S(1)} %pad_add_fusion.where_ref, bf16[512,512]{1,0:T(8,128)(2,1)S(1)} %attend.1.own_ref, bf16[512,512]{1,0:T(8,128)(2,1)S(1)} %collective-permute-done.21.next_ref, bf16[2,1024,256]{2,1,0:T(8,128)(2,1)S(1)} %pad_maximum_fusion.4.w_own, ...), custom_call_target="tpu_custom_call" | custom-call | tf_op jit(solution)/shard_map/output/pallas_call | solution.py:604
  171.6 2.7 %collective-permute-done.23 = bf16[512,1024]{1,0:T(8,128)(2,1)S(1)} collective-permute-done((bf16[512,1024]{1,0:T(8,128)(2,1)S(1)}, bf16[512,1024]{1,0:T(8,128)(2,1)S(1)}, u32[]{:S(2)}, u32[]{:S(2)}) %collective-permute-start.23) | collective-permute-done | bytes 1048608 | tf_op jit(solution)/shard_map/ppermute | solution.py:200
  174.2 1.9 convert_add_fusion
  176.1 0.8 fusion.7
  176.9 3.4 %collective-permute-start.24 = (bf16[128,1024]{1,0:T(8,128)(2,1)}, bf16[128,1024]{1,0:T(8,128)(2,1)S(1)}, u32[]{:S(2)}, u32[]{:S(2)}) collective-permute-start(bf16[128,1024]{1,0:T(8,128)(2,1)} %get-tuple-element.67), channel_id=1, source_target_pairs={{0,16},{1,17},{2,18},{3,19},{4,20},{5,21},{6,22},{7,23},{8,24},{9,... | collective-permute-start | bytes 786440 | tf_op jit(solution)/shard_map/ppermute | solution.py:200
  180.3 1.3 collective-permute-start.25
  182.3 9.7 %collective-permute-done.24 = bf16[128,1024]{1,0:T(8,128)(2,1)S(1)} collective-permute-done((bf16[128,1024]{1,0:T(8,128)(2,1)}, bf16[128,1024]{1,0:T(8,128)(2,1)S(1)}, u32[]{:S(2)}, u32[]{:S(2)}) %collective-permute-start.24) | collective-permute-done | bytes 262176 | tf_op jit(solution)/shard_map/ppermute | solution.py:200
  192.0 10.8 %collective-permute-done.25 = bf16[128,1024]{1,0:T(8,128)(2,1)S(1)} collective-permute-done((bf16[128,1024]{1,0:T(8,128)(2,1)S(1)}, bf16[128,1024]{1,0:T(8,128)(2,1)S(1)}, u32[]{:S(2)}, u32[]{:S(2)}) %collective-permute-start.25) | collective-permute-done | bytes 262176 | tf_op jit(solution)/shard_map/ppermute | solution.py:200
  202.8 1.2 collective-permute-done.26
  204.3 0.8 pad_maximum_fusion.8
  (104 shorter events, 8.3 us)
Async XLA Ops:
  0.0 3.0 %copy-start.20 = (bf16[256,512]{1,0:T(8,128)(2,1)S(1)}, bf16[256,512]{1,0:T(8,128)(2,1)}, u32[]{:S(2)}) copy-start(bf16[256,512]{1,0:T(8,128)(2,1)} %param.18) | copy-start | bytes 786436
  0.0 3.0 %copy-start.21 = (bf16[256,512]{1,0:T(8,128)(2,1)S(1)}, bf16[256,512]{1,0:T(8,128)(2,1)}, u32[]{:S(2)}) copy-start(bf16[256,512]{1,0:T(8,128)(2,1)} %param.17) | copy-start | bytes 786436
  1.3 3.9 %copy-start.26 = (s32[8]{0:T(128)S(1)}, s32[8]{0:T(128)}, u32[]{:S(2)}) copy-start(s32[8]{0:T(128)} %param.23) | copy-start | bytes 100
  1.4 4.5 %copy-start.18 = (bf16[32,2048]{1,0:T(8,128)(2,1)S(1)}, bf16[32,2048]{1,0:T(8,128)(2,1)}, u32[]{:S(2)}) copy-start(bf16[32,2048]{1,0:T(8,128)(2,1)} %param.14) | copy-start | bytes 393220
  1.4 4.7 %copy-start.11 = (bf16[128,2048]{1,0:T(8,128)(2,1)S(1)}, bf16[128,2048]{1,0:T(8,128)(2,1)}, u32[]{:S(2)}) copy-start(bf16[128,2048]{1,0:T(8,128)(2,1)} %param.13) | copy-start | bytes 1572868
  1.4 4.7 %copy-start.19 = (bf16[8,2048]{1,0:T(8,128)(2,1)S(1)}, bf16[8,2048]{1,0:T(8,128)(2,1)}, u32[]{:S(2)}) copy-start(bf16[8,2048]{1,0:T(8,128)(2,1)} %param.22) | copy-start | bytes 98308
  1.4 20.4 %collective-permute-start.2 = (bf16[1,256,1024]{2,1,0:T(8,128)(2,1)S(1)}, bf16[1,256,1024]{2,1,0:T(8,128)(2,1)S(1)}, u32[]{:S(2)}, u32[]{:S(2)}) collective-permute-start(bf16[1,256,1024]{2,1,0:T(8,128)(2,1)S(1)} %maximum_bitcast_fusion.refs_0_), channel_id=1, source_target_pairs={{0,2},{1,5},{2,0},{3,7},{4,6},{5,1},{6,4},{7,3},{8,10},{9,13},{10,... | collective-permute-start | bytes 1572872 | tf_op jit(solution)/shard_map/ppermute | solution.py:200
  3.8 5.1 %copy-start.25 = (f32[4096]{0:T(1024)S(1)}, f32[4096]{0:T(1024)}, u32[]{:S(2)}) copy-start(f32[4096]{0:T(1024)} %param.15) | copy-start | bytes 49156
  5.4 16.4 %collective-permute-start.1 = (bf16[336,512]{1,0:T(8,128)(2,1)S(1)}, bf16[336,512]{1,0:T(8,128)(2,1)}, u32[]{:S(2)}, u32[]{:S(2)}) collective-permute-start(bf16[336,512]{1,0:T(8,128)(2,1)S(1)} %pad_maximum_fusion.11), channel_id=1, source_target_pairs={{0,8},{1,9},{2,10},{3,11},{4,12},{5,13},{6,14},{7,15},{8,0},{9,1},... | collective-permute-start | bytes 1032200 | tf_op jit(solution)/shard_map/ppermute | solution.py:200
  9.3 12.5 %collective-permute-start = (bf16[144,2048]{1,0:T(8,128)(2,1)S(1)}, bf16[144,2048]{1,0:T(8,128)(2,1)}, u32[]{:S(2)}, u32[]{:S(2)}) collective-permute-start(bf16[144,2048]{1,0:T(8,128)(2,1)S(1)} %fusion.2), channel_id=1, source_target_pairs={{1,16},{3,18},{5,20},{7,22},{9,24},{11,26},{13,28},{15,30},{16,1},... | collective-permute-start | bytes 1769480 | tf_op jit(solution)/shard_map/ppermute | solution.py:200
  11.6 9.5 %collective-permute-start.3 = (bf16[32,2048]{1,0:T(8,128)(2,1)}, bf16[32,2048]{1,0:T(8,128)(2,1)}, u32[]{:S(2)}, u32[]{:S(2)}) collective-permute-start(bf16[32,2048]{1,0:T(8,128)(2,1)} %fusion.6), channel_id=1, source_target_pairs={{0,0},{1,16},{2,8},{3,24},{4,1},{5,17},{6,9},{7,25},{8,2},{9,18},{... | collective-permute-start | bytes 393224 | tf_op jit(solution)/shard_map/ppermute | solution.py:200
  15.0 6.8 %collective-permute-start.4 = (bf16[32,2048]{1,0:T(8,128)(2,1)}, bf16[32,2048]{1,0:T(8,128)(2,1)}, u32[]{:S(2)}, u32[]{:S(2)}) collective-permute-start(bf16[32,2048]{1,0:T(8,128)(2,1)} %fusion.6), channel_id=1, source_target_pairs={{0,8},{1,24},{2,0},{3,16},{4,9},{5,25},{6,1},{7,17},{8,10},{9,26},... | collective-permute-start | bytes 393224 | tf_op jit(solution)/shard_map/ppermute | solution.py:200
  16.0 21.8 %copy-start.12 = (bf16[1,256,512]{2,1,0:T(8,128)(2,1)}, bf16[1,256,512]{2,1,0:T(8,128)(2,1)S(1)}, u32[]{:S(2)}) copy-start(bf16[1,256,512]{2,1,0:T(8,128)(2,1)S(1)} %maximum_bitcast_fusion.2) | copy-start | bytes 786436
  21.1 26.6 %collective-permute-start.8 = (bf16[1,256,1024]{2,1,0:T(8,128)(2,1)}, bf16[1,256,1024]{2,1,0:T(8,128)(2,1)}, u32[]{:S(2)}, u32[]{:S(2)}) collective-permute-start(bf16[1,256,1024]{2,1,0:T(8,128)(2,1)} %maximum_bitcast_fusion.1), channel_id=1, source_target_pairs={{0,8},{1,9},{2,10},{3,11},{4,12},{5,13},{6,14},{7,15},{8,0},{9,1},... | collective-permute-start | bytes 1572872 | tf_op jit(solution)/shard_map/ppermute | solution.py:200
  21.8 15.9 %copy-start.5 = (bf16[1,256,1024]{2,1,0:T(8,128)(2,1)}, bf16[1,256,1024]{2,1,0:T(8,128)(2,1)S(1)}, u32[]{:S(2)}) copy-start(bf16[1,256,1024]{2,1,0:T(8,128)(2,1)S(1)} %collective-permute-done.2.refs_1_) | copy-start | bytes 1572868
  23.0 37.6 %collective-permute-start.9 = (bf16[2,256,1024]{2,1,0:T(8,128)(2,1)}, bf16[2,256,1024]{2,1,0:T(8,128)(2,1)S(1)}, u32[]{:S(2)}, u32[]{:S(2)}) collective-permute-start(bf16[2,256,1024]{2,1,0:T(8,128)(2,1)} %pad_maximum_fusion.2), channel_id=1, source_target_pairs={{0,4},{1,3},{2,6},{3,1},{4,0},{5,7},{6,2},{7,5},{8,12},{9,11},{10,... | collective-permute-start | bytes 3145736 | tf_op jit(solution)/shard_map/ppermute | solution.py:200
  37.8 0.7 copy-start.14
  38.5 4.3 %copy-start.27 = (s32[4]{0:T(128)S(1)}, s32[4]{0:T(128)}, u32[]{:S(2)}) copy-start(s32[4]{0:T(128)} %constant.117.clone) | copy-start | bytes 52
  38.5 14.9 %collective-permute-start.6 = (bf16[2,256,512]{2,1,0:T(8,128)(2,1)S(1)}, bf16[2,256,512]{2,1,0:T(8,128)(2,1)S(1)}, u32[]{:S(2)}, u32[]{:S(2)}) collective-permute-start(bf16[2,256,512]{2,1,0:T(8,128)(2,1)S(1)} %pad_maximum_fusion.6.own), channel_id=1, source_target_pairs={{0,2},{1,5},{2,0},{3,7},{4,6},{5,1},{6,4},{7,3},{8,10},{9,13},{10,... | collective-permute-start | bytes 1572872 | tf_op jit(solution)/shard_map/ppermute | solution.py:200
  39.8 20.8 %collective-permute-start.5 = (bf16[144,2048]{1,0:T(8,128)(2,1)}, bf16[144,2048]{1,0:T(8,128)(2,1)}, u32[]{:S(2)}, u32[]{:S(2)}) collective-permute-start(bf16[144,2048]{1,0:T(8,128)(2,1)} %broadcast_select_fusion), channel_id=1, source_target_pairs={{0,8},{1,9},{2,10},{3,11},{4,12},{5,13},{6,14},{7,15},{8,0},{9,1},... | collective-permute-start | bytes 1769480 | tf_op jit(solution)/shard_map/ppermute | solution.py:200
  42.3 6.6 %collective-permute-start.7 = (bf16[64,2048]{1,0:T(8,128)(2,1)S(1)}, bf16[64,2048]{1,0:T(8,128)(2,1)}, u32[]{:S(2)}, u32[]{:S(2)}) collective-permute-start(bf16[64,2048]{1,0:T(8,128)(2,1)S(1)} %pad_maximum_fusion.12), channel_id=1, source_target_pairs={{0,1},{1,0},{2,3},{3,2},{4,5},{5,4},{6,7},{7,6},{8,9},{9,8},{10,11... | collective-permute-start | bytes 786440 | tf_op jit(solution)/shard_map/ppermute | solution.py:200
  47.6 44.4 %collective-permute-start.12 = (bf16[1024,256]{1,0:T(8,128)(2,1)}, bf16[1024,256]{1,0:T(8,128)(2,1)}, u32[]{:S(2)}, u32[]{:S(2)}) collective-permute-start(bf16[1024,256]{1,0:T(8,128)(2,1)} %get-tuple-element.71), channel_id=1, source_target_pairs={{0,16},{1,17},{2,18},{3,19},{4,20},{5,21},{6,22},{7,23},{8,24},{9,... | collective-permute-start | bytes 1572872 | tf_op jit(solution)/shard_map/ppermute | solution.py:200
  53.4 15.8 %copy-start.2 = (bf16[2,256,512]{2,1,0:T(8,128)(2,1)}, bf16[2,256,512]{2,1,0:T(8,128)(2,1)S(1)}, u32[]{:S(2)}) copy-start(bf16[2,256,512]{2,1,0:T(8,128)(2,1)S(1)} %collective-permute-done.6.near) | copy-start | bytes 1572868
  60.6 8.6 %copy-start.9 = (bf16[2,256,1024]{2,1,0:T(8,128)(2,1)}, bf16[2,256,1024]{2,1,0:T(8,128)(2,1)S(1)}, u32[]{:S(2)}) copy-start(bf16[2,256,1024]{2,1,0:T(8,128)(2,1)S(1)} %collective-permute-done.9.refs_2_) | copy-start | bytes 3145732
  60.6 13.7 %collective-permute-start.13 = (bf16[1,256,1024]{2,1,0:T(8,128)(2,1)}, bf16[1,256,1024]{2,1,0:T(8,128)(2,1)S(1)}, u32[]{:S(2)}, u32[]{:S(2)}) collective-permute-start(bf16[1,256,1024]{2,1,0:T(8,128)(2,1)} %collective-permute-done.8.refs_3_), channel_id=1, source_target_pairs={{0,2},{1,5},{2,0},{3,7},{4,6},{5,1},{6,4},{7,3},{8,10},{9,13},{10,... | collective-permute-start | bytes 1572872 | tf_op jit(solution)/shard_map/ppermute | solution.py:200
  70.0 1.1 copy-start.3
  70.0 1.4 copy-start.13
  70.0 1.6 copy-start.15
  70.1 17.7 %copy-start = (bf16[288,2048]{1,0:T(8,128)(2,1)}, bf16[288,2048]{1,0:T(8,128)(2,1)S(1)}, u32[]{:S(2)}) copy-start(bf16[288,2048]{1,0:T(8,128)(2,1)S(1)} %pad_maximum_fusion.1.x0) | copy-start | bytes 3538948
  70.2 17.7 %collective-permute-start.10 = (bf16[288,2048]{1,0:T(8,128)(2,1)S(1)}, bf16[288,2048]{1,0:T(8,128)(2,1)S(1)}, u32[]{:S(2)}, u32[]{:S(2)}) collective-permute-start(bf16[288,2048]{1,0:T(8,128)(2,1)S(1)} %pad_maximum_fusion.1.x0), channel_id=1, source_target_pairs={{0,1},{1,0},{2,3},{3,2},{4,5},{5,4},{6,7},{7,6},{8,9},{9,8},{10,11... | collective-permute-start | bytes 3538952 | tf_op jit(solution)/shard_map/ppermute | solution.py:200
  72.7 5.2 %copy-start.22 = (bf16[64,128]{1,0:T(8,128)(2,1)S(1)}, bf16[64,128]{1,0:T(8,128)(2,1)}, u32[]{:S(2)}) copy-start(bf16[64,128]{1,0:T(8,128)(2,1)} %get-tuple-element.97) | copy-start | bytes 49156
  72.7 5.2 %copy-start.23 = (bf16[64,128]{1,0:T(8,128)(2,1)S(1)}, bf16[64,128]{1,0:T(8,128)(2,1)}, u32[]{:S(2)}) copy-start(bf16[64,128]{1,0:T(8,128)(2,1)} %get-tuple-element.103) | copy-start | bytes 49156
  72.7 5.2 %copy-start.24 = (bf16[64,128]{1,0:T(8,128)(2,1)S(1)}, bf16[64,128]{1,0:T(8,128)(2,1)}, u32[]{:S(2)}) copy-start(bf16[64,128]{1,0:T(8,128)(2,1)} %get-tuple-element.106) | copy-start | bytes 49156
  72.7 15.1 %collective-permute-start.11 = (bf16[4,256,512]{2,1,0:T(8,128)(2,1)}, bf16[4,256,512]{2,1,0:T(8,128)(2,1)}, u32[]{:S(2)}, u32[]{:S(2)}) collective-permute-start(bf16[4,256,512]{2,1,0:T(8,128)(2,1)} %pad_maximum_fusion.3), channel_id=1, source_target_pairs={{0,4},{1,3},{2,6},{3,1},{4,0},{5,7},{6,2},{7,5},{8,12},{9,11},{10,... | collective-permute-start | bytes 3145736 | tf_op jit(solution)/shard_map/ppermute | solution.py:200
  76.4 0.8 copy-start.7
  77.2 21.9 %collective-permute-start.14 = (bf16[2,256,1024]{2,1,0:T(8,128)(2,1)}, bf16[2,256,1024]{2,1,0:T(8,128)(2,1)}, u32[]{:S(2)}, u32[]{:S(2)}) collective-permute-start(bf16[2,256,1024]{2,1,0:T(8,128)(2,1)} %pad_maximum_fusion.5), channel_id=1, source_target_pairs={{0,4},{1,3},{2,6},{3,1},{4,0},{5,7},{6,2},{7,5},{8,12},{9,11},{10,... | collective-permute-start | bytes 3145736 | tf_op jit(solution)/shard_map/ppermute | solution.py:200
  87.9 1.0 copy-start.4
  88.9 3.1 %copy-start.1 = (bf16[288,2048]{1,0:T(8,128)(2,1)}, bf16[288,2048]{1,0:T(8,128)(2,1)S(1)}, u32[]{:S(2)}) copy-start(bf16[288,2048]{1,0:T(8,128)(2,1)S(1)} %collective-permute-done.10.x1) | copy-start | bytes 3538948
  88.9 4.5 %copy-start.17 = (bf16[1,1024,256]{2,1,0:T(8,128)(2,1)S(1)}, bf16[1,1024,256]{2,1,0:T(8,128)(2,1)}, u32[]{:S(2)}) copy-start(bf16[1,1024,256]{2,1,0:T(8,128)(2,1)} %get-tuple-element.70) | copy-start | bytes 1572868
  92.0 16.0 %collective-permute-start.15 = (bf16[736,256]{1,0:T(8,128)(2,1)S(1)}, bf16[736,256]{1,0:T(8,128)(2,1)S(1)}, u32[]{:S(2)}, u32[]{:S(2)}) collective-permute-start(bf16[736,256]{1,0:T(8,128)(2,1)S(1)} %get-tuple-element.52), channel_id=1, source_target_pairs={{0,16},{1,17},{2,18},{3,19},{4,20},{5,21},{6,22},{7,23},{8,24},{9,... | collective-permute-start | bytes 1130504 | tf_op jit(solution)/shard_map/ppermute | solution.py:200
  99.1 36.1 %collective-permute-start.19 = (bf16[2,1024,256]{2,1,0:T(8,128)(2,1)S(1)}, bf16[2,1024,256]{2,1,0:T(8,128)(2,1)S(1)}, u32[]{:S(2)}, u32[]{:S(2)}) collective-permute-start(bf16[2,1024,256]{2,1,0:T(8,128)(2,1)S(1)} %pad_maximum_fusion.4.w_own), channel_id=1, source_target_pairs={{0,2},{1,5},{2,0},{3,7},{4,6},{5,1},{6,4},{7,3},{8,10},{9,13},{10,... | collective-permute-start | bytes 3145736 | tf_op jit(solution)/shard_map/ppermute | solution.py:200
  99.3 1.8 copy-start.10
  100.7 1.0 copy-start.6
  100.7 1.2 copy-start.8
  109.0 11.2 %collective-permute-start.17 = (bf16[6,128,256]{2,1,0:T(8,128)(2,1)S(1)}, bf16[6,128,256]{2,1,0:T(8,128)(2,1)S(1)}, u32[]{:S(2)}, u32[]{:S(2)}) collective-permute-start(bf16[6,128,256]{2,1,0:T(8,128)(2,1)S(1)} %keys_join.1.kv0), channel_id=1, source_target_pairs={{0,2},{1,5},{2,0},{3,7},{4,6},{5,1},{6,4},{7,3},{8,10},{9,13},{10,... | collective-permute-start | bytes 1179656 | tf_op jit(solution)/shard_map/ppermute | solution.py:200
  110.8 24.3 %collective-permute-start.20 = (bf16[4,128,512]{2,1,0:T(8,128)(2,1)S(1)}, bf16[4,128,512]{2,1,0:T(8,128)(2,1)S(1)}, u32[]{:S(2)}, u32[]{:S(2)}) collective-permute-start(bf16[4,128,512]{2,1,0:T(8,128)(2,1)S(1)} %get-tuple-element.56), channel_id=1, source_target_pairs={{0,16},{1,17},{2,18},{3,19},{4,20},{5,21},{6,22},{7,23},{8,24},{9,... | collective-permute-start | bytes 1572872 | tf_op jit(solution)/shard_map/ppermute | solution.py:200
  114.2 7.8 %collective-permute-start.16 = (bf16[6,128,256]{2,1,0:T(8,128)(2,1)S(1)}, bf16[6,128,256]{2,1,0:T(8,128)(2,1)S(1)}, u32[]{:S(2)}, u32[]{:S(2)}) collective-permute-start(bf16[6,128,256]{2,1,0:T(8,128)(2,1)S(1)} %keys_join.1.kv0), channel_id=1, source_target_pairs={{0,4},{1,3},{2,6},{3,1},{4,0},{5,7},{6,2},{7,5},{8,12},{9,11},{10,... | collective-permute-start | bytes 1179656 | tf_op jit(solution)/shard_map/ppermute | solution.py:200
  120.2 15.0 %collective-permute-start.18 = (bf16[6,128,256]{2,1,0:T(8,128)(2,1)S(1)}, bf16[6,128,256]{2,1,0:T(8,128)(2,1)S(1)}, u32[]{:S(2)}, u32[]{:S(2)}) collective-permute-start(bf16[6,128,256]{2,1,0:T(8,128)(2,1)S(1)} %collective-permute-done.17.kv1), channel_id=1, source_target_pairs={{0,4},{1,3},{2,6},{3,1},{4,0},{5,7},{6,2},{7,5},{8,12},{9,11},{10,... | collective-permute-start | bytes 1179656 | tf_op jit(solution)/shard_map/ppermute | solution.py:200
  135.4 26.1 %collective-permute-start.22 = (bf16[4,1024,256]{2,1,0:T(8,128)(2,1)S(1)}, bf16[4,1024,256]{2,1,0:T(8,128)(2,1)S(1)}, u32[]{:S(2)}, u32[]{:S(2)}) collective-permute-start(bf16[4,1024,256]{2,1,0:T(8,128)(2,1)S(1)} %pad_maximum_fusion), channel_id=1, source_target_pairs={{0,4},{1,3},{2,6},{3,1},{4,0},{5,7},{6,2},{7,5},{8,12},{9,11},{10,... | collective-permute-start | bytes 6291464 | tf_op jit(solution)/shard_map/ppermute | solution.py:200
  145.8 14.8 %collective-permute-start.21 = (bf16[512,512]{1,0:T(8,128)(2,1)S(1)}, bf16[512,512]{1,0:T(8,128)(2,1)S(1)}, u32[]{:S(2)}, u32[]{:S(2)}) collective-permute-start(bf16[512,512]{1,0:T(8,128)(2,1)S(1)} %attend.1.own_ref), channel_id=1, source_target_pairs={{0,8},{1,9},{2,10},{3,11},{4,12},{5,13},{6,14},{7,15},{8,0},{9,1},... | collective-permute-start | bytes 1572872 | tf_op jit(solution)/shard_map/ppermute | solution.py:200
  161.5 1.4 copy-start.16
  171.6 2.7 %collective-permute-start.23 = (bf16[512,1024]{1,0:T(8,128)(2,1)S(1)}, bf16[512,1024]{1,0:T(8,128)(2,1)S(1)}, u32[]{:S(2)}, u32[]{:S(2)}) collective-permute-start(bf16[512,1024]{1,0:T(8,128)(2,1)S(1)} %get-tuple-element.62), channel_id=1, source_target_pairs={{0,1},{1,0},{2,3},{3,2},{4,5},{5,4},{6,7},{7,6},{8,9},{9,8},{10,11... | collective-permute-start | bytes 3145736 | tf_op jit(solution)/shard_map/ppermute | solution.py:200
  176.9 15.1 %collective-permute-start.24 = (bf16[128,1024]{1,0:T(8,128)(2,1)}, bf16[128,1024]{1,0:T(8,128)(2,1)S(1)}, u32[]{:S(2)}, u32[]{:S(2)}) collective-permute-start(bf16[128,1024]{1,0:T(8,128)(2,1)} %get-tuple-element.67), channel_id=1, source_target_pairs={{0,16},{1,17},{2,18},{3,19},{4,20},{5,21},{6,22},{7,23},{8,24},{9,... | collective-permute-start | bytes 786440 | tf_op jit(solution)/shard_map/ppermute | solution.py:200
  180.3 22.5 %collective-permute-start.25 = (bf16[128,1024]{1,0:T(8,128)(2,1)S(1)}, bf16[128,1024]{1,0:T(8,128)(2,1)S(1)}, u32[]{:S(2)}, u32[]{:S(2)}) collective-permute-start(bf16[128,1024]{1,0:T(8,128)(2,1)S(1)} %get-tuple-element.69), channel_id=1, source_target_pairs={{0,8},{1,9},{2,10},{3,11},{4,12},{5,13},{6,14},{7,15},{8,16},{9,17... | collective-permute-start | bytes 786440 | tf_op jit(solution)/shard_map/ppermute | solution.py:200
  181.6 22.4 %collective-permute-start.26 = (bf16[128,1024]{1,0:T(8,128)(2,1)S(1)}, bf16[128,1024]{1,0:T(8,128)(2,1)S(1)}, u32[]{:S(2)}, u32[]{:S(2)}) collective-permute-start(bf16[128,1024]{1,0:T(8,128)(2,1)S(1)} %get-tuple-element.68), channel_id=1, source_target_pairs={{0,24},{1,25},{2,26},{3,27},{4,28},{5,29},{6,30},{7,31},{8,0},{9,1... | collective-permute-start | bytes 786440 | tf_op jit(solution)/shard_map/ppermute | solution.py:200

commit v6 on v5

--- a/solution.py
+++ b/solution.py
@@ -302,10 +302,12 @@
 
 
 def queries_part_kernel(where_ref, x0, x1, *refs):
-    pieces = []
-    for own, near, far in (refs[0:3], refs[3:6]):
-        pieces.append([own.at[0], near.at[0], far.at[0], far.at[1]])
-    keep_ref, send_ref = refs[6:]
+    next_own, next_near, next_far = refs[4:7]
+    pieces = [
+        [ref.at[0] for ref in refs[:4]],
+        [next_own.at[0], next_near.at[0], next_far.at[0], next_far.at[1]],
+    ]
+    keep_ref, send_ref = refs[7:]
     block = x0.shape[0] // 2
     tok = block - REC_PAD
     width = 4 * HD
@@ -369,32 +371,24 @@
             ]
 
 
-def output_kernel(where_ref, own_ref, next_ref, w_own, w_near, w_far, mine_ref, other_ref):
+def output_kernel(where_ref, own_ref, next_ref, w_own, w_near, w_far, mine_ref, other_ref, x_ref):
     level, place, core = where_ref[0], where_ref[1], where_ref[2]
     depth = own_ref.shape[1]
     width = w_own.shape[2]
-    start = pl.multiple_of(lax.rem(level, 2) * depth, depth)
-    start_next = pl.multiple_of(lax.rem(level + 1, 2) * depth, depth)
-    for i in range(2):
+    tok = mine_ref.shape[1]
+    x_ref[:, pl.ds(pl.multiple_of(lax.rem(level, 2) * depth, depth), depth)] = own_ref[...]
+    x_ref[:, pl.ds(pl.multiple_of(lax.rem(level + 1, 2) * depth, depth), depth)] = next_ref[...]
+    swap = jnp.where(core == level // 2, 0, 1)
+    for s, out_ref in enumerate((mine_ref, other_ref)):
+        i = jnp.bitwise_xor(swap, s)
         for j in range(PLANE):
             weights = (w_own.at[i], w_near.at[i], w_far.at[i], w_far.at[2 + i])[j]
-            part = jnp.dot(
-                own_ref[...], weights[pl.ds(start, depth), :], preferred_element_type=jnp.float32
-            ) + jnp.dot(
-                next_ref[...],
-                weights[pl.ds(start_next, depth), :],
-                preferred_element_type=jnp.float32,
-            )
+            part = jnp.dot(x_ref[...], weights[...], preferred_element_type=jnp.float32)
             to = pl.multiple_of(place_of(j, place, core) * width, width)
-            mine = (core == level // 2) if i == 0 else (core != level // 2)
-
-            @pl.when(mine)
-            def _():
-                mine_ref[:, pl.ds(to, width)] = part
-
-            @pl.when(jnp.logical_not(mine))
-            def _():
-                other_ref[:, pl.ds(to, width)] = part.astype(jnp.bfloat16)
+            for t in range(LEVELS):
+                out_ref[lax.rem(t + LEVELS - level, LEVELS), :, pl.ds(to, width)] = part[
+                    t * tok : (t + 1) * tok
+                ].astype(out_ref.dtype)
 
 
 SMEM = pl.BlockSpec(memory_space=pltpu.SMEM)
@@ -443,25 +437,32 @@
     def columns(array, size, at):
         return lax.dynamic_slice_in_dim(array, at * size, size, 1)
 
-    def key_piece(to_level):
+    def key_columns(to_level):
         def pair(k, v):
             return [columns(a, HD, at) for at in (to_level, to_level ^ 2) for a in (k, v)]
 
-        weights = jnp.concatenate(pair(w_key, w_value), axis=1)
         old = jnp.concatenate(pair(cache_keys, cache_values), axis=1)
-        return jnp.concatenate([weights, old, slot_rows], axis=0)
-
-    def query_piece(to_level):
-        return jnp.concatenate(
-            [columns(w_query, 4 * HD, at) for at in (to_level, to_level ^ 2)], axis=1
-        )[None]
+        return pair(w_key, w_value), jnp.concatenate([old, slot_rows], axis=0)
+
+    def query_columns(to_level):
+        return [columns(w_query, 4 * HD, at) for at in (to_level, to_level ^ 2)]
 
     depth = w_query.shape[0]
-    key_own = key_piece(level)
-    key_next = across(key_piece(level ^ 1), 1)
-    query_own = query_piece(level)
-    query_next = across(query_piece(level ^ 1), 1)
+    query_own = jnp.concatenate(query_columns(level), axis=1)[None]
     query_near = to_near(query_own)
+    query_far = to_far(query_own)
+    own_columns, old_own = key_columns(level)
+    give_columns, old_give = key_columns(level ^ 1)
+    third = (CACHED + REC_PAD + 2) // 3 // 16 * 16 + 16
+    old_give = jnp.pad(old_give, ((0, 3 * third - CACHED - REC_PAD), (0, 0)))
+    given = jnp.concatenate(
+        [
+            jnp.concatenate(give_columns + query_columns(level ^ 1), axis=1),
+            jnp.concatenate([old_give[i * third : (i + 1) * third] for i in range(3)], axis=1),
+        ],
+        axis=0,
+    )
+    taken = across(given, 1)
 
     rows = jnp.concatenate(
         [text_rows, recompute_rows, jnp.zeros((REC_PAD - REC, width), text_rows.dtype)], axis=0
@@ -477,26 +478,36 @@
         permuted(pictures, lambda z, p, c, k=k: (2 * c + (k ^ (p % 2)), z, p // 2)) for k in (0, 1)
     ]
 
+    out_rows = w_out.shape[0] // 2
+    out_own, out_give = (
+        lax.dynamic_slice_in_dim(w_out, at * out_rows, out_rows, 0) for at in (half_at, 1 - half_at)
+    )
+    out_half = out_rows // 2
+    out_got0, out_got1 = across(out_give[:out_half], 2), across(out_give[out_half:], 2)
+
     crossed = permuted(normed, lambda z, p, c: (z ^ 2, p, 1 - c) if c == 1 - z // 2 else None)
-    crossed, key_next, query_near, *shown = lax.optimization_barrier(
-        (crossed, key_next, query_near, *shown)
-    )
-    query_far = to_far(jnp.concatenate([query_own, query_near], axis=0))
-    keys = jnp.stack([key_own[:depth], key_next[:depth]])
-    old_own, old_next = key_own[depth:], key_next[depth:]
-    keys_near = to_near(keys)
+    crossed, taken, query_near, query_far, *shown = lax.optimization_barrier(
+        (crossed, taken, query_near, query_far, *shown)
+    )
+    query_both = to_far(query_near)
+    key_cols = 4 * HD
+    keys = jnp.stack([jnp.concatenate(own_columns, axis=1), taken[:depth, :key_cols]])
+    query_next = taken[None, :depth, key_cols:]
+    old_next = jnp.concatenate(
+        [taken[depth:, i * key_cols : (i + 1) * key_cols] for i in range(3)], axis=0
+    )[: CACHED + REC_PAD]
     held = jnp.where(own_first, normed, crossed)
     next_rows = across(held, 1)
+    keys_near, next_near = to_near(keys), to_near(query_next)
     odd = level % 2 == 1
     shown_mine = jnp.concatenate(
         [jnp.where(odd, shown[1], shown[0]), jnp.where(odd, shown[0], shown[1])], axis=0
     )
     shown_other = other_core(shown_mine)
-    next_rows, keys_near, shown_other, query_next, query_far = lax.optimization_barrier(
-        (next_rows, keys_near, shown_other, query_next, query_far)
+    next_rows, keys_near, shown_other, next_near, out_got0, query_both = lax.optimization_barrier(
+        (next_rows, keys_near, shown_other, next_near, out_got0, query_both)
     )
     keys_far = to_far(jnp.concatenate([keys, keys_near], axis=0))
-    next_near = to_near(query_next)
     shown_all = jnp.concatenate(
         [
             jnp.where(core == 0, shown_mine, shown_other),
@@ -514,14 +525,10 @@
         with_pictures(held, held_at) + with_pictures(next_rows, held_at ^ 1), axis=0
     )
     rows_other = other_core(rows_mine)
-    rows_other, keys_far = lax.optimization_barrier((rows_other, keys_far))
+    rows_other, keys_far, next_near, out_got1 = lax.optimization_barrier(
+        (rows_other, keys_far, next_near, out_got1)
+    )
     next_far = to_far(jnp.concatenate([query_next, next_near], axis=0))
-
-    out_rows = w_out.shape[0] // 2
-    out_own, out_give = (
-        lax.dynamic_slice_in_dim(w_out, at * out_rows, out_rows, 0) for at in (half_at, 1 - half_at)
-    )
-    out_got = across(out_give, 2)
 
     half = HD // 2
     freqs = ROPE_BASE ** (-jnp.arange(half, dtype=jnp.float32) / half)
@@ -547,8 +554,8 @@
         compiler_params=PARAMS,
         name="keys_part",
     )(where, rows_mine, rows_other, keys, keys_near, keys_far, old_own, old_next)
-    send, rows_after, out_got = lax.optimization_barrier((send, rows_mine, out_got))
-    out_pair = jnp.stack([out_own, out_got])
+    send, rows_after = lax.optimization_barrier((send, rows_mine))
+    out_pair = jnp.stack([out_own, jnp.concatenate([out_got0, out_got1], axis=0)])
     out_pair, next_far = lax.optimization_barrier((out_pair, next_far))
     out_near = to_near(out_pair)
     q_keep, q_send = pl.pallas_call(
@@ -557,7 +564,7 @@
             shaped((LEVELS, tok, 4 * HD), jnp.float32),
             shaped((LEVELS, tok, 4 * HD)),
         ),
-        in_specs=[SMEM] + [VMEM] * 8,
+        in_specs=[SMEM] + [VMEM] * 9,
         out_specs=(VMEM, VMEM),
         compiler_params=PARAMS,
         name="queries_part",
@@ -568,6 +575,7 @@
         query_own,
         query_near,
         query_far,
+        query_both,
         query_next,
         next_near,
         next_far,
@@ -604,18 +612,19 @@
     mine, other = pl.pallas_call(
         output_kernel,
         out_shape=(
-            shaped((LEVELS * tok, wide_cols), jnp.float32),
-            shaped((LEVELS * tok, wide_cols)),
+            shaped((LEVELS, tok, wide_cols), jnp.float32),
+            shaped((LEVELS, tok, wide_cols)),
         ),
         in_specs=[SMEM] + [VMEM] * 5,
         out_specs=(VMEM, VMEM),
+        scratch_shapes=[pltpu.VMEM((LEVELS * tok, out_rows), jnp.bfloat16)],
         compiler_params=PARAMS,
         name="output",
     )(where, attended, across(attended, 1), out_pair, out_near, out_far)
-    summed = (mine + other_core(other).astype(jnp.float32)).reshape(LEVELS, tok, wide_cols)
+    got = other_core(other)
 
     def block_for(steps):
-        return lax.dynamic_index_in_dim(summed, (level + steps) % LEVELS, 0, keepdims=False)
+        return mine[steps] + got[steps].astype(jnp.float32)
 
     second, first, third = (up(block_for(d).astype(jnp.bfloat16), d) for d in (2, 1, 3))
     same = (block_for(0) + second.astype(jnp.float32)).astype(jnp.bfloat16)

time: 207 us -> 222 us (1.072)
  waiting for transfers between devices: 90.2 us -> 108 us
  Pallas kernels: 26.5 us -> 22.1 us
  starting transfers between devices: 48 us -> 44.7 us
    ppermute x27 -> x28, waiting for transfers between devices: 90.2 us -> 108 us  [permuted(): return lax.ppermute(value, ('seq', 'head'), perm)]
    pallas_call x1, Pallas kernels: 8.73 us -> 5.09 us  [by_levels(): pl.pallas_call(output_kernel, out_shape=(shaped((LEVELS, tok, wide_cols),...]
    ppermute x27 -> x28, starting transfers between devices: 48 us -> 44.7 us  [permuted(): return lax.ppermute(value, ('seq', 'head'), perm)]
    unnamed x56 -> x81, local copies, waits for them, and re-layouts: 6.18 us -> 8.49 us
  transfers between devices with their start and end apart: 27 -> 28, of which waited for: 17 -> 17; matrix products, arithmetic and copies ran while one was open for 12% -> 8% of each run, Pallas kernels for 9% -> 8%
where the time goes in v6:
time: 222 us; the launch traced here: 218 us
  waiting for transfers between devices  108 us (49%)
  starting transfers between devices  44.7 us (20%)
  Pallas kernels  22.1 us (10%)
  other arithmetic  20.3 us (9%)
  local copies, waits for them, and re-layouts  18.9 us (9%)
  blocking collectives  2.47 us (1%)
    ppermute x28, waiting for transfers between devices, permuted(): return lax.ppermute(value, ('seq', 'head'), perm)  108 us
    ppermute x28, starting transfers between devices, permuted(): return lax.ppermute(value, ('seq', 'head'), perm)  44.7 us
    pallas_call x1, Pallas kernels, by_levels(): pl.pallas_call(attend_kernel, out_shape=shaped((LEVELS * tok, 4 * HD)), i...  8.99 us
    unnamed x81, local copies, waits for them, and re-layouts  8.49 us
    pallas_call x1, Pallas kernels, by_levels(): pl.pallas_call(output_kernel, out_shape=(shaped((LEVELS, tok, wide_cols),...  5.09 us
  transfers between devices with their start and end apart: 28, of which 17 were waited for; matrix products, arithmetic and copies ran while one was open for 8% of the time, Pallas kernels for 8%

profile of v6, /device:TPU:8, one launch (start us, length us, event | category | flops | bytes accessed | tf_op | source)
XLA Modules:
  0.0 218.4 jit_solution(9247244424719754707)
XLA Ops:
  0.0 1.6 dynamic-slice_dynamic-update-slice_fusion.5
  1.6 1.5 dynamic-slice_dynamic-update-slice_fusion.4
  3.1 1.6 constant_dynamic-slice_fusion.9
  4.7 1.6 constant_dynamic-slice_fusion.8
  7.0 0.8 constant_dynamic-slice_fusion.11
  7.9 1.6 collective-permute-start.2
  9.4 1.5 collective-permute-start.3
  11.5 2.5 %all-reduce.2 = (f32[144]{0:T(256)S(1)}, f32[32]{0:T(128)S(1)}) all-reduce(f32[144]{0:T(256)S(1)} %fusion, f32[32]{0:T(128)S(1)} %fusion.4), channel_id=1, replica_groups=mesh['seq'=16,'head'=2] {'head'}, use_global_device_ids=true, to_apply=%region_1.2 | all-reduce | flops 176 | bytes 1408 | tf_op jit(solution)/shard_map/psum | solution.py:472
  14.0 1.2 fusion.2
  15.2 1.5 collective-permute-start
  17.0 2.2 %maximum_maximum_fusion = bf16[288,1536]{1,0:T(8,128)(2,1)} fusion(bf16[32,512]{1,0:T(8,128)(2,1)S(1)} %pad_slice_fusion, bf16[32,512]{1,0:T(8,128)(2,1)S(1)} %get-tuple-element.105, bf16[32,512]{1,0:T(8,128)(2,1)S(1)} %get-tuple-element.104, bf16[256,1536]{1,0:T(8,128)(2,1)} %get-tuple-element.79), kind=kLoop, calls=%fused_computation.10 | loop fusion | flops 3538944 | bytes 1769472 | tf_op jit(solution)/shard_map/concatenate | solution.py:458
  20.4 3.4 %collective-permute-start.4 = (bf16[32,2048]{1,0:T(8,128)(2,1)}, bf16[32,2048]{1,0:T(8,128)(2,1)S(1)}, u32[]{:S(2)}, u32[]{:S(2)}) collective-permute-start(bf16[32,2048]{1,0:T(8,128)(2,1)} %fusion.6), channel_id=1, source_target_pairs={{0,0},{1,16},{2,8},{3,24},{4,1},{5,17},{6,9},{7,25},{8,2},{9,18},{... | collective-permute-start | bytes 393224 | tf_op jit(solution)/shard_map/ppermute | solution.py:200
  23.9 23.6 %collective-permute-done.4 = bf16[32,2048]{1,0:T(8,128)(2,1)S(1)} collective-permute-done((bf16[32,2048]{1,0:T(8,128)(2,1)}, bf16[32,2048]{1,0:T(8,128)(2,1)S(1)}, u32[]{:S(2)}, u32[]{:S(2)}) %collective-permute-start.4) | collective-permute-done | bytes 131104 | tf_op jit(solution)/shard_map/ppermute | solution.py:200
  48.3 0.8 constant_dynamic-slice_fusion.5
  49.1 3.7 %collective-permute-done.5 = bf16[32,2048]{1,0:T(8,128)(2,1)} collective-permute-done((bf16[32,2048]{1,0:T(8,128)(2,1)}, bf16[32,2048]{1,0:T(8,128)(2,1)}, u32[]{:S(2)}, u32[]{:S(2)}) %collective-permute-start.5) | collective-permute-done | bytes 131104 | tf_op jit(solution)/shard_map/ppermute | solution.py:200
  52.8 5.5 %collective-permute-start.10 = (bf16[512,256]{1,0:T(8,128)(2,1)S(1)}, bf16[512,256]{1,0:T(8,128)(2,1)S(1)}, u32[]{:S(2)}, u32[]{:S(2)}) collective-permute-start(bf16[512,256]{1,0:T(8,128)(2,1)S(1)} %get-tuple-element.77), channel_id=1, source_target_pairs={{0,16},{1,17},{2,18},{3,19},{4,20},{5,21},{6,22},{7,23},{8,24},{9,... | collective-permute-start | bytes 786440 | tf_op jit(solution)/shard_map/ppermute | solution.py:200
  58.4 1.2 slice_bitcast_fusion.1
  59.5 1.2 slice_bitcast_fusion.refs_4_
  60.7 1.3 broadcast_select_fusion
  62.1 1.7 collective-permute-start.7
  64.2 3.1 %collective-permute-start.11 = (bf16[1,256,1024]{2,1,0:T(8,128)(2,1)S(1)}, bf16[1,256,1024]{2,1,0:T(8,128)(2,1)S(1)}, u32[]{:S(2)}, u32[]{:S(2)}) collective-permute-start(bf16[1,256,1024]{2,1,0:T(8,128)(2,1)S(1)} %collective-permute-done.2.refs_1_), channel_id=1, source_target_pairs={{0,4},{1,3},{2,6},{3,1},{4,0},{5,7},{6,2},{7,5},{8,12},{9,11},{10,... | collective-permute-start | bytes 1572872 | tf_op jit(solution)/shard_map/ppermute | solution.py:200
  67.3 0.9 broadcast_select_fusion.6
  72.0 0.8 slice.99
  72.9 2.2 %collective-permute-done.7.near = bf16[2,256,512]{2,1,0:T(8,128)(2,1)S(1)} collective-permute-done((bf16[2,256,512]{2,1,0:T(8,128)(2,1)S(1)}, bf16[2,256,512]{2,1,0:T(8,128)(2,1)S(1)}, u32[]{:S(2)}, u32[]{:S(2)}) %collective-permute-start.7) | collective-permute-done | bytes 524320 | tf_op jit(solution)/shard_map/ppermute | solution.py:200
  75.1 7.5 %collective-permute-done.9.refs_5_ = bf16[1,256,1024]{2,1,0:T(8,128)(2,1)S(1)} collective-permute-done((bf16[1,256,1024]{2,1,0:T(8,128)(2,1)S(1)}, bf16[1,256,1024]{2,1,0:T(8,128)(2,1)S(1)}, u32[]{:S(2)}, u32[]{:S(2)}) %collective-permute-start.9) | collective-permute-done | bytes 524320 | tf_op jit(solution)/shard_map/ppermute | solution.py:200
  82.6 0.9 slice.82
  83.5 1.0 broadcast_select_fusion.2
  84.6 1.5 slice_select_fusion
  87.7 1.1 pad_maximum_fusion.2
  88.8 3.0 %collective-permute-start.13 = (bf16[4,256,512]{2,1,0:T(8,128)(2,1)}, bf16[4,256,512]{2,1,0:T(8,128)(2,1)}, u32[]{:S(2)}, u32[]{:S(2)}) collective-permute-start(bf16[4,256,512]{2,1,0:T(8,128)(2,1)} %pad_maximum_fusion.2), channel_id=1, source_target_pairs={{0,4},{1,3},{2,6},{3,1},{4,0},{5,7},{6,2},{7,5},{8,12},{9,11},{10,... | collective-permute-start | bytes 3145736 | tf_op jit(solution)/shard_map/ppermute | solution.py:200
  92.2 10.9 %collective-permute-done.14 = bf16[512,256]{1,0:T(8,128)(2,1)} collective-permute-done((bf16[512,256]{1,0:T(8,128)(2,1)}, bf16[512,256]{1,0:T(8,128)(2,1)}, u32[]{:S(2)}, u32[]{:S(2)}) %collective-permute-start.14) | collective-permute-done | bytes 262176 | tf_op jit(solution)/shard_map/ppermute | solution.py:200
  103.1 1.8 collective-permute-done.13.far
  104.9 1.5 pad_maximum_fusion.4
  106.4 2.1 collective-permute-start.15
  108.6 0.8 fusion.13
  109.5 2.7 %keys_part.1 = (f32[576,256]{1,0:T(8,128)S(1)}, bf16[736,256]{1,0:T(8,128)(2,1)S(1)}) custom-call(s32[4]{0:T(128)S(1)} %pad_add_fusion.where_ref, bf16[288,2048]{1,0:T(8,128)(2,1)S(1)} %pad_maximum_fusion.1.x0, bf16[288,2048]{1,0:T(8,128)(2,1)S(1)} %collective-permute-done.12.x1, bf16[2,256,512]{2,1,0:T(8,128)(2,1)S(1)} %pad_maximum_fusion.5.own, ...), custom_call_target="tpu_custom_call" | custom-call | tf_op jit(solution)/shard_map/keys_part/pallas_call | solution.py:546
  112.2 0.8 collective-permute-start.16
  113.0 1.0 maximum_bitcast_fusion.1
  114.1 7.2 %collective-permute-done.15.refs_6_ = bf16[2,256,1024]{2,1,0:T(8,128)(2,1)S(1)} collective-permute-done((bf16[2,256,1024]{2,1,0:T(8,128)(2,1)S(1)}, bf16[2,256,1024]{2,1,0:T(8,128)(2,1)S(1)}, u32[]{:S(2)}, u32[]{:S(2)}) %collective-permute-start.15) | collective-permute-done | bytes 1048608 | tf_op jit(solution)/shard_map/ppermute | solution.py:200
  121.3 0.9 collective-permute-start.20
  122.2 1.4 fusion.10
  125.0 4.3 %queries_part.1 = (f32[4,128,512]{2,1,0:T(8,128)S(1)}, bf16[4,128,512]{2,1,0:T(8,128)(2,1)S(1)}) custom-call(s32[4]{0:T(128)S(1)} %pad_add_fusion.where_ref, bf16[288,2048]{1,0:T(8,128)(2,1)} %copy-done, bf16[288,2048]{1,0:T(8,128)(2,1)} %copy-done.1, bf16[1,256,1024]{2,1,0:T(8,128)(2,1)S(1)} %copy-done.6, bf16[1,256,1024]{2,1,0:T(8,128)(2,1)S(1)} %copy-done.10, ...), custom_call_target="tpu_custom_call" | custom-call | tf_op jit(solution)/shard_map/queries_part/pallas_call | solution.py:561
  129.3 1.0 keys_join.1.kv0
  130.3 1.2 collective-permute-start.18
  131.5 2.3 %collective-permute-start.21 = (bf16[4,128,512]{2,1,0:T(8,128)(2,1)S(1)}, bf16[4,128,512]{2,1,0:T(8,128)(2,1)S(1)}, u32[]{:S(2)}, u32[]{:S(2)}) collective-permute-start(bf16[4,128,512]{2,1,0:T(8,128)(2,1)S(1)} %get-tuple-element.62), channel_id=1, source_target_pairs={{0,16},{1,17},{2,18},{3,19},{4,20},{5,21},{6,22},{7,23},{8,24},{9,... | collective-permute-start | bytes 1572872 | tf_op jit(solution)/shard_map/ppermute | solution.py:200
  133.8 0.8 collective-permute-start.17
  134.6 11.4 %collective-permute-done.18.kv1 = bf16[6,128,256]{2,1,0:T(8,128)(2,1)S(1)} collective-permute-done((bf16[6,128,256]{2,1,0:T(8,128)(2,1)S(1)}, bf16[6,128,256]{2,1,0:T(8,128)(2,1)S(1)}, u32[]{:S(2)}, u32[]{:S(2)}) %collective-permute-start.18) | collective-permute-done | bytes 393248 | tf_op jit(solution)/shard_map/ppermute | solution.py:200
  146.1 2.4 %collective-permute-start.19 = (bf16[6,128,256]{2,1,0:T(8,128)(2,1)S(1)}, bf16[6,128,256]{2,1,0:T(8,128)(2,1)S(1)}, u32[]{:S(2)}, u32[]{:S(2)}) collective-permute-start(bf16[6,128,256]{2,1,0:T(8,128)(2,1)S(1)} %collective-permute-done.18.kv1), channel_id=1, source_target_pairs={{0,4},{1,3},{2,6},{3,1},{4,0},{5,7},{6,2},{7,5},{8,12},{9,11},{10,... | collective-permute-start | bytes 1179656 | tf_op jit(solution)/shard_map/ppermute | solution.py:200
  148.4 5.4 %collective-permute-done.21.got_ref = bf16[4,128,512]{2,1,0:T(8,128)(2,1)S(1)} collective-permute-done((bf16[4,128,512]{2,1,0:T(8,128)(2,1)S(1)}, bf16[4,128,512]{2,1,0:T(8,128)(2,1)S(1)}, u32[]{:S(2)}, u32[]{:S(2)}) %collective-permute-start.21) | collective-permute-done | bytes 524320 | tf_op jit(solution)/shard_map/ppermute | solution.py:200
  154.4 2.1 collective-permute-start.23
  156.5 9.0 %attend.1.own_ref = bf16[512,512]{1,0:T(8,128)(2,1)S(1)} custom-call(s32[4]{0:T(128)S(1)} %pad_add_fusion.where_ref, f32[4,128,512]{2,1,0:T(8,128)S(1)} %get-tuple-element.56.keep_ref, bf16[4,128,512]{2,1,0:T(8,128)(2,1)S(1)} %collective-permute-done.21.got_ref, f32[4,192,128]{2,1,0:T(8,128)S(1)} %pad_maximum_fusion.8.cos_ref, ...), custom_call_target="tpu_custom_call" | custom-call | tf_op jit(solution)/shard_map/attend/pallas_call | solution.py:601
  165.5 2.3 %collective-permute-start.22 = (bf16[512,512]{1,0:T(8,128)(2,1)S(1)}, bf16[512,512]{1,0:T(8,128)(2,1)S(1)}, u32[]{:S(2)}, u32[]{:S(2)}) collective-permute-start(bf16[512,512]{1,0:T(8,128)(2,1)S(1)} %attend.1.own_ref), channel_id=1, source_target_pairs={{0,8},{1,9},{2,10},{3,11},{4,12},{5,13},{6,14},{7,15},{8,0},{9,1},... | collective-permute-start | bytes 1572872 | tf_op jit(solution)/shard_map/ppermute | solution.py:200
  167.8 12.1 %collective-permute-done.22.next_ref = bf16[512,512]{1,0:T(8,128)(2,1)S(1)} collective-permute-done((bf16[512,512]{1,0:T(8,128)(2,1)S(1)}, bf16[512,512]{1,0:T(8,128)(2,1)S(1)}, u32[]{:S(2)}, u32[]{:S(2)}) %collective-permute-start.22) | collective-permute-done | bytes 524320 | tf_op jit(solution)/shard_map/ppermute | solution.py:200
  180.5 1.3 copy-done.20
  181.8 5.1 %output.1 = (f32[4,128,1024]{2,1,0:T(8,128)}, bf16[4,128,1024]{2,1,0:T(8,128)(2,1)S(1)}) custom-call(s32[4]{0:T(128)S(1)} %pad_add_fusion.where_ref, bf16[512,512]{1,0:T(8,128)(2,1)S(1)} %attend.1.own_ref, bf16[512,512]{1,0:T(8,128)(2,1)S(1)} %collective-permute-done.22.next_ref, bf16[2,1024,256]{2,1,0:T(8,128)(2,1)S(1)} %pad_maximum_fusion.3.w_own, ...), custom_call_target="tpu_custom_call" | custom-call | tf_op jit(solution)/shard_map/output/pallas_call | solution.py:612
  186.9 2.7 %collective-permute-done.24 = bf16[4,128,1024]{2,1,0:T(8,128)(2,1)S(1)} collective-permute-done((bf16[4,128,1024]{2,1,0:T(8,128)(2,1)S(1)}, bf16[4,128,1024]{2,1,0:T(8,128)(2,1)S(1)}, u32[]{:S(2)}, u32[]{:S(2)}) %collective-permute-start.24) | collective-permute-done | bytes 1048608 | tf_op jit(solution)/shard_map/ppermute | solution.py:200
  189.6 1.6 fusion.7
  191.2 2.3 %collective-permute-start.27 = (bf16[128,1024]{1,0:T(8,128)(2,1)S(1)}, bf16[128,1024]{1,0:T(8,128)(2,1)S(1)}, u32[]{:S(2)}, u32[]{:S(2)}) collective-permute-start(bf16[128,1024]{1,0:T(8,128)(2,1)S(1)} %get-tuple-element.74), channel_id=1, source_target_pairs={{0,24},{1,25},{2,26},{3,27},{4,28},{5,29},{6,30},{7,31},{8,0},{9,1... | collective-permute-start | bytes 786440 | tf_op jit(solution)/shard_map/ppermute | solution.py:200
  193.5 4.6 %collective-permute-start.25 = (bf16[128,1024]{1,0:T(8,128)(2,1)S(1)}, bf16[128,1024]{1,0:T(8,128)(2,1)S(1)}, u32[]{:S(2)}, u32[]{:S(2)}) collective-permute-start(bf16[128,1024]{1,0:T(8,128)(2,1)S(1)} %get-tuple-element.73), channel_id=1, source_target_pairs={{0,16},{1,17},{2,18},{3,19},{4,20},{5,21},{6,22},{7,23},{8,24},{9,... | collective-permute-start | bytes 786440 | tf_op jit(solution)/shard_map/ppermute | solution.py:200
  198.1 8.3 %collective-permute-done.27 = bf16[128,1024]{1,0:T(8,128)(2,1)S(1)} collective-permute-done((bf16[128,1024]{1,0:T(8,128)(2,1)S(1)}, bf16[128,1024]{1,0:T(8,128)(2,1)S(1)}, u32[]{:S(2)}, u32[]{:S(2)}) %collective-permute-start.27) | collective-permute-done | bytes 262176 | tf_op jit(solution)/shard_map/ppermute | solution.py:200
  206.4 2.2 collective-permute-done.26
  208.5 7.7 %collective-permute-done.25 = bf16[128,1024]{1,0:T(8,128)(2,1)S(1)} collective-permute-done((bf16[128,1024]{1,0:T(8,128)(2,1)S(1)}, bf16[128,1024]{1,0:T(8,128)(2,1)S(1)}, u32[]{:S(2)}, u32[]{:S(2)}) %collective-permute-start.25) | collective-permute-done | bytes 262176 | tf_op jit(solution)/shard_map/ppermute | solution.py:200
  216.2 1.2 broadcast_select_fusion.4
  217.6 0.8 pad_maximum_fusion.7
  (135 shorter events, 11.5 us)
Async XLA Ops:
  0.0 6.3 %copy-start.21 = (bf16[256,2048]{1,0:T(8,128)(2,1)S(1)}, bf16[256,2048]{1,0:T(8,128)(2,1)}, u32[]{:S(2)}) copy-start(bf16[256,2048]{1,0:T(8,128)(2,1)} %param.16) | copy-start | bytes 3145732
  7.0 4.0 %copy-start.24 = (bf16[32,2048]{1,0:T(8,128)(2,1)S(1)}, bf16[32,2048]{1,0:T(8,128)(2,1)}, u32[]{:S(2)}) copy-start(bf16[32,2048]{1,0:T(8,128)(2,1)} %param.14) | copy-start | bytes 393220
  7.0 4.2 %copy-start.15 = (bf16[128,2048]{1,0:T(8,128)(2,1)S(1)}, bf16[128,2048]{1,0:T(8,128)(2,1)}, u32[]{:S(2)}) copy-start(bf16[128,2048]{1,0:T(8,128)(2,1)} %param.13) | copy-start | bytes 1572868
  7.0 4.2 %copy-start.25 = (bf16[8,2048]{1,0:T(8,128)(2,1)S(1)}, bf16[8,2048]{1,0:T(8,128)(2,1)}, u32[]{:S(2)}) copy-start(bf16[8,2048]{1,0:T(8,128)(2,1)} %param.22) | copy-start | bytes 98308
  7.8 6.2 %copy-start.36 = (f32[4096]{0:T(1024)S(1)}, f32[4096]{0:T(1024)}, u32[]{:S(2)}) copy-start(f32[4096]{0:T(1024)} %param.15) | copy-start | bytes 49156
  7.8 9.1 %copy-start.5 = (bf16[1,256,1024]{2,1,0:T(8,128)(2,1)}, bf16[1,256,1024]{2,1,0:T(8,128)(2,1)S(1)}, u32[]{:S(2)}) copy-start(bf16[1,256,1024]{2,1,0:T(8,128)(2,1)S(1)} %maximum_bitcast_fusion.refs_0_) | copy-start | bytes 1572868
  7.8 8.8 %copy-start.37 = (s32[8]{0:T(128)S(1)}, s32[8]{0:T(128)}, u32[]{:S(2)}) copy-start(s32[8]{0:T(128)} %param.23) | copy-start | bytes 100
  7.8 8.9 %copy-start.34 = (bf16[64,512]{1,0:T(8,128)(2,1)S(1)}, bf16[64,512]{1,0:T(8,128)(2,1)}, u32[]{:S(2)}) copy-start(bf16[64,512]{1,0:T(8,128)(2,1)} %param.21) | copy-start | bytes 196612
  7.9 8.9 %copy-start.35 = (bf16[64,512]{1,0:T(8,128)(2,1)S(1)}, bf16[64,512]{1,0:T(8,128)(2,1)}, u32[]{:S(2)}) copy-start(bf16[64,512]{1,0:T(8,128)(2,1)} %param.20) | copy-start | bytes 196612
  7.9 50.5 %collective-permute-start.2 = (bf16[1,256,1024]{2,1,0:T(8,128)(2,1)S(1)}, bf16[1,256,1024]{2,1,0:T(8,128)(2,1)S(1)}, u32[]{:S(2)}, u32[]{:S(2)}) collective-permute-start(bf16[1,256,1024]{2,1,0:T(8,128)(2,1)S(1)} %maximum_bitcast_fusion.refs_0_), channel_id=1, source_target_pairs={{0,2},{1,5},{2,0},{3,7},{4,6},{5,1},{6,4},{7,3},{8,10},{9,13},{10,... | collective-permute-start | bytes 1572872 | tf_op jit(solution)/shard_map/ppermute | solution.py:200
  9.4 48.9 %collective-permute-start.3 = (bf16[1,256,1024]{2,1,0:T(8,128)(2,1)S(1)}, bf16[1,256,1024]{2,1,0:T(8,128)(2,1)S(1)}, u32[]{:S(2)}, u32[]{:S(2)}) collective-permute-start(bf16[1,256,1024]{2,1,0:T(8,128)(2,1)S(1)} %maximum_bitcast_fusion.refs_0_), channel_id=1, source_target_pairs={{0,4},{1,3},{2,6},{3,1},{4,0},{5,7},{6,2},{7,5},{8,12},{9,11},{10,... | collective-permute-start | bytes 1572872 | tf_op jit(solution)/shard_map/ppermute | solution.py:200
  15.2 43.2 %collective-permute-start = (bf16[144,2048]{1,0:T(8,128)(2,1)}, bf16[144,2048]{1,0:T(8,128)(2,1)}, u32[]{:S(2)}, u32[]{:S(2)}) collective-permute-start(bf16[144,2048]{1,0:T(8,128)(2,1)} %fusion.2), channel_id=1, source_target_pairs={{1,16},{3,18},{5,20},{7,22},{9,24},{11,26},{13,28},{15,30},{16,1},... | collective-permute-start | bytes 1769480 | tf_op jit(solution)/shard_map/ppermute | solution.py:200
  16.9 31.3 %copy-start.28 = (bf16[256,128]{1,0:T(8,128)(2,1)S(1)}, bf16[256,128]{1,0:T(8,128)(2,1)}, u32[]{:S(2)}) copy-start(bf16[256,128]{1,0:T(8,128)(2,1)} %get-tuple-element.90) | copy-start | bytes 196612
  16.9 31.3 %copy-start.29 = (bf16[256,128]{1,0:T(8,128)(2,1)S(1)}, bf16[256,128]{1,0:T(8,128)(2,1)}, u32[]{:S(2)}) copy-start(bf16[256,128]{1,0:T(8,128)(2,1)} %get-tuple-element.92) | copy-start | bytes 196612
  16.9 31.3 %copy-start.30 = (bf16[256,128]{1,0:T(8,128)(2,1)S(1)}, bf16[256,128]{1,0:T(8,128)(2,1)}, u32[]{:S(2)}) copy-start(bf16[256,128]{1,0:T(8,128)(2,1)} %get-tuple-element.93) | copy-start | bytes 196612
  16.9 31.3 %copy-start.31 = (bf16[256,128]{1,0:T(8,128)(2,1)S(1)}, bf16[256,128]{1,0:T(8,128)(2,1)}, u32[]{:S(2)}) copy-start(bf16[256,128]{1,0:T(8,128)(2,1)} %get-tuple-element.95) | copy-start | bytes 196612
  17.0 31.3 %copy-start.22 = (bf16[2048,256]{1,0:T(8,128)(2,1)S(1)}, bf16[2048,256]{1,0:T(8,128)(2,1)}, u32[]{:S(2)}) copy-start(bf16[2048,256]{1,0:T(8,128)(2,1)} %param.19) | copy-start | bytes 3145732
  19.2 39.1 %collective-permute-start.1 = (bf16[288,1536]{1,0:T(8,128)(2,1)}, bf16[288,1536]{1,0:T(8,128)(2,1)}, u32[]{:S(2)}, u32[]{:S(2)}) collective-permute-start(bf16[288,1536]{1,0:T(8,128)(2,1)} %maximum_maximum_fusion), channel_id=1, source_target_pairs={{0,8},{1,9},{2,10},{3,11},{4,12},{5,13},{6,14},{7,15},{8,0},{9,1},... | collective-permute-start | bytes 2654216 | tf_op jit(solution)/shard_map/ppermute | solution.py:200
  20.4 27.1 %collective-permute-start.4 = (bf16[32,2048]{1,0:T(8,128)(2,1)}, bf16[32,2048]{1,0:T(8,128)(2,1)S(1)}, u32[]{:S(2)}, u32[]{:S(2)}) collective-permute-start(bf16[32,2048]{1,0:T(8,128)(2,1)} %fusion.6), channel_id=1, source_target_pairs={{0,0},{1,16},{2,8},{3,24},{4,1},{5,17},{6,9},{7,25},{8,2},{9,18},{... | collective-permute-start | bytes 393224 | tf_op jit(solution)/shard_map/ppermute | solution.py:200
  47.5 5.3 %collective-permute-start.5 = (bf16[32,2048]{1,0:T(8,128)(2,1)}, bf16[32,2048]{1,0:T(8,128)(2,1)}, u32[]{:S(2)}, u32[]{:S(2)}) collective-permute-start(bf16[32,2048]{1,0:T(8,128)(2,1)} %fusion.6), channel_id=1, source_target_pairs={{0,8},{1,24},{2,0},{3,16},{4,9},{5,25},{6,1},{7,17},{8,10},{9,26},... | collective-permute-start | bytes 393224 | tf_op jit(solution)/shard_map/ppermute | solution.py:200
  48.2 13.8 %copy-start.16 = (bf16[1,256,512]{2,1,0:T(8,128)(2,1)}, bf16[1,256,512]{2,1,0:T(8,128)(2,1)S(1)}, u32[]{:S(2)}) copy-start(bf16[1,256,512]{2,1,0:T(8,128)(2,1)S(1)} %maximum_bitcast_fusion.2) | copy-start | bytes 786436
  52.8 16.6 %collective-permute-start.10 = (bf16[512,256]{1,0:T(8,128)(2,1)S(1)}, bf16[512,256]{1,0:T(8,128)(2,1)S(1)}, u32[]{:S(2)}, u32[]{:S(2)}) collective-permute-start(bf16[512,256]{1,0:T(8,128)(2,1)S(1)} %get-tuple-element.77), channel_id=1, source_target_pairs={{0,16},{1,17},{2,18},{3,19},{4,20},{5,21},{6,22},{7,23},{8,24},{9,... | collective-permute-start | bytes 786440 | tf_op jit(solution)/shard_map/ppermute | solution.py:200
  58.3 5.9 %copy-start.9 = (bf16[1,256,1024]{2,1,0:T(8,128)(2,1)}, bf16[1,256,1024]{2,1,0:T(8,128)(2,1)S(1)}, u32[]{:S(2)}) copy-start(bf16[1,256,1024]{2,1,0:T(8,128)(2,1)S(1)} %collective-permute-done.2.refs_1_) | copy-start | bytes 1572868
  58.3 3.7 %copy-start.11 = (bf16[1,256,1024]{2,1,0:T(8,128)(2,1)}, bf16[1,256,1024]{2,1,0:T(8,128)(2,1)S(1)}, u32[]{:S(2)}) copy-start(bf16[1,256,1024]{2,1,0:T(8,128)(2,1)S(1)} %collective-permute-done.3.refs_2_) | copy-start | bytes 1572868
  59.5 2.5 %copy-start.18 = (bf16[1,256,512]{2,1,0:T(8,128)(2,1)}, bf16[1,256,512]{2,1,0:T(8,128)(2,1)S(1)}, u32[]{:S(2)}) copy-start(bf16[1,256,512]{2,1,0:T(8,128)(2,1)S(1)} %slice_bitcast_fusion.1) | copy-start | bytes 786436
  60.7 6.6 %copy-start.33 = (bf16[32,2048]{1,0:T(8,128)(2,1)S(1)}, bf16[32,2048]{1,0:T(8,128)(2,1)}, u32[]{:S(2)}) copy-start(bf16[32,2048]{1,0:T(8,128)(2,1)} %copy-done.32) | copy-start | bytes 393220
  62.0 8.2 %copy-start.38 = (s32[4]{0:T(128)S(1)}, s32[4]{0:T(128)}, u32[]{:S(2)}) copy-start(s32[4]{0:T(128)} %constant.90.clone) | copy-start | bytes 52
  62.0 20.6 %collective-permute-start.6 = (bf16[144,2048]{1,0:T(8,128)(2,1)}, bf16[144,2048]{1,0:T(8,128)(2,1)}, u32[]{:S(2)}, u32[]{:S(2)}) collective-permute-start(bf16[144,2048]{1,0:T(8,128)(2,1)} %broadcast_select_fusion), channel_id=1, source_target_pairs={{0,8},{1,9},{2,10},{3,11},{4,12},{5,13},{6,14},{7,15},{8,0},{9,1},... | collective-permute-start | bytes 1769480 | tf_op jit(solution)/shard_map/ppermute | solution.py:200
  62.1 13.0 %collective-permute-start.7 = (bf16[2,256,512]{2,1,0:T(8,128)(2,1)S(1)}, bf16[2,256,512]{2,1,0:T(8,128)(2,1)S(1)}, u32[]{:S(2)}, u32[]{:S(2)}) collective-permute-start(bf16[2,256,512]{2,1,0:T(8,128)(2,1)S(1)} %pad_maximum_fusion.5.own), channel_id=1, source_target_pairs={{0,2},{1,5},{2,0},{3,7},{4,6},{5,1},{6,4},{7,3},{8,10},{9,13},{10,... | collective-permute-start | bytes 1572872 | tf_op jit(solution)/shard_map/ppermute | solution.py:200
  63.8 18.8 %collective-permute-start.9 = (bf16[1,256,1024]{2,1,0:T(8,128)(2,1)S(1)}, bf16[1,256,1024]{2,1,0:T(8,128)(2,1)S(1)}, u32[]{:S(2)}, u32[]{:S(2)}) collective-permute-start(bf16[1,256,1024]{2,1,0:T(8,128)(2,1)S(1)} %slice_bitcast_fusion.refs_4_), channel_id=1, source_target_pairs={{0,2},{1,5},{2,0},{3,7},{4,6},{5,1},{6,4},{7,3},{8,10},{9,13},{10,... | collective-permute-start | bytes 1572872 | tf_op jit(solution)/shard_map/ppermute | solution.py:200
  64.2 18.4 %collective-permute-start.11 = (bf16[1,256,1024]{2,1,0:T(8,128)(2,1)S(1)}, bf16[1,256,1024]{2,1,0:T(8,128)(2,1)S(1)}, u32[]{:S(2)}, u32[]{:S(2)}) collective-permute-start(bf16[1,256,1024]{2,1,0:T(8,128)(2,1)S(1)} %collective-permute-done.2.refs_1_), channel_id=1, source_target_pairs={{0,4},{1,3},{2,6},{3,1},{4,0},{5,7},{6,2},{7,5},{8,12},{9,11},{10,... | collective-permute-start | bytes 1572872 | tf_op jit(solution)/shard_map/ppermute | solution.py:200
  70.2 2.7 %collective-permute-start.8 = (bf16[64,2048]{1,0:T(8,128)(2,1)}, bf16[64,2048]{1,0:T(8,128)(2,1)}, u32[]{:S(2)}, u32[]{:S(2)}) collective-permute-start(bf16[64,2048]{1,0:T(8,128)(2,1)} %pad_maximum_fusion.10), channel_id=1, source_target_pairs={{0,1},{1,0},{2,3},{3,2},{4,5},{5,4},{6,7},{7,6},{8,9},{9,8},{10,11... | collective-permute-start | bytes 786440 | tf_op jit(solution)/shard_map/ppermute | solution.py:200
  75.1 11.0 %copy-start.2 = (bf16[2,256,512]{2,1,0:T(8,128)(2,1)}, bf16[2,256,512]{2,1,0:T(8,128)(2,1)S(1)}, u32[]{:S(2)}) copy-start(bf16[2,256,512]{2,1,0:T(8,128)(2,1)S(1)} %collective-permute-done.7.near) | copy-start | bytes 1572868
  82.6 3.5 %copy-start.7 = (bf16[1,256,1024]{2,1,0:T(8,128)(2,1)}, bf16[1,256,1024]{2,1,0:T(8,128)(2,1)S(1)}, u32[]{:S(2)}) copy-start(bf16[1,256,1024]{2,1,0:T(8,128)(2,1)S(1)} %collective-permute-done.9.refs_5_) | copy-start | bytes 1572868
  82.6 3.5 %copy-start.13 = (bf16[1,256,1024]{2,1,0:T(8,128)(2,1)}, bf16[1,256,1024]{2,1,0:T(8,128)(2,1)S(1)}, u32[]{:S(2)}) copy-start(bf16[1,256,1024]{2,1,0:T(8,128)(2,1)S(1)} %collective-permute-done.11.refs_3_) | copy-start | bytes 1572868
  86.1 1.1 copy-start.3
  86.1 1.4 copy-start.17
  86.2 1.6 copy-start.19
  86.2 23.2 %copy-start = (bf16[288,2048]{1,0:T(8,128)(2,1)}, bf16[288,2048]{1,0:T(8,128)(2,1)S(1)}, u32[]{:S(2)}) copy-start(bf16[288,2048]{1,0:T(8,128)(2,1)S(1)} %pad_maximum_fusion.1.x0) | copy-start | bytes 3538948
  86.3 18.6 %collective-permute-start.12 = (bf16[288,2048]{1,0:T(8,128)(2,1)S(1)}, bf16[288,2048]{1,0:T(8,128)(2,1)S(1)}, u32[]{:S(2)}, u32[]{:S(2)}) collective-permute-start(bf16[288,2048]{1,0:T(8,128)(2,1)S(1)} %pad_maximum_fusion.1.x0), channel_id=1, source_target_pairs={{0,1},{1,0},{2,3},{3,2},{4,5},{5,4},{6,7},{7,6},{8,9},{9,8},{10,11... | collective-permute-start | bytes 3538952 | tf_op jit(solution)/shard_map/ppermute | solution.py:200
  88.8 16.1 %collective-permute-start.13 = (bf16[4,256,512]{2,1,0:T(8,128)(2,1)}, bf16[4,256,512]{2,1,0:T(8,128)(2,1)}, u32[]{:S(2)}, u32[]{:S(2)}) collective-permute-start(bf16[4,256,512]{2,1,0:T(8,128)(2,1)} %pad_maximum_fusion.2), channel_id=1, source_target_pairs={{0,4},{1,3},{2,6},{3,1},{4,0},{5,7},{6,2},{7,5},{8,12},{9,11},{10,... | collective-permute-start | bytes 3145736 | tf_op jit(solution)/shard_map/ppermute | solution.py:200
  91.8 11.3 %collective-permute-start.14 = (bf16[512,256]{1,0:T(8,128)(2,1)}, bf16[512,256]{1,0:T(8,128)(2,1)}, u32[]{:S(2)}, u32[]{:S(2)}) collective-permute-start(bf16[512,256]{1,0:T(8,128)(2,1)} %get-tuple-element.76), channel_id=1, source_target_pairs={{0,16},{1,17},{2,18},{3,19},{4,20},{5,21},{6,22},{7,23},{8,24},{9,... | collective-permute-start | bytes 786440 | tf_op jit(solution)/shard_map/ppermute | solution.py:200
  92.2 16.4 %copy-start.23 = (bf16[2048,256]{1,0:T(8,128)(2,1)S(1)}, bf16[2048,256]{1,0:T(8,128)(2,1)}, u32[]{:S(2)}) copy-start(bf16[2048,256]{1,0:T(8,128)(2,1)} %param.19) | copy-start | bytes 3145732
  104.9 4.6 %copy-start.1 = (bf16[288,2048]{1,0:T(8,128)(2,1)}, bf16[288,2048]{1,0:T(8,128)(2,1)S(1)}, u32[]{:S(2)}) copy-start(bf16[288,2048]{1,0:T(8,128)(2,1)S(1)} %collective-permute-done.12.x1) | copy-start | bytes 3538948
  106.4 3.1 %copy-start.4 = (bf16[2,256,512]{2,1,0:T(8,128)(2,1)S(1)}, bf16[2,256,512]{2,1,0:T(8,128)(2,1)}, u32[]{:S(2)}) copy-start(bf16[2,256,512]{2,1,0:T(8,128)(2,1)} %copy-done.2) | copy-start | bytes 1572868
  106.4 14.9 %collective-permute-start.15 = (bf16[2,256,1024]{2,1,0:T(8,128)(2,1)S(1)}, bf16[2,256,1024]{2,1,0:T(8,128)(2,1)S(1)}, u32[]{:S(2)}, u32[]{:S(2)}) collective-permute-start(bf16[2,256,1024]{2,1,0:T(8,128)(2,1)S(1)} %pad_maximum_fusion.4), channel_id=1, source_target_pairs={{0,4},{1,3},{2,6},{3,1},{4,0},{5,7},{6,2},{7,5},{8,12},{9,11},{10,... | collective-permute-start | bytes 3145736 | tf_op jit(solution)/shard_map/ppermute | solution.py:200
  109.5 3.5 %copy-start.27 = (bf16[512,256]{1,0:T(8,128)(2,1)S(1)}, bf16[512,256]{1,0:T(8,128)(2,1)}, u32[]{:S(2)}) copy-start(bf16[512,256]{1,0:T(8,128)(2,1)} %copy-done.26) | copy-start | bytes 786436
  112.2 17.1 %collective-permute-start.16 = (bf16[736,256]{1,0:T(8,128)(2,1)S(1)}, bf16[736,256]{1,0:T(8,128)(2,1)S(1)}, u32[]{:S(2)}, u32[]{:S(2)}) collective-permute-start(bf16[736,256]{1,0:T(8,128)(2,1)S(1)} %get-tuple-element.58), channel_id=1, source_target_pairs={{0,16},{1,17},{2,18},{3,19},{4,20},{5,21},{6,22},{7,23},{8,24},{9,... | collective-permute-start | bytes 1130504 | tf_op jit(solution)/shard_map/ppermute | solution.py:200
  121.3 32.9 %collective-permute-start.20 = (bf16[2,1024,256]{2,1,0:T(8,128)(2,1)S(1)}, bf16[2,1024,256]{2,1,0:T(8,128)(2,1)S(1)}, u32[]{:S(2)}, u32[]{:S(2)}) collective-permute-start(bf16[2,1024,256]{2,1,0:T(8,128)(2,1)S(1)} %pad_maximum_fusion.3.w_own), channel_id=1, source_target_pairs={{0,2},{1,5},{2,0},{3,7},{4,6},{5,1},{6,4},{7,3},{8,10},{9,13},{10,... | collective-permute-start | bytes 3145736 | tf_op jit(solution)/shard_map/ppermute | solution.py:200
  122.2 1.8 copy-start.12
  122.2 1.8 copy-start.14
  123.6 1.2 copy-start.8
  123.6 1.3 copy-start.10
  130.3 15.8 %collective-permute-start.18 = (bf16[6,128,256]{2,1,0:T(8,128)(2,1)S(1)}, bf16[6,128,256]{2,1,0:T(8,128)(2,1)S(1)}, u32[]{:S(2)}, u32[]{:S(2)}) collective-permute-start(bf16[6,128,256]{2,1,0:T(8,128)(2,1)S(1)} %keys_join.1.kv0), channel_id=1, source_target_pairs={{0,2},{1,5},{2,0},{3,7},{4,6},{5,1},{6,4},{7,3},{8,10},{9,13},{10,... | collective-permute-start | bytes 1179656 | tf_op jit(solution)/shard_map/ppermute | solution.py:200
  131.5 22.3 %collective-permute-start.21 = (bf16[4,128,512]{2,1,0:T(8,128)(2,1)S(1)}, bf16[4,128,512]{2,1,0:T(8,128)(2,1)S(1)}, u32[]{:S(2)}, u32[]{:S(2)}) collective-permute-start(bf16[4,128,512]{2,1,0:T(8,128)(2,1)S(1)} %get-tuple-element.62), channel_id=1, source_target_pairs={{0,16},{1,17},{2,18},{3,19},{4,20},{5,21},{6,22},{7,23},{8,24},{9,... | collective-permute-start | bytes 1572872 | tf_op jit(solution)/shard_map/ppermute | solution.py:200
  133.8 14.7 %collective-permute-start.17 = (bf16[6,128,256]{2,1,0:T(8,128)(2,1)S(1)}, bf16[6,128,256]{2,1,0:T(8,128)(2,1)S(1)}, u32[]{:S(2)}, u32[]{:S(2)}) collective-permute-start(bf16[6,128,256]{2,1,0:T(8,128)(2,1)S(1)} %keys_join.1.kv0), channel_id=1, source_target_pairs={{0,4},{1,3},{2,6},{3,1},{4,0},{5,7},{6,2},{7,5},{8,12},{9,11},{10,... | collective-permute-start | bytes 1179656 | tf_op jit(solution)/shard_map/ppermute | solution.py:200
  146.1 8.1 %collective-permute-start.19 = (bf16[6,128,256]{2,1,0:T(8,128)(2,1)S(1)}, bf16[6,128,256]{2,1,0:T(8,128)(2,1)S(1)}, u32[]{:S(2)}, u32[]{:S(2)}) collective-permute-start(bf16[6,128,256]{2,1,0:T(8,128)(2,1)S(1)} %collective-permute-done.18.kv1), channel_id=1, source_target_pairs={{0,4},{1,3},{2,6},{3,1},{4,0},{5,7},{6,2},{7,5},{8,12},{9,11},{10,... | collective-permute-start | bytes 1179656 | tf_op jit(solution)/shard_map/ppermute | solution.py:200
  154.4 26.1 %collective-permute-start.23 = (bf16[4,1024,256]{2,1,0:T(8,128)(2,1)S(1)}, bf16[4,1024,256]{2,1,0:T(8,128)(2,1)S(1)}, u32[]{:S(2)}, u32[]{:S(2)}) collective-permute-start(bf16[4,1024,256]{2,1,0:T(8,128)(2,1)S(1)} %pad_maximum_fusion), channel_id=1, source_target_pairs={{0,4},{1,3},{2,6},{3,1},{4,0},{5,7},{6,2},{7,5},{8,12},{9,11},{10,... | collective-permute-start | bytes 6291464 | tf_op jit(solution)/shard_map/ppermute | solution.py:200
  165.5 14.3 %collective-permute-start.22 = (bf16[512,512]{1,0:T(8,128)(2,1)S(1)}, bf16[512,512]{1,0:T(8,128)(2,1)S(1)}, u32[]{:S(2)}, u32[]{:S(2)}) collective-permute-start(bf16[512,512]{1,0:T(8,128)(2,1)S(1)} %attend.1.own_ref), channel_id=1, source_target_pairs={{0,8},{1,9},{2,10},{3,11},{4,12},{5,13},{6,14},{7,15},{8,0},{9,1},... | collective-permute-start | bytes 1572872 | tf_op jit(solution)/shard_map/ppermute | solution.py:200
  180.5 1.3 copy-start.20
  186.9 2.7 %collective-permute-start.24 = (bf16[4,128,1024]{2,1,0:T(8,128)(2,1)S(1)}, bf16[4,128,1024]{2,1,0:T(8,128)(2,1)S(1)}, u32[]{:S(2)}, u32[]{:S(2)}) collective-permute-start(bf16[4,128,1024]{2,1,0:T(8,128)(2,1)S(1)} %get-tuple-element.68), channel_id=1, source_target_pairs={{0,1},{1,0},{2,3},{3,2},{4,5},{5,4},{6,7},{7,6},{8,9},{9,8},{10,11... | collective-permute-start | bytes 3145736 | tf_op jit(solution)/shard_map/ppermute | solution.py:200
  191.2 15.2 %collective-permute-start.27 = (bf16[128,1024]{1,0:T(8,128)(2,1)S(1)}, bf16[128,1024]{1,0:T(8,128)(2,1)S(1)}, u32[]{:S(2)}, u32[]{:S(2)}) collective-permute-start(bf16[128,1024]{1,0:T(8,128)(2,1)S(1)} %get-tuple-element.74), channel_id=1, source_target_pairs={{0,24},{1,25},{2,26},{3,27},{4,28},{5,29},{6,30},{7,31},{8,0},{9,1... | collective-permute-start | bytes 786440 | tf_op jit(solution)/shard_map/ppermute | solution.py:200
  193.5 15.1 %collective-permute-start.26 = (bf16[128,1024]{1,0:T(8,128)(2,1)S(1)}, bf16[128,1024]{1,0:T(8,128)(2,1)S(1)}, u32[]{:S(2)}, u32[]{:S(2)}) collective-permute-start(bf16[128,1024]{1,0:T(8,128)(2,1)S(1)} %get-tuple-element.75), channel_id=1, source_target_pairs={{0,8},{1,9},{2,10},{3,11},{4,12},{5,13},{6,14},{7,15},{8,16},{9,17... | collective-permute-start | bytes 786440 | tf_op jit(solution)/shard_map/ppermute | solution.py:200
  193.5 22.7 %collective-permute-start.25 = (bf16[128,1024]{1,0:T(8,128)(2,1)S(1)}, bf16[128,1024]{1,0:T(8,128)(2,1)S(1)}, u32[]{:S(2)}, u32[]{:S(2)}) collective-permute-start(bf16[128,1024]{1,0:T(8,128)(2,1)S(1)} %get-tuple-element.73), channel_id=1, source_target_pairs={{0,16},{1,17},{2,18},{3,19},{4,20},{5,21},{6,22},{7,23},{8,24},{9,... | collective-permute-start | bytes 786440 | tf_op jit(solution)/shard_map/ppermute | solution.py:200
  (3 other events, 2.4 us)

commit v7 on v6

--- a/solution.py
+++ b/solution.py
@@ -232,31 +232,76 @@
     return values * cosine + pltpu.roll(values, HD // 2, 1) * sine
 
 
-def products(where_ref, x_refs, pieces):
+def pack_kernel(where_ref, *refs):
+    w_query, w_key, w_value, cache_keys, cache_values, slots = refs[:6]
+    outs, sems = refs[6:10], refs[10]
+    level = where_ref[0]
+    depth = w_query.shape[0]
+    copies = []
+
+    def copy(source, target):
+        copies.append(pltpu.make_async_copy(source, target, sems.at[len(copies)]))
+        copies[-1].start()
+
+    for n in range(2):
+        keys, queries = outs[2 * n : 2 * n + 2]
+        for m in range(2):
+            at = jnp.bitwise_xor(level, n + 2 * m)
+            small = pl.ds(pl.multiple_of(at * HD, HD), HD)
+            large = pl.ds(pl.multiple_of(at * 4 * HD, 4 * HD), 4 * HD)
+            for k, (new, old) in enumerate(((w_key, cache_keys), (w_value, cache_values))):
+                to = pl.ds((2 * m + k) * HD, HD)
+                copy(new.at[:, small], keys.at[0:depth, to])
+                copy(old.at[:, small], keys.at[depth : depth + CACHED, to])
+            copy(w_query.at[:, large], queries.at[0, :, pl.ds(m * 4 * HD, 4 * HD)])
+        copy(slots, keys.at[depth + CACHED : depth + CACHED + REC_PAD])
+    for each in copies:
+        each.wait()
+
+
+PACK_COPIES = 22
+
+
+def assemble(where_ref, parts, x_ref):
+    level, core = where_ref[0], where_ref[2]
+    shown = TILE_RUN // 2 // PLANE
+    rows = parts[0].shape[0] - shown
+    for n, part in enumerate(parts):
+        x_ref[n * rows : (n + 1) * rows] = part[0:rows]
+    start = where_ref[4] * rows
+    for n, part in enumerate(parts):
+        which = 2 * lax.rem(level + n % 2, 2) + (core if n < 2 else 1 - core)
+        to = pl.multiple_of(start + which * shown, 16)
+        x_ref[pl.ds(to, shown)] = part[rows : rows + shown]
+
+
+def products(where_ref, x_ref, pieces):
     level, place, core = where_ref[0], where_ref[1], where_ref[2]
-    totals = [None] * len(x_refs)
+    total = None
     for i in range(2):
         for j in range(PLANE):
             depth = pieces[i][j].shape[0]
             block = lax.rem(level + i, 2) * PLANE + place_of(j, place, core)
             start = pl.multiple_of(block * depth, depth)
-            weights = pieces[i][j][...]
-            for r, x_ref in enumerate(x_refs):
-                part = jnp.dot(
-                    x_ref[:, pl.ds(start, depth)], weights, preferred_element_type=jnp.float32
-                )
-                totals[r] = part if totals[r] is None else totals[r] + part
-    return totals
-
-
-def keys_part_kernel(where_ref, x0, x1, own, near, far, old0, old1, keep_ref, send_ref):
+            part = jnp.dot(
+                x_ref[:, pl.ds(start, depth)],
+                pieces[i][j][...],
+                preferred_element_type=jnp.float32,
+            )
+            total = part if total is None else total + part
+    return total
+
+
+def keys_part_kernel(
+    where_ref, x0, x1, x2, x3, own, near, far, old0, old1, keep_ref, send_ref, x_ref
+):
+    assemble(where_ref, (x0, x1, x2, x3), x_ref)
     pieces = [[own.at[i], near.at[i], far.at[i], far.at[2 + i]] for i in range(2)]
-    rows = x0.shape[0]
     width = 2 * HD
-    for r, total in enumerate(products(where_ref, (x0, x1), pieces)):
-        keep_ref[r * rows : (r + 1) * rows] = total[:, :width]
-        send_ref[r * rows : (r + 1) * rows] = total[:, width:].astype(jnp.bfloat16)
-    at = 2 * rows
+    total = products(where_ref, x_ref, pieces)
+    at = total.shape[0]
+    keep_ref[...] = total[:, :width]
+    send_ref[0:at] = total[:, width:].astype(jnp.bfloat16)
     for old in (old0, old1):
         send_ref[at : at + CACHED + REC_PAD] = old[:, width:]
         at += CACHED + REC_PAD
@@ -301,21 +346,20 @@
         ).astype(jnp.bfloat16)
 
 
-def queries_part_kernel(where_ref, x0, x1, *refs):
-    next_own, next_near, next_far = refs[4:7]
+def queries_part_kernel(where_ref, x0, x1, x2, x3, *refs):
+    keep_ref, send_ref, x_ref = refs[6:]
+    assemble(where_ref, (x0, x1, x2, x3), x_ref)
     pieces = [
-        [ref.at[0] for ref in refs[:4]],
-        [next_own.at[0], next_near.at[0], next_far.at[0], next_far.at[1]],
+        [own.at[0], near.at[0], far.at[0], far.at[1]] for own, near, far in (refs[0:3], refs[3:6])
     ]
-    keep_ref, send_ref = refs[7:]
-    block = x0.shape[0] // 2
+    total = products(where_ref, x_ref, pieces)
+    block = total.shape[0] // LEVELS
     tok = block - REC_PAD
     width = 4 * HD
-    for r, total in enumerate(products(where_ref, (x0, x1), pieces)):
-        for k in range(2):
-            fresh = total[k * block : k * block + tok]
-            keep_ref[2 * r + k] = fresh[:, :width]
-            send_ref[2 * r + k] = fresh[:, width:].astype(jnp.bfloat16)
+    for k in range(LEVELS):
+        fresh = total[k * block : k * block + tok]
+        keep_ref[k] = fresh[:, :width]
+        send_ref[k] = fresh[:, width:].astype(jnp.bfloat16)
 
 
 def attend_kernel(
@@ -393,6 +437,7 @@
 
 SMEM = pl.BlockSpec(memory_space=pltpu.SMEM)
 VMEM = pl.BlockSpec(memory_space=pltpu.VMEM)
+ANY = pl.BlockSpec(memory_space=pl.ANY)
 PARAMS = pltpu.CompilerParams(vmem_limit_bytes=48 * 1024 * 1024)
 
 
@@ -419,7 +464,6 @@
     level, place = seq_index // PLANE, seq_index % PLANE
     half_at = level // 2
     own_first = core == half_at
-    where = jnp.stack([level, place, core, jnp.where(own_first, 0, 2)]).astype(jnp.int32)
     tok, width = text_rows.shape
     block_rows = tok + REC_PAD
 
@@ -431,39 +475,27 @@
     assert [owner % PLANE for owner in owners] == list(range(LEVELS))
     owner_levels = jnp.array([owner // PLANE for owner in owners], jnp.int32)
 
+    first_block = jnp.where(own_first, 0, 2)
+    shown_block = (first_block + (level ^ owner_levels[place])) % LEVELS
+    where = jnp.stack([level, place, core, first_block, shown_block]).astype(jnp.int32)
+
     slots = (recompute_slots - seq_index * CACHED).astype(jnp.bfloat16)
     slot_rows = jnp.broadcast_to(jnp.pad(slots, (0, REC_PAD - REC))[:, None], (REC_PAD, 4 * HD))
-
-    def columns(array, size, at):
-        return lax.dynamic_slice_in_dim(array, at * size, size, 1)
-
-    def key_columns(to_level):
-        def pair(k, v):
-            return [columns(a, HD, at) for at in (to_level, to_level ^ 2) for a in (k, v)]
-
-        old = jnp.concatenate(pair(cache_keys, cache_values), axis=1)
-        return pair(w_key, w_value), jnp.concatenate([old, slot_rows], axis=0)
-
-    def query_columns(to_level):
-        return [columns(w_query, 4 * HD, at) for at in (to_level, to_level ^ 2)]
-
     depth = w_query.shape[0]
-    query_own = jnp.concatenate(query_columns(level), axis=1)[None]
+    key_shape = shaped((depth + CACHED + REC_PAD, 4 * HD))
+    query_shape = shaped((1, depth, 8 * HD))
+    key_own, query_own, key_give, query_give = pl.pallas_call(
+        pack_kernel,
+        out_shape=(key_shape, query_shape) * 2,
+        in_specs=[SMEM] + [ANY] * 6,
+        out_specs=(ANY,) * 4,
+        scratch_shapes=[pltpu.SemaphoreType.DMA((PACK_COPIES,))],
+        compiler_params=PARAMS,
+        name="pack",
+    )(where, w_query, w_key, w_value, cache_keys, cache_values, slot_rows)
     query_near = to_near(query_own)
-    query_far = to_far(query_own)
-    own_columns, old_own = key_columns(level)
-    give_columns, old_give = key_columns(level ^ 1)
-    third = (CACHED + REC_PAD + 2) // 3 // 16 * 16 + 16
-    old_give = jnp.pad(old_give, ((0, 3 * third - CACHED - REC_PAD), (0, 0)))
-    given = jnp.concatenate(
-        [
-            jnp.concatenate(give_columns + query_columns(level ^ 1), axis=1),
-            jnp.concatenate([old_give[i * third : (i + 1) * third] for i in range(3)], axis=1),
-        ],
-        axis=0,
-    )
-    taken = across(given, 1)
-
+
+    text_rows, key_give = lax.optimization_barrier((text_rows, key_give))
     rows = jnp.concatenate(
         [text_rows, recompute_rows, jnp.zeros((REC_PAD - REC, width), text_rows.dtype)], axis=0
     )
@@ -474,9 +506,6 @@
     )
     normed = scaled(wide, squares, gain)
     pictures = scaled(pictures, picture_squares, gain)
-    shown = [
-        permuted(pictures, lambda z, p, c, k=k: (2 * c + (k ^ (p % 2)), z, p // 2)) for k in (0, 1)
-    ]
 
     out_rows = w_out.shape[0] // 2
     out_own, out_give = (
@@ -486,49 +515,29 @@
     out_got0, out_got1 = across(out_give[:out_half], 2), across(out_give[out_half:], 2)
 
     crossed = permuted(normed, lambda z, p, c: (z ^ 2, p, 1 - c) if c == 1 - z // 2 else None)
-    crossed, taken, query_near, query_far, *shown = lax.optimization_barrier(
-        (crossed, taken, query_near, query_far, *shown)
-    )
-    query_both = to_far(query_near)
-    key_cols = 4 * HD
-    keys = jnp.stack([jnp.concatenate(own_columns, axis=1), taken[:depth, :key_cols]])
-    query_next = taken[None, :depth, key_cols:]
-    old_next = jnp.concatenate(
-        [taken[depth:, i * key_cols : (i + 1) * key_cols] for i in range(3)], axis=0
-    )[: CACHED + REC_PAD]
-    held = jnp.where(own_first, normed, crossed)
+    normed, pictures, query_give = lax.optimization_barrier((normed, pictures, query_give))
+    shown = permuted(pictures, lambda z, p, c: (2 * c + p // 2, z, p % 2))
+    query_next = across(query_give, 1)
+    key_next = across(key_give, 1)
+    keys = jnp.stack([key_own[:depth], key_next[:depth]])
+    old_own, old_next = key_own[depth:], key_next[depth:]
+    keys_near = to_near(keys)
+    crossed, shown, keys_near, query_next = lax.optimization_barrier(
+        (crossed, shown, keys_near, query_next)
+    )
+    held = jnp.concatenate([jnp.where(own_first, normed, crossed), shown], axis=0)
     next_rows = across(held, 1)
-    keys_near, next_near = to_near(keys), to_near(query_next)
-    odd = level % 2 == 1
-    shown_mine = jnp.concatenate(
-        [jnp.where(odd, shown[1], shown[0]), jnp.where(odd, shown[0], shown[1])], axis=0
-    )
-    shown_other = other_core(shown_mine)
-    next_rows, keys_near, shown_other, next_near, out_got0, query_both = lax.optimization_barrier(
-        (next_rows, keys_near, shown_other, next_near, out_got0, query_both)
-    )
+    held_other = other_core(held)
     keys_far = to_far(jnp.concatenate([keys, keys_near], axis=0))
-    shown_all = jnp.concatenate(
-        [
-            jnp.where(core == 0, shown_mine, shown_other),
-            jnp.where(core == 0, shown_other, shown_mine),
-        ],
-        axis=0,
-    )
-    shown_at = owner_levels[place]
-
-    def with_pictures(block, at):
-        return [jnp.where(at == shown_at, shown_all, block[:tok]), block[tok:]]
-
-    held_at = jnp.where(own_first, level, level ^ 2)
-    rows_mine = jnp.concatenate(
-        with_pictures(held, held_at) + with_pictures(next_rows, held_at ^ 1), axis=0
-    )
-    rows_other = other_core(rows_mine)
-    rows_other, keys_far, next_near, out_got1 = lax.optimization_barrier(
-        (rows_other, keys_far, next_near, out_got1)
-    )
+    query_far = to_far(jnp.concatenate([query_own, query_near], axis=0))
+    next_near = to_near(query_next)
+    next_rows, held_other, keys_far, query_far, out_got0, next_near = lax.optimization_barrier(
+        (next_rows, held_other, keys_far, query_far, out_got0, next_near)
+    )
+    next_other = other_core(next_rows)
+    next_other, out_got1 = lax.optimization_barrier((next_other, out_got1))
     next_far = to_far(jnp.concatenate([query_next, next_near], axis=0))
+    parts = (held, next_rows, held_other, next_other)
 
     half = HD // 2
     freqs = ROPE_BASE ** (-jnp.arange(half, dtype=jnp.float32) / half)
@@ -549,12 +558,13 @@
             shaped((all_rows, 2 * HD), jnp.float32),
             shaped((all_rows + 2 * (CACHED + REC_PAD), 2 * HD)),
         ),
-        in_specs=[SMEM] + [VMEM] * 7,
+        in_specs=[SMEM] + [VMEM] * 9,
         out_specs=(VMEM, VMEM),
+        scratch_shapes=[pltpu.VMEM((all_rows, width), jnp.bfloat16)],
         compiler_params=PARAMS,
         name="keys_part",
-    )(where, rows_mine, rows_other, keys, keys_near, keys_far, old_own, old_next)
-    send, rows_after = lax.optimization_barrier((send, rows_mine))
+    )(where, *parts, keys, keys_near, keys_far, old_own, old_next)
+    send, *parts = lax.optimization_barrier((send, *parts))
     out_pair = jnp.stack([out_own, jnp.concatenate([out_got0, out_got1], axis=0)])
     out_pair, next_far = lax.optimization_barrier((out_pair, next_far))
     out_near = to_near(out_pair)
@@ -564,22 +574,12 @@
             shaped((LEVELS, tok, 4 * HD), jnp.float32),
             shaped((LEVELS, tok, 4 * HD)),
         ),
-        in_specs=[SMEM] + [VMEM] * 9,
+        in_specs=[SMEM] + [VMEM] * 10,
         out_specs=(VMEM, VMEM),
+        scratch_shapes=[pltpu.VMEM((all_rows, width), jnp.bfloat16)],
         compiler_params=PARAMS,
         name="queries_part",
-    )(
-        where,
-        rows_after,
-        rows_other,
-        query_own,
-        query_near,
-        query_far,
-        query_both,
-        query_next,
-        next_near,
-        next_far,
-    )
+    )(where, *parts, query_own, query_near, query_far, query_next, next_near, next_far)
     got_keys, q_send = lax.optimization_barrier((across(send, 2), q_send))
     kv = pl.pallas_call(
         keys_join_kernel,

time: 222 us -> 208 us (0.937)
  waiting for transfers between devices: 108 us -> 88.1 us
  starting transfers between devices: 44.7 us -> 57 us
  other arithmetic: 20.3 us -> 15.1 us
    ppermute x28 -> x27, waiting for transfers between devices: 108 us -> 88.1 us  [permuted(): return lax.ppermute(value, ('seq', 'head'), perm)]
    ppermute x28 -> x27, starting transfers between devices: 44.7 us -> 57 us  [permuted(): return lax.ppermute(value, ('seq', 'head'), perm)]
    select_n x4 -> x1, other arithmetic: 4.78 us -> 1.27 us  [by_levels(): jnp.where(own_first, normed, crossed)]
    dynamic_slice x5 -> x1, local copies, waits for them, and re-layouts: 4.58 us -> 1.34 us  [by_levels(): shown_block = (first_block + (level ^ owner_levels[place])) % LEVELS]
    unnamed x81 -> x58, local copies, waits for them, and re-layouts: 8.49 us -> 9.92 us
  transfers between devices with their start and end apart: 28 -> 27, of which waited for: 17 -> 14; matrix products, arithmetic and copies ran while one was open for 8% -> 7% of each run, Pallas kernels for 8% -> 8%
where the time goes in v7:
time: 208 us; the launch traced here: 204 us
  waiting for transfers between devices  88.1 us (42%)
  starting transfers between devices  57 us (27%)
  Pallas kernels  23.3 us (11%)
  local copies, waits for them, and re-layouts  17.2 us (8%)
  other arithmetic  15.1 us (7%)
  blocking collectives  2.47 us (1%)
    ppermute x27, waiting for transfers between devices, permuted(): return lax.ppermute(value, ('seq', 'head'), perm)  88.1 us
    ppermute x27, starting transfers between devices, permuted(): return lax.ppermute(value, ('seq', 'head'), perm)  57 us
    unnamed x58, local copies, waits for them, and re-layouts  9.92 us
    pallas_call x1, Pallas kernels, by_levels(): pl.pallas_call(attend_kernel, out_shape=shaped((LEVELS * tok, 4 * HD)), i...  8.89 us
    pallas_call x1, Pallas kernels, by_levels(): pl.pallas_call(queries_part_kernel, out_shape=(shaped((LEVELS, tok, 4 * H...  5.18 us
    pallas_call x1, Pallas kernels, by_levels(): pl.pallas_call(output_kernel, out_shape=(shaped((LEVELS, tok, wide_cols),...  5.1 us
  transfers between devices with their start and end apart: 27, of which 14 were waited for; matrix products, arithmetic and copies ran while one was open for 7% of the time, Pallas kernels for 8%

profile of v7, /device:TPU:8, one launch (start us, length us, event | category | flops | bytes accessed | tf_op | source)
XLA Modules:
  0.0 204.3 jit_solution(685847161438391451)
XLA Ops:
  0.0 1.3 dynamic_slice.12
  2.0 0.7 subtract_convert_fusion
  2.9 1.2 copy-done.11
  4.1 0.9 copy-done.15
  5.0 0.9 copy-done.16
  6.0 0.8 copy-done.17
  6.8 0.8 copy-done.18
  7.7 1.0 pack.1
  9.3 2.5 %all-reduce.1 = (f32[144]{0:T(256)S(1)}, f32[32]{0:T(128)S(1)}) all-reduce(f32[144]{0:T(256)S(1)} %fusion, f32[32]{0:T(128)S(1)} %fusion.4), channel_id=1, replica_groups=mesh['seq'=16,'head'=2] {'head'}, use_global_device_ids=true, to_apply=%region_1.2 | all-reduce | flops 176 | bytes 1408 | tf_op jit(solution)/shard_map/psum | solution.py:504
  11.8 1.2 fusion.2
  13.0 1.5 collective-permute-start
  14.5 0.8 fusion.6
  15.2 2.0 collective-permute-start.4
  17.3 1.5 collective-permute-start.8
  18.8 6.8 %collective-permute-done.2 = bf16[336,512]{1,0:T(8,128)(2,1)} collective-permute-done((bf16[336,512]{1,0:T(8,128)(2,1)S(1)}, bf16[336,512]{1,0:T(8,128)(2,1)}, u32[]{:S(2)}, u32[]{:S(2)}) %collective-permute-start.2) | collective-permute-done | bytes 344096 | tf_op jit(solution)/shard_map/ppermute | solution.py:200
  25.6 1.0 slice_bitcast_fusion
  26.6 0.7 copy-done.19
  27.3 3.0 %collective-permute-start.3 = (bf16[2,256,512]{2,1,0:T(8,128)(2,1)S(1)}, bf16[2,256,512]{2,1,0:T(8,128)(2,1)S(1)}, u32[]{:S(2)}, u32[]{:S(2)}) collective-permute-start(bf16[2,256,512]{2,1,0:T(8,128)(2,1)S(1)} %pad_maximum_fusion.6.own), channel_id=1, source_target_pairs={{0,2},{1,5},{2,0},{3,7},{4,6},{5,1},{6,4},{7,3},{8,10},{9,13},{10,... | collective-permute-start | bytes 1572872 | tf_op jit(solution)/shard_map/ppermute | solution.py:200
  30.3 4.4 %collective-permute-start.1 = (bf16[32,2048]{1,0:T(8,128)(2,1)}, bf16[32,2048]{1,0:T(8,128)(2,1)}, u32[]{:S(2)}, u32[]{:S(2)}) collective-permute-start(bf16[32,2048]{1,0:T(8,128)(2,1)} %fusion.6), channel_id=1, source_target_pairs={{0,0},{1,16},{2,1},{3,17},{4,8},{5,24},{6,9},{7,25},{8,2},{9,18},{... | collective-permute-start | bytes 393224 | tf_op jit(solution)/shard_map/ppermute | solution.py:200
  34.7 1.8 constant_dynamic-slice_fusion.1
  36.5 9.0 %collective-permute-start.10 = (bf16[512,256]{1,0:T(8,128)(2,1)S(1)}, bf16[512,256]{1,0:T(8,128)(2,1)S(1)}, u32[]{:S(2)}, u32[]{:S(2)}) collective-permute-start(bf16[512,256]{1,0:T(8,128)(2,1)S(1)} %get-tuple-element.93), channel_id=1, source_target_pairs={{0,16},{1,17},{2,18},{3,19},{4,20},{5,21},{6,22},{7,23},{8,24},{9,... | collective-permute-start | bytes 786440 | tf_op jit(solution)/shard_map/ppermute | solution.py:200
  45.7 9.5 %collective-permute-start.9 = (bf16[2,256,1024]{2,1,0:T(8,128)(2,1)S(1)}, bf16[2,256,1024]{2,1,0:T(8,128)(2,1)S(1)}, u32[]{:S(2)}, u32[]{:S(2)}) collective-permute-start(bf16[2,256,1024]{2,1,0:T(8,128)(2,1)S(1)} %pad_maximum_fusion.2), channel_id=1, source_target_pairs={{0,4},{1,3},{2,6},{3,1},{4,0},{5,7},{6,2},{7,5},{8,12},{9,11},{10,... | collective-permute-start | bytes 3145736 | tf_op jit(solution)/shard_map/ppermute | solution.py:200
  55.4 1.3 broadcast_select_fusion
  56.7 1.0 pad_maximum_fusion.5.x0
  57.8 1.4 collective-permute-done.10
  59.2 14.9 %collective-permute-done.11.refs_4_ = bf16[1,256,1024]{2,1,0:T(8,128)(2,1)S(1)} collective-permute-done((bf16[1,256,1024]{2,1,0:T(8,128)(2,1)S(1)}, bf16[1,256,1024]{2,1,0:T(8,128)(2,1)S(1)}, u32[]{:S(2)}, u32[]{:S(2)}) %collective-permute-start.11) | collective-permute-done | bytes 524320 | tf_op jit(solution)/shard_map/ppermute | solution.py:200
  74.1 3.4 %collective-permute-start.13 = (bf16[512,256]{1,0:T(8,128)(2,1)}, bf16[512,256]{1,0:T(8,128)(2,1)}, u32[]{:S(2)}, u32[]{:S(2)}) collective-permute-start(bf16[512,256]{1,0:T(8,128)(2,1)} %get-tuple-element.92), channel_id=1, source_target_pairs={{0,16},{1,17},{2,18},{3,19},{4,20},{5,21},{6,22},{7,23},{8,24},{9,... | collective-permute-start | bytes 786440 | tf_op jit(solution)/shard_map/ppermute | solution.py:200
  77.6 7.2 %collective-permute-done.7.far = bf16[4,256,512]{2,1,0:T(8,128)(2,1)S(1)} collective-permute-done((bf16[4,256,512]{2,1,0:T(8,128)(2,1)S(1)}, bf16[4,256,512]{2,1,0:T(8,128)(2,1)S(1)}, u32[]{:S(2)}, u32[]{:S(2)}) %collective-permute-start.7) | collective-permute-done | bytes 1048608 | tf_op jit(solution)/shard_map/ppermute | solution.py:200
  84.8 2.5 %pad_maximum_fusion.4 = bf16[2,256,1024]{2,1,0:T(8,128)(2,1)} fusion(bf16[1,256,1024]{2,1,0:T(8,128)(2,1)S(1)} %collective-permute-done.11.refs_4_, bf16[1,256,1024]{2,1,0:T(8,128)(2,1)} %copy-done), kind=kLoop, calls=%fused_computation.9 | loop fusion | flops 524288 | bytes 2097152 | tf_op jit(solution)/shard_map/concatenate | solution.py:539
  87.3 0.8 copy-done.4
  88.1 2.3 %collective-permute-start.14 = (bf16[2,256,1024]{2,1,0:T(8,128)(2,1)}, bf16[2,256,1024]{2,1,0:T(8,128)(2,1)}, u32[]{:S(2)}, u32[]{:S(2)}) collective-permute-start(bf16[2,256,1024]{2,1,0:T(8,128)(2,1)} %pad_maximum_fusion.4), channel_id=1, source_target_pairs={{0,4},{1,3},{2,6},{3,1},{4,0},{5,7},{6,2},{7,5},{8,12},{9,11},{10,... | collective-permute-start | bytes 3145736 | tf_op jit(solution)/shard_map/ppermute | solution.py:200
  90.5 0.9 slice.46.old0
  91.4 1.2 dynamic-slice_bitcast_fusion
  92.6 0.9 slice.57.old1
  93.5 1.2 copy-done.13
  94.8 2.1 %keys_part.1 = (f32[576,256]{1,0:T(8,128)S(1)}, bf16[736,256]{1,0:T(8,128)(2,1)S(1)}) custom-call(s32[5]{0:T(128)S(1)} %stack.41.where_ref, bf16[176,2048]{1,0:T(8,128)(2,1)S(1)} %pad_maximum_fusion.5.x0, bf16[176,2048]{1,0:T(8,128)(2,1)S(1)} %collective-permute-done.5.x1, bf16[176,2048]{1,0:T(8,128)(2,1)S(1)} %collective-permute-done.6.x2, ...), custom_call_target="tpu_custom_call" | custom-call | tf_op jit(solution)/shard_map/keys_part/pallas_call | solution.py:555
  96.9 1.0 maximum_bitcast_fusion
  98.0 5.4 %collective-permute-done.14.refs_5_ = bf16[2,256,1024]{2,1,0:T(8,128)(2,1)} collective-permute-done((bf16[2,256,1024]{2,1,0:T(8,128)(2,1)}, bf16[2,256,1024]{2,1,0:T(8,128)(2,1)}, u32[]{:S(2)}, u32[]{:S(2)}) %collective-permute-start.14) | collective-permute-done | bytes 1048608 | tf_op jit(solution)/shard_map/ppermute | solution.py:200
  103.7 1.4 fusion.10
  105.6 0.7 copy-done.1
  106.5 5.2 %queries_part.1 = (f32[4,128,512]{2,1,0:T(8,128)}, bf16[4,128,512]{2,1,0:T(8,128)(2,1)S(1)}) custom-call(s32[5]{0:T(128)S(1)} %stack.41.where_ref, bf16[176,2048]{1,0:T(8,128)(2,1)S(1)} %pad_maximum_fusion.5.x0, bf16[176,2048]{1,0:T(8,128)(2,1)S(1)} %collective-permute-done.5.x1, bf16[176,2048]{1,0:T(8,128)(2,1)S(1)} %collective-permute-done.6.x2, ...), custom_call_target="tpu_custom_call" | custom-call | tf_op jit(solution)/shard_map/queries_part/pallas_call | solution.py:571
  111.7 1.6 collective-permute-done.15.got_ref
  113.3 1.0 keys_join.1.kv0
  114.7 3.4 %collective-permute-start.20 = (bf16[4,128,512]{2,1,0:T(8,128)(2,1)S(1)}, bf16[4,128,512]{2,1,0:T(8,128)(2,1)S(1)}, u32[]{:S(2)}, u32[]{:S(2)}) collective-permute-start(bf16[4,128,512]{2,1,0:T(8,128)(2,1)S(1)} %get-tuple-element.78), channel_id=1, source_target_pairs={{0,16},{1,17},{2,18},{3,19},{4,20},{5,21},{6,22},{7,23},{8,24},{9,... | collective-permute-start | bytes 1572872 | tf_op jit(solution)/shard_map/ppermute | solution.py:200
  118.1 2.0 collective-permute-start.16
  120.1 4.9 %collective-permute-done.17.kv1 = bf16[6,128,256]{2,1,0:T(8,128)(2,1)S(1)} collective-permute-done((bf16[6,128,256]{2,1,0:T(8,128)(2,1)S(1)}, bf16[6,128,256]{2,1,0:T(8,128)(2,1)S(1)}, u32[]{:S(2)}, u32[]{:S(2)}) %collective-permute-start.17) | collective-permute-done | bytes 393248 | tf_op jit(solution)/shard_map/ppermute | solution.py:200
  124.9 2.8 %collective-permute-start.18 = (bf16[6,128,256]{2,1,0:T(8,128)(2,1)S(1)}, bf16[6,128,256]{2,1,0:T(8,128)(2,1)S(1)}, u32[]{:S(2)}, u32[]{:S(2)}) collective-permute-start(bf16[6,128,256]{2,1,0:T(8,128)(2,1)S(1)} %collective-permute-done.17.kv1), channel_id=1, source_target_pairs={{0,4},{1,3},{2,6},{3,1},{4,0},{5,7},{6,2},{7,5},{8,12},{9,11},{10,... | collective-permute-start | bytes 1179656 | tf_op jit(solution)/shard_map/ppermute | solution.py:200
  127.8 12.0 %collective-permute-done.20.got_ref = bf16[4,128,512]{2,1,0:T(8,128)(2,1)S(1)} collective-permute-done((bf16[4,128,512]{2,1,0:T(8,128)(2,1)S(1)}, bf16[4,128,512]{2,1,0:T(8,128)(2,1)S(1)}, u32[]{:S(2)}, u32[]{:S(2)}) %collective-permute-start.20) | collective-permute-done | bytes 524320 | tf_op jit(solution)/shard_map/ppermute | solution.py:200
  140.0 1.7 collective-permute-start.22
  141.7 8.9 %attend.1.own_ref = bf16[512,512]{1,0:T(8,128)(2,1)S(1)} custom-call(s32[5]{0:T(128)S(1)} %stack.41.where_ref, f32[4,128,512]{2,1,0:T(8,128)S(1)} %copy-done.10, bf16[4,128,512]{2,1,0:T(8,128)(2,1)S(1)} %collective-permute-done.20.got_ref, f32[4,192,128]{2,1,0:T(8,128)S(1)} %pad_maximum_fusion.8.cos_ref, f32[4,192,128]{2,1,0:T(8,128)S(1)} %pad_maximum_fusion.9.sin_ref, ...), custom_call_target="tpu_custom_call" | custom-call | tf_op jit(solution)/shard_map/attend/pallas_call | solution.py:601
  150.5 2.3 %collective-permute-start.21 = (bf16[512,512]{1,0:T(8,128)(2,1)S(1)}, bf16[512,512]{1,0:T(8,128)(2,1)S(1)}, u32[]{:S(2)}, u32[]{:S(2)}) collective-permute-start(bf16[512,512]{1,0:T(8,128)(2,1)S(1)} %attend.1.own_ref), channel_id=1, source_target_pairs={{0,8},{1,9},{2,10},{3,11},{4,12},{5,13},{6,14},{7,15},{8,0},{9,1},... | collective-permute-start | bytes 1572872 | tf_op jit(solution)/shard_map/ppermute | solution.py:200
  152.8 12.4 %collective-permute-done.21.next_ref = bf16[512,512]{1,0:T(8,128)(2,1)S(1)} collective-permute-done((bf16[512,512]{1,0:T(8,128)(2,1)S(1)}, bf16[512,512]{1,0:T(8,128)(2,1)S(1)}, u32[]{:S(2)}, u32[]{:S(2)}) %collective-permute-start.21) | collective-permute-done | bytes 524320 | tf_op jit(solution)/shard_map/ppermute | solution.py:200
  165.2 0.9 collective-permute-done.22.w_far
  166.1 1.3 copy-done.22
  167.4 5.1 %output.1 = (f32[4,128,1024]{2,1,0:T(8,128)}, bf16[4,128,1024]{2,1,0:T(8,128)(2,1)S(1)}) custom-call(s32[5]{0:T(128)S(1)} %stack.41.where_ref, bf16[512,512]{1,0:T(8,128)(2,1)S(1)} %attend.1.own_ref, bf16[512,512]{1,0:T(8,128)(2,1)S(1)} %collective-permute-done.21.next_ref, bf16[2,1024,256]{2,1,0:T(8,128)(2,1)S(1)} %pad_maximum_fusion.3.w_own, ...), custom_call_target="tpu_custom_call" | custom-call | tf_op jit(solution)/shard_map/output/pallas_call | solution.py:612
  172.5 2.7 %collective-permute-done.23 = bf16[4,128,1024]{2,1,0:T(8,128)(2,1)S(1)} collective-permute-done((bf16[4,128,1024]{2,1,0:T(8,128)(2,1)S(1)}, bf16[4,128,1024]{2,1,0:T(8,128)(2,1)S(1)}, u32[]{:S(2)}, u32[]{:S(2)}) %collective-permute-start.23) | collective-permute-done | bytes 1048608 | tf_op jit(solution)/shard_map/ppermute | solution.py:200
  175.2 1.6 fusion.7
  176.8 2.6 %collective-permute-start.26 = (bf16[128,1024]{1,0:T(8,128)(2,1)S(1)}, bf16[128,1024]{1,0:T(8,128)(2,1)S(1)}, u32[]{:S(2)}, u32[]{:S(2)}) collective-permute-start(bf16[128,1024]{1,0:T(8,128)(2,1)S(1)} %get-tuple-element.90), channel_id=1, source_target_pairs={{0,24},{1,25},{2,26},{3,27},{4,28},{5,29},{6,30},{7,31},{8,0},{9,1... | collective-permute-start | bytes 786440 | tf_op jit(solution)/shard_map/ppermute | solution.py:200
  179.3 4.7 %collective-permute-start.24 = (bf16[128,1024]{1,0:T(8,128)(2,1)S(1)}, bf16[128,1024]{1,0:T(8,128)(2,1)S(1)}, u32[]{:S(2)}, u32[]{:S(2)}) collective-permute-start(bf16[128,1024]{1,0:T(8,128)(2,1)S(1)} %get-tuple-element.89), channel_id=1, source_target_pairs={{0,16},{1,17},{2,18},{3,19},{4,20},{5,21},{6,22},{7,23},{8,24},{9,... | collective-permute-start | bytes 786440 | tf_op jit(solution)/shard_map/ppermute | solution.py:200
  184.0 8.4 %collective-permute-done.26 = bf16[128,1024]{1,0:T(8,128)(2,1)S(1)} collective-permute-done((bf16[128,1024]{1,0:T(8,128)(2,1)S(1)}, bf16[128,1024]{1,0:T(8,128)(2,1)S(1)}, u32[]{:S(2)}, u32[]{:S(2)}) %collective-permute-start.26) | collective-permute-done | bytes 262176 | tf_op jit(solution)/shard_map/ppermute | solution.py:200
  192.5 2.0 collective-permute-done.25
  194.5 7.6 %collective-permute-done.24 = bf16[128,1024]{1,0:T(8,128)(2,1)S(1)} collective-permute-done((bf16[128,1024]{1,0:T(8,128)(2,1)S(1)}, bf16[128,1024]{1,0:T(8,128)(2,1)S(1)}, u32[]{:S(2)}, u32[]{:S(2)}) %collective-permute-start.24) | collective-permute-done | bytes 262176 | tf_op jit(solution)/shard_map/ppermute | solution.py:200
  202.1 1.2 broadcast_select_fusion.2
  203.4 0.8 pad_maximum_fusion.7
  (96 shorter events, 3.3 us)
Async XLA Ops:
  0.0 8.7 %copy-start.24 = (bf16[32,2048]{1,0:T(8,128)(2,1)S(1)}, bf16[32,2048]{1,0:T(8,128)(2,1)}, u32[]{:S(2)}) copy-start(bf16[32,2048]{1,0:T(8,128)(2,1)} %param.14) | copy-start | bytes 393220
  2.9 1.2 copy-start.11
  4.1 0.9 copy-start.15
  5.0 0.9 copy-start.16
  6.0 0.8 copy-start.17
  6.8 0.8 copy-start.18
  7.7 1.3 copy-start.21
  7.7 1.3 copy-start.27
  7.7 4.1 %copy-start.28 = (f32[4096]{0:T(1024)S(1)}, f32[4096]{0:T(1024)}, u32[]{:S(2)}) copy-start(f32[4096]{0:T(1024)} %param.15) | copy-start | bytes 49156
  8.7 10.1 %copy-start.14 = (bf16[336,512]{1,0:T(8,128)(2,1)}, bf16[336,512]{1,0:T(8,128)(2,1)S(1)}, u32[]{:S(2)}) copy-start(bf16[336,512]{1,0:T(8,128)(2,1)S(1)} %get-tuple-element.50) | copy-start | bytes 1032196
  13.0 42.2 %collective-permute-start = (bf16[144,2048]{1,0:T(8,128)(2,1)}, bf16[144,2048]{1,0:T(8,128)(2,1)}, u32[]{:S(2)}, u32[]{:S(2)}) collective-permute-start(bf16[144,2048]{1,0:T(8,128)(2,1)} %fusion.2), channel_id=1, source_target_pairs={{1,16},{3,18},{5,20},{7,22},{9,24},{11,26},{13,28},{15,30},{16,1},... | collective-permute-start | bytes 1769480 | tf_op jit(solution)/shard_map/ppermute | solution.py:200
  14.5 11.1 %collective-permute-start.2 = (bf16[336,512]{1,0:T(8,128)(2,1)S(1)}, bf16[336,512]{1,0:T(8,128)(2,1)}, u32[]{:S(2)}, u32[]{:S(2)}) collective-permute-start(bf16[336,512]{1,0:T(8,128)(2,1)S(1)} %get-tuple-element.51), channel_id=1, source_target_pairs={{0,8},{1,9},{2,10},{3,11},{4,12},{5,13},{6,14},{7,15},{8,0},{9,1},... | collective-permute-start | bytes 1032200 | tf_op jit(solution)/shard_map/ppermute | solution.py:200
  15.2 39.9 %collective-permute-start.4 = (bf16[1,256,1024]{2,1,0:T(8,128)(2,1)S(1)}, bf16[1,256,1024]{2,1,0:T(8,128)(2,1)S(1)}, u32[]{:S(2)}, u32[]{:S(2)}) collective-permute-start(bf16[1,256,1024]{2,1,0:T(8,128)(2,1)S(1)} %get-tuple-element.52), channel_id=1, source_target_pairs={{0,8},{1,9},{2,10},{3,11},{4,12},{5,13},{6,14},{7,15},{8,0},{9,1},... | collective-permute-start | bytes 1572872 | tf_op jit(solution)/shard_map/ppermute | solution.py:200
  17.3 19.3 %collective-permute-start.8 = (bf16[1,256,1024]{2,1,0:T(8,128)(2,1)S(1)}, bf16[1,256,1024]{2,1,0:T(8,128)(2,1)S(1)}, u32[]{:S(2)}, u32[]{:S(2)}) collective-permute-start(bf16[1,256,1024]{2,1,0:T(8,128)(2,1)S(1)} %get-tuple-element.56.refs_0_), channel_id=1, source_target_pairs={{0,2},{1,5},{2,0},{3,7},{4,6},{5,1},{6,4},{7,3},{8,10},{9,13},{10,... | collective-permute-start | bytes 1572872 | tf_op jit(solution)/shard_map/ppermute | solution.py:200
  26.5 0.7 copy-start.19
  27.3 18.3 %copy-start.6 = (bf16[2,256,512]{2,1,0:T(8,128)(2,1)}, bf16[2,256,512]{2,1,0:T(8,128)(2,1)S(1)}, u32[]{:S(2)}) copy-start(bf16[2,256,512]{2,1,0:T(8,128)(2,1)S(1)} %pad_maximum_fusion.6.own) | copy-start | bytes 1572868
  27.3 27.8 %collective-permute-start.3 = (bf16[2,256,512]{2,1,0:T(8,128)(2,1)S(1)}, bf16[2,256,512]{2,1,0:T(8,128)(2,1)S(1)}, u32[]{:S(2)}, u32[]{:S(2)}) collective-permute-start(bf16[2,256,512]{2,1,0:T(8,128)(2,1)S(1)} %pad_maximum_fusion.6.own), channel_id=1, source_target_pairs={{0,2},{1,5},{2,0},{3,7},{4,6},{5,1},{6,4},{7,3},{8,10},{9,13},{10,... | collective-permute-start | bytes 1572872 | tf_op jit(solution)/shard_map/ppermute | solution.py:200
  30.3 15.4 %collective-permute-start.1 = (bf16[32,2048]{1,0:T(8,128)(2,1)}, bf16[32,2048]{1,0:T(8,128)(2,1)}, u32[]{:S(2)}, u32[]{:S(2)}) collective-permute-start(bf16[32,2048]{1,0:T(8,128)(2,1)} %fusion.6), channel_id=1, source_target_pairs={{0,0},{1,16},{2,1},{3,17},{4,8},{5,24},{6,9},{7,25},{8,2},{9,18},{... | collective-permute-start | bytes 393224 | tf_op jit(solution)/shard_map/ppermute | solution.py:200
  36.5 18.6 %copy-start.20 = (bf16[1,256,512]{2,1,0:T(8,128)(2,1)S(1)}, bf16[1,256,512]{2,1,0:T(8,128)(2,1)}, u32[]{:S(2)}) copy-start(bf16[1,256,512]{2,1,0:T(8,128)(2,1)} %copy-done.19) | copy-start | bytes 786436
  36.5 18.8 %copy-start.2 = (bf16[1,256,1024]{2,1,0:T(8,128)(2,1)}, bf16[1,256,1024]{2,1,0:T(8,128)(2,1)S(1)}, u32[]{:S(2)}) copy-start(bf16[1,256,1024]{2,1,0:T(8,128)(2,1)S(1)} %collective-permute-done.8.refs_1_) | copy-start | bytes 1572868
  36.5 22.7 %collective-permute-start.10 = (bf16[512,256]{1,0:T(8,128)(2,1)S(1)}, bf16[512,256]{1,0:T(8,128)(2,1)S(1)}, u32[]{:S(2)}, u32[]{:S(2)}) collective-permute-start(bf16[512,256]{1,0:T(8,128)(2,1)S(1)} %get-tuple-element.93), channel_id=1, source_target_pairs={{0,16},{1,17},{2,18},{3,19},{4,20},{5,21},{6,22},{7,23},{8,24},{9,... | collective-permute-start | bytes 786440 | tf_op jit(solution)/shard_map/ppermute | solution.py:200
  45.7 31.9 %collective-permute-start.9 = (bf16[2,256,1024]{2,1,0:T(8,128)(2,1)S(1)}, bf16[2,256,1024]{2,1,0:T(8,128)(2,1)S(1)}, u32[]{:S(2)}, u32[]{:S(2)}) collective-permute-start(bf16[2,256,1024]{2,1,0:T(8,128)(2,1)S(1)} %pad_maximum_fusion.2), channel_id=1, source_target_pairs={{0,4},{1,3},{2,6},{3,1},{4,0},{5,7},{6,2},{7,5},{8,12},{9,11},{10,... | collective-permute-start | bytes 3145736 | tf_op jit(solution)/shard_map/ppermute | solution.py:200
  55.1 4.1 %copy-start = (bf16[1,256,1024]{2,1,0:T(8,128)(2,1)}, bf16[1,256,1024]{2,1,0:T(8,128)(2,1)S(1)}, u32[]{:S(2)}) copy-start(bf16[1,256,1024]{2,1,0:T(8,128)(2,1)S(1)} %collective-permute-done.4.refs_3_) | copy-start | bytes 1572868
  55.2 1.5 copy-start.8
  55.3 29.5 %collective-permute-start.7 = (bf16[4,256,512]{2,1,0:T(8,128)(2,1)S(1)}, bf16[4,256,512]{2,1,0:T(8,128)(2,1)S(1)}, u32[]{:S(2)}, u32[]{:S(2)}) collective-permute-start(bf16[4,256,512]{2,1,0:T(8,128)(2,1)S(1)} %pad_maximum_fusion.1), channel_id=1, source_target_pairs={{0,4},{1,3},{2,6},{3,1},{4,0},{5,7},{6,2},{7,5},{8,12},{9,11},{10,... | collective-permute-start | bytes 3145736 | tf_op jit(solution)/shard_map/ppermute | solution.py:200
  57.6 19.9 %collective-permute-start.5 = (bf16[176,2048]{1,0:T(8,128)(2,1)S(1)}, bf16[176,2048]{1,0:T(8,128)(2,1)S(1)}, u32[]{:S(2)}, u32[]{:S(2)}) collective-permute-start(bf16[176,2048]{1,0:T(8,128)(2,1)S(1)} %pad_maximum_fusion.5.x0), channel_id=1, source_target_pairs={{0,8},{1,9},{2,10},{3,11},{4,12},{5,13},{6,14},{7,15},{8,0},{9,1},... | collective-permute-start | bytes 2162696 | tf_op jit(solution)/shard_map/ppermute | solution.py:200
  57.7 19.8 %collective-permute-start.6 = (bf16[176,2048]{1,0:T(8,128)(2,1)S(1)}, bf16[176,2048]{1,0:T(8,128)(2,1)S(1)}, u32[]{:S(2)}, u32[]{:S(2)}) collective-permute-start(bf16[176,2048]{1,0:T(8,128)(2,1)S(1)} %pad_maximum_fusion.5.x0), channel_id=1, source_target_pairs={{0,1},{1,0},{2,3},{3,2},{4,5},{5,4},{6,7},{7,6},{8,9},{9,8},{10,11... | collective-permute-start | bytes 2162696 | tf_op jit(solution)/shard_map/ppermute | solution.py:200
  59.2 31.3 %copy-start.25 = (bf16[512,256]{1,0:T(8,128)(2,1)}, bf16[512,256]{1,0:T(8,128)(2,1)S(1)}, u32[]{:S(2)}) copy-start(bf16[512,256]{1,0:T(8,128)(2,1)S(1)} %collective-permute-done.10) | copy-start | bytes 786436
  59.2 14.9 %collective-permute-start.11 = (bf16[1,256,1024]{2,1,0:T(8,128)(2,1)S(1)}, bf16[1,256,1024]{2,1,0:T(8,128)(2,1)S(1)}, u32[]{:S(2)}, u32[]{:S(2)}) collective-permute-start(bf16[1,256,1024]{2,1,0:T(8,128)(2,1)S(1)} %collective-permute-done.4.refs_3_), channel_id=1, source_target_pairs={{0,2},{1,5},{2,0},{3,7},{4,6},{5,1},{6,4},{7,3},{8,10},{9,13},{10,... | collective-permute-start | bytes 1572872 | tf_op jit(solution)/shard_map/ppermute | solution.py:200
  74.1 19.4 %collective-permute-start.13 = (bf16[512,256]{1,0:T(8,128)(2,1)}, bf16[512,256]{1,0:T(8,128)(2,1)}, u32[]{:S(2)}, u32[]{:S(2)}) collective-permute-start(bf16[512,256]{1,0:T(8,128)(2,1)} %get-tuple-element.92), channel_id=1, source_target_pairs={{0,16},{1,17},{2,18},{3,19},{4,20},{5,21},{6,22},{7,23},{8,24},{9,... | collective-permute-start | bytes 786440 | tf_op jit(solution)/shard_map/ppermute | solution.py:200
  77.5 13.0 %copy-start.23 = (bf16[2,256,1024]{2,1,0:T(8,128)(2,1)}, bf16[2,256,1024]{2,1,0:T(8,128)(2,1)S(1)}, u32[]{:S(2)}) copy-start(bf16[2,256,1024]{2,1,0:T(8,128)(2,1)S(1)} %collective-permute-done.9.refs_2_) | copy-start | bytes 3145732
  84.8 2.5 %copy-start.12 = (bf16[4,256,512]{2,1,0:T(8,128)(2,1)}, bf16[4,256,512]{2,1,0:T(8,128)(2,1)S(1)}, u32[]{:S(2)}) copy-start(bf16[4,256,512]{2,1,0:T(8,128)(2,1)S(1)} %collective-permute-done.7.far) | copy-start | bytes 3145732
  84.8 8.7 %collective-permute-start.12 = (bf16[176,2048]{1,0:T(8,128)(2,1)S(1)}, bf16[176,2048]{1,0:T(8,128)(2,1)S(1)}, u32[]{:S(2)}, u32[]{:S(2)}) collective-permute-start(bf16[176,2048]{1,0:T(8,128)(2,1)S(1)} %collective-permute-done.5.x1), channel_id=1, source_target_pairs={{0,1},{1,0},{2,3},{3,2},{4,5},{5,4},{6,7},{7,6},{8,9},{9,8},{10,11... | collective-permute-start | bytes 2162696 | tf_op jit(solution)/shard_map/ppermute | solution.py:200
  87.3 0.8 copy-start.4
  88.1 15.4 %collective-permute-start.14 = (bf16[2,256,1024]{2,1,0:T(8,128)(2,1)}, bf16[2,256,1024]{2,1,0:T(8,128)(2,1)}, u32[]{:S(2)}, u32[]{:S(2)}) collective-permute-start(bf16[2,256,1024]{2,1,0:T(8,128)(2,1)} %pad_maximum_fusion.4), channel_id=1, source_target_pairs={{0,4},{1,3},{2,6},{3,1},{4,0},{5,7},{6,2},{7,5},{8,12},{9,11},{10,... | collective-permute-start | bytes 3145736 | tf_op jit(solution)/shard_map/ppermute | solution.py:200
  91.4 2.1 %copy-start.7 = (bf16[2,256,512]{2,1,0:T(8,128)(2,1)S(1)}, bf16[2,256,512]{2,1,0:T(8,128)(2,1)}, u32[]{:S(2)}) copy-start(bf16[2,256,512]{2,1,0:T(8,128)(2,1)} %copy-done.6) | copy-start | bytes 1572868
  91.4 2.1 %copy-start.9 = (bf16[2,256,512]{2,1,0:T(8,128)(2,1)S(1)}, bf16[2,256,512]{2,1,0:T(8,128)(2,1)}, u32[]{:S(2)}) copy-start(bf16[2,256,512]{2,1,0:T(8,128)(2,1)} %copy-done.8) | copy-start | bytes 1572868
  93.5 1.2 copy-start.13
  94.8 2.2 %copy-start.26 = (bf16[512,256]{1,0:T(8,128)(2,1)S(1)}, bf16[512,256]{1,0:T(8,128)(2,1)}, u32[]{:S(2)}) copy-start(bf16[512,256]{1,0:T(8,128)(2,1)} %copy-done.25) | copy-start | bytes 786436
  96.9 16.4 %collective-permute-start.15 = (bf16[736,256]{1,0:T(8,128)(2,1)S(1)}, bf16[736,256]{1,0:T(8,128)(2,1)S(1)}, u32[]{:S(2)}, u32[]{:S(2)}) collective-permute-start(bf16[736,256]{1,0:T(8,128)(2,1)S(1)} %get-tuple-element.74), channel_id=1, source_target_pairs={{0,16},{1,17},{2,18},{3,19},{4,20},{5,21},{6,22},{7,23},{8,24},{9,... | collective-permute-start | bytes 1130504 | tf_op jit(solution)/shard_map/ppermute | solution.py:200
  103.4 36.3 %collective-permute-start.19 = (bf16[2,1024,256]{2,1,0:T(8,128)(2,1)S(1)}, bf16[2,1024,256]{2,1,0:T(8,128)(2,1)S(1)}, u32[]{:S(2)}, u32[]{:S(2)}) collective-permute-start(bf16[2,1024,256]{2,1,0:T(8,128)(2,1)S(1)} %pad_maximum_fusion.3.w_own), channel_id=1, source_target_pairs={{0,2},{1,5},{2,0},{3,7},{4,6},{5,1},{6,4},{7,3},{8,10},{9,13},{10,... | collective-permute-start | bytes 3145736 | tf_op jit(solution)/shard_map/ppermute | solution.py:200
  105.2 1.0 copy-start.1
  105.2 1.2 copy-start.3
  105.2 1.3 copy-start.5
  114.3 27.3 %copy-start.10 = (f32[4,128,512]{2,1,0:T(8,128)S(1)}, f32[4,128,512]{2,1,0:T(8,128)}, u32[]{:S(2)}) copy-start(f32[4,128,512]{2,1,0:T(8,128)} %get-tuple-element.72.keep_ref) | copy-start | bytes 3145732
  114.3 10.6 %collective-permute-start.17 = (bf16[6,128,256]{2,1,0:T(8,128)(2,1)S(1)}, bf16[6,128,256]{2,1,0:T(8,128)(2,1)S(1)}, u32[]{:S(2)}, u32[]{:S(2)}) collective-permute-start(bf16[6,128,256]{2,1,0:T(8,128)(2,1)S(1)} %keys_join.1.kv0), channel_id=1, source_target_pairs={{0,2},{1,5},{2,0},{3,7},{4,6},{5,1},{6,4},{7,3},{8,10},{9,13},{10,... | collective-permute-start | bytes 1179656 | tf_op jit(solution)/shard_map/ppermute | solution.py:200
  114.7 25.1 %collective-permute-start.20 = (bf16[4,128,512]{2,1,0:T(8,128)(2,1)S(1)}, bf16[4,128,512]{2,1,0:T(8,128)(2,1)S(1)}, u32[]{:S(2)}, u32[]{:S(2)}) collective-permute-start(bf16[4,128,512]{2,1,0:T(8,128)(2,1)S(1)} %get-tuple-element.78), channel_id=1, source_target_pairs={{0,16},{1,17},{2,18},{3,19},{4,20},{5,21},{6,22},{7,23},{8,24},{9,... | collective-permute-start | bytes 1572872 | tf_op jit(solution)/shard_map/ppermute | solution.py:200
  118.1 9.7 %collective-permute-start.16 = (bf16[6,128,256]{2,1,0:T(8,128)(2,1)S(1)}, bf16[6,128,256]{2,1,0:T(8,128)(2,1)S(1)}, u32[]{:S(2)}, u32[]{:S(2)}) collective-permute-start(bf16[6,128,256]{2,1,0:T(8,128)(2,1)S(1)} %keys_join.1.kv0), channel_id=1, source_target_pairs={{0,4},{1,3},{2,6},{3,1},{4,0},{5,7},{6,2},{7,5},{8,12},{9,11},{10,... | collective-permute-start | bytes 1179656 | tf_op jit(solution)/shard_map/ppermute | solution.py:200
  124.9 14.8 %collective-permute-start.18 = (bf16[6,128,256]{2,1,0:T(8,128)(2,1)S(1)}, bf16[6,128,256]{2,1,0:T(8,128)(2,1)S(1)}, u32[]{:S(2)}, u32[]{:S(2)}) collective-permute-start(bf16[6,128,256]{2,1,0:T(8,128)(2,1)S(1)} %collective-permute-done.17.kv1), channel_id=1, source_target_pairs={{0,4},{1,3},{2,6},{3,1},{4,0},{5,7},{6,2},{7,5},{8,12},{9,11},{10,... | collective-permute-start | bytes 1179656 | tf_op jit(solution)/shard_map/ppermute | solution.py:200
  140.0 26.1 %collective-permute-start.22 = (bf16[4,1024,256]{2,1,0:T(8,128)(2,1)S(1)}, bf16[4,1024,256]{2,1,0:T(8,128)(2,1)S(1)}, u32[]{:S(2)}, u32[]{:S(2)}) collective-permute-start(bf16[4,1024,256]{2,1,0:T(8,128)(2,1)S(1)} %pad_maximum_fusion), channel_id=1, source_target_pairs={{0,4},{1,3},{2,6},{3,1},{4,0},{5,7},{6,2},{7,5},{8,12},{9,11},{10,... | collective-permute-start | bytes 6291464 | tf_op jit(solution)/shard_map/ppermute | solution.py:200
  150.5 14.6 %collective-permute-start.21 = (bf16[512,512]{1,0:T(8,128)(2,1)S(1)}, bf16[512,512]{1,0:T(8,128)(2,1)S(1)}, u32[]{:S(2)}, u32[]{:S(2)}) collective-permute-start(bf16[512,512]{1,0:T(8,128)(2,1)S(1)} %attend.1.own_ref), channel_id=1, source_target_pairs={{0,8},{1,9},{2,10},{3,11},{4,12},{5,13},{6,14},{7,15},{8,0},{9,1},... | collective-permute-start | bytes 1572872 | tf_op jit(solution)/shard_map/ppermute | solution.py:200
  166.1 1.3 copy-start.22
  172.5 2.7 %collective-permute-start.23 = (bf16[4,128,1024]{2,1,0:T(8,128)(2,1)S(1)}, bf16[4,128,1024]{2,1,0:T(8,128)(2,1)S(1)}, u32[]{:S(2)}, u32[]{:S(2)}) collective-permute-start(bf16[4,128,1024]{2,1,0:T(8,128)(2,1)S(1)} %get-tuple-element.84), channel_id=1, source_target_pairs={{0,1},{1,0},{2,3},{3,2},{4,5},{5,4},{6,7},{7,6},{8,9},{9,8},{10,11... | collective-permute-start | bytes 3145736 | tf_op jit(solution)/shard_map/ppermute | solution.py:200
  176.8 15.7 %collective-permute-start.26 = (bf16[128,1024]{1,0:T(8,128)(2,1)S(1)}, bf16[128,1024]{1,0:T(8,128)(2,1)S(1)}, u32[]{:S(2)}, u32[]{:S(2)}) collective-permute-start(bf16[128,1024]{1,0:T(8,128)(2,1)S(1)} %get-tuple-element.90), channel_id=1, source_target_pairs={{0,24},{1,25},{2,26},{3,27},{4,28},{5,29},{6,30},{7,31},{8,0},{9,1... | collective-permute-start | bytes 786440 | tf_op jit(solution)/shard_map/ppermute | solution.py:200
  179.3 15.1 %collective-permute-start.25 = (bf16[128,1024]{1,0:T(8,128)(2,1)S(1)}, bf16[128,1024]{1,0:T(8,128)(2,1)S(1)}, u32[]{:S(2)}, u32[]{:S(2)}) collective-permute-start(bf16[128,1024]{1,0:T(8,128)(2,1)S(1)} %get-tuple-element.91), channel_id=1, source_target_pairs={{0,8},{1,9},{2,10},{3,11},{4,12},{5,13},{6,14},{7,15},{8,16},{9,17... | collective-permute-start | bytes 786440 | tf_op jit(solution)/shard_map/ppermute | solution.py:200
  179.3 22.7 %collective-permute-start.24 = (bf16[128,1024]{1,0:T(8,128)(2,1)S(1)}, bf16[128,1024]{1,0:T(8,128)(2,1)S(1)}, u32[]{:S(2)}, u32[]{:S(2)}) collective-permute-start(bf16[128,1024]{1,0:T(8,128)(2,1)S(1)} %get-tuple-element.89), channel_id=1, source_target_pairs={{0,16},{1,17},{2,18},{3,19},{4,20},{5,21},{6,22},{7,23},{8,24},{9,... | collective-permute-start | bytes 786440 | tf_op jit(solution)/shard_map/ppermute | solution.py:200

commit v8 on v7

--- a/solution.py
+++ b/solution.py
@@ -437,7 +437,7 @@
 
 SMEM = pl.BlockSpec(memory_space=pltpu.SMEM)
 VMEM = pl.BlockSpec(memory_space=pltpu.VMEM)
-ANY = pl.BlockSpec(memory_space=pl.ANY)
+HBM = pl.BlockSpec(memory_space=pltpu.MemorySpace.HBM)
 PARAMS = pltpu.CompilerParams(vmem_limit_bytes=48 * 1024 * 1024)
 
 
@@ -473,10 +473,10 @@
     last = (stream_len - TILE_RUN) // tok
     owners = [first + i for i in range(tile_owners)] + [last + i for i in range(tile_owners)]
     assert [owner % PLANE for owner in owners] == list(range(LEVELS))
-    owner_levels = jnp.array([owner // PLANE for owner in owners], jnp.int32)
+    owner_level = jnp.where(place < tile_owners, first // PLANE, last // PLANE)
 
     first_block = jnp.where(own_first, 0, 2)
-    shown_block = (first_block + (level ^ owner_levels[place])) % LEVELS
+    shown_block = (first_block + (level ^ owner_level)) % LEVELS
     where = jnp.stack([level, place, core, first_block, shown_block]).astype(jnp.int32)
 
     slots = (recompute_slots - seq_index * CACHED).astype(jnp.bfloat16)
@@ -487,15 +487,14 @@
     key_own, query_own, key_give, query_give = pl.pallas_call(
         pack_kernel,
         out_shape=(key_shape, query_shape) * 2,
-        in_specs=[SMEM] + [ANY] * 6,
-        out_specs=(ANY,) * 4,
+        in_specs=[SMEM] + [HBM] * 6,
+        out_specs=(HBM,) * 4,
         scratch_shapes=[pltpu.SemaphoreType.DMA((PACK_COPIES,))],
         compiler_params=PARAMS,
         name="pack",
     )(where, w_query, w_key, w_value, cache_keys, cache_values, slot_rows)
     query_near = to_near(query_own)
 
-    text_rows, key_give = lax.optimization_barrier((text_rows, key_give))
     rows = jnp.concatenate(
         [text_rows, recompute_rows, jnp.zeros((REC_PAD - REC, width), text_rows.dtype)], axis=0
     )
@@ -512,31 +511,31 @@
         lax.dynamic_slice_in_dim(w_out, at * out_rows, out_rows, 0) for at in (half_at, 1 - half_at)
     )
     out_half = out_rows // 2
-    out_got0, out_got1 = across(out_give[:out_half], 2), across(out_give[out_half:], 2)
 
     crossed = permuted(normed, lambda z, p, c: (z ^ 2, p, 1 - c) if c == 1 - z // 2 else None)
-    normed, pictures, query_give = lax.optimization_barrier((normed, pictures, query_give))
     shown = permuted(pictures, lambda z, p, c: (2 * c + p // 2, z, p % 2))
+    key_next = across(key_give, 1)
+    query_far = to_far(jnp.concatenate([query_own, query_near], axis=0))
+    query_near, query_give = lax.optimization_barrier((query_near, query_give))
     query_next = across(query_give, 1)
-    key_next = across(key_give, 1)
+    shown, key_next = lax.optimization_barrier((shown, key_next))
     keys = jnp.stack([key_own[:depth], key_next[:depth]])
     old_own, old_next = key_own[depth:], key_next[depth:]
     keys_near = to_near(keys)
-    crossed, shown, keys_near, query_next = lax.optimization_barrier(
-        (crossed, shown, keys_near, query_next)
-    )
+    crossed, keys_near = lax.optimization_barrier((crossed, keys_near))
     held = jnp.concatenate([jnp.where(own_first, normed, crossed), shown], axis=0)
     next_rows = across(held, 1)
-    held_other = other_core(held)
+    held_other, out_give = lax.optimization_barrier((other_core(held), out_give))
+    out_got0 = across(out_give[:out_half], 2)
     keys_far = to_far(jnp.concatenate([keys, keys_near], axis=0))
-    query_far = to_far(jnp.concatenate([query_own, query_near], axis=0))
     next_near = to_near(query_next)
-    next_rows, held_other, keys_far, query_far, out_got0, next_near = lax.optimization_barrier(
-        (next_rows, held_other, keys_far, query_far, out_got0, next_near)
-    )
+    next_rows, held_other, keys_far, query_far, next_near, out_got0, out_give = (
+        lax.optimization_barrier(
+            (next_rows, held_other, keys_far, query_far, next_near, out_got0, out_give)
+        )
+    )
+    out_got1 = across(out_give[out_half:], 2)
     next_other = other_core(next_rows)
-    next_other, out_got1 = lax.optimization_barrier((next_other, out_got1))
-    next_far = to_far(jnp.concatenate([query_next, next_near], axis=0))
     parts = (held, next_rows, held_other, next_other)
 
     half = HD // 2
@@ -564,10 +563,8 @@
         compiler_params=PARAMS,
         name="keys_part",
     )(where, *parts, keys, keys_near, keys_far, old_own, old_next)
-    send, *parts = lax.optimization_barrier((send, *parts))
-    out_pair = jnp.stack([out_own, jnp.concatenate([out_got0, out_got1], axis=0)])
-    out_pair, next_far = lax.optimization_barrier((out_pair, next_far))
-    out_near = to_near(out_pair)
+    send, next_near, *parts = lax.optimization_barrier((send, next_near, *parts))
+    next_far = to_far(jnp.concatenate([query_next, next_near], axis=0))
     q_keep, q_send = pl.pallas_call(
         queries_part_kernel,
         out_shape=(
@@ -580,7 +577,7 @@
         compiler_params=PARAMS,
         name="queries_part",
     )(where, *parts, query_own, query_near, query_far, query_next, next_near, next_far)
-    got_keys, q_send = lax.optimization_barrier((across(send, 2), q_send))
+    got_keys, q_send, out_got1 = lax.optimization_barrier((across(send, 2), q_send, out_got1))
     kv = pl.pallas_call(
         keys_join_kernel,
         out_shape=shaped((LEVELS // 2 + LEVELS, tok, 2 * HD)),
@@ -591,8 +588,11 @@
         name="keys_join",
     )(where, keep, got_keys, old_own, old_next, cosine, sine)
     kv_near, kv_far = to_near(kv), to_far(kv)
-    kv_both = to_far(kv_near)
-
+    kv_both = permuted(kv, lambda z, p, c: (z, p ^ 3, c))
+
+    out_pair = jnp.stack([out_own, jnp.concatenate([out_got0, out_got1], axis=0)])
+    out_pair, kv_near, kv_far = lax.optimization_barrier((out_pair, kv_near, kv_far))
+    out_near = to_near(out_pair)
     kv_far, kv_both, out_near, got_queries = lax.optimization_barrier(
         (kv_far, kv_both, out_near, across(q_send, 2))
     )

time: 208 us -> 213 us (1.024)
  waiting for transfers between devices: 88.1 us -> 120 us
  starting transfers between devices: 57 us -> 37.5 us
  local copies, waits for them, and re-layouts: 17.2 us -> 10.3 us
    ppermute x27, waiting for transfers between devices: 88.1 us -> 120 us  [permuted(): return lax.ppermute(value, ('seq', 'head'), perm)]
    ppermute x27, starting transfers between devices: 57 us -> 37.5 us  [permuted(): return lax.ppermute(value, ('seq', 'head'), perm)]
    unnamed x58 -> x40, local copies, waits for them, and re-layouts: 9.92 us -> 7 us
  transfers between devices with their start and end apart: 27 -> 27, of which waited for: 14 -> 18; matrix products, arithmetic and copies ran while one was open for 7% -> 4% of each run, Pallas kernels for 8% -> 7%
where the time goes in v8:
time: 213 us; the launch traced here: 211 us
  waiting for transfers between devices  120 us (56%)
  starting transfers between devices  37.5 us (18%)
  Pallas kernels  24.4 us (11%)
  other arithmetic  15.6 us (7%)
  local copies, waits for them, and re-layouts  10.3 us (5%)
  blocking collectives  3.02 us (1%)
    ppermute x27, waiting for transfers between devices, permuted(): return lax.ppermute(value, ('seq', 'head'), perm)  120 us
    ppermute x27, starting transfers between devices, permuted(): return lax.ppermute(value, ('seq', 'head'), perm)  37.5 us
    pallas_call x1, Pallas kernels, by_levels(): pl.pallas_call(attend_kernel, out_shape=shaped((LEVELS * tok, 4 * HD)), i...  8.96 us
    unnamed x40, local copies, waits for them, and re-layouts  7 us
    pallas_call x1, Pallas kernels, by_levels(): pl.pallas_call(queries_part_kernel, out_shape=(shaped((LEVELS, tok, 4 * H...  5.49 us
    pallas_call x1, Pallas kernels, by_levels(): pl.pallas_call(output_kernel, out_shape=(shaped((LEVELS, tok, wide_cols),...  5.07 us
  transfers between devices with their start and end apart: 27, of which 18 were waited for; matrix products, arithmetic and copies ran while one was open for 4% of the time, Pallas kernels for 7%

profile of v8, /device:TPU:8, one launch (start us, length us, event | category | flops | bytes accessed | tf_op | source)
XLA Modules:
  0.0 211.1 jit_solution(7171019979423449556)
XLA Ops:
  0.0 1.1 fusion.4
  1.2 0.5 copy-done.17
  1.7 1.4 fusion
  3.1 3.0 %all-reduce.1 = (f32[32]{0:T(128)S(1)}, f32[144]{0:T(256)}) all-reduce(f32[32]{0:T(128)S(1)} %fusion.4, f32[144]{0:T(256)S(1)} %fusion), channel_id=1, replica_groups=mesh['seq'=16,'head'=2] {'head'}, use_global_device_ids=true, to_apply=%region_3.4 | all-reduce | flops 176 | bytes 1408 | tf_op jit(solution)/shard_map/psum | solution.py:503
  6.1 0.7 dynamic_slice.9
  6.8 1.0 fusion.6
  7.8 3.3 %collective-permute-start.1 = (bf16[32,2048]{1,0:T(8,128)(2,1)S(1)}, bf16[32,2048]{1,0:T(8,128)(2,1)}, u32[]{:S(2)}, u32[]{:S(2)}) collective-permute-start(bf16[32,2048]{1,0:T(8,128)(2,1)S(1)} %fusion.6), channel_id=1, source_target_pairs={{0,0},{1,16},{2,1},{3,17},{4,8},{5,24},{6,9},{7,25},{8,2},{9,18},{... | collective-permute-start | bytes 393224 | tf_op jit(solution)/shard_map/ppermute | solution.py:200
  11.2 0.7 subtract_convert_fusion
  12.0 0.9 copy-done.6
  13.0 0.9 copy-done.7
  13.9 0.8 copy-done.9
  14.8 1.0 pack.1
  16.4 0.7 collective-permute-start
  17.1 0.6 collective-permute-start.7
  17.7 10.6 %collective-permute-done.2 = bf16[336,512]{1,0:T(8,128)(2,1)S(1)} collective-permute-done((bf16[336,512]{1,0:T(8,128)(2,1)S(1)}, bf16[336,512]{1,0:T(8,128)(2,1)S(1)}, u32[]{:S(2)}, u32[]{:S(2)}) %collective-permute-start.2) | collective-permute-done | bytes 344096 | tf_op jit(solution)/shard_map/ppermute | solution.py:200
  28.4 0.6 copy-done.15
  29.0 0.8 copy-done
  29.8 1.1 pad_maximum_fusion.2
  30.9 0.6 collective-permute-start.8
  31.4 2.6 %collective-permute-start.9 = (bf16[1,256,1024]{2,1,0:T(8,128)(2,1)S(1)}, bf16[1,256,1024]{2,1,0:T(8,128)(2,1)}, u32[]{:S(2)}, u32[]{:S(2)}) collective-permute-start(bf16[1,256,1024]{2,1,0:T(8,128)(2,1)S(1)} %get-tuple-element.55), channel_id=1, source_target_pairs={{0,8},{1,9},{2,10},{3,11},{4,12},{5,13},{6,14},{7,15},{8,0},{9,1},... | collective-permute-start | bytes 1572872 | tf_op jit(solution)/shard_map/ppermute | solution.py:200
  34.1 6.8 %collective-permute-done.3.near = bf16[2,256,512]{2,1,0:T(8,128)(2,1)S(1)} collective-permute-done((bf16[2,256,512]{2,1,0:T(8,128)(2,1)S(1)}, bf16[2,256,512]{2,1,0:T(8,128)(2,1)S(1)}, u32[]{:S(2)}, u32[]{:S(2)}) %collective-permute-start.3) | collective-permute-done | bytes 524320 | tf_op jit(solution)/shard_map/ppermute | solution.py:200
  40.9 0.5 broadcast_select_fusion
  41.4 1.1 pad_maximum_fusion.1
  42.5 1.0 pad_maximum_fusion.5.x0
  43.5 2.8 %collective-permute-start.4 = (bf16[176,2048]{1,0:T(8,128)(2,1)S(1)}, bf16[176,2048]{1,0:T(8,128)(2,1)S(1)}, u32[]{:S(2)}, u32[]{:S(2)}) collective-permute-start(bf16[176,2048]{1,0:T(8,128)(2,1)S(1)} %pad_maximum_fusion.5.x0), channel_id=1, source_target_pairs={{0,8},{1,9},{2,10},{3,11},{4,12},{5,13},{6,14},{7,15},{8,0},{9,1},... | collective-permute-start | bytes 2162696 | tf_op jit(solution)/shard_map/ppermute | solution.py:200
  46.7 0.8 collective-permute-start.10
  47.5 1.4 dynamic-slice_bitcast_fusion
  48.9 4.5 %collective-permute-start.11 = (bf16[512,256]{1,0:T(8,128)(2,1)S(1)}, bf16[512,256]{1,0:T(8,128)(2,1)S(1)}, u32[]{:S(2)}, u32[]{:S(2)}) collective-permute-start(bf16[512,256]{1,0:T(8,128)(2,1)S(1)} %slice.44), channel_id=1, source_target_pairs={{0,16},{1,17},{2,18},{3,19},{4,20},{5,21},{6,22},{7,23},{8,24},{9,... | collective-permute-start | bytes 786440 | tf_op jit(solution)/shard_map/ppermute | solution.py:200
  53.4 8.5 %collective-permute-done.10.refs_4_ = bf16[1,256,1024]{2,1,0:T(8,128)(2,1)} collective-permute-done((bf16[1,256,1024]{2,1,0:T(8,128)(2,1)}, bf16[1,256,1024]{2,1,0:T(8,128)(2,1)}, u32[]{:S(2)}, u32[]{:S(2)}) %collective-permute-start.10) | collective-permute-done | bytes 524320 | tf_op jit(solution)/shard_map/ppermute | solution.py:200
  61.9 6.1 %collective-permute-done.4.x1 = bf16[176,2048]{1,0:T(8,128)(2,1)S(1)} collective-permute-done((bf16[176,2048]{1,0:T(8,128)(2,1)S(1)}, bf16[176,2048]{1,0:T(8,128)(2,1)S(1)}, u32[]{:S(2)}, u32[]{:S(2)}) %collective-permute-start.4) | collective-permute-done | bytes 720928 | tf_op jit(solution)/shard_map/ppermute | solution.py:200
  68.0 5.6 %collective-permute-done.11 = bf16[512,256]{1,0:T(8,128)(2,1)S(1)} collective-permute-done((bf16[512,256]{1,0:T(8,128)(2,1)S(1)}, bf16[512,256]{1,0:T(8,128)(2,1)S(1)}, u32[]{:S(2)}, u32[]{:S(2)}) %collective-permute-start.11) | collective-permute-done | bytes 262176 | tf_op jit(solution)/shard_map/ppermute | solution.py:200
  73.6 0.9 slice.46.old1
  74.5 1.3 collective-permute-done.12.x3
  75.8 2.8 %keys_part.1 = (f32[576,256]{1,0:T(8,128)S(1)}, bf16[736,256]{1,0:T(8,128)(2,1)S(1)}) custom-call(s32[5]{0:T(128)S(1)} %copy-done.11, bf16[176,2048]{1,0:T(8,128)(2,1)S(1)} %pad_maximum_fusion.5.x0, bf16[176,2048]{1,0:T(8,128)(2,1)S(1)} %collective-permute-done.4.x1, bf16[176,2048]{1,0:T(8,128)(2,1)S(1)} %collective-permute-done.5.x2, ...), custom_call_target="tpu_custom_call" | custom-call | tf_op jit(solution)/shard_map/keys_part/pallas_call | solution.py:554
  78.6 1.3 pad_maximum_fusion.3
  80.1 1.8 collective-permute-start.15
  82.0 1.2 collective-permute-start.14
  83.1 1.4 fusion.10
  84.9 9.8 %collective-permute-done.13.refs_5_ = bf16[2,256,1024]{2,1,0:T(8,128)(2,1)S(1)} collective-permute-done((bf16[2,256,1024]{2,1,0:T(8,128)(2,1)S(1)}, bf16[2,256,1024]{2,1,0:T(8,128)(2,1)S(1)}, u32[]{:S(2)}, u32[]{:S(2)}) %collective-permute-start.13) | collective-permute-done | bytes 1048608 | tf_op jit(solution)/shard_map/ppermute | solution.py:200
  94.7 1.0 copy-done.14
  95.7 5.5 %queries_part.1 = (f32[4,128,512]{2,1,0:T(8,128)}, bf16[4,128,512]{2,1,0:T(8,128)(2,1)S(1)}) custom-call(s32[5]{0:T(128)S(1)} %copy-done.11, bf16[176,2048]{1,0:T(8,128)(2,1)S(1)} %pad_maximum_fusion.5.x0, bf16[176,2048]{1,0:T(8,128)(2,1)S(1)} %collective-permute-done.4.x1, bf16[176,2048]{1,0:T(8,128)(2,1)S(1)} %collective-permute-done.5.x2, ...), custom_call_target="tpu_custom_call" | custom-call | tf_op jit(solution)/shard_map/queries_part/pallas_call | solution.py:568
  101.2 7.3 %collective-permute-done.14.got_ref = bf16[736,256]{1,0:T(8,128)(2,1)S(1)} collective-permute-done((bf16[736,256]{1,0:T(8,128)(2,1)S(1)}, bf16[736,256]{1,0:T(8,128)(2,1)S(1)}, u32[]{:S(2)}, u32[]{:S(2)}) %collective-permute-start.14) | collective-permute-done | bytes 376864 | tf_op jit(solution)/shard_map/ppermute | solution.py:200
  108.6 1.0 keys_join.1.kv0
  109.6 0.5 collective-permute-start.16
  110.1 1.3 collective-permute-start.17
  111.6 9.2 %collective-permute-done.16.kv1 = bf16[6,128,256]{2,1,0:T(8,128)(2,1)S(1)} collective-permute-done((bf16[6,128,256]{2,1,0:T(8,128)(2,1)S(1)}, bf16[6,128,256]{2,1,0:T(8,128)(2,1)S(1)}, u32[]{:S(2)}, u32[]{:S(2)}) %collective-permute-start.16) | collective-permute-done | bytes 393248 | tf_op jit(solution)/shard_map/ppermute | solution.py:200
  120.8 1.2 collective-permute-start.19
  122.0 3.4 %collective-permute-start.20 = (bf16[4,128,512]{2,1,0:T(8,128)(2,1)S(1)}, bf16[4,128,512]{2,1,0:T(8,128)(2,1)S(1)}, u32[]{:S(2)}, u32[]{:S(2)}) collective-permute-start(bf16[4,128,512]{2,1,0:T(8,128)(2,1)S(1)} %get-tuple-element.79), channel_id=1, source_target_pairs={{0,16},{1,17},{2,18},{3,19},{4,20},{5,21},{6,22},{7,23},{8,24},{9,... | collective-permute-start | bytes 1572872 | tf_op jit(solution)/shard_map/ppermute | solution.py:200
  125.9 18.0 %collective-permute-done.18.kv3 = bf16[6,128,256]{2,1,0:T(8,128)(2,1)S(1)} collective-permute-done((bf16[6,128,256]{2,1,0:T(8,128)(2,1)S(1)}, bf16[6,128,256]{2,1,0:T(8,128)(2,1)S(1)}, u32[]{:S(2)}, u32[]{:S(2)}) %collective-permute-start.18) | collective-permute-done | bytes 393248 | tf_op jit(solution)/shard_map/ppermute | solution.py:200
  143.8 1.6 collective-permute-done.20.got_ref
  146.1 9.0 %attend.1.own_ref = bf16[512,512]{1,0:T(8,128)(2,1)S(1)} custom-call(s32[5]{0:T(128)S(1)} %copy-done.11, f32[4,128,512]{2,1,0:T(8,128)S(1)} %copy-done.4, bf16[4,128,512]{2,1,0:T(8,128)(2,1)S(1)} %collective-permute-done.20.got_ref, f32[4,192,128]{2,1,0:T(8,128)S(1)} %pad_maximum_fusion.8.cos_ref, f32[4,192,128]{2,1,0:T(8,128)S(1)} %pad_maximum_fusion.9.sin_ref, ...), custom_call_target="tpu_custom_call" | custom-call | tf_op jit(solution)/shard_map/attend/pallas_call | solution.py:601
  155.1 3.7 %collective-permute-start.21 = (bf16[512,512]{1,0:T(8,128)(2,1)S(1)}, bf16[512,512]{1,0:T(8,128)(2,1)S(1)}, u32[]{:S(2)}, u32[]{:S(2)}) collective-permute-start(bf16[512,512]{1,0:T(8,128)(2,1)S(1)} %attend.1.own_ref), channel_id=1, source_target_pairs={{0,8},{1,9},{2,10},{3,11},{4,12},{5,13},{6,14},{7,15},{8,0},{9,1},... | collective-permute-start | bytes 1572872 | tf_op jit(solution)/shard_map/ppermute | solution.py:200
  158.8 12.5 %collective-permute-done.21.next_ref = bf16[512,512]{1,0:T(8,128)(2,1)S(1)} collective-permute-done((bf16[512,512]{1,0:T(8,128)(2,1)S(1)}, bf16[512,512]{1,0:T(8,128)(2,1)S(1)}, u32[]{:S(2)}, u32[]{:S(2)}) %collective-permute-start.21) | collective-permute-done | bytes 524320 | tf_op jit(solution)/shard_map/ppermute | solution.py:200
  171.7 1.3 copy-done.13
  173.1 5.1 %output.1 = (f32[4,128,1024]{2,1,0:T(8,128)}, bf16[4,128,1024]{2,1,0:T(8,128)(2,1)S(1)}) custom-call(s32[5]{0:T(128)S(1)} %copy-done.11, bf16[512,512]{1,0:T(8,128)(2,1)S(1)} %attend.1.own_ref, bf16[512,512]{1,0:T(8,128)(2,1)S(1)} %collective-permute-done.21.next_ref, bf16[2,1024,256]{2,1,0:T(8,128)(2,1)S(1)} %pad_maximum_fusion.4.w_own, ...), custom_call_target="tpu_custom_call" | custom-call | tf_op jit(solution)/shard_map/output/pallas_call | solution.py:612
  178.2 2.7 %collective-permute-done.23 = bf16[4,128,1024]{2,1,0:T(8,128)(2,1)S(1)} collective-permute-done((bf16[4,128,1024]{2,1,0:T(8,128)(2,1)S(1)}, bf16[4,128,1024]{2,1,0:T(8,128)(2,1)S(1)}, u32[]{:S(2)}, u32[]{:S(2)}) %collective-permute-start.23) | collective-permute-done | bytes 1048608 | tf_op jit(solution)/shard_map/ppermute | solution.py:200
  180.8 1.6 fusion.7
  182.4 3.7 %collective-permute-start.26 = (bf16[128,1024]{1,0:T(8,128)(2,1)S(1)}, bf16[128,1024]{1,0:T(8,128)(2,1)S(1)}, u32[]{:S(2)}, u32[]{:S(2)}) collective-permute-start(bf16[128,1024]{1,0:T(8,128)(2,1)S(1)} %get-tuple-element.92), channel_id=1, source_target_pairs={{0,24},{1,25},{2,26},{3,27},{4,28},{5,29},{6,30},{7,31},{8,0},{9,1... | collective-permute-start | bytes 786440 | tf_op jit(solution)/shard_map/ppermute | solution.py:200
  186.1 3.5 %collective-permute-start.24 = (bf16[128,1024]{1,0:T(8,128)(2,1)S(1)}, bf16[128,1024]{1,0:T(8,128)(2,1)S(1)}, u32[]{:S(2)}, u32[]{:S(2)}) collective-permute-start(bf16[128,1024]{1,0:T(8,128)(2,1)S(1)} %get-tuple-element.91), channel_id=1, source_target_pairs={{0,16},{1,17},{2,18},{3,19},{4,20},{5,21},{6,22},{7,23},{8,24},{9,... | collective-permute-start | bytes 786440 | tf_op jit(solution)/shard_map/ppermute | solution.py:200
  189.7 9.5 %collective-permute-done.26 = bf16[128,1024]{1,0:T(8,128)(2,1)S(1)} collective-permute-done((bf16[128,1024]{1,0:T(8,128)(2,1)S(1)}, bf16[128,1024]{1,0:T(8,128)(2,1)S(1)}, u32[]{:S(2)}, u32[]{:S(2)}) %collective-permute-start.26) | collective-permute-done | bytes 262176 | tf_op jit(solution)/shard_map/ppermute | solution.py:200
  199.2 0.9 collective-permute-done.25
  200.1 8.8 %collective-permute-done.24 = bf16[128,1024]{1,0:T(8,128)(2,1)S(1)} collective-permute-done((bf16[128,1024]{1,0:T(8,128)(2,1)S(1)}, bf16[128,1024]{1,0:T(8,128)(2,1)S(1)}, u32[]{:S(2)}, u32[]{:S(2)}) %collective-permute-start.24) | collective-permute-done | bytes 262176 | tf_op jit(solution)/shard_map/ppermute | solution.py:200
  208.9 1.2 broadcast_select_fusion.2
  210.3 0.8 pad_maximum_fusion.7
  (78 shorter events, 3.8 us)
Async XLA Ops:
  0.0 12.0 %copy-start.5 = (bf16[256,2048]{1,0:T(8,128)(2,1)S(1)}, bf16[256,2048]{1,0:T(8,128)(2,1)}, u32[]{:S(2)}) copy-start(bf16[256,2048]{1,0:T(8,128)(2,1)} %refs_0_.1) | copy-start | bytes 3145732
  0.0 12.0 %copy-start.8 = (bf16[64,512]{1,0:T(8,128)(2,1)S(1)}, bf16[64,512]{1,0:T(8,128)(2,1)}, u32[]{:S(2)}) copy-start(bf16[64,512]{1,0:T(8,128)(2,1)} %refs_3_.1) | copy-start | bytes 196612
  1.2 0.5 copy-start.17
  7.8 9.9 %collective-permute-start.1 = (bf16[32,2048]{1,0:T(8,128)(2,1)S(1)}, bf16[32,2048]{1,0:T(8,128)(2,1)}, u32[]{:S(2)}, u32[]{:S(2)}) collective-permute-start(bf16[32,2048]{1,0:T(8,128)(2,1)S(1)} %fusion.6), channel_id=1, source_target_pairs={{0,0},{1,16},{2,1},{3,17},{4,8},{5,24},{6,9},{7,25},{8,2},{9,18},{... | collective-permute-start | bytes 393224 | tf_op jit(solution)/shard_map/ppermute | solution.py:200
  11.9 4.4 %copy-start.10 = (s32[5]{0:T(128)}, s32[5]{0:T(128)S(1)}, u32[]{:S(2)}) copy-start(s32[5]{0:T(128)S(1)} %stack.41.where_ref) | copy-start | bytes 64
  11.9 4.0 %copy-start.19 = (f32[144]{0:T(256)S(1)}, f32[144]{0:T(256)}, u32[]{:S(2)}) copy-start(f32[144]{0:T(256)} %get-tuple-element.88) | copy-start | bytes 1732
  11.9 4.0 %copy-start.18 = (bf16[144]{0:T(256)(128)(2,1)S(1)}, bf16[144]{0:T(256)(128)(2,1)}, u32[]{:S(2)}) copy-start(bf16[144]{0:T(256)(128)(2,1)} %copy-done.17) | copy-start | bytes 868
  12.0 1.0 copy-start.6
  13.0 0.9 copy-start.7
  13.9 0.8 copy-start.9
  14.8 1.2 copy-start.12
  14.8 1.2 copy-start.16
  15.8 12.4 %collective-permute-start.2 = (bf16[336,512]{1,0:T(8,128)(2,1)S(1)}, bf16[336,512]{1,0:T(8,128)(2,1)S(1)}, u32[]{:S(2)}, u32[]{:S(2)}) collective-permute-start(bf16[336,512]{1,0:T(8,128)(2,1)S(1)} %get-tuple-element.47), channel_id=1, source_target_pairs={{0,8},{1,9},{2,10},{3,11},{4,12},{5,13},{6,14},{7,15},{8,0},{9,1},... | collective-permute-start | bytes 1032200 | tf_op jit(solution)/shard_map/ppermute | solution.py:200
  16.4 17.7 %collective-permute-start = (bf16[144,2048]{1,0:T(8,128)(2,1)S(1)}, bf16[144,2048]{1,0:T(8,128)(2,1)S(1)}, u32[]{:S(2)}, u32[]{:S(2)}) collective-permute-start(bf16[144,2048]{1,0:T(8,128)(2,1)S(1)} %fusion.2), channel_id=1, source_target_pairs={{1,16},{3,18},{5,20},{7,22},{9,24},{11,26},{13,28},{15,30},{16,1},... | collective-permute-start | bytes 1769480 | tf_op jit(solution)/shard_map/ppermute | solution.py:200
  17.1 12.7 %collective-permute-start.7 = (bf16[1,256,1024]{2,1,0:T(8,128)(2,1)S(1)}, bf16[1,256,1024]{2,1,0:T(8,128)(2,1)S(1)}, u32[]{:S(2)}, u32[]{:S(2)}) collective-permute-start(bf16[1,256,1024]{2,1,0:T(8,128)(2,1)S(1)} %get-tuple-element.53.refs_0_), channel_id=1, source_target_pairs={{0,2},{1,5},{2,0},{3,7},{4,6},{5,1},{6,4},{7,3},{8,10},{9,13},{10,... | collective-permute-start | bytes 1572872 | tf_op jit(solution)/shard_map/ppermute | solution.py:200
  28.3 0.7 copy-start.15
  28.3 12.5 %collective-permute-start.3 = (bf16[2,256,512]{2,1,0:T(8,128)(2,1)S(1)}, bf16[2,256,512]{2,1,0:T(8,128)(2,1)S(1)}, u32[]{:S(2)}, u32[]{:S(2)}) collective-permute-start(bf16[2,256,512]{2,1,0:T(8,128)(2,1)S(1)} %pad_maximum_fusion.6.own), channel_id=1, source_target_pairs={{0,2},{1,5},{2,0},{3,7},{4,6},{5,1},{6,4},{7,3},{8,10},{9,13},{10,... | collective-permute-start | bytes 1572872 | tf_op jit(solution)/shard_map/ppermute | solution.py:200
  29.0 0.8 copy-start
  30.9 22.6 %collective-permute-start.8 = (bf16[2,256,1024]{2,1,0:T(8,128)(2,1)}, bf16[2,256,1024]{2,1,0:T(8,128)(2,1)}, u32[]{:S(2)}, u32[]{:S(2)}) collective-permute-start(bf16[2,256,1024]{2,1,0:T(8,128)(2,1)} %pad_maximum_fusion.2), channel_id=1, source_target_pairs={{0,4},{1,3},{2,6},{3,1},{4,0},{5,7},{6,2},{7,5},{8,12},{9,11},{10,... | collective-permute-start | bytes 3145736 | tf_op jit(solution)/shard_map/ppermute | solution.py:200
  31.4 15.3 %collective-permute-start.9 = (bf16[1,256,1024]{2,1,0:T(8,128)(2,1)S(1)}, bf16[1,256,1024]{2,1,0:T(8,128)(2,1)}, u32[]{:S(2)}, u32[]{:S(2)}) collective-permute-start(bf16[1,256,1024]{2,1,0:T(8,128)(2,1)S(1)} %get-tuple-element.55), channel_id=1, source_target_pairs={{0,8},{1,9},{2,10},{3,11},{4,12},{5,13},{6,14},{7,15},{8,0},{9,1},... | collective-permute-start | bytes 1572872 | tf_op jit(solution)/shard_map/ppermute | solution.py:200
  40.9 1.6 copy-start.2
  42.5 31.1 %collective-permute-start.6 = (bf16[4,256,512]{2,1,0:T(8,128)(2,1)}, bf16[4,256,512]{2,1,0:T(8,128)(2,1)}, u32[]{:S(2)}, u32[]{:S(2)}) collective-permute-start(bf16[4,256,512]{2,1,0:T(8,128)(2,1)} %pad_maximum_fusion.1), channel_id=1, source_target_pairs={{0,4},{1,3},{2,6},{3,1},{4,0},{5,7},{6,2},{7,5},{8,12},{9,11},{10,... | collective-permute-start | bytes 3145736 | tf_op jit(solution)/shard_map/ppermute | solution.py:200
  43.4 5.5 %collective-permute-start.5 = (bf16[176,2048]{1,0:T(8,128)(2,1)S(1)}, bf16[176,2048]{1,0:T(8,128)(2,1)S(1)}, u32[]{:S(2)}, u32[]{:S(2)}) collective-permute-start(bf16[176,2048]{1,0:T(8,128)(2,1)S(1)} %pad_maximum_fusion.5.x0), channel_id=1, source_target_pairs={{0,1},{1,0},{2,3},{3,2},{4,5},{5,4},{6,7},{7,6},{8,9},{9,8},{10,11... | collective-permute-start | bytes 2162696 | tf_op jit(solution)/shard_map/ppermute | solution.py:200
  43.5 24.5 %collective-permute-start.4 = (bf16[176,2048]{1,0:T(8,128)(2,1)S(1)}, bf16[176,2048]{1,0:T(8,128)(2,1)S(1)}, u32[]{:S(2)}, u32[]{:S(2)}) collective-permute-start(bf16[176,2048]{1,0:T(8,128)(2,1)S(1)} %pad_maximum_fusion.5.x0), channel_id=1, source_target_pairs={{0,8},{1,9},{2,10},{3,11},{4,12},{5,13},{6,14},{7,15},{8,0},{9,1},... | collective-permute-start | bytes 2162696 | tf_op jit(solution)/shard_map/ppermute | solution.py:200
  46.7 15.2 %collective-permute-start.10 = (bf16[1,256,1024]{2,1,0:T(8,128)(2,1)}, bf16[1,256,1024]{2,1,0:T(8,128)(2,1)}, u32[]{:S(2)}, u32[]{:S(2)}) collective-permute-start(bf16[1,256,1024]{2,1,0:T(8,128)(2,1)} %collective-permute-done.9.refs_3_), channel_id=1, source_target_pairs={{0,2},{1,5},{2,0},{3,7},{4,6},{5,1},{6,4},{7,3},{8,10},{9,13},{10,... | collective-permute-start | bytes 1572872 | tf_op jit(solution)/shard_map/ppermute | solution.py:200
  47.5 28.2 %copy-start.1 = (bf16[2,256,512]{2,1,0:T(8,128)(2,1)S(1)}, bf16[2,256,512]{2,1,0:T(8,128)(2,1)}, u32[]{:S(2)}) copy-start(bf16[2,256,512]{2,1,0:T(8,128)(2,1)} %copy-done) | copy-start | bytes 1572868
  47.5 28.2 %copy-start.3 = (bf16[2,256,512]{2,1,0:T(8,128)(2,1)S(1)}, bf16[2,256,512]{2,1,0:T(8,128)(2,1)}, u32[]{:S(2)}) copy-start(bf16[2,256,512]{2,1,0:T(8,128)(2,1)} %copy-done.2) | copy-start | bytes 1572868
  47.5 28.2 %copy-start.11 = (s32[5]{0:T(128)S(1)}, s32[5]{0:T(128)}, u32[]{:S(2)}) copy-start(s32[5]{0:T(128)} %copy-done.10) | copy-start | bytes 64
  48.9 24.6 %collective-permute-start.11 = (bf16[512,256]{1,0:T(8,128)(2,1)S(1)}, bf16[512,256]{1,0:T(8,128)(2,1)S(1)}, u32[]{:S(2)}, u32[]{:S(2)}) collective-permute-start(bf16[512,256]{1,0:T(8,128)(2,1)S(1)} %slice.44), channel_id=1, source_target_pairs={{0,16},{1,17},{2,18},{3,19},{4,20},{5,21},{6,22},{7,23},{8,24},{9,... | collective-permute-start | bytes 786440 | tf_op jit(solution)/shard_map/ppermute | solution.py:200
  73.6 2.2 %collective-permute-start.12 = (bf16[176,2048]{1,0:T(8,128)(2,1)S(1)}, bf16[176,2048]{1,0:T(8,128)(2,1)S(1)}, u32[]{:S(2)}, u32[]{:S(2)}) collective-permute-start(bf16[176,2048]{1,0:T(8,128)(2,1)S(1)} %collective-permute-done.4.x1), channel_id=1, source_target_pairs={{0,1},{1,0},{2,3},{3,2},{4,5},{5,4},{6,7},{7,6},{8,9},{9,8},{10,11... | collective-permute-start | bytes 2162696 | tf_op jit(solution)/shard_map/ppermute | solution.py:200
  79.9 14.9 %collective-permute-start.13 = (bf16[2,256,1024]{2,1,0:T(8,128)(2,1)S(1)}, bf16[2,256,1024]{2,1,0:T(8,128)(2,1)S(1)}, u32[]{:S(2)}, u32[]{:S(2)}) collective-permute-start(bf16[2,256,1024]{2,1,0:T(8,128)(2,1)S(1)} %pad_maximum_fusion.3), channel_id=1, source_target_pairs={{0,4},{1,3},{2,6},{3,1},{4,0},{5,7},{6,2},{7,5},{8,12},{9,11},{10,... | collective-permute-start | bytes 3145736 | tf_op jit(solution)/shard_map/ppermute | solution.py:200
  80.1 21.1 %collective-permute-start.15 = (bf16[512,256]{1,0:T(8,128)(2,1)S(1)}, bf16[512,256]{1,0:T(8,128)(2,1)S(1)}, u32[]{:S(2)}, u32[]{:S(2)}) collective-permute-start(bf16[512,256]{1,0:T(8,128)(2,1)S(1)} %slice.47), channel_id=1, source_target_pairs={{0,16},{1,17},{2,18},{3,19},{4,20},{5,21},{6,22},{7,23},{8,24},{9,... | collective-permute-start | bytes 786440 | tf_op jit(solution)/shard_map/ppermute | solution.py:200
  82.0 26.6 %collective-permute-start.14 = (bf16[736,256]{1,0:T(8,128)(2,1)S(1)}, bf16[736,256]{1,0:T(8,128)(2,1)S(1)}, u32[]{:S(2)}, u32[]{:S(2)}) collective-permute-start(bf16[736,256]{1,0:T(8,128)(2,1)S(1)} %get-tuple-element.71), channel_id=1, source_target_pairs={{0,16},{1,17},{2,18},{3,19},{4,20},{5,21},{6,22},{7,23},{8,24},{9,... | collective-permute-start | bytes 1130504 | tf_op jit(solution)/shard_map/ppermute | solution.py:200
  94.7 1.0 copy-start.14
  109.6 11.2 %collective-permute-start.16 = (bf16[6,128,256]{2,1,0:T(8,128)(2,1)S(1)}, bf16[6,128,256]{2,1,0:T(8,128)(2,1)S(1)}, u32[]{:S(2)}, u32[]{:S(2)}) collective-permute-start(bf16[6,128,256]{2,1,0:T(8,128)(2,1)S(1)} %keys_join.1.kv0), channel_id=1, source_target_pairs={{0,2},{1,5},{2,0},{3,7},{4,6},{5,1},{6,4},{7,3},{8,10},{9,13},{10,... | collective-permute-start | bytes 1179656 | tf_op jit(solution)/shard_map/ppermute | solution.py:200
  110.1 10.7 %collective-permute-start.17 = (bf16[6,128,256]{2,1,0:T(8,128)(2,1)S(1)}, bf16[6,128,256]{2,1,0:T(8,128)(2,1)S(1)}, u32[]{:S(2)}, u32[]{:S(2)}) collective-permute-start(bf16[6,128,256]{2,1,0:T(8,128)(2,1)S(1)} %keys_join.1.kv0), channel_id=1, source_target_pairs={{0,4},{1,3},{2,6},{3,1},{4,0},{5,7},{6,2},{7,5},{8,12},{9,11},{10,... | collective-permute-start | bytes 1179656 | tf_op jit(solution)/shard_map/ppermute | solution.py:200
  111.6 34.5 %copy-start.4 = (f32[4,128,512]{2,1,0:T(8,128)S(1)}, f32[4,128,512]{2,1,0:T(8,128)}, u32[]{:S(2)}) copy-start(f32[4,128,512]{2,1,0:T(8,128)} %get-tuple-element.69.keep_ref) | copy-start | bytes 3145732
  120.8 24.6 %collective-permute-start.19 = (bf16[2,1024,256]{2,1,0:T(8,128)(2,1)S(1)}, bf16[2,1024,256]{2,1,0:T(8,128)(2,1)S(1)}, u32[]{:S(2)}, u32[]{:S(2)}) collective-permute-start(bf16[2,1024,256]{2,1,0:T(8,128)(2,1)S(1)} %pad_maximum_fusion.4.w_own), channel_id=1, source_target_pairs={{0,2},{1,5},{2,0},{3,7},{4,6},{5,1},{6,4},{7,3},{8,10},{9,13},{10,... | collective-permute-start | bytes 3145736 | tf_op jit(solution)/shard_map/ppermute | solution.py:200
  122.0 23.4 %collective-permute-start.20 = (bf16[4,128,512]{2,1,0:T(8,128)(2,1)S(1)}, bf16[4,128,512]{2,1,0:T(8,128)(2,1)S(1)}, u32[]{:S(2)}, u32[]{:S(2)}) collective-permute-start(bf16[4,128,512]{2,1,0:T(8,128)(2,1)S(1)} %get-tuple-element.79), channel_id=1, source_target_pairs={{0,16},{1,17},{2,18},{3,19},{4,20},{5,21},{6,22},{7,23},{8,24},{9,... | collective-permute-start | bytes 1572872 | tf_op jit(solution)/shard_map/ppermute | solution.py:200
  125.4 18.4 %collective-permute-start.18 = (bf16[6,128,256]{2,1,0:T(8,128)(2,1)S(1)}, bf16[6,128,256]{2,1,0:T(8,128)(2,1)S(1)}, u32[]{:S(2)}, u32[]{:S(2)}) collective-permute-start(bf16[6,128,256]{2,1,0:T(8,128)(2,1)S(1)} %keys_join.1.kv0), channel_id=1, source_target_pairs={{0,6},{1,7},{2,4},{3,5},{4,2},{5,3},{6,0},{7,1},{8,14},{9,15},{10,... | collective-permute-start | bytes 1179656 | tf_op jit(solution)/shard_map/ppermute | solution.py:200
  145.6 26.1 %collective-permute-start.22 = (bf16[4,1024,256]{2,1,0:T(8,128)(2,1)S(1)}, bf16[4,1024,256]{2,1,0:T(8,128)(2,1)S(1)}, u32[]{:S(2)}, u32[]{:S(2)}) collective-permute-start(bf16[4,1024,256]{2,1,0:T(8,128)(2,1)S(1)} %pad_maximum_fusion), channel_id=1, source_target_pairs={{0,4},{1,3},{2,6},{3,1},{4,0},{5,7},{6,2},{7,5},{8,12},{9,11},{10,... | collective-permute-start | bytes 6291464 | tf_op jit(solution)/shard_map/ppermute | solution.py:200
  155.1 16.2 %collective-permute-start.21 = (bf16[512,512]{1,0:T(8,128)(2,1)S(1)}, bf16[512,512]{1,0:T(8,128)(2,1)S(1)}, u32[]{:S(2)}, u32[]{:S(2)}) collective-permute-start(bf16[512,512]{1,0:T(8,128)(2,1)S(1)} %attend.1.own_ref), channel_id=1, source_target_pairs={{0,8},{1,9},{2,10},{3,11},{4,12},{5,13},{6,14},{7,15},{8,0},{9,1},... | collective-permute-start | bytes 1572872 | tf_op jit(solution)/shard_map/ppermute | solution.py:200
  171.7 1.3 copy-start.13
  178.1 2.7 %collective-permute-start.23 = (bf16[4,128,1024]{2,1,0:T(8,128)(2,1)S(1)}, bf16[4,128,1024]{2,1,0:T(8,128)(2,1)S(1)}, u32[]{:S(2)}, u32[]{:S(2)}) collective-permute-start(bf16[4,128,1024]{2,1,0:T(8,128)(2,1)S(1)} %get-tuple-element.86), channel_id=1, source_target_pairs={{0,1},{1,0},{2,3},{3,2},{4,5},{5,4},{6,7},{7,6},{8,9},{9,8},{10,11... | collective-permute-start | bytes 3145736 | tf_op jit(solution)/shard_map/ppermute | solution.py:200
  182.4 16.8 %collective-permute-start.26 = (bf16[128,1024]{1,0:T(8,128)(2,1)S(1)}, bf16[128,1024]{1,0:T(8,128)(2,1)S(1)}, u32[]{:S(2)}, u32[]{:S(2)}) collective-permute-start(bf16[128,1024]{1,0:T(8,128)(2,1)S(1)} %get-tuple-element.92), channel_id=1, source_target_pairs={{0,24},{1,25},{2,26},{3,27},{4,28},{5,29},{6,30},{7,31},{8,0},{9,1... | collective-permute-start | bytes 786440 | tf_op jit(solution)/shard_map/ppermute | solution.py:200
  186.1 14.0 %collective-permute-start.25 = (bf16[128,1024]{1,0:T(8,128)(2,1)S(1)}, bf16[128,1024]{1,0:T(8,128)(2,1)S(1)}, u32[]{:S(2)}, u32[]{:S(2)}) collective-permute-start(bf16[128,1024]{1,0:T(8,128)(2,1)S(1)} %get-tuple-element.93), channel_id=1, source_target_pairs={{0,8},{1,9},{2,10},{3,11},{4,12},{5,13},{6,14},{7,15},{8,16},{9,17... | collective-permute-start | bytes 786440 | tf_op jit(solution)/shard_map/ppermute | solution.py:200
  186.1 22.7 %collective-permute-start.24 = (bf16[128,1024]{1,0:T(8,128)(2,1)S(1)}, bf16[128,1024]{1,0:T(8,128)(2,1)S(1)}, u32[]{:S(2)}, u32[]{:S(2)}) collective-permute-start(bf16[128,1024]{1,0:T(8,128)(2,1)S(1)} %get-tuple-element.91), channel_id=1, source_target_pairs={{0,16},{1,17},{2,18},{3,19},{4,20},{5,21},{6,22},{7,23},{8,24},{9,... | collective-permute-start | bytes 786440 | tf_op jit(solution)/shard_map/ppermute | solution.py:200

commit v9 on v8

--- a/solution.py
+++ b/solution.py
@@ -522,10 +522,12 @@
     keys = jnp.stack([key_own[:depth], key_next[:depth]])
     old_own, old_next = key_own[depth:], key_next[depth:]
     keys_near = to_near(keys)
-    crossed, keys_near = lax.optimization_barrier((crossed, keys_near))
+    crossed, shown = lax.optimization_barrier((crossed, shown))
     held = jnp.concatenate([jnp.where(own_first, normed, crossed), shown], axis=0)
     next_rows = across(held, 1)
-    held_other, out_give = lax.optimization_barrier((other_core(held), out_give))
+    held_other, out_give, keys_near = lax.optimization_barrier(
+        (other_core(held), out_give, keys_near)
+    )
     out_got0 = across(out_give[:out_half], 2)
     keys_far = to_far(jnp.concatenate([keys, keys_near], axis=0))
     next_near = to_near(query_next)
@@ -535,7 +537,9 @@
         )
     )
     out_got1 = across(out_give[out_half:], 2)
+    next_far = to_far(jnp.concatenate([query_next, next_near], axis=0))
     next_other = other_core(next_rows)
+    next_other, out_got1 = lax.optimization_barrier((next_other, out_got1))
     parts = (held, next_rows, held_other, next_other)
 
     half = HD // 2
@@ -563,8 +567,10 @@
         compiler_params=PARAMS,
         name="keys_part",
     )(where, *parts, keys, keys_near, keys_far, old_own, old_next)
-    send, next_near, *parts = lax.optimization_barrier((send, next_near, *parts))
-    next_far = to_far(jnp.concatenate([query_next, next_near], axis=0))
+    send, *parts = lax.optimization_barrier((send, *parts))
+    out_pair = jnp.stack([out_own, jnp.concatenate([out_got0, out_got1], axis=0)])
+    out_pair, next_far = lax.optimization_barrier((out_pair, next_far))
+    out_near = to_near(out_pair)
     q_keep, q_send = pl.pallas_call(
         queries_part_kernel,
         out_shape=(
@@ -577,7 +583,7 @@
         compiler_params=PARAMS,
         name="queries_part",
     )(where, *parts, query_own, query_near, query_far, query_next, next_near, next_far)
-    got_keys, q_send, out_got1 = lax.optimization_barrier((across(send, 2), q_send, out_got1))
+    got_keys, q_send = lax.optimization_barrier((across(send, 2), q_send))
     kv = pl.pallas_call(
         keys_join_kernel,
         out_shape=shaped((LEVELS // 2 + LEVELS, tok, 2 * HD)),
@@ -590,11 +596,8 @@
     kv_near, kv_far = to_near(kv), to_far(kv)
     kv_both = permuted(kv, lambda z, p, c: (z, p ^ 3, c))
 
-    out_pair = jnp.stack([out_own, jnp.concatenate([out_got0, out_got1], axis=0)])
-    out_pair, kv_near, kv_far = lax.optimization_barrier((out_pair, kv_near, kv_far))
-    out_near = to_near(out_pair)
-    kv_far, kv_both, out_near, got_queries = lax.optimization_barrier(
-        (kv_far, kv_both, out_near, across(q_send, 2))
+    kv_near, kv_far, kv_both, out_near, got_queries = lax.optimization_barrier(
+        (kv_near, kv_far, kv_both, out_near, across(q_send, 2))
     )
     out_far = to_far(jnp.concatenate([out_pair, out_near], axis=0))
 

time: 213 us -> 202 us (0.948)
  waiting for transfers between devices: 120 us -> 97.5 us
  starting transfers between devices: 37.5 us -> 55.8 us
  local copies, waits for them, and re-layouts: 10.3 us -> 6.19 us
  other arithmetic: 15.6 us -> 12.9 us
    ppermute x27, waiting for transfers between devices: 120 us -> 97.5 us  [permuted(): return lax.ppermute(value, ('seq', 'head'), perm)]
    ppermute x27, starting transfers between devices: 37.5 us -> 55.8 us  [permuted(): return lax.ppermute(value, ('seq', 'head'), perm)]
    unnamed x40, local copies, waits for them, and re-layouts: 7 us -> 2.12 us
  transfers between devices with their start and end apart: 27 -> 27, of which waited for: 18 -> 16; matrix products, arithmetic and copies ran while one was open for 4% -> 4% of each run, Pallas kernels for 7% -> 9%
where the time goes in v9:
time: 202 us; the launch traced here: 199 us
  waiting for transfers between devices  97.5 us (48%)
  starting transfers between devices  55.8 us (28%)
  Pallas kernels  23.4 us (12%)
  other arithmetic  12.9 us (6%)
  local copies, waits for them, and re-layouts  6.19 us (3%)
  blocking collectives  2.46 us (1%)
    ppermute x27, waiting for transfers between devices, permuted(): return lax.ppermute(value, ('seq', 'head'), perm)  97.5 us
    ppermute x27, starting transfers between devices, permuted(): return lax.ppermute(value, ('seq', 'head'), perm)  55.8 us
    pallas_call x1, Pallas kernels, by_levels(): pl.pallas_call(attend_kernel, out_shape=shaped((LEVELS * tok, 4 * HD)), i...  8.96 us
    pallas_call x1, Pallas kernels, by_levels(): pl.pallas_call(queries_part_kernel, out_shape=(shaped((LEVELS, tok, 4 * H...  5.18 us
    pallas_call x1, Pallas kernels, by_levels(): pl.pallas_call(output_kernel, out_shape=(shaped((LEVELS, tok, wide_cols),...  5.08 us
  transfers between devices with their start and end apart: 27, of which 16 were waited for; matrix products, arithmetic and copies ran while one was open for 4% of the time, Pallas kernels for 9%

profile of v9, /device:TPU:8, one launch (start us, length us, event | category | flops | bytes accessed | tf_op | source)
XLA Modules:
  0.0 198.7 jit_solution(8858370185954675448)
XLA Ops:
  0.0 1.2 fusion.4
  1.3 1.4 fusion
  2.7 2.5 %all-reduce.1 = (f32[144]{0:T(256)S(1)}, f32[32]{0:T(128)S(1)}) all-reduce(f32[144]{0:T(256)S(1)} %fusion, f32[32]{0:T(128)S(1)} %fusion.4), channel_id=1, replica_groups=mesh['seq'=16,'head'=2] {'head'}, use_global_device_ids=true, to_apply=%region_1.2 | all-reduce | flops 176 | bytes 1408 | tf_op jit(solution)/shard_map/psum | solution.py:503
  5.1 0.7 dynamic_slice.9
  5.8 2.3 %fusion.2 = bf16[144,2048]{1,0:T(8,128)(2,1)} fusion(f32[2048]{0:T(1024)S(1)} %dynamic_slice.9, f32[144]{0:T(256)S(1)} %add_rsqrt_fusion, bf16[8,2048]{1,0:T(8,128)(2,1)} %param.21, bf16[128,2048]{1,0:T(8,128)(2,1)} %param.12, bf16[144]{0:T(256)(128)(2,1)S(1)} %pad.32.clone), kind=kLoop, calls=%fused_computation.5 | loop fusion | flops 2654208 | bytes 1155936 | tf_op jit(solution)/shard_map/convert_element_type | solution.py:31
  8.1 1.5 collective-permute-start
  9.8 1.0 pack.1
  11.0 1.2 fusion.6
  12.1 4.7 %collective-permute-start.1 = (bf16[32,2048]{1,0:T(8,128)(2,1)S(1)}, bf16[32,2048]{1,0:T(8,128)(2,1)S(1)}, u32[]{:S(2)}, u32[]{:S(2)}) collective-permute-start(bf16[32,2048]{1,0:T(8,128)(2,1)S(1)} %fusion.6), channel_id=1, source_target_pairs={{0,0},{1,16},{2,1},{3,17},{4,8},{5,24},{6,9},{7,25},{8,2},{9,18},{... | collective-permute-start | bytes 393224 | tf_op jit(solution)/shard_map/ppermute | solution.py:200
  16.8 3.2 %collective-permute-start.7 = (bf16[1,256,1024]{2,1,0:T(8,128)(2,1)S(1)}, bf16[1,256,1024]{2,1,0:T(8,128)(2,1)S(1)}, u32[]{:S(2)}, u32[]{:S(2)}) collective-permute-start(bf16[1,256,1024]{2,1,0:T(8,128)(2,1)S(1)} %get-tuple-element.55.refs_0_), channel_id=1, source_target_pairs={{0,2},{1,5},{2,0},{3,7},{4,6},{5,1},{6,4},{7,3},{8,10},{9,13},{10,... | collective-permute-start | bytes 1572872 | tf_op jit(solution)/shard_map/ppermute | solution.py:200
  20.0 8.5 %collective-permute-done.1 = bf16[32,2048]{1,0:T(8,128)(2,1)S(1)} collective-permute-done((bf16[32,2048]{1,0:T(8,128)(2,1)S(1)}, bf16[32,2048]{1,0:T(8,128)(2,1)S(1)}, u32[]{:S(2)}, u32[]{:S(2)}) %collective-permute-start.1) | collective-permute-done | bytes 131104 | tf_op jit(solution)/shard_map/ppermute | solution.py:200
  28.6 0.5 broadcast_select_fusion
  29.1 1.5 collective-permute-start.4
  30.7 0.7 copy-done.12
  31.5 1.7 collective-permute-start.5
  33.2 1.3 dynamic-slice_bitcast_fusion
  34.6 2.2 %collective-permute-start.8 = (bf16[2,256,1024]{2,1,0:T(8,128)(2,1)S(1)}, bf16[2,256,1024]{2,1,0:T(8,128)(2,1)S(1)}, u32[]{:S(2)}, u32[]{:S(2)}) collective-permute-start(bf16[2,256,1024]{2,1,0:T(8,128)(2,1)S(1)} %pad_maximum_fusion.2), channel_id=1, source_target_pairs={{0,4},{1,3},{2,6},{3,1},{4,0},{5,7},{6,2},{7,5},{8,12},{9,11},{10,... | collective-permute-start | bytes 3145736 | tf_op jit(solution)/shard_map/ppermute | solution.py:200
  36.8 3.9 %collective-permute-start.9 = (bf16[1,256,1024]{2,1,0:T(8,128)(2,1)S(1)}, bf16[1,256,1024]{2,1,0:T(8,128)(2,1)S(1)}, u32[]{:S(2)}, u32[]{:S(2)}) collective-permute-start(bf16[1,256,1024]{2,1,0:T(8,128)(2,1)S(1)} %copy-done.8), channel_id=1, source_target_pairs={{0,8},{1,9},{2,10},{3,11},{4,12},{5,13},{6,14},{7,15},{8,0},{9,1},... | collective-permute-start | bytes 1572872 | tf_op jit(solution)/shard_map/ppermute | solution.py:200
  40.7 3.2 %collective-permute-done.5.near = bf16[2,256,512]{2,1,0:T(8,128)(2,1)S(1)} collective-permute-done((bf16[2,256,512]{2,1,0:T(8,128)(2,1)S(1)}, bf16[2,256,512]{2,1,0:T(8,128)(2,1)S(1)}, u32[]{:S(2)}, u32[]{:S(2)}) %collective-permute-start.5) | collective-permute-done | bytes 524320 | tf_op jit(solution)/shard_map/ppermute | solution.py:200
  44.1 3.4 %collective-permute-start.6 = (bf16[4,256,512]{2,1,0:T(8,128)(2,1)S(1)}, bf16[4,256,512]{2,1,0:T(8,128)(2,1)S(1)}, u32[]{:S(2)}, u32[]{:S(2)}) collective-permute-start(bf16[4,256,512]{2,1,0:T(8,128)(2,1)S(1)} %pad_maximum_fusion.1), channel_id=1, source_target_pairs={{0,4},{1,3},{2,6},{3,1},{4,0},{5,7},{6,2},{7,5},{8,12},{9,11},{10,... | collective-permute-start | bytes 3145736 | tf_op jit(solution)/shard_map/ppermute | solution.py:200
  47.5 3.9 %collective-permute-start.3 = (bf16[176,2048]{1,0:T(8,128)(2,1)S(1)}, bf16[176,2048]{1,0:T(8,128)(2,1)S(1)}, u32[]{:S(2)}, u32[]{:S(2)}) collective-permute-start(bf16[176,2048]{1,0:T(8,128)(2,1)S(1)} %pad_maximum_fusion.5.x0), channel_id=1, source_target_pairs={{0,8},{1,9},{2,10},{3,11},{4,12},{5,13},{6,14},{7,15},{8,0},{9,1},... | collective-permute-start | bytes 2162696 | tf_op jit(solution)/shard_map/ppermute | solution.py:200
  51.4 2.2 %collective-permute-done.9.refs_3_ = bf16[1,256,1024]{2,1,0:T(8,128)(2,1)S(1)} collective-permute-done((bf16[1,256,1024]{2,1,0:T(8,128)(2,1)S(1)}, bf16[1,256,1024]{2,1,0:T(8,128)(2,1)S(1)}, u32[]{:S(2)}, u32[]{:S(2)}) %collective-permute-start.9) | collective-permute-done | bytes 524320 | tf_op jit(solution)/shard_map/ppermute | solution.py:200
  53.5 0.2 collective-permute-start.10
  53.8 3.1 %collective-permute-start.11 = (bf16[512,256]{1,0:T(8,128)(2,1)S(1)}, bf16[512,256]{1,0:T(8,128)(2,1)S(1)}, u32[]{:S(2)}, u32[]{:S(2)}) collective-permute-start(bf16[512,256]{1,0:T(8,128)(2,1)S(1)} %slice.44), channel_id=1, source_target_pairs={{0,16},{1,17},{2,18},{3,19},{4,20},{5,21},{6,22},{7,23},{8,24},{9,... | collective-permute-start | bytes 786440 | tf_op jit(solution)/shard_map/ppermute | solution.py:200
  56.8 15.8 %collective-permute-done.3.x1 = bf16[176,2048]{1,0:T(8,128)(2,1)S(1)} collective-permute-done((bf16[176,2048]{1,0:T(8,128)(2,1)S(1)}, bf16[176,2048]{1,0:T(8,128)(2,1)S(1)}, u32[]{:S(2)}, u32[]{:S(2)}) %collective-permute-start.3) | collective-permute-done | bytes 720928 | tf_op jit(solution)/shard_map/ppermute | solution.py:200
  72.6 1.5 collective-permute-done.11
  74.3 0.9 collective-permute-start.14
  75.2 1.8 collective-permute-start.13
  77.1 0.9 slice.46.old0
  78.1 0.9 slice.47.old1
  79.0 9.2 %collective-permute-done.13 = bf16[512,256]{1,0:T(8,128)(2,1)S(1)} collective-permute-done((bf16[512,256]{1,0:T(8,128)(2,1)S(1)}, bf16[512,256]{1,0:T(8,128)(2,1)S(1)}, u32[]{:S(2)}, u32[]{:S(2)}) %collective-permute-start.13) | collective-permute-done | bytes 262176 | tf_op jit(solution)/shard_map/ppermute | solution.py:200
  88.2 2.1 %keys_part.1 = (f32[576,256]{1,0:T(8,128)S(1)}, bf16[736,256]{1,0:T(8,128)(2,1)S(1)}) custom-call(s32[5]{0:T(128)S(1)} %stack.41.where_ref, bf16[176,2048]{1,0:T(8,128)(2,1)S(1)} %pad_maximum_fusion.5.x0, bf16[176,2048]{1,0:T(8,128)(2,1)S(1)} %collective-permute-done.3.x1, bf16[176,2048]{1,0:T(8,128)(2,1)S(1)} %collective-permute-done.4.x2, ...), custom_call_target="tpu_custom_call" | custom-call | tf_op jit(solution)/shard_map/keys_part/pallas_call | solution.py:558
  90.3 3.4 %collective-permute-start.15 = (bf16[736,256]{1,0:T(8,128)(2,1)S(1)}, bf16[736,256]{1,0:T(8,128)(2,1)S(1)}, u32[]{:S(2)}, u32[]{:S(2)}) collective-permute-start(bf16[736,256]{1,0:T(8,128)(2,1)S(1)} %get-tuple-element.77), channel_id=1, source_target_pairs={{0,16},{1,17},{2,18},{3,19},{4,20},{5,21},{6,22},{7,23},{8,24},{9,... | collective-permute-start | bytes 1130504 | tf_op jit(solution)/shard_map/ppermute | solution.py:200
  93.9 1.2 collective-permute-start.19
  95.1 1.4 fusion.10
  96.5 5.2 %queries_part.1 = (f32[4,128,512]{2,1,0:T(8,128)}, bf16[4,128,512]{2,1,0:T(8,128)(2,1)S(1)}) custom-call(s32[5]{0:T(128)S(1)} %stack.41.where_ref, bf16[176,2048]{1,0:T(8,128)(2,1)S(1)} %pad_maximum_fusion.5.x0, bf16[176,2048]{1,0:T(8,128)(2,1)S(1)} %collective-permute-done.3.x1, bf16[176,2048]{1,0:T(8,128)(2,1)S(1)} %collective-permute-done.4.x2, ...), custom_call_target="tpu_custom_call" | custom-call | tf_op jit(solution)/shard_map/queries_part/pallas_call | solution.py:574
  101.7 6.7 %collective-permute-done.15.got_ref = bf16[736,256]{1,0:T(8,128)(2,1)S(1)} collective-permute-done((bf16[736,256]{1,0:T(8,128)(2,1)S(1)}, bf16[736,256]{1,0:T(8,128)(2,1)S(1)}, u32[]{:S(2)}, u32[]{:S(2)}) %collective-permute-start.15) | collective-permute-done | bytes 376864 | tf_op jit(solution)/shard_map/ppermute | solution.py:200
  108.4 3.4 %collective-permute-start.20 = (bf16[4,128,512]{2,1,0:T(8,128)(2,1)S(1)}, bf16[4,128,512]{2,1,0:T(8,128)(2,1)S(1)}, u32[]{:S(2)}, u32[]{:S(2)}) collective-permute-start(bf16[4,128,512]{2,1,0:T(8,128)(2,1)S(1)} %get-tuple-element.81), channel_id=1, source_target_pairs={{0,16},{1,17},{2,18},{3,19},{4,20},{5,21},{6,22},{7,23},{8,24},{9,... | collective-permute-start | bytes 1572872 | tf_op jit(solution)/shard_map/ppermute | solution.py:200
  111.8 0.2 pad_maximum_fusion.8.cos_ref
  112.0 0.2 pad_maximum_fusion.9.sin_ref
  112.1 1.0 keys_join.1.kv0
  113.2 1.2 collective-permute-start.16
  114.4 2.1 %collective-permute-start.17 = (bf16[6,128,256]{2,1,0:T(8,128)(2,1)S(1)}, bf16[6,128,256]{2,1,0:T(8,128)(2,1)S(1)}, u32[]{:S(2)}, u32[]{:S(2)}) collective-permute-start(bf16[6,128,256]{2,1,0:T(8,128)(2,1)S(1)} %keys_join.1.kv0), channel_id=1, source_target_pairs={{0,4},{1,3},{2,6},{3,1},{4,0},{5,7},{6,2},{7,5},{8,12},{9,11},{10,... | collective-permute-start | bytes 1179656 | tf_op jit(solution)/shard_map/ppermute | solution.py:200
  116.5 0.4 collective-permute-start.18
  116.9 7.8 %collective-permute-done.16.kv1 = bf16[6,128,256]{2,1,0:T(8,128)(2,1)S(1)} collective-permute-done((bf16[6,128,256]{2,1,0:T(8,128)(2,1)S(1)}, bf16[6,128,256]{2,1,0:T(8,128)(2,1)S(1)}, u32[]{:S(2)}, u32[]{:S(2)}) %collective-permute-start.16) | collective-permute-done | bytes 393248 | tf_op jit(solution)/shard_map/ppermute | solution.py:200
  124.6 9.5 %collective-permute-done.18.kv3 = bf16[6,128,256]{2,1,0:T(8,128)(2,1)S(1)} collective-permute-done((bf16[6,128,256]{2,1,0:T(8,128)(2,1)S(1)}, bf16[6,128,256]{2,1,0:T(8,128)(2,1)S(1)}, u32[]{:S(2)}, u32[]{:S(2)}) %collective-permute-start.18) | collective-permute-done | bytes 393248 | tf_op jit(solution)/shard_map/ppermute | solution.py:200
  134.2 0.2 pad_maximum_fusion
  134.4 2.2 %collective-permute-start.22 = (bf16[4,1024,256]{2,1,0:T(8,128)(2,1)S(1)}, bf16[4,1024,256]{2,1,0:T(8,128)(2,1)S(1)}, u32[]{:S(2)}, u32[]{:S(2)}) collective-permute-start(bf16[4,1024,256]{2,1,0:T(8,128)(2,1)S(1)} %pad_maximum_fusion), channel_id=1, source_target_pairs={{0,4},{1,3},{2,6},{3,1},{4,0},{5,7},{6,2},{7,5},{8,12},{9,11},{10,... | collective-permute-start | bytes 6291464 | tf_op jit(solution)/shard_map/ppermute | solution.py:200
  136.6 9.0 %attend.1.own_ref = bf16[512,512]{1,0:T(8,128)(2,1)S(1)} custom-call(s32[5]{0:T(128)S(1)} %stack.41.where_ref, f32[4,128,512]{2,1,0:T(8,128)S(1)} %copy-done, bf16[4,128,512]{2,1,0:T(8,128)(2,1)S(1)} %collective-permute-done.20.got_ref, f32[4,192,128]{2,1,0:T(8,128)S(1)} %pad_maximum_fusion.8.cos_ref, f32[4,192,128]{2,1,0:T(8,128)S(1)} %pad_maximum_fusion.9.sin_ref, ...), custom_call_target="tpu_custom_call" | custom-call | tf_op jit(solution)/shard_map/attend/pallas_call | solution.py:604
  145.5 2.5 %collective-permute-start.21 = (bf16[512,512]{1,0:T(8,128)(2,1)S(1)}, bf16[512,512]{1,0:T(8,128)(2,1)S(1)}, u32[]{:S(2)}, u32[]{:S(2)}) collective-permute-start(bf16[512,512]{1,0:T(8,128)(2,1)S(1)} %attend.1.own_ref), channel_id=1, source_target_pairs={{0,8},{1,9},{2,10},{3,11},{4,12},{5,13},{6,14},{7,15},{8,0},{9,1},... | collective-permute-start | bytes 1572872 | tf_op jit(solution)/shard_map/ppermute | solution.py:200
  148.0 10.8 %collective-permute-done.21.next_ref = bf16[512,512]{1,0:T(8,128)(2,1)S(1)} collective-permute-done((bf16[512,512]{1,0:T(8,128)(2,1)S(1)}, bf16[512,512]{1,0:T(8,128)(2,1)S(1)}, u32[]{:S(2)}, u32[]{:S(2)}) %collective-permute-start.21) | collective-permute-done | bytes 524320 | tf_op jit(solution)/shard_map/ppermute | solution.py:200
  158.8 1.7 collective-permute-done.22.w_far
  160.6 1.3 copy-done.14
  161.9 5.1 %output.1 = (f32[4,128,1024]{2,1,0:T(8,128)}, bf16[4,128,1024]{2,1,0:T(8,128)(2,1)S(1)}) custom-call(s32[5]{0:T(128)S(1)} %stack.41.where_ref, bf16[512,512]{1,0:T(8,128)(2,1)S(1)} %attend.1.own_ref, bf16[512,512]{1,0:T(8,128)(2,1)S(1)} %collective-permute-done.21.next_ref, bf16[2,1024,256]{2,1,0:T(8,128)(2,1)S(1)} %pad_maximum_fusion.3.w_own, ...), custom_call_target="tpu_custom_call" | custom-call | tf_op jit(solution)/shard_map/output/pallas_call | solution.py:615
  167.0 2.7 %collective-permute-done.23 = bf16[4,128,1024]{2,1,0:T(8,128)(2,1)S(1)} collective-permute-done((bf16[4,128,1024]{2,1,0:T(8,128)(2,1)S(1)}, bf16[4,128,1024]{2,1,0:T(8,128)(2,1)S(1)}, u32[]{:S(2)}, u32[]{:S(2)}) %collective-permute-start.23) | collective-permute-done | bytes 1048608 | tf_op jit(solution)/shard_map/ppermute | solution.py:200
  169.6 1.6 fusion.7
  171.3 2.5 %collective-permute-start.26 = (bf16[128,1024]{1,0:T(8,128)(2,1)S(1)}, bf16[128,1024]{1,0:T(8,128)(2,1)S(1)}, u32[]{:S(2)}, u32[]{:S(2)}) collective-permute-start(bf16[128,1024]{1,0:T(8,128)(2,1)S(1)} %get-tuple-element.94), channel_id=1, source_target_pairs={{0,24},{1,25},{2,26},{3,27},{4,28},{5,29},{6,30},{7,31},{8,0},{9,1... | collective-permute-start | bytes 786440 | tf_op jit(solution)/shard_map/ppermute | solution.py:200
  173.8 4.7 %collective-permute-start.24 = (bf16[128,1024]{1,0:T(8,128)(2,1)S(1)}, bf16[128,1024]{1,0:T(8,128)(2,1)S(1)}, u32[]{:S(2)}, u32[]{:S(2)}) collective-permute-start(bf16[128,1024]{1,0:T(8,128)(2,1)S(1)} %get-tuple-element.93), channel_id=1, source_target_pairs={{0,16},{1,17},{2,18},{3,19},{4,20},{5,21},{6,22},{7,23},{8,24},{9,... | collective-permute-start | bytes 786440 | tf_op jit(solution)/shard_map/ppermute | solution.py:200
  178.5 8.4 %collective-permute-done.26 = bf16[128,1024]{1,0:T(8,128)(2,1)S(1)} collective-permute-done((bf16[128,1024]{1,0:T(8,128)(2,1)S(1)}, bf16[128,1024]{1,0:T(8,128)(2,1)S(1)}, u32[]{:S(2)}, u32[]{:S(2)}) %collective-permute-start.26) | collective-permute-done | bytes 262176 | tf_op jit(solution)/shard_map/ppermute | solution.py:200
  186.9 2.1 %collective-permute-done.25 = bf16[128,1024]{1,0:T(8,128)(2,1)S(1)} collective-permute-done((bf16[128,1024]{1,0:T(8,128)(2,1)S(1)}, bf16[128,1024]{1,0:T(8,128)(2,1)S(1)}, u32[]{:S(2)}, u32[]{:S(2)}) %collective-permute-start.25) | collective-permute-done | bytes 262176 | tf_op jit(solution)/shard_map/ppermute | solution.py:200
  188.9 7.6 %collective-permute-done.24 = bf16[128,1024]{1,0:T(8,128)(2,1)S(1)} collective-permute-done((bf16[128,1024]{1,0:T(8,128)(2,1)S(1)}, bf16[128,1024]{1,0:T(8,128)(2,1)S(1)}, u32[]{:S(2)}, u32[]{:S(2)}) %collective-permute-start.24) | collective-permute-done | bytes 262176 | tf_op jit(solution)/shard_map/ppermute | solution.py:200
  196.5 1.2 broadcast_select_fusion.2
  197.8 0.1 broadcast_select_fusion.1
  197.9 0.8 pad_maximum_fusion.7
  (78 shorter events, 1.3 us)
Async XLA Ops:
  0.0 9.6 %copy-start.19 = (s32[8]{0:T(128)S(1)}, s32[8]{0:T(128)}, u32[]{:S(2)}) copy-start(s32[8]{0:T(128)} %param.22) | copy-start | bytes 100
  0.0 9.8 %copy-start.1 = (bf16[256,2048]{1,0:T(8,128)(2,1)S(1)}, bf16[256,2048]{1,0:T(8,128)(2,1)}, u32[]{:S(2)}) copy-start(bf16[256,2048]{1,0:T(8,128)(2,1)} %refs_0_.1) | copy-start | bytes 3145732
  0.0 9.8 %copy-start.3 = (bf16[256,512]{1,0:T(8,128)(2,1)S(1)}, bf16[256,512]{1,0:T(8,128)(2,1)}, u32[]{:S(2)}) copy-start(bf16[256,512]{1,0:T(8,128)(2,1)} %refs_1_.1) | copy-start | bytes 786436
  0.0 9.8 %copy-start.4 = (bf16[256,512]{1,0:T(8,128)(2,1)S(1)}, bf16[256,512]{1,0:T(8,128)(2,1)}, u32[]{:S(2)}) copy-start(bf16[256,512]{1,0:T(8,128)(2,1)} %refs_2_.1) | copy-start | bytes 786436
  0.0 9.8 %copy-start.5 = (bf16[64,512]{1,0:T(8,128)(2,1)S(1)}, bf16[64,512]{1,0:T(8,128)(2,1)}, u32[]{:S(2)}) copy-start(bf16[64,512]{1,0:T(8,128)(2,1)} %refs_3_.1) | copy-start | bytes 196612
  0.0 9.8 %copy-start.6 = (bf16[64,512]{1,0:T(8,128)(2,1)S(1)}, bf16[64,512]{1,0:T(8,128)(2,1)}, u32[]{:S(2)}) copy-start(bf16[64,512]{1,0:T(8,128)(2,1)} %refs_4_.1) | copy-start | bytes 196612
  8.1 20.4 %collective-permute-start = (bf16[144,2048]{1,0:T(8,128)(2,1)}, bf16[144,2048]{1,0:T(8,128)(2,1)}, u32[]{:S(2)}, u32[]{:S(2)}) collective-permute-start(bf16[144,2048]{1,0:T(8,128)(2,1)} %fusion.2), channel_id=1, source_target_pairs={{1,16},{3,18},{5,20},{7,22},{9,24},{11,26},{13,28},{15,30},{16,1},... | collective-permute-start | bytes 1769480 | tf_op jit(solution)/shard_map/ppermute | solution.py:200
  9.8 18.8 %copy-start.9 = (bf16[128,2048]{1,0:T(8,128)(2,1)S(1)}, bf16[128,2048]{1,0:T(8,128)(2,1)}, u32[]{:S(2)}) copy-start(bf16[128,2048]{1,0:T(8,128)(2,1)} %param.12) | copy-start | bytes 1572868
  9.8 18.7 %copy-start.18 = (bf16[8,2048]{1,0:T(8,128)(2,1)S(1)}, bf16[8,2048]{1,0:T(8,128)(2,1)}, u32[]{:S(2)}) copy-start(bf16[8,2048]{1,0:T(8,128)(2,1)} %param.21) | copy-start | bytes 98308
  10.9 18.2 %copy-start.2 = (bf16[336,512]{1,0:T(8,128)(2,1)}, bf16[336,512]{1,0:T(8,128)(2,1)S(1)}, u32[]{:S(2)}) copy-start(bf16[336,512]{1,0:T(8,128)(2,1)S(1)} %get-tuple-element.51) | copy-start | bytes 1032196
  10.9 18.2 %copy-start.7 = (bf16[1,256,1024]{2,1,0:T(8,128)(2,1)}, bf16[1,256,1024]{2,1,0:T(8,128)(2,1)S(1)}, u32[]{:S(2)}) copy-start(bf16[1,256,1024]{2,1,0:T(8,128)(2,1)S(1)} %get-tuple-element.57) | copy-start | bytes 1572868
  10.9 17.7 %collective-permute-start.2 = (bf16[336,512]{1,0:T(8,128)(2,1)S(1)}, bf16[336,512]{1,0:T(8,128)(2,1)S(1)}, u32[]{:S(2)}, u32[]{:S(2)}) collective-permute-start(bf16[336,512]{1,0:T(8,128)(2,1)S(1)} %get-tuple-element.47), channel_id=1, source_target_pairs={{0,8},{1,9},{2,10},{3,11},{4,12},{5,13},{6,14},{7,15},{8,0},{9,1},... | collective-permute-start | bytes 1032200 | tf_op jit(solution)/shard_map/ppermute | solution.py:200
  12.1 16.4 %collective-permute-start.1 = (bf16[32,2048]{1,0:T(8,128)(2,1)S(1)}, bf16[32,2048]{1,0:T(8,128)(2,1)S(1)}, u32[]{:S(2)}, u32[]{:S(2)}) collective-permute-start(bf16[32,2048]{1,0:T(8,128)(2,1)S(1)} %fusion.6), channel_id=1, source_target_pairs={{0,0},{1,16},{2,1},{3,17},{4,8},{5,24},{6,9},{7,25},{8,2},{9,18},{... | collective-permute-start | bytes 393224 | tf_op jit(solution)/shard_map/ppermute | solution.py:200
  16.8 17.6 %collective-permute-start.7 = (bf16[1,256,1024]{2,1,0:T(8,128)(2,1)S(1)}, bf16[1,256,1024]{2,1,0:T(8,128)(2,1)S(1)}, u32[]{:S(2)}, u32[]{:S(2)}) collective-permute-start(bf16[1,256,1024]{2,1,0:T(8,128)(2,1)S(1)} %get-tuple-element.55.refs_0_), channel_id=1, source_target_pairs={{0,2},{1,5},{2,0},{3,7},{4,6},{5,1},{6,4},{7,3},{8,10},{9,13},{10,... | collective-permute-start | bytes 1572872 | tf_op jit(solution)/shard_map/ppermute | solution.py:200
  20.0 10.7 %copy-start.10 = (bf16[1,256,512]{2,1,0:T(8,128)(2,1)}, bf16[1,256,512]{2,1,0:T(8,128)(2,1)S(1)}, u32[]{:S(2)}) copy-start(bf16[1,256,512]{2,1,0:T(8,128)(2,1)S(1)} %slice_bitcast_fusion.1) | copy-start | bytes 786436
  28.5 2.1 %copy-start.17 = (bf16[336,512]{1,0:T(8,128)(2,1)}, bf16[336,512]{1,0:T(8,128)(2,1)S(1)}, u32[]{:S(2)}) copy-start(bf16[336,512]{1,0:T(8,128)(2,1)S(1)} %collective-permute-done.2) | copy-start | bytes 1032196
  29.1 14.8 %collective-permute-start.4 = (bf16[176,2048]{1,0:T(8,128)(2,1)S(1)}, bf16[176,2048]{1,0:T(8,128)(2,1)S(1)}, u32[]{:S(2)}, u32[]{:S(2)}) collective-permute-start(bf16[176,2048]{1,0:T(8,128)(2,1)S(1)} %pad_maximum_fusion.5.x0), channel_id=1, source_target_pairs={{0,1},{1,0},{2,3},{3,2},{4,5},{5,4},{6,7},{7,6},{8,9},{9,8},{10,11... | collective-permute-start | bytes 2162696 | tf_op jit(solution)/shard_map/ppermute | solution.py:200
  30.7 0.7 copy-start.12
  31.5 12.5 %collective-permute-start.5 = (bf16[2,256,512]{2,1,0:T(8,128)(2,1)S(1)}, bf16[2,256,512]{2,1,0:T(8,128)(2,1)S(1)}, u32[]{:S(2)}, u32[]{:S(2)}) collective-permute-start(bf16[2,256,512]{2,1,0:T(8,128)(2,1)S(1)} %pad_maximum_fusion.6.own), channel_id=1, source_target_pairs={{0,2},{1,5},{2,0},{3,7},{4,6},{5,1},{6,4},{7,3},{8,10},{9,13},{10,... | collective-permute-start | bytes 1572872 | tf_op jit(solution)/shard_map/ppermute | solution.py:200
  34.4 2.4 %copy-start.8 = (bf16[1,256,1024]{2,1,0:T(8,128)(2,1)S(1)}, bf16[1,256,1024]{2,1,0:T(8,128)(2,1)}, u32[]{:S(2)}) copy-start(bf16[1,256,1024]{2,1,0:T(8,128)(2,1)} %copy-done.7) | copy-start | bytes 1572868
  34.5 9.5 %copy-start.11 = (bf16[1,256,512]{2,1,0:T(8,128)(2,1)S(1)}, bf16[1,256,512]{2,1,0:T(8,128)(2,1)}, u32[]{:S(2)}) copy-start(bf16[1,256,512]{2,1,0:T(8,128)(2,1)} %copy-done.10) | copy-start | bytes 786436
  34.5 9.5 %copy-start.13 = (bf16[1,256,512]{2,1,0:T(8,128)(2,1)S(1)}, bf16[1,256,512]{2,1,0:T(8,128)(2,1)}, u32[]{:S(2)}) copy-start(bf16[1,256,512]{2,1,0:T(8,128)(2,1)} %copy-done.12) | copy-start | bytes 786436
  34.6 38.0 %collective-permute-start.8 = (bf16[2,256,1024]{2,1,0:T(8,128)(2,1)S(1)}, bf16[2,256,1024]{2,1,0:T(8,128)(2,1)S(1)}, u32[]{:S(2)}, u32[]{:S(2)}) collective-permute-start(bf16[2,256,1024]{2,1,0:T(8,128)(2,1)S(1)} %pad_maximum_fusion.2), channel_id=1, source_target_pairs={{0,4},{1,3},{2,6},{3,1},{4,0},{5,7},{6,2},{7,5},{8,12},{9,11},{10,... | collective-permute-start | bytes 3145736 | tf_op jit(solution)/shard_map/ppermute | solution.py:200
  36.8 16.7 %collective-permute-start.9 = (bf16[1,256,1024]{2,1,0:T(8,128)(2,1)S(1)}, bf16[1,256,1024]{2,1,0:T(8,128)(2,1)S(1)}, u32[]{:S(2)}, u32[]{:S(2)}) collective-permute-start(bf16[1,256,1024]{2,1,0:T(8,128)(2,1)S(1)} %copy-done.8), channel_id=1, source_target_pairs={{0,8},{1,9},{2,10},{3,11},{4,12},{5,13},{6,14},{7,15},{8,0},{9,1},... | collective-permute-start | bytes 1572872 | tf_op jit(solution)/shard_map/ppermute | solution.py:200
  44.1 30.1 %collective-permute-start.6 = (bf16[4,256,512]{2,1,0:T(8,128)(2,1)S(1)}, bf16[4,256,512]{2,1,0:T(8,128)(2,1)S(1)}, u32[]{:S(2)}, u32[]{:S(2)}) collective-permute-start(bf16[4,256,512]{2,1,0:T(8,128)(2,1)S(1)} %pad_maximum_fusion.1), channel_id=1, source_target_pairs={{0,4},{1,3},{2,6},{3,1},{4,0},{5,7},{6,2},{7,5},{8,12},{9,11},{10,... | collective-permute-start | bytes 3145736 | tf_op jit(solution)/shard_map/ppermute | solution.py:200
  47.5 25.1 %collective-permute-start.3 = (bf16[176,2048]{1,0:T(8,128)(2,1)S(1)}, bf16[176,2048]{1,0:T(8,128)(2,1)S(1)}, u32[]{:S(2)}, u32[]{:S(2)}) collective-permute-start(bf16[176,2048]{1,0:T(8,128)(2,1)S(1)} %pad_maximum_fusion.5.x0), channel_id=1, source_target_pairs={{0,8},{1,9},{2,10},{3,11},{4,12},{5,13},{6,14},{7,15},{8,0},{9,1},... | collective-permute-start | bytes 2162696 | tf_op jit(solution)/shard_map/ppermute | solution.py:200
  53.5 19.1 %collective-permute-start.10 = (bf16[1,256,1024]{2,1,0:T(8,128)(2,1)S(1)}, bf16[1,256,1024]{2,1,0:T(8,128)(2,1)S(1)}, u32[]{:S(2)}, u32[]{:S(2)}) collective-permute-start(bf16[1,256,1024]{2,1,0:T(8,128)(2,1)S(1)} %collective-permute-done.9.refs_3_), channel_id=1, source_target_pairs={{0,2},{1,5},{2,0},{3,7},{4,6},{5,1},{6,4},{7,3},{8,10},{9,13},{10,... | collective-permute-start | bytes 1572872 | tf_op jit(solution)/shard_map/ppermute | solution.py:200
  53.8 20.4 %collective-permute-start.11 = (bf16[512,256]{1,0:T(8,128)(2,1)S(1)}, bf16[512,256]{1,0:T(8,128)(2,1)S(1)}, u32[]{:S(2)}, u32[]{:S(2)}) collective-permute-start(bf16[512,256]{1,0:T(8,128)(2,1)S(1)} %slice.44), channel_id=1, source_target_pairs={{0,16},{1,17},{2,18},{3,19},{4,20},{5,21},{6,22},{7,23},{8,24},{9,... | collective-permute-start | bytes 786440 | tf_op jit(solution)/shard_map/ppermute | solution.py:200
  72.6 2.6 %copy-start.15 = (bf16[2,256,1024]{2,1,0:T(8,128)(2,1)}, bf16[2,256,1024]{2,1,0:T(8,128)(2,1)S(1)}, u32[]{:S(2)}) copy-start(bf16[2,256,1024]{2,1,0:T(8,128)(2,1)S(1)} %collective-permute-done.8.refs_2_) | copy-start | bytes 3145732
  74.3 19.6 %collective-permute-start.14 = (bf16[2,256,1024]{2,1,0:T(8,128)(2,1)S(1)}, bf16[2,256,1024]{2,1,0:T(8,128)(2,1)S(1)}, u32[]{:S(2)}, u32[]{:S(2)}) collective-permute-start(bf16[2,256,1024]{2,1,0:T(8,128)(2,1)S(1)} %pad_maximum_fusion.4), channel_id=1, source_target_pairs={{0,4},{1,3},{2,6},{3,1},{4,0},{5,7},{6,2},{7,5},{8,12},{9,11},{10,... | collective-permute-start | bytes 3145736 | tf_op jit(solution)/shard_map/ppermute | solution.py:200
  75.2 13.0 %collective-permute-start.12 = (bf16[176,2048]{1,0:T(8,128)(2,1)S(1)}, bf16[176,2048]{1,0:T(8,128)(2,1)S(1)}, u32[]{:S(2)}, u32[]{:S(2)}) collective-permute-start(bf16[176,2048]{1,0:T(8,128)(2,1)S(1)} %collective-permute-done.3.x1), channel_id=1, source_target_pairs={{0,1},{1,0},{2,3},{3,2},{4,5},{5,4},{6,7},{7,6},{8,9},{9,8},{10,11... | collective-permute-start | bytes 2162696 | tf_op jit(solution)/shard_map/ppermute | solution.py:200
  75.2 13.0 %collective-permute-start.13 = (bf16[512,256]{1,0:T(8,128)(2,1)S(1)}, bf16[512,256]{1,0:T(8,128)(2,1)S(1)}, u32[]{:S(2)}, u32[]{:S(2)}) collective-permute-start(bf16[512,256]{1,0:T(8,128)(2,1)S(1)} %slice.45), channel_id=1, source_target_pairs={{0,16},{1,17},{2,18},{3,19},{4,20},{5,21},{6,22},{7,23},{8,24},{9,... | collective-permute-start | bytes 786440 | tf_op jit(solution)/shard_map/ppermute | solution.py:200
  90.3 18.1 %collective-permute-start.15 = (bf16[736,256]{1,0:T(8,128)(2,1)S(1)}, bf16[736,256]{1,0:T(8,128)(2,1)S(1)}, u32[]{:S(2)}, u32[]{:S(2)}) collective-permute-start(bf16[736,256]{1,0:T(8,128)(2,1)S(1)} %get-tuple-element.77), channel_id=1, source_target_pairs={{0,16},{1,17},{2,18},{3,19},{4,20},{5,21},{6,22},{7,23},{8,24},{9,... | collective-permute-start | bytes 1130504 | tf_op jit(solution)/shard_map/ppermute | solution.py:200
  93.9 2.6 %copy-start.16 = (bf16[2,256,1024]{2,1,0:T(8,128)(2,1)}, bf16[2,256,1024]{2,1,0:T(8,128)(2,1)S(1)}, u32[]{:S(2)}) copy-start(bf16[2,256,1024]{2,1,0:T(8,128)(2,1)S(1)} %collective-permute-done.14.refs_5_) | copy-start | bytes 3145732
  93.9 40.3 %collective-permute-start.19 = (bf16[2,1024,256]{2,1,0:T(8,128)(2,1)S(1)}, bf16[2,1024,256]{2,1,0:T(8,128)(2,1)S(1)}, u32[]{:S(2)}, u32[]{:S(2)}) collective-permute-start(bf16[2,1024,256]{2,1,0:T(8,128)(2,1)S(1)} %pad_maximum_fusion.3.w_own), channel_id=1, source_target_pairs={{0,2},{1,5},{2,0},{3,7},{4,6},{5,1},{6,4},{7,3},{8,10},{9,13},{10,... | collective-permute-start | bytes 3145736 | tf_op jit(solution)/shard_map/ppermute | solution.py:200
  108.4 25.8 %collective-permute-start.20 = (bf16[4,128,512]{2,1,0:T(8,128)(2,1)S(1)}, bf16[4,128,512]{2,1,0:T(8,128)(2,1)S(1)}, u32[]{:S(2)}, u32[]{:S(2)}) collective-permute-start(bf16[4,128,512]{2,1,0:T(8,128)(2,1)S(1)} %get-tuple-element.81), channel_id=1, source_target_pairs={{0,16},{1,17},{2,18},{3,19},{4,20},{5,21},{6,22},{7,23},{8,24},{9,... | collective-permute-start | bytes 1572872 | tf_op jit(solution)/shard_map/ppermute | solution.py:200
  113.2 23.4 %copy-start = (f32[4,128,512]{2,1,0:T(8,128)S(1)}, f32[4,128,512]{2,1,0:T(8,128)}, u32[]{:S(2)}) copy-start(f32[4,128,512]{2,1,0:T(8,128)} %get-tuple-element.75.keep_ref) | copy-start | bytes 3145732
  113.2 11.4 %collective-permute-start.16 = (bf16[6,128,256]{2,1,0:T(8,128)(2,1)S(1)}, bf16[6,128,256]{2,1,0:T(8,128)(2,1)S(1)}, u32[]{:S(2)}, u32[]{:S(2)}) collective-permute-start(bf16[6,128,256]{2,1,0:T(8,128)(2,1)S(1)} %keys_join.1.kv0), channel_id=1, source_target_pairs={{0,2},{1,5},{2,0},{3,7},{4,6},{5,1},{6,4},{7,3},{8,10},{9,13},{10,... | collective-permute-start | bytes 1179656 | tf_op jit(solution)/shard_map/ppermute | solution.py:200
  114.4 10.3 %collective-permute-start.17 = (bf16[6,128,256]{2,1,0:T(8,128)(2,1)S(1)}, bf16[6,128,256]{2,1,0:T(8,128)(2,1)S(1)}, u32[]{:S(2)}, u32[]{:S(2)}) collective-permute-start(bf16[6,128,256]{2,1,0:T(8,128)(2,1)S(1)} %keys_join.1.kv0), channel_id=1, source_target_pairs={{0,4},{1,3},{2,6},{3,1},{4,0},{5,7},{6,2},{7,5},{8,12},{9,11},{10,... | collective-permute-start | bytes 1179656 | tf_op jit(solution)/shard_map/ppermute | solution.py:200
  116.5 17.6 %collective-permute-start.18 = (bf16[6,128,256]{2,1,0:T(8,128)(2,1)S(1)}, bf16[6,128,256]{2,1,0:T(8,128)(2,1)S(1)}, u32[]{:S(2)}, u32[]{:S(2)}) collective-permute-start(bf16[6,128,256]{2,1,0:T(8,128)(2,1)S(1)} %keys_join.1.kv0), channel_id=1, source_target_pairs={{0,6},{1,7},{2,4},{3,5},{4,2},{5,3},{6,0},{7,1},{8,14},{9,15},{10,... | collective-permute-start | bytes 1179656 | tf_op jit(solution)/shard_map/ppermute | solution.py:200
  134.4 26.2 %collective-permute-start.22 = (bf16[4,1024,256]{2,1,0:T(8,128)(2,1)S(1)}, bf16[4,1024,256]{2,1,0:T(8,128)(2,1)S(1)}, u32[]{:S(2)}, u32[]{:S(2)}) collective-permute-start(bf16[4,1024,256]{2,1,0:T(8,128)(2,1)S(1)} %pad_maximum_fusion), channel_id=1, source_target_pairs={{0,4},{1,3},{2,6},{3,1},{4,0},{5,7},{6,2},{7,5},{8,12},{9,11},{10,... | collective-permute-start | bytes 6291464 | tf_op jit(solution)/shard_map/ppermute | solution.py:200
  145.5 13.3 %collective-permute-start.21 = (bf16[512,512]{1,0:T(8,128)(2,1)S(1)}, bf16[512,512]{1,0:T(8,128)(2,1)S(1)}, u32[]{:S(2)}, u32[]{:S(2)}) collective-permute-start(bf16[512,512]{1,0:T(8,128)(2,1)S(1)} %attend.1.own_ref), channel_id=1, source_target_pairs={{0,8},{1,9},{2,10},{3,11},{4,12},{5,13},{6,14},{7,15},{8,0},{9,1},... | collective-permute-start | bytes 1572872 | tf_op jit(solution)/shard_map/ppermute | solution.py:200
  160.6 1.3 copy-start.14
  167.0 2.7 %collective-permute-start.23 = (bf16[4,128,1024]{2,1,0:T(8,128)(2,1)S(1)}, bf16[4,128,1024]{2,1,0:T(8,128)(2,1)S(1)}, u32[]{:S(2)}, u32[]{:S(2)}) collective-permute-start(bf16[4,128,1024]{2,1,0:T(8,128)(2,1)S(1)} %get-tuple-element.88), channel_id=1, source_target_pairs={{0,1},{1,0},{2,3},{3,2},{4,5},{5,4},{6,7},{7,6},{8,9},{9,8},{10,11... | collective-permute-start | bytes 3145736 | tf_op jit(solution)/shard_map/ppermute | solution.py:200
  171.3 15.6 %collective-permute-start.26 = (bf16[128,1024]{1,0:T(8,128)(2,1)S(1)}, bf16[128,1024]{1,0:T(8,128)(2,1)S(1)}, u32[]{:S(2)}, u32[]{:S(2)}) collective-permute-start(bf16[128,1024]{1,0:T(8,128)(2,1)S(1)} %get-tuple-element.94), channel_id=1, source_target_pairs={{0,24},{1,25},{2,26},{3,27},{4,28},{5,29},{6,30},{7,31},{8,0},{9,1... | collective-permute-start | bytes 786440 | tf_op jit(solution)/shard_map/ppermute | solution.py:200
  173.8 15.2 %collective-permute-start.25 = (bf16[128,1024]{1,0:T(8,128)(2,1)S(1)}, bf16[128,1024]{1,0:T(8,128)(2,1)S(1)}, u32[]{:S(2)}, u32[]{:S(2)}) collective-permute-start(bf16[128,1024]{1,0:T(8,128)(2,1)S(1)} %get-tuple-element.95), channel_id=1, source_target_pairs={{0,8},{1,9},{2,10},{3,11},{4,12},{5,13},{6,14},{7,15},{8,16},{9,17... | collective-permute-start | bytes 786440 | tf_op jit(solution)/shard_map/ppermute | solution.py:200
  173.8 22.7 %collective-permute-start.24 = (bf16[128,1024]{1,0:T(8,128)(2,1)S(1)}, bf16[128,1024]{1,0:T(8,128)(2,1)S(1)}, u32[]{:S(2)}, u32[]{:S(2)}) collective-permute-start(bf16[128,1024]{1,0:T(8,128)(2,1)S(1)} %get-tuple-element.93), channel_id=1, source_target_pairs={{0,16},{1,17},{2,18},{3,19},{4,20},{5,21},{6,22},{7,23},{8,24},{9,... | collective-permute-start | bytes 786440 | tf_op jit(solution)/shard_map/ppermute | solution.py:200

commit v10 on v9

--- a/solution.py
+++ b/solution.py
@@ -1,3 +1,5 @@
+import functools
+
 import jax
 import jax.numpy as jnp
 from jax import lax
@@ -347,7 +349,7 @@
 
 
 def queries_part_kernel(where_ref, x0, x1, x2, x3, *refs):
-    keep_ref, send_ref, x_ref = refs[6:]
+    keep_refs, send_ref, x_ref = refs[6:8], refs[8], refs[9]
     assemble(where_ref, (x0, x1, x2, x3), x_ref)
     pieces = [
         [own.at[0], near.at[0], far.at[0], far.at[1]] for own, near, far in (refs[0:3], refs[3:6])
@@ -355,26 +357,28 @@
     total = products(where_ref, x_ref, pieces)
     block = total.shape[0] // LEVELS
     tok = block - REC_PAD
-    width = 4 * HD
+    width = 2 * HD
     for k in range(LEVELS):
         fresh = total[k * block : k * block + tok]
-        keep_ref[k] = fresh[:, :width]
-        send_ref[k] = fresh[:, width:].astype(jnp.bfloat16)
+        for n in range(2):
+            keep_refs[n][k] = fresh[:, n * width : (n + 1) * width]
+            send_ref[n, k] = fresh[:, (2 + n) * width : (3 + n) * width].astype(jnp.bfloat16)
 
 
 def attend_kernel(
-    where_ref, keep_ref, got_ref, cos_ref, sin_ref, kv0, kv1, kv2, kv3, out_ref, query_ref
+    pair, where_ref, keep_ref, got_ref, cos_ref, sin_ref, kv0, kv1, kv2, kv3, out_ref, query_ref
 ):
     level, place, core = where_ref[0], where_ref[1], where_ref[2]
     pieces = (kv0, kv1, kv2, kv3)
     tok = keep_ref.shape[1]
     old = LEVELS // 2
+    heads = query_ref.shape[1]
     for n in range(LEVELS):
         at = jnp.bitwise_xor(level, n)
         block = lax.rem(where_ref[3] + n, LEVELS)
-        total = keep_ref[block] + got_ref[block].astype(jnp.float32)
+        total = keep_ref[block] + got_ref[pair, block].astype(jnp.float32)
         cosine, sine = cos_ref[at][:tok], sin_ref[at][:tok]
-        for h in range(4):
+        for h in range(heads):
             head = turned(total[:, h * HD : (h + 1) * HD], cosine, sine)
             query_ref[at, h] = head.astype(jnp.bfloat16)
     row = lax.broadcasted_iota(jnp.int32, (tok, tok), 0)
@@ -382,7 +386,7 @@
     scale = HD ** (-0.5) * 1.4426950408889634
     for i in range(LEVELS):
         count = (old + i + 1) * tok
-        queries = query_ref[i].reshape(4 * tok, HD)
+        queries = query_ref[i].reshape(heads * tok, HD)
         scores = []
         best = None
         for j in range(PLANE):
@@ -394,7 +398,7 @@
                 allowed = col <= row
             else:
                 allowed = jnp.broadcast_to(place_of(j, place, core), (tok, tok)) < place
-            allowed = jnp.concatenate([allowed] * 4, axis=0)
+            allowed = jnp.concatenate([allowed] * heads, axis=0)
             last = jnp.where(allowed, raw[:, count - tok :], NEG_FILL)
             raw = jnp.concatenate([raw[:, : count - tok], last], axis=1)
             top = jnp.max(raw, axis=1, keepdims=True)
@@ -409,30 +413,47 @@
                 weights.astype(jnp.bfloat16), values, preferred_element_type=jnp.float32
             )
         result = (accum / total).astype(jnp.bfloat16)
-        for h in range(4):
+        for h in range(heads):
             out_ref[i * tok : (i + 1) * tok, h * HD : (h + 1) * HD] = result[
                 h * tok : (h + 1) * tok
             ]
 
 
-def output_kernel(where_ref, own_ref, next_ref, w_own, w_near, w_far, mine_ref, other_ref, x_ref):
-    level, place, core = where_ref[0], where_ref[1], where_ref[2]
-    depth = own_ref.shape[1]
-    width = w_own.shape[2]
+def output_kernel(where_ref, *refs):
+    heads, weights, (mine_ref, other_ref, x_ref) = refs[:4], refs[4:-3], refs[-3:]
+    level, core = where_ref[0], where_ref[2]
+    depth = heads[0].shape[1]
+    width = weights[0].shape[2]
     tok = mine_ref.shape[1]
-    x_ref[:, pl.ds(pl.multiple_of(lax.rem(level, 2) * depth, depth), depth)] = own_ref[...]
-    x_ref[:, pl.ds(pl.multiple_of(lax.rem(level + 1, 2) * depth, depth), depth)] = next_ref[...]
+    for n, ref in enumerate(heads):
+        at = 2 * lax.rem(level + n // 2, 2) + n % 2
+        x_ref[:, pl.ds(pl.multiple_of(at * depth, depth), depth)] = ref[...]
     swap = jnp.where(core == level // 2, 0, 1)
     for s, out_ref in enumerate((mine_ref, other_ref)):
         i = jnp.bitwise_xor(swap, s)
+        for j, piece in enumerate(weights):
+            slot = (0, 2, 1, 3)[j] if s else j
+            part = jnp.dot(x_ref[...], piece[i], preferred_element_type=jnp.float32)
+            for t in range(LEVELS):
+                out_ref[
+                    lax.rem(t + LEVELS - level, LEVELS), :, slot * width : (slot + 1) * width
+                ] = part[t * tok : (t + 1) * tok].astype(out_ref.dtype)
+
+
+def finish_kernel(where_ref, own, first, second, third, out_ref):
+    level, place, core = where_ref[0], where_ref[1], where_ref[2]
+    half = out_ref.shape[1] // 2
+    width = half // PLANE
+    sums = (
+        own[...] + second[...].astype(jnp.float32),
+        first[...].astype(jnp.float32) + third[...].astype(jnp.float32),
+    )
+    for steps, total in enumerate(sums):
         for j in range(PLANE):
-            weights = (w_own.at[i], w_near.at[i], w_far.at[i], w_far.at[2 + i])[j]
-            part = jnp.dot(x_ref[...], weights[...], preferred_element_type=jnp.float32)
-            to = pl.multiple_of(place_of(j, place, core) * width, width)
-            for t in range(LEVELS):
-                out_ref[lax.rem(t + LEVELS - level, LEVELS), :, pl.ds(to, width)] = part[
-                    t * tok : (t + 1) * tok
-                ].astype(out_ref.dtype)
+            at = lax.rem(level + steps, 2) * half + place_of(j, place, core) * width
+            out_ref[:, pl.ds(pl.multiple_of(at, width), width)] = total[
+                :, j * width : (j + 1) * width
+            ].astype(out_ref.dtype)
 
 
 SMEM = pl.BlockSpec(memory_space=pltpu.SMEM)
@@ -510,7 +531,6 @@
     out_own, out_give = (
         lax.dynamic_slice_in_dim(w_out, at * out_rows, out_rows, 0) for at in (half_at, 1 - half_at)
     )
-    out_half = out_rows // 2
 
     crossed = permuted(normed, lambda z, p, c: (z ^ 2, p, 1 - c) if c == 1 - z // 2 else None)
     shown = permuted(pictures, lambda z, p, c: (2 * c + p // 2, z, p % 2))
@@ -522,24 +542,18 @@
     keys = jnp.stack([key_own[:depth], key_next[:depth]])
     old_own, old_next = key_own[depth:], key_next[depth:]
     keys_near = to_near(keys)
-    crossed, shown = lax.optimization_barrier((crossed, shown))
+    crossed, shown, out_give = lax.optimization_barrier((crossed, shown, out_give))
     held = jnp.concatenate([jnp.where(own_first, normed, crossed), shown], axis=0)
     next_rows = across(held, 1)
-    held_other, out_give, keys_near = lax.optimization_barrier(
-        (other_core(held), out_give, keys_near)
-    )
-    out_got0 = across(out_give[:out_half], 2)
+    held_other = other_core(held)
+    next_other = other_core(next_rows)
+    out_got = across(out_give, 2)
     keys_far = to_far(jnp.concatenate([keys, keys_near], axis=0))
     next_near = to_near(query_next)
-    next_rows, held_other, keys_far, query_far, next_near, out_got0, out_give = (
-        lax.optimization_barrier(
-            (next_rows, held_other, keys_far, query_far, next_near, out_got0, out_give)
-        )
-    )
-    out_got1 = across(out_give[out_half:], 2)
+    next_other, keys_far, query_far, next_near, out_got = lax.optimization_barrier(
+        (next_other, keys_far, query_far, next_near, out_got)
+    )
     next_far = to_far(jnp.concatenate([query_next, next_near], axis=0))
-    next_other = other_core(next_rows)
-    next_other, out_got1 = lax.optimization_barrier((next_other, out_got1))
     parts = (held, next_rows, held_other, next_other)
 
     half = HD // 2
@@ -567,18 +581,16 @@
         compiler_params=PARAMS,
         name="keys_part",
     )(where, *parts, keys, keys_near, keys_far, old_own, old_next)
-    send, *parts = lax.optimization_barrier((send, *parts))
-    out_pair = jnp.stack([out_own, jnp.concatenate([out_got0, out_got1], axis=0)])
+    send, out_got, *parts = lax.optimization_barrier((send, out_got, *parts))
+    out_pair = jnp.stack([out_own, out_got])
     out_pair, next_far = lax.optimization_barrier((out_pair, next_far))
     out_near = to_near(out_pair)
-    q_keep, q_send = pl.pallas_call(
+    *q_keep, q_send = pl.pallas_call(
         queries_part_kernel,
-        out_shape=(
-            shaped((LEVELS, tok, 4 * HD), jnp.float32),
-            shaped((LEVELS, tok, 4 * HD)),
-        ),
+        out_shape=(shaped((LEVELS, tok, 2 * HD), jnp.float32),) * 2
+        + (shaped((2, LEVELS, tok, 2 * HD)),),
         in_specs=[SMEM] + [VMEM] * 10,
-        out_specs=(VMEM, VMEM),
+        out_specs=(VMEM,) * 3,
         scratch_shapes=[pltpu.VMEM((all_rows, width), jnp.bfloat16)],
         compiler_params=PARAMS,
         name="queries_part",
@@ -596,20 +608,24 @@
     kv_near, kv_far = to_near(kv), to_far(kv)
     kv_both = permuted(kv, lambda z, p, c: (z, p ^ 3, c))
 
-    kv_near, kv_far, kv_both, out_near, got_queries = lax.optimization_barrier(
-        (kv_near, kv_far, kv_both, out_near, across(q_send, 2))
-    )
-    out_far = to_far(jnp.concatenate([out_pair, out_near], axis=0))
-
-    attended = pl.pallas_call(
-        attend_kernel,
-        out_shape=shaped((LEVELS * tok, 4 * HD)),
-        in_specs=[SMEM] + [VMEM] * 8,
-        out_specs=VMEM,
-        scratch_shapes=[pltpu.VMEM((LEVELS, 4, tok, HD), jnp.bfloat16)],
-        compiler_params=PARAMS,
-        name="attend",
-    )(where, q_keep, got_queries, cosine, sine, kv, kv_near, kv_far, kv_both)
+    kv_near, kv_far, kv_both, out_near, out_pair, got_queries = lax.optimization_barrier(
+        (kv_near, kv_far, kv_both, out_near, out_pair, across(q_send, 2))
+    )
+    out_far, out_both = to_far(out_pair), to_far(out_near)
+
+    attended = [
+        pl.pallas_call(
+            functools.partial(attend_kernel, pair),
+            out_shape=shaped((LEVELS * tok, 2 * HD)),
+            in_specs=[SMEM] + [VMEM] * 8,
+            out_specs=VMEM,
+            scratch_shapes=[pltpu.VMEM((LEVELS, 2, tok, HD), jnp.bfloat16)],
+            compiler_params=PARAMS,
+            name="attend",
+        )(where, q_keep[pair], got_queries, cosine, sine, kv, kv_near, kv_far, kv_both)
+        for pair in range(2)
+    ]
+    attended += [across(each, 1) for each in attended]
 
     wide_cols = PLANE * w_out.shape[1]
     mine, other = pl.pallas_call(
@@ -618,22 +634,23 @@
             shaped((LEVELS, tok, wide_cols), jnp.float32),
             shaped((LEVELS, tok, wide_cols)),
         ),
-        in_specs=[SMEM] + [VMEM] * 5,
+        in_specs=[SMEM] + [VMEM] * 8,
         out_specs=(VMEM, VMEM),
         scratch_shapes=[pltpu.VMEM((LEVELS * tok, out_rows), jnp.bfloat16)],
         compiler_params=PARAMS,
         name="output",
-    )(where, attended, across(attended, 1), out_pair, out_near, out_far)
+    )(where, *attended, out_pair, out_near, out_far, out_both)
     got = other_core(other)
-
-    def block_for(steps):
-        return mine[steps] + got[steps].astype(jnp.float32)
-
-    second, first, third = (up(block_for(d).astype(jnp.bfloat16), d) for d in (2, 1, 3))
-    same = (block_for(0) + second.astype(jnp.float32)).astype(jnp.bfloat16)
-    cross = (first.astype(jnp.float32) + third.astype(jnp.float32)).astype(jnp.bfloat16)
-    even = level % 2 == 0
-    return jnp.concatenate([jnp.where(even, same, cross), jnp.where(even, cross, same)], axis=1)
+    block = [mine[d] + got[d].astype(jnp.float32) for d in range(LEVELS)]
+    shares = [up(block[d].astype(jnp.bfloat16), d) for d in range(1, LEVELS)]
+    return pl.pallas_call(
+        finish_kernel,
+        out_shape=shaped((tok, width)),
+        in_specs=[SMEM] + [VMEM] * 4,
+        out_specs=VMEM,
+        compiler_params=PARAMS,
+        name="finish",
+    )(where, block[0], *shares)
 
 
 def solution(mesh):

time: 202 us -> 196 us (0.970); the launches traced: 199 us -> 195 us
  starting transfers between devices: 55.8 us -> 42.9 us
  waiting for transfers between devices: 97.5 us -> 110 us
    ppermute x27 -> x28, starting transfers between devices: 55.8 us -> 42.9 us  [permuted(): return lax.ppermute(value, ('seq', 'head'), perm)]
    ppermute x27 -> x28, waiting for transfers between devices: 97.5 us -> 110 us  [permuted(): return lax.ppermute(value, ('seq', 'head'), perm)]
    pallas_call x2 -> x4, Pallas kernels: 14.1 us -> 15.5 us  [the longest x2 9.5 us: by_levels(): pl.pallas_call(functools.partial(attend_kernel, pair), out_shape=shaped((...]
  transfers between devices with their start and end apart: 27 -> 28, of which waited for: 16 -> 17; matrix products, arithmetic and copies ran while one was open for 4% -> 4% of each run, Pallas kernels for 9% -> 9%
where the time goes in v10:
time: 196 us; the launch traced here: 195 us
  waiting for transfers between devices  110 us (56%)
  starting transfers between devices  42.9 us (22%)
  Pallas kernels  23.6 us (12%)
  other arithmetic  11.3 us (6%)
  local copies, waits for them, and re-layouts  4.3 us (2%)
  blocking collectives  2.46 us (1%)
    ppermute x28, waiting for transfers between devices, permuted(): return lax.ppermute(value, ('seq', 'head'), perm)  110 us
    ppermute x28, starting transfers between devices, permuted(): return lax.ppermute(value, ('seq', 'head'), perm)  42.9 us
    pallas_call x2, Pallas kernels, by_levels(): pl.pallas_call(functools.partial(attend_kernel, pair), out_shape=shaped((...  9.5 us
    pallas_call x1, Pallas kernels, by_levels(): pl.pallas_call(queries_part_kernel, out_shape=(shaped((LEVELS, tok, 2 * H...  4.56 us
  transfers between devices with their start and end apart: 28, of which 17 were waited for; matrix products, arithmetic and copies ran while one was open for 4% of the time, Pallas kernels for 9%

profile of v10, /device:TPU:8, one launch (start us, length us, event | category | flops | bytes accessed | tf_op | source)
XLA Modules:
  0.0 195.4 jit_solution(3440023384847050695)
XLA Ops:
  0.1 1.2 fusion.3
  1.3 1.4 fusion
  2.7 2.5 %all-reduce.1 = (f32[144]{0:T(256)S(1)}, f32[32]{0:T(128)S(1)}) all-reduce(f32[144]{0:T(256)S(1)} %fusion, f32[32]{0:T(128)S(1)} %fusion.3), channel_id=1, replica_groups=mesh['seq'=16,'head'=2] {'head'}, use_global_device_ids=true, to_apply=%region_1.2 | all-reduce | flops 176 | bytes 1408 | tf_op jit(solution)/shard_map/psum | solution.py:524
  5.1 0.7 dynamic_slice.9
  5.8 2.3 %fusion.2 = bf16[144,2048]{1,0:T(8,128)(2,1)} fusion(f32[2048]{0:T(1024)S(1)} %dynamic_slice.9, f32[144]{0:T(256)S(1)} %add_rsqrt_fusion, bf16[8,2048]{1,0:T(8,128)(2,1)} %param.21, bf16[128,2048]{1,0:T(8,128)(2,1)} %param.12, bf16[144]{0:T(256)(128)(2,1)S(1)} %pad.26.clone), kind=kLoop, calls=%fused_computation.4 | loop fusion | flops 2654208 | bytes 1155936 | tf_op jit(solution)/shard_map/convert_element_type | solution.py:33
  8.1 1.5 collective-permute-start
  9.6 0.8 fusion.5
  10.4 3.3 %collective-permute-start.1 = (bf16[32,2048]{1,0:T(8,128)(2,1)}, bf16[32,2048]{1,0:T(8,128)(2,1)}, u32[]{:S(2)}, u32[]{:S(2)}) collective-permute-start(bf16[32,2048]{1,0:T(8,128)(2,1)} %fusion.5), channel_id=1, source_target_pairs={{0,0},{1,16},{2,1},{3,17},{4,8},{5,24},{6,9},{7,25},{8,2},{9,18},{... | collective-permute-start | bytes 393224 | tf_op jit(solution)/shard_map/ppermute | solution.py:202
  14.0 1.0 pack.1
  15.1 3.8 %collective-permute-start.8 = (bf16[1,256,1024]{2,1,0:T(8,128)(2,1)S(1)}, bf16[1,256,1024]{2,1,0:T(8,128)(2,1)S(1)}, u32[]{:S(2)}, u32[]{:S(2)}) collective-permute-start(bf16[1,256,1024]{2,1,0:T(8,128)(2,1)S(1)} %get-tuple-element.50.refs_0_), channel_id=1, source_target_pairs={{0,2},{1,5},{2,0},{3,7},{4,6},{5,1},{6,4},{7,3},{8,10},{9,13},{10,... | collective-permute-start | bytes 1572872 | tf_op jit(solution)/shard_map/ppermute | solution.py:202
  19.0 1.4 dynamic-slice_bitcast_fusion
  20.4 10.2 %collective-permute-done.2 = bf16[336,512]{1,0:T(8,128)(2,1)S(1)} collective-permute-done((bf16[336,512]{1,0:T(8,128)(2,1)S(1)}, bf16[336,512]{1,0:T(8,128)(2,1)S(1)}, u32[]{:S(2)}, u32[]{:S(2)}) %collective-permute-start.2) | collective-permute-done | bytes 344096 | tf_op jit(solution)/shard_map/ppermute | solution.py:202
  30.6 4.4 %collective-permute-start.6 = (bf16[2,256,512]{2,1,0:T(8,128)(2,1)S(1)}, bf16[2,256,512]{2,1,0:T(8,128)(2,1)S(1)}, u32[]{:S(2)}, u32[]{:S(2)}) collective-permute-start(bf16[2,256,512]{2,1,0:T(8,128)(2,1)S(1)} %pad_maximum_fusion.5.own), channel_id=1, source_target_pairs={{0,2},{1,5},{2,0},{3,7},{4,6},{5,1},{6,4},{7,3},{8,10},{9,13},{10,... | collective-permute-start | bytes 1572872 | tf_op jit(solution)/shard_map/ppermute | solution.py:202
  35.0 0.5 broadcast_select_fusion
  35.5 1.0 pad_maximum_fusion.4.x0
  36.5 2.5 %collective-permute-start.3 = (bf16[176,2048]{1,0:T(8,128)(2,1)S(1)}, bf16[176,2048]{1,0:T(8,128)(2,1)S(1)}, u32[]{:S(2)}, u32[]{:S(2)}) collective-permute-start(bf16[176,2048]{1,0:T(8,128)(2,1)S(1)} %pad_maximum_fusion.4.x0), channel_id=1, source_target_pairs={{0,8},{1,9},{2,10},{3,11},{4,12},{5,13},{6,14},{7,15},{8,0},{9,1},... | collective-permute-start | bytes 2162696 | tf_op jit(solution)/shard_map/ppermute | solution.py:202
  39.0 0.1 pad_maximum_fusion.1
  39.2 0.1 collective-permute-start.10
  39.3 4.5 %collective-permute-done.6.near = bf16[2,256,512]{2,1,0:T(8,128)(2,1)S(1)} collective-permute-done((bf16[2,256,512]{2,1,0:T(8,128)(2,1)S(1)}, bf16[2,256,512]{2,1,0:T(8,128)(2,1)S(1)}, u32[]{:S(2)}, u32[]{:S(2)}) %collective-permute-start.6) | collective-permute-done | bytes 524320 | tf_op jit(solution)/shard_map/ppermute | solution.py:202
  43.8 0.1 pad_maximum_fusion
  44.0 12.1 %collective-permute-done.3.x1 = bf16[176,2048]{1,0:T(8,128)(2,1)S(1)} collective-permute-done((bf16[176,2048]{1,0:T(8,128)(2,1)S(1)}, bf16[176,2048]{1,0:T(8,128)(2,1)S(1)}, u32[]{:S(2)}, u32[]{:S(2)}) %collective-permute-start.3) | collective-permute-done | bytes 720928 | tf_op jit(solution)/shard_map/ppermute | solution.py:202
  56.1 1.6 collective-permute-start.12
  57.7 12.7 %collective-permute-done.10.refs_3_ = bf16[1,256,1024]{2,1,0:T(8,128)(2,1)S(1)} collective-permute-done((bf16[1,256,1024]{2,1,0:T(8,128)(2,1)S(1)}, bf16[1,256,1024]{2,1,0:T(8,128)(2,1)S(1)}, u32[]{:S(2)}, u32[]{:S(2)}) %collective-permute-start.10) | collective-permute-done | bytes 524320 | tf_op jit(solution)/shard_map/ppermute | solution.py:202
  70.4 0.7 collective-permute-start.11
  71.1 9.8 %collective-permute-done.12 = bf16[1024,256]{1,0:T(8,128)(2,1)S(1)} collective-permute-done((bf16[1024,256]{1,0:T(8,128)(2,1)S(1)}, bf16[1024,256]{1,0:T(8,128)(2,1)S(1)}, u32[]{:S(2)}, u32[]{:S(2)}) %collective-permute-start.12) | collective-permute-done | bytes 524320 | tf_op jit(solution)/shard_map/ppermute | solution.py:202
  80.9 0.1 pad_maximum_fusion.3
  81.0 2.8 %collective-permute-start.13 = (bf16[2,256,1024]{2,1,0:T(8,128)(2,1)S(1)}, bf16[2,256,1024]{2,1,0:T(8,128)(2,1)}, u32[]{:S(2)}, u32[]{:S(2)}) collective-permute-start(bf16[2,256,1024]{2,1,0:T(8,128)(2,1)S(1)} %pad_maximum_fusion.3), channel_id=1, source_target_pairs={{0,4},{1,3},{2,6},{3,1},{4,0},{5,7},{6,2},{7,5},{8,12},{9,11},{10,... | collective-permute-start | bytes 3145736 | tf_op jit(solution)/shard_map/ppermute | solution.py:202
  84.0 0.9 slice.39.old1
  84.9 1.1 collective-permute-done.4.x2
  86.0 2.1 %keys_part.1 = (f32[576,256]{1,0:T(8,128)S(1)}, bf16[736,256]{1,0:T(8,128)(2,1)S(1)}) custom-call(s32[5]{0:T(128)S(1)} %stack.41.where_ref, bf16[176,2048]{1,0:T(8,128)(2,1)S(1)} %pad_maximum_fusion.4.x0, bf16[176,2048]{1,0:T(8,128)(2,1)S(1)} %collective-permute-done.3.x1, bf16[176,2048]{1,0:T(8,128)(2,1)S(1)} %collective-permute-done.4.x2, ...), custom_call_target="tpu_custom_call" | custom-call | tf_op jit(solution)/shard_map/keys_part/pallas_call | solution.py:572
  88.1 3.4 %collective-permute-start.14 = (bf16[736,256]{1,0:T(8,128)(2,1)S(1)}, bf16[736,256]{1,0:T(8,128)(2,1)S(1)}, u32[]{:S(2)}, u32[]{:S(2)}) collective-permute-start(bf16[736,256]{1,0:T(8,128)(2,1)S(1)} %get-tuple-element.69), channel_id=1, source_target_pairs={{0,16},{1,17},{2,18},{3,19},{4,20},{5,21},{6,22},{7,23},{8,24},{9,... | collective-permute-start | bytes 1130504 | tf_op jit(solution)/shard_map/ppermute | solution.py:202
  91.6 0.1 pad_maximum_fusion.2.refs_4_
  91.7 5.0 %collective-permute-done.13.refs_5_ = bf16[2,256,1024]{2,1,0:T(8,128)(2,1)} collective-permute-done((bf16[2,256,1024]{2,1,0:T(8,128)(2,1)S(1)}, bf16[2,256,1024]{2,1,0:T(8,128)(2,1)}, u32[]{:S(2)}, u32[]{:S(2)}) %collective-permute-start.13) | collective-permute-done | bytes 1048608 | tf_op jit(solution)/shard_map/ppermute | solution.py:202
  96.7 1.2 collective-permute-start.18
  97.9 1.4 fusion.9
  99.4 4.6 %queries_part.1 = (f32[4,128,256]{2,1,0:T(8,128)S(1)}, f32[4,128,256]{2,1,0:T(8,128)S(1)}, bf16[2,4,128,256]{3,2,1,0:T(8,128)(2,1)S(1)}) custom-call(s32[5]{0:T(128)S(1)} %stack.41.where_ref, bf16[176,2048]{1,0:T(8,128)(2,1)S(1)} %pad_maximum_fusion.4.x0, bf16[176,2048]{1,0:T(8,128)(2,1)S(1)} %collective-permute-done.3.x1, ...), custom_call_target="tpu_custom_call" | custom-call | tf_op jit(solution)/shard_map/queries_part/pallas_call | solution.py:588
  103.9 1.5 collective-permute-done.14.got_ref
  105.4 3.4 %collective-permute-start.19 = (bf16[2,4,128,256]{3,2,1,0:T(8,128)(2,1)S(1)}, bf16[2,4,128,256]{3,2,1,0:T(8,128)(2,1)S(1)}, u32[]{:S(2)}, u32[]{:S(2)}) collective-permute-start(bf16[2,4,128,256]{3,2,1,0:T(8,128)(2,1)S(1)} %get-tuple-element.73), channel_id=1, source_target_pairs={{0,16},{1,17},{2,18},{3,19},{4,20},{5,21},{6,22},{7,23},{8,24},{9,... | collective-permute-start | bytes 1572872 | tf_op jit(solution)/shard_map/ppermute | solution.py:202
  108.8 0.2 pad_maximum_fusion.6.cos_ref
  109.0 0.2 pad_maximum_fusion.7.sin_ref
  109.1 1.0 keys_join.1.kv0
  110.2 1.3 collective-permute-start.15
  111.5 1.2 collective-permute-start.16
  112.7 1.1 collective-permute-start.17
  113.7 8.1 %collective-permute-done.15.kv1 = bf16[6,128,256]{2,1,0:T(8,128)(2,1)S(1)} collective-permute-done((bf16[6,128,256]{2,1,0:T(8,128)(2,1)S(1)}, bf16[6,128,256]{2,1,0:T(8,128)(2,1)S(1)}, u32[]{:S(2)}, u32[]{:S(2)}) %collective-permute-start.15) | collective-permute-done | bytes 393248 | tf_op jit(solution)/shard_map/ppermute | solution.py:202
  121.8 9.1 %collective-permute-done.17.kv3 = bf16[6,128,256]{2,1,0:T(8,128)(2,1)S(1)} collective-permute-done((bf16[6,128,256]{2,1,0:T(8,128)(2,1)S(1)}, bf16[6,128,256]{2,1,0:T(8,128)(2,1)S(1)}, u32[]{:S(2)}, u32[]{:S(2)}) %collective-permute-start.17) | collective-permute-done | bytes 393248 | tf_op jit(solution)/shard_map/ppermute | solution.py:202
  130.9 2.1 %collective-permute-start.22 = (bf16[2,1024,256]{2,1,0:T(8,128)(2,1)S(1)}, bf16[2,1024,256]{2,1,0:T(8,128)(2,1)S(1)}, u32[]{:S(2)}, u32[]{:S(2)}) collective-permute-start(bf16[2,1024,256]{2,1,0:T(8,128)(2,1)S(1)} %pad_maximum_fusion.2.refs_4_), channel_id=1, source_target_pairs={{0,4},{1,3},{2,6},{3,1},{4,0},{5,7},{6,2},{7,5},{8,12},{9,11},{10,... | collective-permute-start | bytes 3145736 | tf_op jit(solution)/shard_map/ppermute | solution.py:202
  133.0 4.7 %attend.2.refs_0_ = bf16[512,256]{1,0:T(8,128)(2,1)S(1)} custom-call(s32[5]{0:T(128)S(1)} %stack.41.where_ref, f32[4,128,256]{2,1,0:T(8,128)S(1)} %get-tuple-element.67.keep_ref, bf16[2,4,128,256]{3,2,1,0:T(8,128)(2,1)S(1)} %collective-permute-done.19.got_ref, f32[4,192,128]{2,1,0:T(8,128)S(1)} %pad_maximum_fusion.6.cos_ref, ...), custom_call_target="tpu_custom_call" | custom-call | tf_op jit(solution)/shard_map/attend/pallas_call | solution.py:617
  137.7 4.8 %attend.3.refs_1_ = bf16[512,256]{1,0:T(8,128)(2,1)S(1)} custom-call(s32[5]{0:T(128)S(1)} %stack.41.where_ref, f32[4,128,256]{2,1,0:T(8,128)S(1)} %get-tuple-element.78.keep_ref, bf16[2,4,128,256]{3,2,1,0:T(8,128)(2,1)S(1)} %collective-permute-done.19.got_ref, f32[4,192,128]{2,1,0:T(8,128)S(1)} %pad_maximum_fusion.6.cos_ref, ...), custom_call_target="tpu_custom_call" | custom-call | tf_op jit(solution)/shard_map/attend/pallas_call | solution.py:617
  142.6 2.6 %collective-permute-start.20 = (bf16[512,256]{1,0:T(8,128)(2,1)S(1)}, bf16[512,256]{1,0:T(8,128)(2,1)S(1)}, u32[]{:S(2)}, u32[]{:S(2)}) collective-permute-start(bf16[512,256]{1,0:T(8,128)(2,1)S(1)} %attend.2.refs_0_), channel_id=1, source_target_pairs={{0,8},{1,9},{2,10},{3,11},{4,12},{5,13},{6,14},{7,15},{8,0},{9,1},... | collective-permute-start | bytes 786440 | tf_op jit(solution)/shard_map/ppermute | solution.py:202
  145.3 7.1 %collective-permute-done.20.refs_2_ = bf16[512,256]{1,0:T(8,128)(2,1)S(1)} collective-permute-done((bf16[512,256]{1,0:T(8,128)(2,1)S(1)}, bf16[512,256]{1,0:T(8,128)(2,1)S(1)}, u32[]{:S(2)}, u32[]{:S(2)}) %collective-permute-start.20) | collective-permute-done | bytes 262176 | tf_op jit(solution)/shard_map/ppermute | solution.py:202
  152.4 4.4 %collective-permute-done.21.refs_3_ = bf16[512,256]{1,0:T(8,128)(2,1)S(1)} collective-permute-done((bf16[512,256]{1,0:T(8,128)(2,1)S(1)}, bf16[512,256]{1,0:T(8,128)(2,1)S(1)}, u32[]{:S(2)}, u32[]{:S(2)}) %collective-permute-start.21) | collective-permute-done | bytes 262176 | tf_op jit(solution)/shard_map/ppermute | solution.py:202
  156.8 0.3 collective-permute-done.23.refs_7_
  157.0 1.0 copy-done.10
  158.0 3.9 %output.1 = (f32[4,128,1024]{2,1,0:T(8,128)}, bf16[4,128,1024]{2,1,0:T(8,128)(2,1)S(1)}) custom-call(s32[5]{0:T(128)S(1)} %stack.41.where_ref, bf16[512,256]{1,0:T(8,128)(2,1)S(1)} %attend.2.refs_0_, bf16[512,256]{1,0:T(8,128)(2,1)S(1)} %attend.3.refs_1_, bf16[512,256]{1,0:T(8,128)(2,1)S(1)} %collective-permute-done.20.refs_2_, ...), custom_call_target="tpu_custom_call" | custom-call | tf_op jit(solution)/shard_map/output/pallas_call | solution.py:631
  161.9 2.7 %collective-permute-done.24 = bf16[4,128,1024]{2,1,0:T(8,128)(2,1)S(1)} collective-permute-done((bf16[4,128,1024]{2,1,0:T(8,128)(2,1)S(1)}, bf16[4,128,1024]{2,1,0:T(8,128)(2,1)S(1)}, u32[]{:S(2)}, u32[]{:S(2)}) %collective-permute-start.24) | collective-permute-done | bytes 1048608 | tf_op jit(solution)/shard_map/ppermute | solution.py:202
  164.6 1.9 fusion.8
  166.5 1.4 collective-permute-start.25
  167.9 3.7 %collective-permute-start.26 = (bf16[128,1024]{1,0:T(8,128)(2,1)S(1)}, bf16[128,1024]{1,0:T(8,128)(2,1)S(1)}, u32[]{:S(2)}, u32[]{:S(2)}) collective-permute-start(bf16[128,1024]{1,0:T(8,128)(2,1)S(1)} %get-tuple-element.86), channel_id=1, source_target_pairs={{0,16},{1,17},{2,18},{3,19},{4,20},{5,21},{6,22},{7,23},{8,24},{9,... | collective-permute-start | bytes 786440 | tf_op jit(solution)/shard_map/ppermute | solution.py:202
  171.5 0.4 collective-permute-start.27
  171.9 4.3 %collective-permute-done.25.first = bf16[128,1024]{1,0:T(8,128)(2,1)S(1)} collective-permute-done((bf16[128,1024]{1,0:T(8,128)(2,1)S(1)}, bf16[128,1024]{1,0:T(8,128)(2,1)S(1)}, u32[]{:S(2)}, u32[]{:S(2)}) %collective-permute-start.25) | collective-permute-done | bytes 262176 | tf_op jit(solution)/shard_map/ppermute | solution.py:202
  176.2 14.3 %collective-permute-done.26.second = bf16[128,1024]{1,0:T(8,128)(2,1)S(1)} collective-permute-done((bf16[128,1024]{1,0:T(8,128)(2,1)S(1)}, bf16[128,1024]{1,0:T(8,128)(2,1)S(1)}, u32[]{:S(2)}, u32[]{:S(2)}) %collective-permute-start.26) | collective-permute-done | bytes 262176 | tf_op jit(solution)/shard_map/ppermute | solution.py:202
  190.6 3.3 %collective-permute-done.27.third = bf16[128,1024]{1,0:T(8,128)(2,1)S(1)} collective-permute-done((bf16[128,1024]{1,0:T(8,128)(2,1)S(1)}, bf16[128,1024]{1,0:T(8,128)(2,1)S(1)}, u32[]{:S(2)}, u32[]{:S(2)}) %collective-permute-start.27) | collective-permute-done | bytes 262176 | tf_op jit(solution)/shard_map/ppermute | solution.py:202
  193.9 1.4 finish.1
  (65 shorter events, 0.9 us)
Async XLA Ops:
  0.0 9.6 %copy-start.11 = (bf16[32,2048]{1,0:T(8,128)(2,1)S(1)}, bf16[32,2048]{1,0:T(8,128)(2,1)}, u32[]{:S(2)}) copy-start(bf16[32,2048]{1,0:T(8,128)(2,1)} %param.13) | copy-start | bytes 393220
  0.0 13.7 %copy-start.14 = (s32[8]{0:T(128)S(1)}, s32[8]{0:T(128)}, u32[]{:S(2)}) copy-start(s32[8]{0:T(128)} %param.22) | copy-start | bytes 100
  0.0 13.9 %copy-start.1 = (bf16[256,2048]{1,0:T(8,128)(2,1)S(1)}, bf16[256,2048]{1,0:T(8,128)(2,1)}, u32[]{:S(2)}) copy-start(bf16[256,2048]{1,0:T(8,128)(2,1)} %refs_0_.1) | copy-start | bytes 3145732
  0.0 13.9 %copy-start.2 = (bf16[256,512]{1,0:T(8,128)(2,1)S(1)}, bf16[256,512]{1,0:T(8,128)(2,1)}, u32[]{:S(2)}) copy-start(bf16[256,512]{1,0:T(8,128)(2,1)} %refs_1_.1) | copy-start | bytes 786436
  0.0 13.9 %copy-start.3 = (bf16[256,512]{1,0:T(8,128)(2,1)S(1)}, bf16[256,512]{1,0:T(8,128)(2,1)}, u32[]{:S(2)}) copy-start(bf16[256,512]{1,0:T(8,128)(2,1)} %refs_2_.1) | copy-start | bytes 786436
  0.0 13.9 %copy-start.4 = (bf16[64,512]{1,0:T(8,128)(2,1)S(1)}, bf16[64,512]{1,0:T(8,128)(2,1)}, u32[]{:S(2)}) copy-start(bf16[64,512]{1,0:T(8,128)(2,1)} %refs_3_.1) | copy-start | bytes 196612
  0.0 13.9 %copy-start.5 = (bf16[64,512]{1,0:T(8,128)(2,1)S(1)}, bf16[64,512]{1,0:T(8,128)(2,1)}, u32[]{:S(2)}) copy-start(bf16[64,512]{1,0:T(8,128)(2,1)} %refs_4_.1) | copy-start | bytes 196612
  8.1 26.9 %collective-permute-start = (bf16[144,2048]{1,0:T(8,128)(2,1)}, bf16[144,2048]{1,0:T(8,128)(2,1)}, u32[]{:S(2)}, u32[]{:S(2)}) collective-permute-start(bf16[144,2048]{1,0:T(8,128)(2,1)} %fusion.2), channel_id=1, source_target_pairs={{1,16},{3,18},{5,20},{7,22},{9,24},{11,26},{13,28},{15,30},{16,1},... | collective-permute-start | bytes 1769480 | tf_op jit(solution)/shard_map/ppermute | solution.py:202
  10.4 10.0 %collective-permute-start.1 = (bf16[32,2048]{1,0:T(8,128)(2,1)}, bf16[32,2048]{1,0:T(8,128)(2,1)}, u32[]{:S(2)}, u32[]{:S(2)}) collective-permute-start(bf16[32,2048]{1,0:T(8,128)(2,1)} %fusion.5), channel_id=1, source_target_pairs={{0,0},{1,16},{2,1},{3,17},{4,8},{5,24},{6,9},{7,25},{8,2},{9,18},{... | collective-permute-start | bytes 393224 | tf_op jit(solution)/shard_map/ppermute | solution.py:202
  15.0 15.5 %collective-permute-start.2 = (bf16[336,512]{1,0:T(8,128)(2,1)S(1)}, bf16[336,512]{1,0:T(8,128)(2,1)S(1)}, u32[]{:S(2)}, u32[]{:S(2)}) collective-permute-start(bf16[336,512]{1,0:T(8,128)(2,1)S(1)} %get-tuple-element.44), channel_id=1, source_target_pairs={{0,8},{1,9},{2,10},{3,11},{4,12},{5,13},{6,14},{7,15},{8,0},{9,1},... | collective-permute-start | bytes 1032200 | tf_op jit(solution)/shard_map/ppermute | solution.py:202
  15.1 23.9 %collective-permute-start.8 = (bf16[1,256,1024]{2,1,0:T(8,128)(2,1)S(1)}, bf16[1,256,1024]{2,1,0:T(8,128)(2,1)S(1)}, u32[]{:S(2)}, u32[]{:S(2)}) collective-permute-start(bf16[1,256,1024]{2,1,0:T(8,128)(2,1)S(1)} %get-tuple-element.50.refs_0_), channel_id=1, source_target_pairs={{0,2},{1,5},{2,0},{3,7},{4,6},{5,1},{6,4},{7,3},{8,10},{9,13},{10,... | collective-permute-start | bytes 1572872 | tf_op jit(solution)/shard_map/ppermute | solution.py:202
  18.9 11.6 %copy-start.7 = (bf16[1,256,512]{2,1,0:T(8,128)(2,1)}, bf16[1,256,512]{2,1,0:T(8,128)(2,1)S(1)}, u32[]{:S(2)}) copy-start(bf16[1,256,512]{2,1,0:T(8,128)(2,1)S(1)} %slice_bitcast_fusion.1) | copy-start | bytes 786436
  20.3 14.7 %copy-start.6 = (bf16[128,2048]{1,0:T(8,128)(2,1)S(1)}, bf16[128,2048]{1,0:T(8,128)(2,1)}, u32[]{:S(2)}) copy-start(bf16[128,2048]{1,0:T(8,128)(2,1)} %param.12) | copy-start | bytes 1572868
  20.3 14.7 %copy-start.13 = (bf16[8,2048]{1,0:T(8,128)(2,1)S(1)}, bf16[8,2048]{1,0:T(8,128)(2,1)}, u32[]{:S(2)}) copy-start(bf16[8,2048]{1,0:T(8,128)(2,1)} %param.21) | copy-start | bytes 98308
  30.5 4.5 %copy-start.12 = (bf16[336,512]{1,0:T(8,128)(2,1)}, bf16[336,512]{1,0:T(8,128)(2,1)S(1)}, u32[]{:S(2)}) copy-start(bf16[336,512]{1,0:T(8,128)(2,1)S(1)} %collective-permute-done.2) | copy-start | bytes 1032196
  30.6 13.2 %collective-permute-start.6 = (bf16[2,256,512]{2,1,0:T(8,128)(2,1)S(1)}, bf16[2,256,512]{2,1,0:T(8,128)(2,1)S(1)}, u32[]{:S(2)}, u32[]{:S(2)}) collective-permute-start(bf16[2,256,512]{2,1,0:T(8,128)(2,1)S(1)} %pad_maximum_fusion.5.own), channel_id=1, source_target_pairs={{0,2},{1,5},{2,0},{3,7},{4,6},{5,1},{6,4},{7,3},{8,10},{9,13},{10,... | collective-permute-start | bytes 1572872 | tf_op jit(solution)/shard_map/ppermute | solution.py:202
  36.5 7.3 %copy-start.8 = (bf16[1,256,512]{2,1,0:T(8,128)(2,1)S(1)}, bf16[1,256,512]{2,1,0:T(8,128)(2,1)}, u32[]{:S(2)}) copy-start(bf16[1,256,512]{2,1,0:T(8,128)(2,1)} %copy-done.7) | copy-start | bytes 786436
  36.5 19.6 %collective-permute-start.3 = (bf16[176,2048]{1,0:T(8,128)(2,1)S(1)}, bf16[176,2048]{1,0:T(8,128)(2,1)S(1)}, u32[]{:S(2)}, u32[]{:S(2)}) collective-permute-start(bf16[176,2048]{1,0:T(8,128)(2,1)S(1)} %pad_maximum_fusion.4.x0), channel_id=1, source_target_pairs={{0,8},{1,9},{2,10},{3,11},{4,12},{5,13},{6,14},{7,15},{8,0},{9,1},... | collective-permute-start | bytes 2162696 | tf_op jit(solution)/shard_map/ppermute | solution.py:202
  39.1 41.7 %collective-permute-start.9 = (bf16[2,256,1024]{2,1,0:T(8,128)(2,1)S(1)}, bf16[2,256,1024]{2,1,0:T(8,128)(2,1)S(1)}, u32[]{:S(2)}, u32[]{:S(2)}) collective-permute-start(bf16[2,256,1024]{2,1,0:T(8,128)(2,1)S(1)} %pad_maximum_fusion.1), channel_id=1, source_target_pairs={{0,4},{1,3},{2,6},{3,1},{4,0},{5,7},{6,2},{7,5},{8,12},{9,11},{10,... | collective-permute-start | bytes 3145736 | tf_op jit(solution)/shard_map/ppermute | solution.py:202
  39.2 31.2 %collective-permute-start.10 = (bf16[1,256,1024]{2,1,0:T(8,128)(2,1)S(1)}, bf16[1,256,1024]{2,1,0:T(8,128)(2,1)S(1)}, u32[]{:S(2)}, u32[]{:S(2)}) collective-permute-start(bf16[1,256,1024]{2,1,0:T(8,128)(2,1)S(1)} %get-tuple-element.52), channel_id=1, source_target_pairs={{0,8},{1,9},{2,10},{3,11},{4,12},{5,13},{6,14},{7,15},{8,0},{9,1},... | collective-permute-start | bytes 1572872 | tf_op jit(solution)/shard_map/ppermute | solution.py:202
  43.9 37.0 %collective-permute-start.7 = (bf16[4,256,512]{2,1,0:T(8,128)(2,1)S(1)}, bf16[4,256,512]{2,1,0:T(8,128)(2,1)S(1)}, u32[]{:S(2)}, u32[]{:S(2)}) collective-permute-start(bf16[4,256,512]{2,1,0:T(8,128)(2,1)S(1)} %pad_maximum_fusion), channel_id=1, source_target_pairs={{0,4},{1,3},{2,6},{3,1},{4,0},{5,7},{6,2},{7,5},{8,12},{9,11},{10,... | collective-permute-start | bytes 3145736 | tf_op jit(solution)/shard_map/ppermute | solution.py:202
  56.1 24.8 %collective-permute-start.5 = (bf16[176,2048]{1,0:T(8,128)(2,1)S(1)}, bf16[176,2048]{1,0:T(8,128)(2,1)S(1)}, u32[]{:S(2)}, u32[]{:S(2)}) collective-permute-start(bf16[176,2048]{1,0:T(8,128)(2,1)S(1)} %collective-permute-done.3.x1), channel_id=1, source_target_pairs={{0,1},{1,0},{2,3},{3,2},{4,5},{5,4},{6,7},{7,6},{8,9},{9,8},{10,11... | collective-permute-start | bytes 2162696 | tf_op jit(solution)/shard_map/ppermute | solution.py:202
  56.1 24.8 %collective-permute-start.12 = (bf16[1024,256]{1,0:T(8,128)(2,1)S(1)}, bf16[1024,256]{1,0:T(8,128)(2,1)S(1)}, u32[]{:S(2)}, u32[]{:S(2)}) collective-permute-start(bf16[1024,256]{1,0:T(8,128)(2,1)S(1)} %get-tuple-element.53), channel_id=1, source_target_pairs={{0,16},{1,17},{2,18},{3,19},{4,20},{5,21},{6,22},{7,23},{8,24},{9,... | collective-permute-start | bytes 1572872 | tf_op jit(solution)/shard_map/ppermute | solution.py:202
  70.4 10.5 %collective-permute-start.11 = (bf16[1,256,1024]{2,1,0:T(8,128)(2,1)S(1)}, bf16[1,256,1024]{2,1,0:T(8,128)(2,1)S(1)}, u32[]{:S(2)}, u32[]{:S(2)}) collective-permute-start(bf16[1,256,1024]{2,1,0:T(8,128)(2,1)S(1)} %collective-permute-done.10.refs_3_), channel_id=1, source_target_pairs={{0,2},{1,5},{2,0},{3,7},{4,6},{5,1},{6,4},{7,3},{8,10},{9,13},{10,... | collective-permute-start | bytes 1572872 | tf_op jit(solution)/shard_map/ppermute | solution.py:202
  80.9 4.0 %copy-start.9 = (bf16[2,256,1024]{2,1,0:T(8,128)(2,1)}, bf16[2,256,1024]{2,1,0:T(8,128)(2,1)S(1)}, u32[]{:S(2)}) copy-start(bf16[2,256,1024]{2,1,0:T(8,128)(2,1)S(1)} %collective-permute-done.9.refs_2_) | copy-start | bytes 3145732
  80.9 5.1 %copy-start = (bf16[176,2048]{1,0:T(8,128)(2,1)}, bf16[176,2048]{1,0:T(8,128)(2,1)S(1)}, u32[]{:S(2)}) copy-start(bf16[176,2048]{1,0:T(8,128)(2,1)S(1)} %collective-permute-done.5.x3) | copy-start | bytes 2162692
  81.0 15.7 %collective-permute-start.13 = (bf16[2,256,1024]{2,1,0:T(8,128)(2,1)S(1)}, bf16[2,256,1024]{2,1,0:T(8,128)(2,1)}, u32[]{:S(2)}, u32[]{:S(2)}) collective-permute-start(bf16[2,256,1024]{2,1,0:T(8,128)(2,1)S(1)} %pad_maximum_fusion.3), channel_id=1, source_target_pairs={{0,4},{1,3},{2,6},{3,1},{4,0},{5,7},{6,2},{7,5},{8,12},{9,11},{10,... | collective-permute-start | bytes 3145736 | tf_op jit(solution)/shard_map/ppermute | solution.py:202
  83.8 2.2 %collective-permute-start.4 = (bf16[176,2048]{1,0:T(8,128)(2,1)S(1)}, bf16[176,2048]{1,0:T(8,128)(2,1)S(1)}, u32[]{:S(2)}, u32[]{:S(2)}) collective-permute-start(bf16[176,2048]{1,0:T(8,128)(2,1)S(1)} %pad_maximum_fusion.4.x0), channel_id=1, source_target_pairs={{0,1},{1,0},{2,3},{3,2},{4,5},{5,4},{6,7},{7,6},{8,9},{9,8},{10,11... | collective-permute-start | bytes 2162696 | tf_op jit(solution)/shard_map/ppermute | solution.py:202
  88.1 17.3 %collective-permute-start.14 = (bf16[736,256]{1,0:T(8,128)(2,1)S(1)}, bf16[736,256]{1,0:T(8,128)(2,1)S(1)}, u32[]{:S(2)}, u32[]{:S(2)}) collective-permute-start(bf16[736,256]{1,0:T(8,128)(2,1)S(1)} %get-tuple-element.69), channel_id=1, source_target_pairs={{0,16},{1,17},{2,18},{3,19},{4,20},{5,21},{6,22},{7,23},{8,24},{9,... | collective-permute-start | bytes 1130504 | tf_op jit(solution)/shard_map/ppermute | solution.py:202
  96.7 34.2 %collective-permute-start.18 = (bf16[2,1024,256]{2,1,0:T(8,128)(2,1)S(1)}, bf16[2,1024,256]{2,1,0:T(8,128)(2,1)S(1)}, u32[]{:S(2)}, u32[]{:S(2)}) collective-permute-start(bf16[2,1024,256]{2,1,0:T(8,128)(2,1)S(1)} %pad_maximum_fusion.2.refs_4_), channel_id=1, source_target_pairs={{0,2},{1,5},{2,0},{3,7},{4,6},{5,1},{6,4},{7,3},{8,10},{9,13},{10,... | collective-permute-start | bytes 3145736 | tf_op jit(solution)/shard_map/ppermute | solution.py:202
  105.4 25.5 %collective-permute-start.19 = (bf16[2,4,128,256]{3,2,1,0:T(8,128)(2,1)S(1)}, bf16[2,4,128,256]{3,2,1,0:T(8,128)(2,1)S(1)}, u32[]{:S(2)}, u32[]{:S(2)}) collective-permute-start(bf16[2,4,128,256]{3,2,1,0:T(8,128)(2,1)S(1)} %get-tuple-element.73), channel_id=1, source_target_pairs={{0,16},{1,17},{2,18},{3,19},{4,20},{5,21},{6,22},{7,23},{8,24},{9,... | collective-permute-start | bytes 1572872 | tf_op jit(solution)/shard_map/ppermute | solution.py:202
  110.2 11.7 %collective-permute-start.15 = (bf16[6,128,256]{2,1,0:T(8,128)(2,1)S(1)}, bf16[6,128,256]{2,1,0:T(8,128)(2,1)S(1)}, u32[]{:S(2)}, u32[]{:S(2)}) collective-permute-start(bf16[6,128,256]{2,1,0:T(8,128)(2,1)S(1)} %keys_join.1.kv0), channel_id=1, source_target_pairs={{0,2},{1,5},{2,0},{3,7},{4,6},{5,1},{6,4},{7,3},{8,10},{9,13},{10,... | collective-permute-start | bytes 1179656 | tf_op jit(solution)/shard_map/ppermute | solution.py:202
  111.5 10.3 %collective-permute-start.16 = (bf16[6,128,256]{2,1,0:T(8,128)(2,1)S(1)}, bf16[6,128,256]{2,1,0:T(8,128)(2,1)S(1)}, u32[]{:S(2)}, u32[]{:S(2)}) collective-permute-start(bf16[6,128,256]{2,1,0:T(8,128)(2,1)S(1)} %keys_join.1.kv0), channel_id=1, source_target_pairs={{0,4},{1,3},{2,6},{3,1},{4,0},{5,7},{6,2},{7,5},{8,12},{9,11},{10,... | collective-permute-start | bytes 1179656 | tf_op jit(solution)/shard_map/ppermute | solution.py:202
  112.7 18.3 %collective-permute-start.17 = (bf16[6,128,256]{2,1,0:T(8,128)(2,1)S(1)}, bf16[6,128,256]{2,1,0:T(8,128)(2,1)S(1)}, u32[]{:S(2)}, u32[]{:S(2)}) collective-permute-start(bf16[6,128,256]{2,1,0:T(8,128)(2,1)S(1)} %keys_join.1.kv0), channel_id=1, source_target_pairs={{0,6},{1,7},{2,4},{3,5},{4,2},{5,3},{6,0},{7,1},{8,14},{9,15},{10,... | collective-permute-start | bytes 1179656 | tf_op jit(solution)/shard_map/ppermute | solution.py:202
  130.9 25.8 %collective-permute-start.22 = (bf16[2,1024,256]{2,1,0:T(8,128)(2,1)S(1)}, bf16[2,1024,256]{2,1,0:T(8,128)(2,1)S(1)}, u32[]{:S(2)}, u32[]{:S(2)}) collective-permute-start(bf16[2,1024,256]{2,1,0:T(8,128)(2,1)S(1)} %pad_maximum_fusion.2.refs_4_), channel_id=1, source_target_pairs={{0,4},{1,3},{2,6},{3,1},{4,0},{5,7},{6,2},{7,5},{8,12},{9,11},{10,... | collective-permute-start | bytes 3145736 | tf_op jit(solution)/shard_map/ppermute | solution.py:202
  133.0 24.0 %collective-permute-start.23 = (bf16[2,1024,256]{2,1,0:T(8,128)(2,1)S(1)}, bf16[2,1024,256]{2,1,0:T(8,128)(2,1)S(1)}, u32[]{:S(2)}, u32[]{:S(2)}) collective-permute-start(bf16[2,1024,256]{2,1,0:T(8,128)(2,1)S(1)} %collective-permute-done.18.refs_5_), channel_id=1, source_target_pairs={{0,4},{1,3},{2,6},{3,1},{4,0},{5,7},{6,2},{7,5},{8,12},{9,11},{10,... | collective-permute-start | bytes 3145736 | tf_op jit(solution)/shard_map/ppermute | solution.py:202
  142.6 9.8 %collective-permute-start.20 = (bf16[512,256]{1,0:T(8,128)(2,1)S(1)}, bf16[512,256]{1,0:T(8,128)(2,1)S(1)}, u32[]{:S(2)}, u32[]{:S(2)}) collective-permute-start(bf16[512,256]{1,0:T(8,128)(2,1)S(1)} %attend.2.refs_0_), channel_id=1, source_target_pairs={{0,8},{1,9},{2,10},{3,11},{4,12},{5,13},{6,14},{7,15},{8,0},{9,1},... | collective-permute-start | bytes 786440 | tf_op jit(solution)/shard_map/ppermute | solution.py:202
  145.2 11.5 %collective-permute-start.21 = (bf16[512,256]{1,0:T(8,128)(2,1)S(1)}, bf16[512,256]{1,0:T(8,128)(2,1)S(1)}, u32[]{:S(2)}, u32[]{:S(2)}) collective-permute-start(bf16[512,256]{1,0:T(8,128)(2,1)S(1)} %attend.3.refs_1_), channel_id=1, source_target_pairs={{0,8},{1,9},{2,10},{3,11},{4,12},{5,13},{6,14},{7,15},{8,0},{9,1},... | collective-permute-start | bytes 786440 | tf_op jit(solution)/shard_map/ppermute | solution.py:202
  157.0 1.0 copy-start.10
  161.9 2.7 %collective-permute-start.24 = (bf16[4,128,1024]{2,1,0:T(8,128)(2,1)S(1)}, bf16[4,128,1024]{2,1,0:T(8,128)(2,1)S(1)}, u32[]{:S(2)}, u32[]{:S(2)}) collective-permute-start(bf16[4,128,1024]{2,1,0:T(8,128)(2,1)S(1)} %get-tuple-element.82), channel_id=1, source_target_pairs={{0,1},{1,0},{2,3},{3,2},{4,5},{5,4},{6,7},{7,6},{8,9},{9,8},{10,11... | collective-permute-start | bytes 3145736 | tf_op jit(solution)/shard_map/ppermute | solution.py:202
  166.5 9.8 %collective-permute-start.25 = (bf16[128,1024]{1,0:T(8,128)(2,1)S(1)}, bf16[128,1024]{1,0:T(8,128)(2,1)S(1)}, u32[]{:S(2)}, u32[]{:S(2)}) collective-permute-start(bf16[128,1024]{1,0:T(8,128)(2,1)S(1)} %get-tuple-element.87), channel_id=1, source_target_pairs={{0,8},{1,9},{2,10},{3,11},{4,12},{5,13},{6,14},{7,15},{8,16},{9,17... | collective-permute-start | bytes 786440 | tf_op jit(solution)/shard_map/ppermute | solution.py:202
  167.9 22.7 %collective-permute-start.26 = (bf16[128,1024]{1,0:T(8,128)(2,1)S(1)}, bf16[128,1024]{1,0:T(8,128)(2,1)S(1)}, u32[]{:S(2)}, u32[]{:S(2)}) collective-permute-start(bf16[128,1024]{1,0:T(8,128)(2,1)S(1)} %get-tuple-element.86), channel_id=1, source_target_pairs={{0,16},{1,17},{2,18},{3,19},{4,20},{5,21},{6,22},{7,23},{8,24},{9,... | collective-permute-start | bytes 786440 | tf_op jit(solution)/shard_map/ppermute | solution.py:202
  171.5 22.4 %collective-permute-start.27 = (bf16[128,1024]{1,0:T(8,128)(2,1)S(1)}, bf16[128,1024]{1,0:T(8,128)(2,1)S(1)}, u32[]{:S(2)}, u32[]{:S(2)}) collective-permute-start(bf16[128,1024]{1,0:T(8,128)(2,1)S(1)} %get-tuple-element.85), channel_id=1, source_target_pairs={{0,24},{1,25},{2,26},{3,27},{4,28},{5,29},{6,30},{7,31},{8,0},{9,1... | collective-permute-start | bytes 786440 | tf_op jit(solution)/shard_map/ppermute | solution.py:202

commit v11 on v10

--- a/solution.py
+++ b/solution.py
@@ -235,10 +235,10 @@
 
 
 def pack_kernel(where_ref, *refs):
-    w_query, w_key, w_value, cache_keys, cache_values, slots = refs[:6]
-    outs, sems = refs[6:10], refs[10]
+    w_key, w_value, cache_keys, cache_values, slots = refs[:5]
+    outs, sems = refs[5:7], refs[7]
     level = where_ref[0]
-    depth = w_query.shape[0]
+    depth = w_key.shape[0]
     copies = []
 
     def copy(source, target):
@@ -246,22 +246,20 @@
         copies[-1].start()
 
     for n in range(2):
-        keys, queries = outs[2 * n : 2 * n + 2]
+        keys = outs[n]
         for m in range(2):
             at = jnp.bitwise_xor(level, n + 2 * m)
             small = pl.ds(pl.multiple_of(at * HD, HD), HD)
-            large = pl.ds(pl.multiple_of(at * 4 * HD, 4 * HD), 4 * HD)
             for k, (new, old) in enumerate(((w_key, cache_keys), (w_value, cache_values))):
                 to = pl.ds((2 * m + k) * HD, HD)
                 copy(new.at[:, small], keys.at[0:depth, to])
                 copy(old.at[:, small], keys.at[depth : depth + CACHED, to])
-            copy(w_query.at[:, large], queries.at[0, :, pl.ds(m * 4 * HD, 4 * HD)])
         copy(slots, keys.at[depth + CACHED : depth + CACHED + REC_PAD])
     for each in copies:
         each.wait()
 
 
-PACK_COPIES = 22
+PACK_COPIES = 18
 
 
 def assemble(where_ref, parts, x_ref):
@@ -349,34 +347,43 @@
 
 
 def queries_part_kernel(where_ref, x0, x1, x2, x3, *refs):
-    keep_refs, send_ref, x_ref = refs[6:8], refs[8], refs[9]
+    weights, outs, x_ref = refs[:4], refs[4:8], refs[8]
+    level, place, core = where_ref[0], where_ref[1], where_ref[2]
     assemble(where_ref, (x0, x1, x2, x3), x_ref)
-    pieces = [
-        [own.at[0], near.at[0], far.at[0], far.at[1]] for own, near, far in (refs[0:3], refs[3:6])
-    ]
-    total = products(where_ref, x_ref, pieces)
-    block = total.shape[0] // LEVELS
+    depth = weights[0].shape[0]
+    width = 4 * HD
+    block = x_ref.shape[0] // LEVELS
     tok = block - REC_PAD
-    width = 2 * HD
-    for k in range(LEVELS):
-        fresh = total[k * block : k * block + tok]
-        for n in range(2):
-            keep_refs[n][k] = fresh[:, n * width : (n + 1) * width]
-            send_ref[n, k] = fresh[:, (2 + n) * width : (3 + n) * width].astype(jnp.bfloat16)
+    for m, out_ref in zip((0, 2, 1, 3), outs):
+        group = pl.ds(pl.multiple_of(jnp.bitwise_xor(level, m) * width, width), width)
+        total = None
+        for j in range(PLANE):
+            at = lax.rem(level, 2) * PLANE + place_of(j, place, core)
+            part = jnp.dot(
+                x_ref[:, pl.ds(pl.multiple_of(at * depth, depth), depth)],
+                weights[j][:, group],
+                preferred_element_type=jnp.float32,
+            )
+            total = part if total is None else total + part
+        for k in range(LEVELS):
+            at = jnp.bitwise_xor(level, lax.rem(k + LEVELS - where_ref[3], LEVELS))
+            out_ref[at] = total[k * block : k * block + tok].astype(out_ref.dtype)
 
 
 def attend_kernel(
-    pair, where_ref, keep_ref, got_ref, cos_ref, sin_ref, kv0, kv1, kv2, kv3, out_ref, query_ref
+    pair, where_ref, keep_ref, near_ref, got_ref, cos_ref, sin_ref, kv0, kv1, kv2, kv3, out_ref, query_ref
 ):
     level, place, core = where_ref[0], where_ref[1], where_ref[2]
     pieces = (kv0, kv1, kv2, kv3)
     tok = keep_ref.shape[1]
     old = LEVELS // 2
     heads = query_ref.shape[1]
-    for n in range(LEVELS):
-        at = jnp.bitwise_xor(level, n)
-        block = lax.rem(where_ref[3] + n, LEVELS)
-        total = keep_ref[block] + got_ref[pair, block].astype(jnp.float32)
+    columns = slice(pair * heads * HD, (pair + 1) * heads * HD)
+    for at in range(LEVELS):
+        total = keep_ref[at, :, columns] + (
+            near_ref[at, :, columns].astype(jnp.float32)
+            + got_ref[at, :, columns].astype(jnp.float32)
+        )
         cosine, sine = cos_ref[at][:tok], sin_ref[at][:tok]
         for h in range(heads):
             head = turned(total[:, h * HD : (h + 1) * HD], cosine, sine)
@@ -502,19 +509,16 @@
 
     slots = (recompute_slots - seq_index * CACHED).astype(jnp.bfloat16)
     slot_rows = jnp.broadcast_to(jnp.pad(slots, (0, REC_PAD - REC))[:, None], (REC_PAD, 4 * HD))
-    depth = w_query.shape[0]
-    key_shape = shaped((depth + CACHED + REC_PAD, 4 * HD))
-    query_shape = shaped((1, depth, 8 * HD))
-    key_own, query_own, key_give, query_give = pl.pallas_call(
+    depth = w_key.shape[0]
+    key_own, key_give = pl.pallas_call(
         pack_kernel,
-        out_shape=(key_shape, query_shape) * 2,
-        in_specs=[SMEM] + [HBM] * 6,
-        out_specs=(HBM,) * 4,
+        out_shape=(shaped((depth + CACHED + REC_PAD, 4 * HD)),) * 2,
+        in_specs=[SMEM] + [HBM] * 5,
+        out_specs=(HBM,) * 2,
         scratch_shapes=[pltpu.SemaphoreType.DMA((PACK_COPIES,))],
         compiler_params=PARAMS,
         name="pack",
-    )(where, w_query, w_key, w_value, cache_keys, cache_values, slot_rows)
-    query_near = to_near(query_own)
+    )(where, w_key, w_value, cache_keys, cache_values, slot_rows)
 
     rows = jnp.concatenate(
         [text_rows, recompute_rows, jnp.zeros((REC_PAD - REC, width), text_rows.dtype)], axis=0
@@ -535,9 +539,8 @@
     crossed = permuted(normed, lambda z, p, c: (z ^ 2, p, 1 - c) if c == 1 - z // 2 else None)
     shown = permuted(pictures, lambda z, p, c: (2 * c + p // 2, z, p % 2))
     key_next = across(key_give, 1)
-    query_far = to_far(jnp.concatenate([query_own, query_near], axis=0))
-    query_near, query_give = lax.optimization_barrier((query_near, query_give))
-    query_next = across(query_give, 1)
+    query_near, query_far = to_near(w_query), to_far(w_query)
+    query_both = to_far(query_near)
     shown, key_next = lax.optimization_barrier((shown, key_next))
     keys = jnp.stack([key_own[:depth], key_next[:depth]])
     old_own, old_next = key_own[depth:], key_next[depth:]
@@ -549,11 +552,9 @@
     next_other = other_core(next_rows)
     out_got = across(out_give, 2)
     keys_far = to_far(jnp.concatenate([keys, keys_near], axis=0))
-    next_near = to_near(query_next)
-    next_other, keys_far, query_far, next_near, out_got = lax.optimization_barrier(
-        (next_other, keys_far, query_far, next_near, out_got)
-    )
-    next_far = to_far(jnp.concatenate([query_next, next_near], axis=0))
+    next_other, held_other, keys_far, query_far, query_both, out_got = lax.optimization_barrier(
+        (next_other, held_other, keys_far, query_far, query_both, out_got)
+    )
     parts = (held, next_rows, held_other, next_other)
 
     half = HD // 2
@@ -581,21 +582,24 @@
         compiler_params=PARAMS,
         name="keys_part",
     )(where, *parts, keys, keys_near, keys_far, old_own, old_next)
-    send, out_got, *parts = lax.optimization_barrier((send, out_got, *parts))
-    out_pair = jnp.stack([out_own, out_got])
-    out_pair, next_far = lax.optimization_barrier((out_pair, next_far))
-    out_near = to_near(out_pair)
-    *q_keep, q_send = pl.pallas_call(
+    send, *parts = lax.optimization_barrier((send, *parts))
+    group_shape = (LEVELS, tok, 4 * HD)
+    q_keep, q_keep2, q_send, q_send2 = pl.pallas_call(
         queries_part_kernel,
-        out_shape=(shaped((LEVELS, tok, 2 * HD), jnp.float32),) * 2
-        + (shaped((2, LEVELS, tok, 2 * HD)),),
-        in_specs=[SMEM] + [VMEM] * 10,
-        out_specs=(VMEM,) * 3,
+        out_shape=(shaped(group_shape, jnp.float32),) * 2 + (shaped(group_shape),) * 2,
+        in_specs=[SMEM] + [VMEM] * 8,
+        out_specs=(VMEM,) * 4,
         scratch_shapes=[pltpu.VMEM((all_rows, width), jnp.bfloat16)],
         compiler_params=PARAMS,
         name="queries_part",
-    )(where, *parts, query_own, query_near, query_far, query_next, next_near, next_far)
-    got_keys, q_send = lax.optimization_barrier((across(send, 2), q_send))
+    )(where, *parts, w_query, query_near, query_far, query_both)
+    got_near2 = across(q_send2, 1)
+    got_near = across(q_send, 1)
+    got_queries = across((q_keep2 + got_near2.astype(jnp.float32)).astype(jnp.bfloat16), 2)
+    out_pair = jnp.stack([out_own, out_got])
+    out_pair, q_send2 = lax.optimization_barrier((out_pair, q_send2))
+    out_near = to_near(out_pair)
+    got_keys, q_send2 = lax.optimization_barrier((across(send, 2), q_send2))
     kv = pl.pallas_call(
         keys_join_kernel,
         out_shape=shaped((LEVELS // 2 + LEVELS, tok, 2 * HD)),
@@ -609,7 +613,7 @@
     kv_both = permuted(kv, lambda z, p, c: (z, p ^ 3, c))
 
     kv_near, kv_far, kv_both, out_near, out_pair, got_queries = lax.optimization_barrier(
-        (kv_near, kv_far, kv_both, out_near, out_pair, across(q_send, 2))
+        (kv_near, kv_far, kv_both, out_near, out_pair, got_queries)
     )
     out_far, out_both = to_far(out_pair), to_far(out_near)
 
@@ -617,12 +621,15 @@
         pl.pallas_call(
             functools.partial(attend_kernel, pair),
             out_shape=shaped((LEVELS * tok, 2 * HD)),
-            in_specs=[SMEM] + [VMEM] * 8,
+            in_specs=[SMEM] + [VMEM] * 9,
             out_specs=VMEM,
             scratch_shapes=[pltpu.VMEM((LEVELS, 2, tok, HD), jnp.bfloat16)],
             compiler_params=PARAMS,
+            cost_estimate=pl.CostEstimate(
+                flops=4_000_000_000, bytes_accessed=4_000_000, transcendentals=2_400_000
+            ),
             name="attend",
-        )(where, q_keep[pair], got_queries, cosine, sine, kv, kv_near, kv_far, kv_both)
+        )(where, q_keep, got_near, got_queries, cosine, sine, kv, kv_near, kv_far, kv_both)
         for pair in range(2)
     ]
     attended += [across(each, 1) for each in attended]

time: 196 us -> 198 us (1.010)
  starting transfers between devices: 42.9 us -> 47.8 us
  waiting for transfers between devices: 110 us -> 107 us
    ppermute x28, starting transfers between devices: 42.9 us -> 47.8 us  [permuted(): return lax.ppermute(value, ('seq', 'head'), perm)]
    unnamed x30 -> x22, local copies, waits for them, and re-layouts: 1.06 us -> 4.58 us
    ppermute x28, waiting for transfers between devices: 110 us -> 107 us  [permuted(): return lax.ppermute(value, ('seq', 'head'), perm)]
  transfers between devices with their start and end apart: 28 -> 28, of which waited for: 17 -> 15; matrix products, arithmetic and copies ran while one was open for 4% -> 5% of each run, Pallas kernels for 9% -> 6%
where the time goes in v11:
time: 198 us; the launch traced here: 197 us
  waiting for transfers between devices  107 us (54%)
  starting transfers between devices  47.8 us (24%)
  Pallas kernels  23.5 us (12%)
  other arithmetic  9.9 us (5%)
  local copies, waits for them, and re-layouts  6.15 us (3%)
  blocking collectives  2.46 us (1%)
    ppermute x28, waiting for transfers between devices, permuted(): return lax.ppermute(value, ('seq', 'head'), perm)  107 us
    ppermute x28, starting transfers between devices, permuted(): return lax.ppermute(value, ('seq', 'head'), perm)  47.8 us
    pallas_call x2, Pallas kernels, by_levels(): pl.pallas_call(functools.partial(attend_kernel, pair), out_shape=shaped((...  9.19 us
    pallas_call x1, Pallas kernels, by_levels(): pl.pallas_call(queries_part_kernel, out_shape=(shaped(group_shape, jnp.fl...  5 us
    unnamed x22, local copies, waits for them, and re-layouts  4.58 us
  transfers between devices with their start and end apart: 28, of which 15 were waited for; matrix products, arithmetic and copies ran while one was open for 5% of the time, Pallas kernels for 6%

profile of v11, /device:TPU:8, one launch (start us, length us, event | category | flops | bytes accessed | tf_op | source)
XLA Modules:
  0.0 197.1 jit_solution(10169296833165595208)
XLA Ops:
  0.0 1.5 collective-permute-start.9
  1.5 1.5 collective-permute-start.8
  3.0 0.7 subtract_convert_fusion
  3.8 0.9 copy-done
  4.8 0.9 copy-done.1
  5.7 0.8 copy-done.2
  6.6 0.8 copy-done.3
  7.4 0.9 pack.1
  8.3 0.5 collective-permute-start.2
  8.9 1.0 fusion.3
  10.0 1.4 fusion
  11.3 2.5 %all-reduce.1 = (f32[144]{0:T(256)S(1)}, f32[32]{0:T(128)S(1)}) all-reduce(f32[144]{0:T(256)S(1)} %fusion, f32[32]{0:T(128)S(1)} %fusion.3), channel_id=1, replica_groups=mesh['seq'=16,'head'=2] {'head'}, use_global_device_ids=true, to_apply=%region_1.2 | all-reduce | flops 176 | bytes 1408 | tf_op jit(solution)/shard_map/psum | solution.py:528
  13.8 0.8 fusion.5
  14.6 3.4 %collective-permute-start.1 = (bf16[32,2048]{1,0:T(8,128)(2,1)}, bf16[32,2048]{1,0:T(8,128)(2,1)}, u32[]{:S(2)}, u32[]{:S(2)}) collective-permute-start(bf16[32,2048]{1,0:T(8,128)(2,1)} %fusion.5), channel_id=1, source_target_pairs={{0,0},{1,16},{2,1},{3,17},{4,8},{5,24},{6,9},{7,25},{8,2},{9,18},{... | collective-permute-start | bytes 393224 | tf_op jit(solution)/shard_map/ppermute | solution.py:202
  18.1 0.4 fusion.2
  18.5 1.5 collective-permute-start
  20.0 1.3 dynamic-slice_bitcast_fusion
  21.3 2.1 %collective-permute-done.1 = bf16[32,2048]{1,0:T(8,128)(2,1)} collective-permute-done((bf16[32,2048]{1,0:T(8,128)(2,1)}, bf16[32,2048]{1,0:T(8,128)(2,1)}, u32[]{:S(2)}, u32[]{:S(2)}) %collective-permute-start.1) | collective-permute-done | bytes 131104 | tf_op jit(solution)/shard_map/ppermute | solution.py:202
  23.5 7.4 %collective-permute-start.6 = (bf16[2,256,512]{2,1,0:T(8,128)(2,1)S(1)}, bf16[2,256,512]{2,1,0:T(8,128)(2,1)S(1)}, u32[]{:S(2)}, u32[]{:S(2)}) collective-permute-start(bf16[2,256,512]{2,1,0:T(8,128)(2,1)S(1)} %pad_maximum_fusion.3.own), channel_id=1, source_target_pairs={{0,2},{1,5},{2,0},{3,7},{4,6},{5,1},{6,4},{7,3},{8,10},{9,13},{10,... | collective-permute-start | bytes 1572872 | tf_op jit(solution)/shard_map/ppermute | solution.py:202
  30.9 0.5 broadcast_select_fusion
  31.3 1.0 pad_maximum_fusion.2.x0
  32.4 5.6 %collective-permute-done.6.near = bf16[2,256,512]{2,1,0:T(8,128)(2,1)S(1)} collective-permute-done((bf16[2,256,512]{2,1,0:T(8,128)(2,1)S(1)}, bf16[2,256,512]{2,1,0:T(8,128)(2,1)S(1)}, u32[]{:S(2)}, u32[]{:S(2)}) %collective-permute-start.6) | collective-permute-done | bytes 524320 | tf_op jit(solution)/shard_map/ppermute | solution.py:202
  38.3 1.9 collective-permute-start.10
  40.2 3.6 %collective-permute-start.5 = (bf16[176,2048]{1,0:T(8,128)(2,1)S(1)}, bf16[176,2048]{1,0:T(8,128)(2,1)S(1)}, u32[]{:S(2)}, u32[]{:S(2)}) collective-permute-start(bf16[176,2048]{1,0:T(8,128)(2,1)S(1)} %pad_maximum_fusion.2.x0), channel_id=1, source_target_pairs={{0,1},{1,0},{2,3},{3,2},{4,5},{5,4},{6,7},{7,6},{8,9},{9,8},{10,11... | collective-permute-start | bytes 2162696 | tf_op jit(solution)/shard_map/ppermute | solution.py:202
  43.8 3.7 %collective-permute-done.3.x1 = bf16[176,2048]{1,0:T(8,128)(2,1)S(1)} collective-permute-done((bf16[176,2048]{1,0:T(8,128)(2,1)S(1)}, bf16[176,2048]{1,0:T(8,128)(2,1)S(1)}, u32[]{:S(2)}, u32[]{:S(2)}) %collective-permute-start.3) | collective-permute-done | bytes 720928 | tf_op jit(solution)/shard_map/ppermute | solution.py:202
  47.5 5.4 %collective-permute-start.4 = (bf16[176,2048]{1,0:T(8,128)(2,1)S(1)}, bf16[176,2048]{1,0:T(8,128)(2,1)S(1)}, u32[]{:S(2)}, u32[]{:S(2)}) collective-permute-start(bf16[176,2048]{1,0:T(8,128)(2,1)S(1)} %collective-permute-done.3.x1), channel_id=1, source_target_pairs={{0,1},{1,0},{2,3},{3,2},{4,5},{5,4},{6,7},{7,6},{8,9},{9,8},{10,11... | collective-permute-start | bytes 2162696 | tf_op jit(solution)/shard_map/ppermute | solution.py:202
  52.9 1.9 collective-permute-start.11
  54.9 22.9 %collective-permute-done.11 = bf16[1024,256]{1,0:T(8,128)(2,1)S(1)} collective-permute-done((bf16[1024,256]{1,0:T(8,128)(2,1)S(1)}, bf16[1024,256]{1,0:T(8,128)(2,1)S(1)}, u32[]{:S(2)}, u32[]{:S(2)}) %collective-permute-start.11) | collective-permute-done | bytes 524320 | tf_op jit(solution)/shard_map/ppermute | solution.py:202
  77.8 2.1 %keys_part.1 = (f32[576,256]{1,0:T(8,128)S(1)}, bf16[736,256]{1,0:T(8,128)(2,1)S(1)}) custom-call(s32[5]{0:T(128)S(1)} %stack.41.where_ref, bf16[176,2048]{1,0:T(8,128)(2,1)S(1)} %pad_maximum_fusion.2.x0, bf16[176,2048]{1,0:T(8,128)(2,1)S(1)} %collective-permute-done.3.x1, bf16[176,2048]{1,0:T(8,128)(2,1)S(1)} %collective-permute-done.5.x2, ...), custom_call_target="tpu_custom_call" | custom-call | tf_op jit(solution)/shard_map/keys_part/pallas_call | solution.py:573
  80.0 5.0 %queries_part.1 = (f32[4,128,512]{2,1,0:T(8,128)S(1)}, f32[4,128,512]{2,1,0:T(8,128)S(1)}, bf16[4,128,512]{2,1,0:T(8,128)(2,1)S(1)}, bf16[4,128,512]{2,1,0:T(8,128)(2,1)S(1)}) custom-call(s32[5]{0:T(128)S(1)} %stack.41.where_ref, bf16[176,2048]{1,0:T(8,128)(2,1)S(1)} %pad_maximum_fusion.2.x0, bf16[176,2048]{1,0:T(8,128)(2,1)S(1)} %collective-permute-done.3.x1, ...), custom_call_target="tpu_custom_call" | custom-call | tf_op jit(solution)/shard_map/queries_part/pallas_call | solution.py:587
  85.0 2.7 %collective-permute-start.18 = (bf16[4,128,512]{2,1,0:T(8,128)(2,1)S(1)}, bf16[4,128,512]{2,1,0:T(8,128)(2,1)S(1)}, u32[]{:S(2)}, u32[]{:S(2)}) collective-permute-start(bf16[4,128,512]{2,1,0:T(8,128)(2,1)S(1)} %get-tuple-element.60), channel_id=1, source_target_pairs={{0,8},{1,9},{2,10},{3,11},{4,12},{5,13},{6,14},{7,15},{8,0},{9,1},... | collective-permute-start | bytes 1572872 | tf_op jit(solution)/shard_map/ppermute | solution.py:202
  87.7 0.4 collective-permute-start.17
  88.1 0.8 collective-permute-start.13
  88.9 1.4 fusion.9
  90.3 0.2 pad_maximum_fusion.4.cos_ref
  90.7 17.9 %collective-permute-done.13.got_ref = bf16[736,256]{1,0:T(8,128)(2,1)S(1)} collective-permute-done((bf16[736,256]{1,0:T(8,128)(2,1)S(1)}, bf16[736,256]{1,0:T(8,128)(2,1)S(1)}, u32[]{:S(2)}, u32[]{:S(2)}) %collective-permute-start.13) | collective-permute-done | bytes 376864 | tf_op jit(solution)/shard_map/ppermute | solution.py:202
  108.6 1.0 keys_join.1.kv0
  109.7 0.4 collective-permute-start.14
  110.2 0.4 collective-permute-start.19
  110.6 1.8 collective-permute-start.12
  112.4 1.3 collective-permute-start.15
  113.8 7.2 %collective-permute-done.14.kv1 = bf16[6,128,256]{2,1,0:T(8,128)(2,1)S(1)} collective-permute-done((bf16[6,128,256]{2,1,0:T(8,128)(2,1)S(1)}, bf16[6,128,256]{2,1,0:T(8,128)(2,1)S(1)}, u32[]{:S(2)}, u32[]{:S(2)}) %collective-permute-start.14) | collective-permute-done | bytes 393248 | tf_op jit(solution)/shard_map/ppermute | solution.py:202
  120.9 1.2 collective-permute-start.16
  122.2 8.2 %collective-permute-done.16.kv3 = bf16[6,128,256]{2,1,0:T(8,128)(2,1)S(1)} collective-permute-done((bf16[6,128,256]{2,1,0:T(8,128)(2,1)S(1)}, bf16[6,128,256]{2,1,0:T(8,128)(2,1)S(1)}, u32[]{:S(2)}, u32[]{:S(2)}) %collective-permute-start.16) | collective-permute-done | bytes 393248 | tf_op jit(solution)/shard_map/ppermute | solution.py:202
  130.4 2.6 %collective-permute-done.19.got_ref = bf16[4,128,512]{2,1,0:T(8,128)(2,1)S(1)} collective-permute-done((bf16[4,128,512]{2,1,0:T(8,128)(2,1)S(1)}, bf16[4,128,512]{2,1,0:T(8,128)(2,1)S(1)}, u32[]{:S(2)}, u32[]{:S(2)}) %collective-permute-start.19) | collective-permute-done | bytes 524320 | tf_op jit(solution)/shard_map/ppermute | solution.py:202
  132.9 1.2 collective-permute-start.22
  134.2 0.8 collective-permute-start.23
  135.0 0.2 collective-permute-done.12.near_ref
  135.2 4.5 %attend.3.refs_1_ = bf16[512,256]{1,0:T(8,128)(2,1)S(1)} custom-call(s32[5]{0:T(128)S(1)} %stack.41.where_ref, f32[4,128,512]{2,1,0:T(8,128)S(1)} %get-tuple-element.55.keep_ref, bf16[4,128,512]{2,1,0:T(8,128)(2,1)S(1)} %collective-permute-done.12.near_ref, bf16[4,128,512]{2,1,0:T(8,128)(2,1)S(1)} %collective-permute-done.19.got_ref, ...), custom_call_target="tpu_custom_call" | custom-call | flops 4000000000 | bytes 4000000 | tf_op jit(solution)/shard_map/attend/pallas_call | solution.py:621
  139.7 2.3 %collective-permute-start.21 = (bf16[512,256]{1,0:T(8,128)(2,1)S(1)}, bf16[512,256]{1,0:T(8,128)(2,1)S(1)}, u32[]{:S(2)}, u32[]{:S(2)}) collective-permute-start(bf16[512,256]{1,0:T(8,128)(2,1)S(1)} %attend.3.refs_1_), channel_id=1, source_target_pairs={{0,8},{1,9},{2,10},{3,11},{4,12},{5,13},{6,14},{7,15},{8,0},{9,1},... | collective-permute-start | bytes 786440 | tf_op jit(solution)/shard_map/ppermute | solution.py:202
  142.0 4.7 %attend.2.refs_0_ = bf16[512,256]{1,0:T(8,128)(2,1)S(1)} custom-call(s32[5]{0:T(128)S(1)} %stack.41.where_ref, f32[4,128,512]{2,1,0:T(8,128)S(1)} %get-tuple-element.55.keep_ref, bf16[4,128,512]{2,1,0:T(8,128)(2,1)S(1)} %collective-permute-done.12.near_ref, bf16[4,128,512]{2,1,0:T(8,128)(2,1)S(1)} %collective-permute-done.19.got_ref, ...), custom_call_target="tpu_custom_call" | custom-call | flops 4000000000 | bytes 4000000 | tf_op jit(solution)/shard_map/attend/pallas_call | solution.py:621
  146.8 6.3 %collective-permute-done.20.refs_2_ = bf16[512,256]{1,0:T(8,128)(2,1)S(1)} collective-permute-done((bf16[512,256]{1,0:T(8,128)(2,1)S(1)}, bf16[512,256]{1,0:T(8,128)(2,1)S(1)}, u32[]{:S(2)}, u32[]{:S(2)}) %collective-permute-start.20) | collective-permute-done | bytes 262176 | tf_op jit(solution)/shard_map/ppermute | solution.py:202
  153.1 5.8 %collective-permute-done.23.refs_7_ = bf16[2,1024,256]{2,1,0:T(8,128)(2,1)S(1)} collective-permute-done((bf16[2,1024,256]{2,1,0:T(8,128)(2,1)S(1)}, bf16[2,1024,256]{2,1,0:T(8,128)(2,1)S(1)}, u32[]{:S(2)}, u32[]{:S(2)}) %collective-permute-start.23) | collective-permute-done | bytes 1048608 | tf_op jit(solution)/shard_map/ppermute | solution.py:202
  159.0 1.0 copy-done.7
  160.0 3.9 %output.1 = (f32[4,128,1024]{2,1,0:T(8,128)}, bf16[4,128,1024]{2,1,0:T(8,128)(2,1)S(1)}) custom-call(s32[5]{0:T(128)S(1)} %stack.41.where_ref, bf16[512,256]{1,0:T(8,128)(2,1)S(1)} %attend.2.refs_0_, bf16[512,256]{1,0:T(8,128)(2,1)S(1)} %attend.3.refs_1_, bf16[512,256]{1,0:T(8,128)(2,1)S(1)} %collective-permute-done.20.refs_2_, ...), custom_call_target="tpu_custom_call" | custom-call | tf_op jit(solution)/shard_map/output/pallas_call | solution.py:638
  163.8 2.7 %collective-permute-done.24 = bf16[4,128,1024]{2,1,0:T(8,128)(2,1)S(1)} collective-permute-done((bf16[4,128,1024]{2,1,0:T(8,128)(2,1)S(1)}, bf16[4,128,1024]{2,1,0:T(8,128)(2,1)S(1)}, u32[]{:S(2)}, u32[]{:S(2)}) %collective-permute-start.24) | collective-permute-done | bytes 1048608 | tf_op jit(solution)/shard_map/ppermute | solution.py:202
  166.5 1.9 fusion.8
  168.4 0.6 collective-permute-start.25
  169.0 4.3 %collective-permute-start.26 = (bf16[128,1024]{1,0:T(8,128)(2,1)S(1)}, bf16[128,1024]{1,0:T(8,128)(2,1)S(1)}, u32[]{:S(2)}, u32[]{:S(2)}) collective-permute-start(bf16[128,1024]{1,0:T(8,128)(2,1)S(1)} %get-tuple-element.74), channel_id=1, source_target_pairs={{0,16},{1,17},{2,18},{3,19},{4,20},{5,21},{6,22},{7,23},{8,24},{9,... | collective-permute-start | bytes 786440 | tf_op jit(solution)/shard_map/ppermute | solution.py:202
  173.2 0.6 collective-permute-start.27
  173.9 4.1 %collective-permute-done.25.first = bf16[128,1024]{1,0:T(8,128)(2,1)S(1)} collective-permute-done((bf16[128,1024]{1,0:T(8,128)(2,1)S(1)}, bf16[128,1024]{1,0:T(8,128)(2,1)S(1)}, u32[]{:S(2)}, u32[]{:S(2)}) %collective-permute-start.25) | collective-permute-done | bytes 262176 | tf_op jit(solution)/shard_map/ppermute | solution.py:202
  178.0 13.7 %collective-permute-done.26.second = bf16[128,1024]{1,0:T(8,128)(2,1)S(1)} collective-permute-done((bf16[128,1024]{1,0:T(8,128)(2,1)S(1)}, bf16[128,1024]{1,0:T(8,128)(2,1)S(1)}, u32[]{:S(2)}, u32[]{:S(2)}) %collective-permute-start.26) | collective-permute-done | bytes 262176 | tf_op jit(solution)/shard_map/ppermute | solution.py:202
  191.7 4.0 %collective-permute-done.27.third = bf16[128,1024]{1,0:T(8,128)(2,1)S(1)} collective-permute-done((bf16[128,1024]{1,0:T(8,128)(2,1)S(1)}, bf16[128,1024]{1,0:T(8,128)(2,1)S(1)}, u32[]{:S(2)}, u32[]{:S(2)}) %collective-permute-start.27) | collective-permute-done | bytes 262176 | tf_op jit(solution)/shard_map/ppermute | solution.py:202
  195.6 1.4 finish.1
  (56 shorter events, 1.4 us)
Async XLA Ops:
  0.0 13.8 %copy-start.8 = (bf16[32,2048]{1,0:T(8,128)(2,1)S(1)}, bf16[32,2048]{1,0:T(8,128)(2,1)}, u32[]{:S(2)}) copy-start(bf16[32,2048]{1,0:T(8,128)(2,1)} %param.13) | copy-start | bytes 393220
  0.0 38.3 %collective-permute-start.9 = (bf16[256,2048]{1,0:T(8,128)(2,1)}, bf16[256,2048]{1,0:T(8,128)(2,1)S(1)}, u32[]{:S(2)}, u32[]{:S(2)}) collective-permute-start(bf16[256,2048]{1,0:T(8,128)(2,1)} %refs_0_.3), channel_id=1, source_target_pairs={{0,2},{1,5},{2,0},{3,7},{4,6},{5,1},{6,4},{7,3},{8,10},{9,13},{10,... | collective-permute-start | bytes 3145736 | tf_op jit(solution)/shard_map/ppermute | solution.py:202
  1.5 51.4 %collective-permute-start.8 = (bf16[256,2048]{1,0:T(8,128)(2,1)}, bf16[256,2048]{1,0:T(8,128)(2,1)}, u32[]{:S(2)}, u32[]{:S(2)}) collective-permute-start(bf16[256,2048]{1,0:T(8,128)(2,1)} %refs_0_.3), channel_id=1, source_target_pairs={{0,4},{1,3},{2,6},{3,1},{4,0},{5,7},{6,2},{7,5},{8,12},{9,11},{10,... | collective-permute-start | bytes 3145736 | tf_op jit(solution)/shard_map/ppermute | solution.py:202
  3.8 1.0 copy-start
  4.8 0.9 copy-start.1
  5.7 0.8 copy-start.2
  6.6 0.8 copy-start.3
  7.4 6.4 %copy-start.10 = (f32[4096]{0:T(1024)S(1)}, f32[4096]{0:T(1024)}, u32[]{:S(2)}) copy-start(f32[4096]{0:T(1024)} %param.14) | copy-start | bytes 49156
  7.4 10.6 %copy-start.4 = (bf16[128,2048]{1,0:T(8,128)(2,1)S(1)}, bf16[128,2048]{1,0:T(8,128)(2,1)}, u32[]{:S(2)}) copy-start(bf16[128,2048]{1,0:T(8,128)(2,1)} %param.12) | copy-start | bytes 1572868
  7.4 10.7 %copy-start.9 = (bf16[8,2048]{1,0:T(8,128)(2,1)S(1)}, bf16[8,2048]{1,0:T(8,128)(2,1)}, u32[]{:S(2)}) copy-start(bf16[8,2048]{1,0:T(8,128)(2,1)} %param.21) | copy-start | bytes 98308
  8.3 15.0 %collective-permute-start.2 = (bf16[336,512]{1,0:T(8,128)(2,1)S(1)}, bf16[336,512]{1,0:T(8,128)(2,1)S(1)}, u32[]{:S(2)}, u32[]{:S(2)}) collective-permute-start(bf16[336,512]{1,0:T(8,128)(2,1)S(1)} %get-tuple-element.38), channel_id=1, source_target_pairs={{0,8},{1,9},{2,10},{3,11},{4,12},{5,13},{6,14},{7,15},{8,0},{9,1},... | collective-permute-start | bytes 1032200 | tf_op jit(solution)/shard_map/ppermute | solution.py:202
  14.6 8.8 %collective-permute-start.1 = (bf16[32,2048]{1,0:T(8,128)(2,1)}, bf16[32,2048]{1,0:T(8,128)(2,1)}, u32[]{:S(2)}, u32[]{:S(2)}) collective-permute-start(bf16[32,2048]{1,0:T(8,128)(2,1)} %fusion.5), channel_id=1, source_target_pairs={{0,0},{1,16},{2,1},{3,17},{4,8},{5,24},{6,9},{7,25},{8,2},{9,18},{... | collective-permute-start | bytes 393224 | tf_op jit(solution)/shard_map/ppermute | solution.py:202
  18.5 12.4 %collective-permute-start = (bf16[144,2048]{1,0:T(8,128)(2,1)S(1)}, bf16[144,2048]{1,0:T(8,128)(2,1)}, u32[]{:S(2)}, u32[]{:S(2)}) collective-permute-start(bf16[144,2048]{1,0:T(8,128)(2,1)S(1)} %fusion.2), channel_id=1, source_target_pairs={{1,16},{3,18},{5,20},{7,22},{9,24},{11,26},{13,28},{15,30},{16,1},... | collective-permute-start | bytes 1769480 | tf_op jit(solution)/shard_map/ppermute | solution.py:202
  23.5 14.5 %collective-permute-start.6 = (bf16[2,256,512]{2,1,0:T(8,128)(2,1)S(1)}, bf16[2,256,512]{2,1,0:T(8,128)(2,1)S(1)}, u32[]{:S(2)}, u32[]{:S(2)}) collective-permute-start(bf16[2,256,512]{2,1,0:T(8,128)(2,1)S(1)} %pad_maximum_fusion.3.own), channel_id=1, source_target_pairs={{0,2},{1,5},{2,0},{3,7},{4,6},{5,1},{6,4},{7,3},{8,10},{9,13},{10,... | collective-permute-start | bytes 1572872 | tf_op jit(solution)/shard_map/ppermute | solution.py:202
  32.3 15.2 %collective-permute-start.3 = (bf16[176,2048]{1,0:T(8,128)(2,1)S(1)}, bf16[176,2048]{1,0:T(8,128)(2,1)S(1)}, u32[]{:S(2)}, u32[]{:S(2)}) collective-permute-start(bf16[176,2048]{1,0:T(8,128)(2,1)S(1)} %pad_maximum_fusion.2.x0), channel_id=1, source_target_pairs={{0,8},{1,9},{2,10},{3,11},{4,12},{5,13},{6,14},{7,15},{8,0},{9,1},... | collective-permute-start | bytes 2162696 | tf_op jit(solution)/shard_map/ppermute | solution.py:202
  38.1 39.7 %collective-permute-start.7 = (bf16[4,256,512]{2,1,0:T(8,128)(2,1)S(1)}, bf16[4,256,512]{2,1,0:T(8,128)(2,1)S(1)}, u32[]{:S(2)}, u32[]{:S(2)}) collective-permute-start(bf16[4,256,512]{2,1,0:T(8,128)(2,1)S(1)} %pad_maximum_fusion), channel_id=1, source_target_pairs={{0,4},{1,3},{2,6},{3,1},{4,0},{5,7},{6,2},{7,5},{8,12},{9,11},{10,... | collective-permute-start | bytes 3145736 | tf_op jit(solution)/shard_map/ppermute | solution.py:202
  38.3 41.6 %copy-start.5 = (bf16[256,2048]{1,0:T(8,128)(2,1)}, bf16[256,2048]{1,0:T(8,128)(2,1)S(1)}, u32[]{:S(2)}) copy-start(bf16[256,2048]{1,0:T(8,128)(2,1)S(1)} %collective-permute-done.9.refs_1_) | copy-start | bytes 3145732
  38.3 39.5 %collective-permute-start.10 = (bf16[256,2048]{1,0:T(8,128)(2,1)S(1)}, bf16[256,2048]{1,0:T(8,128)(2,1)S(1)}, u32[]{:S(2)}, u32[]{:S(2)}) collective-permute-start(bf16[256,2048]{1,0:T(8,128)(2,1)S(1)} %collective-permute-done.9.refs_1_), channel_id=1, source_target_pairs={{0,4},{1,3},{2,6},{3,1},{4,0},{5,7},{6,2},{7,5},{8,12},{9,11},{10,... | collective-permute-start | bytes 3145736 | tf_op jit(solution)/shard_map/ppermute | solution.py:202
  40.2 37.6 %collective-permute-start.5 = (bf16[176,2048]{1,0:T(8,128)(2,1)S(1)}, bf16[176,2048]{1,0:T(8,128)(2,1)S(1)}, u32[]{:S(2)}, u32[]{:S(2)}) collective-permute-start(bf16[176,2048]{1,0:T(8,128)(2,1)S(1)} %pad_maximum_fusion.2.x0), channel_id=1, source_target_pairs={{0,1},{1,0},{2,3},{3,2},{4,5},{5,4},{6,7},{7,6},{8,9},{9,8},{10,11... | collective-permute-start | bytes 2162696 | tf_op jit(solution)/shard_map/ppermute | solution.py:202
  47.5 30.3 %collective-permute-start.4 = (bf16[176,2048]{1,0:T(8,128)(2,1)S(1)}, bf16[176,2048]{1,0:T(8,128)(2,1)S(1)}, u32[]{:S(2)}, u32[]{:S(2)}) collective-permute-start(bf16[176,2048]{1,0:T(8,128)(2,1)S(1)} %collective-permute-done.3.x1), channel_id=1, source_target_pairs={{0,1},{1,0},{2,3},{3,2},{4,5},{5,4},{6,7},{7,6},{8,9},{9,8},{10,11... | collective-permute-start | bytes 2162696 | tf_op jit(solution)/shard_map/ppermute | solution.py:202
  52.9 24.9 %collective-permute-start.11 = (bf16[1024,256]{1,0:T(8,128)(2,1)S(1)}, bf16[1024,256]{1,0:T(8,128)(2,1)S(1)}, u32[]{:S(2)}, u32[]{:S(2)}) collective-permute-start(bf16[1024,256]{1,0:T(8,128)(2,1)S(1)} %get-tuple-element.44), channel_id=1, source_target_pairs={{0,16},{1,17},{2,18},{3,19},{4,20},{5,21},{6,22},{7,23},{8,24},{9,... | collective-permute-start | bytes 1572872 | tf_op jit(solution)/shard_map/ppermute | solution.py:202
  77.8 2.1 %copy-start.6 = (bf16[256,2048]{1,0:T(8,128)(2,1)}, bf16[256,2048]{1,0:T(8,128)(2,1)S(1)}, u32[]{:S(2)}) copy-start(bf16[256,2048]{1,0:T(8,128)(2,1)S(1)} %collective-permute-done.10.refs_3_) | copy-start | bytes 3145732
  85.0 25.1 %collective-permute-start.18 = (bf16[4,128,512]{2,1,0:T(8,128)(2,1)S(1)}, bf16[4,128,512]{2,1,0:T(8,128)(2,1)S(1)}, u32[]{:S(2)}, u32[]{:S(2)}) collective-permute-start(bf16[4,128,512]{2,1,0:T(8,128)(2,1)S(1)} %get-tuple-element.60), channel_id=1, source_target_pairs={{0,8},{1,9},{2,10},{3,11},{4,12},{5,13},{6,14},{7,15},{8,0},{9,1},... | collective-permute-start | bytes 1572872 | tf_op jit(solution)/shard_map/ppermute | solution.py:202
  87.7 42.6 %collective-permute-start.17 = (bf16[2,1024,256]{2,1,0:T(8,128)(2,1)S(1)}, bf16[2,1024,256]{2,1,0:T(8,128)(2,1)S(1)}, u32[]{:S(2)}, u32[]{:S(2)}) collective-permute-start(bf16[2,1024,256]{2,1,0:T(8,128)(2,1)S(1)} %pad_maximum_fusion.1.refs_4_), channel_id=1, source_target_pairs={{0,2},{1,5},{2,0},{3,7},{4,6},{5,1},{6,4},{7,3},{8,10},{9,13},{10,... | collective-permute-start | bytes 3145736 | tf_op jit(solution)/shard_map/ppermute | solution.py:202
  88.1 20.5 %collective-permute-start.13 = (bf16[736,256]{1,0:T(8,128)(2,1)S(1)}, bf16[736,256]{1,0:T(8,128)(2,1)S(1)}, u32[]{:S(2)}, u32[]{:S(2)}) collective-permute-start(bf16[736,256]{1,0:T(8,128)(2,1)S(1)} %get-tuple-element.58), channel_id=1, source_target_pairs={{0,16},{1,17},{2,18},{3,19},{4,20},{5,21},{6,22},{7,23},{8,24},{9,... | collective-permute-start | bytes 1130504 | tf_op jit(solution)/shard_map/ppermute | solution.py:202
  109.7 11.3 %collective-permute-start.14 = (bf16[6,128,256]{2,1,0:T(8,128)(2,1)S(1)}, bf16[6,128,256]{2,1,0:T(8,128)(2,1)S(1)}, u32[]{:S(2)}, u32[]{:S(2)}) collective-permute-start(bf16[6,128,256]{2,1,0:T(8,128)(2,1)S(1)} %keys_join.1.kv0), channel_id=1, source_target_pairs={{0,2},{1,5},{2,0},{3,7},{4,6},{5,1},{6,4},{7,3},{8,10},{9,13},{10,... | collective-permute-start | bytes 1179656 | tf_op jit(solution)/shard_map/ppermute | solution.py:202
  110.2 22.7 %collective-permute-start.19 = (bf16[4,128,512]{2,1,0:T(8,128)(2,1)S(1)}, bf16[4,128,512]{2,1,0:T(8,128)(2,1)S(1)}, u32[]{:S(2)}, u32[]{:S(2)}) collective-permute-start(bf16[4,128,512]{2,1,0:T(8,128)(2,1)S(1)} %add_convert_fusion), channel_id=1, source_target_pairs={{0,16},{1,17},{2,18},{3,19},{4,20},{5,21},{6,22},{7,23},{8,24},{9,... | collective-permute-start | bytes 1572872 | tf_op jit(solution)/shard_map/ppermute | solution.py:202
  110.6 24.6 %collective-permute-start.12 = (bf16[4,128,512]{2,1,0:T(8,128)(2,1)S(1)}, bf16[4,128,512]{2,1,0:T(8,128)(2,1)S(1)}, u32[]{:S(2)}, u32[]{:S(2)}) collective-permute-start(bf16[4,128,512]{2,1,0:T(8,128)(2,1)S(1)} %get-tuple-element.56), channel_id=1, source_target_pairs={{0,8},{1,9},{2,10},{3,11},{4,12},{5,13},{6,14},{7,15},{8,0},{9,1},... | collective-permute-start | bytes 1572872 | tf_op jit(solution)/shard_map/ppermute | solution.py:202
  112.4 9.7 %collective-permute-start.15 = (bf16[6,128,256]{2,1,0:T(8,128)(2,1)S(1)}, bf16[6,128,256]{2,1,0:T(8,128)(2,1)S(1)}, u32[]{:S(2)}, u32[]{:S(2)}) collective-permute-start(bf16[6,128,256]{2,1,0:T(8,128)(2,1)S(1)} %keys_join.1.kv0), channel_id=1, source_target_pairs={{0,4},{1,3},{2,6},{3,1},{4,0},{5,7},{6,2},{7,5},{8,12},{9,11},{10,... | collective-permute-start | bytes 1179656 | tf_op jit(solution)/shard_map/ppermute | solution.py:202
  120.9 9.5 %collective-permute-start.16 = (bf16[6,128,256]{2,1,0:T(8,128)(2,1)S(1)}, bf16[6,128,256]{2,1,0:T(8,128)(2,1)S(1)}, u32[]{:S(2)}, u32[]{:S(2)}) collective-permute-start(bf16[6,128,256]{2,1,0:T(8,128)(2,1)S(1)} %keys_join.1.kv0), channel_id=1, source_target_pairs={{0,6},{1,7},{2,4},{3,5},{4,2},{5,3},{6,0},{7,1},{8,14},{9,15},{10,... | collective-permute-start | bytes 1179656 | tf_op jit(solution)/shard_map/ppermute | solution.py:202
  132.9 20.2 %collective-permute-start.22 = (bf16[2,1024,256]{2,1,0:T(8,128)(2,1)S(1)}, bf16[2,1024,256]{2,1,0:T(8,128)(2,1)S(1)}, u32[]{:S(2)}, u32[]{:S(2)}) collective-permute-start(bf16[2,1024,256]{2,1,0:T(8,128)(2,1)S(1)} %pad_maximum_fusion.1.refs_4_), channel_id=1, source_target_pairs={{0,4},{1,3},{2,6},{3,1},{4,0},{5,7},{6,2},{7,5},{8,12},{9,11},{10,... | collective-permute-start | bytes 3145736 | tf_op jit(solution)/shard_map/ppermute | solution.py:202
  134.2 24.8 %collective-permute-start.23 = (bf16[2,1024,256]{2,1,0:T(8,128)(2,1)S(1)}, bf16[2,1024,256]{2,1,0:T(8,128)(2,1)S(1)}, u32[]{:S(2)}, u32[]{:S(2)}) collective-permute-start(bf16[2,1024,256]{2,1,0:T(8,128)(2,1)S(1)} %collective-permute-done.17.refs_5_), channel_id=1, source_target_pairs={{0,4},{1,3},{2,6},{3,1},{4,0},{5,7},{6,2},{7,5},{8,12},{9,11},{10,... | collective-permute-start | bytes 3145736 | tf_op jit(solution)/shard_map/ppermute | solution.py:202
  139.7 7.1 %collective-permute-start.21 = (bf16[512,256]{1,0:T(8,128)(2,1)S(1)}, bf16[512,256]{1,0:T(8,128)(2,1)S(1)}, u32[]{:S(2)}, u32[]{:S(2)}) collective-permute-start(bf16[512,256]{1,0:T(8,128)(2,1)S(1)} %attend.3.refs_1_), channel_id=1, source_target_pairs={{0,8},{1,9},{2,10},{3,11},{4,12},{5,13},{6,14},{7,15},{8,0},{9,1},... | collective-permute-start | bytes 786440 | tf_op jit(solution)/shard_map/ppermute | solution.py:202
  146.7 6.4 %collective-permute-start.20 = (bf16[512,256]{1,0:T(8,128)(2,1)S(1)}, bf16[512,256]{1,0:T(8,128)(2,1)S(1)}, u32[]{:S(2)}, u32[]{:S(2)}) collective-permute-start(bf16[512,256]{1,0:T(8,128)(2,1)S(1)} %attend.2.refs_0_), channel_id=1, source_target_pairs={{0,8},{1,9},{2,10},{3,11},{4,12},{5,13},{6,14},{7,15},{8,0},{9,1},... | collective-permute-start | bytes 786440 | tf_op jit(solution)/shard_map/ppermute | solution.py:202
  159.0 1.0 copy-start.7
  163.8 2.7 %collective-permute-start.24 = (bf16[4,128,1024]{2,1,0:T(8,128)(2,1)S(1)}, bf16[4,128,1024]{2,1,0:T(8,128)(2,1)S(1)}, u32[]{:S(2)}, u32[]{:S(2)}) collective-permute-start(bf16[4,128,1024]{2,1,0:T(8,128)(2,1)S(1)} %get-tuple-element.70), channel_id=1, source_target_pairs={{0,1},{1,0},{2,3},{3,2},{4,5},{5,4},{6,7},{7,6},{8,9},{9,8},{10,11... | collective-permute-start | bytes 3145736 | tf_op jit(solution)/shard_map/ppermute | solution.py:202
  168.4 9.6 %collective-permute-start.25 = (bf16[128,1024]{1,0:T(8,128)(2,1)S(1)}, bf16[128,1024]{1,0:T(8,128)(2,1)S(1)}, u32[]{:S(2)}, u32[]{:S(2)}) collective-permute-start(bf16[128,1024]{1,0:T(8,128)(2,1)S(1)} %get-tuple-element.75), channel_id=1, source_target_pairs={{0,8},{1,9},{2,10},{3,11},{4,12},{5,13},{6,14},{7,15},{8,16},{9,17... | collective-permute-start | bytes 786440 | tf_op jit(solution)/shard_map/ppermute | solution.py:202
  169.0 22.7 %collective-permute-start.26 = (bf16[128,1024]{1,0:T(8,128)(2,1)S(1)}, bf16[128,1024]{1,0:T(8,128)(2,1)S(1)}, u32[]{:S(2)}, u32[]{:S(2)}) collective-permute-start(bf16[128,1024]{1,0:T(8,128)(2,1)S(1)} %get-tuple-element.74), channel_id=1, source_target_pairs={{0,16},{1,17},{2,18},{3,19},{4,20},{5,21},{6,22},{7,23},{8,24},{9,... | collective-permute-start | bytes 786440 | tf_op jit(solution)/shard_map/ppermute | solution.py:202
  173.2 22.4 %collective-permute-start.27 = (bf16[128,1024]{1,0:T(8,128)(2,1)S(1)}, bf16[128,1024]{1,0:T(8,128)(2,1)S(1)}, u32[]{:S(2)}, u32[]{:S(2)}) collective-permute-start(bf16[128,1024]{1,0:T(8,128)(2,1)S(1)} %get-tuple-element.73), channel_id=1, source_target_pairs={{0,24},{1,25},{2,26},{3,27},{4,28},{5,29},{6,30},{7,31},{8,0},{9,1... | collective-permute-start | bytes 786440 | tf_op jit(solution)/shard_map/ppermute | solution.py:202

commit v12 on v11

--- a/solution.py
+++ b/solution.py
@@ -540,6 +540,7 @@
     shown = permuted(pictures, lambda z, p, c: (2 * c + p // 2, z, p % 2))
     key_next = across(key_give, 1)
     query_near, query_far = to_near(w_query), to_far(w_query)
+    query_near, query_far = lax.optimization_barrier((query_near, query_far))
     query_both = to_far(query_near)
     shown, key_next = lax.optimization_barrier((shown, key_next))
     keys = jnp.stack([key_own[:depth], key_next[:depth]])
@@ -549,11 +550,14 @@
     held = jnp.concatenate([jnp.where(own_first, normed, crossed), shown], axis=0)
     next_rows = across(held, 1)
     held_other = other_core(held)
+    out_half = out_rows // 2
+    out_got0 = across(out_give[:out_half], 2)
+    out_got1 = across(out_give[out_half:], 2)
+    next_rows, out_got0 = lax.optimization_barrier((next_rows, out_got0))
     next_other = other_core(next_rows)
-    out_got = across(out_give, 2)
     keys_far = to_far(jnp.concatenate([keys, keys_near], axis=0))
-    next_other, held_other, keys_far, query_far, query_both, out_got = lax.optimization_barrier(
-        (next_other, held_other, keys_far, query_far, query_both, out_got)
+    next_other, held_other, keys_far, query_both, out_got1 = lax.optimization_barrier(
+        (next_other, held_other, keys_far, query_both, out_got1)
     )
     parts = (held, next_rows, held_other, next_other)
 
@@ -580,6 +584,9 @@
         out_specs=(VMEM, VMEM),
         scratch_shapes=[pltpu.VMEM((all_rows, width), jnp.bfloat16)],
         compiler_params=PARAMS,
+        cost_estimate=pl.CostEstimate(
+            flops=3_000_000_000, bytes_accessed=4_000_000, transcendentals=0
+        ),
         name="keys_part",
     )(where, *parts, keys, keys_near, keys_far, old_own, old_next)
     send, *parts = lax.optimization_barrier((send, *parts))
@@ -591,12 +598,15 @@
         out_specs=(VMEM,) * 4,
         scratch_shapes=[pltpu.VMEM((all_rows, width), jnp.bfloat16)],
         compiler_params=PARAMS,
+        cost_estimate=pl.CostEstimate(
+            flops=5_000_000_000, bytes_accessed=4_000_000, transcendentals=0
+        ),
         name="queries_part",
     )(where, *parts, w_query, query_near, query_far, query_both)
     got_near2 = across(q_send2, 1)
     got_near = across(q_send, 1)
     got_queries = across((q_keep2 + got_near2.astype(jnp.float32)).astype(jnp.bfloat16), 2)
-    out_pair = jnp.stack([out_own, out_got])
+    out_pair = jnp.stack([out_own, jnp.concatenate([out_got0, out_got1], axis=0)])
     out_pair, q_send2 = lax.optimization_barrier((out_pair, q_send2))
     out_near = to_near(out_pair)
     got_keys, q_send2 = lax.optimization_barrier((across(send, 2), q_send2))
@@ -607,6 +617,9 @@
         out_specs=VMEM,
         scratch_shapes=[pltpu.VMEM((all_rows, 2 * HD), jnp.float32)],
         compiler_params=PARAMS,
+        cost_estimate=pl.CostEstimate(
+            flops=12_000_000_000, bytes_accessed=4_000_000, transcendentals=0
+        ),
         name="keys_join",
     )(where, keep, got_keys, old_own, old_next, cosine, sine)
     kv_near, kv_far = to_near(kv), to_far(kv)
@@ -645,6 +658,9 @@
         out_specs=(VMEM, VMEM),
         scratch_shapes=[pltpu.VMEM((LEVELS * tok, out_rows), jnp.bfloat16)],
         compiler_params=PARAMS,
+        cost_estimate=pl.CostEstimate(
+            flops=5_000_000_000, bytes_accessed=4_000_000, transcendentals=0
+        ),
         name="output",
     )(where, *attended, out_pair, out_near, out_far, out_both)
     got = other_core(other)

time: 198 us -> 191 us (0.965)
  waiting for transfers between devices: 107 us -> 100 us
    ppermute x28 -> x29, waiting for transfers between devices: 107 us -> 100 us  [permuted(): return lax.ppermute(value, ('seq', 'head'), perm)]
    ppermute x28 -> x29, starting transfers between devices: 47.8 us -> 49.1 us  [permuted(): return lax.ppermute(value, ('seq', 'head'), perm)]
  transfers between devices with their start and end apart: 28 -> 29, of which waited for: 15 -> 14; matrix products, arithmetic and copies ran while one was open for 5% -> 4% of each run, Pallas kernels for 6% -> 9%
where the time goes in v12:
time: 191 us
  waiting for transfers between devices  100 us (52%)
  starting transfers between devices  49.1 us (26%)
  Pallas kernels  23.8 us (12%)
  other arithmetic  10 us (5%)
  local copies, waits for them, and re-layouts  5 us (3%)
  blocking collectives  2.46 us (1%)
    ppermute x29, waiting for transfers between devices, permuted(): return lax.ppermute(value, ('seq', 'head'), perm)  100 us
    ppermute x29, starting transfers between devices, permuted(): return lax.ppermute(value, ('seq', 'head'), perm)  49.1 us
    pallas_call x2, Pallas kernels, by_levels(): pl.pallas_call(functools.partial(attend_kernel, pair), out_shape=shaped((...  9.47 us
    pallas_call x1, Pallas kernels, by_levels(): pl.pallas_call(queries_part_kernel, out_shape=(shaped(group_shape, jnp.fl...  4.99 us
    unnamed x22, local copies, waits for them, and re-layouts  4.59 us
    pallas_call x1, Pallas kernels, by_levels(): pl.pallas_call(output_kernel, out_shape=(shaped((LEVELS, tok, wide_cols),...  3.87 us
  transfers between devices with their start and end apart: 29, of which 14 were waited for; matrix products, arithmetic and copies ran while one was open for 4% of the time, Pallas kernels for 9%

profile of v12, /device:TPU:8, one launch (start us, length us, event | category | flops | bytes accessed | tf_op | source)
XLA Modules:
  0.0 191.0 jit_solution(17615621640830417025)
XLA Ops:
  0.0 1.5 collective-permute-start.10
  1.5 1.5 collective-permute-start.9
  3.0 0.7 subtract_convert_fusion
  3.7 0.1 stack.41.where_ref
  3.8 0.9 copy-done
  4.8 0.9 copy-done.1
  5.7 0.8 copy-done.2
  6.6 0.8 copy-done.3
  7.4 0.9 pack.1
  8.3 0.5 collective-permute-start.2
  8.9 1.0 fusion.3
  10.0 1.5 fusion
  11.4 2.5 %all-reduce.1 = (f32[144]{0:T(256)S(1)}, f32[32]{0:T(128)S(1)}) all-reduce(f32[144]{0:T(256)S(1)} %fusion, f32[32]{0:T(128)S(1)} %fusion.3), channel_id=1, replica_groups=mesh['seq'=16,'head'=2] {'head'}, use_global_device_ids=true, to_apply=%region_1.2 | all-reduce | flops 176 | bytes 1408 | tf_op jit(solution)/shard_map/psum | solution.py:528
  13.9 0.8 fusion.5
  14.7 3.4 %collective-permute-start.1 = (bf16[32,2048]{1,0:T(8,128)(2,1)}, bf16[32,2048]{1,0:T(8,128)(2,1)}, u32[]{:S(2)}, u32[]{:S(2)}) collective-permute-start(bf16[32,2048]{1,0:T(8,128)(2,1)} %fusion.5), channel_id=1, source_target_pairs={{0,0},{1,16},{2,1},{3,17},{4,8},{5,24},{6,9},{7,25},{8,2},{9,18},{... | collective-permute-start | bytes 393224 | tf_op jit(solution)/shard_map/ppermute | solution.py:202
  18.2 0.4 fusion.2
  18.6 1.5 collective-permute-start
  20.2 3.3 %collective-permute-done.1 = bf16[32,2048]{1,0:T(8,128)(2,1)} collective-permute-done((bf16[32,2048]{1,0:T(8,128)(2,1)}, bf16[32,2048]{1,0:T(8,128)(2,1)}, u32[]{:S(2)}, u32[]{:S(2)}) %collective-permute-start.1) | collective-permute-done | bytes 131104 | tf_op jit(solution)/shard_map/ppermute | solution.py:202
  23.6 7.1 %collective-permute-start.7 = (bf16[2,256,512]{2,1,0:T(8,128)(2,1)S(1)}, bf16[2,256,512]{2,1,0:T(8,128)(2,1)S(1)}, u32[]{:S(2)}, u32[]{:S(2)}) collective-permute-start(bf16[2,256,512]{2,1,0:T(8,128)(2,1)S(1)} %pad_maximum_fusion.3.own), channel_id=1, source_target_pairs={{0,2},{1,5},{2,0},{3,7},{4,6},{5,1},{6,4},{7,3},{8,10},{9,13},{10,... | collective-permute-start | bytes 1572872 | tf_op jit(solution)/shard_map/ppermute | solution.py:202
  30.6 0.5 broadcast_select_fusion
  31.1 1.0 pad_maximum_fusion.2.x0
  32.2 10.0 %collective-permute-start.4 = (bf16[512,256]{1,0:T(8,128)(2,1)S(1)}, bf16[512,256]{1,0:T(8,128)(2,1)S(1)}, u32[]{:S(2)}, u32[]{:S(2)}) collective-permute-start(bf16[512,256]{1,0:T(8,128)(2,1)S(1)} %get-tuple-element.86), channel_id=1, source_target_pairs={{0,16},{1,17},{2,18},{3,19},{4,20},{5,21},{6,22},{7,23},{8,24},{9,... | collective-permute-start | bytes 786440 | tf_op jit(solution)/shard_map/ppermute | solution.py:202
  42.2 0.1 pad_maximum_fusion
  42.3 1.4 collective-permute-start.8
  43.7 0.7 collective-permute-start.11
  44.6 12.4 %collective-permute-done.4 = bf16[512,256]{1,0:T(8,128)(2,1)S(1)} collective-permute-done((bf16[512,256]{1,0:T(8,128)(2,1)S(1)}, bf16[512,256]{1,0:T(8,128)(2,1)S(1)}, u32[]{:S(2)}, u32[]{:S(2)}) %collective-permute-start.4) | collective-permute-done | bytes 262176 | tf_op jit(solution)/shard_map/ppermute | solution.py:202
  57.0 1.6 collective-permute-start.5
  58.6 1.9 collective-permute-start.12
  60.5 1.4 fusion.9
  61.9 0.2 pad_maximum_fusion.4.cos_ref
  62.1 0.2 pad_maximum_fusion.5.sin_ref
  62.3 10.0 %collective-permute-done.12 = bf16[512,256]{1,0:T(8,128)(2,1)S(1)} collective-permute-done((bf16[512,256]{1,0:T(8,128)(2,1)S(1)}, bf16[512,256]{1,0:T(8,128)(2,1)S(1)}, u32[]{:S(2)}, u32[]{:S(2)}) %collective-permute-start.12) | collective-permute-done | bytes 262176 | tf_op jit(solution)/shard_map/ppermute | solution.py:202
  72.3 2.1 %keys_part.1 = (f32[576,256]{1,0:T(8,128)S(1)}, bf16[736,256]{1,0:T(8,128)(2,1)S(1)}) custom-call(s32[5]{0:T(128)S(1)} %stack.41.where_ref, bf16[176,2048]{1,0:T(8,128)(2,1)S(1)} %pad_maximum_fusion.2.x0, bf16[176,2048]{1,0:T(8,128)(2,1)S(1)} %collective-permute-done.3.x1, bf16[176,2048]{1,0:T(8,128)(2,1)S(1)} %collective-permute-done.6.x2, ...), custom_call_target="tpu_custom_call" | custom-call | flops 3000000000 | bytes 4000000 | tf_op jit(solution)/shard_map/keys_part/pallas_call | solution.py:577
  74.4 3.4 %collective-permute-start.14 = (bf16[736,256]{1,0:T(8,128)(2,1)S(1)}, bf16[736,256]{1,0:T(8,128)(2,1)S(1)}, u32[]{:S(2)}, u32[]{:S(2)}) collective-permute-start(bf16[736,256]{1,0:T(8,128)(2,1)S(1)} %get-tuple-element.63), channel_id=1, source_target_pairs={{0,16},{1,17},{2,18},{3,19},{4,20},{5,21},{6,22},{7,23},{8,24},{9,... | collective-permute-start | bytes 1130504 | tf_op jit(solution)/shard_map/ppermute | solution.py:202
  77.8 5.0 %queries_part.1 = (f32[4,128,512]{2,1,0:T(8,128)S(1)}, f32[4,128,512]{2,1,0:T(8,128)S(1)}, bf16[4,128,512]{2,1,0:T(8,128)(2,1)S(1)}, bf16[4,128,512]{2,1,0:T(8,128)(2,1)S(1)}) custom-call(s32[5]{0:T(128)S(1)} %stack.41.where_ref, bf16[176,2048]{1,0:T(8,128)(2,1)S(1)} %pad_maximum_fusion.2.x0, bf16[176,2048]{1,0:T(8,128)(2,1)S(1)} %collective-permute-done.3.x1, ...), custom_call_target="tpu_custom_call" | custom-call | flops 5000000000 | bytes 4000000 | tf_op jit(solution)/shard_map/queries_part/pallas_call | solution.py:594
  82.9 0.1 pad_maximum_fusion.1.refs_4_
  83.1 10.0 %collective-permute-done.14.got_ref = bf16[736,256]{1,0:T(8,128)(2,1)S(1)} collective-permute-done((bf16[736,256]{1,0:T(8,128)(2,1)S(1)}, bf16[736,256]{1,0:T(8,128)(2,1)S(1)}, u32[]{:S(2)}, u32[]{:S(2)}) %collective-permute-start.14) | collective-permute-done | bytes 376864 | tf_op jit(solution)/shard_map/ppermute | solution.py:202
  93.1 1.0 keys_join.1.kv0
  94.2 8.0 %collective-permute-done.19 = bf16[4,128,512]{2,1,0:T(8,128)(2,1)S(1)} collective-permute-done((bf16[4,128,512]{2,1,0:T(8,128)(2,1)S(1)}, bf16[4,128,512]{2,1,0:T(8,128)(2,1)S(1)}, u32[]{:S(2)}, u32[]{:S(2)}) %collective-permute-start.19) | collective-permute-done | bytes 524320 | tf_op jit(solution)/shard_map/ppermute | solution.py:202
  102.3 0.2 add_convert_fusion
  102.4 2.7 %collective-permute-start.20 = (bf16[4,128,512]{2,1,0:T(8,128)(2,1)S(1)}, bf16[4,128,512]{2,1,0:T(8,128)(2,1)S(1)}, u32[]{:S(2)}, u32[]{:S(2)}) collective-permute-start(bf16[4,128,512]{2,1,0:T(8,128)(2,1)S(1)} %add_convert_fusion), channel_id=1, source_target_pairs={{0,16},{1,17},{2,18},{3,19},{4,20},{5,21},{6,22},{7,23},{8,24},{9,... | collective-permute-start | bytes 1572872 | tf_op jit(solution)/shard_map/ppermute | solution.py:202
  105.1 0.8 collective-permute-start.16
  105.9 0.4 collective-permute-start.17
  106.3 15.0 %collective-permute-done.16.kv2 = bf16[6,128,256]{2,1,0:T(8,128)(2,1)S(1)} collective-permute-done((bf16[6,128,256]{2,1,0:T(8,128)(2,1)S(1)}, bf16[6,128,256]{2,1,0:T(8,128)(2,1)S(1)}, u32[]{:S(2)}, u32[]{:S(2)}) %collective-permute-start.16) | collective-permute-done | bytes 393248 | tf_op jit(solution)/shard_map/ppermute | solution.py:202
  121.3 5.3 %collective-permute-done.20.got_ref = bf16[4,128,512]{2,1,0:T(8,128)(2,1)S(1)} collective-permute-done((bf16[4,128,512]{2,1,0:T(8,128)(2,1)S(1)}, bf16[4,128,512]{2,1,0:T(8,128)(2,1)S(1)}, u32[]{:S(2)}, u32[]{:S(2)}) %collective-permute-start.20) | collective-permute-done | bytes 524320 | tf_op jit(solution)/shard_map/ppermute | solution.py:202
  126.6 0.8 collective-permute-start.23
  127.4 1.2 collective-permute-start.24
  128.6 4.7 %attend.3.refs_1_ = bf16[512,256]{1,0:T(8,128)(2,1)S(1)} custom-call(s32[5]{0:T(128)S(1)} %stack.41.where_ref, f32[4,128,512]{2,1,0:T(8,128)S(1)} %get-tuple-element.60.keep_ref, bf16[4,128,512]{2,1,0:T(8,128)(2,1)S(1)} %collective-permute-done.13.near_ref, bf16[4,128,512]{2,1,0:T(8,128)(2,1)S(1)} %collective-permute-done.20.got_ref, ...), custom_call_target="tpu_custom_call" | custom-call | flops 4000000000 | bytes 4000000 | tf_op jit(solution)/shard_map/attend/pallas_call | solution.py:634
  133.3 2.8 %collective-permute-start.22 = (bf16[512,256]{1,0:T(8,128)(2,1)S(1)}, bf16[512,256]{1,0:T(8,128)(2,1)S(1)}, u32[]{:S(2)}, u32[]{:S(2)}) collective-permute-start(bf16[512,256]{1,0:T(8,128)(2,1)S(1)} %attend.3.refs_1_), channel_id=1, source_target_pairs={{0,8},{1,9},{2,10},{3,11},{4,12},{5,13},{6,14},{7,15},{8,0},{9,1},... | collective-permute-start | bytes 786440 | tf_op jit(solution)/shard_map/ppermute | solution.py:202
  136.0 4.8 %attend.2.refs_0_ = bf16[512,256]{1,0:T(8,128)(2,1)S(1)} custom-call(s32[5]{0:T(128)S(1)} %stack.41.where_ref, f32[4,128,512]{2,1,0:T(8,128)S(1)} %get-tuple-element.60.keep_ref, bf16[4,128,512]{2,1,0:T(8,128)(2,1)S(1)} %collective-permute-done.13.near_ref, bf16[4,128,512]{2,1,0:T(8,128)(2,1)S(1)} %collective-permute-done.20.got_ref, ...), custom_call_target="tpu_custom_call" | custom-call | flops 4000000000 | bytes 4000000 | tf_op jit(solution)/shard_map/attend/pallas_call | solution.py:634
  140.9 1.0 collective-permute-done.22.refs_3_
  141.9 6.3 %collective-permute-done.21.refs_2_ = bf16[512,256]{1,0:T(8,128)(2,1)S(1)} collective-permute-done((bf16[512,256]{1,0:T(8,128)(2,1)S(1)}, bf16[512,256]{1,0:T(8,128)(2,1)S(1)}, u32[]{:S(2)}, u32[]{:S(2)}) %collective-permute-start.21) | collective-permute-done | bytes 262176 | tf_op jit(solution)/shard_map/ppermute | solution.py:202
  148.2 4.4 %collective-permute-done.24.refs_7_ = bf16[2,1024,256]{2,1,0:T(8,128)(2,1)S(1)} collective-permute-done((bf16[2,1024,256]{2,1,0:T(8,128)(2,1)S(1)}, bf16[2,1024,256]{2,1,0:T(8,128)(2,1)S(1)}, u32[]{:S(2)}, u32[]{:S(2)}) %collective-permute-start.24) | collective-permute-done | bytes 1048608 | tf_op jit(solution)/shard_map/ppermute | solution.py:202
  152.6 1.0 copy-done.10
  153.6 3.9 %output.1 = (f32[4,128,1024]{2,1,0:T(8,128)}, bf16[4,128,1024]{2,1,0:T(8,128)(2,1)S(1)}) custom-call(s32[5]{0:T(128)S(1)} %stack.41.where_ref, bf16[512,256]{1,0:T(8,128)(2,1)S(1)} %attend.2.refs_0_, bf16[512,256]{1,0:T(8,128)(2,1)S(1)} %attend.3.refs_1_, bf16[512,256]{1,0:T(8,128)(2,1)S(1)} %collective-permute-done.21.refs_2_, ...), custom_call_target="tpu_custom_call" | custom-call | flops 5000000000 | bytes 4000000 | tf_op jit(solution)/shard_map/output/pallas_call | solution.py:651
  157.5 2.7 %collective-permute-done.25 = bf16[4,128,1024]{2,1,0:T(8,128)(2,1)S(1)} collective-permute-done((bf16[4,128,1024]{2,1,0:T(8,128)(2,1)S(1)}, bf16[4,128,1024]{2,1,0:T(8,128)(2,1)S(1)}, u32[]{:S(2)}, u32[]{:S(2)}) %collective-permute-start.25) | collective-permute-done | bytes 1048608 | tf_op jit(solution)/shard_map/ppermute | solution.py:202
  160.1 1.9 fusion.8
  162.0 0.8 collective-permute-start.26
  162.8 4.3 %collective-permute-start.27 = (bf16[128,1024]{1,0:T(8,128)(2,1)S(1)}, bf16[128,1024]{1,0:T(8,128)(2,1)S(1)}, u32[]{:S(2)}, u32[]{:S(2)}) collective-permute-start(bf16[128,1024]{1,0:T(8,128)(2,1)S(1)} %get-tuple-element.80), channel_id=1, source_target_pairs={{0,16},{1,17},{2,18},{3,19},{4,20},{5,21},{6,22},{7,23},{8,24},{9,... | collective-permute-start | bytes 786440 | tf_op jit(solution)/shard_map/ppermute | solution.py:202
  167.1 0.4 collective-permute-start.28
  167.5 4.3 %collective-permute-done.26.first = bf16[128,1024]{1,0:T(8,128)(2,1)S(1)} collective-permute-done((bf16[128,1024]{1,0:T(8,128)(2,1)S(1)}, bf16[128,1024]{1,0:T(8,128)(2,1)S(1)}, u32[]{:S(2)}, u32[]{:S(2)}) %collective-permute-start.26) | collective-permute-done | bytes 262176 | tf_op jit(solution)/shard_map/ppermute | solution.py:202
  171.9 13.7 %collective-permute-done.27.second = bf16[128,1024]{1,0:T(8,128)(2,1)S(1)} collective-permute-done((bf16[128,1024]{1,0:T(8,128)(2,1)S(1)}, bf16[128,1024]{1,0:T(8,128)(2,1)S(1)}, u32[]{:S(2)}, u32[]{:S(2)}) %collective-permute-start.27) | collective-permute-done | bytes 262176 | tf_op jit(solution)/shard_map/ppermute | solution.py:202
  185.5 4.0 %collective-permute-done.28.third = bf16[128,1024]{1,0:T(8,128)(2,1)S(1)} collective-permute-done((bf16[128,1024]{1,0:T(8,128)(2,1)S(1)}, bf16[128,1024]{1,0:T(8,128)(2,1)S(1)}, u32[]{:S(2)}, u32[]{:S(2)}) %collective-permute-start.28) | collective-permute-done | bytes 262176 | tf_op jit(solution)/shard_map/ppermute | solution.py:202
  189.5 1.4 finish.1
  (60 shorter events, 1.0 us)
Async XLA Ops:
  0.0 13.9 %copy-start.6 = (bf16[32,2048]{1,0:T(8,128)(2,1)S(1)}, bf16[32,2048]{1,0:T(8,128)(2,1)}, u32[]{:S(2)}) copy-start(bf16[32,2048]{1,0:T(8,128)(2,1)} %param.13) | copy-start | bytes 393220
  0.0 43.7 %collective-permute-start.10 = (bf16[256,2048]{1,0:T(8,128)(2,1)}, bf16[256,2048]{1,0:T(8,128)(2,1)}, u32[]{:S(2)}, u32[]{:S(2)}) collective-permute-start(bf16[256,2048]{1,0:T(8,128)(2,1)} %refs_0_.3), channel_id=1, source_target_pairs={{0,4},{1,3},{2,6},{3,1},{4,0},{5,7},{6,2},{7,5},{8,12},{9,11},{10,... | collective-permute-start | bytes 3145736 | tf_op jit(solution)/shard_map/ppermute | solution.py:202
  1.5 42.1 %collective-permute-start.9 = (bf16[256,2048]{1,0:T(8,128)(2,1)}, bf16[256,2048]{1,0:T(8,128)(2,1)}, u32[]{:S(2)}, u32[]{:S(2)}) collective-permute-start(bf16[256,2048]{1,0:T(8,128)(2,1)} %refs_0_.3), channel_id=1, source_target_pairs={{0,2},{1,5},{2,0},{3,7},{4,6},{5,1},{6,4},{7,3},{8,10},{9,13},{10,... | collective-permute-start | bytes 3145736 | tf_op jit(solution)/shard_map/ppermute | solution.py:202
  3.8 1.0 copy-start
  4.8 0.9 copy-start.1
  5.7 0.8 copy-start.2
  6.6 0.8 copy-start.3
  7.4 6.5 %copy-start.8 = (f32[4096]{0:T(1024)S(1)}, f32[4096]{0:T(1024)}, u32[]{:S(2)}) copy-start(f32[4096]{0:T(1024)} %param.14) | copy-start | bytes 49156
  7.4 10.7 %copy-start.4 = (bf16[128,2048]{1,0:T(8,128)(2,1)S(1)}, bf16[128,2048]{1,0:T(8,128)(2,1)}, u32[]{:S(2)}) copy-start(bf16[128,2048]{1,0:T(8,128)(2,1)} %param.12) | copy-start | bytes 1572868
  7.4 10.7 %copy-start.7 = (bf16[8,2048]{1,0:T(8,128)(2,1)S(1)}, bf16[8,2048]{1,0:T(8,128)(2,1)}, u32[]{:S(2)}) copy-start(bf16[8,2048]{1,0:T(8,128)(2,1)} %param.21) | copy-start | bytes 98308
  8.3 15.1 %collective-permute-start.2 = (bf16[336,512]{1,0:T(8,128)(2,1)S(1)}, bf16[336,512]{1,0:T(8,128)(2,1)S(1)}, u32[]{:S(2)}, u32[]{:S(2)}) collective-permute-start(bf16[336,512]{1,0:T(8,128)(2,1)S(1)} %get-tuple-element.41), channel_id=1, source_target_pairs={{0,8},{1,9},{2,10},{3,11},{4,12},{5,13},{6,14},{7,15},{8,0},{9,1},... | collective-permute-start | bytes 1032200 | tf_op jit(solution)/shard_map/ppermute | solution.py:202
  10.0 10.1 %copy-start.5 = (bf16[2048,256]{1,0:T(8,128)(2,1)S(1)}, bf16[2048,256]{1,0:T(8,128)(2,1)}, u32[]{:S(2)}) copy-start(bf16[2048,256]{1,0:T(8,128)(2,1)} %param.18) | copy-start | bytes 3145732
  14.7 8.8 %collective-permute-start.1 = (bf16[32,2048]{1,0:T(8,128)(2,1)}, bf16[32,2048]{1,0:T(8,128)(2,1)}, u32[]{:S(2)}, u32[]{:S(2)}) collective-permute-start(bf16[32,2048]{1,0:T(8,128)(2,1)} %fusion.5), channel_id=1, source_target_pairs={{0,0},{1,16},{2,1},{3,17},{4,8},{5,24},{6,9},{7,25},{8,2},{9,18},{... | collective-permute-start | bytes 393224 | tf_op jit(solution)/shard_map/ppermute | solution.py:202
  18.6 12.1 %collective-permute-start = (bf16[144,2048]{1,0:T(8,128)(2,1)S(1)}, bf16[144,2048]{1,0:T(8,128)(2,1)}, u32[]{:S(2)}, u32[]{:S(2)}) collective-permute-start(bf16[144,2048]{1,0:T(8,128)(2,1)S(1)} %fusion.2), channel_id=1, source_target_pairs={{1,16},{3,18},{5,20},{7,22},{9,24},{11,26},{13,28},{15,30},{16,1},... | collective-permute-start | bytes 1769480 | tf_op jit(solution)/shard_map/ppermute | solution.py:202
  23.6 18.6 %collective-permute-start.7 = (bf16[2,256,512]{2,1,0:T(8,128)(2,1)S(1)}, bf16[2,256,512]{2,1,0:T(8,128)(2,1)S(1)}, u32[]{:S(2)}, u32[]{:S(2)}) collective-permute-start(bf16[2,256,512]{2,1,0:T(8,128)(2,1)S(1)} %pad_maximum_fusion.3.own), channel_id=1, source_target_pairs={{0,2},{1,5},{2,0},{3,7},{4,6},{5,1},{6,4},{7,3},{8,10},{9,13},{10,... | collective-permute-start | bytes 1572872 | tf_op jit(solution)/shard_map/ppermute | solution.py:202
  32.1 24.9 %collective-permute-start.3 = (bf16[176,2048]{1,0:T(8,128)(2,1)S(1)}, bf16[176,2048]{1,0:T(8,128)(2,1)S(1)}, u32[]{:S(2)}, u32[]{:S(2)}) collective-permute-start(bf16[176,2048]{1,0:T(8,128)(2,1)S(1)} %pad_maximum_fusion.2.x0), channel_id=1, source_target_pairs={{0,8},{1,9},{2,10},{3,11},{4,12},{5,13},{6,14},{7,15},{8,0},{9,1},... | collective-permute-start | bytes 2162696 | tf_op jit(solution)/shard_map/ppermute | solution.py:202
  32.2 24.8 %collective-permute-start.4 = (bf16[512,256]{1,0:T(8,128)(2,1)S(1)}, bf16[512,256]{1,0:T(8,128)(2,1)S(1)}, u32[]{:S(2)}, u32[]{:S(2)}) collective-permute-start(bf16[512,256]{1,0:T(8,128)(2,1)S(1)} %get-tuple-element.86), channel_id=1, source_target_pairs={{0,16},{1,17},{2,18},{3,19},{4,20},{5,21},{6,22},{7,23},{8,24},{9,... | collective-permute-start | bytes 786440 | tf_op jit(solution)/shard_map/ppermute | solution.py:202
  42.3 29.9 %collective-permute-start.8 = (bf16[4,256,512]{2,1,0:T(8,128)(2,1)S(1)}, bf16[4,256,512]{2,1,0:T(8,128)(2,1)S(1)}, u32[]{:S(2)}, u32[]{:S(2)}) collective-permute-start(bf16[4,256,512]{2,1,0:T(8,128)(2,1)S(1)} %pad_maximum_fusion), channel_id=1, source_target_pairs={{0,4},{1,3},{2,6},{3,1},{4,0},{5,7},{6,2},{7,5},{8,12},{9,11},{10,... | collective-permute-start | bytes 3145736 | tf_op jit(solution)/shard_map/ppermute | solution.py:202
  43.7 28.6 %collective-permute-start.11 = (bf16[256,2048]{1,0:T(8,128)(2,1)}, bf16[256,2048]{1,0:T(8,128)(2,1)S(1)}, u32[]{:S(2)}, u32[]{:S(2)}) collective-permute-start(bf16[256,2048]{1,0:T(8,128)(2,1)} %collective-permute-done.9.refs_1_), channel_id=1, source_target_pairs={{0,4},{1,3},{2,6},{3,1},{4,0},{5,7},{6,2},{7,5},{8,12},{9,11},{10,... | collective-permute-start | bytes 3145736 | tf_op jit(solution)/shard_map/ppermute | solution.py:202
  44.6 27.7 %collective-permute-start.6 = (bf16[176,2048]{1,0:T(8,128)(2,1)S(1)}, bf16[176,2048]{1,0:T(8,128)(2,1)S(1)}, u32[]{:S(2)}, u32[]{:S(2)}) collective-permute-start(bf16[176,2048]{1,0:T(8,128)(2,1)S(1)} %pad_maximum_fusion.2.x0), channel_id=1, source_target_pairs={{0,1},{1,0},{2,3},{3,2},{4,5},{5,4},{6,7},{7,6},{8,9},{9,8},{10,11... | collective-permute-start | bytes 2162696 | tf_op jit(solution)/shard_map/ppermute | solution.py:202
  57.0 15.3 %collective-permute-start.5 = (bf16[176,2048]{1,0:T(8,128)(2,1)S(1)}, bf16[176,2048]{1,0:T(8,128)(2,1)S(1)}, u32[]{:S(2)}, u32[]{:S(2)}) collective-permute-start(bf16[176,2048]{1,0:T(8,128)(2,1)S(1)} %collective-permute-done.3.x1), channel_id=1, source_target_pairs={{0,1},{1,0},{2,3},{3,2},{4,5},{5,4},{6,7},{7,6},{8,9},{9,8},{10,11... | collective-permute-start | bytes 2162696 | tf_op jit(solution)/shard_map/ppermute | solution.py:202
  58.6 13.7 %collective-permute-start.12 = (bf16[512,256]{1,0:T(8,128)(2,1)S(1)}, bf16[512,256]{1,0:T(8,128)(2,1)S(1)}, u32[]{:S(2)}, u32[]{:S(2)}) collective-permute-start(bf16[512,256]{1,0:T(8,128)(2,1)S(1)} %get-tuple-element.85), channel_id=1, source_target_pairs={{0,16},{1,17},{2,18},{3,19},{4,20},{5,21},{6,22},{7,23},{8,24},{9,... | collective-permute-start | bytes 786440 | tf_op jit(solution)/shard_map/ppermute | solution.py:202
  72.3 2.1 %copy-start.9 = (bf16[256,2048]{1,0:T(8,128)(2,1)}, bf16[256,2048]{1,0:T(8,128)(2,1)S(1)}, u32[]{:S(2)}) copy-start(bf16[256,2048]{1,0:T(8,128)(2,1)S(1)} %collective-permute-done.11.refs_3_) | copy-start | bytes 3145732
  74.4 18.7 %collective-permute-start.14 = (bf16[736,256]{1,0:T(8,128)(2,1)S(1)}, bf16[736,256]{1,0:T(8,128)(2,1)S(1)}, u32[]{:S(2)}, u32[]{:S(2)}) collective-permute-start(bf16[736,256]{1,0:T(8,128)(2,1)S(1)} %get-tuple-element.63), channel_id=1, source_target_pairs={{0,16},{1,17},{2,18},{3,19},{4,20},{5,21},{6,22},{7,23},{8,24},{9,... | collective-permute-start | bytes 1130504 | tf_op jit(solution)/shard_map/ppermute | solution.py:202
  82.8 19.5 %collective-permute-start.19 = (bf16[4,128,512]{2,1,0:T(8,128)(2,1)S(1)}, bf16[4,128,512]{2,1,0:T(8,128)(2,1)S(1)}, u32[]{:S(2)}, u32[]{:S(2)}) collective-permute-start(bf16[4,128,512]{2,1,0:T(8,128)(2,1)S(1)} %get-tuple-element.66), channel_id=1, source_target_pairs={{0,8},{1,9},{2,10},{3,11},{4,12},{5,13},{6,14},{7,15},{8,0},{9,1},... | collective-permute-start | bytes 1572872 | tf_op jit(solution)/shard_map/ppermute | solution.py:202
  83.0 38.3 %collective-permute-start.18 = (bf16[2,1024,256]{2,1,0:T(8,128)(2,1)S(1)}, bf16[2,1024,256]{2,1,0:T(8,128)(2,1)S(1)}, u32[]{:S(2)}, u32[]{:S(2)}) collective-permute-start(bf16[2,1024,256]{2,1,0:T(8,128)(2,1)S(1)} %pad_maximum_fusion.1.refs_4_), channel_id=1, source_target_pairs={{0,2},{1,5},{2,0},{3,7},{4,6},{5,1},{6,4},{7,3},{8,10},{9,13},{10,... | collective-permute-start | bytes 3145736 | tf_op jit(solution)/shard_map/ppermute | solution.py:202
  94.2 11.7 %collective-permute-start.15 = (bf16[6,128,256]{2,1,0:T(8,128)(2,1)S(1)}, bf16[6,128,256]{2,1,0:T(8,128)(2,1)S(1)}, u32[]{:S(2)}, u32[]{:S(2)}) collective-permute-start(bf16[6,128,256]{2,1,0:T(8,128)(2,1)S(1)} %keys_join.1.kv0), channel_id=1, source_target_pairs={{0,2},{1,5},{2,0},{3,7},{4,6},{5,1},{6,4},{7,3},{8,10},{9,13},{10,... | collective-permute-start | bytes 1179656 | tf_op jit(solution)/shard_map/ppermute | solution.py:202
  102.4 24.1 %collective-permute-start.20 = (bf16[4,128,512]{2,1,0:T(8,128)(2,1)S(1)}, bf16[4,128,512]{2,1,0:T(8,128)(2,1)S(1)}, u32[]{:S(2)}, u32[]{:S(2)}) collective-permute-start(bf16[4,128,512]{2,1,0:T(8,128)(2,1)S(1)} %add_convert_fusion), channel_id=1, source_target_pairs={{0,16},{1,17},{2,18},{3,19},{4,20},{5,21},{6,22},{7,23},{8,24},{9,... | collective-permute-start | bytes 1572872 | tf_op jit(solution)/shard_map/ppermute | solution.py:202
  105.1 23.5 %collective-permute-start.13 = (bf16[4,128,512]{2,1,0:T(8,128)(2,1)S(1)}, bf16[4,128,512]{2,1,0:T(8,128)(2,1)S(1)}, u32[]{:S(2)}, u32[]{:S(2)}) collective-permute-start(bf16[4,128,512]{2,1,0:T(8,128)(2,1)S(1)} %get-tuple-element.61), channel_id=1, source_target_pairs={{0,8},{1,9},{2,10},{3,11},{4,12},{5,13},{6,14},{7,15},{8,0},{9,1},... | collective-permute-start | bytes 1572872 | tf_op jit(solution)/shard_map/ppermute | solution.py:202
  105.1 16.2 %collective-permute-start.16 = (bf16[6,128,256]{2,1,0:T(8,128)(2,1)S(1)}, bf16[6,128,256]{2,1,0:T(8,128)(2,1)S(1)}, u32[]{:S(2)}, u32[]{:S(2)}) collective-permute-start(bf16[6,128,256]{2,1,0:T(8,128)(2,1)S(1)} %keys_join.1.kv0), channel_id=1, source_target_pairs={{0,4},{1,3},{2,6},{3,1},{4,0},{5,7},{6,2},{7,5},{8,12},{9,11},{10,... | collective-permute-start | bytes 1179656 | tf_op jit(solution)/shard_map/ppermute | solution.py:202
  105.9 15.4 %collective-permute-start.17 = (bf16[6,128,256]{2,1,0:T(8,128)(2,1)S(1)}, bf16[6,128,256]{2,1,0:T(8,128)(2,1)S(1)}, u32[]{:S(2)}, u32[]{:S(2)}) collective-permute-start(bf16[6,128,256]{2,1,0:T(8,128)(2,1)S(1)} %keys_join.1.kv0), channel_id=1, source_target_pairs={{0,6},{1,7},{2,4},{3,5},{4,2},{5,3},{6,0},{7,1},{8,14},{9,15},{10,... | collective-permute-start | bytes 1179656 | tf_op jit(solution)/shard_map/ppermute | solution.py:202
  126.6 21.7 %collective-permute-start.23 = (bf16[2,1024,256]{2,1,0:T(8,128)(2,1)S(1)}, bf16[2,1024,256]{2,1,0:T(8,128)(2,1)S(1)}, u32[]{:S(2)}, u32[]{:S(2)}) collective-permute-start(bf16[2,1024,256]{2,1,0:T(8,128)(2,1)S(1)} %pad_maximum_fusion.1.refs_4_), channel_id=1, source_target_pairs={{0,4},{1,3},{2,6},{3,1},{4,0},{5,7},{6,2},{7,5},{8,12},{9,11},{10,... | collective-permute-start | bytes 3145736 | tf_op jit(solution)/shard_map/ppermute | solution.py:202
  127.4 25.2 %collective-permute-start.24 = (bf16[2,1024,256]{2,1,0:T(8,128)(2,1)S(1)}, bf16[2,1024,256]{2,1,0:T(8,128)(2,1)S(1)}, u32[]{:S(2)}, u32[]{:S(2)}) collective-permute-start(bf16[2,1024,256]{2,1,0:T(8,128)(2,1)S(1)} %collective-permute-done.18.refs_5_), channel_id=1, source_target_pairs={{0,4},{1,3},{2,6},{3,1},{4,0},{5,7},{6,2},{7,5},{8,12},{9,11},{10,... | collective-permute-start | bytes 3145736 | tf_op jit(solution)/shard_map/ppermute | solution.py:202
  133.3 8.6 %collective-permute-start.22 = (bf16[512,256]{1,0:T(8,128)(2,1)S(1)}, bf16[512,256]{1,0:T(8,128)(2,1)S(1)}, u32[]{:S(2)}, u32[]{:S(2)}) collective-permute-start(bf16[512,256]{1,0:T(8,128)(2,1)S(1)} %attend.3.refs_1_), channel_id=1, source_target_pairs={{0,8},{1,9},{2,10},{3,11},{4,12},{5,13},{6,14},{7,15},{8,0},{9,1},... | collective-permute-start | bytes 786440 | tf_op jit(solution)/shard_map/ppermute | solution.py:202
  140.8 7.4 %collective-permute-start.21 = (bf16[512,256]{1,0:T(8,128)(2,1)S(1)}, bf16[512,256]{1,0:T(8,128)(2,1)S(1)}, u32[]{:S(2)}, u32[]{:S(2)}) collective-permute-start(bf16[512,256]{1,0:T(8,128)(2,1)S(1)} %attend.2.refs_0_), channel_id=1, source_target_pairs={{0,8},{1,9},{2,10},{3,11},{4,12},{5,13},{6,14},{7,15},{8,0},{9,1},... | collective-permute-start | bytes 786440 | tf_op jit(solution)/shard_map/ppermute | solution.py:202
  152.6 1.0 copy-start.10
  157.5 2.7 %collective-permute-start.25 = (bf16[4,128,1024]{2,1,0:T(8,128)(2,1)S(1)}, bf16[4,128,1024]{2,1,0:T(8,128)(2,1)S(1)}, u32[]{:S(2)}, u32[]{:S(2)}) collective-permute-start(bf16[4,128,1024]{2,1,0:T(8,128)(2,1)S(1)} %get-tuple-element.76), channel_id=1, source_target_pairs={{0,1},{1,0},{2,3},{3,2},{4,5},{5,4},{6,7},{7,6},{8,9},{9,8},{10,11... | collective-permute-start | bytes 3145736 | tf_op jit(solution)/shard_map/ppermute | solution.py:202
  162.0 9.8 %collective-permute-start.26 = (bf16[128,1024]{1,0:T(8,128)(2,1)S(1)}, bf16[128,1024]{1,0:T(8,128)(2,1)S(1)}, u32[]{:S(2)}, u32[]{:S(2)}) collective-permute-start(bf16[128,1024]{1,0:T(8,128)(2,1)S(1)} %get-tuple-element.81), channel_id=1, source_target_pairs={{0,8},{1,9},{2,10},{3,11},{4,12},{5,13},{6,14},{7,15},{8,16},{9,17... | collective-permute-start | bytes 786440 | tf_op jit(solution)/shard_map/ppermute | solution.py:202
  162.8 22.7 %collective-permute-start.27 = (bf16[128,1024]{1,0:T(8,128)(2,1)S(1)}, bf16[128,1024]{1,0:T(8,128)(2,1)S(1)}, u32[]{:S(2)}, u32[]{:S(2)}) collective-permute-start(bf16[128,1024]{1,0:T(8,128)(2,1)S(1)} %get-tuple-element.80), channel_id=1, source_target_pairs={{0,16},{1,17},{2,18},{3,19},{4,20},{5,21},{6,22},{7,23},{8,24},{9,... | collective-permute-start | bytes 786440 | tf_op jit(solution)/shard_map/ppermute | solution.py:202
  167.1 22.4 %collective-permute-start.28 = (bf16[128,1024]{1,0:T(8,128)(2,1)S(1)}, bf16[128,1024]{1,0:T(8,128)(2,1)S(1)}, u32[]{:S(2)}, u32[]{:S(2)}) collective-permute-start(bf16[128,1024]{1,0:T(8,128)(2,1)S(1)} %get-tuple-element.79), channel_id=1, source_target_pairs={{0,24},{1,25},{2,26},{3,27},{4,28},{5,29},{6,30},{7,31},{8,0},{9,1... | collective-permute-start | bytes 786440 | tf_op jit(solution)/shard_map/ppermute | solution.py:202

commit v13 on v12

--- a/solution.py
+++ b/solution.py
@@ -510,6 +510,18 @@
     slots = (recompute_slots - seq_index * CACHED).astype(jnp.bfloat16)
     slot_rows = jnp.broadcast_to(jnp.pad(slots, (0, REC_PAD - REC))[:, None], (REC_PAD, 4 * HD))
     depth = w_key.shape[0]
+    rows = jnp.concatenate(
+        [text_rows, recompute_rows, jnp.zeros((REC_PAD - REC, width), text_rows.dtype)], axis=0
+    )
+    gain = lax.dynamic_slice_in_dim(norm_gain, core * width, width, 0)
+    wide, pictures = rows.astype(jnp.float32), picture_rows.astype(jnp.float32)
+    squares, picture_squares = lax.psum(
+        (jnp.sum(wide * wide, axis=1), jnp.sum(pictures * pictures, axis=1)), "head"
+    )
+    normed = scaled(wide, squares, gain)
+    pictures = scaled(pictures, picture_squares, gain)
+
+    normed, pictures, slot_rows = lax.optimization_barrier((normed, pictures, slot_rows))
     key_own, key_give = pl.pallas_call(
         pack_kernel,
         out_shape=(shaped((depth + CACHED + REC_PAD, 4 * HD)),) * 2,
@@ -517,19 +529,11 @@
         out_specs=(HBM,) * 2,
         scratch_shapes=[pltpu.SemaphoreType.DMA((PACK_COPIES,))],
         compiler_params=PARAMS,
+        cost_estimate=pl.CostEstimate(
+            flops=6_000_000_000, bytes_accessed=4_000_000, transcendentals=0
+        ),
         name="pack",
     )(where, w_key, w_value, cache_keys, cache_values, slot_rows)
-
-    rows = jnp.concatenate(
-        [text_rows, recompute_rows, jnp.zeros((REC_PAD - REC, width), text_rows.dtype)], axis=0
-    )
-    gain = lax.dynamic_slice_in_dim(norm_gain, core * width, width, 0)
-    wide, pictures = rows.astype(jnp.float32), picture_rows.astype(jnp.float32)
-    squares, picture_squares = lax.psum(
-        (jnp.sum(wide * wide, axis=1), jnp.sum(pictures * pictures, axis=1)), "head"
-    )
-    normed = scaled(wide, squares, gain)
-    pictures = scaled(pictures, picture_squares, gain)
 
     out_rows = w_out.shape[0] // 2
     out_own, out_give = (
@@ -550,14 +554,11 @@
     held = jnp.concatenate([jnp.where(own_first, normed, crossed), shown], axis=0)
     next_rows = across(held, 1)
     held_other = other_core(held)
-    out_half = out_rows // 2
-    out_got0 = across(out_give[:out_half], 2)
-    out_got1 = across(out_give[out_half:], 2)
-    next_rows, out_got0 = lax.optimization_barrier((next_rows, out_got0))
+    next_rows, out_got = lax.optimization_barrier((next_rows, across(out_give, 2)))
     next_other = other_core(next_rows)
     keys_far = to_far(jnp.concatenate([keys, keys_near], axis=0))
-    next_other, held_other, keys_far, query_both, out_got1 = lax.optimization_barrier(
-        (next_other, held_other, keys_far, query_both, out_got1)
+    next_other, held_other, keys_far, query_both = lax.optimization_barrier(
+        (next_other, held_other, keys_far, query_both)
     )
     parts = (held, next_rows, held_other, next_other)
 
@@ -606,7 +607,7 @@
     got_near2 = across(q_send2, 1)
     got_near = across(q_send, 1)
     got_queries = across((q_keep2 + got_near2.astype(jnp.float32)).astype(jnp.bfloat16), 2)
-    out_pair = jnp.stack([out_own, jnp.concatenate([out_got0, out_got1], axis=0)])
+    out_pair = jnp.stack([out_own, out_got])
     out_pair, q_send2 = lax.optimization_barrier((out_pair, q_send2))
     out_near = to_near(out_pair)
     got_keys, q_send2 = lax.optimization_barrier((across(send, 2), q_send2))
@@ -618,15 +619,15 @@
         scratch_shapes=[pltpu.VMEM((all_rows, 2 * HD), jnp.float32)],
         compiler_params=PARAMS,
         cost_estimate=pl.CostEstimate(
-            flops=12_000_000_000, bytes_accessed=4_000_000, transcendentals=0
+            flops=24_000_000_000, bytes_accessed=4_000_000, transcendentals=0
         ),
         name="keys_join",
     )(where, keep, got_keys, old_own, old_next, cosine, sine)
     kv_near, kv_far = to_near(kv), to_far(kv)
     kv_both = permuted(kv, lambda z, p, c: (z, p ^ 3, c))
 
-    kv_near, kv_far, kv_both, out_near, out_pair, got_queries = lax.optimization_barrier(
-        (kv_near, kv_far, kv_both, out_near, out_pair, got_queries)
+    kv_near, kv_far, kv_both, out_near, out_pair, got_near = lax.optimization_barrier(
+        (kv_near, kv_far, kv_both, out_near, out_pair, got_near)
     )
     out_far, out_both = to_far(out_pair), to_far(out_near)
 

time: 191 us -> 189 us (0.990)
  waiting for transfers between devices: 100 us -> 109 us
  starting transfers between devices: 49.1 us -> 43 us
  local copies, waits for them, and re-layouts: 5 us -> 2.09 us
  other arithmetic: 10 us -> 8.05 us
    ppermute x29 -> x28, waiting for transfers between devices: 100 us -> 109 us  [permuted(): return lax.ppermute(value, ('seq', 'head'), perm)]
    ppermute x29 -> x28, starting transfers between devices: 49.1 us -> 43 us  [permuted(): return lax.ppermute(value, ('seq', 'head'), perm)]
    unnamed x22 -> x20, local copies, waits for them, and re-layouts: 4.59 us -> 1.02 us
  transfers between devices with their start and end apart: 29 -> 28, of which waited for: 14 -> 14; matrix products, arithmetic and copies ran while one was open for 4% -> 4% of each run, Pallas kernels for 9% -> 6%
where the time goes in v13:
time: 189 us
  waiting for transfers between devices  109 us (58%)
  starting transfers between devices  43 us (23%)
  Pallas kernels  23.9 us (13%)
  other arithmetic  8.05 us (4%)
  blocking collectives  2.46 us (1%)
  local copies, waits for them, and re-layouts  2.09 us (1%)
    ppermute x28, waiting for transfers between devices, permuted(): return lax.ppermute(value, ('seq', 'head'), perm)  109 us
    ppermute x28, starting transfers between devices, permuted(): return lax.ppermute(value, ('seq', 'head'), perm)  43 us
    pallas_call x2, Pallas kernels, by_levels(): pl.pallas_call(functools.partial(attend_kernel, pair), out_shape=shaped((...  9.47 us
    pallas_call x1, Pallas kernels, by_levels(): pl.pallas_call(queries_part_kernel, out_shape=(shaped(group_shape, jnp.fl...  5 us
    pallas_call x1, Pallas kernels, by_levels(): pl.pallas_call(output_kernel, out_shape=(shaped((LEVELS, tok, wide_cols),...  3.89 us
  transfers between devices with their start and end apart: 28, of which 14 were waited for; matrix products, arithmetic and copies ran while one was open for 4% of the time, Pallas kernels for 6%

profile of v13, /device:TPU:8, one launch (start us, length us, event | category | flops | bytes accessed | tf_op | source)
XLA Modules:
  0.0 188.9 jit_solution(14331276600376030097)
XLA Ops:
  0.0 1.6 collective-permute-start.10
  1.6 1.5 collective-permute-start.9
  3.1 1.0 fusion.3
  4.2 0.1 pad.22.clone
  4.2 1.4 fusion
  5.6 2.5 %all-reduce.1 = (f32[144]{0:T(256)S(1)}, f32[32]{0:T(128)S(1)}) all-reduce(f32[144]{0:T(256)S(1)} %fusion, f32[32]{0:T(128)S(1)} %fusion.3), channel_id=1, replica_groups=mesh['seq'=16,'head'=2] {'head'}, use_global_device_ids=true, to_apply=%region_1.2 | all-reduce | flops 176 | bytes 1408 | tf_op jit(solution)/shard_map/psum | solution.py:518
  8.1 0.7 dynamic_slice.9
  8.8 1.1 fusion.2
  10.0 0.1 fusion.5
  10.1 0.1 broadcast_in_dim.5.refs_4_
  10.2 0.1 stack.41.where_ref
  10.3 0.9 pack.1
  11.2 0.5 collective-permute-start.2
  11.7 3.4 %collective-permute-start.1 = (bf16[32,2048]{1,0:T(8,128)(2,1)S(1)}, bf16[32,2048]{1,0:T(8,128)(2,1)S(1)}, u32[]{:S(2)}, u32[]{:S(2)}) collective-permute-start(bf16[32,2048]{1,0:T(8,128)(2,1)S(1)} %fusion.5), channel_id=1, source_target_pairs={{0,0},{1,16},{2,1},{3,17},{4,8},{5,24},{6,9},{7,25},{8,2},{9,18},{... | collective-permute-start | bytes 393224 | tf_op jit(solution)/shard_map/ppermute | solution.py:202
  15.2 1.5 collective-permute-start
  16.7 0.1 dynamic-slice_bitcast_fusion
  16.8 8.2 %collective-permute-done.1 = bf16[32,2048]{1,0:T(8,128)(2,1)S(1)} collective-permute-done((bf16[32,2048]{1,0:T(8,128)(2,1)S(1)}, bf16[32,2048]{1,0:T(8,128)(2,1)S(1)}, u32[]{:S(2)}, u32[]{:S(2)}) %collective-permute-start.1) | collective-permute-done | bytes 131104 | tf_op jit(solution)/shard_map/ppermute | solution.py:202
  25.1 5.5 %collective-permute-start.7 = (bf16[2,256,512]{2,1,0:T(8,128)(2,1)S(1)}, bf16[2,256,512]{2,1,0:T(8,128)(2,1)S(1)}, u32[]{:S(2)}, u32[]{:S(2)}) collective-permute-start(bf16[2,256,512]{2,1,0:T(8,128)(2,1)S(1)} %pad_maximum_fusion.3.own), channel_id=1, source_target_pairs={{0,2},{1,5},{2,0},{3,7},{4,6},{5,1},{6,4},{7,3},{8,10},{9,13},{10,... | collective-permute-start | bytes 1572872 | tf_op jit(solution)/shard_map/ppermute | solution.py:202
  30.9 8.0 %collective-permute-start.4 = (bf16[1024,256]{1,0:T(8,128)(2,1)S(1)}, bf16[1024,256]{1,0:T(8,128)(2,1)S(1)}, u32[]{:S(2)}, u32[]{:S(2)}) collective-permute-start(bf16[1024,256]{1,0:T(8,128)(2,1)S(1)} %get-tuple-element.50), channel_id=1, source_target_pairs={{0,16},{1,17},{2,18},{3,19},{4,20},{5,21},{6,22},{7,23},{8,24},{9,... | collective-permute-start | bytes 1572872 | tf_op jit(solution)/shard_map/ppermute | solution.py:202
  38.8 0.1 pad_maximum_fusion
  38.9 0.5 collective-permute-start.8
  39.5 1.6 collective-permute-start.11
  41.0 20.9 %collective-permute-done.4 = bf16[1024,256]{1,0:T(8,128)(2,1)S(1)} collective-permute-done((bf16[1024,256]{1,0:T(8,128)(2,1)S(1)}, bf16[1024,256]{1,0:T(8,128)(2,1)S(1)}, u32[]{:S(2)}, u32[]{:S(2)}) %collective-permute-start.4) | collective-permute-done | bytes 524320 | tf_op jit(solution)/shard_map/ppermute | solution.py:202
  61.9 0.1 add_convert_fusion.4
  62.0 0.1 add_convert_fusion.5
  62.1 2.0 %collective-permute-done.5.x3 = bf16[176,2048]{1,0:T(8,128)(2,1)S(1)} collective-permute-done((bf16[176,2048]{1,0:T(8,128)(2,1)S(1)}, bf16[176,2048]{1,0:T(8,128)(2,1)S(1)}, u32[]{:S(2)}, u32[]{:S(2)}) %collective-permute-start.5) | collective-permute-done | bytes 720928 | tf_op jit(solution)/shard_map/ppermute | solution.py:202
  64.1 0.9 collective-permute-done.11.refs_3_
  65.0 2.1 %keys_part.1 = (f32[576,256]{1,0:T(8,128)S(1)}, bf16[736,256]{1,0:T(8,128)(2,1)S(1)}) custom-call(s32[5]{0:T(128)S(1)} %stack.41.where_ref, bf16[176,2048]{1,0:T(8,128)(2,1)S(1)} %pad_maximum_fusion.2.x0, bf16[176,2048]{1,0:T(8,128)(2,1)S(1)} %collective-permute-done.3.x1, bf16[176,2048]{1,0:T(8,128)(2,1)S(1)} %collective-permute-done.6.x2, ...), custom_call_target="tpu_custom_call" | custom-call | flops 3000000000 | bytes 4000000 | tf_op jit(solution)/shard_map/keys_part/pallas_call | solution.py:578
  67.1 5.0 %queries_part.1 = (f32[4,128,512]{2,1,0:T(8,128)S(1)}, f32[4,128,512]{2,1,0:T(8,128)S(1)}, bf16[4,128,512]{2,1,0:T(8,128)(2,1)S(1)}, bf16[4,128,512]{2,1,0:T(8,128)(2,1)S(1)}) custom-call(s32[5]{0:T(128)S(1)} %stack.41.where_ref, bf16[176,2048]{1,0:T(8,128)(2,1)S(1)} %pad_maximum_fusion.2.x0, bf16[176,2048]{1,0:T(8,128)(2,1)S(1)} %collective-permute-done.3.x1, ...), custom_call_target="tpu_custom_call" | custom-call | flops 5000000000 | bytes 4000000 | tf_op jit(solution)/shard_map/queries_part/pallas_call | solution.py:595
  72.2 1.9 %collective-permute-start.18 = (bf16[4,128,512]{2,1,0:T(8,128)(2,1)S(1)}, bf16[4,128,512]{2,1,0:T(8,128)(2,1)S(1)}, u32[]{:S(2)}, u32[]{:S(2)}) collective-permute-start(bf16[4,128,512]{2,1,0:T(8,128)(2,1)S(1)} %get-tuple-element.69), channel_id=1, source_target_pairs={{0,8},{1,9},{2,10},{3,11},{4,12},{5,13},{6,14},{7,15},{8,0},{9,1},... | collective-permute-start | bytes 1572872 | tf_op jit(solution)/shard_map/ppermute | solution.py:202
  74.1 1.4 fusion.9
  75.5 0.7 collective-permute-start.12
  76.2 0.2 pad_maximum_fusion.4.cos_ref
  76.4 0.2 pad_maximum_fusion.5.sin_ref
  76.5 0.1 pad_maximum_fusion.1.refs_4_
  76.6 1.0 collective-permute-start.16
  77.7 2.0 %collective-permute-start.17 = (bf16[4,128,512]{2,1,0:T(8,128)(2,1)S(1)}, bf16[4,128,512]{2,1,0:T(8,128)(2,1)S(1)}, u32[]{:S(2)}, u32[]{:S(2)}) collective-permute-start(bf16[4,128,512]{2,1,0:T(8,128)(2,1)S(1)} %get-tuple-element.71), channel_id=1, source_target_pairs={{0,8},{1,9},{2,10},{3,11},{4,12},{5,13},{6,14},{7,15},{8,0},{9,1},... | collective-permute-start | bytes 1572872 | tf_op jit(solution)/shard_map/ppermute | solution.py:202
  79.7 15.8 %collective-permute-done.12.got_ref = bf16[736,256]{1,0:T(8,128)(2,1)S(1)} collective-permute-done((bf16[736,256]{1,0:T(8,128)(2,1)S(1)}, bf16[736,256]{1,0:T(8,128)(2,1)S(1)}, u32[]{:S(2)}, u32[]{:S(2)}) %collective-permute-start.12) | collective-permute-done | bytes 376864 | tf_op jit(solution)/shard_map/ppermute | solution.py:202
  95.5 0.2 add_convert_fusion
  95.6 2.1 %collective-permute-start.19 = (bf16[4,128,512]{2,1,0:T(8,128)(2,1)S(1)}, bf16[4,128,512]{2,1,0:T(8,128)(2,1)S(1)}, u32[]{:S(2)}, u32[]{:S(2)}) collective-permute-start(bf16[4,128,512]{2,1,0:T(8,128)(2,1)S(1)} %add_convert_fusion), channel_id=1, source_target_pairs={{0,16},{1,17},{2,18},{3,19},{4,20},{5,21},{6,22},{7,23},{8,24},{9,... | collective-permute-start | bytes 1572872 | tf_op jit(solution)/shard_map/ppermute | solution.py:202
  97.7 1.0 keys_join.1.kv0
  98.8 1.0 collective-permute-start.13
  99.8 0.5 collective-permute-start.14
  100.3 13.5 %collective-permute-done.17.near_ref = bf16[4,128,512]{2,1,0:T(8,128)(2,1)S(1)} collective-permute-done((bf16[4,128,512]{2,1,0:T(8,128)(2,1)S(1)}, bf16[4,128,512]{2,1,0:T(8,128)(2,1)S(1)}, u32[]{:S(2)}, u32[]{:S(2)}) %collective-permute-start.17) | collective-permute-done | bytes 524320 | tf_op jit(solution)/shard_map/ppermute | solution.py:202
  113.8 10.9 %collective-permute-done.15.kv3 = bf16[6,128,256]{2,1,0:T(8,128)(2,1)S(1)} collective-permute-done((bf16[6,128,256]{2,1,0:T(8,128)(2,1)S(1)}, bf16[6,128,256]{2,1,0:T(8,128)(2,1)S(1)}, u32[]{:S(2)}, u32[]{:S(2)}) %collective-permute-start.15) | collective-permute-done | bytes 393248 | tf_op jit(solution)/shard_map/ppermute | solution.py:202
  124.7 0.5 collective-permute-start.22
  125.1 1.6 collective-permute-start.23
  126.7 4.7 %attend.3.refs_1_ = bf16[512,256]{1,0:T(8,128)(2,1)S(1)} custom-call(s32[5]{0:T(128)S(1)} %stack.41.where_ref, f32[4,128,512]{2,1,0:T(8,128)S(1)} %get-tuple-element.65.keep_ref, bf16[4,128,512]{2,1,0:T(8,128)(2,1)S(1)} %collective-permute-done.17.near_ref, bf16[4,128,512]{2,1,0:T(8,128)(2,1)S(1)} %collective-permute-done.19.got_ref, ...), custom_call_target="tpu_custom_call" | custom-call | flops 4000000000 | bytes 4000000 | tf_op jit(solution)/shard_map/attend/pallas_call | solution.py:635
  131.4 2.5 %collective-permute-start.21 = (bf16[512,256]{1,0:T(8,128)(2,1)S(1)}, bf16[512,256]{1,0:T(8,128)(2,1)S(1)}, u32[]{:S(2)}, u32[]{:S(2)}) collective-permute-start(bf16[512,256]{1,0:T(8,128)(2,1)S(1)} %attend.3.refs_1_), channel_id=1, source_target_pairs={{0,8},{1,9},{2,10},{3,11},{4,12},{5,13},{6,14},{7,15},{8,0},{9,1},... | collective-permute-start | bytes 786440 | tf_op jit(solution)/shard_map/ppermute | solution.py:202
  133.9 4.8 %attend.2.refs_0_ = bf16[512,256]{1,0:T(8,128)(2,1)S(1)} custom-call(s32[5]{0:T(128)S(1)} %stack.41.where_ref, f32[4,128,512]{2,1,0:T(8,128)S(1)} %get-tuple-element.65.keep_ref, bf16[4,128,512]{2,1,0:T(8,128)(2,1)S(1)} %collective-permute-done.17.near_ref, bf16[4,128,512]{2,1,0:T(8,128)(2,1)S(1)} %collective-permute-done.19.got_ref, ...), custom_call_target="tpu_custom_call" | custom-call | flops 4000000000 | bytes 4000000 | tf_op jit(solution)/shard_map/attend/pallas_call | solution.py:635
  138.7 0.1 collective-permute-start.20
  138.8 0.3 collective-permute-done.21.refs_3_
  139.1 6.1 %collective-permute-done.20.refs_2_ = bf16[512,256]{1,0:T(8,128)(2,1)S(1)} collective-permute-done((bf16[512,256]{1,0:T(8,128)(2,1)S(1)}, bf16[512,256]{1,0:T(8,128)(2,1)S(1)}, u32[]{:S(2)}, u32[]{:S(2)}) %collective-permute-start.20) | collective-permute-done | bytes 262176 | tf_op jit(solution)/shard_map/ppermute | solution.py:202
  145.2 5.5 %collective-permute-done.23.refs_7_ = bf16[2,1024,256]{2,1,0:T(8,128)(2,1)S(1)} collective-permute-done((bf16[2,1024,256]{2,1,0:T(8,128)(2,1)S(1)}, bf16[2,1024,256]{2,1,0:T(8,128)(2,1)S(1)}, u32[]{:S(2)}, u32[]{:S(2)}) %collective-permute-start.23) | collective-permute-done | bytes 1048608 | tf_op jit(solution)/shard_map/ppermute | solution.py:202
  150.7 1.0 copy-done.8
  151.7 3.9 %output.1 = (f32[4,128,1024]{2,1,0:T(8,128)}, bf16[4,128,1024]{2,1,0:T(8,128)(2,1)S(1)}) custom-call(s32[5]{0:T(128)S(1)} %stack.41.where_ref, bf16[512,256]{1,0:T(8,128)(2,1)S(1)} %attend.2.refs_0_, bf16[512,256]{1,0:T(8,128)(2,1)S(1)} %attend.3.refs_1_, bf16[512,256]{1,0:T(8,128)(2,1)S(1)} %collective-permute-done.20.refs_2_, ...), custom_call_target="tpu_custom_call" | custom-call | flops 5000000000 | bytes 4000000 | tf_op jit(solution)/shard_map/output/pallas_call | solution.py:652
  155.6 2.7 %collective-permute-done.24 = bf16[4,128,1024]{2,1,0:T(8,128)(2,1)S(1)} collective-permute-done((bf16[4,128,1024]{2,1,0:T(8,128)(2,1)S(1)}, bf16[4,128,1024]{2,1,0:T(8,128)(2,1)S(1)}, u32[]{:S(2)}, u32[]{:S(2)}) %collective-permute-start.24) | collective-permute-done | bytes 1048608 | tf_op jit(solution)/shard_map/ppermute | solution.py:202
  158.2 1.9 fusion.8
  160.1 0.7 collective-permute-start.25
  160.8 4.2 %collective-permute-start.26 = (bf16[128,1024]{1,0:T(8,128)(2,1)S(1)}, bf16[128,1024]{1,0:T(8,128)(2,1)S(1)}, u32[]{:S(2)}, u32[]{:S(2)}) collective-permute-start(bf16[128,1024]{1,0:T(8,128)(2,1)S(1)} %get-tuple-element.84), channel_id=1, source_target_pairs={{0,16},{1,17},{2,18},{3,19},{4,20},{5,21},{6,22},{7,23},{8,24},{9,... | collective-permute-start | bytes 786440 | tf_op jit(solution)/shard_map/ppermute | solution.py:202
  165.0 4.7 %collective-permute-done.25.first = bf16[128,1024]{1,0:T(8,128)(2,1)S(1)} collective-permute-done((bf16[128,1024]{1,0:T(8,128)(2,1)S(1)}, bf16[128,1024]{1,0:T(8,128)(2,1)S(1)}, u32[]{:S(2)}, u32[]{:S(2)}) %collective-permute-start.25) | collective-permute-done | bytes 262176 | tf_op jit(solution)/shard_map/ppermute | solution.py:202
  169.7 13.8 %collective-permute-done.26.second = bf16[128,1024]{1,0:T(8,128)(2,1)S(1)} collective-permute-done((bf16[128,1024]{1,0:T(8,128)(2,1)S(1)}, bf16[128,1024]{1,0:T(8,128)(2,1)S(1)}, u32[]{:S(2)}, u32[]{:S(2)}) %collective-permute-start.26) | collective-permute-done | bytes 262176 | tf_op jit(solution)/shard_map/ppermute | solution.py:202
  183.5 3.9 %collective-permute-done.27.third = bf16[128,1024]{1,0:T(8,128)(2,1)S(1)} collective-permute-done((bf16[128,1024]{1,0:T(8,128)(2,1)S(1)}, bf16[128,1024]{1,0:T(8,128)(2,1)S(1)}, u32[]{:S(2)}, u32[]{:S(2)}) %collective-permute-start.27) | collective-permute-done | bytes 262176 | tf_op jit(solution)/shard_map/ppermute | solution.py:202
  187.4 1.4 finish.1
  (54 shorter events, 0.4 us)
Async XLA Ops:
  0.0 10.0 %copy-start.6 = (bf16[32,2048]{1,0:T(8,128)(2,1)S(1)}, bf16[32,2048]{1,0:T(8,128)(2,1)}, u32[]{:S(2)}) copy-start(bf16[32,2048]{1,0:T(8,128)(2,1)} %param.13) | copy-start | bytes 393220
  0.0 8.8 %copy-start.4 = (bf16[128,2048]{1,0:T(8,128)(2,1)S(1)}, bf16[128,2048]{1,0:T(8,128)(2,1)}, u32[]{:S(2)}) copy-start(bf16[128,2048]{1,0:T(8,128)(2,1)} %param.12) | copy-start | bytes 1572868
  0.0 10.1 %copy-start.9 = (s32[8]{0:T(128)S(1)}, s32[8]{0:T(128)}, u32[]{:S(2)}) copy-start(s32[8]{0:T(128)} %param.22) | copy-start | bytes 100
  0.0 10.3 %copy-start = (bf16[256,512]{1,0:T(8,128)(2,1)S(1)}, bf16[256,512]{1,0:T(8,128)(2,1)}, u32[]{:S(2)}) copy-start(bf16[256,512]{1,0:T(8,128)(2,1)} %refs_0_.2) | copy-start | bytes 786436
  0.0 10.2 %copy-start.1 = (bf16[256,512]{1,0:T(8,128)(2,1)S(1)}, bf16[256,512]{1,0:T(8,128)(2,1)}, u32[]{:S(2)}) copy-start(bf16[256,512]{1,0:T(8,128)(2,1)} %refs_1_.1) | copy-start | bytes 786436
  0.0 10.2 %copy-start.2 = (bf16[64,512]{1,0:T(8,128)(2,1)S(1)}, bf16[64,512]{1,0:T(8,128)(2,1)}, u32[]{:S(2)}) copy-start(bf16[64,512]{1,0:T(8,128)(2,1)} %refs_2_.1) | copy-start | bytes 196612
  0.0 10.2 %copy-start.3 = (bf16[64,512]{1,0:T(8,128)(2,1)S(1)}, bf16[64,512]{1,0:T(8,128)(2,1)}, u32[]{:S(2)}) copy-start(bf16[64,512]{1,0:T(8,128)(2,1)} %refs_3_.1) | copy-start | bytes 196612
  0.0 39.4 %collective-permute-start.10 = (bf16[256,2048]{1,0:T(8,128)(2,1)}, bf16[256,2048]{1,0:T(8,128)(2,1)}, u32[]{:S(2)}, u32[]{:S(2)}) collective-permute-start(bf16[256,2048]{1,0:T(8,128)(2,1)} %refs_0_.3), channel_id=1, source_target_pairs={{0,4},{1,3},{2,6},{3,1},{4,0},{5,7},{6,2},{7,5},{8,12},{9,11},{10,... | collective-permute-start | bytes 3145736 | tf_op jit(solution)/shard_map/ppermute | solution.py:202
  1.6 37.8 %collective-permute-start.9 = (bf16[256,2048]{1,0:T(8,128)(2,1)}, bf16[256,2048]{1,0:T(8,128)(2,1)}, u32[]{:S(2)}, u32[]{:S(2)}) collective-permute-start(bf16[256,2048]{1,0:T(8,128)(2,1)} %refs_0_.3), channel_id=1, source_target_pairs={{0,2},{1,5},{2,0},{3,7},{4,6},{5,1},{6,4},{7,3},{8,10},{9,13},{10,... | collective-permute-start | bytes 3145736 | tf_op jit(solution)/shard_map/ppermute | solution.py:202
  10.3 6.4 %copy-start.5 = (bf16[2048,256]{1,0:T(8,128)(2,1)S(1)}, bf16[2048,256]{1,0:T(8,128)(2,1)}, u32[]{:S(2)}) copy-start(bf16[2048,256]{1,0:T(8,128)(2,1)} %param.18) | copy-start | bytes 3145732
  11.2 13.8 %collective-permute-start.2 = (bf16[336,512]{1,0:T(8,128)(2,1)S(1)}, bf16[336,512]{1,0:T(8,128)(2,1)S(1)}, u32[]{:S(2)}, u32[]{:S(2)}) collective-permute-start(bf16[336,512]{1,0:T(8,128)(2,1)S(1)} %get-tuple-element.46), channel_id=1, source_target_pairs={{0,8},{1,9},{2,10},{3,11},{4,12},{5,13},{6,14},{7,15},{8,0},{9,1},... | collective-permute-start | bytes 1032200 | tf_op jit(solution)/shard_map/ppermute | solution.py:202
  11.7 13.3 %collective-permute-start.1 = (bf16[32,2048]{1,0:T(8,128)(2,1)S(1)}, bf16[32,2048]{1,0:T(8,128)(2,1)S(1)}, u32[]{:S(2)}, u32[]{:S(2)}) collective-permute-start(bf16[32,2048]{1,0:T(8,128)(2,1)S(1)} %fusion.5), channel_id=1, source_target_pairs={{0,0},{1,16},{2,1},{3,17},{4,8},{5,24},{6,9},{7,25},{8,2},{9,18},{... | collective-permute-start | bytes 393224 | tf_op jit(solution)/shard_map/ppermute | solution.py:202
  15.2 15.5 %collective-permute-start = (bf16[144,2048]{1,0:T(8,128)(2,1)S(1)}, bf16[144,2048]{1,0:T(8,128)(2,1)}, u32[]{:S(2)}, u32[]{:S(2)}) collective-permute-start(bf16[144,2048]{1,0:T(8,128)(2,1)S(1)} %fusion.2), channel_id=1, source_target_pairs={{1,16},{3,18},{5,20},{7,22},{9,24},{11,26},{13,28},{15,30},{16,1},... | collective-permute-start | bytes 1769480 | tf_op jit(solution)/shard_map/ppermute | solution.py:202
  25.1 13.7 %collective-permute-start.7 = (bf16[2,256,512]{2,1,0:T(8,128)(2,1)S(1)}, bf16[2,256,512]{2,1,0:T(8,128)(2,1)S(1)}, u32[]{:S(2)}, u32[]{:S(2)}) collective-permute-start(bf16[2,256,512]{2,1,0:T(8,128)(2,1)S(1)} %pad_maximum_fusion.3.own), channel_id=1, source_target_pairs={{0,2},{1,5},{2,0},{3,7},{4,6},{5,1},{6,4},{7,3},{8,10},{9,13},{10,... | collective-permute-start | bytes 1572872 | tf_op jit(solution)/shard_map/ppermute | solution.py:202
  30.8 31.1 %collective-permute-start.3 = (bf16[176,2048]{1,0:T(8,128)(2,1)S(1)}, bf16[176,2048]{1,0:T(8,128)(2,1)S(1)}, u32[]{:S(2)}, u32[]{:S(2)}) collective-permute-start(bf16[176,2048]{1,0:T(8,128)(2,1)S(1)} %pad_maximum_fusion.2.x0), channel_id=1, source_target_pairs={{0,8},{1,9},{2,10},{3,11},{4,12},{5,13},{6,14},{7,15},{8,0},{9,1},... | collective-permute-start | bytes 2162696 | tf_op jit(solution)/shard_map/ppermute | solution.py:202
  30.9 31.0 %collective-permute-start.4 = (bf16[1024,256]{1,0:T(8,128)(2,1)S(1)}, bf16[1024,256]{1,0:T(8,128)(2,1)S(1)}, u32[]{:S(2)}, u32[]{:S(2)}) collective-permute-start(bf16[1024,256]{1,0:T(8,128)(2,1)S(1)} %get-tuple-element.50), channel_id=1, source_target_pairs={{0,16},{1,17},{2,18},{3,19},{4,20},{5,21},{6,22},{7,23},{8,24},{9,... | collective-permute-start | bytes 1572872 | tf_op jit(solution)/shard_map/ppermute | solution.py:202
  38.9 23.2 %collective-permute-start.8 = (bf16[4,256,512]{2,1,0:T(8,128)(2,1)S(1)}, bf16[4,256,512]{2,1,0:T(8,128)(2,1)S(1)}, u32[]{:S(2)}, u32[]{:S(2)}) collective-permute-start(bf16[4,256,512]{2,1,0:T(8,128)(2,1)S(1)} %pad_maximum_fusion), channel_id=1, source_target_pairs={{0,4},{1,3},{2,6},{3,1},{4,0},{5,7},{6,2},{7,5},{8,12},{9,11},{10,... | collective-permute-start | bytes 3145736 | tf_op jit(solution)/shard_map/ppermute | solution.py:202
  39.5 25.6 %collective-permute-start.11 = (bf16[256,2048]{1,0:T(8,128)(2,1)}, bf16[256,2048]{1,0:T(8,128)(2,1)S(1)}, u32[]{:S(2)}, u32[]{:S(2)}) collective-permute-start(bf16[256,2048]{1,0:T(8,128)(2,1)} %collective-permute-done.9.refs_1_), channel_id=1, source_target_pairs={{0,4},{1,3},{2,6},{3,1},{4,0},{5,7},{6,2},{7,5},{8,12},{9,11},{10,... | collective-permute-start | bytes 3145736 | tf_op jit(solution)/shard_map/ppermute | solution.py:202
  41.0 21.1 %collective-permute-start.6 = (bf16[176,2048]{1,0:T(8,128)(2,1)S(1)}, bf16[176,2048]{1,0:T(8,128)(2,1)S(1)}, u32[]{:S(2)}, u32[]{:S(2)}) collective-permute-start(bf16[176,2048]{1,0:T(8,128)(2,1)S(1)} %pad_maximum_fusion.2.x0), channel_id=1, source_target_pairs={{0,1},{1,0},{2,3},{3,2},{4,5},{5,4},{6,7},{7,6},{8,9},{9,8},{10,11... | collective-permute-start | bytes 2162696 | tf_op jit(solution)/shard_map/ppermute | solution.py:202
  61.9 2.2 %collective-permute-start.5 = (bf16[176,2048]{1,0:T(8,128)(2,1)S(1)}, bf16[176,2048]{1,0:T(8,128)(2,1)S(1)}, u32[]{:S(2)}, u32[]{:S(2)}) collective-permute-start(bf16[176,2048]{1,0:T(8,128)(2,1)S(1)} %collective-permute-done.3.x1), channel_id=1, source_target_pairs={{0,1},{1,0},{2,3},{3,2},{4,5},{5,4},{6,7},{7,6},{8,9},{9,8},{10,11... | collective-permute-start | bytes 2162696 | tf_op jit(solution)/shard_map/ppermute | solution.py:202
  65.0 2.1 %copy-start.7 = (bf16[256,2048]{1,0:T(8,128)(2,1)}, bf16[256,2048]{1,0:T(8,128)(2,1)S(1)}, u32[]{:S(2)}) copy-start(bf16[256,2048]{1,0:T(8,128)(2,1)S(1)} %collective-permute-done.11.refs_3_) | copy-start | bytes 3145732
  72.2 23.3 %collective-permute-start.18 = (bf16[4,128,512]{2,1,0:T(8,128)(2,1)S(1)}, bf16[4,128,512]{2,1,0:T(8,128)(2,1)S(1)}, u32[]{:S(2)}, u32[]{:S(2)}) collective-permute-start(bf16[4,128,512]{2,1,0:T(8,128)(2,1)S(1)} %get-tuple-element.69), channel_id=1, source_target_pairs={{0,8},{1,9},{2,10},{3,11},{4,12},{5,13},{6,14},{7,15},{8,0},{9,1},... | collective-permute-start | bytes 1572872 | tf_op jit(solution)/shard_map/ppermute | solution.py:202
  75.5 19.9 %collective-permute-start.12 = (bf16[736,256]{1,0:T(8,128)(2,1)S(1)}, bf16[736,256]{1,0:T(8,128)(2,1)S(1)}, u32[]{:S(2)}, u32[]{:S(2)}) collective-permute-start(bf16[736,256]{1,0:T(8,128)(2,1)S(1)} %get-tuple-element.67), channel_id=1, source_target_pairs={{0,16},{1,17},{2,18},{3,19},{4,20},{5,21},{6,22},{7,23},{8,24},{9,... | collective-permute-start | bytes 1130504 | tf_op jit(solution)/shard_map/ppermute | solution.py:202
  76.6 48.0 %collective-permute-start.16 = (bf16[2,1024,256]{2,1,0:T(8,128)(2,1)S(1)}, bf16[2,1024,256]{2,1,0:T(8,128)(2,1)S(1)}, u32[]{:S(2)}, u32[]{:S(2)}) collective-permute-start(bf16[2,1024,256]{2,1,0:T(8,128)(2,1)S(1)} %pad_maximum_fusion.1.refs_4_), channel_id=1, source_target_pairs={{0,2},{1,5},{2,0},{3,7},{4,6},{5,1},{6,4},{7,3},{8,10},{9,13},{10,... | collective-permute-start | bytes 3145736 | tf_op jit(solution)/shard_map/ppermute | solution.py:202
  77.7 36.1 %collective-permute-start.17 = (bf16[4,128,512]{2,1,0:T(8,128)(2,1)S(1)}, bf16[4,128,512]{2,1,0:T(8,128)(2,1)S(1)}, u32[]{:S(2)}, u32[]{:S(2)}) collective-permute-start(bf16[4,128,512]{2,1,0:T(8,128)(2,1)S(1)} %get-tuple-element.71), channel_id=1, source_target_pairs={{0,8},{1,9},{2,10},{3,11},{4,12},{5,13},{6,14},{7,15},{8,0},{9,1},... | collective-permute-start | bytes 1572872 | tf_op jit(solution)/shard_map/ppermute | solution.py:202
  95.6 31.1 %collective-permute-start.19 = (bf16[4,128,512]{2,1,0:T(8,128)(2,1)S(1)}, bf16[4,128,512]{2,1,0:T(8,128)(2,1)S(1)}, u32[]{:S(2)}, u32[]{:S(2)}) collective-permute-start(bf16[4,128,512]{2,1,0:T(8,128)(2,1)S(1)} %add_convert_fusion), channel_id=1, source_target_pairs={{0,16},{1,17},{2,18},{3,19},{4,20},{5,21},{6,22},{7,23},{8,24},{9,... | collective-permute-start | bytes 1572872 | tf_op jit(solution)/shard_map/ppermute | solution.py:202
  98.8 15.0 %collective-permute-start.13 = (bf16[6,128,256]{2,1,0:T(8,128)(2,1)S(1)}, bf16[6,128,256]{2,1,0:T(8,128)(2,1)S(1)}, u32[]{:S(2)}, u32[]{:S(2)}) collective-permute-start(bf16[6,128,256]{2,1,0:T(8,128)(2,1)S(1)} %keys_join.1.kv0), channel_id=1, source_target_pairs={{0,2},{1,5},{2,0},{3,7},{4,6},{5,1},{6,4},{7,3},{8,10},{9,13},{10,... | collective-permute-start | bytes 1179656 | tf_op jit(solution)/shard_map/ppermute | solution.py:202
  99.8 13.9 %collective-permute-start.14 = (bf16[6,128,256]{2,1,0:T(8,128)(2,1)S(1)}, bf16[6,128,256]{2,1,0:T(8,128)(2,1)S(1)}, u32[]{:S(2)}, u32[]{:S(2)}) collective-permute-start(bf16[6,128,256]{2,1,0:T(8,128)(2,1)S(1)} %keys_join.1.kv0), channel_id=1, source_target_pairs={{0,4},{1,3},{2,6},{3,1},{4,0},{5,7},{6,2},{7,5},{8,12},{9,11},{10,... | collective-permute-start | bytes 1179656 | tf_op jit(solution)/shard_map/ppermute | solution.py:202
  113.7 10.9 %collective-permute-start.15 = (bf16[6,128,256]{2,1,0:T(8,128)(2,1)S(1)}, bf16[6,128,256]{2,1,0:T(8,128)(2,1)S(1)}, u32[]{:S(2)}, u32[]{:S(2)}) collective-permute-start(bf16[6,128,256]{2,1,0:T(8,128)(2,1)S(1)} %keys_join.1.kv0), channel_id=1, source_target_pairs={{0,6},{1,7},{2,4},{3,5},{4,2},{5,3},{6,0},{7,1},{8,14},{9,15},{10,... | collective-permute-start | bytes 1179656 | tf_op jit(solution)/shard_map/ppermute | solution.py:202
  124.7 20.5 %collective-permute-start.22 = (bf16[2,1024,256]{2,1,0:T(8,128)(2,1)S(1)}, bf16[2,1024,256]{2,1,0:T(8,128)(2,1)S(1)}, u32[]{:S(2)}, u32[]{:S(2)}) collective-permute-start(bf16[2,1024,256]{2,1,0:T(8,128)(2,1)S(1)} %pad_maximum_fusion.1.refs_4_), channel_id=1, source_target_pairs={{0,4},{1,3},{2,6},{3,1},{4,0},{5,7},{6,2},{7,5},{8,12},{9,11},{10,... | collective-permute-start | bytes 3145736 | tf_op jit(solution)/shard_map/ppermute | solution.py:202
  125.1 25.6 %collective-permute-start.23 = (bf16[2,1024,256]{2,1,0:T(8,128)(2,1)S(1)}, bf16[2,1024,256]{2,1,0:T(8,128)(2,1)S(1)}, u32[]{:S(2)}, u32[]{:S(2)}) collective-permute-start(bf16[2,1024,256]{2,1,0:T(8,128)(2,1)S(1)} %collective-permute-done.16.refs_5_), channel_id=1, source_target_pairs={{0,4},{1,3},{2,6},{3,1},{4,0},{5,7},{6,2},{7,5},{8,12},{9,11},{10,... | collective-permute-start | bytes 3145736 | tf_op jit(solution)/shard_map/ppermute | solution.py:202
  131.4 7.7 %collective-permute-start.21 = (bf16[512,256]{1,0:T(8,128)(2,1)S(1)}, bf16[512,256]{1,0:T(8,128)(2,1)S(1)}, u32[]{:S(2)}, u32[]{:S(2)}) collective-permute-start(bf16[512,256]{1,0:T(8,128)(2,1)S(1)} %attend.3.refs_1_), channel_id=1, source_target_pairs={{0,8},{1,9},{2,10},{3,11},{4,12},{5,13},{6,14},{7,15},{8,0},{9,1},... | collective-permute-start | bytes 786440 | tf_op jit(solution)/shard_map/ppermute | solution.py:202
  138.7 6.4 %collective-permute-start.20 = (bf16[512,256]{1,0:T(8,128)(2,1)S(1)}, bf16[512,256]{1,0:T(8,128)(2,1)S(1)}, u32[]{:S(2)}, u32[]{:S(2)}) collective-permute-start(bf16[512,256]{1,0:T(8,128)(2,1)S(1)} %attend.2.refs_0_), channel_id=1, source_target_pairs={{0,8},{1,9},{2,10},{3,11},{4,12},{5,13},{6,14},{7,15},{8,0},{9,1},... | collective-permute-start | bytes 786440 | tf_op jit(solution)/shard_map/ppermute | solution.py:202
  150.7 1.0 copy-start.8
  155.6 2.7 %collective-permute-start.24 = (bf16[4,128,1024]{2,1,0:T(8,128)(2,1)S(1)}, bf16[4,128,1024]{2,1,0:T(8,128)(2,1)S(1)}, u32[]{:S(2)}, u32[]{:S(2)}) collective-permute-start(bf16[4,128,1024]{2,1,0:T(8,128)(2,1)S(1)} %get-tuple-element.80), channel_id=1, source_target_pairs={{0,1},{1,0},{2,3},{3,2},{4,5},{5,4},{6,7},{7,6},{8,9},{9,8},{10,11... | collective-permute-start | bytes 3145736 | tf_op jit(solution)/shard_map/ppermute | solution.py:202
  160.1 9.6 %collective-permute-start.25 = (bf16[128,1024]{1,0:T(8,128)(2,1)S(1)}, bf16[128,1024]{1,0:T(8,128)(2,1)S(1)}, u32[]{:S(2)}, u32[]{:S(2)}) collective-permute-start(bf16[128,1024]{1,0:T(8,128)(2,1)S(1)} %get-tuple-element.85), channel_id=1, source_target_pairs={{0,8},{1,9},{2,10},{3,11},{4,12},{5,13},{6,14},{7,15},{8,16},{9,17... | collective-permute-start | bytes 786440 | tf_op jit(solution)/shard_map/ppermute | solution.py:202
  160.8 22.7 %collective-permute-start.26 = (bf16[128,1024]{1,0:T(8,128)(2,1)S(1)}, bf16[128,1024]{1,0:T(8,128)(2,1)S(1)}, u32[]{:S(2)}, u32[]{:S(2)}) collective-permute-start(bf16[128,1024]{1,0:T(8,128)(2,1)S(1)} %get-tuple-element.84), channel_id=1, source_target_pairs={{0,16},{1,17},{2,18},{3,19},{4,20},{5,21},{6,22},{7,23},{8,24},{9,... | collective-permute-start | bytes 786440 | tf_op jit(solution)/shard_map/ppermute | solution.py:202
  165.0 22.4 %collective-permute-start.27 = (bf16[128,1024]{1,0:T(8,128)(2,1)S(1)}, bf16[128,1024]{1,0:T(8,128)(2,1)S(1)}, u32[]{:S(2)}, u32[]{:S(2)}) collective-permute-start(bf16[128,1024]{1,0:T(8,128)(2,1)S(1)} %get-tuple-element.83), channel_id=1, source_target_pairs={{0,24},{1,25},{2,26},{3,27},{4,28},{5,29},{6,30},{7,31},{8,0},{9,1... | collective-permute-start | bytes 786440 | tf_op jit(solution)/shard_map/ppermute | solution.py:202

commit v14 on v13

--- a/solution.py
+++ b/solution.py
@@ -626,8 +626,8 @@
     kv_near, kv_far = to_near(kv), to_far(kv)
     kv_both = permuted(kv, lambda z, p, c: (z, p ^ 3, c))
 
-    kv_near, kv_far, kv_both, out_near, out_pair, got_near = lax.optimization_barrier(
-        (kv_near, kv_far, kv_both, out_near, out_pair, got_near)
+    kv_near, kv_far, kv_both, out_near, out_pair = lax.optimization_barrier(
+        (kv_near, kv_far, kv_both, out_near, out_pair)
     )
     out_far, out_both = to_far(out_pair), to_far(out_near)
 

time: 189 us -> 179 us (0.947)
  waiting for transfers between devices: 109 us -> 93 us
  starting transfers between devices: 43 us -> 49.1 us
    ppermute x28, waiting for transfers between devices: 109 us -> 93 us  [permuted(): return lax.ppermute(value, ('seq', 'head'), perm)]
    ppermute x28, starting transfers between devices: 43 us -> 49.1 us  [permuted(): return lax.ppermute(value, ('seq', 'head'), perm)]
  transfers between devices with their start and end apart: 28 -> 28, of which waited for: 14 -> 14; matrix products, arithmetic and copies ran while one was open for 4% -> 4% of each run, Pallas kernels for 6% -> 9%
where the time goes in v14:
time: 179 us
  waiting for transfers between devices  93 us (52%)
  starting transfers between devices  49.1 us (27%)
  Pallas kernels  23.8 us (13%)
  other arithmetic  8.06 us (5%)
  blocking collectives  2.46 us (1%)
  local copies, waits for them, and re-layouts  2.09 us (1%)
    ppermute x28, waiting for transfers between devices, permuted(): return lax.ppermute(value, ('seq', 'head'), perm)  93 us
    ppermute x28, starting transfers between devices, permuted(): return lax.ppermute(value, ('seq', 'head'), perm)  49.1 us
    pallas_call x2, Pallas kernels, by_levels(): pl.pallas_call(functools.partial(attend_kernel, pair), out_shape=shaped((...  9.47 us
    pallas_call x1, Pallas kernels, by_levels(): pl.pallas_call(queries_part_kernel, out_shape=(shaped(group_shape, jnp.fl...  4.99 us
    pallas_call x1, Pallas kernels, by_levels(): pl.pallas_call(output_kernel, out_shape=(shaped((LEVELS, tok, wide_cols),...  3.89 us
  transfers between devices with their start and end apart: 28, of which 14 were waited for; matrix products, arithmetic and copies ran while one was open for 4% of the time, Pallas kernels for 9%

profile of v14, /device:TPU:8, one launch (start us, length us, event | category | flops | bytes accessed | tf_op | source)
XLA Modules:
  0.0 178.9 jit_solution(7385798779253009251)
XLA Ops:
  0.0 1.6 collective-permute-start.10
  1.6 1.5 collective-permute-start.9
  3.1 1.0 fusion.3
  4.2 0.1 pad.22.clone
  4.2 1.4 fusion
  5.6 2.5 %all-reduce.1 = (f32[144]{0:T(256)S(1)}, f32[32]{0:T(128)S(1)}) all-reduce(f32[144]{0:T(256)S(1)} %fusion, f32[32]{0:T(128)S(1)} %fusion.3), channel_id=1, replica_groups=mesh['seq'=16,'head'=2] {'head'}, use_global_device_ids=true, to_apply=%region_1.2 | all-reduce | flops 176 | bytes 1408 | tf_op jit(solution)/shard_map/psum | solution.py:518
  8.1 0.7 dynamic_slice.9
  8.8 1.1 fusion.2
  10.0 0.1 fusion.5
  10.1 0.1 broadcast_in_dim.5.refs_4_
  10.2 0.1 stack.41.where_ref
  10.3 0.9 pack.1
  11.2 0.5 collective-permute-start.2
  11.7 3.4 %collective-permute-start.1 = (bf16[32,2048]{1,0:T(8,128)(2,1)S(1)}, bf16[32,2048]{1,0:T(8,128)(2,1)S(1)}, u32[]{:S(2)}, u32[]{:S(2)}) collective-permute-start(bf16[32,2048]{1,0:T(8,128)(2,1)S(1)} %fusion.5), channel_id=1, source_target_pairs={{0,0},{1,16},{2,1},{3,17},{4,8},{5,24},{6,9},{7,25},{8,2},{9,18},{... | collective-permute-start | bytes 393224 | tf_op jit(solution)/shard_map/ppermute | solution.py:202
  15.2 1.5 collective-permute-start
  16.7 0.1 dynamic-slice_bitcast_fusion
  16.8 8.2 %collective-permute-done.1 = bf16[32,2048]{1,0:T(8,128)(2,1)S(1)} collective-permute-done((bf16[32,2048]{1,0:T(8,128)(2,1)S(1)}, bf16[32,2048]{1,0:T(8,128)(2,1)S(1)}, u32[]{:S(2)}, u32[]{:S(2)}) %collective-permute-start.1) | collective-permute-done | bytes 131104 | tf_op jit(solution)/shard_map/ppermute | solution.py:202
  25.1 5.5 %collective-permute-start.7 = (bf16[2,256,512]{2,1,0:T(8,128)(2,1)S(1)}, bf16[2,256,512]{2,1,0:T(8,128)(2,1)S(1)}, u32[]{:S(2)}, u32[]{:S(2)}) collective-permute-start(bf16[2,256,512]{2,1,0:T(8,128)(2,1)S(1)} %pad_maximum_fusion.3.own), channel_id=1, source_target_pairs={{0,2},{1,5},{2,0},{3,7},{4,6},{5,1},{6,4},{7,3},{8,10},{9,13},{10,... | collective-permute-start | bytes 1572872 | tf_op jit(solution)/shard_map/ppermute | solution.py:202
  30.9 8.0 %collective-permute-start.4 = (bf16[1024,256]{1,0:T(8,128)(2,1)S(1)}, bf16[1024,256]{1,0:T(8,128)(2,1)S(1)}, u32[]{:S(2)}, u32[]{:S(2)}) collective-permute-start(bf16[1024,256]{1,0:T(8,128)(2,1)S(1)} %get-tuple-element.49), channel_id=1, source_target_pairs={{0,16},{1,17},{2,18},{3,19},{4,20},{5,21},{6,22},{7,23},{8,24},{9,... | collective-permute-start | bytes 1572872 | tf_op jit(solution)/shard_map/ppermute | solution.py:202
  38.8 0.1 add_convert_fusion.4
  38.9 0.1 pad_maximum_fusion
  39.0 0.5 collective-permute-start.8
  39.6 1.6 collective-permute-start.11
  41.2 20.7 %collective-permute-done.4 = bf16[1024,256]{1,0:T(8,128)(2,1)S(1)} collective-permute-done((bf16[1024,256]{1,0:T(8,128)(2,1)S(1)}, bf16[1024,256]{1,0:T(8,128)(2,1)S(1)}, u32[]{:S(2)}, u32[]{:S(2)}) %collective-permute-start.4) | collective-permute-done | bytes 524320 | tf_op jit(solution)/shard_map/ppermute | solution.py:202
  61.9 1.5 fusion.9
  63.4 0.2 pad_maximum_fusion.4.cos_ref
  63.6 0.2 pad_maximum_fusion.5.sin_ref
  63.8 0.1 pad_maximum_fusion.1.refs_4_
  63.9 0.2 collective-permute-done.5.x3
  64.1 1.0 collective-permute-done.11.refs_3_
  65.1 2.1 %keys_part.1 = (f32[576,256]{1,0:T(8,128)S(1)}, bf16[736,256]{1,0:T(8,128)(2,1)S(1)}) custom-call(s32[5]{0:T(128)S(1)} %stack.41.where_ref, bf16[176,2048]{1,0:T(8,128)(2,1)S(1)} %pad_maximum_fusion.2.x0, bf16[176,2048]{1,0:T(8,128)(2,1)S(1)} %collective-permute-done.3.x1, bf16[176,2048]{1,0:T(8,128)(2,1)S(1)} %collective-permute-done.6.x2, ...), custom_call_target="tpu_custom_call" | custom-call | flops 3000000000 | bytes 4000000 | tf_op jit(solution)/shard_map/keys_part/pallas_call | solution.py:578
  67.2 2.4 %collective-permute-start.15 = (bf16[736,256]{1,0:T(8,128)(2,1)S(1)}, bf16[736,256]{1,0:T(8,128)(2,1)S(1)}, u32[]{:S(2)}, u32[]{:S(2)}) collective-permute-start(bf16[736,256]{1,0:T(8,128)(2,1)S(1)} %get-tuple-element.69), channel_id=1, source_target_pairs={{0,16},{1,17},{2,18},{3,19},{4,20},{5,21},{6,22},{7,23},{8,24},{9,... | collective-permute-start | bytes 1130504 | tf_op jit(solution)/shard_map/ppermute | solution.py:202
  69.7 5.0 %queries_part.1 = (f32[4,128,512]{2,1,0:T(8,128)S(1)}, f32[4,128,512]{2,1,0:T(8,128)S(1)}, bf16[4,128,512]{2,1,0:T(8,128)(2,1)S(1)}, bf16[4,128,512]{2,1,0:T(8,128)(2,1)S(1)}) custom-call(s32[5]{0:T(128)S(1)} %stack.41.where_ref, bf16[176,2048]{1,0:T(8,128)(2,1)S(1)} %pad_maximum_fusion.2.x0, bf16[176,2048]{1,0:T(8,128)(2,1)S(1)} %collective-permute-done.3.x1, ...), custom_call_target="tpu_custom_call" | custom-call | flops 5000000000 | bytes 4000000 | tf_op jit(solution)/shard_map/queries_part/pallas_call | solution.py:595
  74.7 1.0 collective-permute-start.19
  75.8 9.6 %collective-permute-done.15.got_ref = bf16[736,256]{1,0:T(8,128)(2,1)S(1)} collective-permute-done((bf16[736,256]{1,0:T(8,128)(2,1)S(1)}, bf16[736,256]{1,0:T(8,128)(2,1)S(1)}, u32[]{:S(2)}, u32[]{:S(2)}) %collective-permute-start.15) | collective-permute-done | bytes 376864 | tf_op jit(solution)/shard_map/ppermute | solution.py:202
  85.3 1.0 keys_join.1.kv0
  86.4 0.9 collective-permute-start.16
  87.3 3.4 %collective-permute-start.12 = (bf16[4,128,512]{2,1,0:T(8,128)(2,1)S(1)}, bf16[4,128,512]{2,1,0:T(8,128)(2,1)S(1)}, u32[]{:S(2)}, u32[]{:S(2)}) collective-permute-start(bf16[4,128,512]{2,1,0:T(8,128)(2,1)S(1)} %get-tuple-element.65), channel_id=1, source_target_pairs={{0,8},{1,9},{2,10},{3,11},{4,12},{5,13},{6,14},{7,15},{8,0},{9,1},... | collective-permute-start | bytes 1572872 | tf_op jit(solution)/shard_map/ppermute | solution.py:202
  90.6 4.4 %collective-permute-done.13 = bf16[4,128,512]{2,1,0:T(8,128)(2,1)S(1)} collective-permute-done((bf16[4,128,512]{2,1,0:T(8,128)(2,1)S(1)}, bf16[4,128,512]{2,1,0:T(8,128)(2,1)S(1)}, u32[]{:S(2)}, u32[]{:S(2)}) %collective-permute-start.13) | collective-permute-done | bytes 524320 | tf_op jit(solution)/shard_map/ppermute | solution.py:202
  95.0 0.2 add_convert_fusion
  95.1 3.2 %collective-permute-start.14 = (bf16[4,128,512]{2,1,0:T(8,128)(2,1)S(1)}, bf16[4,128,512]{2,1,0:T(8,128)(2,1)S(1)}, u32[]{:S(2)}, u32[]{:S(2)}) collective-permute-start(bf16[4,128,512]{2,1,0:T(8,128)(2,1)S(1)} %add_convert_fusion), channel_id=1, source_target_pairs={{0,16},{1,17},{2,18},{3,19},{4,20},{5,21},{6,22},{7,23},{8,24},{9,... | collective-permute-start | bytes 1572872 | tf_op jit(solution)/shard_map/ppermute | solution.py:202
  98.3 0.5 collective-permute-start.17
  98.8 1.9 %collective-permute-start.18 = (bf16[6,128,256]{2,1,0:T(8,128)(2,1)S(1)}, bf16[6,128,256]{2,1,0:T(8,128)(2,1)S(1)}, u32[]{:S(2)}, u32[]{:S(2)}) collective-permute-start(bf16[6,128,256]{2,1,0:T(8,128)(2,1)S(1)} %keys_join.1.kv0), channel_id=1, source_target_pairs={{0,6},{1,7},{2,4},{3,5},{4,2},{5,3},{6,0},{7,1},{8,14},{9,15},{10,... | collective-permute-start | bytes 1179656 | tf_op jit(solution)/shard_map/ppermute | solution.py:202
  100.7 13.8 %collective-permute-done.17.kv2 = bf16[6,128,256]{2,1,0:T(8,128)(2,1)S(1)} collective-permute-done((bf16[6,128,256]{2,1,0:T(8,128)(2,1)S(1)}, bf16[6,128,256]{2,1,0:T(8,128)(2,1)S(1)}, u32[]{:S(2)}, u32[]{:S(2)}) %collective-permute-start.17) | collective-permute-done | bytes 393248 | tf_op jit(solution)/shard_map/ppermute | solution.py:202
  114.5 0.5 collective-permute-start.22
  115.0 1.6 collective-permute-start.23
  116.6 2.0 %collective-permute-done.14.got_ref = bf16[4,128,512]{2,1,0:T(8,128)(2,1)S(1)} collective-permute-done((bf16[4,128,512]{2,1,0:T(8,128)(2,1)S(1)}, bf16[4,128,512]{2,1,0:T(8,128)(2,1)S(1)}, u32[]{:S(2)}, u32[]{:S(2)}) %collective-permute-start.14) | collective-permute-done | bytes 524320 | tf_op jit(solution)/shard_map/ppermute | solution.py:202
  118.6 4.7 %attend.3.refs_1_ = bf16[512,256]{1,0:T(8,128)(2,1)S(1)} custom-call(s32[5]{0:T(128)S(1)} %stack.41.where_ref, f32[4,128,512]{2,1,0:T(8,128)S(1)} %get-tuple-element.64.keep_ref, bf16[4,128,512]{2,1,0:T(8,128)(2,1)S(1)} %collective-permute-done.12.near_ref, bf16[4,128,512]{2,1,0:T(8,128)(2,1)S(1)} %collective-permute-done.14.got_ref, ...), custom_call_target="tpu_custom_call" | custom-call | flops 4000000000 | bytes 4000000 | tf_op jit(solution)/shard_map/attend/pallas_call | solution.py:635
  123.3 4.0 %collective-permute-start.21 = (bf16[512,256]{1,0:T(8,128)(2,1)S(1)}, bf16[512,256]{1,0:T(8,128)(2,1)S(1)}, u32[]{:S(2)}, u32[]{:S(2)}) collective-permute-start(bf16[512,256]{1,0:T(8,128)(2,1)S(1)} %attend.3.refs_1_), channel_id=1, source_target_pairs={{0,8},{1,9},{2,10},{3,11},{4,12},{5,13},{6,14},{7,15},{8,0},{9,1},... | collective-permute-start | bytes 786440 | tf_op jit(solution)/shard_map/ppermute | solution.py:202
  127.3 4.8 %attend.2.refs_0_ = bf16[512,256]{1,0:T(8,128)(2,1)S(1)} custom-call(s32[5]{0:T(128)S(1)} %stack.41.where_ref, f32[4,128,512]{2,1,0:T(8,128)S(1)} %get-tuple-element.64.keep_ref, bf16[4,128,512]{2,1,0:T(8,128)(2,1)S(1)} %collective-permute-done.12.near_ref, bf16[4,128,512]{2,1,0:T(8,128)(2,1)S(1)} %collective-permute-done.14.got_ref, ...), custom_call_target="tpu_custom_call" | custom-call | flops 4000000000 | bytes 4000000 | tf_op jit(solution)/shard_map/attend/pallas_call | solution.py:635
  132.1 0.1 collective-permute-start.20
  132.2 6.3 %collective-permute-done.20.refs_2_ = bf16[512,256]{1,0:T(8,128)(2,1)S(1)} collective-permute-done((bf16[512,256]{1,0:T(8,128)(2,1)S(1)}, bf16[512,256]{1,0:T(8,128)(2,1)S(1)}, u32[]{:S(2)}, u32[]{:S(2)}) %collective-permute-start.20) | collective-permute-done | bytes 262176 | tf_op jit(solution)/shard_map/ppermute | solution.py:202
  138.6 2.0 %collective-permute-done.23.refs_7_ = bf16[2,1024,256]{2,1,0:T(8,128)(2,1)S(1)} collective-permute-done((bf16[2,1024,256]{2,1,0:T(8,128)(2,1)S(1)}, bf16[2,1024,256]{2,1,0:T(8,128)(2,1)S(1)}, u32[]{:S(2)}, u32[]{:S(2)}) %collective-permute-start.23) | collective-permute-done | bytes 1048608 | tf_op jit(solution)/shard_map/ppermute | solution.py:202
  140.6 1.0 copy-done.8
  141.6 3.9 %output.1 = (f32[4,128,1024]{2,1,0:T(8,128)}, bf16[4,128,1024]{2,1,0:T(8,128)(2,1)S(1)}) custom-call(s32[5]{0:T(128)S(1)} %stack.41.where_ref, bf16[512,256]{1,0:T(8,128)(2,1)S(1)} %attend.2.refs_0_, bf16[512,256]{1,0:T(8,128)(2,1)S(1)} %attend.3.refs_1_, bf16[512,256]{1,0:T(8,128)(2,1)S(1)} %collective-permute-done.20.refs_2_, ...), custom_call_target="tpu_custom_call" | custom-call | flops 5000000000 | bytes 4000000 | tf_op jit(solution)/shard_map/output/pallas_call | solution.py:652
  145.5 2.7 %collective-permute-done.24 = bf16[4,128,1024]{2,1,0:T(8,128)(2,1)S(1)} collective-permute-done((bf16[4,128,1024]{2,1,0:T(8,128)(2,1)S(1)}, bf16[4,128,1024]{2,1,0:T(8,128)(2,1)S(1)}, u32[]{:S(2)}, u32[]{:S(2)}) %collective-permute-start.24) | collective-permute-done | bytes 1048608 | tf_op jit(solution)/shard_map/ppermute | solution.py:202
  148.1 1.9 %fusion.8 = (bf16[128,1024]{1,0:T(8,128)(2,1)S(1)}, bf16[128,1024]{1,0:T(8,128)(2,1)S(1)}, bf16[128,1024]{1,0:T(8,128)(2,1)S(1)}, f32[128,1024]{1,0:T(8,128)S(1)}) fusion(f32[4,128,1024]{2,1,0:T(8,128)} %get-tuple-element.77, bf16[4,128,1024]{2,1,0:T(8,128)(2,1)S(1)} %collective-permute-done.24), kind=kLoop, calls=%fused_computation.28 | loop fusion | flops 1441792 | bytes 4456448 | tf_op jit(solution)/shard_map/convert_element_type | solution.py:669
  150.0 3.8 %collective-permute-start.25 = (bf16[128,1024]{1,0:T(8,128)(2,1)S(1)}, bf16[128,1024]{1,0:T(8,128)(2,1)S(1)}, u32[]{:S(2)}, u32[]{:S(2)}) collective-permute-start(bf16[128,1024]{1,0:T(8,128)(2,1)S(1)} %get-tuple-element.83), channel_id=1, source_target_pairs={{0,8},{1,9},{2,10},{3,11},{4,12},{5,13},{6,14},{7,15},{8,16},{9,17... | collective-permute-start | bytes 786440 | tf_op jit(solution)/shard_map/ppermute | solution.py:202
  153.8 1.0 collective-permute-start.26
  154.8 0.6 collective-permute-start.27
  155.4 16.4 %collective-permute-done.25.first = bf16[128,1024]{1,0:T(8,128)(2,1)S(1)} collective-permute-done((bf16[128,1024]{1,0:T(8,128)(2,1)S(1)}, bf16[128,1024]{1,0:T(8,128)(2,1)S(1)}, u32[]{:S(2)}, u32[]{:S(2)}) %collective-permute-start.25) | collective-permute-done | bytes 262176 | tf_op jit(solution)/shard_map/ppermute | solution.py:202
  171.7 4.8 %collective-permute-done.26.second = bf16[128,1024]{1,0:T(8,128)(2,1)S(1)} collective-permute-done((bf16[128,1024]{1,0:T(8,128)(2,1)S(1)}, bf16[128,1024]{1,0:T(8,128)(2,1)S(1)}, u32[]{:S(2)}, u32[]{:S(2)}) %collective-permute-start.26) | collective-permute-done | bytes 262176 | tf_op jit(solution)/shard_map/ppermute | solution.py:202
  176.6 0.9 collective-permute-done.27.third
  177.4 1.4 finish.1
  (54 shorter events, 0.6 us)
Async XLA Ops:
  0.0 10.0 %copy-start.6 = (bf16[32,2048]{1,0:T(8,128)(2,1)S(1)}, bf16[32,2048]{1,0:T(8,128)(2,1)}, u32[]{:S(2)}) copy-start(bf16[32,2048]{1,0:T(8,128)(2,1)} %param.13) | copy-start | bytes 393220
  0.0 8.8 %copy-start.4 = (bf16[128,2048]{1,0:T(8,128)(2,1)S(1)}, bf16[128,2048]{1,0:T(8,128)(2,1)}, u32[]{:S(2)}) copy-start(bf16[128,2048]{1,0:T(8,128)(2,1)} %param.12) | copy-start | bytes 1572868
  0.0 10.1 %copy-start.9 = (s32[8]{0:T(128)S(1)}, s32[8]{0:T(128)}, u32[]{:S(2)}) copy-start(s32[8]{0:T(128)} %param.22) | copy-start | bytes 100
  0.0 10.3 %copy-start = (bf16[256,512]{1,0:T(8,128)(2,1)S(1)}, bf16[256,512]{1,0:T(8,128)(2,1)}, u32[]{:S(2)}) copy-start(bf16[256,512]{1,0:T(8,128)(2,1)} %refs_0_.2) | copy-start | bytes 786436
  0.0 10.2 %copy-start.1 = (bf16[256,512]{1,0:T(8,128)(2,1)S(1)}, bf16[256,512]{1,0:T(8,128)(2,1)}, u32[]{:S(2)}) copy-start(bf16[256,512]{1,0:T(8,128)(2,1)} %refs_1_.1) | copy-start | bytes 786436
  0.0 10.2 %copy-start.2 = (bf16[64,512]{1,0:T(8,128)(2,1)S(1)}, bf16[64,512]{1,0:T(8,128)(2,1)}, u32[]{:S(2)}) copy-start(bf16[64,512]{1,0:T(8,128)(2,1)} %refs_2_.1) | copy-start | bytes 196612
  0.0 10.2 %copy-start.3 = (bf16[64,512]{1,0:T(8,128)(2,1)S(1)}, bf16[64,512]{1,0:T(8,128)(2,1)}, u32[]{:S(2)}) copy-start(bf16[64,512]{1,0:T(8,128)(2,1)} %refs_3_.1) | copy-start | bytes 196612
  0.0 39.5 %collective-permute-start.10 = (bf16[256,2048]{1,0:T(8,128)(2,1)}, bf16[256,2048]{1,0:T(8,128)(2,1)}, u32[]{:S(2)}, u32[]{:S(2)}) collective-permute-start(bf16[256,2048]{1,0:T(8,128)(2,1)} %refs_0_.3), channel_id=1, source_target_pairs={{0,4},{1,3},{2,6},{3,1},{4,0},{5,7},{6,2},{7,5},{8,12},{9,11},{10,... | collective-permute-start | bytes 3145736 | tf_op jit(solution)/shard_map/ppermute | solution.py:202
  1.6 37.9 %collective-permute-start.9 = (bf16[256,2048]{1,0:T(8,128)(2,1)}, bf16[256,2048]{1,0:T(8,128)(2,1)}, u32[]{:S(2)}, u32[]{:S(2)}) collective-permute-start(bf16[256,2048]{1,0:T(8,128)(2,1)} %refs_0_.3), channel_id=1, source_target_pairs={{0,2},{1,5},{2,0},{3,7},{4,6},{5,1},{6,4},{7,3},{8,10},{9,13},{10,... | collective-permute-start | bytes 3145736 | tf_op jit(solution)/shard_map/ppermute | solution.py:202
  10.3 6.4 %copy-start.5 = (bf16[2048,256]{1,0:T(8,128)(2,1)S(1)}, bf16[2048,256]{1,0:T(8,128)(2,1)}, u32[]{:S(2)}) copy-start(bf16[2048,256]{1,0:T(8,128)(2,1)} %param.18) | copy-start | bytes 3145732
  11.2 13.8 %collective-permute-start.2 = (bf16[336,512]{1,0:T(8,128)(2,1)S(1)}, bf16[336,512]{1,0:T(8,128)(2,1)S(1)}, u32[]{:S(2)}, u32[]{:S(2)}) collective-permute-start(bf16[336,512]{1,0:T(8,128)(2,1)S(1)} %get-tuple-element.45), channel_id=1, source_target_pairs={{0,8},{1,9},{2,10},{3,11},{4,12},{5,13},{6,14},{7,15},{8,0},{9,1},... | collective-permute-start | bytes 1032200 | tf_op jit(solution)/shard_map/ppermute | solution.py:202
  11.7 13.3 %collective-permute-start.1 = (bf16[32,2048]{1,0:T(8,128)(2,1)S(1)}, bf16[32,2048]{1,0:T(8,128)(2,1)S(1)}, u32[]{:S(2)}, u32[]{:S(2)}) collective-permute-start(bf16[32,2048]{1,0:T(8,128)(2,1)S(1)} %fusion.5), channel_id=1, source_target_pairs={{0,0},{1,16},{2,1},{3,17},{4,8},{5,24},{6,9},{7,25},{8,2},{9,18},{... | collective-permute-start | bytes 393224 | tf_op jit(solution)/shard_map/ppermute | solution.py:202
  15.2 15.5 %collective-permute-start = (bf16[144,2048]{1,0:T(8,128)(2,1)S(1)}, bf16[144,2048]{1,0:T(8,128)(2,1)}, u32[]{:S(2)}, u32[]{:S(2)}) collective-permute-start(bf16[144,2048]{1,0:T(8,128)(2,1)S(1)} %fusion.2), channel_id=1, source_target_pairs={{1,16},{3,18},{5,20},{7,22},{9,24},{11,26},{13,28},{15,30},{16,1},... | collective-permute-start | bytes 1769480 | tf_op jit(solution)/shard_map/ppermute | solution.py:202
  25.1 13.8 %collective-permute-start.7 = (bf16[2,256,512]{2,1,0:T(8,128)(2,1)S(1)}, bf16[2,256,512]{2,1,0:T(8,128)(2,1)S(1)}, u32[]{:S(2)}, u32[]{:S(2)}) collective-permute-start(bf16[2,256,512]{2,1,0:T(8,128)(2,1)S(1)} %pad_maximum_fusion.3.own), channel_id=1, source_target_pairs={{0,2},{1,5},{2,0},{3,7},{4,6},{5,1},{6,4},{7,3},{8,10},{9,13},{10,... | collective-permute-start | bytes 1572872 | tf_op jit(solution)/shard_map/ppermute | solution.py:202
  30.8 31.1 %collective-permute-start.3 = (bf16[176,2048]{1,0:T(8,128)(2,1)S(1)}, bf16[176,2048]{1,0:T(8,128)(2,1)S(1)}, u32[]{:S(2)}, u32[]{:S(2)}) collective-permute-start(bf16[176,2048]{1,0:T(8,128)(2,1)S(1)} %pad_maximum_fusion.2.x0), channel_id=1, source_target_pairs={{0,8},{1,9},{2,10},{3,11},{4,12},{5,13},{6,14},{7,15},{8,0},{9,1},... | collective-permute-start | bytes 2162696 | tf_op jit(solution)/shard_map/ppermute | solution.py:202
  30.9 31.0 %collective-permute-start.4 = (bf16[1024,256]{1,0:T(8,128)(2,1)S(1)}, bf16[1024,256]{1,0:T(8,128)(2,1)S(1)}, u32[]{:S(2)}, u32[]{:S(2)}) collective-permute-start(bf16[1024,256]{1,0:T(8,128)(2,1)S(1)} %get-tuple-element.49), channel_id=1, source_target_pairs={{0,16},{1,17},{2,18},{3,19},{4,20},{5,21},{6,22},{7,23},{8,24},{9,... | collective-permute-start | bytes 1572872 | tf_op jit(solution)/shard_map/ppermute | solution.py:202
  39.0 24.8 %collective-permute-start.8 = (bf16[4,256,512]{2,1,0:T(8,128)(2,1)S(1)}, bf16[4,256,512]{2,1,0:T(8,128)(2,1)S(1)}, u32[]{:S(2)}, u32[]{:S(2)}) collective-permute-start(bf16[4,256,512]{2,1,0:T(8,128)(2,1)S(1)} %pad_maximum_fusion), channel_id=1, source_target_pairs={{0,4},{1,3},{2,6},{3,1},{4,0},{5,7},{6,2},{7,5},{8,12},{9,11},{10,... | collective-permute-start | bytes 3145736 | tf_op jit(solution)/shard_map/ppermute | solution.py:202
  39.6 25.6 %collective-permute-start.11 = (bf16[256,2048]{1,0:T(8,128)(2,1)}, bf16[256,2048]{1,0:T(8,128)(2,1)S(1)}, u32[]{:S(2)}, u32[]{:S(2)}) collective-permute-start(bf16[256,2048]{1,0:T(8,128)(2,1)} %collective-permute-done.9.refs_1_), channel_id=1, source_target_pairs={{0,4},{1,3},{2,6},{3,1},{4,0},{5,7},{6,2},{7,5},{8,12},{9,11},{10,... | collective-permute-start | bytes 3145736 | tf_op jit(solution)/shard_map/ppermute | solution.py:202
  41.2 22.6 %collective-permute-start.6 = (bf16[176,2048]{1,0:T(8,128)(2,1)S(1)}, bf16[176,2048]{1,0:T(8,128)(2,1)S(1)}, u32[]{:S(2)}, u32[]{:S(2)}) collective-permute-start(bf16[176,2048]{1,0:T(8,128)(2,1)S(1)} %pad_maximum_fusion.2.x0), channel_id=1, source_target_pairs={{0,1},{1,0},{2,3},{3,2},{4,5},{5,4},{6,7},{7,6},{8,9},{9,8},{10,11... | collective-permute-start | bytes 2162696 | tf_op jit(solution)/shard_map/ppermute | solution.py:202
  61.9 2.2 %collective-permute-start.5 = (bf16[176,2048]{1,0:T(8,128)(2,1)S(1)}, bf16[176,2048]{1,0:T(8,128)(2,1)S(1)}, u32[]{:S(2)}, u32[]{:S(2)}) collective-permute-start(bf16[176,2048]{1,0:T(8,128)(2,1)S(1)} %collective-permute-done.3.x1), channel_id=1, source_target_pairs={{0,1},{1,0},{2,3},{3,2},{4,5},{5,4},{6,7},{7,6},{8,9},{9,8},{10,11... | collective-permute-start | bytes 2162696 | tf_op jit(solution)/shard_map/ppermute | solution.py:202
  65.1 2.1 %copy-start.7 = (bf16[256,2048]{1,0:T(8,128)(2,1)}, bf16[256,2048]{1,0:T(8,128)(2,1)S(1)}, u32[]{:S(2)}) copy-start(bf16[256,2048]{1,0:T(8,128)(2,1)S(1)} %collective-permute-done.11.refs_3_) | copy-start | bytes 3145732
  67.2 18.1 %collective-permute-start.15 = (bf16[736,256]{1,0:T(8,128)(2,1)S(1)}, bf16[736,256]{1,0:T(8,128)(2,1)S(1)}, u32[]{:S(2)}, u32[]{:S(2)}) collective-permute-start(bf16[736,256]{1,0:T(8,128)(2,1)S(1)} %get-tuple-element.69), channel_id=1, source_target_pairs={{0,16},{1,17},{2,18},{3,19},{4,20},{5,21},{6,22},{7,23},{8,24},{9,... | collective-permute-start | bytes 1130504 | tf_op jit(solution)/shard_map/ppermute | solution.py:202
  74.7 20.3 %collective-permute-start.13 = (bf16[4,128,512]{2,1,0:T(8,128)(2,1)S(1)}, bf16[4,128,512]{2,1,0:T(8,128)(2,1)S(1)}, u32[]{:S(2)}, u32[]{:S(2)}) collective-permute-start(bf16[4,128,512]{2,1,0:T(8,128)(2,1)S(1)} %get-tuple-element.67), channel_id=1, source_target_pairs={{0,8},{1,9},{2,10},{3,11},{4,12},{5,13},{6,14},{7,15},{8,0},{9,1},... | collective-permute-start | bytes 1572872 | tf_op jit(solution)/shard_map/ppermute | solution.py:202
  74.7 39.8 %collective-permute-start.19 = (bf16[2,1024,256]{2,1,0:T(8,128)(2,1)S(1)}, bf16[2,1024,256]{2,1,0:T(8,128)(2,1)S(1)}, u32[]{:S(2)}, u32[]{:S(2)}) collective-permute-start(bf16[2,1024,256]{2,1,0:T(8,128)(2,1)S(1)} %pad_maximum_fusion.1.refs_4_), channel_id=1, source_target_pairs={{0,2},{1,5},{2,0},{3,7},{4,6},{5,1},{6,4},{7,3},{8,10},{9,13},{10,... | collective-permute-start | bytes 3145736 | tf_op jit(solution)/shard_map/ppermute | solution.py:202
  86.4 12.4 %collective-permute-start.16 = (bf16[6,128,256]{2,1,0:T(8,128)(2,1)S(1)}, bf16[6,128,256]{2,1,0:T(8,128)(2,1)S(1)}, u32[]{:S(2)}, u32[]{:S(2)}) collective-permute-start(bf16[6,128,256]{2,1,0:T(8,128)(2,1)S(1)} %keys_join.1.kv0), channel_id=1, source_target_pairs={{0,2},{1,5},{2,0},{3,7},{4,6},{5,1},{6,4},{7,3},{8,10},{9,13},{10,... | collective-permute-start | bytes 1179656 | tf_op jit(solution)/shard_map/ppermute | solution.py:202
  87.3 29.3 %collective-permute-start.12 = (bf16[4,128,512]{2,1,0:T(8,128)(2,1)S(1)}, bf16[4,128,512]{2,1,0:T(8,128)(2,1)S(1)}, u32[]{:S(2)}, u32[]{:S(2)}) collective-permute-start(bf16[4,128,512]{2,1,0:T(8,128)(2,1)S(1)} %get-tuple-element.65), channel_id=1, source_target_pairs={{0,8},{1,9},{2,10},{3,11},{4,12},{5,13},{6,14},{7,15},{8,0},{9,1},... | collective-permute-start | bytes 1572872 | tf_op jit(solution)/shard_map/ppermute | solution.py:202
  95.1 23.5 %collective-permute-start.14 = (bf16[4,128,512]{2,1,0:T(8,128)(2,1)S(1)}, bf16[4,128,512]{2,1,0:T(8,128)(2,1)S(1)}, u32[]{:S(2)}, u32[]{:S(2)}) collective-permute-start(bf16[4,128,512]{2,1,0:T(8,128)(2,1)S(1)} %add_convert_fusion), channel_id=1, source_target_pairs={{0,16},{1,17},{2,18},{3,19},{4,20},{5,21},{6,22},{7,23},{8,24},{9,... | collective-permute-start | bytes 1572872 | tf_op jit(solution)/shard_map/ppermute | solution.py:202
  98.3 16.2 %collective-permute-start.17 = (bf16[6,128,256]{2,1,0:T(8,128)(2,1)S(1)}, bf16[6,128,256]{2,1,0:T(8,128)(2,1)S(1)}, u32[]{:S(2)}, u32[]{:S(2)}) collective-permute-start(bf16[6,128,256]{2,1,0:T(8,128)(2,1)S(1)} %keys_join.1.kv0), channel_id=1, source_target_pairs={{0,4},{1,3},{2,6},{3,1},{4,0},{5,7},{6,2},{7,5},{8,12},{9,11},{10,... | collective-permute-start | bytes 1179656 | tf_op jit(solution)/shard_map/ppermute | solution.py:202
  98.8 15.7 %collective-permute-start.18 = (bf16[6,128,256]{2,1,0:T(8,128)(2,1)S(1)}, bf16[6,128,256]{2,1,0:T(8,128)(2,1)S(1)}, u32[]{:S(2)}, u32[]{:S(2)}) collective-permute-start(bf16[6,128,256]{2,1,0:T(8,128)(2,1)S(1)} %keys_join.1.kv0), channel_id=1, source_target_pairs={{0,6},{1,7},{2,4},{3,5},{4,2},{5,3},{6,0},{7,1},{8,14},{9,15},{10,... | collective-permute-start | bytes 1179656 | tf_op jit(solution)/shard_map/ppermute | solution.py:202
  114.5 24.0 %collective-permute-start.22 = (bf16[2,1024,256]{2,1,0:T(8,128)(2,1)S(1)}, bf16[2,1024,256]{2,1,0:T(8,128)(2,1)S(1)}, u32[]{:S(2)}, u32[]{:S(2)}) collective-permute-start(bf16[2,1024,256]{2,1,0:T(8,128)(2,1)S(1)} %pad_maximum_fusion.1.refs_4_), channel_id=1, source_target_pairs={{0,4},{1,3},{2,6},{3,1},{4,0},{5,7},{6,2},{7,5},{8,12},{9,11},{10,... | collective-permute-start | bytes 3145736 | tf_op jit(solution)/shard_map/ppermute | solution.py:202
  115.0 25.6 %collective-permute-start.23 = (bf16[2,1024,256]{2,1,0:T(8,128)(2,1)S(1)}, bf16[2,1024,256]{2,1,0:T(8,128)(2,1)S(1)}, u32[]{:S(2)}, u32[]{:S(2)}) collective-permute-start(bf16[2,1024,256]{2,1,0:T(8,128)(2,1)S(1)} %collective-permute-done.19.refs_5_), channel_id=1, source_target_pairs={{0,4},{1,3},{2,6},{3,1},{4,0},{5,7},{6,2},{7,5},{8,12},{9,11},{10,... | collective-permute-start | bytes 3145736 | tf_op jit(solution)/shard_map/ppermute | solution.py:202
  123.3 8.9 %collective-permute-start.21 = (bf16[512,256]{1,0:T(8,128)(2,1)S(1)}, bf16[512,256]{1,0:T(8,128)(2,1)S(1)}, u32[]{:S(2)}, u32[]{:S(2)}) collective-permute-start(bf16[512,256]{1,0:T(8,128)(2,1)S(1)} %attend.3.refs_1_), channel_id=1, source_target_pairs={{0,8},{1,9},{2,10},{3,11},{4,12},{5,13},{6,14},{7,15},{8,0},{9,1},... | collective-permute-start | bytes 786440 | tf_op jit(solution)/shard_map/ppermute | solution.py:202
  132.1 6.4 %collective-permute-start.20 = (bf16[512,256]{1,0:T(8,128)(2,1)S(1)}, bf16[512,256]{1,0:T(8,128)(2,1)S(1)}, u32[]{:S(2)}, u32[]{:S(2)}) collective-permute-start(bf16[512,256]{1,0:T(8,128)(2,1)S(1)} %attend.2.refs_0_), channel_id=1, source_target_pairs={{0,8},{1,9},{2,10},{3,11},{4,12},{5,13},{6,14},{7,15},{8,0},{9,1},... | collective-permute-start | bytes 786440 | tf_op jit(solution)/shard_map/ppermute | solution.py:202
  140.6 1.0 copy-start.8
  145.5 2.7 %collective-permute-start.24 = (bf16[4,128,1024]{2,1,0:T(8,128)(2,1)S(1)}, bf16[4,128,1024]{2,1,0:T(8,128)(2,1)S(1)}, u32[]{:S(2)}, u32[]{:S(2)}) collective-permute-start(bf16[4,128,1024]{2,1,0:T(8,128)(2,1)S(1)} %get-tuple-element.78), channel_id=1, source_target_pairs={{0,1},{1,0},{2,3},{3,2},{4,5},{5,4},{6,7},{7,6},{8,9},{9,8},{10,11... | collective-permute-start | bytes 3145736 | tf_op jit(solution)/shard_map/ppermute | solution.py:202
  150.0 21.7 %collective-permute-start.25 = (bf16[128,1024]{1,0:T(8,128)(2,1)S(1)}, bf16[128,1024]{1,0:T(8,128)(2,1)S(1)}, u32[]{:S(2)}, u32[]{:S(2)}) collective-permute-start(bf16[128,1024]{1,0:T(8,128)(2,1)S(1)} %get-tuple-element.83), channel_id=1, source_target_pairs={{0,8},{1,9},{2,10},{3,11},{4,12},{5,13},{6,14},{7,15},{8,16},{9,17... | collective-permute-start | bytes 786440 | tf_op jit(solution)/shard_map/ppermute | solution.py:202
  153.8 22.7 %collective-permute-start.26 = (bf16[128,1024]{1,0:T(8,128)(2,1)S(1)}, bf16[128,1024]{1,0:T(8,128)(2,1)S(1)}, u32[]{:S(2)}, u32[]{:S(2)}) collective-permute-start(bf16[128,1024]{1,0:T(8,128)(2,1)S(1)} %get-tuple-element.82), channel_id=1, source_target_pairs={{0,16},{1,17},{2,18},{3,19},{4,20},{5,21},{6,22},{7,23},{8,24},{9,... | collective-permute-start | bytes 786440 | tf_op jit(solution)/shard_map/ppermute | solution.py:202
  154.8 22.6 %collective-permute-start.27 = (bf16[128,1024]{1,0:T(8,128)(2,1)S(1)}, bf16[128,1024]{1,0:T(8,128)(2,1)S(1)}, u32[]{:S(2)}, u32[]{:S(2)}) collective-permute-start(bf16[128,1024]{1,0:T(8,128)(2,1)S(1)} %get-tuple-element.81), channel_id=1, source_target_pairs={{0,24},{1,25},{2,26},{3,27},{4,28},{5,29},{6,30},{7,31},{8,0},{9,1... | collective-permute-start | bytes 786440 | tf_op jit(solution)/shard_map/ppermute | solution.py:202

commit v15 on v14

--- a/solution.py
+++ b/solution.py
@@ -554,7 +554,9 @@
     held = jnp.concatenate([jnp.where(own_first, normed, crossed), shown], axis=0)
     next_rows = across(held, 1)
     held_other = other_core(held)
-    next_rows, out_got = lax.optimization_barrier((next_rows, across(out_give, 2)))
+    out_half = out_rows // 2
+    next_rows, out_got0 = lax.optimization_barrier((next_rows, across(out_give[:out_half], 2)))
+    out_got1 = across(out_give[out_half:], 2)
     next_other = other_core(next_rows)
     keys_far = to_far(jnp.concatenate([keys, keys_near], axis=0))
     next_other, held_other, keys_far, query_both = lax.optimization_barrier(
@@ -607,8 +609,8 @@
     got_near2 = across(q_send2, 1)
     got_near = across(q_send, 1)
     got_queries = across((q_keep2 + got_near2.astype(jnp.float32)).astype(jnp.bfloat16), 2)
-    out_pair = jnp.stack([out_own, out_got])
-    out_pair, q_send2 = lax.optimization_barrier((out_pair, q_send2))
+    out_got1, q_send2 = lax.optimization_barrier((out_got1, q_send2))
+    out_pair = jnp.stack([out_own, jnp.concatenate([out_got0, out_got1], axis=0)])
     out_near = to_near(out_pair)
     got_keys, q_send2 = lax.optimization_barrier((across(send, 2), q_send2))
     kv = pl.pallas_call(

time: 179 us -> 182 us (1.017)
  starting transfers between devices: 49.1 us -> 51.8 us
    ppermute x28 -> x29, starting transfers between devices: 49.1 us -> 51.8 us  [permuted(): return lax.ppermute(value, ('seq', 'head'), perm)]
    ppermute x28 -> x29, waiting for transfers between devices: 93 us -> 92.9 us  [permuted(): return lax.ppermute(value, ('seq', 'head'), perm)]
  transfers between devices with their start and end apart: 28 -> 29, of which waited for: 14 -> 15; matrix products, arithmetic and copies ran while one was open for 4% -> 4% of each run, Pallas kernels for 9% -> 10%
where the time goes in v15:
time: 182 us
  waiting for transfers between devices  92.9 us (51%)
  starting transfers between devices  51.8 us (28%)
  Pallas kernels  23.8 us (13%)
  other arithmetic  8.09 us (4%)
  blocking collectives  2.46 us (1%)
  local copies, waits for them, and re-layouts  2.12 us (1%)
    ppermute x29, waiting for transfers between devices, permuted(): return lax.ppermute(value, ('seq', 'head'), perm)  92.9 us
    ppermute x29, starting transfers between devices, permuted(): return lax.ppermute(value, ('seq', 'head'), perm)  51.8 us
    pallas_call x2, Pallas kernels, by_levels(): pl.pallas_call(functools.partial(attend_kernel, pair), out_shape=shaped((...  9.48 us
    pallas_call x1, Pallas kernels, by_levels(): pl.pallas_call(queries_part_kernel, out_shape=(shaped(group_shape, jnp.fl...  4.98 us
    pallas_call x1, Pallas kernels, by_levels(): pl.pallas_call(output_kernel, out_shape=(shaped((LEVELS, tok, wide_cols),...  3.88 us
  transfers between devices with their start and end apart: 29, of which 15 were waited for; matrix products, arithmetic and copies ran while one was open for 4% of the time, Pallas kernels for 10%

profile of v15, /device:TPU:8, one launch (start us, length us, event | category | flops | bytes accessed | tf_op | source)
XLA Modules:
  0.0 181.6 jit_solution(6326795733050336121)
XLA Ops:
  0.0 1.6 collective-permute-start.10
  1.6 1.5 collective-permute-start.9
  3.1 1.0 fusion.3
  4.2 0.1 pad.24.clone
  4.2 1.4 fusion
  5.6 2.5 %all-reduce.1 = (f32[144]{0:T(256)S(1)}, f32[32]{0:T(128)S(1)}) all-reduce(f32[144]{0:T(256)S(1)} %fusion, f32[32]{0:T(128)S(1)} %fusion.3), channel_id=1, replica_groups=mesh['seq'=16,'head'=2] {'head'}, use_global_device_ids=true, to_apply=%region_1.2 | all-reduce | flops 176 | bytes 1408 | tf_op jit(solution)/shard_map/psum | solution.py:518
  8.1 0.7 dynamic_slice.9
  8.8 1.1 fusion.2
  10.0 0.1 fusion.5
  10.2 0.1 stack.41.where_ref
  10.3 0.9 pack.1
  11.2 0.5 collective-permute-start.2
  11.7 3.4 %collective-permute-start.1 = (bf16[32,2048]{1,0:T(8,128)(2,1)S(1)}, bf16[32,2048]{1,0:T(8,128)(2,1)S(1)}, u32[]{:S(2)}, u32[]{:S(2)}) collective-permute-start(bf16[32,2048]{1,0:T(8,128)(2,1)S(1)} %fusion.5), channel_id=1, source_target_pairs={{0,0},{1,16},{2,1},{3,17},{4,8},{5,24},{6,9},{7,25},{8,2},{9,18},{... | collective-permute-start | bytes 393224 | tf_op jit(solution)/shard_map/ppermute | solution.py:202
  15.2 1.5 collective-permute-start
  16.8 8.2 %collective-permute-done.1 = bf16[32,2048]{1,0:T(8,128)(2,1)S(1)} collective-permute-done((bf16[32,2048]{1,0:T(8,128)(2,1)S(1)}, bf16[32,2048]{1,0:T(8,128)(2,1)S(1)}, u32[]{:S(2)}, u32[]{:S(2)}) %collective-permute-start.1) | collective-permute-done | bytes 131104 | tf_op jit(solution)/shard_map/ppermute | solution.py:202
  25.1 5.5 %collective-permute-start.7 = (bf16[2,256,512]{2,1,0:T(8,128)(2,1)S(1)}, bf16[2,256,512]{2,1,0:T(8,128)(2,1)S(1)}, u32[]{:S(2)}, u32[]{:S(2)}) collective-permute-start(bf16[2,256,512]{2,1,0:T(8,128)(2,1)S(1)} %pad_maximum_fusion.3.own), channel_id=1, source_target_pairs={{0,2},{1,5},{2,0},{3,7},{4,6},{5,1},{6,4},{7,3},{8,10},{9,13},{10,... | collective-permute-start | bytes 1572872 | tf_op jit(solution)/shard_map/ppermute | solution.py:202
  30.9 8.0 %collective-permute-start.4 = (bf16[512,256]{1,0:T(8,128)(2,1)S(1)}, bf16[512,256]{1,0:T(8,128)(2,1)S(1)}, u32[]{:S(2)}, u32[]{:S(2)}) collective-permute-start(bf16[512,256]{1,0:T(8,128)(2,1)S(1)} %get-tuple-element.88), channel_id=1, source_target_pairs={{0,16},{1,17},{2,18},{3,19},{4,20},{5,21},{6,22},{7,23},{8,24},{9,... | collective-permute-start | bytes 786440 | tf_op jit(solution)/shard_map/ppermute | solution.py:202
  38.9 0.1 pad_maximum_fusion
  39.0 0.5 collective-permute-start.8
  39.6 1.6 collective-permute-start.11
  41.3 12.4 %collective-permute-done.4 = bf16[512,256]{1,0:T(8,128)(2,1)S(1)} collective-permute-done((bf16[512,256]{1,0:T(8,128)(2,1)S(1)}, bf16[512,256]{1,0:T(8,128)(2,1)S(1)}, u32[]{:S(2)}, u32[]{:S(2)}) %collective-permute-start.4) | collective-permute-done | bytes 262176 | tf_op jit(solution)/shard_map/ppermute | solution.py:202
  53.7 2.9 %collective-permute-start.5 = (bf16[176,2048]{1,0:T(8,128)(2,1)S(1)}, bf16[176,2048]{1,0:T(8,128)(2,1)S(1)}, u32[]{:S(2)}, u32[]{:S(2)}) collective-permute-start(bf16[176,2048]{1,0:T(8,128)(2,1)S(1)} %collective-permute-done.3.x1), channel_id=1, source_target_pairs={{0,1},{1,0},{2,3},{3,2},{4,5},{5,4},{6,7},{7,6},{8,9},{9,8},{10,11... | collective-permute-start | bytes 2162696 | tf_op jit(solution)/shard_map/ppermute | solution.py:202
  56.7 1.4 fusion.9
  58.1 0.2 pad_maximum_fusion.4.cos_ref
  58.3 0.2 pad_maximum_fusion.5.sin_ref
  58.5 1.6 collective-permute-start.19
  60.2 5.0 %collective-permute-done.11.refs_3_ = bf16[256,2048]{1,0:T(8,128)(2,1)S(1)} collective-permute-done((bf16[256,2048]{1,0:T(8,128)(2,1)}, bf16[256,2048]{1,0:T(8,128)(2,1)S(1)}, u32[]{:S(2)}, u32[]{:S(2)}) %collective-permute-start.11) | collective-permute-done | bytes 1048608 | tf_op jit(solution)/shard_map/ppermute | solution.py:202
  65.1 2.1 %keys_part.1 = (f32[576,256]{1,0:T(8,128)S(1)}, bf16[736,256]{1,0:T(8,128)(2,1)S(1)}) custom-call(s32[5]{0:T(128)S(1)} %stack.41.where_ref, bf16[176,2048]{1,0:T(8,128)(2,1)S(1)} %pad_maximum_fusion.2.x0, bf16[176,2048]{1,0:T(8,128)(2,1)S(1)} %collective-permute-done.3.x1, bf16[176,2048]{1,0:T(8,128)(2,1)S(1)} %collective-permute-done.6.x2, ...), custom_call_target="tpu_custom_call" | custom-call | flops 3000000000 | bytes 4000000 | tf_op jit(solution)/shard_map/keys_part/pallas_call | solution.py:580
  67.3 0.1 collective-permute-start.15
  67.3 5.0 %queries_part.1 = (f32[4,128,512]{2,1,0:T(8,128)S(1)}, f32[4,128,512]{2,1,0:T(8,128)S(1)}, bf16[4,128,512]{2,1,0:T(8,128)(2,1)S(1)}, bf16[4,128,512]{2,1,0:T(8,128)(2,1)S(1)}) custom-call(s32[5]{0:T(128)S(1)} %stack.41.where_ref, bf16[176,2048]{1,0:T(8,128)(2,1)S(1)} %pad_maximum_fusion.2.x0, bf16[176,2048]{1,0:T(8,128)(2,1)S(1)} %collective-permute-done.3.x1, ...), custom_call_target="tpu_custom_call" | custom-call | flops 5000000000 | bytes 4000000 | tf_op jit(solution)/shard_map/queries_part/pallas_call | solution.py:597
  72.3 2.1 %collective-permute-start.13 = (bf16[4,128,512]{2,1,0:T(8,128)(2,1)S(1)}, bf16[4,128,512]{2,1,0:T(8,128)(2,1)S(1)}, u32[]{:S(2)}, u32[]{:S(2)}) collective-permute-start(bf16[4,128,512]{2,1,0:T(8,128)(2,1)S(1)} %get-tuple-element.67), channel_id=1, source_target_pairs={{0,8},{1,9},{2,10},{3,11},{4,12},{5,13},{6,14},{7,15},{8,0},{9,1},... | collective-permute-start | bytes 1572872 | tf_op jit(solution)/shard_map/ppermute | solution.py:202
  74.5 5.9 %collective-permute-done.19 = bf16[512,256]{1,0:T(8,128)(2,1)S(1)} collective-permute-done((bf16[512,256]{1,0:T(8,128)(2,1)S(1)}, bf16[512,256]{1,0:T(8,128)(2,1)S(1)}, u32[]{:S(2)}, u32[]{:S(2)}) %collective-permute-start.19) | collective-permute-done | bytes 262176 | tf_op jit(solution)/shard_map/ppermute | solution.py:202
  80.4 0.1 pad_maximum_fusion.1.refs_4_
  80.5 0.4 collective-permute-start.20
  80.9 7.3 %collective-permute-done.15.got_ref = bf16[736,256]{1,0:T(8,128)(2,1)S(1)} collective-permute-done((bf16[736,256]{1,0:T(8,128)(2,1)S(1)}, bf16[736,256]{1,0:T(8,128)(2,1)S(1)}, u32[]{:S(2)}, u32[]{:S(2)}) %collective-permute-start.15) | collective-permute-done | bytes 376864 | tf_op jit(solution)/shard_map/ppermute | solution.py:202
  88.2 1.0 keys_join.1.kv0
  89.3 0.3 collective-permute-start.16
  89.5 3.6 %collective-permute-start.12 = (bf16[4,128,512]{2,1,0:T(8,128)(2,1)S(1)}, bf16[4,128,512]{2,1,0:T(8,128)(2,1)S(1)}, u32[]{:S(2)}, u32[]{:S(2)}) collective-permute-start(bf16[4,128,512]{2,1,0:T(8,128)(2,1)S(1)} %get-tuple-element.65), channel_id=1, source_target_pairs={{0,8},{1,9},{2,10},{3,11},{4,12},{5,13},{6,14},{7,15},{8,0},{9,1},... | collective-permute-start | bytes 1572872 | tf_op jit(solution)/shard_map/ppermute | solution.py:202
  93.1 4.9 %collective-permute-done.13 = bf16[4,128,512]{2,1,0:T(8,128)(2,1)S(1)} collective-permute-done((bf16[4,128,512]{2,1,0:T(8,128)(2,1)S(1)}, bf16[4,128,512]{2,1,0:T(8,128)(2,1)S(1)}, u32[]{:S(2)}, u32[]{:S(2)}) %collective-permute-start.13) | collective-permute-done | bytes 524320 | tf_op jit(solution)/shard_map/ppermute | solution.py:202
  97.9 0.2 add_convert_fusion
  98.1 7.5 %collective-permute-start.14 = (bf16[4,128,512]{2,1,0:T(8,128)(2,1)S(1)}, bf16[4,128,512]{2,1,0:T(8,128)(2,1)S(1)}, u32[]{:S(2)}, u32[]{:S(2)}) collective-permute-start(bf16[4,128,512]{2,1,0:T(8,128)(2,1)S(1)} %add_convert_fusion), channel_id=1, source_target_pairs={{0,16},{1,17},{2,18},{3,19},{4,20},{5,21},{6,22},{7,23},{8,24},{9,... | collective-permute-start | bytes 1572872 | tf_op jit(solution)/shard_map/ppermute | solution.py:202
  105.6 1.6 collective-permute-start.17
  107.2 8.0 %collective-permute-done.17.kv2 = bf16[6,128,256]{2,1,0:T(8,128)(2,1)S(1)} collective-permute-done((bf16[6,128,256]{2,1,0:T(8,128)(2,1)S(1)}, bf16[6,128,256]{2,1,0:T(8,128)(2,1)S(1)}, u32[]{:S(2)}, u32[]{:S(2)}) %collective-permute-start.17) | collective-permute-done | bytes 393248 | tf_op jit(solution)/shard_map/ppermute | solution.py:202
  115.2 4.8 %collective-permute-done.18.kv3 = bf16[6,128,256]{2,1,0:T(8,128)(2,1)S(1)} collective-permute-done((bf16[6,128,256]{2,1,0:T(8,128)(2,1)S(1)}, bf16[6,128,256]{2,1,0:T(8,128)(2,1)S(1)}, u32[]{:S(2)}, u32[]{:S(2)}) %collective-permute-start.18) | collective-permute-done | bytes 393248 | tf_op jit(solution)/shard_map/ppermute | solution.py:202
  120.0 0.5 collective-permute-start.23
  120.5 1.5 collective-permute-start.24
  122.0 4.7 %attend.3.refs_1_ = bf16[512,256]{1,0:T(8,128)(2,1)S(1)} custom-call(s32[5]{0:T(128)S(1)} %stack.41.where_ref, f32[4,128,512]{2,1,0:T(8,128)S(1)} %get-tuple-element.64.keep_ref, bf16[4,128,512]{2,1,0:T(8,128)(2,1)S(1)} %collective-permute-done.12.near_ref, bf16[4,128,512]{2,1,0:T(8,128)(2,1)S(1)} %collective-permute-done.14.got_ref, ...), custom_call_target="tpu_custom_call" | custom-call | flops 4000000000 | bytes 4000000 | tf_op jit(solution)/shard_map/attend/pallas_call | solution.py:637
  126.7 2.6 %collective-permute-start.22 = (bf16[512,256]{1,0:T(8,128)(2,1)S(1)}, bf16[512,256]{1,0:T(8,128)(2,1)S(1)}, u32[]{:S(2)}, u32[]{:S(2)}) collective-permute-start(bf16[512,256]{1,0:T(8,128)(2,1)S(1)} %attend.3.refs_1_), channel_id=1, source_target_pairs={{0,8},{1,9},{2,10},{3,11},{4,12},{5,13},{6,14},{7,15},{8,0},{9,1},... | collective-permute-start | bytes 786440 | tf_op jit(solution)/shard_map/ppermute | solution.py:202
  129.3 4.8 %attend.2.refs_0_ = bf16[512,256]{1,0:T(8,128)(2,1)S(1)} custom-call(s32[5]{0:T(128)S(1)} %stack.41.where_ref, f32[4,128,512]{2,1,0:T(8,128)S(1)} %get-tuple-element.64.keep_ref, bf16[4,128,512]{2,1,0:T(8,128)(2,1)S(1)} %collective-permute-done.12.near_ref, bf16[4,128,512]{2,1,0:T(8,128)(2,1)S(1)} %collective-permute-done.14.got_ref, ...), custom_call_target="tpu_custom_call" | custom-call | flops 4000000000 | bytes 4000000 | tf_op jit(solution)/shard_map/attend/pallas_call | solution.py:637
  134.1 0.1 collective-permute-start.21
  134.2 0.8 collective-permute-done.22.refs_3_
  135.0 5.5 %collective-permute-done.21.refs_2_ = bf16[512,256]{1,0:T(8,128)(2,1)S(1)} collective-permute-done((bf16[512,256]{1,0:T(8,128)(2,1)S(1)}, bf16[512,256]{1,0:T(8,128)(2,1)S(1)}, u32[]{:S(2)}, u32[]{:S(2)}) %collective-permute-start.21) | collective-permute-done | bytes 262176 | tf_op jit(solution)/shard_map/ppermute | solution.py:202
  140.6 5.5 %collective-permute-done.24.refs_7_ = bf16[2,1024,256]{2,1,0:T(8,128)(2,1)S(1)} collective-permute-done((bf16[2,1024,256]{2,1,0:T(8,128)(2,1)S(1)}, bf16[2,1024,256]{2,1,0:T(8,128)(2,1)S(1)}, u32[]{:S(2)}, u32[]{:S(2)}) %collective-permute-start.24) | collective-permute-done | bytes 1048608 | tf_op jit(solution)/shard_map/ppermute | solution.py:202
  146.0 1.0 copy-done.8
  147.0 3.9 %output.1 = (f32[4,128,1024]{2,1,0:T(8,128)}, bf16[4,128,1024]{2,1,0:T(8,128)(2,1)S(1)}) custom-call(s32[5]{0:T(128)S(1)} %stack.41.where_ref, bf16[512,256]{1,0:T(8,128)(2,1)S(1)} %attend.2.refs_0_, bf16[512,256]{1,0:T(8,128)(2,1)S(1)} %attend.3.refs_1_, bf16[512,256]{1,0:T(8,128)(2,1)S(1)} %collective-permute-done.21.refs_2_, ...), custom_call_target="tpu_custom_call" | custom-call | flops 5000000000 | bytes 4000000 | tf_op jit(solution)/shard_map/output/pallas_call | solution.py:654
  150.9 2.7 %collective-permute-done.25 = bf16[4,128,1024]{2,1,0:T(8,128)(2,1)S(1)} collective-permute-done((bf16[4,128,1024]{2,1,0:T(8,128)(2,1)S(1)}, bf16[4,128,1024]{2,1,0:T(8,128)(2,1)S(1)}, u32[]{:S(2)}, u32[]{:S(2)}) %collective-permute-start.25) | collective-permute-done | bytes 1048608 | tf_op jit(solution)/shard_map/ppermute | solution.py:202
  153.6 1.9 %fusion.8 = (bf16[128,1024]{1,0:T(8,128)(2,1)S(1)}, bf16[128,1024]{1,0:T(8,128)(2,1)S(1)}, bf16[128,1024]{1,0:T(8,128)(2,1)S(1)}, f32[128,1024]{1,0:T(8,128)S(1)}) fusion(f32[4,128,1024]{2,1,0:T(8,128)} %get-tuple-element.77, bf16[4,128,1024]{2,1,0:T(8,128)(2,1)S(1)} %collective-permute-done.25), kind=kLoop, calls=%fused_computation.29 | loop fusion | flops 1441792 | bytes 4456448 | tf_op jit(solution)/shard_map/convert_element_type | solution.py:671
  155.4 1.1 collective-permute-start.26
  156.6 0.3 collective-permute-start.27
  156.9 1.2 collective-permute-start.28
  158.1 6.5 %collective-permute-done.26.first = bf16[128,1024]{1,0:T(8,128)(2,1)S(1)} collective-permute-done((bf16[128,1024]{1,0:T(8,128)(2,1)S(1)}, bf16[128,1024]{1,0:T(8,128)(2,1)S(1)}, u32[]{:S(2)}, u32[]{:S(2)}) %collective-permute-start.26) | collective-permute-done | bytes 262176 | tf_op jit(solution)/shard_map/ppermute | solution.py:202
  164.6 14.6 %collective-permute-done.27.second = bf16[128,1024]{1,0:T(8,128)(2,1)S(1)} collective-permute-done((bf16[128,1024]{1,0:T(8,128)(2,1)S(1)}, bf16[128,1024]{1,0:T(8,128)(2,1)S(1)}, u32[]{:S(2)}, u32[]{:S(2)}) %collective-permute-start.27) | collective-permute-done | bytes 262176 | tf_op jit(solution)/shard_map/ppermute | solution.py:202
  179.3 0.8 collective-permute-done.28.third
  180.1 1.4 finish.1
  (58 shorter events, 0.8 us)
Async XLA Ops:
  0.0 10.0 %copy-start.6 = (bf16[32,2048]{1,0:T(8,128)(2,1)S(1)}, bf16[32,2048]{1,0:T(8,128)(2,1)}, u32[]{:S(2)}) copy-start(bf16[32,2048]{1,0:T(8,128)(2,1)} %param.13) | copy-start | bytes 393220
  0.0 8.8 %copy-start.4 = (bf16[128,2048]{1,0:T(8,128)(2,1)S(1)}, bf16[128,2048]{1,0:T(8,128)(2,1)}, u32[]{:S(2)}) copy-start(bf16[128,2048]{1,0:T(8,128)(2,1)} %param.12) | copy-start | bytes 1572868
  0.0 10.1 %copy-start.9 = (s32[8]{0:T(128)S(1)}, s32[8]{0:T(128)}, u32[]{:S(2)}) copy-start(s32[8]{0:T(128)} %param.22) | copy-start | bytes 100
  0.0 10.3 %copy-start = (bf16[256,512]{1,0:T(8,128)(2,1)S(1)}, bf16[256,512]{1,0:T(8,128)(2,1)}, u32[]{:S(2)}) copy-start(bf16[256,512]{1,0:T(8,128)(2,1)} %refs_0_.2) | copy-start | bytes 786436
  0.0 10.2 %copy-start.1 = (bf16[256,512]{1,0:T(8,128)(2,1)S(1)}, bf16[256,512]{1,0:T(8,128)(2,1)}, u32[]{:S(2)}) copy-start(bf16[256,512]{1,0:T(8,128)(2,1)} %refs_1_.1) | copy-start | bytes 786436
  0.0 10.2 %copy-start.2 = (bf16[64,512]{1,0:T(8,128)(2,1)S(1)}, bf16[64,512]{1,0:T(8,128)(2,1)}, u32[]{:S(2)}) copy-start(bf16[64,512]{1,0:T(8,128)(2,1)} %refs_2_.1) | copy-start | bytes 196612
  0.0 10.2 %copy-start.3 = (bf16[64,512]{1,0:T(8,128)(2,1)S(1)}, bf16[64,512]{1,0:T(8,128)(2,1)}, u32[]{:S(2)}) copy-start(bf16[64,512]{1,0:T(8,128)(2,1)} %refs_3_.1) | copy-start | bytes 196612
  0.0 39.5 %collective-permute-start.10 = (bf16[256,2048]{1,0:T(8,128)(2,1)}, bf16[256,2048]{1,0:T(8,128)(2,1)}, u32[]{:S(2)}, u32[]{:S(2)}) collective-permute-start(bf16[256,2048]{1,0:T(8,128)(2,1)} %refs_0_.3), channel_id=1, source_target_pairs={{0,4},{1,3},{2,6},{3,1},{4,0},{5,7},{6,2},{7,5},{8,12},{9,11},{10,... | collective-permute-start | bytes 3145736 | tf_op jit(solution)/shard_map/ppermute | solution.py:202
  1.6 37.9 %collective-permute-start.9 = (bf16[256,2048]{1,0:T(8,128)(2,1)}, bf16[256,2048]{1,0:T(8,128)(2,1)}, u32[]{:S(2)}, u32[]{:S(2)}) collective-permute-start(bf16[256,2048]{1,0:T(8,128)(2,1)} %refs_0_.3), channel_id=1, source_target_pairs={{0,2},{1,5},{2,0},{3,7},{4,6},{5,1},{6,4},{7,3},{8,10},{9,13},{10,... | collective-permute-start | bytes 3145736 | tf_op jit(solution)/shard_map/ppermute | solution.py:202
  10.3 6.5 %copy-start.5 = (bf16[2048,256]{1,0:T(8,128)(2,1)S(1)}, bf16[2048,256]{1,0:T(8,128)(2,1)}, u32[]{:S(2)}) copy-start(bf16[2048,256]{1,0:T(8,128)(2,1)} %param.18) | copy-start | bytes 3145732
  11.2 13.8 %collective-permute-start.2 = (bf16[336,512]{1,0:T(8,128)(2,1)S(1)}, bf16[336,512]{1,0:T(8,128)(2,1)S(1)}, u32[]{:S(2)}, u32[]{:S(2)}) collective-permute-start(bf16[336,512]{1,0:T(8,128)(2,1)S(1)} %get-tuple-element.45), channel_id=1, source_target_pairs={{0,8},{1,9},{2,10},{3,11},{4,12},{5,13},{6,14},{7,15},{8,0},{9,1},... | collective-permute-start | bytes 1032200 | tf_op jit(solution)/shard_map/ppermute | solution.py:202
  11.7 13.3 %collective-permute-start.1 = (bf16[32,2048]{1,0:T(8,128)(2,1)S(1)}, bf16[32,2048]{1,0:T(8,128)(2,1)S(1)}, u32[]{:S(2)}, u32[]{:S(2)}) collective-permute-start(bf16[32,2048]{1,0:T(8,128)(2,1)S(1)} %fusion.5), channel_id=1, source_target_pairs={{0,0},{1,16},{2,1},{3,17},{4,8},{5,24},{6,9},{7,25},{8,2},{9,18},{... | collective-permute-start | bytes 393224 | tf_op jit(solution)/shard_map/ppermute | solution.py:202
  15.2 15.5 %collective-permute-start = (bf16[144,2048]{1,0:T(8,128)(2,1)S(1)}, bf16[144,2048]{1,0:T(8,128)(2,1)}, u32[]{:S(2)}, u32[]{:S(2)}) collective-permute-start(bf16[144,2048]{1,0:T(8,128)(2,1)S(1)} %fusion.2), channel_id=1, source_target_pairs={{1,16},{3,18},{5,20},{7,22},{9,24},{11,26},{13,28},{15,30},{16,1},... | collective-permute-start | bytes 1769480 | tf_op jit(solution)/shard_map/ppermute | solution.py:202
  25.1 13.8 %collective-permute-start.7 = (bf16[2,256,512]{2,1,0:T(8,128)(2,1)S(1)}, bf16[2,256,512]{2,1,0:T(8,128)(2,1)S(1)}, u32[]{:S(2)}, u32[]{:S(2)}) collective-permute-start(bf16[2,256,512]{2,1,0:T(8,128)(2,1)S(1)} %pad_maximum_fusion.3.own), channel_id=1, source_target_pairs={{0,2},{1,5},{2,0},{3,7},{4,6},{5,1},{6,4},{7,3},{8,10},{9,13},{10,... | collective-permute-start | bytes 1572872 | tf_op jit(solution)/shard_map/ppermute | solution.py:202
  30.8 23.0 %collective-permute-start.3 = (bf16[176,2048]{1,0:T(8,128)(2,1)S(1)}, bf16[176,2048]{1,0:T(8,128)(2,1)S(1)}, u32[]{:S(2)}, u32[]{:S(2)}) collective-permute-start(bf16[176,2048]{1,0:T(8,128)(2,1)S(1)} %pad_maximum_fusion.2.x0), channel_id=1, source_target_pairs={{0,8},{1,9},{2,10},{3,11},{4,12},{5,13},{6,14},{7,15},{8,0},{9,1},... | collective-permute-start | bytes 2162696 | tf_op jit(solution)/shard_map/ppermute | solution.py:202
  30.9 22.8 %collective-permute-start.4 = (bf16[512,256]{1,0:T(8,128)(2,1)S(1)}, bf16[512,256]{1,0:T(8,128)(2,1)S(1)}, u32[]{:S(2)}, u32[]{:S(2)}) collective-permute-start(bf16[512,256]{1,0:T(8,128)(2,1)S(1)} %get-tuple-element.88), channel_id=1, source_target_pairs={{0,16},{1,17},{2,18},{3,19},{4,20},{5,21},{6,22},{7,23},{8,24},{9,... | collective-permute-start | bytes 786440 | tf_op jit(solution)/shard_map/ppermute | solution.py:202
  39.0 21.1 %collective-permute-start.8 = (bf16[4,256,512]{2,1,0:T(8,128)(2,1)S(1)}, bf16[4,256,512]{2,1,0:T(8,128)(2,1)S(1)}, u32[]{:S(2)}, u32[]{:S(2)}) collective-permute-start(bf16[4,256,512]{2,1,0:T(8,128)(2,1)S(1)} %pad_maximum_fusion), channel_id=1, source_target_pairs={{0,4},{1,3},{2,6},{3,1},{4,0},{5,7},{6,2},{7,5},{8,12},{9,11},{10,... | collective-permute-start | bytes 3145736 | tf_op jit(solution)/shard_map/ppermute | solution.py:202
  39.6 25.6 %collective-permute-start.11 = (bf16[256,2048]{1,0:T(8,128)(2,1)}, bf16[256,2048]{1,0:T(8,128)(2,1)S(1)}, u32[]{:S(2)}, u32[]{:S(2)}) collective-permute-start(bf16[256,2048]{1,0:T(8,128)(2,1)} %collective-permute-done.9.refs_1_), channel_id=1, source_target_pairs={{0,4},{1,3},{2,6},{3,1},{4,0},{5,7},{6,2},{7,5},{8,12},{9,11},{10,... | collective-permute-start | bytes 3145736 | tf_op jit(solution)/shard_map/ppermute | solution.py:202
  41.3 18.9 %collective-permute-start.6 = (bf16[176,2048]{1,0:T(8,128)(2,1)S(1)}, bf16[176,2048]{1,0:T(8,128)(2,1)S(1)}, u32[]{:S(2)}, u32[]{:S(2)}) collective-permute-start(bf16[176,2048]{1,0:T(8,128)(2,1)S(1)} %pad_maximum_fusion.2.x0), channel_id=1, source_target_pairs={{0,1},{1,0},{2,3},{3,2},{4,5},{5,4},{6,7},{7,6},{8,9},{9,8},{10,11... | collective-permute-start | bytes 2162696 | tf_op jit(solution)/shard_map/ppermute | solution.py:202
  53.7 6.4 %collective-permute-start.5 = (bf16[176,2048]{1,0:T(8,128)(2,1)S(1)}, bf16[176,2048]{1,0:T(8,128)(2,1)S(1)}, u32[]{:S(2)}, u32[]{:S(2)}) collective-permute-start(bf16[176,2048]{1,0:T(8,128)(2,1)S(1)} %collective-permute-done.3.x1), channel_id=1, source_target_pairs={{0,1},{1,0},{2,3},{3,2},{4,5},{5,4},{6,7},{7,6},{8,9},{9,8},{10,11... | collective-permute-start | bytes 2162696 | tf_op jit(solution)/shard_map/ppermute | solution.py:202
  58.5 21.8 %collective-permute-start.19 = (bf16[512,256]{1,0:T(8,128)(2,1)S(1)}, bf16[512,256]{1,0:T(8,128)(2,1)S(1)}, u32[]{:S(2)}, u32[]{:S(2)}) collective-permute-start(bf16[512,256]{1,0:T(8,128)(2,1)S(1)} %get-tuple-element.87), channel_id=1, source_target_pairs={{0,16},{1,17},{2,18},{3,19},{4,20},{5,21},{6,22},{7,23},{8,24},{9,... | collective-permute-start | bytes 786440 | tf_op jit(solution)/shard_map/ppermute | solution.py:202
  65.1 2.1 %copy-start.7 = (bf16[256,2048]{1,0:T(8,128)(2,1)}, bf16[256,2048]{1,0:T(8,128)(2,1)S(1)}, u32[]{:S(2)}) copy-start(bf16[256,2048]{1,0:T(8,128)(2,1)S(1)} %collective-permute-done.11.refs_3_) | copy-start | bytes 3145732
  67.3 21.0 %collective-permute-start.15 = (bf16[736,256]{1,0:T(8,128)(2,1)S(1)}, bf16[736,256]{1,0:T(8,128)(2,1)S(1)}, u32[]{:S(2)}, u32[]{:S(2)}) collective-permute-start(bf16[736,256]{1,0:T(8,128)(2,1)S(1)} %get-tuple-element.69), channel_id=1, source_target_pairs={{0,16},{1,17},{2,18},{3,19},{4,20},{5,21},{6,22},{7,23},{8,24},{9,... | collective-permute-start | bytes 1130504 | tf_op jit(solution)/shard_map/ppermute | solution.py:202
  72.3 25.6 %collective-permute-start.13 = (bf16[4,128,512]{2,1,0:T(8,128)(2,1)S(1)}, bf16[4,128,512]{2,1,0:T(8,128)(2,1)S(1)}, u32[]{:S(2)}, u32[]{:S(2)}) collective-permute-start(bf16[4,128,512]{2,1,0:T(8,128)(2,1)S(1)} %get-tuple-element.67), channel_id=1, source_target_pairs={{0,8},{1,9},{2,10},{3,11},{4,12},{5,13},{6,14},{7,15},{8,0},{9,1},... | collective-permute-start | bytes 1572872 | tf_op jit(solution)/shard_map/ppermute | solution.py:202
  80.5 39.5 %collective-permute-start.20 = (bf16[2,1024,256]{2,1,0:T(8,128)(2,1)S(1)}, bf16[2,1024,256]{2,1,0:T(8,128)(2,1)S(1)}, u32[]{:S(2)}, u32[]{:S(2)}) collective-permute-start(bf16[2,1024,256]{2,1,0:T(8,128)(2,1)S(1)} %pad_maximum_fusion.1.refs_4_), channel_id=1, source_target_pairs={{0,2},{1,5},{2,0},{3,7},{4,6},{5,1},{6,4},{7,3},{8,10},{9,13},{10,... | collective-permute-start | bytes 3145736 | tf_op jit(solution)/shard_map/ppermute | solution.py:202
  89.3 18.0 %collective-permute-start.16 = (bf16[6,128,256]{2,1,0:T(8,128)(2,1)S(1)}, bf16[6,128,256]{2,1,0:T(8,128)(2,1)S(1)}, u32[]{:S(2)}, u32[]{:S(2)}) collective-permute-start(bf16[6,128,256]{2,1,0:T(8,128)(2,1)S(1)} %keys_join.1.kv0), channel_id=1, source_target_pairs={{0,2},{1,5},{2,0},{3,7},{4,6},{5,1},{6,4},{7,3},{8,10},{9,13},{10,... | collective-permute-start | bytes 1179656 | tf_op jit(solution)/shard_map/ppermute | solution.py:202
  89.5 32.5 %collective-permute-start.12 = (bf16[4,128,512]{2,1,0:T(8,128)(2,1)S(1)}, bf16[4,128,512]{2,1,0:T(8,128)(2,1)S(1)}, u32[]{:S(2)}, u32[]{:S(2)}) collective-permute-start(bf16[4,128,512]{2,1,0:T(8,128)(2,1)S(1)} %get-tuple-element.65), channel_id=1, source_target_pairs={{0,8},{1,9},{2,10},{3,11},{4,12},{5,13},{6,14},{7,15},{8,0},{9,1},... | collective-permute-start | bytes 1572872 | tf_op jit(solution)/shard_map/ppermute | solution.py:202
  98.1 23.9 %collective-permute-start.14 = (bf16[4,128,512]{2,1,0:T(8,128)(2,1)S(1)}, bf16[4,128,512]{2,1,0:T(8,128)(2,1)S(1)}, u32[]{:S(2)}, u32[]{:S(2)}) collective-permute-start(bf16[4,128,512]{2,1,0:T(8,128)(2,1)S(1)} %add_convert_fusion), channel_id=1, source_target_pairs={{0,16},{1,17},{2,18},{3,19},{4,20},{5,21},{6,22},{7,23},{8,24},{9,... | collective-permute-start | bytes 1572872 | tf_op jit(solution)/shard_map/ppermute | solution.py:202
  105.6 9.6 %collective-permute-start.17 = (bf16[6,128,256]{2,1,0:T(8,128)(2,1)S(1)}, bf16[6,128,256]{2,1,0:T(8,128)(2,1)S(1)}, u32[]{:S(2)}, u32[]{:S(2)}) collective-permute-start(bf16[6,128,256]{2,1,0:T(8,128)(2,1)S(1)} %keys_join.1.kv0), channel_id=1, source_target_pairs={{0,4},{1,3},{2,6},{3,1},{4,0},{5,7},{6,2},{7,5},{8,12},{9,11},{10,... | collective-permute-start | bytes 1179656 | tf_op jit(solution)/shard_map/ppermute | solution.py:202
  107.2 12.8 %collective-permute-start.18 = (bf16[6,128,256]{2,1,0:T(8,128)(2,1)S(1)}, bf16[6,128,256]{2,1,0:T(8,128)(2,1)S(1)}, u32[]{:S(2)}, u32[]{:S(2)}) collective-permute-start(bf16[6,128,256]{2,1,0:T(8,128)(2,1)S(1)} %keys_join.1.kv0), channel_id=1, source_target_pairs={{0,6},{1,7},{2,4},{3,5},{4,2},{5,3},{6,0},{7,1},{8,14},{9,15},{10,... | collective-permute-start | bytes 1179656 | tf_op jit(solution)/shard_map/ppermute | solution.py:202
  120.0 20.6 %collective-permute-start.23 = (bf16[2,1024,256]{2,1,0:T(8,128)(2,1)S(1)}, bf16[2,1024,256]{2,1,0:T(8,128)(2,1)S(1)}, u32[]{:S(2)}, u32[]{:S(2)}) collective-permute-start(bf16[2,1024,256]{2,1,0:T(8,128)(2,1)S(1)} %pad_maximum_fusion.1.refs_4_), channel_id=1, source_target_pairs={{0,4},{1,3},{2,6},{3,1},{4,0},{5,7},{6,2},{7,5},{8,12},{9,11},{10,... | collective-permute-start | bytes 3145736 | tf_op jit(solution)/shard_map/ppermute | solution.py:202
  120.5 25.5 %collective-permute-start.24 = (bf16[2,1024,256]{2,1,0:T(8,128)(2,1)S(1)}, bf16[2,1024,256]{2,1,0:T(8,128)(2,1)S(1)}, u32[]{:S(2)}, u32[]{:S(2)}) collective-permute-start(bf16[2,1024,256]{2,1,0:T(8,128)(2,1)S(1)} %collective-permute-done.20.refs_5_), channel_id=1, source_target_pairs={{0,4},{1,3},{2,6},{3,1},{4,0},{5,7},{6,2},{7,5},{8,12},{9,11},{10,... | collective-permute-start | bytes 3145736 | tf_op jit(solution)/shard_map/ppermute | solution.py:202
  126.7 8.3 %collective-permute-start.22 = (bf16[512,256]{1,0:T(8,128)(2,1)S(1)}, bf16[512,256]{1,0:T(8,128)(2,1)S(1)}, u32[]{:S(2)}, u32[]{:S(2)}) collective-permute-start(bf16[512,256]{1,0:T(8,128)(2,1)S(1)} %attend.3.refs_1_), channel_id=1, source_target_pairs={{0,8},{1,9},{2,10},{3,11},{4,12},{5,13},{6,14},{7,15},{8,0},{9,1},... | collective-permute-start | bytes 786440 | tf_op jit(solution)/shard_map/ppermute | solution.py:202
  134.1 6.4 %collective-permute-start.21 = (bf16[512,256]{1,0:T(8,128)(2,1)S(1)}, bf16[512,256]{1,0:T(8,128)(2,1)S(1)}, u32[]{:S(2)}, u32[]{:S(2)}) collective-permute-start(bf16[512,256]{1,0:T(8,128)(2,1)S(1)} %attend.2.refs_0_), channel_id=1, source_target_pairs={{0,8},{1,9},{2,10},{3,11},{4,12},{5,13},{6,14},{7,15},{8,0},{9,1},... | collective-permute-start | bytes 786440 | tf_op jit(solution)/shard_map/ppermute | solution.py:202
  146.0 1.0 copy-start.8
  150.9 2.7 %collective-permute-start.25 = (bf16[4,128,1024]{2,1,0:T(8,128)(2,1)S(1)}, bf16[4,128,1024]{2,1,0:T(8,128)(2,1)S(1)}, u32[]{:S(2)}, u32[]{:S(2)}) collective-permute-start(bf16[4,128,1024]{2,1,0:T(8,128)(2,1)S(1)} %get-tuple-element.78), channel_id=1, source_target_pairs={{0,1},{1,0},{2,3},{3,2},{4,5},{5,4},{6,7},{7,6},{8,9},{9,8},{10,11... | collective-permute-start | bytes 3145736 | tf_op jit(solution)/shard_map/ppermute | solution.py:202
  155.4 9.2 %collective-permute-start.26 = (bf16[128,1024]{1,0:T(8,128)(2,1)S(1)}, bf16[128,1024]{1,0:T(8,128)(2,1)S(1)}, u32[]{:S(2)}, u32[]{:S(2)}) collective-permute-start(bf16[128,1024]{1,0:T(8,128)(2,1)S(1)} %get-tuple-element.83), channel_id=1, source_target_pairs={{0,8},{1,9},{2,10},{3,11},{4,12},{5,13},{6,14},{7,15},{8,16},{9,17... | collective-permute-start | bytes 786440 | tf_op jit(solution)/shard_map/ppermute | solution.py:202
  156.6 22.7 %collective-permute-start.27 = (bf16[128,1024]{1,0:T(8,128)(2,1)S(1)}, bf16[128,1024]{1,0:T(8,128)(2,1)S(1)}, u32[]{:S(2)}, u32[]{:S(2)}) collective-permute-start(bf16[128,1024]{1,0:T(8,128)(2,1)S(1)} %get-tuple-element.82), channel_id=1, source_target_pairs={{0,16},{1,17},{2,18},{3,19},{4,20},{5,21},{6,22},{7,23},{8,24},{9,... | collective-permute-start | bytes 786440 | tf_op jit(solution)/shard_map/ppermute | solution.py:202
  156.9 23.2 %collective-permute-start.28 = (bf16[128,1024]{1,0:T(8,128)(2,1)S(1)}, bf16[128,1024]{1,0:T(8,128)(2,1)S(1)}, u32[]{:S(2)}, u32[]{:S(2)}) collective-permute-start(bf16[128,1024]{1,0:T(8,128)(2,1)S(1)} %get-tuple-element.81), channel_id=1, source_target_pairs={{0,24},{1,25},{2,26},{3,27},{4,28},{5,29},{6,30},{7,31},{8,0},{9,1... | collective-permute-start | bytes 786440 | tf_op jit(solution)/shard_map/ppermute | solution.py:202

commit v16 on v15

--- a/solution.py
+++ b/solution.py
@@ -544,9 +544,10 @@
     shown = permuted(pictures, lambda z, p, c: (2 * c + p // 2, z, p % 2))
     key_next = across(key_give, 1)
     query_near, query_far = to_near(w_query), to_far(w_query)
-    query_near, query_far = lax.optimization_barrier((query_near, query_far))
+    shown, key_next, query_near, query_far = lax.optimization_barrier(
+        (shown, key_next, query_near, query_far)
+    )
     query_both = to_far(query_near)
-    shown, key_next = lax.optimization_barrier((shown, key_next))
     keys = jnp.stack([key_own[:depth], key_next[:depth]])
     old_own, old_next = key_own[depth:], key_next[depth:]
     keys_near = to_near(keys)
@@ -555,12 +556,14 @@
     next_rows = across(held, 1)
     held_other = other_core(held)
     out_half = out_rows // 2
-    next_rows, out_got0 = lax.optimization_barrier((next_rows, across(out_give[:out_half], 2)))
+    next_rows, out_got0, query_both = lax.optimization_barrier(
+        (next_rows, across(out_give[:out_half], 2), query_both)
+    )
     out_got1 = across(out_give[out_half:], 2)
     next_other = other_core(next_rows)
     keys_far = to_far(jnp.concatenate([keys, keys_near], axis=0))
-    next_other, held_other, keys_far, query_both = lax.optimization_barrier(
-        (next_other, held_other, keys_far, query_both)
+    next_other, held_other, keys_far = lax.optimization_barrier(
+        (next_other, held_other, keys_far)
     )
     parts = (held, next_rows, held_other, next_other)
 

time: 182 us -> 181 us (level)
  starting transfers between devices: 51.8 us -> 43.9 us
  waiting for transfers between devices: 92.9 us -> 99 us
    ppermute x29, starting transfers between devices: 51.8 us -> 43.9 us  [permuted(): return lax.ppermute(value, ('seq', 'head'), perm)]
    ppermute x29, waiting for transfers between devices: 92.9 us -> 99 us  [permuted(): return lax.ppermute(value, ('seq', 'head'), perm)]
  transfers between devices with their start and end apart: 29 -> 29, of which waited for: 15 -> 16; matrix products, arithmetic and copies ran while one was open for 4% -> 4% of each run, Pallas kernels for 10% -> 10%
where the time goes in v16:
time: 181 us; the launch traced here: 180 us
  waiting for transfers between devices  99 us (55%)
  starting transfers between devices  43.9 us (24%)
  Pallas kernels  23.8 us (13%)
  other arithmetic  8.39 us (5%)
  blocking collectives  2.46 us (1%)
  local copies, waits for them, and re-layouts  2.12 us (1%)
    ppermute x29, waiting for transfers between devices, permuted(): return lax.ppermute(value, ('seq', 'head'), perm)  99 us
    ppermute x29, starting transfers between devices, permuted(): return lax.ppermute(value, ('seq', 'head'), perm)  43.9 us
    pallas_call x2, Pallas kernels, by_levels(): pl.pallas_call(functools.partial(attend_kernel, pair), out_shape=shaped((...  9.48 us
    pallas_call x1, Pallas kernels, by_levels(): pl.pallas_call(queries_part_kernel, out_shape=(shaped(group_shape, jnp.fl...  4.98 us
    pallas_call x1, Pallas kernels, by_levels(): pl.pallas_call(output_kernel, out_shape=(shaped((LEVELS, tok, wide_cols),...  3.88 us
  transfers between devices with their start and end apart: 29, of which 16 were waited for; matrix products, arithmetic and copies ran while one was open for 4% of the time, Pallas kernels for 10%

profile of v16, /device:TPU:8, one launch (start us, length us, event | category | flops | bytes accessed | tf_op | source)
XLA Modules:
  0.0 180.1 jit_solution(14310410130828699326)
XLA Ops:
  0.0 1.6 collective-permute-start.3
  1.6 1.5 collective-permute-start.4
  3.1 1.0 fusion.3
  4.2 1.4 fusion
  5.6 2.5 %all-reduce.1 = (f32[144]{0:T(256)S(1)}, f32[32]{0:T(128)S(1)}) all-reduce(f32[144]{0:T(256)S(1)} %fusion, f32[32]{0:T(128)S(1)} %fusion.3), channel_id=1, replica_groups=mesh['seq'=16,'head'=2] {'head'}, use_global_device_ids=true, to_apply=%region_1.2 | all-reduce | flops 176 | bytes 1408 | tf_op jit(solution)/shard_map/psum | solution.py:518
  8.1 0.7 dynamic_slice.9
  8.8 1.5 fusion.2
  10.3 0.1 fusion.5
  10.5 0.1 stack.41.where_ref
  10.7 0.9 pack.1
  11.6 0.5 collective-permute-start.2
  12.1 3.4 %collective-permute-start.1 = (bf16[32,2048]{1,0:T(8,128)(2,1)S(1)}, bf16[32,2048]{1,0:T(8,128)(2,1)S(1)}, u32[]{:S(2)}, u32[]{:S(2)}) collective-permute-start(bf16[32,2048]{1,0:T(8,128)(2,1)S(1)} %fusion.5), channel_id=1, source_target_pairs={{0,0},{1,16},{2,1},{3,17},{4,8},{5,24},{6,9},{7,25},{8,2},{9,18},{... | collective-permute-start | bytes 393224 | tf_op jit(solution)/shard_map/ppermute | solution.py:202
  15.5 1.5 collective-permute-start
  17.1 0.1 dynamic-slice_bitcast_fusion
  17.2 8.2 %collective-permute-done.1 = bf16[32,2048]{1,0:T(8,128)(2,1)S(1)} collective-permute-done((bf16[32,2048]{1,0:T(8,128)(2,1)S(1)}, bf16[32,2048]{1,0:T(8,128)(2,1)S(1)}, u32[]{:S(2)}, u32[]{:S(2)}) %collective-permute-start.1) | collective-permute-done | bytes 131104 | tf_op jit(solution)/shard_map/ppermute | solution.py:202
  25.4 0.9 collective-permute-done.3.refs_1_
  26.3 1.8 collective-permute-done.4.refs_2_
  28.2 2.7 %collective-permute-start.10 = (bf16[2,256,512]{2,1,0:T(8,128)(2,1)S(1)}, bf16[2,256,512]{2,1,0:T(8,128)(2,1)S(1)}, u32[]{:S(2)}, u32[]{:S(2)}) collective-permute-start(bf16[2,256,512]{2,1,0:T(8,128)(2,1)S(1)} %pad_maximum_fusion.3.own), channel_id=1, source_target_pairs={{0,2},{1,5},{2,0},{3,7},{4,6},{5,1},{6,4},{7,3},{8,10},{9,13},{10,... | collective-permute-start | bytes 1572872 | tf_op jit(solution)/shard_map/ppermute | solution.py:202
  31.1 0.9 collective-permute-start.5
  32.0 7.7 %collective-permute-start.6 = (bf16[512,256]{1,0:T(8,128)(2,1)S(1)}, bf16[512,256]{1,0:T(8,128)(2,1)S(1)}, u32[]{:S(2)}, u32[]{:S(2)}) collective-permute-start(bf16[512,256]{1,0:T(8,128)(2,1)S(1)} %get-tuple-element.88), channel_id=1, source_target_pairs={{0,16},{1,17},{2,18},{3,19},{4,20},{5,21},{6,22},{7,23},{8,24},{9,... | collective-permute-start | bytes 786440 | tf_op jit(solution)/shard_map/ppermute | solution.py:202
  39.8 0.1 pad_maximum_fusion
  39.9 1.6 collective-permute-start.11
  41.7 14.0 %collective-permute-done.6 = bf16[512,256]{1,0:T(8,128)(2,1)S(1)} collective-permute-done((bf16[512,256]{1,0:T(8,128)(2,1)S(1)}, bf16[512,256]{1,0:T(8,128)(2,1)S(1)}, u32[]{:S(2)}, u32[]{:S(2)}) %collective-permute-start.6) | collective-permute-done | bytes 262176 | tf_op jit(solution)/shard_map/ppermute | solution.py:202
  55.7 1.3 collective-permute-start.8
  57.1 1.4 fusion.9
  58.5 0.2 pad_maximum_fusion.4.cos_ref
  58.7 0.2 pad_maximum_fusion.5.sin_ref
  58.9 1.7 collective-permute-start.19
  60.6 2.1 %keys_part.1 = (f32[576,256]{1,0:T(8,128)S(1)}, bf16[736,256]{1,0:T(8,128)(2,1)S(1)}) custom-call(s32[5]{0:T(128)S(1)} %stack.41.where_ref, bf16[176,2048]{1,0:T(8,128)(2,1)S(1)} %pad_maximum_fusion.2.x0, bf16[176,2048]{1,0:T(8,128)(2,1)S(1)} %collective-permute-done.5.x1, bf16[176,2048]{1,0:T(8,128)(2,1)S(1)} %collective-permute-done.9.x2, ...), custom_call_target="tpu_custom_call" | custom-call | flops 3000000000 | bytes 4000000 | tf_op jit(solution)/shard_map/keys_part/pallas_call | solution.py:583
  62.7 4.7 %collective-permute-start.15 = (bf16[736,256]{1,0:T(8,128)(2,1)S(1)}, bf16[736,256]{1,0:T(8,128)(2,1)S(1)}, u32[]{:S(2)}, u32[]{:S(2)}) collective-permute-start(bf16[736,256]{1,0:T(8,128)(2,1)S(1)} %get-tuple-element.69), channel_id=1, source_target_pairs={{0,16},{1,17},{2,18},{3,19},{4,20},{5,21},{6,22},{7,23},{8,24},{9,... | collective-permute-start | bytes 1130504 | tf_op jit(solution)/shard_map/ppermute | solution.py:202
  67.4 5.0 %queries_part.1 = (f32[4,128,512]{2,1,0:T(8,128)S(1)}, f32[4,128,512]{2,1,0:T(8,128)S(1)}, bf16[4,128,512]{2,1,0:T(8,128)(2,1)S(1)}, bf16[4,128,512]{2,1,0:T(8,128)(2,1)S(1)}) custom-call(s32[5]{0:T(128)S(1)} %stack.41.where_ref, bf16[176,2048]{1,0:T(8,128)(2,1)S(1)} %pad_maximum_fusion.2.x0, bf16[176,2048]{1,0:T(8,128)(2,1)S(1)} %collective-permute-done.5.x1, ...), custom_call_target="tpu_custom_call" | custom-call | flops 5000000000 | bytes 4000000 | tf_op jit(solution)/shard_map/queries_part/pallas_call | solution.py:600
  72.4 0.2 collective-permute-start.13
  72.6 8.1 %collective-permute-done.19 = bf16[512,256]{1,0:T(8,128)(2,1)S(1)} collective-permute-done((bf16[512,256]{1,0:T(8,128)(2,1)S(1)}, bf16[512,256]{1,0:T(8,128)(2,1)S(1)}, u32[]{:S(2)}, u32[]{:S(2)}) %collective-permute-start.19) | collective-permute-done | bytes 262176 | tf_op jit(solution)/shard_map/ppermute | solution.py:202
  80.8 0.1 pad_maximum_fusion.1.refs_4_
  80.9 0.4 collective-permute-start.20
  81.3 7.3 %collective-permute-done.15.got_ref = bf16[736,256]{1,0:T(8,128)(2,1)S(1)} collective-permute-done((bf16[736,256]{1,0:T(8,128)(2,1)S(1)}, bf16[736,256]{1,0:T(8,128)(2,1)S(1)}, u32[]{:S(2)}, u32[]{:S(2)}) %collective-permute-start.15) | collective-permute-done | bytes 376864 | tf_op jit(solution)/shard_map/ppermute | solution.py:202
  88.6 1.0 keys_join.1.kv0
  89.6 0.3 collective-permute-start.16
  89.9 3.6 %collective-permute-start.12 = (bf16[4,128,512]{2,1,0:T(8,128)(2,1)S(1)}, bf16[4,128,512]{2,1,0:T(8,128)(2,1)S(1)}, u32[]{:S(2)}, u32[]{:S(2)}) collective-permute-start(bf16[4,128,512]{2,1,0:T(8,128)(2,1)S(1)} %get-tuple-element.65), channel_id=1, source_target_pairs={{0,8},{1,9},{2,10},{3,11},{4,12},{5,13},{6,14},{7,15},{8,0},{9,1},... | collective-permute-start | bytes 1572872 | tf_op jit(solution)/shard_map/ppermute | solution.py:202
  93.5 5.1 %collective-permute-done.13 = bf16[4,128,512]{2,1,0:T(8,128)(2,1)S(1)} collective-permute-done((bf16[4,128,512]{2,1,0:T(8,128)(2,1)S(1)}, bf16[4,128,512]{2,1,0:T(8,128)(2,1)S(1)}, u32[]{:S(2)}, u32[]{:S(2)}) %collective-permute-start.13) | collective-permute-done | bytes 524320 | tf_op jit(solution)/shard_map/ppermute | solution.py:202
  98.6 0.2 add_convert_fusion
  98.7 2.1 %collective-permute-start.14 = (bf16[4,128,512]{2,1,0:T(8,128)(2,1)S(1)}, bf16[4,128,512]{2,1,0:T(8,128)(2,1)S(1)}, u32[]{:S(2)}, u32[]{:S(2)}) collective-permute-start(bf16[4,128,512]{2,1,0:T(8,128)(2,1)S(1)} %add_convert_fusion), channel_id=1, source_target_pairs={{0,16},{1,17},{2,18},{3,19},{4,20},{5,21},{6,22},{7,23},{8,24},{9,... | collective-permute-start | bytes 1572872 | tf_op jit(solution)/shard_map/ppermute | solution.py:202
  100.9 0.8 collective-permute-start.18
  101.7 15.4 %collective-permute-done.17.kv2 = bf16[6,128,256]{2,1,0:T(8,128)(2,1)S(1)} collective-permute-done((bf16[6,128,256]{2,1,0:T(8,128)(2,1)S(1)}, bf16[6,128,256]{2,1,0:T(8,128)(2,1)S(1)}, u32[]{:S(2)}, u32[]{:S(2)}) %collective-permute-start.17) | collective-permute-done | bytes 393248 | tf_op jit(solution)/shard_map/ppermute | solution.py:202
  117.1 2.0 %collective-permute-start.24 = (bf16[2,1024,256]{2,1,0:T(8,128)(2,1)S(1)}, bf16[2,1024,256]{2,1,0:T(8,128)(2,1)S(1)}, u32[]{:S(2)}, u32[]{:S(2)}) collective-permute-start(bf16[2,1024,256]{2,1,0:T(8,128)(2,1)S(1)} %collective-permute-done.20.refs_5_), channel_id=1, source_target_pairs={{0,4},{1,3},{2,6},{3,1},{4,0},{5,7},{6,2},{7,5},{8,12},{9,11},{10,... | collective-permute-start | bytes 3145736 | tf_op jit(solution)/shard_map/ppermute | solution.py:202
  119.1 3.4 %collective-permute-done.14.got_ref = bf16[4,128,512]{2,1,0:T(8,128)(2,1)S(1)} collective-permute-done((bf16[4,128,512]{2,1,0:T(8,128)(2,1)S(1)}, bf16[4,128,512]{2,1,0:T(8,128)(2,1)S(1)}, u32[]{:S(2)}, u32[]{:S(2)}) %collective-permute-start.14) | collective-permute-done | bytes 524320 | tf_op jit(solution)/shard_map/ppermute | solution.py:202
  122.5 4.6 %attend.3.refs_1_ = bf16[512,256]{1,0:T(8,128)(2,1)S(1)} custom-call(s32[5]{0:T(128)S(1)} %stack.41.where_ref, f32[4,128,512]{2,1,0:T(8,128)S(1)} %get-tuple-element.64.keep_ref, bf16[4,128,512]{2,1,0:T(8,128)(2,1)S(1)} %collective-permute-done.12.near_ref, bf16[4,128,512]{2,1,0:T(8,128)(2,1)S(1)} %collective-permute-done.14.got_ref, ...), custom_call_target="tpu_custom_call" | custom-call | flops 4000000000 | bytes 4000000 | tf_op jit(solution)/shard_map/attend/pallas_call | solution.py:640
  127.1 1.5 collective-permute-start.22
  128.7 4.8 %attend.2.refs_0_ = bf16[512,256]{1,0:T(8,128)(2,1)S(1)} custom-call(s32[5]{0:T(128)S(1)} %stack.41.where_ref, f32[4,128,512]{2,1,0:T(8,128)S(1)} %get-tuple-element.64.keep_ref, bf16[4,128,512]{2,1,0:T(8,128)(2,1)S(1)} %collective-permute-done.12.near_ref, bf16[4,128,512]{2,1,0:T(8,128)(2,1)S(1)} %collective-permute-done.14.got_ref, ...), custom_call_target="tpu_custom_call" | custom-call | flops 4000000000 | bytes 4000000 | tf_op jit(solution)/shard_map/attend/pallas_call | solution.py:640
  133.5 0.6 collective-permute-start.21
  134.1 0.1 collective-permute-done.22.refs_3_
  134.3 5.7 %collective-permute-done.21.refs_2_ = bf16[512,256]{1,0:T(8,128)(2,1)S(1)} collective-permute-done((bf16[512,256]{1,0:T(8,128)(2,1)S(1)}, bf16[512,256]{1,0:T(8,128)(2,1)S(1)}, u32[]{:S(2)}, u32[]{:S(2)}) %collective-permute-start.21) | collective-permute-done | bytes 262176 | tf_op jit(solution)/shard_map/ppermute | solution.py:202
  140.0 3.2 %collective-permute-done.24.refs_7_ = bf16[2,1024,256]{2,1,0:T(8,128)(2,1)S(1)} collective-permute-done((bf16[2,1024,256]{2,1,0:T(8,128)(2,1)S(1)}, bf16[2,1024,256]{2,1,0:T(8,128)(2,1)S(1)}, u32[]{:S(2)}, u32[]{:S(2)}) %collective-permute-start.24) | collective-permute-done | bytes 1048608 | tf_op jit(solution)/shard_map/ppermute | solution.py:202
  143.1 1.0 copy-done.7
  144.1 3.9 %output.1 = (f32[4,128,1024]{2,1,0:T(8,128)}, bf16[4,128,1024]{2,1,0:T(8,128)(2,1)S(1)}) custom-call(s32[5]{0:T(128)S(1)} %stack.41.where_ref, bf16[512,256]{1,0:T(8,128)(2,1)S(1)} %attend.2.refs_0_, bf16[512,256]{1,0:T(8,128)(2,1)S(1)} %attend.3.refs_1_, bf16[512,256]{1,0:T(8,128)(2,1)S(1)} %collective-permute-done.21.refs_2_, ...), custom_call_target="tpu_custom_call" | custom-call | flops 5000000000 | bytes 4000000 | tf_op jit(solution)/shard_map/output/pallas_call | solution.py:657
  148.0 2.7 %collective-permute-done.25 = bf16[4,128,1024]{2,1,0:T(8,128)(2,1)S(1)} collective-permute-done((bf16[4,128,1024]{2,1,0:T(8,128)(2,1)S(1)}, bf16[4,128,1024]{2,1,0:T(8,128)(2,1)S(1)}, u32[]{:S(2)}, u32[]{:S(2)}) %collective-permute-start.25) | collective-permute-done | bytes 1048608 | tf_op jit(solution)/shard_map/ppermute | solution.py:202
  150.7 1.9 %fusion.8 = (bf16[128,1024]{1,0:T(8,128)(2,1)S(1)}, bf16[128,1024]{1,0:T(8,128)(2,1)S(1)}, bf16[128,1024]{1,0:T(8,128)(2,1)S(1)}, f32[128,1024]{1,0:T(8,128)S(1)}) fusion(f32[4,128,1024]{2,1,0:T(8,128)} %get-tuple-element.77, bf16[4,128,1024]{2,1,0:T(8,128)(2,1)S(1)} %collective-permute-done.25), kind=kLoop, calls=%fused_computation.29 | loop fusion | flops 1441792 | bytes 4456448 | tf_op jit(solution)/shard_map/convert_element_type | solution.py:674
  152.5 1.5 collective-permute-start.26
  154.0 1.4 collective-permute-start.27
  155.4 0.1 collective-permute-start.28
  155.6 16.2 %collective-permute-done.26.first = bf16[128,1024]{1,0:T(8,128)(2,1)S(1)} collective-permute-done((bf16[128,1024]{1,0:T(8,128)(2,1)S(1)}, bf16[128,1024]{1,0:T(8,128)(2,1)S(1)}, u32[]{:S(2)}, u32[]{:S(2)}) %collective-permute-start.26) | collective-permute-done | bytes 262176 | tf_op jit(solution)/shard_map/ppermute | solution.py:202
  171.8 5.0 %collective-permute-done.27.second = bf16[128,1024]{1,0:T(8,128)(2,1)S(1)} collective-permute-done((bf16[128,1024]{1,0:T(8,128)(2,1)S(1)}, bf16[128,1024]{1,0:T(8,128)(2,1)S(1)}, u32[]{:S(2)}, u32[]{:S(2)}) %collective-permute-start.27) | collective-permute-done | bytes 262176 | tf_op jit(solution)/shard_map/ppermute | solution.py:202
  176.7 1.9 %collective-permute-done.28.third = bf16[128,1024]{1,0:T(8,128)(2,1)S(1)} collective-permute-done((bf16[128,1024]{1,0:T(8,128)(2,1)S(1)}, bf16[128,1024]{1,0:T(8,128)(2,1)S(1)}, u32[]{:S(2)}, u32[]{:S(2)}) %collective-permute-start.28) | collective-permute-done | bytes 262176 | tf_op jit(solution)/shard_map/ppermute | solution.py:202
  178.7 1.4 finish.1
  (56 shorter events, 0.8 us)
Async XLA Ops:
  0.0 10.2 %copy-start.5 = (bf16[32,2048]{1,0:T(8,128)(2,1)S(1)}, bf16[32,2048]{1,0:T(8,128)(2,1)}, u32[]{:S(2)}) copy-start(bf16[32,2048]{1,0:T(8,128)(2,1)} %param.13) | copy-start | bytes 393220
  0.0 10.4 %copy-start.8 = (s32[8]{0:T(128)S(1)}, s32[8]{0:T(128)}, u32[]{:S(2)}) copy-start(s32[8]{0:T(128)} %param.22) | copy-start | bytes 100
  0.0 10.6 %copy-start = (bf16[256,512]{1,0:T(8,128)(2,1)S(1)}, bf16[256,512]{1,0:T(8,128)(2,1)}, u32[]{:S(2)}) copy-start(bf16[256,512]{1,0:T(8,128)(2,1)} %refs_0_.2) | copy-start | bytes 786436
  0.0 10.6 %copy-start.1 = (bf16[256,512]{1,0:T(8,128)(2,1)S(1)}, bf16[256,512]{1,0:T(8,128)(2,1)}, u32[]{:S(2)}) copy-start(bf16[256,512]{1,0:T(8,128)(2,1)} %refs_1_.1) | copy-start | bytes 786436
  0.0 10.6 %copy-start.2 = (bf16[64,512]{1,0:T(8,128)(2,1)S(1)}, bf16[64,512]{1,0:T(8,128)(2,1)}, u32[]{:S(2)}) copy-start(bf16[64,512]{1,0:T(8,128)(2,1)} %refs_2_.1) | copy-start | bytes 196612
  0.0 10.6 %copy-start.3 = (bf16[64,512]{1,0:T(8,128)(2,1)S(1)}, bf16[64,512]{1,0:T(8,128)(2,1)}, u32[]{:S(2)}) copy-start(bf16[64,512]{1,0:T(8,128)(2,1)} %refs_3_.1) | copy-start | bytes 196612
  0.0 26.3 %collective-permute-start.3 = (bf16[256,2048]{1,0:T(8,128)(2,1)}, bf16[256,2048]{1,0:T(8,128)(2,1)}, u32[]{:S(2)}, u32[]{:S(2)}) collective-permute-start(bf16[256,2048]{1,0:T(8,128)(2,1)} %refs_0_.3), channel_id=1, source_target_pairs={{0,2},{1,5},{2,0},{3,7},{4,6},{5,1},{6,4},{7,3},{8,10},{9,13},{10,... | collective-permute-start | bytes 3145736 | tf_op jit(solution)/shard_map/ppermute | solution.py:202
  1.6 26.5 %collective-permute-start.4 = (bf16[256,2048]{1,0:T(8,128)(2,1)}, bf16[256,2048]{1,0:T(8,128)(2,1)}, u32[]{:S(2)}, u32[]{:S(2)}) collective-permute-start(bf16[256,2048]{1,0:T(8,128)(2,1)} %refs_0_.3), channel_id=1, source_target_pairs={{0,4},{1,3},{2,6},{3,1},{4,0},{5,7},{6,2},{7,5},{8,12},{9,11},{10,... | collective-permute-start | bytes 3145736 | tf_op jit(solution)/shard_map/ppermute | solution.py:202
  10.6 6.4 %copy-start.4 = (bf16[2048,256]{1,0:T(8,128)(2,1)S(1)}, bf16[2048,256]{1,0:T(8,128)(2,1)}, u32[]{:S(2)}) copy-start(bf16[2048,256]{1,0:T(8,128)(2,1)} %param.18) | copy-start | bytes 3145732
  11.6 13.8 %collective-permute-start.2 = (bf16[336,512]{1,0:T(8,128)(2,1)S(1)}, bf16[336,512]{1,0:T(8,128)(2,1)S(1)}, u32[]{:S(2)}, u32[]{:S(2)}) collective-permute-start(bf16[336,512]{1,0:T(8,128)(2,1)S(1)} %get-tuple-element.45), channel_id=1, source_target_pairs={{0,8},{1,9},{2,10},{3,11},{4,12},{5,13},{6,14},{7,15},{8,0},{9,1},... | collective-permute-start | bytes 1032200 | tf_op jit(solution)/shard_map/ppermute | solution.py:202
  12.1 13.3 %collective-permute-start.1 = (bf16[32,2048]{1,0:T(8,128)(2,1)S(1)}, bf16[32,2048]{1,0:T(8,128)(2,1)S(1)}, u32[]{:S(2)}, u32[]{:S(2)}) collective-permute-start(bf16[32,2048]{1,0:T(8,128)(2,1)S(1)} %fusion.5), channel_id=1, source_target_pairs={{0,0},{1,16},{2,1},{3,17},{4,8},{5,24},{6,9},{7,25},{8,2},{9,18},{... | collective-permute-start | bytes 393224 | tf_op jit(solution)/shard_map/ppermute | solution.py:202
  15.5 15.3 %collective-permute-start = (bf16[144,2048]{1,0:T(8,128)(2,1)S(1)}, bf16[144,2048]{1,0:T(8,128)(2,1)}, u32[]{:S(2)}, u32[]{:S(2)}) collective-permute-start(bf16[144,2048]{1,0:T(8,128)(2,1)S(1)} %fusion.2), channel_id=1, source_target_pairs={{1,16},{3,18},{5,20},{7,22},{9,24},{11,26},{13,28},{15,30},{16,1},... | collective-permute-start | bytes 1769480 | tf_op jit(solution)/shard_map/ppermute | solution.py:202
  28.2 11.6 %collective-permute-start.10 = (bf16[2,256,512]{2,1,0:T(8,128)(2,1)S(1)}, bf16[2,256,512]{2,1,0:T(8,128)(2,1)S(1)}, u32[]{:S(2)}, u32[]{:S(2)}) collective-permute-start(bf16[2,256,512]{2,1,0:T(8,128)(2,1)S(1)} %pad_maximum_fusion.3.own), channel_id=1, source_target_pairs={{0,2},{1,5},{2,0},{3,7},{4,6},{5,1},{6,4},{7,3},{8,10},{9,13},{10,... | collective-permute-start | bytes 1572872 | tf_op jit(solution)/shard_map/ppermute | solution.py:202
  30.9 24.8 %collective-permute-start.7 = (bf16[256,2048]{1,0:T(8,128)(2,1)}, bf16[256,2048]{1,0:T(8,128)(2,1)S(1)}, u32[]{:S(2)}, u32[]{:S(2)}) collective-permute-start(bf16[256,2048]{1,0:T(8,128)(2,1)} %collective-permute-done.3.refs_1_), channel_id=1, source_target_pairs={{0,4},{1,3},{2,6},{3,1},{4,0},{5,7},{6,2},{7,5},{8,12},{9,11},{10,... | collective-permute-start | bytes 3145736 | tf_op jit(solution)/shard_map/ppermute | solution.py:202
  31.1 24.6 %collective-permute-start.5 = (bf16[176,2048]{1,0:T(8,128)(2,1)S(1)}, bf16[176,2048]{1,0:T(8,128)(2,1)S(1)}, u32[]{:S(2)}, u32[]{:S(2)}) collective-permute-start(bf16[176,2048]{1,0:T(8,128)(2,1)S(1)} %pad_maximum_fusion.2.x0), channel_id=1, source_target_pairs={{0,8},{1,9},{2,10},{3,11},{4,12},{5,13},{6,14},{7,15},{8,0},{9,1},... | collective-permute-start | bytes 2162696 | tf_op jit(solution)/shard_map/ppermute | solution.py:202
  32.0 23.6 %collective-permute-start.6 = (bf16[512,256]{1,0:T(8,128)(2,1)S(1)}, bf16[512,256]{1,0:T(8,128)(2,1)S(1)}, u32[]{:S(2)}, u32[]{:S(2)}) collective-permute-start(bf16[512,256]{1,0:T(8,128)(2,1)S(1)} %get-tuple-element.88), channel_id=1, source_target_pairs={{0,16},{1,17},{2,18},{3,19},{4,20},{5,21},{6,22},{7,23},{8,24},{9,... | collective-permute-start | bytes 786440 | tf_op jit(solution)/shard_map/ppermute | solution.py:202
  39.9 20.6 %collective-permute-start.11 = (bf16[4,256,512]{2,1,0:T(8,128)(2,1)S(1)}, bf16[4,256,512]{2,1,0:T(8,128)(2,1)S(1)}, u32[]{:S(2)}, u32[]{:S(2)}) collective-permute-start(bf16[4,256,512]{2,1,0:T(8,128)(2,1)S(1)} %pad_maximum_fusion), channel_id=1, source_target_pairs={{0,4},{1,3},{2,6},{3,1},{4,0},{5,7},{6,2},{7,5},{8,12},{9,11},{10,... | collective-permute-start | bytes 3145736 | tf_op jit(solution)/shard_map/ppermute | solution.py:202
  41.7 18.8 %collective-permute-start.9 = (bf16[176,2048]{1,0:T(8,128)(2,1)S(1)}, bf16[176,2048]{1,0:T(8,128)(2,1)S(1)}, u32[]{:S(2)}, u32[]{:S(2)}) collective-permute-start(bf16[176,2048]{1,0:T(8,128)(2,1)S(1)} %pad_maximum_fusion.2.x0), channel_id=1, source_target_pairs={{0,1},{1,0},{2,3},{3,2},{4,5},{5,4},{6,7},{7,6},{8,9},{9,8},{10,11... | collective-permute-start | bytes 2162696 | tf_op jit(solution)/shard_map/ppermute | solution.py:202
  55.7 3.2 %copy-start.6 = (bf16[256,2048]{1,0:T(8,128)(2,1)}, bf16[256,2048]{1,0:T(8,128)(2,1)S(1)}, u32[]{:S(2)}) copy-start(bf16[256,2048]{1,0:T(8,128)(2,1)S(1)} %collective-permute-done.7.refs_3_) | copy-start | bytes 3145732
  55.7 4.8 %collective-permute-start.8 = (bf16[176,2048]{1,0:T(8,128)(2,1)S(1)}, bf16[176,2048]{1,0:T(8,128)(2,1)S(1)}, u32[]{:S(2)}, u32[]{:S(2)}) collective-permute-start(bf16[176,2048]{1,0:T(8,128)(2,1)S(1)} %collective-permute-done.5.x1), channel_id=1, source_target_pairs={{0,1},{1,0},{2,3},{3,2},{4,5},{5,4},{6,7},{7,6},{8,9},{9,8},{10,11... | collective-permute-start | bytes 2162696 | tf_op jit(solution)/shard_map/ppermute | solution.py:202
  58.9 21.8 %collective-permute-start.19 = (bf16[512,256]{1,0:T(8,128)(2,1)S(1)}, bf16[512,256]{1,0:T(8,128)(2,1)S(1)}, u32[]{:S(2)}, u32[]{:S(2)}) collective-permute-start(bf16[512,256]{1,0:T(8,128)(2,1)S(1)} %get-tuple-element.87), channel_id=1, source_target_pairs={{0,16},{1,17},{2,18},{3,19},{4,20},{5,21},{6,22},{7,23},{8,24},{9,... | collective-permute-start | bytes 786440 | tf_op jit(solution)/shard_map/ppermute | solution.py:202
  62.7 25.9 %collective-permute-start.15 = (bf16[736,256]{1,0:T(8,128)(2,1)S(1)}, bf16[736,256]{1,0:T(8,128)(2,1)S(1)}, u32[]{:S(2)}, u32[]{:S(2)}) collective-permute-start(bf16[736,256]{1,0:T(8,128)(2,1)S(1)} %get-tuple-element.69), channel_id=1, source_target_pairs={{0,16},{1,17},{2,18},{3,19},{4,20},{5,21},{6,22},{7,23},{8,24},{9,... | collective-permute-start | bytes 1130504 | tf_op jit(solution)/shard_map/ppermute | solution.py:202
  72.4 26.2 %collective-permute-start.13 = (bf16[4,128,512]{2,1,0:T(8,128)(2,1)S(1)}, bf16[4,128,512]{2,1,0:T(8,128)(2,1)S(1)}, u32[]{:S(2)}, u32[]{:S(2)}) collective-permute-start(bf16[4,128,512]{2,1,0:T(8,128)(2,1)S(1)} %get-tuple-element.67), channel_id=1, source_target_pairs={{0,8},{1,9},{2,10},{3,11},{4,12},{5,13},{6,14},{7,15},{8,0},{9,1},... | collective-permute-start | bytes 1572872 | tf_op jit(solution)/shard_map/ppermute | solution.py:202
  80.9 36.2 %collective-permute-start.20 = (bf16[2,1024,256]{2,1,0:T(8,128)(2,1)S(1)}, bf16[2,1024,256]{2,1,0:T(8,128)(2,1)S(1)}, u32[]{:S(2)}, u32[]{:S(2)}) collective-permute-start(bf16[2,1024,256]{2,1,0:T(8,128)(2,1)S(1)} %pad_maximum_fusion.1.refs_4_), channel_id=1, source_target_pairs={{0,2},{1,5},{2,0},{3,7},{4,6},{5,1},{6,4},{7,3},{8,10},{9,13},{10,... | collective-permute-start | bytes 3145736 | tf_op jit(solution)/shard_map/ppermute | solution.py:202
  89.6 11.3 %collective-permute-start.16 = (bf16[6,128,256]{2,1,0:T(8,128)(2,1)S(1)}, bf16[6,128,256]{2,1,0:T(8,128)(2,1)S(1)}, u32[]{:S(2)}, u32[]{:S(2)}) collective-permute-start(bf16[6,128,256]{2,1,0:T(8,128)(2,1)S(1)} %keys_join.1.kv0), channel_id=1, source_target_pairs={{0,2},{1,5},{2,0},{3,7},{4,6},{5,1},{6,4},{7,3},{8,10},{9,13},{10,... | collective-permute-start | bytes 1179656 | tf_op jit(solution)/shard_map/ppermute | solution.py:202
  89.9 29.2 %collective-permute-start.12 = (bf16[4,128,512]{2,1,0:T(8,128)(2,1)S(1)}, bf16[4,128,512]{2,1,0:T(8,128)(2,1)S(1)}, u32[]{:S(2)}, u32[]{:S(2)}) collective-permute-start(bf16[4,128,512]{2,1,0:T(8,128)(2,1)S(1)} %get-tuple-element.65), channel_id=1, source_target_pairs={{0,8},{1,9},{2,10},{3,11},{4,12},{5,13},{6,14},{7,15},{8,0},{9,1},... | collective-permute-start | bytes 1572872 | tf_op jit(solution)/shard_map/ppermute | solution.py:202
  98.7 23.8 %collective-permute-start.14 = (bf16[4,128,512]{2,1,0:T(8,128)(2,1)S(1)}, bf16[4,128,512]{2,1,0:T(8,128)(2,1)S(1)}, u32[]{:S(2)}, u32[]{:S(2)}) collective-permute-start(bf16[4,128,512]{2,1,0:T(8,128)(2,1)S(1)} %add_convert_fusion), channel_id=1, source_target_pairs={{0,16},{1,17},{2,18},{3,19},{4,20},{5,21},{6,22},{7,23},{8,24},{9,... | collective-permute-start | bytes 1572872 | tf_op jit(solution)/shard_map/ppermute | solution.py:202
  100.9 16.2 %collective-permute-start.17 = (bf16[6,128,256]{2,1,0:T(8,128)(2,1)S(1)}, bf16[6,128,256]{2,1,0:T(8,128)(2,1)S(1)}, u32[]{:S(2)}, u32[]{:S(2)}) collective-permute-start(bf16[6,128,256]{2,1,0:T(8,128)(2,1)S(1)} %keys_join.1.kv0), channel_id=1, source_target_pairs={{0,4},{1,3},{2,6},{3,1},{4,0},{5,7},{6,2},{7,5},{8,12},{9,11},{10,... | collective-permute-start | bytes 1179656 | tf_op jit(solution)/shard_map/ppermute | solution.py:202
  100.9 16.2 %collective-permute-start.18 = (bf16[6,128,256]{2,1,0:T(8,128)(2,1)S(1)}, bf16[6,128,256]{2,1,0:T(8,128)(2,1)S(1)}, u32[]{:S(2)}, u32[]{:S(2)}) collective-permute-start(bf16[6,128,256]{2,1,0:T(8,128)(2,1)S(1)} %keys_join.1.kv0), channel_id=1, source_target_pairs={{0,6},{1,7},{2,4},{3,5},{4,2},{5,3},{6,0},{7,1},{8,14},{9,15},{10,... | collective-permute-start | bytes 1179656 | tf_op jit(solution)/shard_map/ppermute | solution.py:202
  117.1 22.9 %collective-permute-start.23 = (bf16[2,1024,256]{2,1,0:T(8,128)(2,1)S(1)}, bf16[2,1024,256]{2,1,0:T(8,128)(2,1)S(1)}, u32[]{:S(2)}, u32[]{:S(2)}) collective-permute-start(bf16[2,1024,256]{2,1,0:T(8,128)(2,1)S(1)} %pad_maximum_fusion.1.refs_4_), channel_id=1, source_target_pairs={{0,4},{1,3},{2,6},{3,1},{4,0},{5,7},{6,2},{7,5},{8,12},{9,11},{10,... | collective-permute-start | bytes 3145736 | tf_op jit(solution)/shard_map/ppermute | solution.py:202
  117.1 26.0 %collective-permute-start.24 = (bf16[2,1024,256]{2,1,0:T(8,128)(2,1)S(1)}, bf16[2,1024,256]{2,1,0:T(8,128)(2,1)S(1)}, u32[]{:S(2)}, u32[]{:S(2)}) collective-permute-start(bf16[2,1024,256]{2,1,0:T(8,128)(2,1)S(1)} %collective-permute-done.20.refs_5_), channel_id=1, source_target_pairs={{0,4},{1,3},{2,6},{3,1},{4,0},{5,7},{6,2},{7,5},{8,12},{9,11},{10,... | collective-permute-start | bytes 3145736 | tf_op jit(solution)/shard_map/ppermute | solution.py:202
  127.1 7.1 %collective-permute-start.22 = (bf16[512,256]{1,0:T(8,128)(2,1)S(1)}, bf16[512,256]{1,0:T(8,128)(2,1)S(1)}, u32[]{:S(2)}, u32[]{:S(2)}) collective-permute-start(bf16[512,256]{1,0:T(8,128)(2,1)S(1)} %attend.3.refs_1_), channel_id=1, source_target_pairs={{0,8},{1,9},{2,10},{3,11},{4,12},{5,13},{6,14},{7,15},{8,0},{9,1},... | collective-permute-start | bytes 786440 | tf_op jit(solution)/shard_map/ppermute | solution.py:202
  133.5 6.4 %collective-permute-start.21 = (bf16[512,256]{1,0:T(8,128)(2,1)S(1)}, bf16[512,256]{1,0:T(8,128)(2,1)S(1)}, u32[]{:S(2)}, u32[]{:S(2)}) collective-permute-start(bf16[512,256]{1,0:T(8,128)(2,1)S(1)} %attend.2.refs_0_), channel_id=1, source_target_pairs={{0,8},{1,9},{2,10},{3,11},{4,12},{5,13},{6,14},{7,15},{8,0},{9,1},... | collective-permute-start | bytes 786440 | tf_op jit(solution)/shard_map/ppermute | solution.py:202
  143.1 1.0 copy-start.7
  148.0 2.7 %collective-permute-start.25 = (bf16[4,128,1024]{2,1,0:T(8,128)(2,1)S(1)}, bf16[4,128,1024]{2,1,0:T(8,128)(2,1)S(1)}, u32[]{:S(2)}, u32[]{:S(2)}) collective-permute-start(bf16[4,128,1024]{2,1,0:T(8,128)(2,1)S(1)} %get-tuple-element.78), channel_id=1, source_target_pairs={{0,1},{1,0},{2,3},{3,2},{4,5},{5,4},{6,7},{7,6},{8,9},{9,8},{10,11... | collective-permute-start | bytes 3145736 | tf_op jit(solution)/shard_map/ppermute | solution.py:202
  152.5 19.2 %collective-permute-start.26 = (bf16[128,1024]{1,0:T(8,128)(2,1)S(1)}, bf16[128,1024]{1,0:T(8,128)(2,1)S(1)}, u32[]{:S(2)}, u32[]{:S(2)}) collective-permute-start(bf16[128,1024]{1,0:T(8,128)(2,1)S(1)} %get-tuple-element.83), channel_id=1, source_target_pairs={{0,8},{1,9},{2,10},{3,11},{4,12},{5,13},{6,14},{7,15},{8,16},{9,17... | collective-permute-start | bytes 786440 | tf_op jit(solution)/shard_map/ppermute | solution.py:202
  154.0 22.7 %collective-permute-start.27 = (bf16[128,1024]{1,0:T(8,128)(2,1)S(1)}, bf16[128,1024]{1,0:T(8,128)(2,1)S(1)}, u32[]{:S(2)}, u32[]{:S(2)}) collective-permute-start(bf16[128,1024]{1,0:T(8,128)(2,1)S(1)} %get-tuple-element.82), channel_id=1, source_target_pairs={{0,16},{1,17},{2,18},{3,19},{4,20},{5,21},{6,22},{7,23},{8,24},{9,... | collective-permute-start | bytes 786440 | tf_op jit(solution)/shard_map/ppermute | solution.py:202
  155.4 23.2 %collective-permute-start.28 = (bf16[128,1024]{1,0:T(8,128)(2,1)S(1)}, bf16[128,1024]{1,0:T(8,128)(2,1)S(1)}, u32[]{:S(2)}, u32[]{:S(2)}) collective-permute-start(bf16[128,1024]{1,0:T(8,128)(2,1)S(1)} %get-tuple-element.81), channel_id=1, source_target_pairs={{0,24},{1,25},{2,26},{3,27},{4,28},{5,29},{6,30},{7,31},{8,0},{9,1... | collective-permute-start | bytes 786440 | tf_op jit(solution)/shard_map/ppermute | solution.py:202

commit v17 on v16

--- a/solution.py
+++ b/solution.py
@@ -555,11 +555,11 @@
     held = jnp.concatenate([jnp.where(own_first, normed, crossed), shown], axis=0)
     next_rows = across(held, 1)
     held_other = other_core(held)
-    out_half = out_rows // 2
+    out_first = out_rows * 3 // 4
     next_rows, out_got0, query_both = lax.optimization_barrier(
-        (next_rows, across(out_give[:out_half], 2), query_both)
-    )
-    out_got1 = across(out_give[out_half:], 2)
+        (next_rows, across(out_give[:out_first], 2), query_both)
+    )
+    out_got1 = across(out_give[out_first:], 2)
     next_other = other_core(next_rows)
     keys_far = to_far(jnp.concatenate([keys, keys_near], axis=0))
     next_other, held_other, keys_far = lax.optimization_barrier(

time: 181 us -> 179 us (0.989)
  waiting for transfers between devices: 99 us -> 84 us
  starting transfers between devices: 43.9 us -> 54.3 us
    ppermute x29, waiting for transfers between devices: 99 us -> 84 us  [permuted(): return lax.ppermute(value, ('seq', 'head'), perm)]
    ppermute x29, starting transfers between devices: 43.9 us -> 54.3 us  [permuted(): return lax.ppermute(value, ('seq', 'head'), perm)]
  transfers between devices with their start and end apart: 29 -> 29, of which waited for: 16 -> 18; matrix products, arithmetic and copies ran while one was open for 4% -> 5% of each run, Pallas kernels for 10% -> 10%
where the time goes in v17:
time: 179 us; the launch traced here: 177 us
  waiting for transfers between devices  84 us (47%)
  starting transfers between devices  54.3 us (30%)
  Pallas kernels  23.8 us (13%)
  other arithmetic  9.89 us (6%)
  blocking collectives  2.46 us (1%)
  local copies, waits for them, and re-layouts  2.29 us (1%)
    ppermute x29, waiting for transfers between devices, permuted(): return lax.ppermute(value, ('seq', 'head'), perm)  84 us
    ppermute x29, starting transfers between devices, permuted(): return lax.ppermute(value, ('seq', 'head'), perm)  54.3 us
    pallas_call x2, Pallas kernels, by_levels(): pl.pallas_call(functools.partial(attend_kernel, pair), out_shape=shaped((...  9.46 us
    pallas_call x1, Pallas kernels, by_levels(): pl.pallas_call(queries_part_kernel, out_shape=(shaped(group_shape, jnp.fl...  4.99 us
    pallas_call x1, Pallas kernels, by_levels(): pl.pallas_call(output_kernel, out_shape=(shaped((LEVELS, tok, wide_cols),...  3.89 us
  transfers between devices with their start and end apart: 29, of which 18 were waited for; matrix products, arithmetic and copies ran while one was open for 5% of the time, Pallas kernels for 10%

profile of v17, /device:TPU:8, one launch (start us, length us, event | category | flops | bytes accessed | tf_op | source)
XLA Modules:
  0.0 177.1 jit_solution(10664863364299187287)
XLA Ops:
  0.0 1.6 collective-permute-start.3
  1.6 1.5 collective-permute-start.4
  3.1 1.0 fusion.3
  4.2 1.4 fusion
  5.6 2.5 %all-reduce.1 = (f32[144]{0:T(256)S(1)}, f32[32]{0:T(128)S(1)}) all-reduce(f32[144]{0:T(256)S(1)} %fusion, f32[32]{0:T(128)S(1)} %fusion.3), channel_id=1, replica_groups=mesh['seq'=16,'head'=2] {'head'}, use_global_device_ids=true, to_apply=%region_1.2 | all-reduce | flops 176 | bytes 1408 | tf_op jit(solution)/shard_map/psum | solution.py:518
  8.1 0.7 dynamic_slice.9
  8.8 1.0 fusion.5
  9.8 1.2 fusion.2
  11.1 2.3 %collective-permute-start.1 = (bf16[32,2048]{1,0:T(8,128)(2,1)S(1)}, bf16[32,2048]{1,0:T(8,128)(2,1)}, u32[]{:S(2)}, u32[]{:S(2)}) collective-permute-start(bf16[32,2048]{1,0:T(8,128)(2,1)S(1)} %fusion.5), channel_id=1, source_target_pairs={{0,0},{1,16},{2,1},{3,17},{4,8},{5,24},{6,9},{7,25},{8,2},{9,18},{... | collective-permute-start | bytes 393224 | tf_op jit(solution)/shard_map/ppermute | solution.py:202
  13.4 1.5 collective-permute-start
  15.0 0.9 pack.1
  16.0 0.2 copy-done.5
  16.3 3.4 %collective-permute-done.1 = bf16[32,2048]{1,0:T(8,128)(2,1)} collective-permute-done((bf16[32,2048]{1,0:T(8,128)(2,1)S(1)}, bf16[32,2048]{1,0:T(8,128)(2,1)}, u32[]{:S(2)}, u32[]{:S(2)}) %collective-permute-start.1) | collective-permute-done | bytes 131104 | tf_op jit(solution)/shard_map/ppermute | solution.py:202
  19.7 8.3 %collective-permute-done.2 = bf16[336,512]{1,0:T(8,128)(2,1)S(1)} collective-permute-done((bf16[336,512]{1,0:T(8,128)(2,1)S(1)}, bf16[336,512]{1,0:T(8,128)(2,1)S(1)}, u32[]{:S(2)}, u32[]{:S(2)}) %collective-permute-start.2) | collective-permute-done | bytes 344096 | tf_op jit(solution)/shard_map/ppermute | solution.py:202
  28.0 0.1 collective-permute-done.4.refs_2_
  28.2 2.8 %collective-permute-start.10 = (bf16[2,256,512]{2,1,0:T(8,128)(2,1)S(1)}, bf16[2,256,512]{2,1,0:T(8,128)(2,1)S(1)}, u32[]{:S(2)}, u32[]{:S(2)}) collective-permute-start(bf16[2,256,512]{2,1,0:T(8,128)(2,1)S(1)} %pad_maximum_fusion.3.own), channel_id=1, source_target_pairs={{0,2},{1,5},{2,0},{3,7},{4,6},{5,1},{6,4},{7,3},{8,10},{9,13},{10,... | collective-permute-start | bytes 1572872 | tf_op jit(solution)/shard_map/ppermute | solution.py:202
  31.1 1.0 pad_maximum_fusion.2.x0
  32.0 1.3 collective-permute-start.5
  33.3 7.5 %collective-permute-start.6 = (bf16[768,256]{1,0:T(8,128)(2,1)S(1)}, bf16[768,256]{1,0:T(8,128)(2,1)S(1)}, u32[]{:S(2)}, u32[]{:S(2)}) collective-permute-start(bf16[768,256]{1,0:T(8,128)(2,1)S(1)} %slice.42), channel_id=1, source_target_pairs={{0,16},{1,17},{2,18},{3,19},{4,20},{5,21},{6,22},{7,23},{8,24},{9,... | collective-permute-start | bytes 1179656 | tf_op jit(solution)/shard_map/ppermute | solution.py:202
  40.8 0.1 pad_maximum_fusion
  40.9 0.4 collective-permute-start.11
  41.5 6.9 %collective-permute-start.9 = (bf16[176,2048]{1,0:T(8,128)(2,1)S(1)}, bf16[176,2048]{1,0:T(8,128)(2,1)S(1)}, u32[]{:S(2)}, u32[]{:S(2)}) collective-permute-start(bf16[176,2048]{1,0:T(8,128)(2,1)S(1)} %pad_maximum_fusion.2.x0), channel_id=1, source_target_pairs={{0,1},{1,0},{2,3},{3,2},{4,5},{5,4},{6,7},{7,6},{8,9},{9,8},{10,11... | collective-permute-start | bytes 2162696 | tf_op jit(solution)/shard_map/ppermute | solution.py:202
  48.4 11.8 %collective-permute-done.6 = bf16[768,256]{1,0:T(8,128)(2,1)S(1)} collective-permute-done((bf16[768,256]{1,0:T(8,128)(2,1)S(1)}, bf16[768,256]{1,0:T(8,128)(2,1)S(1)}, u32[]{:S(2)}, u32[]{:S(2)}) %collective-permute-start.6) | collective-permute-done | bytes 393248 | tf_op jit(solution)/shard_map/ppermute | solution.py:202
  60.3 1.4 fusion.9
  61.7 0.2 pad_maximum_fusion.4.cos_ref
  61.9 0.2 pad_maximum_fusion.5.sin_ref
  62.1 1.7 collective-permute-start.19
  63.9 2.1 %keys_part.1 = (f32[576,256]{1,0:T(8,128)S(1)}, bf16[736,256]{1,0:T(8,128)(2,1)S(1)}) custom-call(s32[5]{0:T(128)S(1)} %stack.41.where_ref, bf16[176,2048]{1,0:T(8,128)(2,1)S(1)} %pad_maximum_fusion.2.x0, bf16[176,2048]{1,0:T(8,128)(2,1)S(1)} %collective-permute-done.5.x1, bf16[176,2048]{1,0:T(8,128)(2,1)S(1)} %collective-permute-done.9.x2, ...), custom_call_target="tpu_custom_call" | custom-call | flops 3000000000 | bytes 4000000 | tf_op jit(solution)/shard_map/keys_part/pallas_call | solution.py:583
  66.0 1.6 collective-permute-start.15
  67.5 5.0 %queries_part.1 = (f32[4,128,512]{2,1,0:T(8,128)S(1)}, f32[4,128,512]{2,1,0:T(8,128)S(1)}, bf16[4,128,512]{2,1,0:T(8,128)(2,1)S(1)}, bf16[4,128,512]{2,1,0:T(8,128)(2,1)S(1)}) custom-call(s32[5]{0:T(128)S(1)} %stack.41.where_ref, bf16[176,2048]{1,0:T(8,128)(2,1)S(1)} %pad_maximum_fusion.2.x0, bf16[176,2048]{1,0:T(8,128)(2,1)S(1)} %collective-permute-done.5.x1, ...), custom_call_target="tpu_custom_call" | custom-call | flops 5000000000 | bytes 4000000 | tf_op jit(solution)/shard_map/queries_part/pallas_call | solution.py:600
  72.5 0.4 collective-permute-start.13
  72.9 4.7 %collective-permute-done.19 = bf16[256,256]{1,0:T(8,128)(2,1)S(1)} collective-permute-done((bf16[256,256]{1,0:T(8,128)(2,1)S(1)}, bf16[256,256]{1,0:T(8,128)(2,1)S(1)}, u32[]{:S(2)}, u32[]{:S(2)}) %collective-permute-start.19) | collective-permute-done | bytes 131104 | tf_op jit(solution)/shard_map/ppermute | solution.py:202
  77.7 0.1 pad_maximum_fusion.1.refs_4_
  77.8 1.1 collective-permute-start.20
  78.9 6.8 %collective-permute-done.15.got_ref = bf16[736,256]{1,0:T(8,128)(2,1)S(1)} collective-permute-done((bf16[736,256]{1,0:T(8,128)(2,1)S(1)}, bf16[736,256]{1,0:T(8,128)(2,1)S(1)}, u32[]{:S(2)}, u32[]{:S(2)}) %collective-permute-start.15) | collective-permute-done | bytes 376864 | tf_op jit(solution)/shard_map/ppermute | solution.py:202
  85.7 1.0 keys_join.1.kv0
  86.7 1.1 collective-permute-start.18
  87.8 3.4 %collective-permute-start.12 = (bf16[4,128,512]{2,1,0:T(8,128)(2,1)S(1)}, bf16[4,128,512]{2,1,0:T(8,128)(2,1)S(1)}, u32[]{:S(2)}, u32[]{:S(2)}) collective-permute-start(bf16[4,128,512]{2,1,0:T(8,128)(2,1)S(1)} %get-tuple-element.65), channel_id=1, source_target_pairs={{0,8},{1,9},{2,10},{3,11},{4,12},{5,13},{6,14},{7,15},{8,0},{9,1},... | collective-permute-start | bytes 1572872 | tf_op jit(solution)/shard_map/ppermute | solution.py:202
  91.2 2.7 %collective-permute-done.13 = bf16[4,128,512]{2,1,0:T(8,128)(2,1)S(1)} collective-permute-done((bf16[4,128,512]{2,1,0:T(8,128)(2,1)S(1)}, bf16[4,128,512]{2,1,0:T(8,128)(2,1)S(1)}, u32[]{:S(2)}, u32[]{:S(2)}) %collective-permute-start.13) | collective-permute-done | bytes 524320 | tf_op jit(solution)/shard_map/ppermute | solution.py:202
  93.9 0.2 add_convert_fusion
  94.1 5.2 %collective-permute-start.14 = (bf16[4,128,512]{2,1,0:T(8,128)(2,1)S(1)}, bf16[4,128,512]{2,1,0:T(8,128)(2,1)S(1)}, u32[]{:S(2)}, u32[]{:S(2)}) collective-permute-start(bf16[4,128,512]{2,1,0:T(8,128)(2,1)S(1)} %add_convert_fusion), channel_id=1, source_target_pairs={{0,16},{1,17},{2,18},{3,19},{4,20},{5,21},{6,22},{7,23},{8,24},{9,... | collective-permute-start | bytes 1572872 | tf_op jit(solution)/shard_map/ppermute | solution.py:202
  99.3 3.0 %collective-permute-start.17 = (bf16[6,128,256]{2,1,0:T(8,128)(2,1)S(1)}, bf16[6,128,256]{2,1,0:T(8,128)(2,1)S(1)}, u32[]{:S(2)}, u32[]{:S(2)}) collective-permute-start(bf16[6,128,256]{2,1,0:T(8,128)(2,1)S(1)} %keys_join.1.kv0), channel_id=1, source_target_pairs={{0,4},{1,3},{2,6},{3,1},{4,0},{5,7},{6,2},{7,5},{8,12},{9,11},{10,... | collective-permute-start | bytes 1179656 | tf_op jit(solution)/shard_map/ppermute | solution.py:202
  102.3 2.4 %collective-permute-done.18.kv3 = bf16[6,128,256]{2,1,0:T(8,128)(2,1)S(1)} collective-permute-done((bf16[6,128,256]{2,1,0:T(8,128)(2,1)S(1)}, bf16[6,128,256]{2,1,0:T(8,128)(2,1)S(1)}, u32[]{:S(2)}, u32[]{:S(2)}) %collective-permute-start.18) | collective-permute-done | bytes 393248 | tf_op jit(solution)/shard_map/ppermute | solution.py:202
  104.7 6.8 %collective-permute-done.17.kv2 = bf16[6,128,256]{2,1,0:T(8,128)(2,1)S(1)} collective-permute-done((bf16[6,128,256]{2,1,0:T(8,128)(2,1)S(1)}, bf16[6,128,256]{2,1,0:T(8,128)(2,1)S(1)}, u32[]{:S(2)}, u32[]{:S(2)}) %collective-permute-start.17) | collective-permute-done | bytes 393248 | tf_op jit(solution)/shard_map/ppermute | solution.py:202
  111.6 0.9 collective-permute-done.16.kv1
  112.5 2.0 %collective-permute-start.24 = (bf16[2,1024,256]{2,1,0:T(8,128)(2,1)S(1)}, bf16[2,1024,256]{2,1,0:T(8,128)(2,1)S(1)}, u32[]{:S(2)}, u32[]{:S(2)}) collective-permute-start(bf16[2,1024,256]{2,1,0:T(8,128)(2,1)S(1)} %collective-permute-done.20.refs_5_), channel_id=1, source_target_pairs={{0,4},{1,3},{2,6},{3,1},{4,0},{5,7},{6,2},{7,5},{8,12},{9,11},{10,... | collective-permute-start | bytes 3145736 | tf_op jit(solution)/shard_map/ppermute | solution.py:202
  114.5 5.7 %collective-permute-done.14.got_ref = bf16[4,128,512]{2,1,0:T(8,128)(2,1)S(1)} collective-permute-done((bf16[4,128,512]{2,1,0:T(8,128)(2,1)S(1)}, bf16[4,128,512]{2,1,0:T(8,128)(2,1)S(1)}, u32[]{:S(2)}, u32[]{:S(2)}) %collective-permute-start.14) | collective-permute-done | bytes 524320 | tf_op jit(solution)/shard_map/ppermute | solution.py:202
  120.2 4.6 %attend.2.refs_0_ = bf16[512,256]{1,0:T(8,128)(2,1)S(1)} custom-call(s32[5]{0:T(128)S(1)} %stack.41.where_ref, f32[4,128,512]{2,1,0:T(8,128)S(1)} %get-tuple-element.64.keep_ref, bf16[4,128,512]{2,1,0:T(8,128)(2,1)S(1)} %collective-permute-done.12.near_ref, bf16[4,128,512]{2,1,0:T(8,128)(2,1)S(1)} %collective-permute-done.14.got_ref, ...), custom_call_target="tpu_custom_call" | custom-call | flops 4000000000 | bytes 4000000 | tf_op jit(solution)/shard_map/attend/pallas_call | solution.py:640
  124.9 0.4 collective-permute-start.21
  125.2 4.8 %attend.3.refs_1_ = bf16[512,256]{1,0:T(8,128)(2,1)S(1)} custom-call(s32[5]{0:T(128)S(1)} %stack.41.where_ref, f32[4,128,512]{2,1,0:T(8,128)S(1)} %get-tuple-element.64.keep_ref, bf16[4,128,512]{2,1,0:T(8,128)(2,1)S(1)} %collective-permute-done.12.near_ref, bf16[4,128,512]{2,1,0:T(8,128)(2,1)S(1)} %collective-permute-done.14.got_ref, ...), custom_call_target="tpu_custom_call" | custom-call | flops 4000000000 | bytes 4000000 | tf_op jit(solution)/shard_map/attend/pallas_call | solution.py:640
  130.1 1.8 %collective-permute-start.22 = (bf16[512,256]{1,0:T(8,128)(2,1)S(1)}, bf16[512,256]{1,0:T(8,128)(2,1)S(1)}, u32[]{:S(2)}, u32[]{:S(2)}) collective-permute-start(bf16[512,256]{1,0:T(8,128)(2,1)S(1)} %attend.3.refs_1_), channel_id=1, source_target_pairs={{0,8},{1,9},{2,10},{3,11},{4,12},{5,13},{6,14},{7,15},{8,0},{9,1},... | collective-permute-start | bytes 786440 | tf_op jit(solution)/shard_map/ppermute | solution.py:202
  131.9 0.8 collective-permute-done.21.refs_2_
  132.7 4.3 %collective-permute-done.22.refs_3_ = bf16[512,256]{1,0:T(8,128)(2,1)S(1)} collective-permute-done((bf16[512,256]{1,0:T(8,128)(2,1)S(1)}, bf16[512,256]{1,0:T(8,128)(2,1)S(1)}, u32[]{:S(2)}, u32[]{:S(2)}) %collective-permute-start.22) | collective-permute-done | bytes 262176 | tf_op jit(solution)/shard_map/ppermute | solution.py:202
  136.9 1.6 collective-permute-done.24.refs_7_
  138.5 1.0 copy-done.7
  139.5 3.9 %output.1 = (f32[4,128,1024]{2,1,0:T(8,128)}, bf16[4,128,1024]{2,1,0:T(8,128)(2,1)S(1)}) custom-call(s32[5]{0:T(128)S(1)} %stack.41.where_ref, bf16[512,256]{1,0:T(8,128)(2,1)S(1)} %attend.2.refs_0_, bf16[512,256]{1,0:T(8,128)(2,1)S(1)} %attend.3.refs_1_, bf16[512,256]{1,0:T(8,128)(2,1)S(1)} %collective-permute-done.21.refs_2_, ...), custom_call_target="tpu_custom_call" | custom-call | flops 5000000000 | bytes 4000000 | tf_op jit(solution)/shard_map/output/pallas_call | solution.py:657
  143.4 2.7 %collective-permute-done.25 = bf16[4,128,1024]{2,1,0:T(8,128)(2,1)S(1)} collective-permute-done((bf16[4,128,1024]{2,1,0:T(8,128)(2,1)S(1)}, bf16[4,128,1024]{2,1,0:T(8,128)(2,1)S(1)}, u32[]{:S(2)}, u32[]{:S(2)}) %collective-permute-start.25) | collective-permute-done | bytes 1048608 | tf_op jit(solution)/shard_map/ppermute | solution.py:202
  146.1 1.9 %fusion.8 = (bf16[128,1024]{1,0:T(8,128)(2,1)S(1)}, bf16[128,1024]{1,0:T(8,128)(2,1)S(1)}, bf16[128,1024]{1,0:T(8,128)(2,1)S(1)}, f32[128,1024]{1,0:T(8,128)S(1)}) fusion(f32[4,128,1024]{2,1,0:T(8,128)} %get-tuple-element.77, bf16[4,128,1024]{2,1,0:T(8,128)(2,1)S(1)} %collective-permute-done.25), kind=kLoop, calls=%fused_computation.29 | loop fusion | flops 1441792 | bytes 4456448 | tf_op jit(solution)/shard_map/convert_element_type | solution.py:674
  148.0 5.3 %collective-permute-start.28 = (bf16[128,1024]{1,0:T(8,128)(2,1)S(1)}, bf16[128,1024]{1,0:T(8,128)(2,1)S(1)}, u32[]{:S(2)}, u32[]{:S(2)}) collective-permute-start(bf16[128,1024]{1,0:T(8,128)(2,1)S(1)} %get-tuple-element.81), channel_id=1, source_target_pairs={{0,24},{1,25},{2,26},{3,27},{4,28},{5,29},{6,30},{7,31},{8,0},{9,1... | collective-permute-start | bytes 786440 | tf_op jit(solution)/shard_map/ppermute | solution.py:202
  153.2 1.5 collective-permute-start.26
  154.8 5.6 %collective-permute-done.28.third = bf16[128,1024]{1,0:T(8,128)(2,1)S(1)} collective-permute-done((bf16[128,1024]{1,0:T(8,128)(2,1)S(1)}, bf16[128,1024]{1,0:T(8,128)(2,1)S(1)}, u32[]{:S(2)}, u32[]{:S(2)}) %collective-permute-start.28) | collective-permute-done | bytes 262176 | tf_op jit(solution)/shard_map/ppermute | solution.py:202
  160.4 9.8 %collective-permute-done.27.second = bf16[128,1024]{1,0:T(8,128)(2,1)S(1)} collective-permute-done((bf16[128,1024]{1,0:T(8,128)(2,1)S(1)}, bf16[128,1024]{1,0:T(8,128)(2,1)S(1)}, u32[]{:S(2)}, u32[]{:S(2)}) %collective-permute-start.27) | collective-permute-done | bytes 262176 | tf_op jit(solution)/shard_map/ppermute | solution.py:202
  170.2 5.5 %collective-permute-done.26.first = bf16[128,1024]{1,0:T(8,128)(2,1)S(1)} collective-permute-done((bf16[128,1024]{1,0:T(8,128)(2,1)S(1)}, bf16[128,1024]{1,0:T(8,128)(2,1)S(1)}, u32[]{:S(2)}, u32[]{:S(2)}) %collective-permute-start.26) | collective-permute-done | bytes 262176 | tf_op jit(solution)/shard_map/ppermute | solution.py:202
  175.7 1.4 finish.1
  (57 shorter events, 1.0 us)
Async XLA Ops:
  0.0 9.8 %copy-start.4 = (bf16[128,2048]{1,0:T(8,128)(2,1)S(1)}, bf16[128,2048]{1,0:T(8,128)(2,1)}, u32[]{:S(2)}) copy-start(bf16[128,2048]{1,0:T(8,128)(2,1)} %param.12) | copy-start | bytes 1572868
  0.0 11.0 %copy-start.8 = (s32[8]{0:T(128)S(1)}, s32[8]{0:T(128)}, u32[]{:S(2)}) copy-start(s32[8]{0:T(128)} %param.22) | copy-start | bytes 100
  0.0 15.0 %copy-start.3 = (bf16[64,512]{1,0:T(8,128)(2,1)S(1)}, bf16[64,512]{1,0:T(8,128)(2,1)}, u32[]{:S(2)}) copy-start(bf16[64,512]{1,0:T(8,128)(2,1)} %refs_3_.1) | copy-start | bytes 196612
  0.0 15.0 %copy-start.2 = (bf16[64,512]{1,0:T(8,128)(2,1)S(1)}, bf16[64,512]{1,0:T(8,128)(2,1)}, u32[]{:S(2)}) copy-start(bf16[64,512]{1,0:T(8,128)(2,1)} %refs_2_.1) | copy-start | bytes 196612
  0.0 15.0 %copy-start.1 = (bf16[256,512]{1,0:T(8,128)(2,1)S(1)}, bf16[256,512]{1,0:T(8,128)(2,1)}, u32[]{:S(2)}) copy-start(bf16[256,512]{1,0:T(8,128)(2,1)} %refs_1_.1) | copy-start | bytes 786436
  0.0 15.0 %copy-start = (bf16[256,512]{1,0:T(8,128)(2,1)S(1)}, bf16[256,512]{1,0:T(8,128)(2,1)}, u32[]{:S(2)}) copy-start(bf16[256,512]{1,0:T(8,128)(2,1)} %refs_0_.2) | copy-start | bytes 786436
  0.0 28.0 %collective-permute-start.3 = (bf16[256,2048]{1,0:T(8,128)(2,1)}, bf16[256,2048]{1,0:T(8,128)(2,1)}, u32[]{:S(2)}, u32[]{:S(2)}) collective-permute-start(bf16[256,2048]{1,0:T(8,128)(2,1)} %refs_0_.3), channel_id=1, source_target_pairs={{0,2},{1,5},{2,0},{3,7},{4,6},{5,1},{6,4},{7,3},{8,10},{9,13},{10,... | collective-permute-start | bytes 3145736 | tf_op jit(solution)/shard_map/ppermute | solution.py:202
  1.6 26.5 %collective-permute-start.4 = (bf16[256,2048]{1,0:T(8,128)(2,1)}, bf16[256,2048]{1,0:T(8,128)(2,1)}, u32[]{:S(2)}, u32[]{:S(2)}) collective-permute-start(bf16[256,2048]{1,0:T(8,128)(2,1)} %refs_0_.3), channel_id=1, source_target_pairs={{0,4},{1,3},{2,6},{3,1},{4,0},{5,7},{6,2},{7,5},{8,12},{9,11},{10,... | collective-permute-start | bytes 3145736 | tf_op jit(solution)/shard_map/ppermute | solution.py:202
  11.1 8.6 %collective-permute-start.1 = (bf16[32,2048]{1,0:T(8,128)(2,1)S(1)}, bf16[32,2048]{1,0:T(8,128)(2,1)}, u32[]{:S(2)}, u32[]{:S(2)}) collective-permute-start(bf16[32,2048]{1,0:T(8,128)(2,1)S(1)} %fusion.5), channel_id=1, source_target_pairs={{0,0},{1,16},{2,1},{3,17},{4,8},{5,24},{6,9},{7,25},{8,2},{9,18},{... | collective-permute-start | bytes 393224 | tf_op jit(solution)/shard_map/ppermute | solution.py:202
  13.4 14.7 %collective-permute-start = (bf16[144,2048]{1,0:T(8,128)(2,1)S(1)}, bf16[144,2048]{1,0:T(8,128)(2,1)}, u32[]{:S(2)}, u32[]{:S(2)}) collective-permute-start(bf16[144,2048]{1,0:T(8,128)(2,1)S(1)} %fusion.2), channel_id=1, source_target_pairs={{1,16},{3,18},{5,20},{7,22},{9,24},{11,26},{13,28},{15,30},{16,1},... | collective-permute-start | bytes 1769480 | tf_op jit(solution)/shard_map/ppermute | solution.py:202
  15.0 1.2 copy-start.5
  15.9 12.1 %collective-permute-start.2 = (bf16[336,512]{1,0:T(8,128)(2,1)S(1)}, bf16[336,512]{1,0:T(8,128)(2,1)S(1)}, u32[]{:S(2)}, u32[]{:S(2)}) collective-permute-start(bf16[336,512]{1,0:T(8,128)(2,1)S(1)} %get-tuple-element.45), channel_id=1, source_target_pairs={{0,8},{1,9},{2,10},{3,11},{4,12},{5,13},{6,14},{7,15},{8,0},{9,1},... | collective-permute-start | bytes 1032200 | tf_op jit(solution)/shard_map/ppermute | solution.py:202
  28.2 12.6 %collective-permute-start.10 = (bf16[2,256,512]{2,1,0:T(8,128)(2,1)S(1)}, bf16[2,256,512]{2,1,0:T(8,128)(2,1)S(1)}, u32[]{:S(2)}, u32[]{:S(2)}) collective-permute-start(bf16[2,256,512]{2,1,0:T(8,128)(2,1)S(1)} %pad_maximum_fusion.3.own), channel_id=1, source_target_pairs={{0,2},{1,5},{2,0},{3,7},{4,6},{5,1},{6,4},{7,3},{8,10},{9,13},{10,... | collective-permute-start | bytes 1572872 | tf_op jit(solution)/shard_map/ppermute | solution.py:202
  31.0 29.2 %collective-permute-start.7 = (bf16[256,2048]{1,0:T(8,128)(2,1)}, bf16[256,2048]{1,0:T(8,128)(2,1)S(1)}, u32[]{:S(2)}, u32[]{:S(2)}) collective-permute-start(bf16[256,2048]{1,0:T(8,128)(2,1)} %collective-permute-done.3.refs_1_), channel_id=1, source_target_pairs={{0,4},{1,3},{2,6},{3,1},{4,0},{5,7},{6,2},{7,5},{8,12},{9,11},{10,... | collective-permute-start | bytes 3145736 | tf_op jit(solution)/shard_map/ppermute | solution.py:202
  32.0 28.1 %collective-permute-start.5 = (bf16[176,2048]{1,0:T(8,128)(2,1)S(1)}, bf16[176,2048]{1,0:T(8,128)(2,1)S(1)}, u32[]{:S(2)}, u32[]{:S(2)}) collective-permute-start(bf16[176,2048]{1,0:T(8,128)(2,1)S(1)} %pad_maximum_fusion.2.x0), channel_id=1, source_target_pairs={{0,8},{1,9},{2,10},{3,11},{4,12},{5,13},{6,14},{7,15},{8,0},{9,1},... | collective-permute-start | bytes 2162696 | tf_op jit(solution)/shard_map/ppermute | solution.py:202
  33.3 26.9 %collective-permute-start.6 = (bf16[768,256]{1,0:T(8,128)(2,1)S(1)}, bf16[768,256]{1,0:T(8,128)(2,1)S(1)}, u32[]{:S(2)}, u32[]{:S(2)}) collective-permute-start(bf16[768,256]{1,0:T(8,128)(2,1)S(1)} %slice.42), channel_id=1, source_target_pairs={{0,16},{1,17},{2,18},{3,19},{4,20},{5,21},{6,22},{7,23},{8,24},{9,... | collective-permute-start | bytes 1179656 | tf_op jit(solution)/shard_map/ppermute | solution.py:202
  40.9 22.9 %collective-permute-start.11 = (bf16[4,256,512]{2,1,0:T(8,128)(2,1)S(1)}, bf16[4,256,512]{2,1,0:T(8,128)(2,1)S(1)}, u32[]{:S(2)}, u32[]{:S(2)}) collective-permute-start(bf16[4,256,512]{2,1,0:T(8,128)(2,1)S(1)} %pad_maximum_fusion), channel_id=1, source_target_pairs={{0,4},{1,3},{2,6},{3,1},{4,0},{5,7},{6,2},{7,5},{8,12},{9,11},{10,... | collective-permute-start | bytes 3145736 | tf_op jit(solution)/shard_map/ppermute | solution.py:202
  41.5 22.4 %collective-permute-start.9 = (bf16[176,2048]{1,0:T(8,128)(2,1)S(1)}, bf16[176,2048]{1,0:T(8,128)(2,1)S(1)}, u32[]{:S(2)}, u32[]{:S(2)}) collective-permute-start(bf16[176,2048]{1,0:T(8,128)(2,1)S(1)} %pad_maximum_fusion.2.x0), channel_id=1, source_target_pairs={{0,1},{1,0},{2,3},{3,2},{4,5},{5,4},{6,7},{7,6},{8,9},{9,8},{10,11... | collective-permute-start | bytes 2162696 | tf_op jit(solution)/shard_map/ppermute | solution.py:202
  60.2 1.9 %copy-start.6 = (bf16[256,2048]{1,0:T(8,128)(2,1)}, bf16[256,2048]{1,0:T(8,128)(2,1)S(1)}, u32[]{:S(2)}) copy-start(bf16[256,2048]{1,0:T(8,128)(2,1)S(1)} %collective-permute-done.7.refs_3_) | copy-start | bytes 3145732
  60.2 3.7 %collective-permute-start.8 = (bf16[176,2048]{1,0:T(8,128)(2,1)S(1)}, bf16[176,2048]{1,0:T(8,128)(2,1)S(1)}, u32[]{:S(2)}, u32[]{:S(2)}) collective-permute-start(bf16[176,2048]{1,0:T(8,128)(2,1)S(1)} %collective-permute-done.5.x1), channel_id=1, source_target_pairs={{0,1},{1,0},{2,3},{3,2},{4,5},{5,4},{6,7},{7,6},{8,9},{9,8},{10,11... | collective-permute-start | bytes 2162696 | tf_op jit(solution)/shard_map/ppermute | solution.py:202
  62.1 15.5 %collective-permute-start.19 = (bf16[256,256]{1,0:T(8,128)(2,1)S(1)}, bf16[256,256]{1,0:T(8,128)(2,1)S(1)}, u32[]{:S(2)}, u32[]{:S(2)}) collective-permute-start(bf16[256,256]{1,0:T(8,128)(2,1)S(1)} %slice.47), channel_id=1, source_target_pairs={{0,16},{1,17},{2,18},{3,19},{4,20},{5,21},{6,22},{7,23},{8,24},{9,... | collective-permute-start | bytes 393224 | tf_op jit(solution)/shard_map/ppermute | solution.py:202
  66.0 19.7 %collective-permute-start.15 = (bf16[736,256]{1,0:T(8,128)(2,1)S(1)}, bf16[736,256]{1,0:T(8,128)(2,1)S(1)}, u32[]{:S(2)}, u32[]{:S(2)}) collective-permute-start(bf16[736,256]{1,0:T(8,128)(2,1)S(1)} %get-tuple-element.69), channel_id=1, source_target_pairs={{0,16},{1,17},{2,18},{3,19},{4,20},{5,21},{6,22},{7,23},{8,24},{9,... | collective-permute-start | bytes 1130504 | tf_op jit(solution)/shard_map/ppermute | solution.py:202
  72.5 21.4 %collective-permute-start.13 = (bf16[4,128,512]{2,1,0:T(8,128)(2,1)S(1)}, bf16[4,128,512]{2,1,0:T(8,128)(2,1)S(1)}, u32[]{:S(2)}, u32[]{:S(2)}) collective-permute-start(bf16[4,128,512]{2,1,0:T(8,128)(2,1)S(1)} %get-tuple-element.67), channel_id=1, source_target_pairs={{0,8},{1,9},{2,10},{3,11},{4,12},{5,13},{6,14},{7,15},{8,0},{9,1},... | collective-permute-start | bytes 1572872 | tf_op jit(solution)/shard_map/ppermute | solution.py:202
  77.8 34.7 %collective-permute-start.20 = (bf16[2,1024,256]{2,1,0:T(8,128)(2,1)S(1)}, bf16[2,1024,256]{2,1,0:T(8,128)(2,1)S(1)}, u32[]{:S(2)}, u32[]{:S(2)}) collective-permute-start(bf16[2,1024,256]{2,1,0:T(8,128)(2,1)S(1)} %pad_maximum_fusion.1.refs_4_), channel_id=1, source_target_pairs={{0,2},{1,5},{2,0},{3,7},{4,6},{5,1},{6,4},{7,3},{8,10},{9,13},{10,... | collective-permute-start | bytes 3145736 | tf_op jit(solution)/shard_map/ppermute | solution.py:202
  86.7 18.0 %collective-permute-start.18 = (bf16[6,128,256]{2,1,0:T(8,128)(2,1)S(1)}, bf16[6,128,256]{2,1,0:T(8,128)(2,1)S(1)}, u32[]{:S(2)}, u32[]{:S(2)}) collective-permute-start(bf16[6,128,256]{2,1,0:T(8,128)(2,1)S(1)} %keys_join.1.kv0), channel_id=1, source_target_pairs={{0,6},{1,7},{2,4},{3,5},{4,2},{5,3},{6,0},{7,1},{8,14},{9,15},{10,... | collective-permute-start | bytes 1179656 | tf_op jit(solution)/shard_map/ppermute | solution.py:202
  87.8 26.7 %collective-permute-start.12 = (bf16[4,128,512]{2,1,0:T(8,128)(2,1)S(1)}, bf16[4,128,512]{2,1,0:T(8,128)(2,1)S(1)}, u32[]{:S(2)}, u32[]{:S(2)}) collective-permute-start(bf16[4,128,512]{2,1,0:T(8,128)(2,1)S(1)} %get-tuple-element.65), channel_id=1, source_target_pairs={{0,8},{1,9},{2,10},{3,11},{4,12},{5,13},{6,14},{7,15},{8,0},{9,1},... | collective-permute-start | bytes 1572872 | tf_op jit(solution)/shard_map/ppermute | solution.py:202
  94.1 26.1 %collective-permute-start.14 = (bf16[4,128,512]{2,1,0:T(8,128)(2,1)S(1)}, bf16[4,128,512]{2,1,0:T(8,128)(2,1)S(1)}, u32[]{:S(2)}, u32[]{:S(2)}) collective-permute-start(bf16[4,128,512]{2,1,0:T(8,128)(2,1)S(1)} %add_convert_fusion), channel_id=1, source_target_pairs={{0,16},{1,17},{2,18},{3,19},{4,20},{5,21},{6,22},{7,23},{8,24},{9,... | collective-permute-start | bytes 1572872 | tf_op jit(solution)/shard_map/ppermute | solution.py:202
  99.3 12.2 %collective-permute-start.17 = (bf16[6,128,256]{2,1,0:T(8,128)(2,1)S(1)}, bf16[6,128,256]{2,1,0:T(8,128)(2,1)S(1)}, u32[]{:S(2)}, u32[]{:S(2)}) collective-permute-start(bf16[6,128,256]{2,1,0:T(8,128)(2,1)S(1)} %keys_join.1.kv0), channel_id=1, source_target_pairs={{0,4},{1,3},{2,6},{3,1},{4,0},{5,7},{6,2},{7,5},{8,12},{9,11},{10,... | collective-permute-start | bytes 1179656 | tf_op jit(solution)/shard_map/ppermute | solution.py:202
  104.7 7.8 %collective-permute-start.16 = (bf16[6,128,256]{2,1,0:T(8,128)(2,1)S(1)}, bf16[6,128,256]{2,1,0:T(8,128)(2,1)S(1)}, u32[]{:S(2)}, u32[]{:S(2)}) collective-permute-start(bf16[6,128,256]{2,1,0:T(8,128)(2,1)S(1)} %keys_join.1.kv0), channel_id=1, source_target_pairs={{0,2},{1,5},{2,0},{3,7},{4,6},{5,1},{6,4},{7,3},{8,10},{9,13},{10,... | collective-permute-start | bytes 1179656 | tf_op jit(solution)/shard_map/ppermute | solution.py:202
  112.5 24.4 %collective-permute-start.23 = (bf16[2,1024,256]{2,1,0:T(8,128)(2,1)S(1)}, bf16[2,1024,256]{2,1,0:T(8,128)(2,1)S(1)}, u32[]{:S(2)}, u32[]{:S(2)}) collective-permute-start(bf16[2,1024,256]{2,1,0:T(8,128)(2,1)S(1)} %pad_maximum_fusion.1.refs_4_), channel_id=1, source_target_pairs={{0,4},{1,3},{2,6},{3,1},{4,0},{5,7},{6,2},{7,5},{8,12},{9,11},{10,... | collective-permute-start | bytes 3145736 | tf_op jit(solution)/shard_map/ppermute | solution.py:202
  112.5 26.0 %collective-permute-start.24 = (bf16[2,1024,256]{2,1,0:T(8,128)(2,1)S(1)}, bf16[2,1024,256]{2,1,0:T(8,128)(2,1)S(1)}, u32[]{:S(2)}, u32[]{:S(2)}) collective-permute-start(bf16[2,1024,256]{2,1,0:T(8,128)(2,1)S(1)} %collective-permute-done.20.refs_5_), channel_id=1, source_target_pairs={{0,4},{1,3},{2,6},{3,1},{4,0},{5,7},{6,2},{7,5},{8,12},{9,11},{10,... | collective-permute-start | bytes 3145736 | tf_op jit(solution)/shard_map/ppermute | solution.py:202
  124.9 7.8 %collective-permute-start.21 = (bf16[512,256]{1,0:T(8,128)(2,1)S(1)}, bf16[512,256]{1,0:T(8,128)(2,1)S(1)}, u32[]{:S(2)}, u32[]{:S(2)}) collective-permute-start(bf16[512,256]{1,0:T(8,128)(2,1)S(1)} %attend.2.refs_0_), channel_id=1, source_target_pairs={{0,8},{1,9},{2,10},{3,11},{4,12},{5,13},{6,14},{7,15},{8,0},{9,1},... | collective-permute-start | bytes 786440 | tf_op jit(solution)/shard_map/ppermute | solution.py:202
  130.1 6.9 %collective-permute-start.22 = (bf16[512,256]{1,0:T(8,128)(2,1)S(1)}, bf16[512,256]{1,0:T(8,128)(2,1)S(1)}, u32[]{:S(2)}, u32[]{:S(2)}) collective-permute-start(bf16[512,256]{1,0:T(8,128)(2,1)S(1)} %attend.3.refs_1_), channel_id=1, source_target_pairs={{0,8},{1,9},{2,10},{3,11},{4,12},{5,13},{6,14},{7,15},{8,0},{9,1},... | collective-permute-start | bytes 786440 | tf_op jit(solution)/shard_map/ppermute | solution.py:202
  138.5 1.0 copy-start.7
  143.4 2.7 %collective-permute-start.25 = (bf16[4,128,1024]{2,1,0:T(8,128)(2,1)S(1)}, bf16[4,128,1024]{2,1,0:T(8,128)(2,1)S(1)}, u32[]{:S(2)}, u32[]{:S(2)}) collective-permute-start(bf16[4,128,1024]{2,1,0:T(8,128)(2,1)S(1)} %get-tuple-element.78), channel_id=1, source_target_pairs={{0,1},{1,0},{2,3},{3,2},{4,5},{5,4},{6,7},{7,6},{8,9},{9,8},{10,11... | collective-permute-start | bytes 3145736 | tf_op jit(solution)/shard_map/ppermute | solution.py:202
  148.0 12.4 %collective-permute-start.28 = (bf16[128,1024]{1,0:T(8,128)(2,1)S(1)}, bf16[128,1024]{1,0:T(8,128)(2,1)S(1)}, u32[]{:S(2)}, u32[]{:S(2)}) collective-permute-start(bf16[128,1024]{1,0:T(8,128)(2,1)S(1)} %get-tuple-element.81), channel_id=1, source_target_pairs={{0,24},{1,25},{2,26},{3,27},{4,28},{5,29},{6,30},{7,31},{8,0},{9,1... | collective-permute-start | bytes 786440 | tf_op jit(solution)/shard_map/ppermute | solution.py:202
  153.2 16.9 %collective-permute-start.27 = (bf16[128,1024]{1,0:T(8,128)(2,1)S(1)}, bf16[128,1024]{1,0:T(8,128)(2,1)S(1)}, u32[]{:S(2)}, u32[]{:S(2)}) collective-permute-start(bf16[128,1024]{1,0:T(8,128)(2,1)S(1)} %get-tuple-element.82), channel_id=1, source_target_pairs={{0,16},{1,17},{2,18},{3,19},{4,20},{5,21},{6,22},{7,23},{8,24},{9,... | collective-permute-start | bytes 786440 | tf_op jit(solution)/shard_map/ppermute | solution.py:202
  153.2 22.5 %collective-permute-start.26 = (bf16[128,1024]{1,0:T(8,128)(2,1)S(1)}, bf16[128,1024]{1,0:T(8,128)(2,1)S(1)}, u32[]{:S(2)}, u32[]{:S(2)}) collective-permute-start(bf16[128,1024]{1,0:T(8,128)(2,1)S(1)} %get-tuple-element.83), channel_id=1, source_target_pairs={{0,8},{1,9},{2,10},{3,11},{4,12},{5,13},{6,14},{7,15},{8,16},{9,17... | collective-permute-start | bytes 786440 | tf_op jit(solution)/shard_map/ppermute | solution.py:202

commit v18 on v14

--- a/solution.py
+++ b/solution.py
@@ -626,10 +626,10 @@
     kv_near, kv_far = to_near(kv), to_far(kv)
     kv_both = permuted(kv, lambda z, p, c: (z, p ^ 3, c))
 
-    kv_near, kv_far, kv_both, out_near, out_pair = lax.optimization_barrier(
-        (kv_near, kv_far, kv_both, out_near, out_pair)
-    )
-    out_far, out_both = to_far(out_pair), to_far(out_near)
+    kv_far, out_pair = lax.optimization_barrier((kv_far, out_pair))
+    out_far = to_far(out_pair)
+    kv_near, kv_both, out_near = lax.optimization_barrier((kv_near, kv_both, out_near))
+    out_both = to_far(out_near)
 
     attended = [
         pl.pallas_call(

time: 179 us -> 176 us (0.983)
  starting transfers between devices: 49.1 us -> 45.9 us
    ppermute x28, starting transfers between devices: 49.1 us -> 45.9 us  [permuted(): return lax.ppermute(value, ('seq', 'head'), perm)]
where the time goes in v18:
time: 176 us
  waiting for transfers between devices  93.1 us (53%)
  starting transfers between devices  45.9 us (26%)
  Pallas kernels  23.8 us (14%)
  other arithmetic  8.06 us (5%)
  blocking collectives  2.46 us (1%)
  local copies, waits for them, and re-layouts  2.09 us (1%)
    ppermute x28, waiting for transfers between devices, permuted(): return lax.ppermute(value, ('seq', 'head'), perm)  93.1 us
    ppermute x28, starting transfers between devices, permuted(): return lax.ppermute(value, ('seq', 'head'), perm)  45.9 us
    pallas_call x2, Pallas kernels, by_levels(): pl.pallas_call(functools.partial(attend_kernel, pair), out_shape=shaped((...  9.48 us
    pallas_call x1, Pallas kernels, by_levels(): pl.pallas_call(queries_part_kernel, out_shape=(shaped(group_shape, jnp.fl...  4.99 us
    pallas_call x1, Pallas kernels, by_levels(): pl.pallas_call(output_kernel, out_shape=(shaped((LEVELS, tok, wide_cols),...  3.89 us
  transfers between devices with their start and end apart: 28, of which 14 were waited for; matrix products, arithmetic and copies ran while one was open for 4% of the time, Pallas kernels for 9%

profile of v18, /device:TPU:8, one launch (start us, length us, event | category | flops | bytes accessed | tf_op | source)
XLA Modules:
  0.0 175.8 jit_solution(13071900121366845711)
XLA Ops:
  0.0 1.6 collective-permute-start.10
  1.6 1.5 collective-permute-start.9
  3.1 1.0 fusion.3
  4.2 0.1 pad.22.clone
  4.2 1.4 fusion
  5.6 2.5 %all-reduce.1 = (f32[144]{0:T(256)S(1)}, f32[32]{0:T(128)S(1)}) all-reduce(f32[144]{0:T(256)S(1)} %fusion, f32[32]{0:T(128)S(1)} %fusion.3), channel_id=1, replica_groups=mesh['seq'=16,'head'=2] {'head'}, use_global_device_ids=true, to_apply=%region_1.2 | all-reduce | flops 176 | bytes 1408 | tf_op jit(solution)/shard_map/psum | solution.py:518
  8.1 0.7 dynamic_slice.9
  8.8 1.1 fusion.2
  10.0 0.1 fusion.5
  10.1 0.1 broadcast_in_dim.5.refs_4_
  10.2 0.1 stack.41.where_ref
  10.3 0.9 pack.1
  11.2 0.5 collective-permute-start.2
  11.7 3.4 %collective-permute-start.1 = (bf16[32,2048]{1,0:T(8,128)(2,1)S(1)}, bf16[32,2048]{1,0:T(8,128)(2,1)S(1)}, u32[]{:S(2)}, u32[]{:S(2)}) collective-permute-start(bf16[32,2048]{1,0:T(8,128)(2,1)S(1)} %fusion.5), channel_id=1, source_target_pairs={{0,0},{1,16},{2,1},{3,17},{4,8},{5,24},{6,9},{7,25},{8,2},{9,18},{... | collective-permute-start | bytes 393224 | tf_op jit(solution)/shard_map/ppermute | solution.py:202
  15.2 1.5 collective-permute-start
  16.7 0.1 dynamic-slice_bitcast_fusion
  16.8 8.2 %collective-permute-done.1 = bf16[32,2048]{1,0:T(8,128)(2,1)S(1)} collective-permute-done((bf16[32,2048]{1,0:T(8,128)(2,1)S(1)}, bf16[32,2048]{1,0:T(8,128)(2,1)S(1)}, u32[]{:S(2)}, u32[]{:S(2)}) %collective-permute-start.1) | collective-permute-done | bytes 131104 | tf_op jit(solution)/shard_map/ppermute | solution.py:202
  25.1 5.5 %collective-permute-start.7 = (bf16[2,256,512]{2,1,0:T(8,128)(2,1)S(1)}, bf16[2,256,512]{2,1,0:T(8,128)(2,1)S(1)}, u32[]{:S(2)}, u32[]{:S(2)}) collective-permute-start(bf16[2,256,512]{2,1,0:T(8,128)(2,1)S(1)} %pad_maximum_fusion.3.own), channel_id=1, source_target_pairs={{0,2},{1,5},{2,0},{3,7},{4,6},{5,1},{6,4},{7,3},{8,10},{9,13},{10,... | collective-permute-start | bytes 1572872 | tf_op jit(solution)/shard_map/ppermute | solution.py:202
  30.9 8.0 %collective-permute-start.4 = (bf16[1024,256]{1,0:T(8,128)(2,1)S(1)}, bf16[1024,256]{1,0:T(8,128)(2,1)S(1)}, u32[]{:S(2)}, u32[]{:S(2)}) collective-permute-start(bf16[1024,256]{1,0:T(8,128)(2,1)S(1)} %get-tuple-element.49), channel_id=1, source_target_pairs={{0,16},{1,17},{2,18},{3,19},{4,20},{5,21},{6,22},{7,23},{8,24},{9,... | collective-permute-start | bytes 1572872 | tf_op jit(solution)/shard_map/ppermute | solution.py:202
  38.8 0.1 add_convert_fusion.4
  38.9 0.1 pad_maximum_fusion
  39.0 0.5 collective-permute-start.8
  39.6 1.6 collective-permute-start.11
  41.1 0.1 add_convert_fusion.5
  41.2 20.7 %collective-permute-done.4 = bf16[1024,256]{1,0:T(8,128)(2,1)S(1)} collective-permute-done((bf16[1024,256]{1,0:T(8,128)(2,1)S(1)}, bf16[1024,256]{1,0:T(8,128)(2,1)S(1)}, u32[]{:S(2)}, u32[]{:S(2)}) %collective-permute-start.4) | collective-permute-done | bytes 524320 | tf_op jit(solution)/shard_map/ppermute | solution.py:202
  61.9 1.5 fusion.9
  63.4 0.2 pad_maximum_fusion.4.cos_ref
  63.6 0.2 pad_maximum_fusion.5.sin_ref
  63.8 0.1 pad_maximum_fusion.1.refs_4_
  63.9 0.2 collective-permute-done.5.x3
  64.1 1.0 collective-permute-done.11.refs_3_
  65.1 2.1 %keys_part.1 = (f32[576,256]{1,0:T(8,128)S(1)}, bf16[736,256]{1,0:T(8,128)(2,1)S(1)}) custom-call(s32[5]{0:T(128)S(1)} %stack.41.where_ref, bf16[176,2048]{1,0:T(8,128)(2,1)S(1)} %pad_maximum_fusion.2.x0, bf16[176,2048]{1,0:T(8,128)(2,1)S(1)} %collective-permute-done.3.x1, bf16[176,2048]{1,0:T(8,128)(2,1)S(1)} %collective-permute-done.6.x2, ...), custom_call_target="tpu_custom_call" | custom-call | flops 3000000000 | bytes 4000000 | tf_op jit(solution)/shard_map/keys_part/pallas_call | solution.py:578
  67.2 2.4 %collective-permute-start.15 = (bf16[736,256]{1,0:T(8,128)(2,1)S(1)}, bf16[736,256]{1,0:T(8,128)(2,1)S(1)}, u32[]{:S(2)}, u32[]{:S(2)}) collective-permute-start(bf16[736,256]{1,0:T(8,128)(2,1)S(1)} %get-tuple-element.69), channel_id=1, source_target_pairs={{0,16},{1,17},{2,18},{3,19},{4,20},{5,21},{6,22},{7,23},{8,24},{9,... | collective-permute-start | bytes 1130504 | tf_op jit(solution)/shard_map/ppermute | solution.py:202
  69.7 5.0 %queries_part.1 = (f32[4,128,512]{2,1,0:T(8,128)S(1)}, f32[4,128,512]{2,1,0:T(8,128)S(1)}, bf16[4,128,512]{2,1,0:T(8,128)(2,1)S(1)}, bf16[4,128,512]{2,1,0:T(8,128)(2,1)S(1)}) custom-call(s32[5]{0:T(128)S(1)} %stack.41.where_ref, bf16[176,2048]{1,0:T(8,128)(2,1)S(1)} %pad_maximum_fusion.2.x0, bf16[176,2048]{1,0:T(8,128)(2,1)S(1)} %collective-permute-done.3.x1, ...), custom_call_target="tpu_custom_call" | custom-call | flops 5000000000 | bytes 4000000 | tf_op jit(solution)/shard_map/queries_part/pallas_call | solution.py:595
  74.7 1.0 collective-permute-start.18
  75.8 9.6 %collective-permute-done.15.got_ref = bf16[736,256]{1,0:T(8,128)(2,1)S(1)} collective-permute-done((bf16[736,256]{1,0:T(8,128)(2,1)S(1)}, bf16[736,256]{1,0:T(8,128)(2,1)S(1)}, u32[]{:S(2)}, u32[]{:S(2)}) %collective-permute-start.15) | collective-permute-done | bytes 376864 | tf_op jit(solution)/shard_map/ppermute | solution.py:202
  85.3 1.0 keys_join.1.kv0
  86.4 0.6 collective-permute-start.19
  87.0 3.2 %collective-permute-start.12 = (bf16[4,128,512]{2,1,0:T(8,128)(2,1)S(1)}, bf16[4,128,512]{2,1,0:T(8,128)(2,1)S(1)}, u32[]{:S(2)}, u32[]{:S(2)}) collective-permute-start(bf16[4,128,512]{2,1,0:T(8,128)(2,1)S(1)} %get-tuple-element.65), channel_id=1, source_target_pairs={{0,8},{1,9},{2,10},{3,11},{4,12},{5,13},{6,14},{7,15},{8,0},{9,1},... | collective-permute-start | bytes 1572872 | tf_op jit(solution)/shard_map/ppermute | solution.py:202
  90.1 4.8 %collective-permute-done.13 = bf16[4,128,512]{2,1,0:T(8,128)(2,1)S(1)} collective-permute-done((bf16[4,128,512]{2,1,0:T(8,128)(2,1)S(1)}, bf16[4,128,512]{2,1,0:T(8,128)(2,1)S(1)}, u32[]{:S(2)}, u32[]{:S(2)}) %collective-permute-start.13) | collective-permute-done | bytes 524320 | tf_op jit(solution)/shard_map/ppermute | solution.py:202
  95.0 0.2 add_convert_fusion
  95.1 3.2 %collective-permute-start.14 = (bf16[4,128,512]{2,1,0:T(8,128)(2,1)S(1)}, bf16[4,128,512]{2,1,0:T(8,128)(2,1)S(1)}, u32[]{:S(2)}, u32[]{:S(2)}) collective-permute-start(bf16[4,128,512]{2,1,0:T(8,128)(2,1)S(1)} %add_convert_fusion), channel_id=1, source_target_pairs={{0,16},{1,17},{2,18},{3,19},{4,20},{5,21},{6,22},{7,23},{8,24},{9,... | collective-permute-start | bytes 1572872 | tf_op jit(solution)/shard_map/ppermute | solution.py:202
  98.3 0.9 collective-permute-start.16
  99.3 1.0 collective-permute-start.17
  100.3 7.7 %collective-permute-done.16.kv1 = bf16[6,128,256]{2,1,0:T(8,128)(2,1)S(1)} collective-permute-done((bf16[6,128,256]{2,1,0:T(8,128)(2,1)S(1)}, bf16[6,128,256]{2,1,0:T(8,128)(2,1)S(1)}, u32[]{:S(2)}, u32[]{:S(2)}) %collective-permute-start.16) | collective-permute-done | bytes 393248 | tf_op jit(solution)/shard_map/ppermute | solution.py:202
  108.0 0.5 collective-permute-start.22
  108.4 6.3 %collective-permute-done.17.kv3 = bf16[6,128,256]{2,1,0:T(8,128)(2,1)S(1)} collective-permute-done((bf16[6,128,256]{2,1,0:T(8,128)(2,1)S(1)}, bf16[6,128,256]{2,1,0:T(8,128)(2,1)S(1)}, u32[]{:S(2)}, u32[]{:S(2)}) %collective-permute-start.17) | collective-permute-done | bytes 393248 | tf_op jit(solution)/shard_map/ppermute | solution.py:202
  114.7 1.6 collective-permute-start.23
  116.3 2.3 %collective-permute-done.14.got_ref = bf16[4,128,512]{2,1,0:T(8,128)(2,1)S(1)} collective-permute-done((bf16[4,128,512]{2,1,0:T(8,128)(2,1)S(1)}, bf16[4,128,512]{2,1,0:T(8,128)(2,1)S(1)}, u32[]{:S(2)}, u32[]{:S(2)}) %collective-permute-start.14) | collective-permute-done | bytes 524320 | tf_op jit(solution)/shard_map/ppermute | solution.py:202
  118.6 4.7 %attend.3.refs_1_ = bf16[512,256]{1,0:T(8,128)(2,1)S(1)} custom-call(s32[5]{0:T(128)S(1)} %stack.41.where_ref, f32[4,128,512]{2,1,0:T(8,128)S(1)} %get-tuple-element.64.keep_ref, bf16[4,128,512]{2,1,0:T(8,128)(2,1)S(1)} %collective-permute-done.12.near_ref, bf16[4,128,512]{2,1,0:T(8,128)(2,1)S(1)} %collective-permute-done.14.got_ref, ...), custom_call_target="tpu_custom_call" | custom-call | flops 4000000000 | bytes 4000000 | tf_op jit(solution)/shard_map/attend/pallas_call | solution.py:635
  123.3 4.0 %collective-permute-start.21 = (bf16[512,256]{1,0:T(8,128)(2,1)S(1)}, bf16[512,256]{1,0:T(8,128)(2,1)S(1)}, u32[]{:S(2)}, u32[]{:S(2)}) collective-permute-start(bf16[512,256]{1,0:T(8,128)(2,1)S(1)} %attend.3.refs_1_), channel_id=1, source_target_pairs={{0,8},{1,9},{2,10},{3,11},{4,12},{5,13},{6,14},{7,15},{8,0},{9,1},... | collective-permute-start | bytes 786440 | tf_op jit(solution)/shard_map/ppermute | solution.py:202
  127.3 4.8 %attend.2.refs_0_ = bf16[512,256]{1,0:T(8,128)(2,1)S(1)} custom-call(s32[5]{0:T(128)S(1)} %stack.41.where_ref, f32[4,128,512]{2,1,0:T(8,128)S(1)} %get-tuple-element.64.keep_ref, bf16[4,128,512]{2,1,0:T(8,128)(2,1)S(1)} %collective-permute-done.12.near_ref, bf16[4,128,512]{2,1,0:T(8,128)(2,1)S(1)} %collective-permute-done.14.got_ref, ...), custom_call_target="tpu_custom_call" | custom-call | flops 4000000000 | bytes 4000000 | tf_op jit(solution)/shard_map/attend/pallas_call | solution.py:635
  132.1 0.1 collective-permute-start.20
  132.2 6.3 %collective-permute-done.20.refs_2_ = bf16[512,256]{1,0:T(8,128)(2,1)S(1)} collective-permute-done((bf16[512,256]{1,0:T(8,128)(2,1)S(1)}, bf16[512,256]{1,0:T(8,128)(2,1)S(1)}, u32[]{:S(2)}, u32[]{:S(2)}) %collective-permute-start.20) | collective-permute-done | bytes 262176 | tf_op jit(solution)/shard_map/ppermute | solution.py:202
  138.6 1.0 copy-done.8
  139.6 3.9 %output.1 = (f32[4,128,1024]{2,1,0:T(8,128)}, bf16[4,128,1024]{2,1,0:T(8,128)(2,1)S(1)}) custom-call(s32[5]{0:T(128)S(1)} %stack.41.where_ref, bf16[512,256]{1,0:T(8,128)(2,1)S(1)} %attend.2.refs_0_, bf16[512,256]{1,0:T(8,128)(2,1)S(1)} %attend.3.refs_1_, bf16[512,256]{1,0:T(8,128)(2,1)S(1)} %collective-permute-done.20.refs_2_, ...), custom_call_target="tpu_custom_call" | custom-call | flops 5000000000 | bytes 4000000 | tf_op jit(solution)/shard_map/output/pallas_call | solution.py:652
  143.5 2.7 %collective-permute-done.24 = bf16[4,128,1024]{2,1,0:T(8,128)(2,1)S(1)} collective-permute-done((bf16[4,128,1024]{2,1,0:T(8,128)(2,1)S(1)}, bf16[4,128,1024]{2,1,0:T(8,128)(2,1)S(1)}, u32[]{:S(2)}, u32[]{:S(2)}) %collective-permute-start.24) | collective-permute-done | bytes 1048608 | tf_op jit(solution)/shard_map/ppermute | solution.py:202
  146.1 1.9 %fusion.8 = (bf16[128,1024]{1,0:T(8,128)(2,1)S(1)}, bf16[128,1024]{1,0:T(8,128)(2,1)S(1)}, bf16[128,1024]{1,0:T(8,128)(2,1)S(1)}, f32[128,1024]{1,0:T(8,128)S(1)}) fusion(f32[4,128,1024]{2,1,0:T(8,128)} %get-tuple-element.77, bf16[4,128,1024]{2,1,0:T(8,128)(2,1)S(1)} %collective-permute-done.24), kind=kLoop, calls=%fused_computation.28 | loop fusion | flops 1441792 | bytes 4456448 | tf_op jit(solution)/shard_map/convert_element_type | solution.py:669
  148.0 1.4 collective-permute-start.25
  149.4 1.8 %collective-permute-start.26 = (bf16[128,1024]{1,0:T(8,128)(2,1)S(1)}, bf16[128,1024]{1,0:T(8,128)(2,1)S(1)}, u32[]{:S(2)}, u32[]{:S(2)}) collective-permute-start(bf16[128,1024]{1,0:T(8,128)(2,1)S(1)} %get-tuple-element.82), channel_id=1, source_target_pairs={{0,16},{1,17},{2,18},{3,19},{4,20},{5,21},{6,22},{7,23},{8,24},{9,... | collective-permute-start | bytes 786440 | tf_op jit(solution)/shard_map/ppermute | solution.py:202
  151.1 16.0 %collective-permute-done.25.first = bf16[128,1024]{1,0:T(8,128)(2,1)S(1)} collective-permute-done((bf16[128,1024]{1,0:T(8,128)(2,1)S(1)}, bf16[128,1024]{1,0:T(8,128)(2,1)S(1)}, u32[]{:S(2)}, u32[]{:S(2)}) %collective-permute-start.25) | collective-permute-done | bytes 262176 | tf_op jit(solution)/shard_map/ppermute | solution.py:202
  167.1 5.0 %collective-permute-done.26.second = bf16[128,1024]{1,0:T(8,128)(2,1)S(1)} collective-permute-done((bf16[128,1024]{1,0:T(8,128)(2,1)S(1)}, bf16[128,1024]{1,0:T(8,128)(2,1)S(1)}, u32[]{:S(2)}, u32[]{:S(2)}) %collective-permute-start.26) | collective-permute-done | bytes 262176 | tf_op jit(solution)/shard_map/ppermute | solution.py:202
  172.1 2.3 %collective-permute-done.27.third = bf16[128,1024]{1,0:T(8,128)(2,1)S(1)} collective-permute-done((bf16[128,1024]{1,0:T(8,128)(2,1)S(1)}, bf16[128,1024]{1,0:T(8,128)(2,1)S(1)}, u32[]{:S(2)}, u32[]{:S(2)}) %collective-permute-start.27) | collective-permute-done | bytes 262176 | tf_op jit(solution)/shard_map/ppermute | solution.py:202
  174.4 1.4 finish.1
  (54 shorter events, 0.5 us)
Async XLA Ops:
  0.0 10.0 %copy-start.6 = (bf16[32,2048]{1,0:T(8,128)(2,1)S(1)}, bf16[32,2048]{1,0:T(8,128)(2,1)}, u32[]{:S(2)}) copy-start(bf16[32,2048]{1,0:T(8,128)(2,1)} %param.13) | copy-start | bytes 393220
  0.0 8.8 %copy-start.4 = (bf16[128,2048]{1,0:T(8,128)(2,1)S(1)}, bf16[128,2048]{1,0:T(8,128)(2,1)}, u32[]{:S(2)}) copy-start(bf16[128,2048]{1,0:T(8,128)(2,1)} %param.12) | copy-start | bytes 1572868
  0.0 10.1 %copy-start.9 = (s32[8]{0:T(128)S(1)}, s32[8]{0:T(128)}, u32[]{:S(2)}) copy-start(s32[8]{0:T(128)} %param.22) | copy-start | bytes 100
  0.0 10.3 %copy-start = (bf16[256,512]{1,0:T(8,128)(2,1)S(1)}, bf16[256,512]{1,0:T(8,128)(2,1)}, u32[]{:S(2)}) copy-start(bf16[256,512]{1,0:T(8,128)(2,1)} %refs_0_.2) | copy-start | bytes 786436
  0.0 10.2 %copy-start.1 = (bf16[256,512]{1,0:T(8,128)(2,1)S(1)}, bf16[256,512]{1,0:T(8,128)(2,1)}, u32[]{:S(2)}) copy-start(bf16[256,512]{1,0:T(8,128)(2,1)} %refs_1_.1) | copy-start | bytes 786436
  0.0 10.2 %copy-start.2 = (bf16[64,512]{1,0:T(8,128)(2,1)S(1)}, bf16[64,512]{1,0:T(8,128)(2,1)}, u32[]{:S(2)}) copy-start(bf16[64,512]{1,0:T(8,128)(2,1)} %refs_2_.1) | copy-start | bytes 196612
  0.0 10.2 %copy-start.3 = (bf16[64,512]{1,0:T(8,128)(2,1)S(1)}, bf16[64,512]{1,0:T(8,128)(2,1)}, u32[]{:S(2)}) copy-start(bf16[64,512]{1,0:T(8,128)(2,1)} %refs_3_.1) | copy-start | bytes 196612
  0.0 39.5 %collective-permute-start.10 = (bf16[256,2048]{1,0:T(8,128)(2,1)}, bf16[256,2048]{1,0:T(8,128)(2,1)}, u32[]{:S(2)}, u32[]{:S(2)}) collective-permute-start(bf16[256,2048]{1,0:T(8,128)(2,1)} %refs_0_.3), channel_id=1, source_target_pairs={{0,4},{1,3},{2,6},{3,1},{4,0},{5,7},{6,2},{7,5},{8,12},{9,11},{10,... | collective-permute-start | bytes 3145736 | tf_op jit(solution)/shard_map/ppermute | solution.py:202
  1.6 37.9 %collective-permute-start.9 = (bf16[256,2048]{1,0:T(8,128)(2,1)}, bf16[256,2048]{1,0:T(8,128)(2,1)}, u32[]{:S(2)}, u32[]{:S(2)}) collective-permute-start(bf16[256,2048]{1,0:T(8,128)(2,1)} %refs_0_.3), channel_id=1, source_target_pairs={{0,2},{1,5},{2,0},{3,7},{4,6},{5,1},{6,4},{7,3},{8,10},{9,13},{10,... | collective-permute-start | bytes 3145736 | tf_op jit(solution)/shard_map/ppermute | solution.py:202
  10.3 6.4 %copy-start.5 = (bf16[2048,256]{1,0:T(8,128)(2,1)S(1)}, bf16[2048,256]{1,0:T(8,128)(2,1)}, u32[]{:S(2)}) copy-start(bf16[2048,256]{1,0:T(8,128)(2,1)} %param.18) | copy-start | bytes 3145732
  11.2 13.8 %collective-permute-start.2 = (bf16[336,512]{1,0:T(8,128)(2,1)S(1)}, bf16[336,512]{1,0:T(8,128)(2,1)S(1)}, u32[]{:S(2)}, u32[]{:S(2)}) collective-permute-start(bf16[336,512]{1,0:T(8,128)(2,1)S(1)} %get-tuple-element.45), channel_id=1, source_target_pairs={{0,8},{1,9},{2,10},{3,11},{4,12},{5,13},{6,14},{7,15},{8,0},{9,1},... | collective-permute-start | bytes 1032200 | tf_op jit(solution)/shard_map/ppermute | solution.py:202
  11.7 13.3 %collective-permute-start.1 = (bf16[32,2048]{1,0:T(8,128)(2,1)S(1)}, bf16[32,2048]{1,0:T(8,128)(2,1)S(1)}, u32[]{:S(2)}, u32[]{:S(2)}) collective-permute-start(bf16[32,2048]{1,0:T(8,128)(2,1)S(1)} %fusion.5), channel_id=1, source_target_pairs={{0,0},{1,16},{2,1},{3,17},{4,8},{5,24},{6,9},{7,25},{8,2},{9,18},{... | collective-permute-start | bytes 393224 | tf_op jit(solution)/shard_map/ppermute | solution.py:202
  15.2 15.5 %collective-permute-start = (bf16[144,2048]{1,0:T(8,128)(2,1)S(1)}, bf16[144,2048]{1,0:T(8,128)(2,1)}, u32[]{:S(2)}, u32[]{:S(2)}) collective-permute-start(bf16[144,2048]{1,0:T(8,128)(2,1)S(1)} %fusion.2), channel_id=1, source_target_pairs={{1,16},{3,18},{5,20},{7,22},{9,24},{11,26},{13,28},{15,30},{16,1},... | collective-permute-start | bytes 1769480 | tf_op jit(solution)/shard_map/ppermute | solution.py:202
  25.1 13.8 %collective-permute-start.7 = (bf16[2,256,512]{2,1,0:T(8,128)(2,1)S(1)}, bf16[2,256,512]{2,1,0:T(8,128)(2,1)S(1)}, u32[]{:S(2)}, u32[]{:S(2)}) collective-permute-start(bf16[2,256,512]{2,1,0:T(8,128)(2,1)S(1)} %pad_maximum_fusion.3.own), channel_id=1, source_target_pairs={{0,2},{1,5},{2,0},{3,7},{4,6},{5,1},{6,4},{7,3},{8,10},{9,13},{10,... | collective-permute-start | bytes 1572872 | tf_op jit(solution)/shard_map/ppermute | solution.py:202
  30.8 31.1 %collective-permute-start.3 = (bf16[176,2048]{1,0:T(8,128)(2,1)S(1)}, bf16[176,2048]{1,0:T(8,128)(2,1)S(1)}, u32[]{:S(2)}, u32[]{:S(2)}) collective-permute-start(bf16[176,2048]{1,0:T(8,128)(2,1)S(1)} %pad_maximum_fusion.2.x0), channel_id=1, source_target_pairs={{0,8},{1,9},{2,10},{3,11},{4,12},{5,13},{6,14},{7,15},{8,0},{9,1},... | collective-permute-start | bytes 2162696 | tf_op jit(solution)/shard_map/ppermute | solution.py:202
  30.9 31.0 %collective-permute-start.4 = (bf16[1024,256]{1,0:T(8,128)(2,1)S(1)}, bf16[1024,256]{1,0:T(8,128)(2,1)S(1)}, u32[]{:S(2)}, u32[]{:S(2)}) collective-permute-start(bf16[1024,256]{1,0:T(8,128)(2,1)S(1)} %get-tuple-element.49), channel_id=1, source_target_pairs={{0,16},{1,17},{2,18},{3,19},{4,20},{5,21},{6,22},{7,23},{8,24},{9,... | collective-permute-start | bytes 1572872 | tf_op jit(solution)/shard_map/ppermute | solution.py:202
  39.0 24.8 %collective-permute-start.8 = (bf16[4,256,512]{2,1,0:T(8,128)(2,1)S(1)}, bf16[4,256,512]{2,1,0:T(8,128)(2,1)S(1)}, u32[]{:S(2)}, u32[]{:S(2)}) collective-permute-start(bf16[4,256,512]{2,1,0:T(8,128)(2,1)S(1)} %pad_maximum_fusion), channel_id=1, source_target_pairs={{0,4},{1,3},{2,6},{3,1},{4,0},{5,7},{6,2},{7,5},{8,12},{9,11},{10,... | collective-permute-start | bytes 3145736 | tf_op jit(solution)/shard_map/ppermute | solution.py:202
  39.6 25.6 %collective-permute-start.11 = (bf16[256,2048]{1,0:T(8,128)(2,1)}, bf16[256,2048]{1,0:T(8,128)(2,1)S(1)}, u32[]{:S(2)}, u32[]{:S(2)}) collective-permute-start(bf16[256,2048]{1,0:T(8,128)(2,1)} %collective-permute-done.9.refs_1_), channel_id=1, source_target_pairs={{0,4},{1,3},{2,6},{3,1},{4,0},{5,7},{6,2},{7,5},{8,12},{9,11},{10,... | collective-permute-start | bytes 3145736 | tf_op jit(solution)/shard_map/ppermute | solution.py:202
  41.2 22.6 %collective-permute-start.6 = (bf16[176,2048]{1,0:T(8,128)(2,1)S(1)}, bf16[176,2048]{1,0:T(8,128)(2,1)S(1)}, u32[]{:S(2)}, u32[]{:S(2)}) collective-permute-start(bf16[176,2048]{1,0:T(8,128)(2,1)S(1)} %pad_maximum_fusion.2.x0), channel_id=1, source_target_pairs={{0,1},{1,0},{2,3},{3,2},{4,5},{5,4},{6,7},{7,6},{8,9},{9,8},{10,11... | collective-permute-start | bytes 2162696 | tf_op jit(solution)/shard_map/ppermute | solution.py:202
  61.9 2.2 %collective-permute-start.5 = (bf16[176,2048]{1,0:T(8,128)(2,1)S(1)}, bf16[176,2048]{1,0:T(8,128)(2,1)S(1)}, u32[]{:S(2)}, u32[]{:S(2)}) collective-permute-start(bf16[176,2048]{1,0:T(8,128)(2,1)S(1)} %collective-permute-done.3.x1), channel_id=1, source_target_pairs={{0,1},{1,0},{2,3},{3,2},{4,5},{5,4},{6,7},{7,6},{8,9},{9,8},{10,11... | collective-permute-start | bytes 2162696 | tf_op jit(solution)/shard_map/ppermute | solution.py:202
  65.1 2.1 %copy-start.7 = (bf16[256,2048]{1,0:T(8,128)(2,1)}, bf16[256,2048]{1,0:T(8,128)(2,1)S(1)}, u32[]{:S(2)}) copy-start(bf16[256,2048]{1,0:T(8,128)(2,1)S(1)} %collective-permute-done.11.refs_3_) | copy-start | bytes 3145732
  67.2 18.1 %collective-permute-start.15 = (bf16[736,256]{1,0:T(8,128)(2,1)S(1)}, bf16[736,256]{1,0:T(8,128)(2,1)S(1)}, u32[]{:S(2)}, u32[]{:S(2)}) collective-permute-start(bf16[736,256]{1,0:T(8,128)(2,1)S(1)} %get-tuple-element.69), channel_id=1, source_target_pairs={{0,16},{1,17},{2,18},{3,19},{4,20},{5,21},{6,22},{7,23},{8,24},{9,... | collective-permute-start | bytes 1130504 | tf_op jit(solution)/shard_map/ppermute | solution.py:202
  74.7 20.3 %collective-permute-start.13 = (bf16[4,128,512]{2,1,0:T(8,128)(2,1)S(1)}, bf16[4,128,512]{2,1,0:T(8,128)(2,1)S(1)}, u32[]{:S(2)}, u32[]{:S(2)}) collective-permute-start(bf16[4,128,512]{2,1,0:T(8,128)(2,1)S(1)} %get-tuple-element.67), channel_id=1, source_target_pairs={{0,8},{1,9},{2,10},{3,11},{4,12},{5,13},{6,14},{7,15},{8,0},{9,1},... | collective-permute-start | bytes 1572872 | tf_op jit(solution)/shard_map/ppermute | solution.py:202
  74.7 40.0 %collective-permute-start.18 = (bf16[2,1024,256]{2,1,0:T(8,128)(2,1)S(1)}, bf16[2,1024,256]{2,1,0:T(8,128)(2,1)S(1)}, u32[]{:S(2)}, u32[]{:S(2)}) collective-permute-start(bf16[2,1024,256]{2,1,0:T(8,128)(2,1)S(1)} %pad_maximum_fusion.1.refs_4_), channel_id=1, source_target_pairs={{0,2},{1,5},{2,0},{3,7},{4,6},{5,1},{6,4},{7,3},{8,10},{9,13},{10,... | collective-permute-start | bytes 3145736 | tf_op jit(solution)/shard_map/ppermute | solution.py:202
  86.4 12.9 %collective-permute-start.19 = (bf16[6,128,256]{2,1,0:T(8,128)(2,1)S(1)}, bf16[6,128,256]{2,1,0:T(8,128)(2,1)S(1)}, u32[]{:S(2)}, u32[]{:S(2)}) collective-permute-start(bf16[6,128,256]{2,1,0:T(8,128)(2,1)S(1)} %keys_join.1.kv0), channel_id=1, source_target_pairs={{0,4},{1,3},{2,6},{3,1},{4,0},{5,7},{6,2},{7,5},{8,12},{9,11},{10,... | collective-permute-start | bytes 1179656 | tf_op jit(solution)/shard_map/ppermute | solution.py:202
  87.0 29.3 %collective-permute-start.12 = (bf16[4,128,512]{2,1,0:T(8,128)(2,1)S(1)}, bf16[4,128,512]{2,1,0:T(8,128)(2,1)S(1)}, u32[]{:S(2)}, u32[]{:S(2)}) collective-permute-start(bf16[4,128,512]{2,1,0:T(8,128)(2,1)S(1)} %get-tuple-element.65), channel_id=1, source_target_pairs={{0,8},{1,9},{2,10},{3,11},{4,12},{5,13},{6,14},{7,15},{8,0},{9,1},... | collective-permute-start | bytes 1572872 | tf_op jit(solution)/shard_map/ppermute | solution.py:202
  95.1 23.5 %collective-permute-start.14 = (bf16[4,128,512]{2,1,0:T(8,128)(2,1)S(1)}, bf16[4,128,512]{2,1,0:T(8,128)(2,1)S(1)}, u32[]{:S(2)}, u32[]{:S(2)}) collective-permute-start(bf16[4,128,512]{2,1,0:T(8,128)(2,1)S(1)} %add_convert_fusion), channel_id=1, source_target_pairs={{0,16},{1,17},{2,18},{3,19},{4,20},{5,21},{6,22},{7,23},{8,24},{9,... | collective-permute-start | bytes 1572872 | tf_op jit(solution)/shard_map/ppermute | solution.py:202
  98.3 9.6 %collective-permute-start.16 = (bf16[6,128,256]{2,1,0:T(8,128)(2,1)S(1)}, bf16[6,128,256]{2,1,0:T(8,128)(2,1)S(1)}, u32[]{:S(2)}, u32[]{:S(2)}) collective-permute-start(bf16[6,128,256]{2,1,0:T(8,128)(2,1)S(1)} %keys_join.1.kv0), channel_id=1, source_target_pairs={{0,2},{1,5},{2,0},{3,7},{4,6},{5,1},{6,4},{7,3},{8,10},{9,13},{10,... | collective-permute-start | bytes 1179656 | tf_op jit(solution)/shard_map/ppermute | solution.py:202
  99.3 15.5 %collective-permute-start.17 = (bf16[6,128,256]{2,1,0:T(8,128)(2,1)S(1)}, bf16[6,128,256]{2,1,0:T(8,128)(2,1)S(1)}, u32[]{:S(2)}, u32[]{:S(2)}) collective-permute-start(bf16[6,128,256]{2,1,0:T(8,128)(2,1)S(1)} %keys_join.1.kv0), channel_id=1, source_target_pairs={{0,6},{1,7},{2,4},{3,5},{4,2},{5,3},{6,0},{7,1},{8,14},{9,15},{10,... | collective-permute-start | bytes 1179656 | tf_op jit(solution)/shard_map/ppermute | solution.py:202
  108.0 30.6 %collective-permute-start.22 = (bf16[2,1024,256]{2,1,0:T(8,128)(2,1)S(1)}, bf16[2,1024,256]{2,1,0:T(8,128)(2,1)S(1)}, u32[]{:S(2)}, u32[]{:S(2)}) collective-permute-start(bf16[2,1024,256]{2,1,0:T(8,128)(2,1)S(1)} %pad_maximum_fusion.1.refs_4_), channel_id=1, source_target_pairs={{0,4},{1,3},{2,6},{3,1},{4,0},{5,7},{6,2},{7,5},{8,12},{9,11},{10,... | collective-permute-start | bytes 3145736 | tf_op jit(solution)/shard_map/ppermute | solution.py:202
  114.7 23.8 %collective-permute-start.23 = (bf16[2,1024,256]{2,1,0:T(8,128)(2,1)S(1)}, bf16[2,1024,256]{2,1,0:T(8,128)(2,1)S(1)}, u32[]{:S(2)}, u32[]{:S(2)}) collective-permute-start(bf16[2,1024,256]{2,1,0:T(8,128)(2,1)S(1)} %collective-permute-done.18.refs_5_), channel_id=1, source_target_pairs={{0,4},{1,3},{2,6},{3,1},{4,0},{5,7},{6,2},{7,5},{8,12},{9,11},{10,... | collective-permute-start | bytes 3145736 | tf_op jit(solution)/shard_map/ppermute | solution.py:202
  123.3 9.0 %collective-permute-start.21 = (bf16[512,256]{1,0:T(8,128)(2,1)S(1)}, bf16[512,256]{1,0:T(8,128)(2,1)S(1)}, u32[]{:S(2)}, u32[]{:S(2)}) collective-permute-start(bf16[512,256]{1,0:T(8,128)(2,1)S(1)} %attend.3.refs_1_), channel_id=1, source_target_pairs={{0,8},{1,9},{2,10},{3,11},{4,12},{5,13},{6,14},{7,15},{8,0},{9,1},... | collective-permute-start | bytes 786440 | tf_op jit(solution)/shard_map/ppermute | solution.py:202
  132.1 6.4 %collective-permute-start.20 = (bf16[512,256]{1,0:T(8,128)(2,1)S(1)}, bf16[512,256]{1,0:T(8,128)(2,1)S(1)}, u32[]{:S(2)}, u32[]{:S(2)}) collective-permute-start(bf16[512,256]{1,0:T(8,128)(2,1)S(1)} %attend.2.refs_0_), channel_id=1, source_target_pairs={{0,8},{1,9},{2,10},{3,11},{4,12},{5,13},{6,14},{7,15},{8,0},{9,1},... | collective-permute-start | bytes 786440 | tf_op jit(solution)/shard_map/ppermute | solution.py:202
  138.6 1.0 copy-start.8
  143.5 2.7 %collective-permute-start.24 = (bf16[4,128,1024]{2,1,0:T(8,128)(2,1)S(1)}, bf16[4,128,1024]{2,1,0:T(8,128)(2,1)S(1)}, u32[]{:S(2)}, u32[]{:S(2)}) collective-permute-start(bf16[4,128,1024]{2,1,0:T(8,128)(2,1)S(1)} %get-tuple-element.78), channel_id=1, source_target_pairs={{0,1},{1,0},{2,3},{3,2},{4,5},{5,4},{6,7},{7,6},{8,9},{9,8},{10,11... | collective-permute-start | bytes 3145736 | tf_op jit(solution)/shard_map/ppermute | solution.py:202
  148.0 19.1 %collective-permute-start.25 = (bf16[128,1024]{1,0:T(8,128)(2,1)S(1)}, bf16[128,1024]{1,0:T(8,128)(2,1)S(1)}, u32[]{:S(2)}, u32[]{:S(2)}) collective-permute-start(bf16[128,1024]{1,0:T(8,128)(2,1)S(1)} %get-tuple-element.83), channel_id=1, source_target_pairs={{0,8},{1,9},{2,10},{3,11},{4,12},{5,13},{6,14},{7,15},{8,16},{9,17... | collective-permute-start | bytes 786440 | tf_op jit(solution)/shard_map/ppermute | solution.py:202
  149.4 22.7 %collective-permute-start.26 = (bf16[128,1024]{1,0:T(8,128)(2,1)S(1)}, bf16[128,1024]{1,0:T(8,128)(2,1)S(1)}, u32[]{:S(2)}, u32[]{:S(2)}) collective-permute-start(bf16[128,1024]{1,0:T(8,128)(2,1)S(1)} %get-tuple-element.82), channel_id=1, source_target_pairs={{0,16},{1,17},{2,18},{3,19},{4,20},{5,21},{6,22},{7,23},{8,24},{9,... | collective-permute-start | bytes 786440 | tf_op jit(solution)/shard_map/ppermute | solution.py:202
  151.1 23.2 %collective-permute-start.27 = (bf16[128,1024]{1,0:T(8,128)(2,1)S(1)}, bf16[128,1024]{1,0:T(8,128)(2,1)S(1)}, u32[]{:S(2)}, u32[]{:S(2)}) collective-permute-start(bf16[128,1024]{1,0:T(8,128)(2,1)S(1)} %get-tuple-element.81), channel_id=1, source_target_pairs={{0,24},{1,25},{2,26},{3,27},{4,28},{5,29},{6,30},{7,31},{8,0},{9,1... | collective-permute-start | bytes 786440 | tf_op jit(solution)/shard_map/ppermute | solution.py:202

commit v19 on v17

--- a/solution.py
+++ b/solution.py
@@ -631,10 +631,10 @@
     kv_near, kv_far = to_near(kv), to_far(kv)
     kv_both = permuted(kv, lambda z, p, c: (z, p ^ 3, c))
 
-    kv_near, kv_far, kv_both, out_near, out_pair = lax.optimization_barrier(
-        (kv_near, kv_far, kv_both, out_near, out_pair)
-    )
-    out_far, out_both = to_far(out_pair), to_far(out_near)
+    kv_far, out_pair = lax.optimization_barrier((kv_far, out_pair))
+    out_far = to_far(out_pair)
+    kv_near, kv_both, out_near = lax.optimization_barrier((kv_near, kv_both, out_near))
+    out_both = to_far(out_near)
 
     attended = [
         pl.pallas_call(

time: 179 us -> 180 us (level)
  starting transfers between devices: 54.3 us -> 56.6 us
  waiting for transfers between devices: 84 us -> 82 us
    ppermute x29, starting transfers between devices: 54.3 us -> 56.6 us  [permuted(): return lax.ppermute(value, ('seq', 'head'), perm)]
    ppermute x29, waiting for transfers between devices: 84 us -> 82 us  [permuted(): return lax.ppermute(value, ('seq', 'head'), perm)]
  transfers between devices with their start and end apart: 29 -> 29, of which waited for: 18 -> 16; matrix products, arithmetic and copies ran while one was open for 5% -> 5% of each run, Pallas kernels for 10% -> 10%
where the time goes in v19:
time: 180 us; the launch traced here: 177 us
  waiting for transfers between devices  82 us (46%)
  starting transfers between devices  56.6 us (31%)
  Pallas kernels  23.8 us (13%)
  other arithmetic  9.89 us (5%)
  blocking collectives  2.46 us (1%)
  local copies, waits for them, and re-layouts  2.29 us (1%)
    ppermute x29, waiting for transfers between devices, permuted(): return lax.ppermute(value, ('seq', 'head'), perm)  82 us
    ppermute x29, starting transfers between devices, permuted(): return lax.ppermute(value, ('seq', 'head'), perm)  56.6 us
    pallas_call x2, Pallas kernels, by_levels(): pl.pallas_call(functools.partial(attend_kernel, pair), out_shape=shaped((...  9.46 us
    pallas_call x1, Pallas kernels, by_levels(): pl.pallas_call(queries_part_kernel, out_shape=(shaped(group_shape, jnp.fl...  4.99 us
    pallas_call x1, Pallas kernels, by_levels(): pl.pallas_call(output_kernel, out_shape=(shaped((LEVELS, tok, wide_cols),...  3.89 us
  transfers between devices with their start and end apart: 29, of which 16 were waited for; matrix products, arithmetic and copies ran while one was open for 5% of the time, Pallas kernels for 10%

profile of v19, /device:TPU:8, one launch (start us, length us, event | category | flops | bytes accessed | tf_op | source)
XLA Modules:
  0.0 177.4 jit_solution(17419413392006761948)
XLA Ops:
  0.0 1.6 collective-permute-start.3
  1.6 1.5 collective-permute-start.4
  3.1 1.0 fusion.3
  4.2 1.4 fusion
  5.6 2.5 %all-reduce.1 = (f32[144]{0:T(256)S(1)}, f32[32]{0:T(128)S(1)}) all-reduce(f32[144]{0:T(256)S(1)} %fusion, f32[32]{0:T(128)S(1)} %fusion.3), channel_id=1, replica_groups=mesh['seq'=16,'head'=2] {'head'}, use_global_device_ids=true, to_apply=%region_1.2 | all-reduce | flops 176 | bytes 1408 | tf_op jit(solution)/shard_map/psum | solution.py:518
  8.1 0.7 dynamic_slice.9
  8.8 1.0 fusion.5
  9.8 1.2 fusion.2
  11.1 2.3 %collective-permute-start.1 = (bf16[32,2048]{1,0:T(8,128)(2,1)S(1)}, bf16[32,2048]{1,0:T(8,128)(2,1)}, u32[]{:S(2)}, u32[]{:S(2)}) collective-permute-start(bf16[32,2048]{1,0:T(8,128)(2,1)S(1)} %fusion.5), channel_id=1, source_target_pairs={{0,0},{1,16},{2,1},{3,17},{4,8},{5,24},{6,9},{7,25},{8,2},{9,18},{... | collective-permute-start | bytes 393224 | tf_op jit(solution)/shard_map/ppermute | solution.py:202
  13.4 1.5 collective-permute-start
  14.9 0.1 stack.41.where_ref
  15.0 0.9 pack.1
  16.0 0.2 copy-done.5
  16.3 3.4 %collective-permute-done.1 = bf16[32,2048]{1,0:T(8,128)(2,1)} collective-permute-done((bf16[32,2048]{1,0:T(8,128)(2,1)S(1)}, bf16[32,2048]{1,0:T(8,128)(2,1)}, u32[]{:S(2)}, u32[]{:S(2)}) %collective-permute-start.1) | collective-permute-done | bytes 131104 | tf_op jit(solution)/shard_map/ppermute | solution.py:202
  19.7 8.3 %collective-permute-done.2 = bf16[336,512]{1,0:T(8,128)(2,1)S(1)} collective-permute-done((bf16[336,512]{1,0:T(8,128)(2,1)S(1)}, bf16[336,512]{1,0:T(8,128)(2,1)S(1)}, u32[]{:S(2)}, u32[]{:S(2)}) %collective-permute-start.2) | collective-permute-done | bytes 344096 | tf_op jit(solution)/shard_map/ppermute | solution.py:202
  28.0 0.1 collective-permute-done.4.refs_2_
  28.2 2.8 %collective-permute-start.10 = (bf16[2,256,512]{2,1,0:T(8,128)(2,1)S(1)}, bf16[2,256,512]{2,1,0:T(8,128)(2,1)S(1)}, u32[]{:S(2)}, u32[]{:S(2)}) collective-permute-start(bf16[2,256,512]{2,1,0:T(8,128)(2,1)S(1)} %pad_maximum_fusion.3.own), channel_id=1, source_target_pairs={{0,2},{1,5},{2,0},{3,7},{4,6},{5,1},{6,4},{7,3},{8,10},{9,13},{10,... | collective-permute-start | bytes 1572872 | tf_op jit(solution)/shard_map/ppermute | solution.py:202
  31.1 1.0 pad_maximum_fusion.2.x0
  32.0 1.3 collective-permute-start.5
  33.3 7.5 %collective-permute-start.6 = (bf16[768,256]{1,0:T(8,128)(2,1)S(1)}, bf16[768,256]{1,0:T(8,128)(2,1)S(1)}, u32[]{:S(2)}, u32[]{:S(2)}) collective-permute-start(bf16[768,256]{1,0:T(8,128)(2,1)S(1)} %slice.42), channel_id=1, source_target_pairs={{0,16},{1,17},{2,18},{3,19},{4,20},{5,21},{6,22},{7,23},{8,24},{9,... | collective-permute-start | bytes 1179656 | tf_op jit(solution)/shard_map/ppermute | solution.py:202
  40.8 0.1 pad_maximum_fusion
  40.9 0.4 collective-permute-start.11
  41.5 6.9 %collective-permute-start.9 = (bf16[176,2048]{1,0:T(8,128)(2,1)S(1)}, bf16[176,2048]{1,0:T(8,128)(2,1)S(1)}, u32[]{:S(2)}, u32[]{:S(2)}) collective-permute-start(bf16[176,2048]{1,0:T(8,128)(2,1)S(1)} %pad_maximum_fusion.2.x0), channel_id=1, source_target_pairs={{0,1},{1,0},{2,3},{3,2},{4,5},{5,4},{6,7},{7,6},{8,9},{9,8},{10,11... | collective-permute-start | bytes 2162696 | tf_op jit(solution)/shard_map/ppermute | solution.py:202
  48.4 11.8 %collective-permute-done.6 = bf16[768,256]{1,0:T(8,128)(2,1)S(1)} collective-permute-done((bf16[768,256]{1,0:T(8,128)(2,1)S(1)}, bf16[768,256]{1,0:T(8,128)(2,1)S(1)}, u32[]{:S(2)}, u32[]{:S(2)}) %collective-permute-start.6) | collective-permute-done | bytes 393248 | tf_op jit(solution)/shard_map/ppermute | solution.py:202
  60.3 1.4 fusion.9
  61.7 0.2 pad_maximum_fusion.4.cos_ref
  61.9 0.2 pad_maximum_fusion.5.sin_ref
  62.1 1.7 collective-permute-start.18
  63.9 2.1 %keys_part.1 = (f32[576,256]{1,0:T(8,128)S(1)}, bf16[736,256]{1,0:T(8,128)(2,1)S(1)}) custom-call(s32[5]{0:T(128)S(1)} %stack.41.where_ref, bf16[176,2048]{1,0:T(8,128)(2,1)S(1)} %pad_maximum_fusion.2.x0, bf16[176,2048]{1,0:T(8,128)(2,1)S(1)} %collective-permute-done.5.x1, bf16[176,2048]{1,0:T(8,128)(2,1)S(1)} %collective-permute-done.9.x2, ...), custom_call_target="tpu_custom_call" | custom-call | flops 3000000000 | bytes 4000000 | tf_op jit(solution)/shard_map/keys_part/pallas_call | solution.py:583
  66.0 1.6 collective-permute-start.15
  67.5 5.0 %queries_part.1 = (f32[4,128,512]{2,1,0:T(8,128)S(1)}, f32[4,128,512]{2,1,0:T(8,128)S(1)}, bf16[4,128,512]{2,1,0:T(8,128)(2,1)S(1)}, bf16[4,128,512]{2,1,0:T(8,128)(2,1)S(1)}) custom-call(s32[5]{0:T(128)S(1)} %stack.41.where_ref, bf16[176,2048]{1,0:T(8,128)(2,1)S(1)} %pad_maximum_fusion.2.x0, bf16[176,2048]{1,0:T(8,128)(2,1)S(1)} %collective-permute-done.5.x1, ...), custom_call_target="tpu_custom_call" | custom-call | flops 5000000000 | bytes 4000000 | tf_op jit(solution)/shard_map/queries_part/pallas_call | solution.py:600
  72.5 0.4 collective-permute-start.13
  72.9 4.7 %collective-permute-done.18 = bf16[256,256]{1,0:T(8,128)(2,1)S(1)} collective-permute-done((bf16[256,256]{1,0:T(8,128)(2,1)S(1)}, bf16[256,256]{1,0:T(8,128)(2,1)S(1)}, u32[]{:S(2)}, u32[]{:S(2)}) %collective-permute-start.18) | collective-permute-done | bytes 131104 | tf_op jit(solution)/shard_map/ppermute | solution.py:202
  77.7 0.1 pad_maximum_fusion.1.refs_4_
  77.8 1.1 collective-permute-start.19
  78.9 6.8 %collective-permute-done.15.got_ref = bf16[736,256]{1,0:T(8,128)(2,1)S(1)} collective-permute-done((bf16[736,256]{1,0:T(8,128)(2,1)S(1)}, bf16[736,256]{1,0:T(8,128)(2,1)S(1)}, u32[]{:S(2)}, u32[]{:S(2)}) %collective-permute-start.15) | collective-permute-done | bytes 376864 | tf_op jit(solution)/shard_map/ppermute | solution.py:202
  85.7 1.0 keys_join.1.kv0
  86.7 1.0 collective-permute-start.20
  87.7 2.6 %collective-permute-start.12 = (bf16[4,128,512]{2,1,0:T(8,128)(2,1)S(1)}, bf16[4,128,512]{2,1,0:T(8,128)(2,1)S(1)}, u32[]{:S(2)}, u32[]{:S(2)}) collective-permute-start(bf16[4,128,512]{2,1,0:T(8,128)(2,1)S(1)} %get-tuple-element.65), channel_id=1, source_target_pairs={{0,8},{1,9},{2,10},{3,11},{4,12},{5,13},{6,14},{7,15},{8,0},{9,1},... | collective-permute-start | bytes 1572872 | tf_op jit(solution)/shard_map/ppermute | solution.py:202
  90.4 3.6 %collective-permute-done.13 = bf16[4,128,512]{2,1,0:T(8,128)(2,1)S(1)} collective-permute-done((bf16[4,128,512]{2,1,0:T(8,128)(2,1)S(1)}, bf16[4,128,512]{2,1,0:T(8,128)(2,1)S(1)}, u32[]{:S(2)}, u32[]{:S(2)}) %collective-permute-start.13) | collective-permute-done | bytes 524320 | tf_op jit(solution)/shard_map/ppermute | solution.py:202
  93.9 0.2 add_convert_fusion
  94.1 5.2 %collective-permute-start.14 = (bf16[4,128,512]{2,1,0:T(8,128)(2,1)S(1)}, bf16[4,128,512]{2,1,0:T(8,128)(2,1)S(1)}, u32[]{:S(2)}, u32[]{:S(2)}) collective-permute-start(bf16[4,128,512]{2,1,0:T(8,128)(2,1)S(1)} %add_convert_fusion), channel_id=1, source_target_pairs={{0,16},{1,17},{2,18},{3,19},{4,20},{5,21},{6,22},{7,23},{8,24},{9,... | collective-permute-start | bytes 1572872 | tf_op jit(solution)/shard_map/ppermute | solution.py:202
  99.3 3.3 %collective-permute-start.16 = (bf16[6,128,256]{2,1,0:T(8,128)(2,1)S(1)}, bf16[6,128,256]{2,1,0:T(8,128)(2,1)S(1)}, u32[]{:S(2)}, u32[]{:S(2)}) collective-permute-start(bf16[6,128,256]{2,1,0:T(8,128)(2,1)S(1)} %keys_join.1.kv0), channel_id=1, source_target_pairs={{0,2},{1,5},{2,0},{3,7},{4,6},{5,1},{6,4},{7,3},{8,10},{9,13},{10,... | collective-permute-start | bytes 1179656 | tf_op jit(solution)/shard_map/ppermute | solution.py:202
  102.7 8.1 %collective-permute-done.17.kv3 = bf16[6,128,256]{2,1,0:T(8,128)(2,1)S(1)} collective-permute-done((bf16[6,128,256]{2,1,0:T(8,128)(2,1)S(1)}, bf16[6,128,256]{2,1,0:T(8,128)(2,1)S(1)}, u32[]{:S(2)}, u32[]{:S(2)}) %collective-permute-start.17) | collective-permute-done | bytes 393248 | tf_op jit(solution)/shard_map/ppermute | solution.py:202
  110.7 5.5 %collective-permute-done.16.kv1 = bf16[6,128,256]{2,1,0:T(8,128)(2,1)S(1)} collective-permute-done((bf16[6,128,256]{2,1,0:T(8,128)(2,1)S(1)}, bf16[6,128,256]{2,1,0:T(8,128)(2,1)S(1)}, u32[]{:S(2)}, u32[]{:S(2)}) %collective-permute-start.16) | collective-permute-done | bytes 393248 | tf_op jit(solution)/shard_map/ppermute | solution.py:202
  116.2 3.5 %collective-permute-start.24 = (bf16[2,1024,256]{2,1,0:T(8,128)(2,1)S(1)}, bf16[2,1024,256]{2,1,0:T(8,128)(2,1)S(1)}, u32[]{:S(2)}, u32[]{:S(2)}) collective-permute-start(bf16[2,1024,256]{2,1,0:T(8,128)(2,1)S(1)} %collective-permute-done.19.refs_5_), channel_id=1, source_target_pairs={{0,4},{1,3},{2,6},{3,1},{4,0},{5,7},{6,2},{7,5},{8,12},{9,11},{10,... | collective-permute-start | bytes 3145736 | tf_op jit(solution)/shard_map/ppermute | solution.py:202
  119.7 0.5 collective-permute-done.14.got_ref
  120.2 4.6 %attend.2.refs_0_ = bf16[512,256]{1,0:T(8,128)(2,1)S(1)} custom-call(s32[5]{0:T(128)S(1)} %stack.41.where_ref, f32[4,128,512]{2,1,0:T(8,128)S(1)} %get-tuple-element.64.keep_ref, bf16[4,128,512]{2,1,0:T(8,128)(2,1)S(1)} %collective-permute-done.12.near_ref, bf16[4,128,512]{2,1,0:T(8,128)(2,1)S(1)} %collective-permute-done.14.got_ref, ...), custom_call_target="tpu_custom_call" | custom-call | flops 4000000000 | bytes 4000000 | tf_op jit(solution)/shard_map/attend/pallas_call | solution.py:640
  124.9 1.7 collective-permute-start.21
  126.6 4.8 %attend.3.refs_1_ = bf16[512,256]{1,0:T(8,128)(2,1)S(1)} custom-call(s32[5]{0:T(128)S(1)} %stack.41.where_ref, f32[4,128,512]{2,1,0:T(8,128)S(1)} %get-tuple-element.64.keep_ref, bf16[4,128,512]{2,1,0:T(8,128)(2,1)S(1)} %collective-permute-done.12.near_ref, bf16[4,128,512]{2,1,0:T(8,128)(2,1)S(1)} %collective-permute-done.14.got_ref, ...), custom_call_target="tpu_custom_call" | custom-call | flops 4000000000 | bytes 4000000 | tf_op jit(solution)/shard_map/attend/pallas_call | solution.py:640
  131.4 0.4 collective-permute-start.22
  131.9 0.1 collective-permute-done.21.refs_2_
  132.0 5.9 %collective-permute-done.22.refs_3_ = bf16[512,256]{1,0:T(8,128)(2,1)S(1)} collective-permute-done((bf16[512,256]{1,0:T(8,128)(2,1)S(1)}, bf16[512,256]{1,0:T(8,128)(2,1)S(1)}, u32[]{:S(2)}, u32[]{:S(2)}) %collective-permute-start.22) | collective-permute-done | bytes 262176 | tf_op jit(solution)/shard_map/ppermute | solution.py:202
  137.9 1.0 copy-done.7
  138.9 3.9 %output.1 = (f32[4,128,1024]{2,1,0:T(8,128)}, bf16[4,128,1024]{2,1,0:T(8,128)(2,1)S(1)}) custom-call(s32[5]{0:T(128)S(1)} %stack.41.where_ref, bf16[512,256]{1,0:T(8,128)(2,1)S(1)} %attend.2.refs_0_, bf16[512,256]{1,0:T(8,128)(2,1)S(1)} %attend.3.refs_1_, bf16[512,256]{1,0:T(8,128)(2,1)S(1)} %collective-permute-done.21.refs_2_, ...), custom_call_target="tpu_custom_call" | custom-call | flops 5000000000 | bytes 4000000 | tf_op jit(solution)/shard_map/output/pallas_call | solution.py:657
  142.8 2.7 %collective-permute-done.25 = bf16[4,128,1024]{2,1,0:T(8,128)(2,1)S(1)} collective-permute-done((bf16[4,128,1024]{2,1,0:T(8,128)(2,1)S(1)}, bf16[4,128,1024]{2,1,0:T(8,128)(2,1)S(1)}, u32[]{:S(2)}, u32[]{:S(2)}) %collective-permute-start.25) | collective-permute-done | bytes 1048608 | tf_op jit(solution)/shard_map/ppermute | solution.py:202
  145.4 1.9 %fusion.8 = (bf16[128,1024]{1,0:T(8,128)(2,1)S(1)}, bf16[128,1024]{1,0:T(8,128)(2,1)S(1)}, bf16[128,1024]{1,0:T(8,128)(2,1)S(1)}, f32[128,1024]{1,0:T(8,128)S(1)}) fusion(f32[4,128,1024]{2,1,0:T(8,128)} %get-tuple-element.77, bf16[4,128,1024]{2,1,0:T(8,128)(2,1)S(1)} %collective-permute-done.25), kind=kLoop, calls=%fused_computation.29 | loop fusion | flops 1441792 | bytes 4456448 | tf_op jit(solution)/shard_map/convert_element_type | solution.py:674
  147.3 1.1 collective-permute-start.28
  148.4 5.1 %collective-permute-start.27 = (bf16[128,1024]{1,0:T(8,128)(2,1)S(1)}, bf16[128,1024]{1,0:T(8,128)(2,1)S(1)}, u32[]{:S(2)}, u32[]{:S(2)}) collective-permute-start(bf16[128,1024]{1,0:T(8,128)(2,1)S(1)} %get-tuple-element.82), channel_id=1, source_target_pairs={{0,16},{1,17},{2,18},{3,19},{4,20},{5,21},{6,22},{7,23},{8,24},{9,... | collective-permute-start | bytes 786440 | tf_op jit(solution)/shard_map/ppermute | solution.py:202
  153.5 1.9 %collective-permute-start.26 = (bf16[128,1024]{1,0:T(8,128)(2,1)S(1)}, bf16[128,1024]{1,0:T(8,128)(2,1)S(1)}, u32[]{:S(2)}, u32[]{:S(2)}) collective-permute-start(bf16[128,1024]{1,0:T(8,128)(2,1)S(1)} %get-tuple-element.83), channel_id=1, source_target_pairs={{0,8},{1,9},{2,10},{3,11},{4,12},{5,13},{6,14},{7,15},{8,16},{9,17... | collective-permute-start | bytes 786440 | tf_op jit(solution)/shard_map/ppermute | solution.py:202
  155.4 3.8 %collective-permute-done.28.third = bf16[128,1024]{1,0:T(8,128)(2,1)S(1)} collective-permute-done((bf16[128,1024]{1,0:T(8,128)(2,1)S(1)}, bf16[128,1024]{1,0:T(8,128)(2,1)S(1)}, u32[]{:S(2)}, u32[]{:S(2)}) %collective-permute-start.28) | collective-permute-done | bytes 262176 | tf_op jit(solution)/shard_map/ppermute | solution.py:202
  159.2 11.4 %collective-permute-done.27.second = bf16[128,1024]{1,0:T(8,128)(2,1)S(1)} collective-permute-done((bf16[128,1024]{1,0:T(8,128)(2,1)S(1)}, bf16[128,1024]{1,0:T(8,128)(2,1)S(1)}, u32[]{:S(2)}, u32[]{:S(2)}) %collective-permute-start.27) | collective-permute-done | bytes 262176 | tf_op jit(solution)/shard_map/ppermute | solution.py:202
  170.6 5.4 %collective-permute-done.26.first = bf16[128,1024]{1,0:T(8,128)(2,1)S(1)} collective-permute-done((bf16[128,1024]{1,0:T(8,128)(2,1)S(1)}, bf16[128,1024]{1,0:T(8,128)(2,1)S(1)}, u32[]{:S(2)}, u32[]{:S(2)}) %collective-permute-start.26) | collective-permute-done | bytes 262176 | tf_op jit(solution)/shard_map/ppermute | solution.py:202
  175.9 1.4 finish.1
  (57 shorter events, 0.9 us)
Async XLA Ops:
  0.0 9.8 %copy-start.4 = (bf16[128,2048]{1,0:T(8,128)(2,1)S(1)}, bf16[128,2048]{1,0:T(8,128)(2,1)}, u32[]{:S(2)}) copy-start(bf16[128,2048]{1,0:T(8,128)(2,1)} %param.12) | copy-start | bytes 1572868
  0.0 11.0 %copy-start.8 = (s32[8]{0:T(128)S(1)}, s32[8]{0:T(128)}, u32[]{:S(2)}) copy-start(s32[8]{0:T(128)} %param.22) | copy-start | bytes 100
  0.0 15.0 %copy-start.3 = (bf16[64,512]{1,0:T(8,128)(2,1)S(1)}, bf16[64,512]{1,0:T(8,128)(2,1)}, u32[]{:S(2)}) copy-start(bf16[64,512]{1,0:T(8,128)(2,1)} %refs_3_.1) | copy-start | bytes 196612
  0.0 15.0 %copy-start.2 = (bf16[64,512]{1,0:T(8,128)(2,1)S(1)}, bf16[64,512]{1,0:T(8,128)(2,1)}, u32[]{:S(2)}) copy-start(bf16[64,512]{1,0:T(8,128)(2,1)} %refs_2_.1) | copy-start | bytes 196612
  0.0 15.0 %copy-start.1 = (bf16[256,512]{1,0:T(8,128)(2,1)S(1)}, bf16[256,512]{1,0:T(8,128)(2,1)}, u32[]{:S(2)}) copy-start(bf16[256,512]{1,0:T(8,128)(2,1)} %refs_1_.1) | copy-start | bytes 786436
  0.0 15.0 %copy-start = (bf16[256,512]{1,0:T(8,128)(2,1)S(1)}, bf16[256,512]{1,0:T(8,128)(2,1)}, u32[]{:S(2)}) copy-start(bf16[256,512]{1,0:T(8,128)(2,1)} %refs_0_.2) | copy-start | bytes 786436
  0.0 28.0 %collective-permute-start.3 = (bf16[256,2048]{1,0:T(8,128)(2,1)}, bf16[256,2048]{1,0:T(8,128)(2,1)}, u32[]{:S(2)}, u32[]{:S(2)}) collective-permute-start(bf16[256,2048]{1,0:T(8,128)(2,1)} %refs_0_.3), channel_id=1, source_target_pairs={{0,2},{1,5},{2,0},{3,7},{4,6},{5,1},{6,4},{7,3},{8,10},{9,13},{10,... | collective-permute-start | bytes 3145736 | tf_op jit(solution)/shard_map/ppermute | solution.py:202
  1.6 26.5 %collective-permute-start.4 = (bf16[256,2048]{1,0:T(8,128)(2,1)}, bf16[256,2048]{1,0:T(8,128)(2,1)}, u32[]{:S(2)}, u32[]{:S(2)}) collective-permute-start(bf16[256,2048]{1,0:T(8,128)(2,1)} %refs_0_.3), channel_id=1, source_target_pairs={{0,4},{1,3},{2,6},{3,1},{4,0},{5,7},{6,2},{7,5},{8,12},{9,11},{10,... | collective-permute-start | bytes 3145736 | tf_op jit(solution)/shard_map/ppermute | solution.py:202
  11.1 8.6 %collective-permute-start.1 = (bf16[32,2048]{1,0:T(8,128)(2,1)S(1)}, bf16[32,2048]{1,0:T(8,128)(2,1)}, u32[]{:S(2)}, u32[]{:S(2)}) collective-permute-start(bf16[32,2048]{1,0:T(8,128)(2,1)S(1)} %fusion.5), channel_id=1, source_target_pairs={{0,0},{1,16},{2,1},{3,17},{4,8},{5,24},{6,9},{7,25},{8,2},{9,18},{... | collective-permute-start | bytes 393224 | tf_op jit(solution)/shard_map/ppermute | solution.py:202
  13.4 14.7 %collective-permute-start = (bf16[144,2048]{1,0:T(8,128)(2,1)S(1)}, bf16[144,2048]{1,0:T(8,128)(2,1)}, u32[]{:S(2)}, u32[]{:S(2)}) collective-permute-start(bf16[144,2048]{1,0:T(8,128)(2,1)S(1)} %fusion.2), channel_id=1, source_target_pairs={{1,16},{3,18},{5,20},{7,22},{9,24},{11,26},{13,28},{15,30},{16,1},... | collective-permute-start | bytes 1769480 | tf_op jit(solution)/shard_map/ppermute | solution.py:202
  15.0 1.2 copy-start.5
  15.9 12.1 %collective-permute-start.2 = (bf16[336,512]{1,0:T(8,128)(2,1)S(1)}, bf16[336,512]{1,0:T(8,128)(2,1)S(1)}, u32[]{:S(2)}, u32[]{:S(2)}) collective-permute-start(bf16[336,512]{1,0:T(8,128)(2,1)S(1)} %get-tuple-element.45), channel_id=1, source_target_pairs={{0,8},{1,9},{2,10},{3,11},{4,12},{5,13},{6,14},{7,15},{8,0},{9,1},... | collective-permute-start | bytes 1032200 | tf_op jit(solution)/shard_map/ppermute | solution.py:202
  28.2 12.6 %collective-permute-start.10 = (bf16[2,256,512]{2,1,0:T(8,128)(2,1)S(1)}, bf16[2,256,512]{2,1,0:T(8,128)(2,1)S(1)}, u32[]{:S(2)}, u32[]{:S(2)}) collective-permute-start(bf16[2,256,512]{2,1,0:T(8,128)(2,1)S(1)} %pad_maximum_fusion.3.own), channel_id=1, source_target_pairs={{0,2},{1,5},{2,0},{3,7},{4,6},{5,1},{6,4},{7,3},{8,10},{9,13},{10,... | collective-permute-start | bytes 1572872 | tf_op jit(solution)/shard_map/ppermute | solution.py:202
  31.0 29.2 %collective-permute-start.7 = (bf16[256,2048]{1,0:T(8,128)(2,1)}, bf16[256,2048]{1,0:T(8,128)(2,1)S(1)}, u32[]{:S(2)}, u32[]{:S(2)}) collective-permute-start(bf16[256,2048]{1,0:T(8,128)(2,1)} %collective-permute-done.3.refs_1_), channel_id=1, source_target_pairs={{0,4},{1,3},{2,6},{3,1},{4,0},{5,7},{6,2},{7,5},{8,12},{9,11},{10,... | collective-permute-start | bytes 3145736 | tf_op jit(solution)/shard_map/ppermute | solution.py:202
  32.0 28.1 %collective-permute-start.5 = (bf16[176,2048]{1,0:T(8,128)(2,1)S(1)}, bf16[176,2048]{1,0:T(8,128)(2,1)S(1)}, u32[]{:S(2)}, u32[]{:S(2)}) collective-permute-start(bf16[176,2048]{1,0:T(8,128)(2,1)S(1)} %pad_maximum_fusion.2.x0), channel_id=1, source_target_pairs={{0,8},{1,9},{2,10},{3,11},{4,12},{5,13},{6,14},{7,15},{8,0},{9,1},... | collective-permute-start | bytes 2162696 | tf_op jit(solution)/shard_map/ppermute | solution.py:202
  33.3 26.9 %collective-permute-start.6 = (bf16[768,256]{1,0:T(8,128)(2,1)S(1)}, bf16[768,256]{1,0:T(8,128)(2,1)S(1)}, u32[]{:S(2)}, u32[]{:S(2)}) collective-permute-start(bf16[768,256]{1,0:T(8,128)(2,1)S(1)} %slice.42), channel_id=1, source_target_pairs={{0,16},{1,17},{2,18},{3,19},{4,20},{5,21},{6,22},{7,23},{8,24},{9,... | collective-permute-start | bytes 1179656 | tf_op jit(solution)/shard_map/ppermute | solution.py:202
  40.9 22.9 %collective-permute-start.11 = (bf16[4,256,512]{2,1,0:T(8,128)(2,1)S(1)}, bf16[4,256,512]{2,1,0:T(8,128)(2,1)S(1)}, u32[]{:S(2)}, u32[]{:S(2)}) collective-permute-start(bf16[4,256,512]{2,1,0:T(8,128)(2,1)S(1)} %pad_maximum_fusion), channel_id=1, source_target_pairs={{0,4},{1,3},{2,6},{3,1},{4,0},{5,7},{6,2},{7,5},{8,12},{9,11},{10,... | collective-permute-start | bytes 3145736 | tf_op jit(solution)/shard_map/ppermute | solution.py:202
  41.5 22.4 %collective-permute-start.9 = (bf16[176,2048]{1,0:T(8,128)(2,1)S(1)}, bf16[176,2048]{1,0:T(8,128)(2,1)S(1)}, u32[]{:S(2)}, u32[]{:S(2)}) collective-permute-start(bf16[176,2048]{1,0:T(8,128)(2,1)S(1)} %pad_maximum_fusion.2.x0), channel_id=1, source_target_pairs={{0,1},{1,0},{2,3},{3,2},{4,5},{5,4},{6,7},{7,6},{8,9},{9,8},{10,11... | collective-permute-start | bytes 2162696 | tf_op jit(solution)/shard_map/ppermute | solution.py:202
  60.2 1.9 %copy-start.6 = (bf16[256,2048]{1,0:T(8,128)(2,1)}, bf16[256,2048]{1,0:T(8,128)(2,1)S(1)}, u32[]{:S(2)}) copy-start(bf16[256,2048]{1,0:T(8,128)(2,1)S(1)} %collective-permute-done.7.refs_3_) | copy-start | bytes 3145732
  60.2 3.7 %collective-permute-start.8 = (bf16[176,2048]{1,0:T(8,128)(2,1)S(1)}, bf16[176,2048]{1,0:T(8,128)(2,1)S(1)}, u32[]{:S(2)}, u32[]{:S(2)}) collective-permute-start(bf16[176,2048]{1,0:T(8,128)(2,1)S(1)} %collective-permute-done.5.x1), channel_id=1, source_target_pairs={{0,1},{1,0},{2,3},{3,2},{4,5},{5,4},{6,7},{7,6},{8,9},{9,8},{10,11... | collective-permute-start | bytes 2162696 | tf_op jit(solution)/shard_map/ppermute | solution.py:202
  62.1 15.5 %collective-permute-start.18 = (bf16[256,256]{1,0:T(8,128)(2,1)S(1)}, bf16[256,256]{1,0:T(8,128)(2,1)S(1)}, u32[]{:S(2)}, u32[]{:S(2)}) collective-permute-start(bf16[256,256]{1,0:T(8,128)(2,1)S(1)} %slice.47), channel_id=1, source_target_pairs={{0,16},{1,17},{2,18},{3,19},{4,20},{5,21},{6,22},{7,23},{8,24},{9,... | collective-permute-start | bytes 393224 | tf_op jit(solution)/shard_map/ppermute | solution.py:202
  66.0 19.7 %collective-permute-start.15 = (bf16[736,256]{1,0:T(8,128)(2,1)S(1)}, bf16[736,256]{1,0:T(8,128)(2,1)S(1)}, u32[]{:S(2)}, u32[]{:S(2)}) collective-permute-start(bf16[736,256]{1,0:T(8,128)(2,1)S(1)} %get-tuple-element.69), channel_id=1, source_target_pairs={{0,16},{1,17},{2,18},{3,19},{4,20},{5,21},{6,22},{7,23},{8,24},{9,... | collective-permute-start | bytes 1130504 | tf_op jit(solution)/shard_map/ppermute | solution.py:202
  72.5 21.4 %collective-permute-start.13 = (bf16[4,128,512]{2,1,0:T(8,128)(2,1)S(1)}, bf16[4,128,512]{2,1,0:T(8,128)(2,1)S(1)}, u32[]{:S(2)}, u32[]{:S(2)}) collective-permute-start(bf16[4,128,512]{2,1,0:T(8,128)(2,1)S(1)} %get-tuple-element.67), channel_id=1, source_target_pairs={{0,8},{1,9},{2,10},{3,11},{4,12},{5,13},{6,14},{7,15},{8,0},{9,1},... | collective-permute-start | bytes 1572872 | tf_op jit(solution)/shard_map/ppermute | solution.py:202
  77.8 38.5 %collective-permute-start.19 = (bf16[2,1024,256]{2,1,0:T(8,128)(2,1)S(1)}, bf16[2,1024,256]{2,1,0:T(8,128)(2,1)S(1)}, u32[]{:S(2)}, u32[]{:S(2)}) collective-permute-start(bf16[2,1024,256]{2,1,0:T(8,128)(2,1)S(1)} %pad_maximum_fusion.1.refs_4_), channel_id=1, source_target_pairs={{0,2},{1,5},{2,0},{3,7},{4,6},{5,1},{6,4},{7,3},{8,10},{9,13},{10,... | collective-permute-start | bytes 3145736 | tf_op jit(solution)/shard_map/ppermute | solution.py:202
  86.7 12.6 %collective-permute-start.20 = (bf16[6,128,256]{2,1,0:T(8,128)(2,1)S(1)}, bf16[6,128,256]{2,1,0:T(8,128)(2,1)S(1)}, u32[]{:S(2)}, u32[]{:S(2)}) collective-permute-start(bf16[6,128,256]{2,1,0:T(8,128)(2,1)S(1)} %keys_join.1.kv0), channel_id=1, source_target_pairs={{0,4},{1,3},{2,6},{3,1},{4,0},{5,7},{6,2},{7,5},{8,12},{9,11},{10,... | collective-permute-start | bytes 1179656 | tf_op jit(solution)/shard_map/ppermute | solution.py:202
  87.7 32.0 %collective-permute-start.12 = (bf16[4,128,512]{2,1,0:T(8,128)(2,1)S(1)}, bf16[4,128,512]{2,1,0:T(8,128)(2,1)S(1)}, u32[]{:S(2)}, u32[]{:S(2)}) collective-permute-start(bf16[4,128,512]{2,1,0:T(8,128)(2,1)S(1)} %get-tuple-element.65), channel_id=1, source_target_pairs={{0,8},{1,9},{2,10},{3,11},{4,12},{5,13},{6,14},{7,15},{8,0},{9,1},... | collective-permute-start | bytes 1572872 | tf_op jit(solution)/shard_map/ppermute | solution.py:202
  94.1 26.1 %collective-permute-start.14 = (bf16[4,128,512]{2,1,0:T(8,128)(2,1)S(1)}, bf16[4,128,512]{2,1,0:T(8,128)(2,1)S(1)}, u32[]{:S(2)}, u32[]{:S(2)}) collective-permute-start(bf16[4,128,512]{2,1,0:T(8,128)(2,1)S(1)} %add_convert_fusion), channel_id=1, source_target_pairs={{0,16},{1,17},{2,18},{3,19},{4,20},{5,21},{6,22},{7,23},{8,24},{9,... | collective-permute-start | bytes 1572872 | tf_op jit(solution)/shard_map/ppermute | solution.py:202
  99.3 11.4 %collective-permute-start.17 = (bf16[6,128,256]{2,1,0:T(8,128)(2,1)S(1)}, bf16[6,128,256]{2,1,0:T(8,128)(2,1)S(1)}, u32[]{:S(2)}, u32[]{:S(2)}) collective-permute-start(bf16[6,128,256]{2,1,0:T(8,128)(2,1)S(1)} %keys_join.1.kv0), channel_id=1, source_target_pairs={{0,6},{1,7},{2,4},{3,5},{4,2},{5,3},{6,0},{7,1},{8,14},{9,15},{10,... | collective-permute-start | bytes 1179656 | tf_op jit(solution)/shard_map/ppermute | solution.py:202
  99.3 16.9 %collective-permute-start.16 = (bf16[6,128,256]{2,1,0:T(8,128)(2,1)S(1)}, bf16[6,128,256]{2,1,0:T(8,128)(2,1)S(1)}, u32[]{:S(2)}, u32[]{:S(2)}) collective-permute-start(bf16[6,128,256]{2,1,0:T(8,128)(2,1)S(1)} %keys_join.1.kv0), channel_id=1, source_target_pairs={{0,2},{1,5},{2,0},{3,7},{4,6},{5,1},{6,4},{7,3},{8,10},{9,13},{10,... | collective-permute-start | bytes 1179656 | tf_op jit(solution)/shard_map/ppermute | solution.py:202
  110.7 27.1 %collective-permute-start.23 = (bf16[2,1024,256]{2,1,0:T(8,128)(2,1)S(1)}, bf16[2,1024,256]{2,1,0:T(8,128)(2,1)S(1)}, u32[]{:S(2)}, u32[]{:S(2)}) collective-permute-start(bf16[2,1024,256]{2,1,0:T(8,128)(2,1)S(1)} %pad_maximum_fusion.1.refs_4_), channel_id=1, source_target_pairs={{0,4},{1,3},{2,6},{3,1},{4,0},{5,7},{6,2},{7,5},{8,12},{9,11},{10,... | collective-permute-start | bytes 3145736 | tf_op jit(solution)/shard_map/ppermute | solution.py:202
  116.2 21.6 %collective-permute-start.24 = (bf16[2,1024,256]{2,1,0:T(8,128)(2,1)S(1)}, bf16[2,1024,256]{2,1,0:T(8,128)(2,1)S(1)}, u32[]{:S(2)}, u32[]{:S(2)}) collective-permute-start(bf16[2,1024,256]{2,1,0:T(8,128)(2,1)S(1)} %collective-permute-done.19.refs_5_), channel_id=1, source_target_pairs={{0,4},{1,3},{2,6},{3,1},{4,0},{5,7},{6,2},{7,5},{8,12},{9,11},{10,... | collective-permute-start | bytes 3145736 | tf_op jit(solution)/shard_map/ppermute | solution.py:202
  124.9 7.1 %collective-permute-start.21 = (bf16[512,256]{1,0:T(8,128)(2,1)S(1)}, bf16[512,256]{1,0:T(8,128)(2,1)S(1)}, u32[]{:S(2)}, u32[]{:S(2)}) collective-permute-start(bf16[512,256]{1,0:T(8,128)(2,1)S(1)} %attend.2.refs_0_), channel_id=1, source_target_pairs={{0,8},{1,9},{2,10},{3,11},{4,12},{5,13},{6,14},{7,15},{8,0},{9,1},... | collective-permute-start | bytes 786440 | tf_op jit(solution)/shard_map/ppermute | solution.py:202
  131.4 6.4 %collective-permute-start.22 = (bf16[512,256]{1,0:T(8,128)(2,1)S(1)}, bf16[512,256]{1,0:T(8,128)(2,1)S(1)}, u32[]{:S(2)}, u32[]{:S(2)}) collective-permute-start(bf16[512,256]{1,0:T(8,128)(2,1)S(1)} %attend.3.refs_1_), channel_id=1, source_target_pairs={{0,8},{1,9},{2,10},{3,11},{4,12},{5,13},{6,14},{7,15},{8,0},{9,1},... | collective-permute-start | bytes 786440 | tf_op jit(solution)/shard_map/ppermute | solution.py:202
  137.9 1.0 copy-start.7
  142.8 2.7 %collective-permute-start.25 = (bf16[4,128,1024]{2,1,0:T(8,128)(2,1)S(1)}, bf16[4,128,1024]{2,1,0:T(8,128)(2,1)S(1)}, u32[]{:S(2)}, u32[]{:S(2)}) collective-permute-start(bf16[4,128,1024]{2,1,0:T(8,128)(2,1)S(1)} %get-tuple-element.78), channel_id=1, source_target_pairs={{0,1},{1,0},{2,3},{3,2},{4,5},{5,4},{6,7},{7,6},{8,9},{9,8},{10,11... | collective-permute-start | bytes 3145736 | tf_op jit(solution)/shard_map/ppermute | solution.py:202
  147.3 11.9 %collective-permute-start.28 = (bf16[128,1024]{1,0:T(8,128)(2,1)S(1)}, bf16[128,1024]{1,0:T(8,128)(2,1)S(1)}, u32[]{:S(2)}, u32[]{:S(2)}) collective-permute-start(bf16[128,1024]{1,0:T(8,128)(2,1)S(1)} %get-tuple-element.81), channel_id=1, source_target_pairs={{0,24},{1,25},{2,26},{3,27},{4,28},{5,29},{6,30},{7,31},{8,0},{9,1... | collective-permute-start | bytes 786440 | tf_op jit(solution)/shard_map/ppermute | solution.py:202
  148.4 22.2 %collective-permute-start.27 = (bf16[128,1024]{1,0:T(8,128)(2,1)S(1)}, bf16[128,1024]{1,0:T(8,128)(2,1)S(1)}, u32[]{:S(2)}, u32[]{:S(2)}) collective-permute-start(bf16[128,1024]{1,0:T(8,128)(2,1)S(1)} %get-tuple-element.82), channel_id=1, source_target_pairs={{0,16},{1,17},{2,18},{3,19},{4,20},{5,21},{6,22},{7,23},{8,24},{9,... | collective-permute-start | bytes 786440 | tf_op jit(solution)/shard_map/ppermute | solution.py:202
  153.5 22.5 %collective-permute-start.26 = (bf16[128,1024]{1,0:T(8,128)(2,1)S(1)}, bf16[128,1024]{1,0:T(8,128)(2,1)S(1)}, u32[]{:S(2)}, u32[]{:S(2)}) collective-permute-start(bf16[128,1024]{1,0:T(8,128)(2,1)S(1)} %get-tuple-element.83), channel_id=1, source_target_pairs={{0,8},{1,9},{2,10},{3,11},{4,12},{5,13},{6,14},{7,15},{8,16},{9,17... | collective-permute-start | bytes 786440 | tf_op jit(solution)/shard_map/ppermute | solution.py:202

commit v20 on v18

--- a/solution.py
+++ b/solution.py
@@ -628,7 +628,7 @@
 
     kv_far, out_pair = lax.optimization_barrier((kv_far, out_pair))
     out_far = to_far(out_pair)
-    kv_near, kv_both, out_near = lax.optimization_barrier((kv_near, kv_both, out_near))
+    kv_near, out_near = lax.optimization_barrier((kv_near, out_near))
     out_both = to_far(out_near)
 
     attended = [

time: 176 us -> 176 us (level)
  no operation moved by 1% of the time
where the time goes in v20:
time: 176 us
  waiting for transfers between devices  94 us (53%)
  starting transfers between devices  45 us (26%)
  Pallas kernels  23.8 us (14%)
  other arithmetic  8.06 us (5%)
  blocking collectives  2.46 us (1%)
  local copies, waits for them, and re-layouts  2.09 us (1%)
    ppermute x28, waiting for transfers between devices, permuted(): return lax.ppermute(value, ('seq', 'head'), perm)  94 us
    ppermute x28, starting transfers between devices, permuted(): return lax.ppermute(value, ('seq', 'head'), perm)  45 us
    pallas_call x2, Pallas kernels, by_levels(): pl.pallas_call(functools.partial(attend_kernel, pair), out_shape=shaped((...  9.48 us
    pallas_call x1, Pallas kernels, by_levels(): pl.pallas_call(queries_part_kernel, out_shape=(shaped(group_shape, jnp.fl...  4.99 us
    pallas_call x1, Pallas kernels, by_levels(): pl.pallas_call(output_kernel, out_shape=(shaped((LEVELS, tok, wide_cols),...  3.89 us
  transfers between devices with their start and end apart: 28, of which 14 were waited for; matrix products, arithmetic and copies ran while one was open for 4% of the time, Pallas kernels for 9%

profile of v20, /device:TPU:8, one launch (start us, length us, event | category | flops | bytes accessed | tf_op | source)
XLA Modules:
  0.0 175.8 jit_solution(18081290196489659502)
XLA Ops:
  0.0 1.6 collective-permute-start.10
  1.6 1.5 collective-permute-start.9
  3.1 1.0 fusion.3
  4.2 0.1 pad.22.clone
  4.2 1.4 fusion
  5.6 2.5 %all-reduce.1 = (f32[144]{0:T(256)S(1)}, f32[32]{0:T(128)S(1)}) all-reduce(f32[144]{0:T(256)S(1)} %fusion, f32[32]{0:T(128)S(1)} %fusion.3), channel_id=1, replica_groups=mesh['seq'=16,'head'=2] {'head'}, use_global_device_ids=true, to_apply=%region_1.2 | all-reduce | flops 176 | bytes 1408 | tf_op jit(solution)/shard_map/psum | solution.py:518
  8.1 0.7 dynamic_slice.9
  8.8 1.1 fusion.2
  10.0 0.1 fusion.5
  10.1 0.1 broadcast_in_dim.5.refs_4_
  10.2 0.1 stack.41.where_ref
  10.3 0.9 pack.1
  11.2 0.5 collective-permute-start.2
  11.7 3.4 %collective-permute-start.1 = (bf16[32,2048]{1,0:T(8,128)(2,1)S(1)}, bf16[32,2048]{1,0:T(8,128)(2,1)S(1)}, u32[]{:S(2)}, u32[]{:S(2)}) collective-permute-start(bf16[32,2048]{1,0:T(8,128)(2,1)S(1)} %fusion.5), channel_id=1, source_target_pairs={{0,0},{1,16},{2,1},{3,17},{4,8},{5,24},{6,9},{7,25},{8,2},{9,18},{... | collective-permute-start | bytes 393224 | tf_op jit(solution)/shard_map/ppermute | solution.py:202
  15.2 1.5 collective-permute-start
  16.7 0.1 dynamic-slice_bitcast_fusion
  16.8 8.2 %collective-permute-done.1 = bf16[32,2048]{1,0:T(8,128)(2,1)S(1)} collective-permute-done((bf16[32,2048]{1,0:T(8,128)(2,1)S(1)}, bf16[32,2048]{1,0:T(8,128)(2,1)S(1)}, u32[]{:S(2)}, u32[]{:S(2)}) %collective-permute-start.1) | collective-permute-done | bytes 131104 | tf_op jit(solution)/shard_map/ppermute | solution.py:202
  25.1 5.5 %collective-permute-start.7 = (bf16[2,256,512]{2,1,0:T(8,128)(2,1)S(1)}, bf16[2,256,512]{2,1,0:T(8,128)(2,1)S(1)}, u32[]{:S(2)}, u32[]{:S(2)}) collective-permute-start(bf16[2,256,512]{2,1,0:T(8,128)(2,1)S(1)} %pad_maximum_fusion.3.own), channel_id=1, source_target_pairs={{0,2},{1,5},{2,0},{3,7},{4,6},{5,1},{6,4},{7,3},{8,10},{9,13},{10,... | collective-permute-start | bytes 1572872 | tf_op jit(solution)/shard_map/ppermute | solution.py:202
  30.9 8.0 %collective-permute-start.4 = (bf16[1024,256]{1,0:T(8,128)(2,1)S(1)}, bf16[1024,256]{1,0:T(8,128)(2,1)S(1)}, u32[]{:S(2)}, u32[]{:S(2)}) collective-permute-start(bf16[1024,256]{1,0:T(8,128)(2,1)S(1)} %get-tuple-element.48), channel_id=1, source_target_pairs={{0,16},{1,17},{2,18},{3,19},{4,20},{5,21},{6,22},{7,23},{8,24},{9,... | collective-permute-start | bytes 1572872 | tf_op jit(solution)/shard_map/ppermute | solution.py:202
  38.8 0.1 add_convert_fusion.4
  38.9 0.1 pad_maximum_fusion
  39.0 0.5 collective-permute-start.8
  39.6 1.6 collective-permute-start.11
  41.2 20.7 %collective-permute-done.4 = bf16[1024,256]{1,0:T(8,128)(2,1)S(1)} collective-permute-done((bf16[1024,256]{1,0:T(8,128)(2,1)S(1)}, bf16[1024,256]{1,0:T(8,128)(2,1)S(1)}, u32[]{:S(2)}, u32[]{:S(2)}) %collective-permute-start.4) | collective-permute-done | bytes 524320 | tf_op jit(solution)/shard_map/ppermute | solution.py:202
  61.9 1.5 fusion.9
  63.4 0.2 pad_maximum_fusion.4.cos_ref
  63.6 0.2 pad_maximum_fusion.5.sin_ref
  63.8 0.1 pad_maximum_fusion.1.refs_4_
  63.9 0.2 collective-permute-done.5.x3
  64.1 1.0 collective-permute-done.11.refs_3_
  65.1 2.1 %keys_part.1 = (f32[576,256]{1,0:T(8,128)S(1)}, bf16[736,256]{1,0:T(8,128)(2,1)S(1)}) custom-call(s32[5]{0:T(128)S(1)} %stack.41.where_ref, bf16[176,2048]{1,0:T(8,128)(2,1)S(1)} %pad_maximum_fusion.2.x0, bf16[176,2048]{1,0:T(8,128)(2,1)S(1)} %collective-permute-done.3.x1, bf16[176,2048]{1,0:T(8,128)(2,1)S(1)} %collective-permute-done.6.x2, ...), custom_call_target="tpu_custom_call" | custom-call | flops 3000000000 | bytes 4000000 | tf_op jit(solution)/shard_map/keys_part/pallas_call | solution.py:578
  67.2 2.4 %collective-permute-start.15 = (bf16[736,256]{1,0:T(8,128)(2,1)S(1)}, bf16[736,256]{1,0:T(8,128)(2,1)S(1)}, u32[]{:S(2)}, u32[]{:S(2)}) collective-permute-start(bf16[736,256]{1,0:T(8,128)(2,1)S(1)} %get-tuple-element.68), channel_id=1, source_target_pairs={{0,16},{1,17},{2,18},{3,19},{4,20},{5,21},{6,22},{7,23},{8,24},{9,... | collective-permute-start | bytes 1130504 | tf_op jit(solution)/shard_map/ppermute | solution.py:202
  69.7 5.0 %queries_part.1 = (f32[4,128,512]{2,1,0:T(8,128)S(1)}, f32[4,128,512]{2,1,0:T(8,128)S(1)}, bf16[4,128,512]{2,1,0:T(8,128)(2,1)S(1)}, bf16[4,128,512]{2,1,0:T(8,128)(2,1)S(1)}) custom-call(s32[5]{0:T(128)S(1)} %stack.41.where_ref, bf16[176,2048]{1,0:T(8,128)(2,1)S(1)} %pad_maximum_fusion.2.x0, bf16[176,2048]{1,0:T(8,128)(2,1)S(1)} %collective-permute-done.3.x1, ...), custom_call_target="tpu_custom_call" | custom-call | flops 5000000000 | bytes 4000000 | tf_op jit(solution)/shard_map/queries_part/pallas_call | solution.py:595
  74.7 1.0 collective-permute-start.17
  75.8 1.9 %collective-permute-start.12 = (bf16[4,128,512]{2,1,0:T(8,128)(2,1)S(1)}, bf16[4,128,512]{2,1,0:T(8,128)(2,1)S(1)}, u32[]{:S(2)}, u32[]{:S(2)}) collective-permute-start(bf16[4,128,512]{2,1,0:T(8,128)(2,1)S(1)} %get-tuple-element.64), channel_id=1, source_target_pairs={{0,8},{1,9},{2,10},{3,11},{4,12},{5,13},{6,14},{7,15},{8,0},{9,1},... | collective-permute-start | bytes 1572872 | tf_op jit(solution)/shard_map/ppermute | solution.py:202
  77.7 7.6 %collective-permute-done.15.got_ref = bf16[736,256]{1,0:T(8,128)(2,1)S(1)} collective-permute-done((bf16[736,256]{1,0:T(8,128)(2,1)S(1)}, bf16[736,256]{1,0:T(8,128)(2,1)S(1)}, u32[]{:S(2)}, u32[]{:S(2)}) %collective-permute-start.15) | collective-permute-done | bytes 376864 | tf_op jit(solution)/shard_map/ppermute | solution.py:202
  85.3 1.0 keys_join.1.kv0
  86.4 0.6 collective-permute-start.18
  87.0 8.0 %collective-permute-done.13 = bf16[4,128,512]{2,1,0:T(8,128)(2,1)S(1)} collective-permute-done((bf16[4,128,512]{2,1,0:T(8,128)(2,1)S(1)}, bf16[4,128,512]{2,1,0:T(8,128)(2,1)S(1)}, u32[]{:S(2)}, u32[]{:S(2)}) %collective-permute-start.13) | collective-permute-done | bytes 524320 | tf_op jit(solution)/shard_map/ppermute | solution.py:202
  95.0 0.2 add_convert_fusion
  95.1 3.2 %collective-permute-start.14 = (bf16[4,128,512]{2,1,0:T(8,128)(2,1)S(1)}, bf16[4,128,512]{2,1,0:T(8,128)(2,1)S(1)}, u32[]{:S(2)}, u32[]{:S(2)}) collective-permute-start(bf16[4,128,512]{2,1,0:T(8,128)(2,1)S(1)} %add_convert_fusion), channel_id=1, source_target_pairs={{0,16},{1,17},{2,18},{3,19},{4,20},{5,21},{6,22},{7,23},{8,24},{9,... | collective-permute-start | bytes 1572872 | tf_op jit(solution)/shard_map/ppermute | solution.py:202
  98.3 0.9 collective-permute-start.16
  99.3 1.0 collective-permute-start.19
  100.3 7.7 %collective-permute-done.16.kv1 = bf16[6,128,256]{2,1,0:T(8,128)(2,1)S(1)} collective-permute-done((bf16[6,128,256]{2,1,0:T(8,128)(2,1)S(1)}, bf16[6,128,256]{2,1,0:T(8,128)(2,1)S(1)}, u32[]{:S(2)}, u32[]{:S(2)}) %collective-permute-start.16) | collective-permute-done | bytes 393248 | tf_op jit(solution)/shard_map/ppermute | solution.py:202
  108.0 0.5 collective-permute-start.22
  108.4 1.6 collective-permute-start.23
  110.0 4.8 %collective-permute-done.19.kv3 = bf16[6,128,256]{2,1,0:T(8,128)(2,1)S(1)} collective-permute-done((bf16[6,128,256]{2,1,0:T(8,128)(2,1)S(1)}, bf16[6,128,256]{2,1,0:T(8,128)(2,1)S(1)}, u32[]{:S(2)}, u32[]{:S(2)}) %collective-permute-start.19) | collective-permute-done | bytes 393248 | tf_op jit(solution)/shard_map/ppermute | solution.py:202
  114.7 3.9 %collective-permute-done.14.got_ref = bf16[4,128,512]{2,1,0:T(8,128)(2,1)S(1)} collective-permute-done((bf16[4,128,512]{2,1,0:T(8,128)(2,1)S(1)}, bf16[4,128,512]{2,1,0:T(8,128)(2,1)S(1)}, u32[]{:S(2)}, u32[]{:S(2)}) %collective-permute-start.14) | collective-permute-done | bytes 524320 | tf_op jit(solution)/shard_map/ppermute | solution.py:202
  118.6 4.7 %attend.3.refs_1_ = bf16[512,256]{1,0:T(8,128)(2,1)S(1)} custom-call(s32[5]{0:T(128)S(1)} %stack.41.where_ref, f32[4,128,512]{2,1,0:T(8,128)S(1)} %get-tuple-element.63.keep_ref, bf16[4,128,512]{2,1,0:T(8,128)(2,1)S(1)} %collective-permute-done.12.near_ref, bf16[4,128,512]{2,1,0:T(8,128)(2,1)S(1)} %collective-permute-done.14.got_ref, ...), custom_call_target="tpu_custom_call" | custom-call | flops 4000000000 | bytes 4000000 | tf_op jit(solution)/shard_map/attend/pallas_call | solution.py:635
  123.3 4.0 %collective-permute-start.21 = (bf16[512,256]{1,0:T(8,128)(2,1)S(1)}, bf16[512,256]{1,0:T(8,128)(2,1)S(1)}, u32[]{:S(2)}, u32[]{:S(2)}) collective-permute-start(bf16[512,256]{1,0:T(8,128)(2,1)S(1)} %attend.3.refs_1_), channel_id=1, source_target_pairs={{0,8},{1,9},{2,10},{3,11},{4,12},{5,13},{6,14},{7,15},{8,0},{9,1},... | collective-permute-start | bytes 786440 | tf_op jit(solution)/shard_map/ppermute | solution.py:202
  127.3 4.8 %attend.2.refs_0_ = bf16[512,256]{1,0:T(8,128)(2,1)S(1)} custom-call(s32[5]{0:T(128)S(1)} %stack.41.where_ref, f32[4,128,512]{2,1,0:T(8,128)S(1)} %get-tuple-element.63.keep_ref, bf16[4,128,512]{2,1,0:T(8,128)(2,1)S(1)} %collective-permute-done.12.near_ref, bf16[4,128,512]{2,1,0:T(8,128)(2,1)S(1)} %collective-permute-done.14.got_ref, ...), custom_call_target="tpu_custom_call" | custom-call | flops 4000000000 | bytes 4000000 | tf_op jit(solution)/shard_map/attend/pallas_call | solution.py:635
  132.1 0.1 collective-permute-start.20
  132.2 6.3 %collective-permute-done.20.refs_2_ = bf16[512,256]{1,0:T(8,128)(2,1)S(1)} collective-permute-done((bf16[512,256]{1,0:T(8,128)(2,1)S(1)}, bf16[512,256]{1,0:T(8,128)(2,1)S(1)}, u32[]{:S(2)}, u32[]{:S(2)}) %collective-permute-start.20) | collective-permute-done | bytes 262176 | tf_op jit(solution)/shard_map/ppermute | solution.py:202
  138.6 1.0 copy-done.8
  139.6 3.9 %output.1 = (f32[4,128,1024]{2,1,0:T(8,128)}, bf16[4,128,1024]{2,1,0:T(8,128)(2,1)S(1)}) custom-call(s32[5]{0:T(128)S(1)} %stack.41.where_ref, bf16[512,256]{1,0:T(8,128)(2,1)S(1)} %attend.2.refs_0_, bf16[512,256]{1,0:T(8,128)(2,1)S(1)} %attend.3.refs_1_, bf16[512,256]{1,0:T(8,128)(2,1)S(1)} %collective-permute-done.20.refs_2_, ...), custom_call_target="tpu_custom_call" | custom-call | flops 5000000000 | bytes 4000000 | tf_op jit(solution)/shard_map/output/pallas_call | solution.py:652
  143.5 2.7 %collective-permute-done.24 = bf16[4,128,1024]{2,1,0:T(8,128)(2,1)S(1)} collective-permute-done((bf16[4,128,1024]{2,1,0:T(8,128)(2,1)S(1)}, bf16[4,128,1024]{2,1,0:T(8,128)(2,1)S(1)}, u32[]{:S(2)}, u32[]{:S(2)}) %collective-permute-start.24) | collective-permute-done | bytes 1048608 | tf_op jit(solution)/shard_map/ppermute | solution.py:202
  146.1 1.9 %fusion.8 = (bf16[128,1024]{1,0:T(8,128)(2,1)S(1)}, bf16[128,1024]{1,0:T(8,128)(2,1)S(1)}, bf16[128,1024]{1,0:T(8,128)(2,1)S(1)}, f32[128,1024]{1,0:T(8,128)S(1)}) fusion(f32[4,128,1024]{2,1,0:T(8,128)} %get-tuple-element.75, bf16[4,128,1024]{2,1,0:T(8,128)(2,1)S(1)} %collective-permute-done.24), kind=kLoop, calls=%fused_computation.28 | loop fusion | flops 1441792 | bytes 4456448 | tf_op jit(solution)/shard_map/convert_element_type | solution.py:669
  148.0 1.9 %collective-permute-start.25 = (bf16[128,1024]{1,0:T(8,128)(2,1)S(1)}, bf16[128,1024]{1,0:T(8,128)(2,1)S(1)}, u32[]{:S(2)}, u32[]{:S(2)}) collective-permute-start(bf16[128,1024]{1,0:T(8,128)(2,1)S(1)} %get-tuple-element.81), channel_id=1, source_target_pairs={{0,8},{1,9},{2,10},{3,11},{4,12},{5,13},{6,14},{7,15},{8,16},{9,17... | collective-permute-start | bytes 786440 | tf_op jit(solution)/shard_map/ppermute | solution.py:202
  150.0 1.2 collective-permute-start.26
  151.1 0.4 collective-permute-start.27
  151.5 16.4 %collective-permute-done.25.first = bf16[128,1024]{1,0:T(8,128)(2,1)S(1)} collective-permute-done((bf16[128,1024]{1,0:T(8,128)(2,1)S(1)}, bf16[128,1024]{1,0:T(8,128)(2,1)S(1)}, u32[]{:S(2)}, u32[]{:S(2)}) %collective-permute-start.25) | collective-permute-done | bytes 262176 | tf_op jit(solution)/shard_map/ppermute | solution.py:202
  167.9 4.8 %collective-permute-done.26.second = bf16[128,1024]{1,0:T(8,128)(2,1)S(1)} collective-permute-done((bf16[128,1024]{1,0:T(8,128)(2,1)S(1)}, bf16[128,1024]{1,0:T(8,128)(2,1)S(1)}, u32[]{:S(2)}, u32[]{:S(2)}) %collective-permute-start.26) | collective-permute-done | bytes 262176 | tf_op jit(solution)/shard_map/ppermute | solution.py:202
  172.7 1.7 collective-permute-done.27.third
  174.4 1.4 finish.1
  (54 shorter events, 0.6 us)
Async XLA Ops:
  0.0 10.0 %copy-start.6 = (bf16[32,2048]{1,0:T(8,128)(2,1)S(1)}, bf16[32,2048]{1,0:T(8,128)(2,1)}, u32[]{:S(2)}) copy-start(bf16[32,2048]{1,0:T(8,128)(2,1)} %param.13) | copy-start | bytes 393220
  0.0 8.8 %copy-start.4 = (bf16[128,2048]{1,0:T(8,128)(2,1)S(1)}, bf16[128,2048]{1,0:T(8,128)(2,1)}, u32[]{:S(2)}) copy-start(bf16[128,2048]{1,0:T(8,128)(2,1)} %param.12) | copy-start | bytes 1572868
  0.0 10.1 %copy-start.9 = (s32[8]{0:T(128)S(1)}, s32[8]{0:T(128)}, u32[]{:S(2)}) copy-start(s32[8]{0:T(128)} %param.22) | copy-start | bytes 100
  0.0 10.3 %copy-start = (bf16[256,512]{1,0:T(8,128)(2,1)S(1)}, bf16[256,512]{1,0:T(8,128)(2,1)}, u32[]{:S(2)}) copy-start(bf16[256,512]{1,0:T(8,128)(2,1)} %refs_0_.2) | copy-start | bytes 786436
  0.0 10.2 %copy-start.1 = (bf16[256,512]{1,0:T(8,128)(2,1)S(1)}, bf16[256,512]{1,0:T(8,128)(2,1)}, u32[]{:S(2)}) copy-start(bf16[256,512]{1,0:T(8,128)(2,1)} %refs_1_.1) | copy-start | bytes 786436
  0.0 10.2 %copy-start.2 = (bf16[64,512]{1,0:T(8,128)(2,1)S(1)}, bf16[64,512]{1,0:T(8,128)(2,1)}, u32[]{:S(2)}) copy-start(bf16[64,512]{1,0:T(8,128)(2,1)} %refs_2_.1) | copy-start | bytes 196612
  0.0 10.2 %copy-start.3 = (bf16[64,512]{1,0:T(8,128)(2,1)S(1)}, bf16[64,512]{1,0:T(8,128)(2,1)}, u32[]{:S(2)}) copy-start(bf16[64,512]{1,0:T(8,128)(2,1)} %refs_3_.1) | copy-start | bytes 196612
  0.0 39.5 %collective-permute-start.10 = (bf16[256,2048]{1,0:T(8,128)(2,1)}, bf16[256,2048]{1,0:T(8,128)(2,1)}, u32[]{:S(2)}, u32[]{:S(2)}) collective-permute-start(bf16[256,2048]{1,0:T(8,128)(2,1)} %refs_0_.3), channel_id=1, source_target_pairs={{0,4},{1,3},{2,6},{3,1},{4,0},{5,7},{6,2},{7,5},{8,12},{9,11},{10,... | collective-permute-start | bytes 3145736 | tf_op jit(solution)/shard_map/ppermute | solution.py:202
  1.6 37.9 %collective-permute-start.9 = (bf16[256,2048]{1,0:T(8,128)(2,1)}, bf16[256,2048]{1,0:T(8,128)(2,1)}, u32[]{:S(2)}, u32[]{:S(2)}) collective-permute-start(bf16[256,2048]{1,0:T(8,128)(2,1)} %refs_0_.3), channel_id=1, source_target_pairs={{0,2},{1,5},{2,0},{3,7},{4,6},{5,1},{6,4},{7,3},{8,10},{9,13},{10,... | collective-permute-start | bytes 3145736 | tf_op jit(solution)/shard_map/ppermute | solution.py:202
  10.3 6.4 %copy-start.5 = (bf16[2048,256]{1,0:T(8,128)(2,1)S(1)}, bf16[2048,256]{1,0:T(8,128)(2,1)}, u32[]{:S(2)}) copy-start(bf16[2048,256]{1,0:T(8,128)(2,1)} %param.18) | copy-start | bytes 3145732
  11.2 13.8 %collective-permute-start.2 = (bf16[336,512]{1,0:T(8,128)(2,1)S(1)}, bf16[336,512]{1,0:T(8,128)(2,1)S(1)}, u32[]{:S(2)}, u32[]{:S(2)}) collective-permute-start(bf16[336,512]{1,0:T(8,128)(2,1)S(1)} %get-tuple-element.44), channel_id=1, source_target_pairs={{0,8},{1,9},{2,10},{3,11},{4,12},{5,13},{6,14},{7,15},{8,0},{9,1},... | collective-permute-start | bytes 1032200 | tf_op jit(solution)/shard_map/ppermute | solution.py:202
  11.7 13.3 %collective-permute-start.1 = (bf16[32,2048]{1,0:T(8,128)(2,1)S(1)}, bf16[32,2048]{1,0:T(8,128)(2,1)S(1)}, u32[]{:S(2)}, u32[]{:S(2)}) collective-permute-start(bf16[32,2048]{1,0:T(8,128)(2,1)S(1)} %fusion.5), channel_id=1, source_target_pairs={{0,0},{1,16},{2,1},{3,17},{4,8},{5,24},{6,9},{7,25},{8,2},{9,18},{... | collective-permute-start | bytes 393224 | tf_op jit(solution)/shard_map/ppermute | solution.py:202
  15.2 15.5 %collective-permute-start = (bf16[144,2048]{1,0:T(8,128)(2,1)S(1)}, bf16[144,2048]{1,0:T(8,128)(2,1)}, u32[]{:S(2)}, u32[]{:S(2)}) collective-permute-start(bf16[144,2048]{1,0:T(8,128)(2,1)S(1)} %fusion.2), channel_id=1, source_target_pairs={{1,16},{3,18},{5,20},{7,22},{9,24},{11,26},{13,28},{15,30},{16,1},... | collective-permute-start | bytes 1769480 | tf_op jit(solution)/shard_map/ppermute | solution.py:202
  25.1 13.8 %collective-permute-start.7 = (bf16[2,256,512]{2,1,0:T(8,128)(2,1)S(1)}, bf16[2,256,512]{2,1,0:T(8,128)(2,1)S(1)}, u32[]{:S(2)}, u32[]{:S(2)}) collective-permute-start(bf16[2,256,512]{2,1,0:T(8,128)(2,1)S(1)} %pad_maximum_fusion.3.own), channel_id=1, source_target_pairs={{0,2},{1,5},{2,0},{3,7},{4,6},{5,1},{6,4},{7,3},{8,10},{9,13},{10,... | collective-permute-start | bytes 1572872 | tf_op jit(solution)/shard_map/ppermute | solution.py:202
  30.8 31.1 %collective-permute-start.3 = (bf16[176,2048]{1,0:T(8,128)(2,1)S(1)}, bf16[176,2048]{1,0:T(8,128)(2,1)S(1)}, u32[]{:S(2)}, u32[]{:S(2)}) collective-permute-start(bf16[176,2048]{1,0:T(8,128)(2,1)S(1)} %pad_maximum_fusion.2.x0), channel_id=1, source_target_pairs={{0,8},{1,9},{2,10},{3,11},{4,12},{5,13},{6,14},{7,15},{8,0},{9,1},... | collective-permute-start | bytes 2162696 | tf_op jit(solution)/shard_map/ppermute | solution.py:202
  30.9 31.0 %collective-permute-start.4 = (bf16[1024,256]{1,0:T(8,128)(2,1)S(1)}, bf16[1024,256]{1,0:T(8,128)(2,1)S(1)}, u32[]{:S(2)}, u32[]{:S(2)}) collective-permute-start(bf16[1024,256]{1,0:T(8,128)(2,1)S(1)} %get-tuple-element.48), channel_id=1, source_target_pairs={{0,16},{1,17},{2,18},{3,19},{4,20},{5,21},{6,22},{7,23},{8,24},{9,... | collective-permute-start | bytes 1572872 | tf_op jit(solution)/shard_map/ppermute | solution.py:202
  39.0 24.8 %collective-permute-start.8 = (bf16[4,256,512]{2,1,0:T(8,128)(2,1)S(1)}, bf16[4,256,512]{2,1,0:T(8,128)(2,1)S(1)}, u32[]{:S(2)}, u32[]{:S(2)}) collective-permute-start(bf16[4,256,512]{2,1,0:T(8,128)(2,1)S(1)} %pad_maximum_fusion), channel_id=1, source_target_pairs={{0,4},{1,3},{2,6},{3,1},{4,0},{5,7},{6,2},{7,5},{8,12},{9,11},{10,... | collective-permute-start | bytes 3145736 | tf_op jit(solution)/shard_map/ppermute | solution.py:202
  39.6 25.6 %collective-permute-start.11 = (bf16[256,2048]{1,0:T(8,128)(2,1)}, bf16[256,2048]{1,0:T(8,128)(2,1)S(1)}, u32[]{:S(2)}, u32[]{:S(2)}) collective-permute-start(bf16[256,2048]{1,0:T(8,128)(2,1)} %collective-permute-done.9.refs_1_), channel_id=1, source_target_pairs={{0,4},{1,3},{2,6},{3,1},{4,0},{5,7},{6,2},{7,5},{8,12},{9,11},{10,... | collective-permute-start | bytes 3145736 | tf_op jit(solution)/shard_map/ppermute | solution.py:202
  41.2 22.6 %collective-permute-start.6 = (bf16[176,2048]{1,0:T(8,128)(2,1)S(1)}, bf16[176,2048]{1,0:T(8,128)(2,1)S(1)}, u32[]{:S(2)}, u32[]{:S(2)}) collective-permute-start(bf16[176,2048]{1,0:T(8,128)(2,1)S(1)} %pad_maximum_fusion.2.x0), channel_id=1, source_target_pairs={{0,1},{1,0},{2,3},{3,2},{4,5},{5,4},{6,7},{7,6},{8,9},{9,8},{10,11... | collective-permute-start | bytes 2162696 | tf_op jit(solution)/shard_map/ppermute | solution.py:202
  61.9 2.2 %collective-permute-start.5 = (bf16[176,2048]{1,0:T(8,128)(2,1)S(1)}, bf16[176,2048]{1,0:T(8,128)(2,1)S(1)}, u32[]{:S(2)}, u32[]{:S(2)}) collective-permute-start(bf16[176,2048]{1,0:T(8,128)(2,1)S(1)} %collective-permute-done.3.x1), channel_id=1, source_target_pairs={{0,1},{1,0},{2,3},{3,2},{4,5},{5,4},{6,7},{7,6},{8,9},{9,8},{10,11... | collective-permute-start | bytes 2162696 | tf_op jit(solution)/shard_map/ppermute | solution.py:202
  65.1 2.1 %copy-start.7 = (bf16[256,2048]{1,0:T(8,128)(2,1)}, bf16[256,2048]{1,0:T(8,128)(2,1)S(1)}, u32[]{:S(2)}) copy-start(bf16[256,2048]{1,0:T(8,128)(2,1)S(1)} %collective-permute-done.11.refs_3_) | copy-start | bytes 3145732
  67.2 18.1 %collective-permute-start.15 = (bf16[736,256]{1,0:T(8,128)(2,1)S(1)}, bf16[736,256]{1,0:T(8,128)(2,1)S(1)}, u32[]{:S(2)}, u32[]{:S(2)}) collective-permute-start(bf16[736,256]{1,0:T(8,128)(2,1)S(1)} %get-tuple-element.68), channel_id=1, source_target_pairs={{0,16},{1,17},{2,18},{3,19},{4,20},{5,21},{6,22},{7,23},{8,24},{9,... | collective-permute-start | bytes 1130504 | tf_op jit(solution)/shard_map/ppermute | solution.py:202
  74.7 20.3 %collective-permute-start.13 = (bf16[4,128,512]{2,1,0:T(8,128)(2,1)S(1)}, bf16[4,128,512]{2,1,0:T(8,128)(2,1)S(1)}, u32[]{:S(2)}, u32[]{:S(2)}) collective-permute-start(bf16[4,128,512]{2,1,0:T(8,128)(2,1)S(1)} %get-tuple-element.66), channel_id=1, source_target_pairs={{0,8},{1,9},{2,10},{3,11},{4,12},{5,13},{6,14},{7,15},{8,0},{9,1},... | collective-permute-start | bytes 1572872 | tf_op jit(solution)/shard_map/ppermute | solution.py:202
  74.7 33.7 %collective-permute-start.17 = (bf16[2,1024,256]{2,1,0:T(8,128)(2,1)S(1)}, bf16[2,1024,256]{2,1,0:T(8,128)(2,1)S(1)}, u32[]{:S(2)}, u32[]{:S(2)}) collective-permute-start(bf16[2,1024,256]{2,1,0:T(8,128)(2,1)S(1)} %pad_maximum_fusion.1.refs_4_), channel_id=1, source_target_pairs={{0,2},{1,5},{2,0},{3,7},{4,6},{5,1},{6,4},{7,3},{8,10},{9,13},{10,... | collective-permute-start | bytes 3145736 | tf_op jit(solution)/shard_map/ppermute | solution.py:202
  75.8 34.2 %collective-permute-start.12 = (bf16[4,128,512]{2,1,0:T(8,128)(2,1)S(1)}, bf16[4,128,512]{2,1,0:T(8,128)(2,1)S(1)}, u32[]{:S(2)}, u32[]{:S(2)}) collective-permute-start(bf16[4,128,512]{2,1,0:T(8,128)(2,1)S(1)} %get-tuple-element.64), channel_id=1, source_target_pairs={{0,8},{1,9},{2,10},{3,11},{4,12},{5,13},{6,14},{7,15},{8,0},{9,1},... | collective-permute-start | bytes 1572872 | tf_op jit(solution)/shard_map/ppermute | solution.py:202
  86.4 12.9 %collective-permute-start.18 = (bf16[6,128,256]{2,1,0:T(8,128)(2,1)S(1)}, bf16[6,128,256]{2,1,0:T(8,128)(2,1)S(1)}, u32[]{:S(2)}, u32[]{:S(2)}) collective-permute-start(bf16[6,128,256]{2,1,0:T(8,128)(2,1)S(1)} %keys_join.1.kv0), channel_id=1, source_target_pairs={{0,4},{1,3},{2,6},{3,1},{4,0},{5,7},{6,2},{7,5},{8,12},{9,11},{10,... | collective-permute-start | bytes 1179656 | tf_op jit(solution)/shard_map/ppermute | solution.py:202
  95.1 23.5 %collective-permute-start.14 = (bf16[4,128,512]{2,1,0:T(8,128)(2,1)S(1)}, bf16[4,128,512]{2,1,0:T(8,128)(2,1)S(1)}, u32[]{:S(2)}, u32[]{:S(2)}) collective-permute-start(bf16[4,128,512]{2,1,0:T(8,128)(2,1)S(1)} %add_convert_fusion), channel_id=1, source_target_pairs={{0,16},{1,17},{2,18},{3,19},{4,20},{5,21},{6,22},{7,23},{8,24},{9,... | collective-permute-start | bytes 1572872 | tf_op jit(solution)/shard_map/ppermute | solution.py:202
  98.3 9.6 %collective-permute-start.16 = (bf16[6,128,256]{2,1,0:T(8,128)(2,1)S(1)}, bf16[6,128,256]{2,1,0:T(8,128)(2,1)S(1)}, u32[]{:S(2)}, u32[]{:S(2)}) collective-permute-start(bf16[6,128,256]{2,1,0:T(8,128)(2,1)S(1)} %keys_join.1.kv0), channel_id=1, source_target_pairs={{0,2},{1,5},{2,0},{3,7},{4,6},{5,1},{6,4},{7,3},{8,10},{9,13},{10,... | collective-permute-start | bytes 1179656 | tf_op jit(solution)/shard_map/ppermute | solution.py:202
  99.3 15.5 %collective-permute-start.19 = (bf16[6,128,256]{2,1,0:T(8,128)(2,1)S(1)}, bf16[6,128,256]{2,1,0:T(8,128)(2,1)S(1)}, u32[]{:S(2)}, u32[]{:S(2)}) collective-permute-start(bf16[6,128,256]{2,1,0:T(8,128)(2,1)S(1)} %keys_join.1.kv0), channel_id=1, source_target_pairs={{0,6},{1,7},{2,4},{3,5},{4,2},{5,3},{6,0},{7,1},{8,14},{9,15},{10,... | collective-permute-start | bytes 1179656 | tf_op jit(solution)/shard_map/ppermute | solution.py:202
  108.0 30.6 %collective-permute-start.22 = (bf16[2,1024,256]{2,1,0:T(8,128)(2,1)S(1)}, bf16[2,1024,256]{2,1,0:T(8,128)(2,1)S(1)}, u32[]{:S(2)}, u32[]{:S(2)}) collective-permute-start(bf16[2,1024,256]{2,1,0:T(8,128)(2,1)S(1)} %pad_maximum_fusion.1.refs_4_), channel_id=1, source_target_pairs={{0,4},{1,3},{2,6},{3,1},{4,0},{5,7},{6,2},{7,5},{8,12},{9,11},{10,... | collective-permute-start | bytes 3145736 | tf_op jit(solution)/shard_map/ppermute | solution.py:202
  108.4 30.1 %collective-permute-start.23 = (bf16[2,1024,256]{2,1,0:T(8,128)(2,1)S(1)}, bf16[2,1024,256]{2,1,0:T(8,128)(2,1)S(1)}, u32[]{:S(2)}, u32[]{:S(2)}) collective-permute-start(bf16[2,1024,256]{2,1,0:T(8,128)(2,1)S(1)} %collective-permute-done.17.refs_5_), channel_id=1, source_target_pairs={{0,4},{1,3},{2,6},{3,1},{4,0},{5,7},{6,2},{7,5},{8,12},{9,11},{10,... | collective-permute-start | bytes 3145736 | tf_op jit(solution)/shard_map/ppermute | solution.py:202
  123.3 9.0 %collective-permute-start.21 = (bf16[512,256]{1,0:T(8,128)(2,1)S(1)}, bf16[512,256]{1,0:T(8,128)(2,1)S(1)}, u32[]{:S(2)}, u32[]{:S(2)}) collective-permute-start(bf16[512,256]{1,0:T(8,128)(2,1)S(1)} %attend.3.refs_1_), channel_id=1, source_target_pairs={{0,8},{1,9},{2,10},{3,11},{4,12},{5,13},{6,14},{7,15},{8,0},{9,1},... | collective-permute-start | bytes 786440 | tf_op jit(solution)/shard_map/ppermute | solution.py:202
  132.1 6.4 %collective-permute-start.20 = (bf16[512,256]{1,0:T(8,128)(2,1)S(1)}, bf16[512,256]{1,0:T(8,128)(2,1)S(1)}, u32[]{:S(2)}, u32[]{:S(2)}) collective-permute-start(bf16[512,256]{1,0:T(8,128)(2,1)S(1)} %attend.2.refs_0_), channel_id=1, source_target_pairs={{0,8},{1,9},{2,10},{3,11},{4,12},{5,13},{6,14},{7,15},{8,0},{9,1},... | collective-permute-start | bytes 786440 | tf_op jit(solution)/shard_map/ppermute | solution.py:202
  138.6 1.0 copy-start.8
  143.5 2.7 %collective-permute-start.24 = (bf16[4,128,1024]{2,1,0:T(8,128)(2,1)S(1)}, bf16[4,128,1024]{2,1,0:T(8,128)(2,1)S(1)}, u32[]{:S(2)}, u32[]{:S(2)}) collective-permute-start(bf16[4,128,1024]{2,1,0:T(8,128)(2,1)S(1)} %get-tuple-element.76), channel_id=1, source_target_pairs={{0,1},{1,0},{2,3},{3,2},{4,5},{5,4},{6,7},{7,6},{8,9},{9,8},{10,11... | collective-permute-start | bytes 3145736 | tf_op jit(solution)/shard_map/ppermute | solution.py:202
  148.0 19.9 %collective-permute-start.25 = (bf16[128,1024]{1,0:T(8,128)(2,1)S(1)}, bf16[128,1024]{1,0:T(8,128)(2,1)S(1)}, u32[]{:S(2)}, u32[]{:S(2)}) collective-permute-start(bf16[128,1024]{1,0:T(8,128)(2,1)S(1)} %get-tuple-element.81), channel_id=1, source_target_pairs={{0,8},{1,9},{2,10},{3,11},{4,12},{5,13},{6,14},{7,15},{8,16},{9,17... | collective-permute-start | bytes 786440 | tf_op jit(solution)/shard_map/ppermute | solution.py:202
  150.0 22.7 %collective-permute-start.26 = (bf16[128,1024]{1,0:T(8,128)(2,1)S(1)}, bf16[128,1024]{1,0:T(8,128)(2,1)S(1)}, u32[]{:S(2)}, u32[]{:S(2)}) collective-permute-start(bf16[128,1024]{1,0:T(8,128)(2,1)S(1)} %get-tuple-element.80), channel_id=1, source_target_pairs={{0,16},{1,17},{2,18},{3,19},{4,20},{5,21},{6,22},{7,23},{8,24},{9,... | collective-permute-start | bytes 786440 | tf_op jit(solution)/shard_map/ppermute | solution.py:202
  151.1 23.2 %collective-permute-start.27 = (bf16[128,1024]{1,0:T(8,128)(2,1)S(1)}, bf16[128,1024]{1,0:T(8,128)(2,1)S(1)}, u32[]{:S(2)}, u32[]{:S(2)}) collective-permute-start(bf16[128,1024]{1,0:T(8,128)(2,1)S(1)} %get-tuple-element.79), channel_id=1, source_target_pairs={{0,24},{1,25},{2,26},{3,27},{4,28},{5,29},{6,30},{7,31},{8,0},{9,1... | collective-permute-start | bytes 786440 | tf_op jit(solution)/shard_map/ppermute | solution.py:202
